TPU v7x, 32 devices: a whole 2x2x4 slice. The times are simulated.
32 devices in a mesh: pos: 8 (over z, x), pix: 4 (over y, core).
Axes of the slice: x: 2, y: 2, z: 4, core: 2. Of those that a mesh axis runs over, the one named last changes fastest.
Arguments:
- probes: float32 [4096, 32768], P('pos', 'pix'), may hold values from -1000 to 1000, as said below
- sketch: float32 [32768, 48], P('pix'), may hold values from -0.03125 to 0.03125
Outputs:
- projection: float32 [48, 32768], P(None, 'pix')
Inputs may be any that keep to these rules, and one draw needn't show every extreme that they name: `probes`: real values of varying scale per position and per column.
All inputs are finite; a program needn't handle non-finite values.
Results may differ from a plain program's by a relative error of at most 0.000075.
Values sent between devices are 32-bit elements; how exact they have to be, the bound alone decides.
No kernel may reach another device: no remote copies, remote signals or barrier semaphores. Data moves between devices by JAX's collectives and lax.ppermute only.
A program may use at most 64 MiB of HBM per device.

v0:
```python
import jax
import jax.numpy as jnp
from jax import lax
from jax.sharding import PartitionSpec as P


def gram_of(rows):
    return jnp.dot(
        rows.T, rows, precision=lax.Precision.HIGHEST, preferred_element_type=jnp.float32
    )


def lower_solve(lower, right):
    return lax.linalg.triangular_solve(lower, right, left_side=True, lower=True)


def body(probes, sketch):
    local = jnp.dot(
        probes, sketch, precision=lax.Precision.HIGHEST, preferred_element_type=jnp.float32
    )
    tall = lax.psum(local, "pix")
    gram = lax.psum(gram_of(tall), "pos")
    lower = jnp.linalg.cholesky(gram)
    basis = lower_solve(lower, tall.T).T
    partial_sum = jnp.dot(
        basis.T, probes, precision=lax.Precision.HIGHEST, preferred_element_type=jnp.float32
    )
    projection = lax.psum(partial_sum, "pos")
    return projection


def solution(mesh):
    in_specs = (P("pos", "pix"), P("pix", None))
    out_specs = P(None, "pix")
    return jax.shard_map(body, mesh=mesh, in_specs=in_specs, out_specs=out_specs, check_vma=False)
```

profile of v0, /device:TPU:0, one launch (start us, length us, event | category | flops | bytes accessed | tf_op | source)
XLA Modules:
  0.0 220.9 jit_solution(1163426428896512343)
XLA Ops:
  6.5 0.0 copy-start
  6.5 0.0 all-reduce.3.cloned.1.call-start
  6.5 1.4 copy-done
  7.9 20.2 %fusion.4 = f32[512,48]{0,1:T(8,128)} fusion(f32[512,8192]{1,0:T(8,128)} %param.2, f32[8192,48]{0,1:T(8,128)S(1)} %copy-done), kind=kOutput, calls=%fused_computation.10 | convolution fusion | flops 2415919104 | bytes 18448384 | tf_op jit(solution)/shard_map/dot_general | solution.py:18
  28.1 0.0 all-reduce.3.cloned.1.call-update
  28.2 0.0 all-reduce.5.cloned.1.call-start
  28.2 34.1 %all-reduce.3.cloned.1.call-done = f32[512,48]{0,1:T(8,128)} async-done(((f32[512,48]{0,1:T(8,128)}), f32[512,48]{0,1:T(8,128)}) %all-reduce.3.cloned.1.call-update) | async-done | bytes 98320 | tf_op jit(solution)/shard_map/psum | solution.py:21
  62.3 1.2 fusion.5
  63.5 37.1 %psum.22 = f32[48,48]{0,1:T(8,128)S(1)} all-reduce(f32[48,48]{0,1:T(8,128)S(1)} %fusion.5), channel_id=1, replica_groups=mesh['pos'=8,'pix'=4] {'pos'}, use_global_device_ids=true, to_apply=%region_1.0 | all-reduce | flops 2304 | bytes 18432 | tf_op jit(solution)/shard_map/psum | solution.py:22
  100.6 0.1 copy.4
  100.7 4.4 %cholesky.16 = f32[48,48]{1,0:T(8,128)S(1)} custom-call(f32[48,48]{1,0:T(8,128)S(1)} %fusion.3), custom_call_target="Cholesky" | custom-call | tf_op jit(solution)/shard_map/jit(cholesky)/cholesky | solution.py:23
  105.1 0.6 compare_reduce_fusion
  105.7 0.7 fusion
  106.4 3.7 %custom-call.6 = f32[1,48,48]{1,2,0:T(8,128)S(1)} custom-call(f32[1,48,48]{2,1,0:T(8,128)S(1)} %fusion), custom_call_target="InvertDiagBlocksLowerTriangular" | custom-call | tf_op jit(solution)/shard_map/triangular_solve | solution.py:14
  110.1 1.2 fusion.1
  111.3 14.7 %fusion.6 = f32[48,8192]{1,0:T(8,128)} fusion(f32[48,512]{1,0:T(8,128)S(1)} %fusion.1, f32[512,8192]{1,0:T(8,128)} %param.2), kind=kOutput, calls=%fused_computation.12 | convolution fusion | flops 2415919104 | bytes 18448384 | tf_op jit(solution)/shard_map/dot_general | solution.py:25
  126.0 0.0 all-reduce.5.cloned.1.call-update
  126.0 85.4 %all-reduce.5.cloned.1.call-done = f32[48,8192]{1,0:T(8,128)} async-done(((f32[48,8192]{1,0:T(8,128)}), f32[48,8192]{1,0:T(8,128)}) %all-reduce.5.cloned.1.call-update) | async-done | bytes 1572880 | tf_op jit(solution)/shard_map/psum | solution.py:28
  211.5 2.7 %copy.8 = f32[48,8192]{1,0:T(8,128)} copy(f32[48,8192]{1,0:T(8,128)} %all-reduce.5.cloned.1.call-done) | data formatting | bytes 3145728
  (2 shorter events, 0.0 us)
Async XLA Ops:
  6.5 1.4 copy-start
  6.5 55.8 %all-reduce.3.cloned.1.call-start = ((), (), s32[]{:S(2)}) async-start(), calls=%async_computation | async-start | bytes 196608 | tf_op jit(solution)/shard_map/psum | solution.py:21
  28.2 183.3 %all-reduce.5.cloned.1.call-start = ((), (), s32[]{:S(2)}) async-start(), calls=%async_computation.1 | async-start | bytes 3145728 | tf_op jit(solution)/shard_map/psum | solution.py:28
Sparse Core Ops, SparseCore 0:
  28.3 33.9 all-reduce.2
  126.1 85.2 all-reduce.4
where the time goes:
time: 221 us
  waiting for transfers between devices  120 us (54%)
  matrix products  37.3 us (17%)
  blocking collectives  37.1 us (17%)
  between operations  13.4 us (6%)
  other arithmetic  9.38 us (4%)
  local copies, waits for them, and re-layouts  4.13 us (2%)
    psum x1, waiting for transfers between devices, body(): projection = lax.psum(partial_sum, 'pos')  85.4 us
    psum x1, blocking collectives, body(): gram = lax.psum(gram_of(tall), 'pos')  37.1 us
    psum x1, waiting for transfers between devices, body(): tall = lax.psum(local, 'pix')  34.1 us
    dot_general x1, matrix products, body(): jnp.dot(probes, sketch, precision=lax.Precision.HIGHEST, preferred_elemen...  20.2 us
    dot_general x1, matrix products, body(): jnp.dot(basis.T, probes, precision=lax.Precision.HIGHEST, preferred_eleme...  14.7 us
    another operation x3, other arithmetic, body(): lower = jnp.linalg.cholesky(gram)  5.05 us
  transfers between devices with their start and end apart: 2, of which 2 were waited for; matrix products, arithmetic and copies ran while one was open for 0% of the time, Pallas kernels for 0%

commit v1 on v0

v1 whole, which is shorter than its diff:
```python
import functools

import jax
import jax.numpy as jnp
from jax import lax
from jax.experimental import pallas as pl
from jax.experimental.pallas import tpu as pltpu
from jax.sharding import PartitionSpec as P

F32 = jnp.float32
BF16 = jnp.bfloat16
VMEM_LIMIT = 40 * 1024 * 1024
LAST = (((1,), (1,)), ((), ()))
PLAIN = (((1,), (0,)), ((), ()))


def split(x):
    head = x.astype(BF16)
    return head, (x - head.astype(F32)).astype(BF16)


def dot(a, b, dims):
    return lax.dot_general(a, b, dims, preferred_element_type=F32)


def tall_kernel(x_ref, s_ref, out_ref, acc_ref):
    step = pl.program_id(0)
    rank = s_ref.shape[0]

    @pl.when(step == 0)
    def _():
        acc_ref[...] = jnp.zeros_like(acc_ref)

    s_both = jnp.concatenate(split(s_ref[...]), axis=0)
    x_head, x_rest = split(x_ref[...])
    acc_ref[...] += dot(x_head, s_both, LAST) + dot(x_rest, s_both, LAST)

    @pl.when(step == pl.num_programs(0) - 1)
    def _():
        acc = acc_ref[...].T
        out_ref[...] = acc[:rank] + acc[rank:]


def tall_partial(probes, sketch_t):
    rows, cols = probes.shape
    rank = sketch_t.shape[0]
    width = min(1024, cols)
    return pl.pallas_call(
        tall_kernel,
        grid=(cols // width,),
        in_specs=[
            pl.BlockSpec((rows, width), lambda i: (0, i)),
            pl.BlockSpec((rank, width), lambda i: (0, i)),
        ],
        out_specs=pl.BlockSpec((rank, rows), lambda i: (0, 0)),
        out_shape=jax.ShapeDtypeStruct((rank, rows), F32),
        scratch_shapes=[pltpu.VMEM((rows, 2 * rank), F32)],
        compiler_params=pltpu.CompilerParams(vmem_limit_bytes=VMEM_LIMIT),
        cost_estimate=pl.CostEstimate(
            flops=4 * rows * cols * rank * 2, bytes_accessed=4 * rows * cols, transcendentals=0
        ),
        name="tall_partial",
    )(probes, sketch_t)


def prepare_kernel(*refs):
    parts, (both_ref, gram_ref) = refs[:-2], refs[-2:]
    tall = parts[0][...]
    for part in parts[1:]:
        tall = tall + part[...]
    rank = tall.shape[0]
    head, rest = split(tall)
    tail = (tall - head.astype(F32) - rest.astype(F32)).astype(BF16)
    both_ref[...] = jnp.concatenate([head, rest], axis=0)
    three = jnp.concatenate([head, rest, tail], axis=0)
    g = dot(three, three, LAST)
    r = rank
    big = g[:r, :r]
    cross = g[:r, r : 2 * r] + g[r : 2 * r, :r]
    small = g[:r, 2 * r :] + g[2 * r :, :r] + g[r : 2 * r, r : 2 * r]
    gram_ref[...] = big + (cross + small)


def prepare(parts):
    rank, rows = parts[0].shape
    whole = pl.BlockSpec(memory_space=pltpu.VMEM)
    return pl.pallas_call(
        prepare_kernel,
        in_specs=[whole] * len(parts),
        out_specs=[whole, whole],
        out_shape=[
            jax.ShapeDtypeStruct((2 * rank, rows), BF16),
            jax.ShapeDtypeStruct((rank, rank), F32),
        ],
        compiler_params=pltpu.CompilerParams(vmem_limit_bytes=VMEM_LIMIT),
        cost_estimate=pl.CostEstimate(
            flops=rows * rank * rank * 18, bytes_accessed=24 * rank * rows, transcendentals=0
        ),
        name="prepare",
    )(*parts)


def block_kernel(which_ref, both_ref, x_ref, out_ref):
    rank = out_ref.shape[0]
    both = both_ref[...]
    x_head, x_rest = split(x_ref[...])
    first = dot(both, x_head, PLAIN)
    second = dot(both[:rank], x_rest, PLAIN)
    out_ref[...] = first[:rank] + (first[rank:] + second)


def block_product(which, both, probes, blocks):
    rows, cols = probes.shape
    rank = both.shape[0] // 2
    width = cols // blocks
    sub = min(512, width)
    steps = width // sub
    return pl.pallas_call(
        block_kernel,
        grid_spec=pltpu.PrefetchScalarGridSpec(
            num_scalar_prefetch=1,
            grid=(steps,),
            in_specs=[
                pl.BlockSpec((2 * rank, rows), lambda i, w: (0, 0)),
                pl.BlockSpec((rows, sub), lambda i, w: (0, w[0] * steps + i)),
            ],
            out_specs=pl.BlockSpec((rank, sub), lambda i, w: (0, i)),
        ),
        out_shape=jax.ShapeDtypeStruct((rank, width), F32),
        compiler_params=pltpu.CompilerParams(vmem_limit_bytes=VMEM_LIMIT),
        cost_estimate=pl.CostEstimate(
            flops=6 * rows * width * rank, bytes_accessed=4 * rows * width, transcendentals=0
        ),
        name="block_product",
    )(which, both, probes)


def place_kernel(count, where_ref, *refs):
    parts, (out_ref, sems) = refs[:count], refs[count:]
    width = parts[0].shape[1]
    copies = []
    for r in range(count):
        start = pl.multiple_of(where_ref[r] * width, width)
        copies.append(
            pltpu.make_async_copy(parts[r], out_ref.at[:, pl.ds(start, width)], sems.at[r])
        )
    for copy in copies:
        copy.start()
    for copy in copies:
        copy.wait()


def place(where, parts):
    rank, width = parts[0].shape
    count = len(parts)
    anywhere = pl.BlockSpec(memory_space=pl.ANY)
    return pl.pallas_call(
        functools.partial(place_kernel, count),
        in_specs=[pl.BlockSpec(memory_space=pltpu.SMEM)] + [anywhere] * count,
        out_specs=anywhere,
        out_shape=jax.ShapeDtypeStruct((rank, width * count), F32),
        scratch_shapes=[pltpu.SemaphoreType.DMA((count,))],
        cost_estimate=pl.CostEstimate(
            flops=0, bytes_accessed=8 * rank * width * count, transcendentals=0
        ),
        name="place",
    )(where, *parts)


def body(n_pos, n_pix, probes, sketch):
    def swap(value, axis, size, bit):
        return lax.ppermute(value, axis, [(i, i ^ bit) for i in range(size)])

    me = lax.axis_index("pos").astype(jnp.int32)
    rank = sketch.shape[1]

    own = tall_partial(probes, sketch.T)
    parts = [own] + [swap(own, "pix", n_pix, r) for r in range(1, n_pix)]
    both, gram_part = prepare(parts)

    grams = [gram_part] + [swap(gram_part, "pos", n_pos, r) for r in range(1, n_pos)]

    def product(r):
        return block_product((me ^ r)[None], both, probes, n_pos)

    even = list(range(0, n_pos, 2))
    received = {}
    for s in even[::-1]:
        received[s] = swap(product(s ^ 1), "pos", n_pos, 1)
    pairs = {s: product(s) + received[s] for s in even[::-1]}

    arrived = [swap(pairs[s], "pos", n_pos, s) for s in even[1:][::-1]]

    gram = functools.reduce(jnp.add, grams)
    lower = jnp.linalg.cholesky(gram)
    inverse = lax.linalg.triangular_solve(
        lower, jnp.eye(rank, dtype=F32), left_side=True, lower=True
    )

    mine = functools.reduce(jnp.add, arrived, pairs[0])
    final = jnp.dot(inverse, mine, precision=lax.Precision.HIGHEST, preferred_element_type=F32)

    pieces = {0: final}
    for s in even[1:]:
        pieces[s] = swap(final, "pos", n_pos, s)
    for s in even:
        pieces[s ^ 1] = swap(pieces[s], "pos", n_pos, 1)

    where = me ^ jnp.arange(n_pos, dtype=jnp.int32)
    return place(where, [pieces[r] for r in range(n_pos)])


def solution(mesh):
    in_specs = (P("pos", "pix"), P("pix", None))
    out_specs = P(None, "pix")
    run = functools.partial(body, mesh.shape["pos"], mesh.shape["pix"])
    return jax.shard_map(run, mesh=mesh, in_specs=in_specs, out_specs=out_specs, check_vma=False)
```

time: 221 us -> 157 us (0.71)
  waiting for transfers between devices: 120 us -> 33 us
  Pallas kernels: 0 us -> 75.7 us
  blocking collectives: 37.1 us -> 0 us
  matrix products: 37.3 us -> 0.54 us
  starting transfers between devices: 0.04 us -> 34.9 us
  between operations: 13.4 us -> 0.24 us
    psum x2 -> x0, waiting for transfers between devices: 120 us -> none  [the longest x1 85.4 us: body(): projection = lax.psum(partial_sum, 'pos')]
    pallas_call x0 -> x11, Pallas kernels: none -> 75.7 us  [the longest x1 49.5 us: place(): pl.pallas_call(functools.partial(place_kernel, count), in_specs=[pl.Block...]
    psum x1 -> x0, blocking collectives: 37.1 us -> none  [body(): gram = lax.psum(gram_of(tall), 'pos')]
    dot_general x3 -> x1, matrix products: 36.1 us -> 0.33 us  [body(): jnp.dot(inverse, mine, precision=lax.Precision.HIGHEST, preferred_element...]
    ppermute x0 -> x24, starting transfers between devices: none -> 34.9 us  [swap(): return lax.ppermute(value, axis, [(i, i ^ bit) for i in range(size)])]
    ppermute x0 -> x24, waiting for transfers between devices: none -> 33 us  [swap(): return lax.ppermute(value, axis, [(i, i ^ bit) for i in range(size)])]
  transfers between devices with their start and end apart: 2 -> 24, of which waited for: 2 -> 8; matrix products, arithmetic and copies ran while one was open for 0% -> 7% of each run, Pallas kernels for 0% -> 10%
where the time goes in v1:
time: 157 us
  Pallas kernels  75.7 us (48%)
  starting transfers between devices  34.9 us (22%)
  waiting for transfers between devices  33 us (21%)
  other arithmetic  10.1 us (6%)
  local copies, waits for them, and re-layouts  2.26 us (1%)
    pallas_call x1, Pallas kernels, place(): pl.pallas_call(functools.partial(place_kernel, count), in_specs=[pl.Block...  49.5 us
    ppermute x24, starting transfers between devices, swap(): return lax.ppermute(value, axis, [(i, i ^ bit) for i in range(size)])  34.9 us
    ppermute x24, waiting for transfers between devices, swap(): return lax.ppermute(value, axis, [(i, i ^ bit) for i in range(size)])  33 us
    pallas_call x8, Pallas kernels, block_product(): pl.pallas_call(block_kernel, grid_spec=pltpu.PrefetchScalarGridSpec(num_s...  15.2 us
    pallas_call x1, Pallas kernels, tall_partial(): pl.pallas_call(tall_kernel, grid=(cols // width,), in_specs=[pl.BlockSpec...  10.6 us
    another operation x3, other arithmetic, body(): lower = jnp.linalg.cholesky(gram)  5.13 us
    another operation x2, other arithmetic, body(): lax.linalg.triangular_solve(lower, jnp.eye(rank, dtype=F32), left_side=Tr...  4.37 us
  transfers between devices with their start and end apart: 24, of which 8 were waited for; matrix products, arithmetic and copies ran while one was open for 7% of the time, Pallas kernels for 10%

profile of v1, /device:TPU:0, one launch (start us, length us, event | category | flops | bytes accessed | tf_op | source)
XLA Modules:
  0.0 156.7 jit_solution(17528414303545718067)
XLA Ops:
  1.4 10.6 %tall_partial.1.refs_0_ = f32[48,512]{1,0:T(8,128)S(1)} custom-call(f32[512,8192]{1,0:T(8,128)} %x_ref.17, f32[48,8192]{1,0:T(8,128)S(1)} %bitcast.19), custom_call_target="tpu_custom_call" | custom-call | flops 1610612736 | bytes 16777216 | tf_op jit(solution)/shard_map/tall_partial/pallas_call | solution.py:48
  12.0 2.5 %collective-permute-start.2 = (f32[48,512]{1,0:T(8,128)S(1)}, f32[48,512]{1,0:T(8,128)S(1)}, u32[]{:S(2)}, u32[]{:S(2)}) collective-permute-start(f32[48,512]{1,0:T(8,128)S(1)} %tall_partial.1.refs_0_), channel_id=1, source_target_pairs={{0,3},{1,2},{2,1},{3,0},{4,7},{5,6},{6,5},{7,4},{8,11},{9,10},{10,... | collective-permute-start | bytes 294920 | tf_op jit(solution)/shard_map/ppermute | solution.py:172
  15.2 2.5 %collective-permute-done.2.refs_3_ = f32[48,512]{1,0:T(8,128)S(1)} collective-permute-done((f32[48,512]{1,0:T(8,128)S(1)}, f32[48,512]{1,0:T(8,128)S(1)}, u32[]{:S(2)}, u32[]{:S(2)}) %collective-permute-start.2) | collective-permute-done | bytes 98336 | tf_op jit(solution)/shard_map/ppermute | solution.py:172
  17.7 2.3 %collective-permute-done.1.refs_2_ = f32[48,512]{1,0:T(8,128)S(1)} collective-permute-done((f32[48,512]{1,0:T(8,128)S(1)}, f32[48,512]{1,0:T(8,128)S(1)}, u32[]{:S(2)}, u32[]{:S(2)}) %collective-permute-start.1) | collective-permute-done | bytes 98336 | tf_op jit(solution)/shard_map/ppermute | solution.py:172
  20.4 5.3 %collective-permute-start.9 = (f32[48,48]{0,1:T(8,128)S(1)}, f32[48,48]{0,1:T(8,128)S(1)}, u32[]{:S(2)}, u32[]{:S(2)}) collective-permute-start(f32[48,48]{0,1:T(8,128)S(1)} %copy.4), channel_id=1, source_target_pairs={{0,28},{4,24},{8,20},{12,16},{16,12},{20,8},{24,4},{28,0},{1,29},{... | collective-permute-start | bytes 27656 | tf_op jit(solution)/shard_map/ppermute | solution.py:172
  26.8 2.0 %collective-permute-start.6 = (f32[48,48]{0,1:T(8,128)S(1)}, f32[48,48]{0,1:T(8,128)S(1)}, u32[]{:S(2)}, u32[]{:S(2)}) collective-permute-start(f32[48,48]{0,1:T(8,128)S(1)} %copy.4), channel_id=1, source_target_pairs={{0,16},{4,20},{8,24},{12,28},{16,0},{20,4},{24,8},{28,12},{1,17},{... | collective-permute-start | bytes 27656 | tf_op jit(solution)/shard_map/ppermute | solution.py:172
  28.8 2.3 %collective-permute-start.5 = (f32[48,48]{0,1:T(8,128)S(1)}, f32[48,48]{0,1:T(8,128)S(1)}, u32[]{:S(2)}, u32[]{:S(2)}) collective-permute-start(f32[48,48]{0,1:T(8,128)S(1)} %copy.4), channel_id=1, source_target_pairs={{0,12},{4,8},{8,4},{12,0},{16,28},{20,24},{24,20},{28,16},{1,13},{... | collective-permute-start | bytes 27656 | tf_op jit(solution)/shard_map/ppermute | solution.py:172
  33.0 1.9 %block_product.14 = f32[48,1024]{1,0:T(8,128)S(1)} custom-call(s32[1]{0:T(128)} %bitcast.10.which_ref, bf16[96,512]{1,0:T(8,128)(2,1)S(1)} %get-tuple-element.8.both_ref, f32[512,8192]{1,0:T(8,128)} %x_ref.17), custom_call_target="tpu_custom_call" | custom-call | flops 150994944 | bytes 2097152 | tf_op jit(solution)/shard_map/block_product/pallas_call | solution.py:118
  34.9 1.9 %block_product.13 = f32[48,1024]{1,0:T(8,128)S(1)} custom-call(s32[1]{0:T(128)} %bitcast.9.which_ref, bf16[96,512]{1,0:T(8,128)(2,1)S(1)} %get-tuple-element.8.both_ref, f32[512,8192]{1,0:T(8,128)} %x_ref.17), custom_call_target="tpu_custom_call" | custom-call | flops 150994944 | bytes 2097152 | tf_op jit(solution)/shard_map/block_product/pallas_call | solution.py:118
  36.8 1.9 %block_product.12 = f32[48,1024]{1,0:T(8,128)S(1)} custom-call(s32[1]{0:T(128)} %bitcast.8.which_ref, bf16[96,512]{1,0:T(8,128)(2,1)S(1)} %get-tuple-element.8.both_ref, f32[512,8192]{1,0:T(8,128)} %x_ref.17), custom_call_target="tpu_custom_call" | custom-call | flops 150994944 | bytes 2097152 | tf_op jit(solution)/shard_map/block_product/pallas_call | solution.py:118
  38.7 1.9 %block_product.11 = f32[48,1024]{1,0:T(8,128)S(1)} custom-call(s32[1]{0:T(128)} %bitcast.7.which_ref, bf16[96,512]{1,0:T(8,128)(2,1)S(1)} %get-tuple-element.8.both_ref, f32[512,8192]{1,0:T(8,128)} %x_ref.17), custom_call_target="tpu_custom_call" | custom-call | flops 150994944 | bytes 2097152 | tf_op jit(solution)/shard_map/block_product/pallas_call | solution.py:118
  40.6 1.9 %block_product.10 = f32[48,1024]{1,0:T(8,128)S(1)} custom-call(s32[1]{0:T(128)} %bitcast.6.which_ref, bf16[96,512]{1,0:T(8,128)(2,1)S(1)} %get-tuple-element.8.both_ref, f32[512,8192]{1,0:T(8,128)} %x_ref.17), custom_call_target="tpu_custom_call" | custom-call | flops 150994944 | bytes 2097152 | tf_op jit(solution)/shard_map/block_product/pallas_call | solution.py:118
  51.9 4.4 %cholesky.17 = f32[48,48]{1,0:T(8,128)S(1)} custom-call(f32[48,48]{1,0:T(8,128)S(1)} %fusion.8), custom_call_target="Cholesky" | custom-call | tf_op jit(solution)/shard_map/jit(cholesky)/cholesky | solution.py:195
  57.7 3.7 %custom-call.6 = f32[1,48,48]{1,2,0:T(8,128)S(1)} custom-call(f32[1,48,48]{2,1,0:T(8,128)S(1)} %fusion.5), custom_call_target="InvertDiagBlocksLowerTriangular" | custom-call | tf_op jit(solution)/shard_map/triangular_solve | solution.py:196
  61.4 3.8 %collective-permute-start.12 = (f32[48,1024]{1,0:T(8,128)S(1)}, f32[48,1024]{1,0:T(8,128)S(1)}, u32[]{:S(2)}, u32[]{:S(2)}) collective-permute-start(f32[48,1024]{1,0:T(8,128)S(1)} %add.62), channel_id=1, source_target_pairs={{0,24},{4,28},{8,16},{12,20},{16,8},{20,12},{24,0},{28,4},{1,25},{... | collective-permute-start | bytes 589832 | tf_op jit(solution)/shard_map/ppermute | solution.py:172
  68.1 3.0 %collective-permute-done.12 = f32[48,1024]{1,0:T(8,128)S(1)} collective-permute-done((f32[48,1024]{1,0:T(8,128)S(1)}, f32[48,1024]{1,0:T(8,128)S(1)}, u32[]{:S(2)}, u32[]{:S(2)}) %collective-permute-start.12) | collective-permute-done | bytes 196640 | tf_op jit(solution)/shard_map/ppermute | solution.py:172
  71.0 8.0 %collective-permute-done.14 = f32[48,1024]{1,0:T(8,128)S(1)} collective-permute-done((f32[48,1024]{1,0:T(8,128)S(1)}, f32[48,1024]{1,0:T(8,128)S(1)}, u32[]{:S(2)}, u32[]{:S(2)}) %collective-permute-start.14) | collective-permute-done | bytes 196640 | tf_op jit(solution)/shard_map/ppermute | solution.py:172
  79.4 2.5 %collective-permute-start.22 = (f32[48,1024]{1,0:T(8,128)S(1)}, f32[48,1024]{1,0:T(8,128)S(1)}, u32[]{:S(2)}, u32[]{:S(2)}) collective-permute-start(f32[48,1024]{1,0:T(8,128)S(1)} %fusion.refs_0_), channel_id=1, source_target_pairs={{0,24},{4,28},{8,16},{12,20},{16,8},{20,12},{24,0},{28,4},{1,25},{... | collective-permute-start | bytes 589832 | tf_op jit(solution)/shard_map/ppermute | solution.py:172
  81.8 2.0 %collective-permute-start.18 = (f32[48,1024]{1,0:T(8,128)S(1)}, f32[48,1024]{1,0:T(8,128)S(1)}, u32[]{:S(2)}, u32[]{:S(2)}) collective-permute-start(f32[48,1024]{1,0:T(8,128)S(1)} %fusion.refs_0_), channel_id=1, source_target_pairs={{0,8},{4,12},{8,0},{12,4},{16,24},{20,28},{24,16},{28,20},{1,9},{5... | collective-permute-start | bytes 589832 | tf_op jit(solution)/shard_map/ppermute | solution.py:172
  85.3 3.9 %collective-permute-done.22.refs_6_ = f32[48,1024]{1,0:T(8,128)S(1)} collective-permute-done((f32[48,1024]{1,0:T(8,128)S(1)}, f32[48,1024]{1,0:T(8,128)S(1)}, u32[]{:S(2)}, u32[]{:S(2)}) %collective-permute-start.22) | collective-permute-done | bytes 196640 | tf_op jit(solution)/shard_map/ppermute | solution.py:172
  90.6 6.2 %collective-permute-done.20.refs_4_ = f32[48,1024]{1,0:T(8,128)S(1)} collective-permute-done((f32[48,1024]{1,0:T(8,128)S(1)}, f32[48,1024]{1,0:T(8,128)S(1)}, u32[]{:S(2)}, u32[]{:S(2)}) %collective-permute-start.20) | collective-permute-done | bytes 196640 | tf_op jit(solution)/shard_map/ppermute | solution.py:172
  99.3 5.0 %collective-permute-done.21.refs_5_ = f32[48,1024]{1,0:T(8,128)S(1)} collective-permute-done((f32[48,1024]{1,0:T(8,128)S(1)}, f32[48,1024]{1,0:T(8,128)S(1)}, u32[]{:S(2)}, u32[]{:S(2)}) %collective-permute-start.21) | collective-permute-done | bytes 196640 | tf_op jit(solution)/shard_map/ppermute | solution.py:172
  104.4 2.1 %collective-permute-done.19.refs_3_ = f32[48,1024]{1,0:T(8,128)S(1)} collective-permute-done((f32[48,1024]{1,0:T(8,128)S(1)}, f32[48,1024]{1,0:T(8,128)S(1)}, u32[]{:S(2)}, u32[]{:S(2)}) %collective-permute-start.19) | collective-permute-done | bytes 196640 | tf_op jit(solution)/shard_map/ppermute | solution.py:172
  107.2 49.5 %place.1 = f32[48,8192]{1,0:T(8,128)} custom-call(s32[8]{0:T(128)} %iota_xor_fusion.where_ref, f32[48,1024]{1,0:T(8,128)} %copy-done.1, f32[48,1024]{1,0:T(8,128)} %copy-done.5, f32[48,1024]{1,0:T(8,128)} %copy-done.4, f32[48,1024]{1,0:T(8,128)} %copy-done.8, f32[48,1024]{1,0:T(8,128)} %copy-done.3, f32[48,1024]{1,0:T(8,128)} %copy-done.7, ...), custom_call_target="tpu_custom_call" | custom-call | bytes 3145728 | tf_op jit(solution)/shard_map/place/pallas_call | solution.py:157
  (68 shorter events, 25.5 us)
Async XLA Ops:
  12.0 5.7 %collective-permute-start.2 = (f32[48,512]{1,0:T(8,128)S(1)}, f32[48,512]{1,0:T(8,128)S(1)}, u32[]{:S(2)}, u32[]{:S(2)}) collective-permute-start(f32[48,512]{1,0:T(8,128)S(1)} %tall_partial.1.refs_0_), channel_id=1, source_target_pairs={{0,3},{1,2},{2,1},{3,0},{4,7},{5,6},{6,5},{7,4},{8,11},{9,10},{10,... | collective-permute-start | bytes 294920 | tf_op jit(solution)/shard_map/ppermute | solution.py:172
  14.5 5.5 %collective-permute-start.1 = (f32[48,512]{1,0:T(8,128)S(1)}, f32[48,512]{1,0:T(8,128)S(1)}, u32[]{:S(2)}, u32[]{:S(2)}) collective-permute-start(f32[48,512]{1,0:T(8,128)S(1)} %tall_partial.1.refs_0_), channel_id=1, source_target_pairs={{0,2},{1,3},{2,0},{3,1},{4,6},{5,7},{6,4},{7,5},{8,10},{9,11},{10,... | collective-permute-start | bytes 294920 | tf_op jit(solution)/shard_map/ppermute | solution.py:172
  15.1 4.8 %collective-permute-start = (f32[48,512]{1,0:T(8,128)S(1)}, f32[48,512]{1,0:T(8,128)S(1)}, u32[]{:S(2)}, u32[]{:S(2)}) collective-permute-start(f32[48,512]{1,0:T(8,128)S(1)} %tall_partial.1.refs_0_), channel_id=1, source_target_pairs={{0,1},{1,0},{2,3},{3,2},{4,5},{5,4},{6,7},{7,6},{8,9},{9,8},{10,11... | collective-permute-start | bytes 294920 | tf_op jit(solution)/shard_map/ppermute | solution.py:172
  20.4 24.0 %collective-permute-start.9 = (f32[48,48]{0,1:T(8,128)S(1)}, f32[48,48]{0,1:T(8,128)S(1)}, u32[]{:S(2)}, u32[]{:S(2)}) collective-permute-start(f32[48,48]{0,1:T(8,128)S(1)} %copy.4), channel_id=1, source_target_pairs={{0,28},{4,24},{8,20},{12,16},{16,12},{20,8},{24,4},{28,0},{1,29},{... | collective-permute-start | bytes 27656 | tf_op jit(solution)/shard_map/ppermute | solution.py:172
  25.8 19.5 %collective-permute-start.8 = (f32[48,48]{0,1:T(8,128)S(1)}, f32[48,48]{0,1:T(8,128)S(1)}, u32[]{:S(2)}, u32[]{:S(2)}) collective-permute-start(f32[48,48]{0,1:T(8,128)S(1)} %copy.4), channel_id=1, source_target_pairs={{0,24},{4,28},{8,16},{12,20},{16,8},{20,12},{24,0},{28,4},{1,25},{... | collective-permute-start | bytes 27656 | tf_op jit(solution)/shard_map/ppermute | solution.py:172
  26.0 21.6 %collective-permute-start.7 = (f32[48,48]{0,1:T(8,128)S(1)}, f32[48,48]{0,1:T(8,128)S(1)}, u32[]{:S(2)}, u32[]{:S(2)}) collective-permute-start(f32[48,48]{0,1:T(8,128)S(1)} %copy.4), channel_id=1, source_target_pairs={{0,20},{4,16},{8,28},{12,24},{16,4},{20,0},{24,12},{28,8},{1,21},{... | collective-permute-start | bytes 27656 | tf_op jit(solution)/shard_map/ppermute | solution.py:172
  26.8 22.5 %collective-permute-start.6 = (f32[48,48]{0,1:T(8,128)S(1)}, f32[48,48]{0,1:T(8,128)S(1)}, u32[]{:S(2)}, u32[]{:S(2)}) collective-permute-start(f32[48,48]{0,1:T(8,128)S(1)} %copy.4), channel_id=1, source_target_pairs={{0,16},{4,20},{8,24},{12,28},{16,0},{20,4},{24,8},{28,12},{1,17},{... | collective-permute-start | bytes 27656 | tf_op jit(solution)/shard_map/ppermute | solution.py:172
  28.8 20.9 %collective-permute-start.5 = (f32[48,48]{0,1:T(8,128)S(1)}, f32[48,48]{0,1:T(8,128)S(1)}, u32[]{:S(2)}, u32[]{:S(2)}) collective-permute-start(f32[48,48]{0,1:T(8,128)S(1)} %copy.4), channel_id=1, source_target_pairs={{0,12},{4,8},{8,4},{12,0},{16,28},{20,24},{24,20},{28,16},{1,13},{... | collective-permute-start | bytes 27656 | tf_op jit(solution)/shard_map/ppermute | solution.py:172
  44.4 6.9 %collective-permute-start.4 = (f32[48,48]{0,1:T(8,128)S(1)}, f32[48,48]{0,1:T(8,128)S(1)}, u32[]{:S(2)}, u32[]{:S(2)}) collective-permute-start(f32[48,48]{0,1:T(8,128)S(1)} %copy.4), channel_id=1, source_target_pairs={{0,8},{4,12},{8,0},{12,4},{16,24},{20,28},{24,16},{28,20},{1,9},{5... | collective-permute-start | bytes 27656 | tf_op jit(solution)/shard_map/ppermute | solution.py:172
  45.3 6.5 %collective-permute-start.3 = (f32[48,48]{0,1:T(8,128)S(1)}, f32[48,48]{0,1:T(8,128)S(1)}, u32[]{:S(2)}, u32[]{:S(2)}) collective-permute-start(f32[48,48]{0,1:T(8,128)S(1)} %copy.4), channel_id=1, source_target_pairs={{0,4},{4,0},{8,12},{12,8},{16,20},{20,16},{24,28},{28,24},{1,5},{5... | collective-permute-start | bytes 27656 | tf_op jit(solution)/shard_map/ppermute | solution.py:172
  47.6 20.4 %collective-permute-start.10 = (f32[48,1024]{1,0:T(8,128)S(1)}, f32[48,1024]{1,0:T(8,128)S(1)}, u32[]{:S(2)}, u32[]{:S(2)}) collective-permute-start(f32[48,1024]{1,0:T(8,128)S(1)} %block_product.9), channel_id=1, source_target_pairs={{0,4},{4,0},{8,12},{12,8},{16,20},{20,16},{24,28},{28,24},{1,5},{5... | collective-permute-start | bytes 589832 | tf_op jit(solution)/shard_map/ppermute | solution.py:172
  49.3 12.1 %collective-permute-start.11 = (f32[48,1024]{1,0:T(8,128)S(1)}, f32[48,1024]{1,0:T(8,128)S(1)}, u32[]{:S(2)}, u32[]{:S(2)}) collective-permute-start(f32[48,1024]{1,0:T(8,128)S(1)} %block_product.11), channel_id=1, source_target_pairs={{0,4},{4,0},{8,12},{12,8},{16,20},{20,16},{24,28},{28,24},{1,5},{5... | collective-permute-start | bytes 589832 | tf_op jit(solution)/shard_map/ppermute | solution.py:172
  49.7 15.5 %collective-permute-start.13 = (f32[48,1024]{1,0:T(8,128)S(1)}, f32[48,1024]{1,0:T(8,128)S(1)}, u32[]{:S(2)}, u32[]{:S(2)}) collective-permute-start(f32[48,1024]{1,0:T(8,128)S(1)} %block_product.13), channel_id=1, source_target_pairs={{0,4},{4,0},{8,12},{12,8},{16,20},{20,16},{24,28},{28,24},{1,5},{5... | collective-permute-start | bytes 589832 | tf_op jit(solution)/shard_map/ppermute | solution.py:172
  51.3 14.8 %collective-permute-start.15 = (f32[48,1024]{1,0:T(8,128)S(1)}, f32[48,1024]{1,0:T(8,128)S(1)}, u32[]{:S(2)}, u32[]{:S(2)}) collective-permute-start(f32[48,1024]{1,0:T(8,128)S(1)} %block_product.15), channel_id=1, source_target_pairs={{0,4},{4,0},{8,12},{12,8},{16,20},{20,16},{24,28},{28,24},{1,5},{5... | collective-permute-start | bytes 589832 | tf_op jit(solution)/shard_map/ppermute | solution.py:172
  61.4 9.6 %collective-permute-start.12 = (f32[48,1024]{1,0:T(8,128)S(1)}, f32[48,1024]{1,0:T(8,128)S(1)}, u32[]{:S(2)}, u32[]{:S(2)}) collective-permute-start(f32[48,1024]{1,0:T(8,128)S(1)} %add.62), channel_id=1, source_target_pairs={{0,24},{4,28},{8,16},{12,20},{16,8},{20,12},{24,0},{28,4},{1,25},{... | collective-permute-start | bytes 589832 | tf_op jit(solution)/shard_map/ppermute | solution.py:172
  65.2 13.8 %collective-permute-start.14 = (f32[48,1024]{1,0:T(8,128)S(1)}, f32[48,1024]{1,0:T(8,128)S(1)}, u32[]{:S(2)}, u32[]{:S(2)}) collective-permute-start(f32[48,1024]{1,0:T(8,128)S(1)} %add.64), channel_id=1, source_target_pairs={{0,16},{4,20},{8,24},{12,28},{16,0},{20,4},{24,8},{28,12},{1,17},{... | collective-permute-start | bytes 589832 | tf_op jit(solution)/shard_map/ppermute | solution.py:172
  66.1 12.9 %collective-permute-start.16 = (f32[48,1024]{1,0:T(8,128)S(1)}, f32[48,1024]{1,0:T(8,128)S(1)}, u32[]{:S(2)}, u32[]{:S(2)}) collective-permute-start(f32[48,1024]{1,0:T(8,128)S(1)} %add.66), channel_id=1, source_target_pairs={{0,8},{4,12},{8,0},{12,4},{16,24},{20,28},{24,16},{28,20},{1,9},{5... | collective-permute-start | bytes 589832 | tf_op jit(solution)/shard_map/ppermute | solution.py:172
  79.4 9.8 %collective-permute-start.22 = (f32[48,1024]{1,0:T(8,128)S(1)}, f32[48,1024]{1,0:T(8,128)S(1)}, u32[]{:S(2)}, u32[]{:S(2)}) collective-permute-start(f32[48,1024]{1,0:T(8,128)S(1)} %fusion.refs_0_), channel_id=1, source_target_pairs={{0,24},{4,28},{8,16},{12,20},{16,8},{20,12},{24,0},{28,4},{1,25},{... | collective-permute-start | bytes 589832 | tf_op jit(solution)/shard_map/ppermute | solution.py:172
  81.8 15.0 %collective-permute-start.20 = (f32[48,1024]{1,0:T(8,128)S(1)}, f32[48,1024]{1,0:T(8,128)S(1)}, u32[]{:S(2)}, u32[]{:S(2)}) collective-permute-start(f32[48,1024]{1,0:T(8,128)S(1)} %fusion.refs_0_), channel_id=1, source_target_pairs={{0,16},{4,20},{8,24},{12,28},{16,0},{20,4},{24,8},{28,12},{1,17},{... | collective-permute-start | bytes 589832 | tf_op jit(solution)/shard_map/ppermute | solution.py:172
  81.8 16.5 %collective-permute-start.18 = (f32[48,1024]{1,0:T(8,128)S(1)}, f32[48,1024]{1,0:T(8,128)S(1)}, u32[]{:S(2)}, u32[]{:S(2)}) collective-permute-start(f32[48,1024]{1,0:T(8,128)S(1)} %fusion.refs_0_), channel_id=1, source_target_pairs={{0,8},{4,12},{8,0},{12,4},{16,24},{20,28},{24,16},{28,20},{1,9},{5... | collective-permute-start | bytes 589832 | tf_op jit(solution)/shard_map/ppermute | solution.py:172
  83.8 15.5 %collective-permute-start.17 = (f32[48,1024]{1,0:T(8,128)S(1)}, f32[48,1024]{1,0:T(8,128)S(1)}, u32[]{:S(2)}, u32[]{:S(2)}) collective-permute-start(f32[48,1024]{1,0:T(8,128)S(1)} %fusion.refs_0_), channel_id=1, source_target_pairs={{0,4},{4,0},{8,12},{12,8},{16,20},{20,16},{24,28},{28,24},{1,5},{5... | collective-permute-start | bytes 589832 | tf_op jit(solution)/shard_map/ppermute | solution.py:172
  89.2 10.2 %collective-permute-start.23 = (f32[48,1024]{1,0:T(8,128)S(1)}, f32[48,1024]{1,0:T(8,128)S(1)}, u32[]{:S(2)}, u32[]{:S(2)}) collective-permute-start(f32[48,1024]{1,0:T(8,128)S(1)} %collective-permute-done.22.refs_6_), channel_id=1, source_target_pairs={{0,4},{4,0},{8,12},{12,8},{16,20},{20,16},{24,28},{28,24},{1,5},{5... | collective-permute-start | bytes 589832 | tf_op jit(solution)/shard_map/ppermute | solution.py:172
  96.8 7.6 %collective-permute-start.21 = (f32[48,1024]{1,0:T(8,128)S(1)}, f32[48,1024]{1,0:T(8,128)S(1)}, u32[]{:S(2)}, u32[]{:S(2)}) collective-permute-start(f32[48,1024]{1,0:T(8,128)S(1)} %collective-permute-done.20.refs_4_), channel_id=1, source_target_pairs={{0,4},{4,0},{8,12},{12,8},{16,20},{20,16},{24,28},{28,24},{1,5},{5... | collective-permute-start | bytes 589832 | tf_op jit(solution)/shard_map/ppermute | solution.py:172
  98.3 8.2 %collective-permute-start.19 = (f32[48,1024]{1,0:T(8,128)S(1)}, f32[48,1024]{1,0:T(8,128)S(1)}, u32[]{:S(2)}, u32[]{:S(2)}) collective-permute-start(f32[48,1024]{1,0:T(8,128)S(1)} %collective-permute-done.18.refs_2_), channel_id=1, source_target_pairs={{0,4},{4,0},{8,12},{12,8},{16,20},{20,16},{24,28},{28,24},{1,5},{5... | collective-permute-start | bytes 589832 | tf_op jit(solution)/shard_map/ppermute | solution.py:172
  (9 other events, 80.9 us)

commit v2 on v1

v2 whole, which is shorter than its diff:
```python
import functools

import jax
import jax.numpy as jnp
from jax import lax
from jax.experimental import pallas as pl
from jax.experimental.pallas import tpu as pltpu
from jax.sharding import PartitionSpec as P

F32 = jnp.float32
BF16 = jnp.bfloat16
VMEM_LIMIT = 40 * 1024 * 1024
LANES = 128
CHUNKS = 4
LAST = (((1,), (1,)), ((), ()))
PLAIN = (((1,), (0,)), ((), ()))
ANYWHERE = pl.BlockSpec(memory_space=pl.ANY)
PARAMS = pltpu.CompilerParams(vmem_limit_bytes=VMEM_LIMIT)


def split(x):
    head = x.astype(BF16)
    return head, (x - head.astype(F32)).astype(BF16)


def dot(a, b, dims):
    return lax.dot_general(a, b, dims, preferred_element_type=F32)


def tall_kernel(x_ref, s_ref, out_ref, acc_ref):
    step = pl.program_id(0)
    rank = s_ref.shape[0]

    @pl.when(step == 0)
    def _():
        acc_ref[...] = jnp.zeros_like(acc_ref)

    s_head, s_rest = split(s_ref[...])
    s_both = jnp.concatenate([s_head, s_rest], axis=0)
    x_head, x_rest = split(x_ref[...])
    both = dot(s_both, x_head, LAST)
    acc_ref[...] += both[:rank] + (both[rank:] + dot(s_head, x_rest, LAST))

    @pl.when(step == pl.num_programs(0) - 1)
    def _():
        out_ref[...] = acc_ref[...]


def tall_partial(probes, sketch_t):
    rows, cols = probes.shape
    rank = sketch_t.shape[0]
    width = min(1024, cols)
    return pl.pallas_call(
        tall_kernel,
        grid=(cols // width,),
        in_specs=[
            pl.BlockSpec((rows, width), lambda i: (0, i)),
            pl.BlockSpec((rank, width), lambda i: (0, i)),
        ],
        out_specs=pl.BlockSpec((rank, rows), lambda i: (0, 0)),
        out_shape=jax.ShapeDtypeStruct((rank, rows), F32),
        scratch_shapes=[pltpu.VMEM((rank, rows), F32)],
        compiler_params=PARAMS,
        cost_estimate=pl.CostEstimate(
            flops=6 * rows * cols * rank, bytes_accessed=4 * rows * cols, transcendentals=0
        ),
        name="tall_partial",
    )(probes, sketch_t)


def prepare_kernel(first_ref, second_ref, both_ref, gram_ref):
    tall = first_ref[...] + second_ref[...]
    rank = tall.shape[0]
    head, rest = split(tall)
    tail = (tall - head.astype(F32) - rest.astype(F32)).astype(BF16)
    both_ref[...] = jnp.concatenate([head, rest], axis=0)
    three = jnp.concatenate([head, rest, tail], axis=0)
    g = dot(three, three, LAST)
    r = rank
    big = g[:r, :r]
    cross = g[:r, r : 2 * r] + g[r : 2 * r, :r]
    small = g[:r, 2 * r :] + g[2 * r :, :r] + g[r : 2 * r, r : 2 * r]
    gram = big + (cross + small)
    gram_ref[...] = jnp.concatenate([gram, jnp.zeros((r, LANES - r), F32)], axis=1)


def prepare(first, second):
    rank, rows = first.shape
    whole = pl.BlockSpec(memory_space=pltpu.VMEM)
    return pl.pallas_call(
        prepare_kernel,
        in_specs=[whole, whole],
        out_specs=[whole, whole],
        out_shape=[
            jax.ShapeDtypeStruct((2 * rank, rows), BF16),
            jax.ShapeDtypeStruct((rank, LANES), F32),
        ],
        compiler_params=PARAMS,
        cost_estimate=pl.CostEstimate(
            flops=rows * rank * rank * 18, bytes_accessed=24 * rank * rows, transcendentals=0
        ),
        name="prepare",
    )(first, second)


def block_kernel(has_gram, which_ref, both_ref, x_ref, *refs):
    out_ref = refs[-1]
    step = pl.program_id(0)
    rank = out_ref.shape[0]
    sub = x_ref.shape[1]
    both = both_ref[...]
    x_head, x_rest = split(x_ref[...])
    first = dot(both, x_head, PLAIN)
    second = dot(both[:rank], x_rest, PLAIN)
    where = pl.ds(pl.multiple_of(step * sub, sub), sub)
    out_ref[:, where] = first[:rank] + (first[rank:] + second)
    if has_gram:

        @pl.when(step == 0)
        def _():
            out_ref[:, out_ref.shape[1] - LANES :] = refs[0][...]


def block_product(which, both, probes, width, gram=None, after=None):
    rows = probes.shape[0]
    rank = both.shape[0] // 2
    sub = min(512, width)
    steps = width // sub
    in_specs = [
        pl.BlockSpec((2 * rank, rows), lambda i, w: (0, 0)),
        pl.BlockSpec((rows, sub), lambda i, w: (0, w[0] * steps + i)),
    ]
    args = [both, probes]
    out_width = width
    if gram is not None:
        in_specs.append(pl.BlockSpec((rank, LANES), lambda i, w: (0, 0)))
        args.append(gram)
        out_width += LANES
    if after is not None:
        in_specs.append(ANYWHERE)
        args.append(after)
    return pl.pallas_call(
        functools.partial(block_kernel, gram is not None),
        grid_spec=pltpu.PrefetchScalarGridSpec(
            num_scalar_prefetch=1,
            grid=(steps,),
            in_specs=in_specs,
            out_specs=pl.BlockSpec((rank, out_width), lambda i, w: (0, 0)),
        ),
        out_shape=jax.ShapeDtypeStruct((rank, out_width), F32),
        compiler_params=PARAMS,
        cost_estimate=pl.CostEstimate(
            flops=6 * rows * width * rank, bytes_accessed=4 * rows * width, transcendentals=0
        ),
        name="block_product",
    )(which, *args)


def inverse_kernel(gram_ref, out_ref):
    rank = out_ref.shape[0]
    rows = lax.broadcasted_iota(jnp.int32, (rank, LANES), 0)
    cols = lax.broadcasted_iota(jnp.int32, (rank, LANES), 1)
    work = jnp.where(cols < rank, gram_ref[...], (cols == rows + rank).astype(F32))
    for k in range(rank):
        pivot = work[k : k + 1, :]
        scale = 1.0 / jnp.sqrt(work[k : k + 1, k : k + 1])
        row = pivot * scale
        column = jnp.where(rows[:, :1] > k, work[:, k : k + 1] * scale, 0.0)
        work = jnp.where(rows == k, row, work - column * row)
    out_ref[...] = work[:, rank : 2 * rank]


def inverse_factor(chunk):
    rank, width = chunk.shape
    last = width // LANES - 1
    return pl.pallas_call(
        inverse_kernel,
        grid=(1,),
        in_specs=[pl.BlockSpec((rank, LANES), lambda i: (0, last))],
        out_specs=pl.BlockSpec((rank, rank), lambda i: (0, 0)),
        out_shape=jax.ShapeDtypeStruct((rank, rank), F32),
        compiler_params=PARAMS,
        cost_estimate=pl.CostEstimate(
            flops=20_000_000, bytes_accessed=8 * rank * LANES, transcendentals=rank
        ),
        name="inverse_factor",
    )(chunk)


def finish_kernel(count, where_ref, inverse_ref, *refs):
    parts, out_ref = refs[:count], refs[-1]
    step = pl.program_id(0)
    rank, width = out_ref.shape
    head, rest = split(inverse_ref[...])
    both = jnp.concatenate([head, rest], axis=0)
    for k in range(count):

        @pl.when(step == k)
        def _():
            p_head, p_rest = split(parts[k][:, :width])
            first = dot(both, p_head, PLAIN)
            out_ref[...] = first[:rank] + (first[rank:] + dot(head, p_rest, PLAIN))


def finish(where, inverse, parts, width, total, before=None):
    rank = inverse.shape[0]
    count = len(parts)
    in_specs = [pl.BlockSpec((rank, rank), lambda i, w: (0, 0))]
    in_specs += [pl.BlockSpec(part.shape, lambda i, w: (0, 0)) for part in parts]
    args = [inverse, *parts]
    aliases = {}
    if before is not None:
        in_specs.append(ANYWHERE)
        args.append(before)
        aliases = {len(args): 0}
    return pl.pallas_call(
        functools.partial(finish_kernel, count),
        grid_spec=pltpu.PrefetchScalarGridSpec(
            num_scalar_prefetch=1,
            grid=(count,),
            in_specs=in_specs,
            out_specs=pl.BlockSpec((rank, width), lambda i, w: (0, w[i])),
        ),
        out_shape=jax.ShapeDtypeStruct((rank, total), F32),
        input_output_aliases=aliases,
        compiler_params=PARAMS,
        cost_estimate=pl.CostEstimate(
            flops=6 * rank * rank * width * count,
            bytes_accessed=8 * rank * width * count,
            transcendentals=0,
        ),
        name="finish",
    )(where, *args)


def body(n_pos, n_pix, probes, sketch):
    def swap(value, axis, size, bit):
        return lax.ppermute(value, axis, [(i, i ^ bit) for i in range(size)])

    me = lax.axis_index("pos").astype(jnp.int32)
    side, outer = me % 2, me // 2
    n_outer = n_pos // 2
    cols = probes.shape[1]
    width = cols // 2 // CHUNKS

    def send_outer(value, pairs):
        return lax.ppermute(
            value, "pos", [(2 * a + s, 2 * b + s) for a, b in pairs for s in range(2)]
        )

    def outer_sum(value):
        if n_outer != 4:
            bit = 2
            while bit < n_pos:
                value = value + swap(value, "pos", n_pos, bit)
                bit *= 2
            return value
        value = value + send_outer(value, [(0, 1), (3, 2)])
        value = value + send_outer(value, [(1, 2), (2, 1)])
        back = send_outer(value, [(1, 0), (2, 3)])
        inner = (outer == 1) | (outer == 2)
        return jnp.where(inner, value, back)

    tall = tall_partial(probes, sketch.T)
    bit = 1
    while 2 * bit < n_pix:
        tall = tall + swap(tall, "pix", n_pix, bit)
        bit *= 2
    both, gram = prepare(tall, swap(tall, "pix", n_pix, bit))

    def product(half, i, after):
        which = (half * CHUNKS + i)[None]
        return block_product(which, both, probes, width, gram if i == 0 else None, after)

    received, sums = [], []
    for i in range(CHUNKS):
        away = product(1 - side, i, received[i - 2] if i >= 2 else None)
        received.append(swap(away, "pos", n_pos, 1))
    for i in range(CHUNKS):
        sums.append(outer_sum(product(side, i, None) + received[i]))

    inverse = inverse_factor(sums[0])
    sums[0] = sums[0][:, :width]
    others = [swap(part, "pos", n_pos, 1) for part in sums]

    slots = jnp.stack([side * CHUNKS, (1 - side) * CHUNKS])
    early = [i for i in range(CHUNKS - 1) for _ in range(2)]
    where = jnp.stack([slots[k % 2] + i for k, i in enumerate(early)])
    parts = [part for i in range(CHUNKS - 1) for part in (sums[i], others[i])]
    out = finish(where, inverse, parts, width, cols)
    return finish(slots + (CHUNKS - 1), inverse, [sums[-1], others[-1]], width, cols, out)


def solution(mesh):
    in_specs = (P("pos", "pix"), P("pix", None))
    out_specs = P(None, "pix")
    run = functools.partial(body, mesh.shape["pos"], mesh.shape["pix"])
    return jax.shard_map(run, mesh=mesh, in_specs=in_specs, out_specs=out_specs, check_vma=False)
```

time: 157 us -> 91.1 us (0.58)
  Pallas kernels: 75.7 us -> 35.8 us
  waiting for transfers between devices: 33 us -> 18.6 us
  other arithmetic: 10.1 us -> 0.54 us
    pallas_call x10 -> x12, Pallas kernels: 65.1 us -> 25.1 us  [the longest x8 14.8 us: block_product(): pl.pallas_call(functools.partial(block_kernel, gram is not None), grid_sp...]
    ppermute x24 -> x10, waiting for transfers between devices: 33 us -> 8.06 us  [swap(): return lax.ppermute(value, axis, [(i, i ^ bit) for i in range(size)])]
    ppermute x24 -> x10, starting transfers between devices: 34.9 us -> 13.4 us  [swap(): return lax.ppermute(value, axis, [(i, i ^ bit) for i in range(size)])]
    ppermute x0 -> x12, starting transfers between devices: none -> 20.3 us  [send_outer(): lax.ppermute(value, 'pos', [(2 * a + s, 2 * b + s) for a, b in pairs for...]
    ppermute x0 -> x12, waiting for transfers between devices: none -> 10.6 us  [send_outer(): lax.ppermute(value, 'pos', [(2 * a + s, 2 * b + s) for a, b in pairs for...]
    another operation x5 -> x0, other arithmetic: 9.5 us -> none  [the longest x3 5.13 us: body(): lower = jnp.linalg.cholesky(gram)]
  transfers between devices with their start and end apart: 24 -> 22, of which waited for: 8 -> 8; matrix products, arithmetic and copies ran while one was open for 7% -> 1% of each run, Pallas kernels for 10% -> 23%
where the time goes in v2:
time: 91.1 us; the launch traced here: 90.4 us
  Pallas kernels  35.8 us (39%)
  starting transfers between devices  33.7 us (37%)
  waiting for transfers between devices  18.6 us (20%)
  local copies, waits for them, and re-layouts  1.51 us (2%)
    ppermute x12, starting transfers between devices, send_outer(): lax.ppermute(value, 'pos', [(2 * a + s, 2 * b + s) for a, b in pairs for...  20.3 us
    pallas_call x8, Pallas kernels, block_product(): pl.pallas_call(functools.partial(block_kernel, gram is not None), grid_sp...  14.8 us
    ppermute x10, starting transfers between devices, swap(): return lax.ppermute(value, axis, [(i, i ^ bit) for i in range(size)])  13.4 us
    pallas_call x1, Pallas kernels, tall_partial(): pl.pallas_call(tall_kernel, grid=(cols // width,), in_specs=[pl.BlockSpec...  10.7 us
    ppermute x12, waiting for transfers between devices, send_outer(): lax.ppermute(value, 'pos', [(2 * a + s, 2 * b + s) for a, b in pairs for...  10.6 us
    ppermute x10, waiting for transfers between devices, swap(): return lax.ppermute(value, axis, [(i, i ^ bit) for i in range(size)])  8.06 us
    pallas_call x2, Pallas kernels, finish(): pl.pallas_call(functools.partial(finish_kernel, count), grid_spec=pltpu.P...  5.22 us
    pallas_call x1, Pallas kernels, inverse_factor(): pl.pallas_call(inverse_kernel, grid=(1,), in_specs=[pl.BlockSpec((rank, L...  4.7 us
  transfers between devices with their start and end apart: 22, of which 8 were waited for; matrix products, arithmetic and copies ran while one was open for 1% of the time, Pallas kernels for 23%

profile of v2, /device:TPU:0, one launch (start us, length us, event | category | flops | bytes accessed | tf_op | source)
XLA Modules:
  0.0 90.4 jit_solution(14710266425639581616)
XLA Ops:
  1.4 10.7 %tall_partial.1 = f32[48,512]{1,0:T(8,128)S(1)} custom-call(f32[512,8192]{1,0:T(8,128)} %x_ref.17, f32[48,8192]{1,0:T(8,128)S(1)} %bitcast.9), custom_call_target="tpu_custom_call" | custom-call | flops 1207959552 | bytes 16777216 | tf_op jit(solution)/shard_map/tall_partial/pallas_call | solution.py:53
  13.6 2.9 %collective-permute-start.1 = (f32[48,512]{1,0:T(8,128)S(1)}, f32[48,512]{1,0:T(8,128)S(1)}, u32[]{:S(2)}, u32[]{:S(2)}) collective-permute-start(f32[48,512]{1,0:T(8,128)S(1)} %add.71.first_ref), channel_id=1, source_target_pairs={{0,2},{1,3},{2,0},{3,1},{4,6},{5,7},{6,4},{7,5},{8,10},{9,11},{10,... | collective-permute-start | bytes 294920 | tf_op jit(solution)/shard_map/ppermute | solution.py:238
  16.5 3.1 %collective-permute-done.1.second_ref = f32[48,512]{1,0:T(8,128)S(1)} collective-permute-done((f32[48,512]{1,0:T(8,128)S(1)}, f32[48,512]{1,0:T(8,128)S(1)}, u32[]{:S(2)}, u32[]{:S(2)}) %collective-permute-start.1) | collective-permute-done | bytes 98336 | tf_op jit(solution)/shard_map/ppermute | solution.py:238
  20.1 1.9 %block_product.11 = f32[48,1024]{1,0:T(8,128)S(1)} custom-call(s32[1]{0:T(128)} %bitcast.5.which_ref, bf16[96,512]{1,0:T(8,128)(2,1)S(1)} %get-tuple-element.7.both_ref, f32[512,8192]{1,0:T(8,128)} %x_ref.17), custom_call_target="tpu_custom_call" | custom-call | flops 150994944 | bytes 2097152 | tf_op jit(solution)/shard_map/block_product/pallas_call | solution.py:142
  21.9 1.8 %collective-permute-start.6 = (f32[48,1024]{1,0:T(8,128)S(1)}, f32[48,1024]{1,0:T(8,128)S(1)}, u32[]{:S(2)}, u32[]{:S(2)}) collective-permute-start(f32[48,1024]{1,0:T(8,128)S(1)} %block_product.11), channel_id=1, source_target_pairs={{0,4},{4,0},{8,12},{12,8},{16,20},{20,16},{24,28},{28,24},{1,5},{5... | collective-permute-start | bytes 589832 | tf_op jit(solution)/shard_map/ppermute | solution.py:238
  23.7 1.8 %block_product.9 = f32[48,1152]{1,0:T(8,128)S(1)} custom-call(s32[1]{0:T(128)} %bitcast.1.which_ref, bf16[96,512]{1,0:T(8,128)(2,1)S(1)} %get-tuple-element.7.both_ref, f32[512,8192]{1,0:T(8,128)} %x_ref.17, f32[48,128]{1,0:T(8,128)S(1)} %get-tuple-element.8.refs_0_), custom_call_target="tpu_custom_call" | custom-call | flops 150994944 | bytes 2097152 | tf_op jit(solution)/shard_map/block_product/pallas_call | solution.py:142
  25.9 3.7 %collective-permute-done.6.refs_0_ = f32[48,1024]{1,0:T(8,128)S(1)} collective-permute-done((f32[48,1024]{1,0:T(8,128)S(1)}, f32[48,1024]{1,0:T(8,128)S(1)}, u32[]{:S(2)}, u32[]{:S(2)}) %collective-permute-start.6) | collective-permute-done | bytes 196640 | tf_op jit(solution)/shard_map/ppermute | solution.py:238
  29.6 1.8 %block_product.12 = f32[48,1024]{1,0:T(8,128)S(1)} custom-call(s32[1]{0:T(128)} %bitcast.4.which_ref, bf16[96,512]{1,0:T(8,128)(2,1)S(1)} %get-tuple-element.7.both_ref, f32[512,8192]{1,0:T(8,128)} %x_ref.17, f32[48,1024]{1,0:T(8,128)S(1)} %collective-permute-done.6.refs_0_), custom_call_target="tpu_custom_call" | custom-call | flops 150994944 | bytes 2097152 | tf_op jit(solution)/shard_map/block_product/pallas_call | solution.py:142
  31.4 2.0 %collective-permute-start.7 = (f32[48,1024]{1,0:T(8,128)S(1)}, f32[48,1024]{1,0:T(8,128)S(1)}, u32[]{:S(2)}, u32[]{:S(2)}) collective-permute-start(f32[48,1024]{1,0:T(8,128)S(1)} %block_product.12), channel_id=1, source_target_pairs={{0,4},{4,0},{8,12},{12,8},{16,20},{20,16},{24,28},{28,24},{1,5},{5... | collective-permute-start | bytes 589832 | tf_op jit(solution)/shard_map/ppermute | solution.py:238
  33.4 1.8 %block_product.13 = f32[48,1024]{1,0:T(8,128)S(1)} custom-call(s32[1]{0:T(128)} %bitcast.6.which_ref, bf16[96,512]{1,0:T(8,128)(2,1)S(1)} %get-tuple-element.7.both_ref, f32[512,8192]{1,0:T(8,128)} %x_ref.17), custom_call_target="tpu_custom_call" | custom-call | flops 150994944 | bytes 2097152 | tf_op jit(solution)/shard_map/block_product/pallas_call | solution.py:142
  35.3 3.5 %collective-permute-start.13 = (f32[48,1024]{1,0:T(8,128)S(1)}, f32[48,1024]{1,0:T(8,128)S(1)}, u32[]{:S(2)}, u32[]{:S(2)}) collective-permute-start(f32[48,1024]{1,0:T(8,128)S(1)} %add.84), channel_id=1, source_target_pairs={{0,8},{4,12},{24,16},{28,20},{1,9},{5,13},{25,17},{29,21},{2,10},{... | collective-permute-start | bytes 589832 | tf_op jit(solution)/shard_map/ppermute | solution.py:247
  38.8 1.9 %block_product.8 = f32[48,1152]{1,0:T(8,128)S(1)} custom-call(s32[1]{0:T(128)} %bitcast.which_ref, bf16[96,512]{1,0:T(8,128)(2,1)S(1)} %get-tuple-element.7.both_ref, f32[512,8192]{1,0:T(8,128)} %x_ref.17, f32[48,128]{1,0:T(8,128)S(1)} %get-tuple-element.8.refs_0_), custom_call_target="tpu_custom_call" | custom-call | flops 150994944 | bytes 2097152 | tf_op jit(solution)/shard_map/block_product/pallas_call | solution.py:142
  42.0 1.9 %block_product.15 = f32[48,1024]{1,0:T(8,128)S(1)} custom-call(s32[1]{0:T(128)} %bitcast.8.which_ref, bf16[96,512]{1,0:T(8,128)(2,1)S(1)} %get-tuple-element.7.both_ref, f32[512,8192]{1,0:T(8,128)} %x_ref.17, f32[48,1152]{1,0:T(8,128)S(1)} %collective-permute-done.2.refs_0_), custom_call_target="tpu_custom_call" | custom-call | flops 150994944 | bytes 2097152 | tf_op jit(solution)/shard_map/block_product/pallas_call | solution.py:142
  43.9 1.8 %block_product.10 = f32[48,1024]{1,0:T(8,128)S(1)} custom-call(s32[1]{0:T(128)} %bitcast.3.which_ref, bf16[96,512]{1,0:T(8,128)(2,1)S(1)} %get-tuple-element.7.both_ref, f32[512,8192]{1,0:T(8,128)} %x_ref.17), custom_call_target="tpu_custom_call" | custom-call | flops 150994944 | bytes 2097152 | tf_op jit(solution)/shard_map/block_product/pallas_call | solution.py:142
  48.6 1.9 %block_product.14 = f32[48,1024]{1,0:T(8,128)S(1)} custom-call(s32[1]{0:T(128)} %bitcast.7.which_ref, bf16[96,512]{1,0:T(8,128)(2,1)S(1)} %get-tuple-element.7.both_ref, f32[512,8192]{1,0:T(8,128)} %x_ref.17), custom_call_target="tpu_custom_call" | custom-call | flops 150994944 | bytes 2097152 | tf_op jit(solution)/shard_map/block_product/pallas_call | solution.py:142
  50.5 6.3 %collective-permute-start.18 = (f32[48,1024]{1,0:T(8,128)S(1)}, f32[48,1024]{1,0:T(8,128)S(1)}, u32[]{:S(2)}, u32[]{:S(2)}) collective-permute-start(f32[48,1024]{1,0:T(8,128)S(1)} %add.87), channel_id=1, source_target_pairs={{0,8},{4,12},{24,16},{28,20},{1,9},{5,13},{25,17},{29,21},{2,10},{... | collective-permute-start | bytes 589832 | tf_op jit(solution)/shard_map/ppermute | solution.py:247
  63.4 3.8 %collective-permute-done.15 = f32[48,1024]{1,0:T(8,128)S(1)} collective-permute-done((f32[48,1024]{1,0:T(8,128)S(1)}, f32[48,1024]{1,0:T(8,128)S(1)}, u32[]{:S(2)}, u32[]{:S(2)}) %collective-permute-start.15) | collective-permute-done | bytes 196640 | tf_op jit(solution)/shard_map/ppermute | solution.py:247
  70.0 3.1 %collective-permute-done.5 = f32[48,1152]{1,0:T(8,128)S(1)} collective-permute-done((f32[48,1152]{1,0:T(8,128)S(1)}, f32[48,1152]{1,0:T(8,128)S(1)}, u32[]{:S(2)}, u32[]{:S(2)}) %collective-permute-start.5) | collective-permute-done | bytes 221216 | tf_op jit(solution)/shard_map/ppermute | solution.py:247
  73.1 2.1 %collective-permute-start.12 = (f32[48,1024]{1,0:T(8,128)S(1)}, f32[48,1024]{1,0:T(8,128)S(1)}, u32[]{:S(2)}, u32[]{:S(2)}) collective-permute-start(f32[48,1024]{1,0:T(8,128)S(1)} %slice.4.refs_0_), channel_id=1, source_target_pairs={{0,4},{4,0},{8,12},{12,8},{16,20},{20,16},{24,28},{28,24},{1,5},{5... | collective-permute-start | bytes 589832 | tf_op jit(solution)/shard_map/ppermute | solution.py:238
  75.2 2.6 %collective-permute-done.20 = f32[48,1024]{1,0:T(8,128)S(1)} collective-permute-done((f32[48,1024]{1,0:T(8,128)S(1)}, f32[48,1024]{1,0:T(8,128)S(1)}, u32[]{:S(2)}, u32[]{:S(2)}) %collective-permute-start.20) | collective-permute-done | bytes 196640 | tf_op jit(solution)/shard_map/ppermute | solution.py:247
  77.8 1.6 %collective-permute-start.21 = (f32[48,1024]{1,0:T(8,128)S(1)}, f32[48,1024]{1,0:T(8,128)S(1)}, u32[]{:S(2)}, u32[]{:S(2)}) collective-permute-start(f32[48,1024]{1,0:T(8,128)S(1)} %broadcast_select_fusion.1.refs_4_), channel_id=1, source_target_pairs={{0,4},{4,0},{8,12},{12,8},{16,20},{20,16},{24,28},{28,24},{1,5},{5... | collective-permute-start | bytes 589832 | tf_op jit(solution)/shard_map/ppermute | solution.py:238
  80.2 4.7 %inverse_factor.1.inverse_ref = f32[48,48]{1,0:T(8,128)S(1)} custom-call(f32[48,1152]{1,0:T(8,128)S(1)} %broadcast_select_fusion.gram_ref), custom_call_target="tpu_custom_call" | custom-call | flops 20000000 | bytes 49152 | tf_op jit(solution)/shard_map/inverse_factor/pallas_call | solution.py:176
  85.2 3.5 %finish.2.refs_2_ = f32[48,8192]{1,0:T(8,128)} custom-call(s32[6]{0:T(128)S(1)} %stack.28.where_ref, f32[48,48]{1,0:T(8,128)S(1)} %inverse_factor.1.inverse_ref, f32[48,1024]{1,0:T(8,128)S(1)} %slice.4.refs_0_, f32[48,1024]{1,0:T(8,128)S(1)} %collective-permute-done.12.refs_1_, f32[48,1024]{1,0:T(8,128)S(1)} %broadcast_select_fusion.2.refs_2_, ...), custom_call_target="tpu_custom_call" | custom-call | flops 84934656 | bytes 2359296 | tf_op jit(solution)/shard_map/finish/pallas_call | solution.py:216
  88.7 1.7 %finish.3 = f32[48,8192]{1,0:T(8,128)} custom-call(s32[2]{0:T(128)S(1)} %add_add_fusion.where_ref, f32[48,48]{1,0:T(8,128)S(1)} %inverse_factor.1.inverse_ref, f32[48,1024]{1,0:T(8,128)S(1)} %broadcast_select_fusion.3.refs_0_, f32[48,1024]{1,0:T(8,128)S(1)} %collective-permute-done.11.refs_1_, f32[48,8192]{1,0:T(8,128)} %finish.2.refs_2_), custom_call_target="tpu_custom_call", output_to_operand_aliasing={{}: (4, {})} | custom-call | flops 28311552 | bytes 786432 | tf_op jit(solution)/shard_map/finish/pallas_call | solution.py:216
  (55 shorter events, 18.3 us)
Async XLA Ops:
  0.0 1.4 %copy-start = (f32[8192,48]{0,1:T(8,128)S(1)}, f32[8192,48]{0,1:T(8,128)}, u32[]{:S(2)}) copy-start(f32[8192,48]{0,1:T(8,128)} %param.3) | copy-start | bytes 4718596
  12.1 1.5 %collective-permute-start = (f32[48,512]{1,0:T(8,128)S(1)}, f32[48,512]{1,0:T(8,128)S(1)}, u32[]{:S(2)}, u32[]{:S(2)}) collective-permute-start(f32[48,512]{1,0:T(8,128)S(1)} %tall_partial.1), channel_id=1, source_target_pairs={{0,1},{1,0},{2,3},{3,2},{4,5},{5,4},{6,7},{7,6},{8,9},{9,8},{10,11... | collective-permute-start | bytes 294920 | tf_op jit(solution)/shard_map/ppermute | solution.py:238
  13.6 6.1 %collective-permute-start.1 = (f32[48,512]{1,0:T(8,128)S(1)}, f32[48,512]{1,0:T(8,128)S(1)}, u32[]{:S(2)}, u32[]{:S(2)}) collective-permute-start(f32[48,512]{1,0:T(8,128)S(1)} %add.71.first_ref), channel_id=1, source_target_pairs={{0,2},{1,3},{2,0},{3,1},{4,6},{5,7},{6,4},{7,5},{8,10},{9,11},{10,... | collective-permute-start | bytes 294920 | tf_op jit(solution)/shard_map/ppermute | solution.py:238
  21.9 7.6 %collective-permute-start.6 = (f32[48,1024]{1,0:T(8,128)S(1)}, f32[48,1024]{1,0:T(8,128)S(1)}, u32[]{:S(2)}, u32[]{:S(2)}) collective-permute-start(f32[48,1024]{1,0:T(8,128)S(1)} %block_product.11), channel_id=1, source_target_pairs={{0,4},{4,0},{8,12},{12,8},{16,20},{20,16},{24,28},{28,24},{1,5},{5... | collective-permute-start | bytes 589832 | tf_op jit(solution)/shard_map/ppermute | solution.py:238
  25.5 15.1 %collective-permute-start.2 = (f32[48,1152]{1,0:T(8,128)S(1)}, f32[48,1152]{1,0:T(8,128)S(1)}, u32[]{:S(2)}, u32[]{:S(2)}) collective-permute-start(f32[48,1152]{1,0:T(8,128)S(1)} %block_product.9), channel_id=1, source_target_pairs={{0,4},{4,0},{8,12},{12,8},{16,20},{20,16},{24,28},{28,24},{1,5},{5... | collective-permute-start | bytes 663560 | tf_op jit(solution)/shard_map/ppermute | solution.py:238
  31.4 14.4 %collective-permute-start.7 = (f32[48,1024]{1,0:T(8,128)S(1)}, f32[48,1024]{1,0:T(8,128)S(1)}, u32[]{:S(2)}, u32[]{:S(2)}) collective-permute-start(f32[48,1024]{1,0:T(8,128)S(1)} %block_product.12), channel_id=1, source_target_pairs={{0,4},{4,0},{8,12},{12,8},{16,20},{20,16},{24,28},{28,24},{1,5},{5... | collective-permute-start | bytes 589832 | tf_op jit(solution)/shard_map/ppermute | solution.py:238
  35.3 11.9 %collective-permute-start.13 = (f32[48,1024]{1,0:T(8,128)S(1)}, f32[48,1024]{1,0:T(8,128)S(1)}, u32[]{:S(2)}, u32[]{:S(2)}) collective-permute-start(f32[48,1024]{1,0:T(8,128)S(1)} %add.84), channel_id=1, source_target_pairs={{0,8},{4,12},{24,16},{28,20},{1,9},{5,13},{25,17},{29,21},{2,10},{... | collective-permute-start | bytes 589832 | tf_op jit(solution)/shard_map/ppermute | solution.py:247
  40.7 7.2 %collective-permute-start.3 = (f32[48,1152]{1,0:T(8,128)S(1)}, f32[48,1152]{1,0:T(8,128)S(1)}, u32[]{:S(2)}, u32[]{:S(2)}) collective-permute-start(f32[48,1152]{1,0:T(8,128)S(1)} %add.72), channel_id=1, source_target_pairs={{0,8},{4,12},{24,16},{28,20},{1,9},{5,13},{25,17},{29,21},{2,10},{... | collective-permute-start | bytes 663560 | tf_op jit(solution)/shard_map/ppermute | solution.py:247
  43.9 6.6 %collective-permute-start.17 = (f32[48,1024]{1,0:T(8,128)S(1)}, f32[48,1024]{1,0:T(8,128)S(1)}, u32[]{:S(2)}, u32[]{:S(2)}) collective-permute-start(f32[48,1024]{1,0:T(8,128)S(1)} %block_product.15), channel_id=1, source_target_pairs={{0,4},{4,0},{8,12},{12,8},{16,20},{20,16},{24,28},{28,24},{1,5},{5... | collective-permute-start | bytes 589832 | tf_op jit(solution)/shard_map/ppermute | solution.py:238
  45.8 11.0 %collective-permute-start.8 = (f32[48,1024]{1,0:T(8,128)S(1)}, f32[48,1024]{1,0:T(8,128)S(1)}, u32[]{:S(2)}, u32[]{:S(2)}) collective-permute-start(f32[48,1024]{1,0:T(8,128)S(1)} %add.78), channel_id=1, source_target_pairs={{0,8},{4,12},{24,16},{28,20},{1,9},{5,13},{25,17},{29,21},{2,10},{... | collective-permute-start | bytes 589832 | tf_op jit(solution)/shard_map/ppermute | solution.py:247
  47.2 10.4 %collective-permute-start.14 = (f32[48,1024]{1,0:T(8,128)S(1)}, f32[48,1024]{1,0:T(8,128)S(1)}, u32[]{:S(2)}, u32[]{:S(2)}) collective-permute-start(f32[48,1024]{1,0:T(8,128)S(1)} %add.85), channel_id=1, source_target_pairs={{8,16},{12,20},{16,8},{20,12},{9,17},{13,21},{17,9},{21,13},{10,18... | collective-permute-start | bytes 589832 | tf_op jit(solution)/shard_map/ppermute | solution.py:247
  47.9 12.8 %collective-permute-start.4 = (f32[48,1152]{1,0:T(8,128)S(1)}, f32[48,1152]{1,0:T(8,128)S(1)}, u32[]{:S(2)}, u32[]{:S(2)}) collective-permute-start(f32[48,1152]{1,0:T(8,128)S(1)} %add.73), channel_id=1, source_target_pairs={{8,16},{12,20},{16,8},{20,12},{9,17},{13,21},{17,9},{21,13},{10,18... | collective-permute-start | bytes 663560 | tf_op jit(solution)/shard_map/ppermute | solution.py:247
  50.5 9.5 %collective-permute-start.18 = (f32[48,1024]{1,0:T(8,128)S(1)}, f32[48,1024]{1,0:T(8,128)S(1)}, u32[]{:S(2)}, u32[]{:S(2)}) collective-permute-start(f32[48,1024]{1,0:T(8,128)S(1)} %add.87), channel_id=1, source_target_pairs={{0,8},{4,12},{24,16},{28,20},{1,9},{5,13},{25,17},{29,21},{2,10},{... | collective-permute-start | bytes 589832 | tf_op jit(solution)/shard_map/ppermute | solution.py:247
  56.9 5.2 %collective-permute-start.9 = (f32[48,1024]{1,0:T(8,128)S(1)}, f32[48,1024]{1,0:T(8,128)S(1)}, u32[]{:S(2)}, u32[]{:S(2)}) collective-permute-start(f32[48,1024]{1,0:T(8,128)S(1)} %add.79), channel_id=1, source_target_pairs={{8,16},{12,20},{16,8},{20,12},{9,17},{13,21},{17,9},{21,13},{10,18... | collective-permute-start | bytes 589832 | tf_op jit(solution)/shard_map/ppermute | solution.py:247
  57.6 9.6 %collective-permute-start.15 = (f32[48,1024]{1,0:T(8,128)S(1)}, f32[48,1024]{1,0:T(8,128)S(1)}, u32[]{:S(2)}, u32[]{:S(2)}) collective-permute-start(f32[48,1024]{1,0:T(8,128)S(1)} %add.86), channel_id=1, source_target_pairs={{8,0},{12,4},{16,24},{20,28},{9,1},{13,5},{17,25},{21,29},{10,2},{... | collective-permute-start | bytes 589832 | tf_op jit(solution)/shard_map/ppermute | solution.py:247
  60.0 8.7 %collective-permute-start.19 = (f32[48,1024]{1,0:T(8,128)S(1)}, f32[48,1024]{1,0:T(8,128)S(1)}, u32[]{:S(2)}, u32[]{:S(2)}) collective-permute-start(f32[48,1024]{1,0:T(8,128)S(1)} %add.88), channel_id=1, source_target_pairs={{8,16},{12,20},{16,8},{20,12},{9,17},{13,21},{17,9},{21,13},{10,18... | collective-permute-start | bytes 589832 | tf_op jit(solution)/shard_map/ppermute | solution.py:247
  60.8 12.3 %collective-permute-start.5 = (f32[48,1152]{1,0:T(8,128)S(1)}, f32[48,1152]{1,0:T(8,128)S(1)}, u32[]{:S(2)}, u32[]{:S(2)}) collective-permute-start(f32[48,1152]{1,0:T(8,128)S(1)} %add.74), channel_id=1, source_target_pairs={{8,0},{12,4},{16,24},{20,28},{9,1},{13,5},{17,25},{21,29},{10,2},{... | collective-permute-start | bytes 663560 | tf_op jit(solution)/shard_map/ppermute | solution.py:247
  62.1 17.3 %collective-permute-start.10 = (f32[48,1024]{1,0:T(8,128)S(1)}, f32[48,1024]{1,0:T(8,128)S(1)}, u32[]{:S(2)}, u32[]{:S(2)}) collective-permute-start(f32[48,1024]{1,0:T(8,128)S(1)} %add.80), channel_id=1, source_target_pairs={{8,0},{12,4},{16,24},{20,28},{9,1},{13,5},{17,25},{21,29},{10,2},{... | collective-permute-start | bytes 589832 | tf_op jit(solution)/shard_map/ppermute | solution.py:247
  67.2 17.7 %collective-permute-start.16 = (f32[48,1024]{1,0:T(8,128)S(1)}, f32[48,1024]{1,0:T(8,128)S(1)}, u32[]{:S(2)}, u32[]{:S(2)}) collective-permute-start(f32[48,1024]{1,0:T(8,128)S(1)} %broadcast_select_fusion.2.refs_2_), channel_id=1, source_target_pairs={{0,4},{4,0},{8,12},{12,8},{16,20},{20,16},{24,28},{28,24},{1,5},{5... | collective-permute-start | bytes 589832 | tf_op jit(solution)/shard_map/ppermute | solution.py:238
  68.7 9.1 %collective-permute-start.20 = (f32[48,1024]{1,0:T(8,128)S(1)}, f32[48,1024]{1,0:T(8,128)S(1)}, u32[]{:S(2)}, u32[]{:S(2)}) collective-permute-start(f32[48,1024]{1,0:T(8,128)S(1)} %add.89), channel_id=1, source_target_pairs={{8,0},{12,4},{16,24},{20,28},{9,1},{13,5},{17,25},{21,29},{10,2},{... | collective-permute-start | bytes 589832 | tf_op jit(solution)/shard_map/ppermute | solution.py:247
  73.1 11.8 %collective-permute-start.12 = (f32[48,1024]{1,0:T(8,128)S(1)}, f32[48,1024]{1,0:T(8,128)S(1)}, u32[]{:S(2)}, u32[]{:S(2)}) collective-permute-start(f32[48,1024]{1,0:T(8,128)S(1)} %slice.4.refs_0_), channel_id=1, source_target_pairs={{0,4},{4,0},{8,12},{12,8},{16,20},{20,16},{24,28},{28,24},{1,5},{5... | collective-permute-start | bytes 589832 | tf_op jit(solution)/shard_map/ppermute | solution.py:238
  77.8 7.4 %collective-permute-start.21 = (f32[48,1024]{1,0:T(8,128)S(1)}, f32[48,1024]{1,0:T(8,128)S(1)}, u32[]{:S(2)}, u32[]{:S(2)}) collective-permute-start(f32[48,1024]{1,0:T(8,128)S(1)} %broadcast_select_fusion.1.refs_4_), channel_id=1, source_target_pairs={{0,4},{4,0},{8,12},{12,8},{16,20},{20,16},{24,28},{28,24},{1,5},{5... | collective-permute-start | bytes 589832 | tf_op jit(solution)/shard_map/ppermute | solution.py:238
  79.4 9.3 %collective-permute-start.11 = (f32[48,1024]{1,0:T(8,128)S(1)}, f32[48,1024]{1,0:T(8,128)S(1)}, u32[]{:S(2)}, u32[]{:S(2)}) collective-permute-start(f32[48,1024]{1,0:T(8,128)S(1)} %broadcast_select_fusion.3.refs_0_), channel_id=1, source_target_pairs={{0,4},{4,0},{8,12},{12,8},{16,20},{20,16},{24,28},{28,24},{1,5},{5... | collective-permute-start | bytes 589832 | tf_op jit(solution)/shard_map/ppermute | solution.py:238

commit v3 on v2

v3 whole, which is shorter than its diff:
```python
import functools

import jax
import jax.numpy as jnp
from jax import lax
from jax.experimental import pallas as pl
from jax.experimental.pallas import tpu as pltpu
from jax.sharding import PartitionSpec as P

F32 = jnp.float32
BF16 = jnp.bfloat16
VMEM_LIMIT = 40 * 1024 * 1024
LANES = 128
CHUNKS = 1
STREAMS = 4
PANEL = 4
LAST = (((1,), (1,)), ((), ()))
PLAIN = (((1,), (0,)), ((), ()))
ANYWHERE = pl.BlockSpec(memory_space=pl.ANY)
PARAMS = pltpu.CompilerParams(vmem_limit_bytes=VMEM_LIMIT)


def split(x):
    head = x.astype(BF16)
    return head, (x - head.astype(F32)).astype(BF16)


def dot(a, b, dims):
    return lax.dot_general(a, b, dims, preferred_element_type=F32)


def row_blocks(rows):
    return STREAMS if rows % (16 * STREAMS) == 0 else 1


def tall_kernel(s_ref, *refs):
    x_refs, (out_ref, acc_ref) = refs[:-2], refs[-2:]
    step = pl.program_id(0)
    rank = s_ref.shape[0]

    @pl.when(step == 0)
    def _():
        acc_ref[...] = jnp.zeros_like(acc_ref)

    s_head, s_rest = split(s_ref[...])
    s_both = jnp.concatenate([s_head, s_rest], axis=0)
    x_head, x_rest = split(jnp.concatenate([ref[...] for ref in x_refs], axis=0))
    both = dot(s_both, x_head, LAST)
    acc_ref[...] += both[:rank] + (both[rank:] + dot(s_head, x_rest, LAST))

    @pl.when(step == pl.num_programs(0) - 1)
    def _():
        out_ref[...] = acc_ref[...]


def tall_partial(probes, sketch_t):
    rows, cols = probes.shape
    rank = sketch_t.shape[0]
    width = min(1024, cols)
    streams = row_blocks(rows)
    sketch_t = pltpu.with_memory_space_constraint(sketch_t, pltpu.MemorySpace.HBM)
    x_specs = [
        pl.BlockSpec((rows // streams, width), lambda i, q=q: (q, i)) for q in range(streams)
    ]
    return pl.pallas_call(
        tall_kernel,
        grid=(cols // width,),
        in_specs=[pl.BlockSpec((rank, width), lambda i: (0, i)), *x_specs],
        out_specs=pl.BlockSpec((rank, rows), lambda i: (0, 0)),
        out_shape=jax.ShapeDtypeStruct((rank, rows), F32),
        scratch_shapes=[pltpu.VMEM((rank, rows), F32)],
        compiler_params=PARAMS,
        cost_estimate=pl.CostEstimate(
            flops=6 * rows * cols * rank, bytes_accessed=4 * rows * cols, transcendentals=0
        ),
        name="tall_partial",
    )(sketch_t, *[probes] * streams)


def prepare_kernel(first_ref, second_ref, both_ref, gram_ref):
    tall = first_ref[...] + second_ref[...]
    rank = tall.shape[0]
    head, rest = split(tall)
    tail = (tall - head.astype(F32) - rest.astype(F32)).astype(BF16)
    both_ref[...] = jnp.concatenate([head, rest], axis=0)
    three = jnp.concatenate([head, rest, tail], axis=0)
    g = dot(three, three, LAST)
    r = rank
    big = g[:r, :r]
    cross = g[:r, r : 2 * r] + g[r : 2 * r, :r]
    small = g[:r, 2 * r :] + g[2 * r :, :r] + g[r : 2 * r, r : 2 * r]
    gram = big + (cross + small)
    gram_ref[...] = jnp.concatenate([gram, jnp.zeros((r, LANES - r), F32)], axis=1)


def prepare(first, second):
    rank, rows = first.shape
    whole = pl.BlockSpec(memory_space=pltpu.VMEM)
    return pl.pallas_call(
        prepare_kernel,
        in_specs=[whole, whole],
        out_specs=[whole, whole],
        out_shape=[
            jax.ShapeDtypeStruct((2 * rank, rows), BF16),
            jax.ShapeDtypeStruct((rank, LANES), F32),
        ],
        compiler_params=PARAMS,
        cost_estimate=pl.CostEstimate(
            flops=rows * rank * rank * 18, bytes_accessed=24 * rank * rows, transcendentals=0
        ),
        name="prepare",
    )(first, second)


def product_kernel(streams, plan, grams, which_ref, both_ref, gram_ref, *refs):
    count = 1 + max(out for out, _ in plan)
    x_refs, outs = refs[:streams], refs[len(refs) - count :]
    step = pl.program_id(0)
    rank = outs[0].shape[0]
    sub = x_refs[0].shape[1]
    both = both_ref[...]
    x_head, x_rest = split(jnp.concatenate([ref[...] for ref in x_refs], axis=0))
    first = dot(both, x_head, PLAIN)
    second = dot(both[:rank], x_rest, PLAIN)
    result = first[:rank] + (first[rank:] + second)
    for k, (out, offset) in enumerate(plan):

        @pl.when(step == k)
        def _():
            outs[out][:, offset : offset + sub] = result

    @pl.when(step == 0)
    def _():
        for out, offset in grams:
            outs[out][:, offset : offset + LANES] = gram_ref[...]


def products(both, gram, probes, sub, outputs, after=()):
    rows = probes.shape[0]
    rank = both.shape[0] // 2
    streams = row_blocks(rows)
    plan, grams, widths, which = [], [], [], []
    for out, (blocks, with_gram) in enumerate(outputs):
        extra = LANES if with_gram else 0
        for j, block in enumerate(blocks):
            plan.append((out, j * sub + (extra if j else 0)))
            which.append(block)
        if with_gram:
            grams.append((out, sub))
        widths.append(len(blocks) * sub + extra)
    x_specs = [
        pl.BlockSpec((rows // streams, sub), lambda i, w, q=q: (q, w[i])) for q in range(streams)
    ]
    return pl.pallas_call(
        functools.partial(product_kernel, streams, plan, grams),
        grid_spec=pltpu.PrefetchScalarGridSpec(
            num_scalar_prefetch=1,
            grid=(len(plan),),
            in_specs=[
                pl.BlockSpec((2 * rank, rows), lambda i, w: (0, 0)),
                pl.BlockSpec((rank, LANES), lambda i, w: (0, 0)),
                *x_specs,
                *[ANYWHERE] * len(after),
            ],
            out_specs=[pl.BlockSpec((rank, width), lambda i, w: (0, 0)) for width in widths],
        ),
        out_shape=[jax.ShapeDtypeStruct((rank, width), F32) for width in widths],
        compiler_params=PARAMS,
        cost_estimate=pl.CostEstimate(
            flops=6 * rows * rank * sub * len(plan),
            bytes_accessed=4 * rows * sub * len(plan),
            transcendentals=0,
        ),
        name="products",
    )(jnp.stack(which), both, gram, *[probes] * streams, *after)


def inverse_kernel(gram_ref, out_ref):
    rank = out_ref.shape[0]
    rows = lax.broadcasted_iota(jnp.int32, (rank, LANES), 0)
    cols = lax.broadcasted_iota(jnp.int32, (rank, LANES), 1)
    work = jnp.where(cols < rank, gram_ref[...], (cols == rows + rank).astype(F32))
    scale = jnp.ones((rank, LANES), F32)
    for start in range(0, rank, PANEL):
        panel = [
            jnp.broadcast_to(work[:, k : k + 1], (rank, LANES))
            for k in range(start, start + PANEL)
        ]
        for j in range(PANEL):
            k = start + j
            over = 1.0 / panel[j][k : k + 1, :]
            scale = jnp.where(rows == k, over, scale)
            factor = jnp.where(rows > k, panel[j] * over, 0.0)
            work = work - factor * work[k : k + 1, :]
            for later in range(j + 1, PANEL):
                panel[later] = panel[later] - factor * panel[later][k : k + 1, :]
    out_ref[...] = (work * jnp.sqrt(scale))[:, rank : 2 * rank]


def inverse_factor(chunk, start):
    rank = chunk.shape[0]
    return pl.pallas_call(
        inverse_kernel,
        grid=(1,),
        in_specs=[pl.BlockSpec((rank, LANES), lambda i: (0, start // LANES))],
        out_specs=pl.BlockSpec((rank, rank), lambda i: (0, 0)),
        out_shape=jax.ShapeDtypeStruct((rank, rank), F32),
        compiler_params=PARAMS,
        cost_estimate=pl.CostEstimate(
            flops=20_000_000, bytes_accessed=8 * rank * LANES, transcendentals=rank
        ),
        name="inverse_factor",
    )(chunk)


def finish_kernel(plan, where_ref, inverse_ref, *refs):
    out_ref = refs[-1]
    step = pl.program_id(0)
    rank, width = out_ref.shape
    head, rest = split(inverse_ref[...])
    both = jnp.concatenate([head, rest], axis=0)
    for k, (source, offset) in enumerate(plan):

        @pl.when(step == k)
        def _():
            p_head, p_rest = split(refs[source][:, offset : offset + width])
            first = dot(both, p_head, PLAIN)
            out_ref[...] = first[:rank] + (first[rank:] + dot(head, p_rest, PLAIN))


def finish(inverse, sources, pieces, width, total, before=None):
    rank = inverse.shape[0]
    count = len(pieces)
    in_specs = [pl.BlockSpec((rank, rank), lambda i, w: (0, 0))]
    in_specs += [pl.BlockSpec(source.shape, lambda i, w: (0, 0)) for source in sources]
    args = [inverse, *sources]
    aliases = {}
    if before is not None:
        in_specs.append(ANYWHERE)
        args.append(before)
        aliases = {len(args): 0}
    return pl.pallas_call(
        functools.partial(finish_kernel, [piece[1:] for piece in pieces]),
        grid_spec=pltpu.PrefetchScalarGridSpec(
            num_scalar_prefetch=1,
            grid=(count,),
            in_specs=in_specs,
            out_specs=pl.BlockSpec((rank, width), lambda i, w: (0, w[i])),
        ),
        out_shape=jax.ShapeDtypeStruct((rank, total), F32),
        input_output_aliases=aliases,
        compiler_params=PARAMS,
        cost_estimate=pl.CostEstimate(
            flops=6 * rank * rank * width * count,
            bytes_accessed=8 * rank * width * count,
            transcendentals=0,
        ),
        name="finish",
    )(jnp.stack([piece[0] for piece in pieces]), *args)


def body(n_pos, n_pix, probes, sketch):
    def swap(value, axis, size, bit):
        return lax.ppermute(value, axis, [(i, i ^ bit) for i in range(size)])

    def over(value, bit):
        return swap(value, "pos", n_pos, bit)

    me = lax.axis_index("pos").astype(jnp.int32)
    near, far = me & 1, (me >> 1) & 1
    cols = probes.shape[1]
    width = cols // (8 * CHUNKS)

    tall = tall_partial(probes, sketch.T)
    bit = 1
    while 2 * bit < n_pix:
        tall = tall + swap(tall, "pix", n_pix, bit)
        bit *= 2
    both, gram = prepare(tall, swap(tall, "pix", n_pix, bit))

    def block_a(c, p, q):
        return 8 * c + 2 * (near ^ p) + (far ^ q)

    def block_b(c, p, q):
        return 8 * c + 4 + 2 * (far ^ p) + (near ^ q)

    def outputs(c, p):
        return [
            ([block_a(c, p, 1), block_a(c, p, 0)], c == 0),
            ([block_b(c, p, 1), block_b(c, p, 0)], False),
        ]

    first = products(both, gram, probes, width, outputs(0, 1))
    plan = [(c, p) for c in range(CHUNKS) for p in (1, 0) if (c, p) != (0, 1)]
    rest = products(
        both, gram, probes, width, [out for c, p in plan for out in outputs(c, p)], (first[0],)
    )
    made = {(0, 1): first}
    made.update({key: rest[2 * k : 2 * k + 2] for k, key in enumerate(plan)})

    inverse, out = None, None
    for c in range(CHUNKS):
        g = LANES if c == 0 else 0
        away_a, away_b = made[c, 1]
        own_a, own_b = made[c, 0]
        sum_a = own_a + over(away_a, 1)
        sum_b = own_b + over(away_b, 2)
        got_a = over(sum_a[:, : width + g], 2)
        got_b = over(sum_b[:, :width], 1)
        whole = jnp.concatenate(
            [
                sum_a[:, width + g :] + got_a[:, :width],
                sum_a[:, width : width + g] + got_a[:, width:],
                sum_b[:, width:] + got_b,
            ],
            axis=1,
        )
        bit = 4
        while bit < n_pos:
            whole = whole + over(whole, bit)
            bit *= 2
        if c == 0:
            inverse = inverse_factor(whole, width)
        mine_a, mine_b = whole[:, :width], whole[:, width + g :]
        next_a = over(mine_a, 2)
        next_b = over(mine_b, 1)
        last_a = over(jnp.concatenate([mine_a, next_a], axis=1), 1)
        last_b = over(jnp.concatenate([mine_b, next_b], axis=1), 2)
        out = finish(
            inverse,
            [whole, next_a, next_b],
            [
                (block_a(c, 0, 0), 0, 0),
                (block_b(c, 0, 0), 0, width + g),
                (block_a(c, 0, 1), 1, 0),
                (block_b(c, 0, 1), 2, 0),
            ],
            width,
            cols,
            out,
        )
        out = finish(
            inverse,
            [last_a, last_b],
            [
                (block_a(c, 1, 0), 0, 0),
                (block_a(c, 1, 1), 0, width),
                (block_b(c, 1, 0), 1, 0),
                (block_b(c, 1, 1), 1, width),
            ],
            width,
            cols,
            out,
        )
    return out


def solution(mesh):
    in_specs = (P("pos", "pix"), P("pix", None))
    out_specs = P(None, "pix")
    run = functools.partial(body, mesh.shape["pos"], mesh.shape["pix"])
    return jax.shard_map(run, mesh=mesh, in_specs=in_specs, out_specs=out_specs, check_vma=False)
```

time: 91.1 us -> 81.5 us (0.89)
  starting transfers between devices: 33.7 us -> 16.9 us
  waiting for transfers between devices: 18.6 us -> 34.2 us
  Pallas kernels: 35.8 us -> 29.3 us
  local copies, waits for them, and re-layouts: 1.51 us -> 0.06 us
    ppermute x10 -> x11, waiting for transfers between devices: 8.06 us -> 34.2 us  [swap(): return lax.ppermute(value, axis, [(i, i ^ bit) for i in range(size)])]
    ppermute x12 -> x0, starting transfers between devices: 20.3 us -> none  [send_outer(): lax.ppermute(value, 'pos', [(2 * a + s, 2 * b + s) for a, b in pairs for...]
    ppermute x12 -> x0, waiting for transfers between devices: 10.6 us -> none  [send_outer(): lax.ppermute(value, 'pos', [(2 * a + s, 2 * b + s) for a, b in pairs for...]
    pallas_call x10 -> x4, Pallas kernels: 20 us -> 16.3 us  [the longest x2 11 us: products(): pl.pallas_call(functools.partial(product_kernel, streams, plan, grams), g...]
    ppermute x10 -> x11, starting transfers between devices: 13.4 us -> 16.9 us  [swap(): return lax.ppermute(value, axis, [(i, i ^ bit) for i in range(size)])]
    pallas_call x1, Pallas kernels: 4.7 us -> 2.01 us  [inverse_factor(): pl.pallas_call(inverse_kernel, grid=(1,), in_specs=[pl.BlockSpec((rank, L...]
    unnamed x2 -> x0, local copies, waits for them, and re-layouts: 1.41 us -> none
  transfers between devices with their start and end apart: 22 -> 11, of which waited for: 8 -> 11; matrix products, arithmetic and copies ran while one was open for 1% -> 1% of each run, Pallas kernels for 23% -> 12%
where the time goes in v3:
time: 81.5 us; the launch traced here: 81.2 us
  waiting for transfers between devices  34.2 us (42%)
  Pallas kernels  29.3 us (36%)
  starting transfers between devices  16.9 us (21%)
    ppermute x11, waiting for transfers between devices, swap(): return lax.ppermute(value, axis, [(i, i ^ bit) for i in range(size)])  34.2 us
    ppermute x11, starting transfers between devices, swap(): return lax.ppermute(value, axis, [(i, i ^ bit) for i in range(size)])  16.9 us
    pallas_call x2, Pallas kernels, products(): pl.pallas_call(functools.partial(product_kernel, streams, plan, grams), g...  11 us
    pallas_call x1, Pallas kernels, tall_partial(): pl.pallas_call(tall_kernel, grid=(cols // width,), in_specs=[pl.BlockSpec...  10.7 us
    pallas_call x2, Pallas kernels, finish(): pl.pallas_call(functools.partial(finish_kernel, [piece[1:] for piece in p...  5.22 us
    pallas_call x1, Pallas kernels, inverse_factor(): pl.pallas_call(inverse_kernel, grid=(1,), in_specs=[pl.BlockSpec((rank, L...  2.01 us
  transfers between devices with their start and end apart: 11, of which 11 were waited for; matrix products, arithmetic and copies ran while one was open for 1% of the time, Pallas kernels for 12%

profile of v3, /device:TPU:0, one launch (start us, length us, event | category | flops | bytes accessed | tf_op | source)
XLA Modules:
  0.0 81.2 jit_solution(14483967149556260525)
XLA Ops:
  0.0 10.7 %tall_partial.1 = f32[48,512]{1,0:T(8,128)S(1)} custom-call(f32[48,8192]{1,0:T(8,128)} %bitcast.9, f32[512,8192]{1,0:T(8,128)} %refs_3_.5, f32[512,8192]{1,0:T(8,128)} %refs_3_.5, f32[512,8192]{1,0:T(8,128)} %refs_3_.5, f32[512,8192]{1,0:T(8,128)} %refs_3_.5), custom_call_target="tpu_custom_call" | custom-call | flops 1207959552 | bytes 16777216 | tf_op jit(solution)/shard_map/tall_partial/pallas_call | solution.py:65
  11.2 0.9 %collective-permute-done = f32[48,512]{1,0:T(8,128)S(1)} collective-permute-done((f32[48,512]{1,0:T(8,128)S(1)}, f32[48,512]{1,0:T(8,128)S(1)}, u32[]{:S(2)}, u32[]{:S(2)}) %collective-permute-start) | collective-permute-done | bytes 98336 | tf_op jit(solution)/shard_map/ppermute | solution.py:264
  12.2 2.9 %collective-permute-start.1 = (f32[48,512]{1,0:T(8,128)S(1)}, f32[48,512]{1,0:T(8,128)S(1)}, u32[]{:S(2)}, u32[]{:S(2)}) collective-permute-start(f32[48,512]{1,0:T(8,128)S(1)} %add.75.first_ref), channel_id=1, source_target_pairs={{0,2},{1,3},{2,0},{3,1},{4,6},{5,7},{6,4},{7,5},{8,10},{9,11},{10,... | collective-permute-start | bytes 294920 | tf_op jit(solution)/shard_map/ppermute | solution.py:264
  15.2 3.0 %collective-permute-done.1.second_ref = f32[48,512]{1,0:T(8,128)S(1)} collective-permute-done((f32[48,512]{1,0:T(8,128)S(1)}, f32[48,512]{1,0:T(8,128)S(1)}, u32[]{:S(2)}, u32[]{:S(2)}) %collective-permute-start.1) | collective-permute-done | bytes 98336 | tf_op jit(solution)/shard_map/ppermute | solution.py:264
  18.6 5.5 %products.2 = (f32[48,2176]{1,0:T(8,128)S(1)}, f32[48,2048]{1,0:T(8,128)S(1)}) custom-call(s32[4]{0:T(128)S(1)} %pad_add_fusion.2.which_ref, bf16[96,512]{1,0:T(8,128)(2,1)S(1)} %get-tuple-element.11.both_ref, f32[48,128]{1,0:T(8,128)S(1)} %get-tuple-element.12.gram_ref, f32[512,8192]{1,0:T(8,128)} %refs_3_.5, f32[512,8192]{1,0:T(8,128)} %refs_3_.5, ...), custom_call_target="tpu_custom_call" | custom-call | flops 603979776 | bytes 8388608 | tf_op jit(solution)/shard_map/products/pallas_call | solution.py:154
  24.1 1.9 %collective-permute-start.4 = (f32[48,2048]{1,0:T(8,128)S(1)}, f32[48,2048]{1,0:T(8,128)S(1)}, u32[]{:S(2)}, u32[]{:S(2)}) collective-permute-start(f32[48,2048]{1,0:T(8,128)S(1)} %get-tuple-element.16), channel_id=1, source_target_pairs={{0,8},{4,12},{8,0},{12,4},{16,24},{20,28},{24,16},{28,20},{1,9},{5... | collective-permute-start | bytes 1179656 | tf_op jit(solution)/shard_map/ppermute | solution.py:264
  26.0 1.5 %collective-permute-start.2 = (f32[48,2176]{1,0:T(8,128)S(1)}, f32[48,2176]{1,0:T(8,128)S(1)}, u32[]{:S(2)}, u32[]{:S(2)}) collective-permute-start(f32[48,2176]{1,0:T(8,128)S(1)} %get-tuple-element.13.refs_4_), channel_id=1, source_target_pairs={{0,4},{4,0},{8,12},{12,8},{16,20},{20,16},{24,28},{28,24},{1,5},{5... | collective-permute-start | bytes 1253384 | tf_op jit(solution)/shard_map/ppermute | solution.py:264
  27.6 5.5 %products.3 = (f32[48,2176]{1,0:T(8,128)S(1)}, f32[48,2048]{1,0:T(8,128)S(1)}) custom-call(s32[4]{0:T(128)S(1)} %pad_add_fusion.1.which_ref, bf16[96,512]{1,0:T(8,128)(2,1)S(1)} %get-tuple-element.11.both_ref, f32[48,128]{1,0:T(8,128)S(1)} %get-tuple-element.12.gram_ref, f32[512,8192]{1,0:T(8,128)} %refs_3_.5, f32[512,8192]{1,0:T(8,128)} %refs_3_.5, ...), custom_call_target="tpu_custom_call" | custom-call | flops 603979776 | bytes 8388608 | tf_op jit(solution)/shard_map/products/pallas_call | solution.py:154
  33.1 1.8 %collective-permute-done.4 = f32[48,2048]{1,0:T(8,128)S(1)} collective-permute-done((f32[48,2048]{1,0:T(8,128)S(1)}, f32[48,2048]{1,0:T(8,128)S(1)}, u32[]{:S(2)}, u32[]{:S(2)}) %collective-permute-start.4) | collective-permute-done | bytes 393248 | tf_op jit(solution)/shard_map/ppermute | solution.py:264
  34.9 1.5 %collective-permute-start.5 = (f32[48,1024]{1,0:T(8,128)S(1)}, f32[48,1024]{1,0:T(8,128)S(1)}, u32[]{:S(2)}, u32[]{:S(2)}) collective-permute-start(f32[48,1024]{1,0:T(8,128)S(1)} %slice.42), channel_id=1, source_target_pairs={{0,4},{4,0},{8,12},{12,8},{16,20},{20,16},{24,28},{28,24},{1,5},{5... | collective-permute-start | bytes 589832 | tf_op jit(solution)/shard_map/ppermute | solution.py:264
  36.9 1.3 %collective-permute-start.3 = (f32[48,1152]{1,0:T(8,128)S(1)}, f32[48,1152]{1,0:T(8,128)S(1)}, u32[]{:S(2)}, u32[]{:S(2)}) collective-permute-start(f32[48,1152]{1,0:T(8,128)S(1)} %slice.37), channel_id=1, source_target_pairs={{0,8},{4,12},{8,0},{12,4},{16,24},{20,28},{24,16},{28,20},{1,9},{5... | collective-permute-start | bytes 663560 | tf_op jit(solution)/shard_map/ppermute | solution.py:264
  38.1 2.7 %collective-permute-done.5 = f32[48,1024]{1,0:T(8,128)S(1)} collective-permute-done((f32[48,1024]{1,0:T(8,128)S(1)}, f32[48,1024]{1,0:T(8,128)S(1)}, u32[]{:S(2)}, u32[]{:S(2)}) %collective-permute-start.5) | collective-permute-done | bytes 196640 | tf_op jit(solution)/shard_map/ppermute | solution.py:264
  40.8 2.0 %collective-permute-done.3 = f32[48,1152]{1,0:T(8,128)S(1)} collective-permute-done((f32[48,1152]{1,0:T(8,128)S(1)}, f32[48,1152]{1,0:T(8,128)S(1)}, u32[]{:S(2)}, u32[]{:S(2)}) %collective-permute-start.3) | collective-permute-done | bytes 221216 | tf_op jit(solution)/shard_map/ppermute | solution.py:264
  42.9 4.0 %collective-permute-start.6 = (f32[48,2176]{1,0:T(8,128)S(1)}, f32[48,2176]{1,0:T(8,128)S(1)}, u32[]{:S(2)}, u32[]{:S(2)}) collective-permute-start(f32[48,2176]{1,0:T(8,128)S(1)} %pad_maximum_fusion), channel_id=1, source_target_pairs={{0,16},{4,20},{8,24},{12,28},{16,0},{20,4},{24,8},{28,12},{1,17},{... | collective-permute-start | bytes 1253384 | tf_op jit(solution)/shard_map/ppermute | solution.py:264
  46.9 14.6 %collective-permute-done.6 = f32[48,2176]{1,0:T(8,128)S(1)} collective-permute-done((f32[48,2176]{1,0:T(8,128)S(1)}, f32[48,2176]{1,0:T(8,128)S(1)}, u32[]{:S(2)}, u32[]{:S(2)}) %collective-permute-start.6) | collective-permute-done | bytes 417824 | tf_op jit(solution)/shard_map/ppermute | solution.py:264
  61.6 0.7 collective-permute-start.7
  62.2 0.9 %collective-permute-start.9 = (f32[48,1024]{1,0:T(8,128)S(1)}, f32[48,1024]{1,0:T(8,128)S(1)}, u32[]{:S(2)}, u32[]{:S(2)}) collective-permute-start(f32[48,1024]{1,0:T(8,128)S(1)} %get-tuple-element.17), channel_id=1, source_target_pairs={{0,4},{4,0},{8,12},{12,8},{16,20},{20,16},{24,28},{28,24},{1,5},{5... | collective-permute-start | bytes 589832 | tf_op jit(solution)/shard_map/ppermute | solution.py:264
  63.1 4.2 %collective-permute-done.7.refs_1_ = f32[48,1024]{1,0:T(8,128)S(1)} collective-permute-done((f32[48,1024]{1,0:T(8,128)S(1)}, f32[48,1024]{1,0:T(8,128)S(1)}, u32[]{:S(2)}, u32[]{:S(2)}) %collective-permute-start.7) | collective-permute-done | bytes 196640 | tf_op jit(solution)/shard_map/ppermute | solution.py:264
  67.4 1.5 %collective-permute-start.8 = (f32[48,2048]{1,0:T(8,128)S(1)}, f32[48,2048]{1,0:T(8,128)S(1)}, u32[]{:S(2)}, u32[]{:S(2)}) collective-permute-start(f32[48,2048]{1,0:T(8,128)S(1)} %pad_maximum_fusion.1), channel_id=1, source_target_pairs={{0,4},{4,0},{8,12},{12,8},{16,20},{20,16},{24,28},{28,24},{1,5},{5... | collective-permute-start | bytes 1179656 | tf_op jit(solution)/shard_map/ppermute | solution.py:264
  69.6 2.0 %inverse_factor.1.inverse_ref = f32[48,48]{1,0:T(8,128)S(1)} custom-call(f32[48,2176]{1,0:T(8,128)S(1)} %fusion.gram_ref.refs_0_), custom_call_target="tpu_custom_call" | custom-call | flops 20000000 | bytes 49152 | tf_op jit(solution)/shard_map/inverse_factor/pallas_call | solution.py:202
  71.6 2.6 %finish.2.refs_2_ = f32[48,8192]{1,0:T(8,128)} custom-call(s32[4]{0:T(128)S(1)} %pad_add_fusion.3.where_ref, f32[48,48]{1,0:T(8,128)S(1)} %inverse_factor.1.inverse_ref, f32[48,2176]{1,0:T(8,128)S(1)} %fusion.gram_ref.refs_0_, f32[48,1024]{1,0:T(8,128)S(1)} %collective-permute-done.7.refs_1_, f32[48,1024]{1,0:T(8,128)S(1)} %collective-permute-done.9.refs_2_), custom_call_target="tpu_custom_call" | custom-call | flops 56623104 | bytes 1572864 | tf_op jit(solution)/shard_map/finish/pallas_call | solution.py:242
  74.2 2.9 %collective-permute-done.8.refs_0_ = f32[48,2048]{1,0:T(8,128)S(1)} collective-permute-done((f32[48,2048]{1,0:T(8,128)S(1)}, f32[48,2048]{1,0:T(8,128)S(1)}, u32[]{:S(2)}, u32[]{:S(2)}) %collective-permute-start.8) | collective-permute-done | bytes 393248 | tf_op jit(solution)/shard_map/ppermute | solution.py:264
  77.1 1.4 %collective-permute-done.10.refs_1_ = f32[48,2048]{1,0:T(8,128)S(1)} collective-permute-done((f32[48,2048]{1,0:T(8,128)S(1)}, f32[48,2048]{1,0:T(8,128)S(1)}, u32[]{:S(2)}, u32[]{:S(2)}) %collective-permute-start.10) | collective-permute-done | bytes 393248 | tf_op jit(solution)/shard_map/ppermute | solution.py:264
  78.6 2.6 %finish.3 = f32[48,8192]{1,0:T(8,128)} custom-call(s32[4]{0:T(128)S(1)} %pad_add_fusion.where_ref, f32[48,48]{1,0:T(8,128)S(1)} %inverse_factor.1.inverse_ref, f32[48,2048]{1,0:T(8,128)S(1)} %collective-permute-done.8.refs_0_, f32[48,2048]{1,0:T(8,128)S(1)} %collective-permute-done.10.refs_1_, f32[48,8192]{1,0:T(8,128)} %finish.2.refs_2_), custom_call_target="tpu_custom_call", output_to_operand_aliasing={{}: (4, {})} | custom-call | flops 56623104 | bytes 1572864 | tf_op jit(solution)/shard_map/finish/pallas_call | solution.py:242
  (22 shorter events, 2.6 us)
Async XLA Ops:
  10.7 1.5 %collective-permute-start = (f32[48,512]{1,0:T(8,128)S(1)}, f32[48,512]{1,0:T(8,128)S(1)}, u32[]{:S(2)}, u32[]{:S(2)}) collective-permute-start(f32[48,512]{1,0:T(8,128)S(1)} %tall_partial.1), channel_id=1, source_target_pairs={{0,1},{1,0},{2,3},{3,2},{4,5},{5,4},{6,7},{7,6},{8,9},{9,8},{10,11... | collective-permute-start | bytes 294920 | tf_op jit(solution)/shard_map/ppermute | solution.py:264
  12.2 6.0 %collective-permute-start.1 = (f32[48,512]{1,0:T(8,128)S(1)}, f32[48,512]{1,0:T(8,128)S(1)}, u32[]{:S(2)}, u32[]{:S(2)}) collective-permute-start(f32[48,512]{1,0:T(8,128)S(1)} %add.75.first_ref), channel_id=1, source_target_pairs={{0,2},{1,3},{2,0},{3,1},{4,6},{5,7},{6,4},{7,5},{8,10},{9,11},{10,... | collective-permute-start | bytes 294920 | tf_op jit(solution)/shard_map/ppermute | solution.py:264
  24.1 10.7 %collective-permute-start.4 = (f32[48,2048]{1,0:T(8,128)S(1)}, f32[48,2048]{1,0:T(8,128)S(1)}, u32[]{:S(2)}, u32[]{:S(2)}) collective-permute-start(f32[48,2048]{1,0:T(8,128)S(1)} %get-tuple-element.16), channel_id=1, source_target_pairs={{0,8},{4,12},{8,0},{12,4},{16,24},{20,28},{24,16},{28,20},{1,9},{5... | collective-permute-start | bytes 1179656 | tf_op jit(solution)/shard_map/ppermute | solution.py:264
  26.0 10.8 %collective-permute-start.2 = (f32[48,2176]{1,0:T(8,128)S(1)}, f32[48,2176]{1,0:T(8,128)S(1)}, u32[]{:S(2)}, u32[]{:S(2)}) collective-permute-start(f32[48,2176]{1,0:T(8,128)S(1)} %get-tuple-element.13.refs_4_), channel_id=1, source_target_pairs={{0,4},{4,0},{8,12},{12,8},{16,20},{20,16},{24,28},{28,24},{1,5},{5... | collective-permute-start | bytes 1253384 | tf_op jit(solution)/shard_map/ppermute | solution.py:264
  34.9 5.9 %collective-permute-start.5 = (f32[48,1024]{1,0:T(8,128)S(1)}, f32[48,1024]{1,0:T(8,128)S(1)}, u32[]{:S(2)}, u32[]{:S(2)}) collective-permute-start(f32[48,1024]{1,0:T(8,128)S(1)} %slice.42), channel_id=1, source_target_pairs={{0,4},{4,0},{8,12},{12,8},{16,20},{20,16},{24,28},{28,24},{1,5},{5... | collective-permute-start | bytes 589832 | tf_op jit(solution)/shard_map/ppermute | solution.py:264
  36.9 6.0 %collective-permute-start.3 = (f32[48,1152]{1,0:T(8,128)S(1)}, f32[48,1152]{1,0:T(8,128)S(1)}, u32[]{:S(2)}, u32[]{:S(2)}) collective-permute-start(f32[48,1152]{1,0:T(8,128)S(1)} %slice.37), channel_id=1, source_target_pairs={{0,8},{4,12},{8,0},{12,4},{16,24},{20,28},{24,16},{28,20},{1,9},{5... | collective-permute-start | bytes 663560 | tf_op jit(solution)/shard_map/ppermute | solution.py:264
  42.9 18.5 %collective-permute-start.6 = (f32[48,2176]{1,0:T(8,128)S(1)}, f32[48,2176]{1,0:T(8,128)S(1)}, u32[]{:S(2)}, u32[]{:S(2)}) collective-permute-start(f32[48,2176]{1,0:T(8,128)S(1)} %pad_maximum_fusion), channel_id=1, source_target_pairs={{0,16},{4,20},{8,24},{12,28},{16,0},{20,4},{24,8},{28,12},{1,17},{... | collective-permute-start | bytes 1253384 | tf_op jit(solution)/shard_map/ppermute | solution.py:264
  61.6 5.7 %collective-permute-start.7 = (f32[48,1024]{1,0:T(8,128)S(1)}, f32[48,1024]{1,0:T(8,128)S(1)}, u32[]{:S(2)}, u32[]{:S(2)}) collective-permute-start(f32[48,1024]{1,0:T(8,128)S(1)} %get-tuple-element.18), channel_id=1, source_target_pairs={{0,8},{4,12},{8,0},{12,4},{16,24},{20,28},{24,16},{28,20},{1,9},{5... | collective-permute-start | bytes 589832 | tf_op jit(solution)/shard_map/ppermute | solution.py:264
  62.2 6.8 %collective-permute-start.9 = (f32[48,1024]{1,0:T(8,128)S(1)}, f32[48,1024]{1,0:T(8,128)S(1)}, u32[]{:S(2)}, u32[]{:S(2)}) collective-permute-start(f32[48,1024]{1,0:T(8,128)S(1)} %get-tuple-element.17), channel_id=1, source_target_pairs={{0,4},{4,0},{8,12},{12,8},{16,20},{20,16},{24,28},{28,24},{1,5},{5... | collective-permute-start | bytes 589832 | tf_op jit(solution)/shard_map/ppermute | solution.py:264
  67.4 9.8 %collective-permute-start.8 = (f32[48,2048]{1,0:T(8,128)S(1)}, f32[48,2048]{1,0:T(8,128)S(1)}, u32[]{:S(2)}, u32[]{:S(2)}) collective-permute-start(f32[48,2048]{1,0:T(8,128)S(1)} %pad_maximum_fusion.1), channel_id=1, source_target_pairs={{0,4},{4,0},{8,12},{12,8},{16,20},{20,16},{24,28},{28,24},{1,5},{5... | collective-permute-start | bytes 1179656 | tf_op jit(solution)/shard_map/ppermute | solution.py:264
  69.1 9.5 %collective-permute-start.10 = (f32[48,2048]{1,0:T(8,128)S(1)}, f32[48,2048]{1,0:T(8,128)S(1)}, u32[]{:S(2)}, u32[]{:S(2)}) collective-permute-start(f32[48,2048]{1,0:T(8,128)S(1)} %pad_maximum_fusion.2), channel_id=1, source_target_pairs={{0,8},{4,12},{8,0},{12,4},{16,24},{20,28},{24,16},{28,20},{1,9},{5... | collective-permute-start | bytes 1179656 | tf_op jit(solution)/shard_map/ppermute | solution.py:264

commit v4 on v3

--- a/solution.py
+++ b/solution.py
@@ -9,14 +9,14 @@
 
 F32 = jnp.float32
 BF16 = jnp.bfloat16
-VMEM_LIMIT = 40 * 1024 * 1024
+VMEM_LIMIT = 30 * 1024 * 1024
 LANES = 128
 CHUNKS = 1
-STREAMS = 4
 PANEL = 4
 LAST = (((1,), (1,)), ((), ()))
 PLAIN = (((1,), (0,)), ((), ()))
 ANYWHERE = pl.BlockSpec(memory_space=pl.ANY)
+WHOLE = pl.BlockSpec(memory_space=pltpu.VMEM)
 PARAMS = pltpu.CompilerParams(vmem_limit_bytes=VMEM_LIMIT)
 
 
@@ -29,52 +29,65 @@
     return lax.dot_general(a, b, dims, preferred_element_type=F32)
 
 
-def row_blocks(rows):
-    return STREAMS if rows % (16 * STREAMS) == 0 else 1
-
-
-def tall_kernel(s_ref, *refs):
-    x_refs, (out_ref, acc_ref) = refs[:-2], refs[-2:]
-    step = pl.program_id(0)
-    rank = s_ref.shape[0]
-
-    @pl.when(step == 0)
-    def _():
-        acc_ref[...] = jnp.zeros_like(acc_ref)
-
-    s_head, s_rest = split(s_ref[...])
-    s_both = jnp.concatenate([s_head, s_rest], axis=0)
-    x_head, x_rest = split(jnp.concatenate([ref[...] for ref in x_refs], axis=0))
-    both = dot(s_both, x_head, LAST)
-    acc_ref[...] += both[:rank] + (both[rank:] + dot(s_head, x_rest, LAST))
-
-    @pl.when(step == pl.num_programs(0) - 1)
-    def _():
-        out_ref[...] = acc_ref[...]
-
-
-def tall_partial(probes, sketch_t):
+def tall_kernel(x_hbm, s_hbm, out_ref, head_ref, rest_ref, x_buf, s_buf, x_sems, s_sems):
+    blocks, rows, width = x_buf.shape
+    rank = s_hbm.shape[0]
+
+    def copies(k):
+        where = pl.ds(k * width, width)
+        return (
+            pltpu.make_async_copy(s_hbm.at[:, where], s_buf.at[k], s_sems.at[k]),
+            pltpu.make_async_copy(x_hbm.at[:, where], x_buf.at[k], x_sems.at[k]),
+        )
+
+    for k in range(blocks):
+        for copy in copies(k):
+            copy.start()
+    for k in range(blocks):
+        for copy in copies(k):
+            copy.wait()
+        s_head, s_rest = split(s_buf[k])
+        s_both = jnp.concatenate([s_head, s_rest], axis=0)
+        x_head, x_rest = split(x_buf[k])
+        head_ref[k] = x_head
+        rest_ref[k] = x_rest
+        both = dot(s_both, x_head, LAST)
+        part = both[:rank] + (both[rank:] + dot(s_head, x_rest, LAST))
+        if k == 0:
+            out_ref[...] = part
+        else:
+            out_ref[...] += part
+
+
+def tall_partial(probes, sketch_t, width):
     rows, cols = probes.shape
     rank = sketch_t.shape[0]
-    width = min(1024, cols)
-    streams = row_blocks(rows)
-    sketch_t = pltpu.with_memory_space_constraint(sketch_t, pltpu.MemorySpace.HBM)
-    x_specs = [
-        pl.BlockSpec((rows // streams, width), lambda i, q=q: (q, i)) for q in range(streams)
-    ]
+    blocks = cols // width
+    hbm = pltpu.MemorySpace.HBM
     return pl.pallas_call(
         tall_kernel,
-        grid=(cols // width,),
-        in_specs=[pl.BlockSpec((rank, width), lambda i: (0, i)), *x_specs],
-        out_specs=pl.BlockSpec((rank, rows), lambda i: (0, 0)),
-        out_shape=jax.ShapeDtypeStruct((rank, rows), F32),
-        scratch_shapes=[pltpu.VMEM((rank, rows), F32)],
+        in_specs=[pl.BlockSpec(memory_space=hbm)] * 2,
+        out_specs=[WHOLE] * 3,
+        out_shape=[
+            jax.ShapeDtypeStruct((rank, rows), F32),
+            pltpu.VMEM((blocks, rows, width), BF16),
+            pltpu.VMEM((blocks, rows, width), BF16),
+        ],
+        scratch_shapes=[
+            pltpu.VMEM((blocks, rows, width), F32),
+            pltpu.VMEM((blocks, rank, width), F32),
+            pltpu.SemaphoreType.DMA((blocks,)),
+            pltpu.SemaphoreType.DMA((blocks,)),
+        ],
         compiler_params=PARAMS,
         cost_estimate=pl.CostEstimate(
             flops=6 * rows * cols * rank, bytes_accessed=4 * rows * cols, transcendentals=0
         ),
         name="tall_partial",
-    )(sketch_t, *[probes] * streams)
+    )(
+        pltpu.with_memory_space_constraint(probes, hbm),
+        pltpu.with_memory_space_constraint(sketch_t, hbm),
+    )
 
 
 def prepare_kernel(first_ref, second_ref, both_ref, gram_ref):
@@ -95,11 +108,10 @@
 
 def prepare(first, second):
     rank, rows = first.shape
-    whole = pl.BlockSpec(memory_space=pltpu.VMEM)
     return pl.pallas_call(
         prepare_kernel,
-        in_specs=[whole, whole],
-        out_specs=[whole, whole],
+        in_specs=[WHOLE, WHOLE],
+        out_specs=[WHOLE, WHOLE],
         out_shape=[
             jax.ShapeDtypeStruct((2 * rank, rows), BF16),
             jax.ShapeDtypeStruct((rank, LANES), F32),
@@ -112,33 +124,24 @@
     )(first, second)
 
 
-def product_kernel(streams, plan, grams, which_ref, both_ref, gram_ref, *refs):
+def product_kernel(plan, grams, which_ref, both_ref, gram_ref, head_ref, rest_ref, *refs):
     count = 1 + max(out for out, _ in plan)
-    x_refs, outs = refs[:streams], refs[len(refs) - count :]
-    step = pl.program_id(0)
-    rank = outs[0].shape[0]
-    sub = x_refs[0].shape[1]
+    outs = refs[len(refs) - count :]
+    rank = gram_ref.shape[0]
+    sub = head_ref.shape[2]
     both = both_ref[...]
-    x_head, x_rest = split(jnp.concatenate([ref[...] for ref in x_refs], axis=0))
-    first = dot(both, x_head, PLAIN)
-    second = dot(both[:rank], x_rest, PLAIN)
-    result = first[:rank] + (first[rank:] + second)
     for k, (out, offset) in enumerate(plan):
-
-        @pl.when(step == k)
-        def _():
-            outs[out][:, offset : offset + sub] = result
-
-    @pl.when(step == 0)
-    def _():
-        for out, offset in grams:
-            outs[out][:, offset : offset + LANES] = gram_ref[...]
-
-
-def products(both, gram, probes, sub, outputs, after=()):
-    rows = probes.shape[0]
+        block = which_ref[k]
+        first = dot(both, head_ref[block], PLAIN)
+        second = dot(both[:rank], rest_ref[block], PLAIN)
+        outs[out][:, offset : offset + sub] = first[:rank] + (first[rank:] + second)
+    for out, offset in grams:
+        outs[out][:, offset : offset + LANES] = gram_ref[...]
+
+
+def products(both, gram, head, rest, outputs, after=()):
+    _, rows, sub = head.shape
     rank = both.shape[0] // 2
-    streams = row_blocks(rows)
     plan, grams, widths, which = [], [], [], []
     for out, (blocks, with_gram) in enumerate(outputs):
         extra = LANES if with_gram else 0
@@ -148,31 +151,31 @@
         if with_gram:
             grams.append((out, sub))
         widths.append(len(blocks) * sub + extra)
-    x_specs = [
-        pl.BlockSpec((rows // streams, sub), lambda i, w, q=q: (q, w[i])) for q in range(streams)
-    ]
-    return pl.pallas_call(
-        functools.partial(product_kernel, streams, plan, grams),
-        grid_spec=pltpu.PrefetchScalarGridSpec(
-            num_scalar_prefetch=1,
-            grid=(len(plan),),
-            in_specs=[
-                pl.BlockSpec((2 * rank, rows), lambda i, w: (0, 0)),
-                pl.BlockSpec((rank, LANES), lambda i, w: (0, 0)),
-                *x_specs,
-                *[ANYWHERE] * len(after),
-            ],
-            out_specs=[pl.BlockSpec((rank, width), lambda i, w: (0, 0)) for width in widths],
-        ),
+    vmem = pltpu.MemorySpace.VMEM
+    return pl.pallas_call(
+        functools.partial(product_kernel, plan, grams),
+        in_specs=[
+            pl.BlockSpec(memory_space=pltpu.SMEM),
+            *[WHOLE] * 4,
+            *[ANYWHERE] * len(after),
+        ],
+        out_specs=[WHOLE] * len(widths),
         out_shape=[jax.ShapeDtypeStruct((rank, width), F32) for width in widths],
         compiler_params=PARAMS,
         cost_estimate=pl.CostEstimate(
             flops=6 * rows * rank * sub * len(plan),
-            bytes_accessed=4 * rows * sub * len(plan),
+            bytes_accessed=4 * rank * sub * len(plan),
             transcendentals=0,
         ),
         name="products",
-    )(jnp.stack(which), both, gram, *[probes] * streams, *after)
+    )(
+        jnp.stack(which),
+        both,
+        gram,
+        pltpu.with_memory_space_constraint(head, vmem),
+        pltpu.with_memory_space_constraint(rest, vmem),
+        *after,
+    )
 
 
 def inverse_kernel(gram_ref, out_ref):
@@ -271,7 +274,7 @@
     cols = probes.shape[1]
     width = cols // (8 * CHUNKS)
 
-    tall = tall_partial(probes, sketch.T)
+    tall, head, rest = tall_partial(probes, sketch.T, width)
     bit = 1
     while 2 * bit < n_pix:
         tall = tall + swap(tall, "pix", n_pix, bit)
@@ -290,13 +293,13 @@
             ([block_b(c, p, 1), block_b(c, p, 0)], False),
         ]
 
-    first = products(both, gram, probes, width, outputs(0, 1))
+    first = products(both, gram, head, rest, outputs(0, 1))
     plan = [(c, p) for c in range(CHUNKS) for p in (1, 0) if (c, p) != (0, 1)]
-    rest = products(
-        both, gram, probes, width, [out for c, p in plan for out in outputs(c, p)], (first[0],)
+    others = products(
+        both, gram, head, rest, [out for c, p in plan for out in outputs(c, p)], (first[0],)
     )
     made = {(0, 1): first}
-    made.update({key: rest[2 * k : 2 * k + 2] for k, key in enumerate(plan)})
+    made.update({key: others[2 * k : 2 * k + 2] for k, key in enumerate(plan)})
 
     inverse, out = None, None
     for c in range(CHUNKS):

time: 81.5 us -> 88.9 us (1.091)
  local copies, waits for them, and re-layouts: 0.06 us -> 20 us
  Pallas kernels: 29.3 us -> 19.7 us
  starting transfers between devices: 16.9 us -> 15.2 us
  waiting for transfers between devices: 34.2 us -> 33 us
    unnamed x0 -> x12, local copies, waits for them, and re-layouts: none -> 20 us
    pallas_call x4, Pallas kernels: 22.1 us -> 12.4 us  [the longest x1 7.99 us: tall_partial(): pl.pallas_call(tall_kernel, in_specs=[pl.BlockSpec(memory_space=hbm)] * 2...]
    ppermute x11, starting transfers between devices: 16.9 us -> 15.2 us  [swap(): return lax.ppermute(value, axis, [(i, i ^ bit) for i in range(size)])]
    ppermute x11, waiting for transfers between devices: 34.2 us -> 33 us  [swap(): return lax.ppermute(value, axis, [(i, i ^ bit) for i in range(size)])]
  transfers between devices with their start and end apart: 11 -> 11, of which waited for: 11 -> 8; matrix products, arithmetic and copies ran while one was open for 1% -> 1% of each run, Pallas kernels for 12% -> 7%
where the time goes in v4:
time: 88.9 us; the launch traced here: 88.6 us
  waiting for transfers between devices  33 us (37%)
  local copies, waits for them, and re-layouts  20 us (22%)
  Pallas kernels  19.7 us (22%)
  starting transfers between devices  15.2 us (17%)
    ppermute x11, waiting for transfers between devices, swap(): return lax.ppermute(value, axis, [(i, i ^ bit) for i in range(size)])  33 us
    unnamed x12, local copies, waits for them, and re-layouts  20 us
    ppermute x11, starting transfers between devices, swap(): return lax.ppermute(value, axis, [(i, i ^ bit) for i in range(size)])  15.2 us
    pallas_call x1, Pallas kernels, tall_partial(): pl.pallas_call(tall_kernel, in_specs=[pl.BlockSpec(memory_space=hbm)] * 2...  7.99 us
    pallas_call x2, Pallas kernels, finish(): pl.pallas_call(functools.partial(finish_kernel, [piece[1:] for piece in p...  5.22 us
    pallas_call x2, Pallas kernels, products(): pl.pallas_call(functools.partial(product_kernel, plan, grams), in_specs=[...  4.03 us
    pallas_call x1, Pallas kernels, inverse_factor(): pl.pallas_call(inverse_kernel, grid=(1,), in_specs=[pl.BlockSpec((rank, L...  2.01 us
  transfers between devices with their start and end apart: 11, of which 8 were waited for; matrix products, arithmetic and copies ran while one was open for 1% of the time, Pallas kernels for 7%

profile of v4, /device:TPU:0, one launch (start us, length us, event | category | flops | bytes accessed | tf_op | source)
XLA Modules:
  0.0 88.6 jit_solution(7498343371725771098)
XLA Ops:
  0.0 8.0 %tall_partial.1 = (f32[48,512]{1,0:T(8,128)S(1)}, bf16[8,512,1024]{2,1,0:T(8,128)(2,1)S(1)}, bf16[8,512,1024]{2,1,0:T(8,128)(2,1)S(1)}) custom-call(f32[512,8192]{1,0:T(8,128)} %x_hbm.1, f32[48,8192]{1,0:T(8,128)} %bitcast.9), custom_call_target="tpu_custom_call" | custom-call | flops 1207959552 | bytes 16777216 | tf_op jit(solution)/shard_map/tall_partial/pallas_call | solution.py:67
  8.0 3.2 %copy-done = bf16[8,512,1024]{2,1,0:T(8,128)(2,1)} copy-done((bf16[8,512,1024]{2,1,0:T(8,128)(2,1)}, bf16[8,512,1024]{2,1,0:T(8,128)(2,1)S(1)}, u32[]{:S(2)}) %copy-start) | copy-done | bytes 8388632
  11.3 3.2 %copy-done.3 = bf16[8,512,1024]{2,1,0:T(8,128)(2,1)} copy-done((bf16[8,512,1024]{2,1,0:T(8,128)(2,1)}, bf16[8,512,1024]{2,1,0:T(8,128)(2,1)S(1)}, u32[]{:S(2)}) %copy-start.3) | copy-done | bytes 8388632
  15.9 2.9 %collective-permute-start.1 = (f32[48,512]{1,0:T(8,128)S(1)}, f32[48,512]{1,0:T(8,128)S(1)}, u32[]{:S(2)}, u32[]{:S(2)}) collective-permute-start(f32[48,512]{1,0:T(8,128)S(1)} %add.75.first_ref), channel_id=1, source_target_pairs={{0,2},{1,3},{2,0},{3,1},{4,6},{5,7},{6,4},{7,5},{8,10},{9,11},{10,... | collective-permute-start | bytes 294920 | tf_op jit(solution)/shard_map/ppermute | solution.py:267
  18.9 3.0 %collective-permute-done.1.second_ref = f32[48,512]{1,0:T(8,128)S(1)} collective-permute-done((f32[48,512]{1,0:T(8,128)S(1)}, f32[48,512]{1,0:T(8,128)S(1)}, u32[]{:S(2)}, u32[]{:S(2)}) %collective-permute-start.1) | collective-permute-done | bytes 98336 | tf_op jit(solution)/shard_map/ppermute | solution.py:267
  22.4 3.4 %copy-done.1 = bf16[8,512,1024]{2,1,0:T(8,128)(2,1)S(1)} copy-done((bf16[8,512,1024]{2,1,0:T(8,128)(2,1)S(1)}, bf16[8,512,1024]{2,1,0:T(8,128)(2,1)}, u32[]{:S(2)}) %copy-start.1) | copy-done | bytes 8388632
  25.7 3.4 %copy-done.4 = bf16[8,512,1024]{2,1,0:T(8,128)(2,1)S(1)} copy-done((bf16[8,512,1024]{2,1,0:T(8,128)(2,1)S(1)}, bf16[8,512,1024]{2,1,0:T(8,128)(2,1)}, u32[]{:S(2)}) %copy-start.4) | copy-done | bytes 8388632
  29.1 2.0 %products.2 = (f32[48,2176]{1,0:T(8,128)S(1)}, f32[48,2048]{1,0:T(8,128)S(1)}) custom-call(s32[4]{0:T(128)S(1)} %pad_add_fusion.2.which_ref, bf16[96,512]{1,0:T(8,128)(2,1)S(1)} %get-tuple-element.15.both_ref, f32[48,128]{1,0:T(8,128)S(1)} %get-tuple-element.16.gram_ref, bf16[8,512,1024]{2,1,0:T(8,128)(2,1)S(1)} %copy-done.1, bf16[8,512,1024]{2,1,0:T(8,128)(2,1)S(1)} %copy-done.4), custom_call_target="tpu_custom_call" | custom-call | flops 603979776 | bytes 786432 | tf_op jit(solution)/shard_map/products/pallas_call | solution.py:155
  31.1 1.8 %collective-permute-start.4 = (f32[48,2048]{1,0:T(8,128)S(1)}, f32[48,2048]{1,0:T(8,128)S(1)}, u32[]{:S(2)}, u32[]{:S(2)}) collective-permute-start(f32[48,2048]{1,0:T(8,128)S(1)} %get-tuple-element.22), channel_id=1, source_target_pairs={{0,8},{4,12},{8,0},{12,4},{16,24},{20,28},{24,16},{28,20},{1,9},{5... | collective-permute-start | bytes 1179656 | tf_op jit(solution)/shard_map/ppermute | solution.py:267
  33.0 1.5 %collective-permute-start.2 = (f32[48,2176]{1,0:T(8,128)S(1)}, f32[48,2176]{1,0:T(8,128)S(1)}, u32[]{:S(2)}, u32[]{:S(2)}) collective-permute-start(f32[48,2176]{1,0:T(8,128)S(1)} %get-tuple-element.19.refs_0_), channel_id=1, source_target_pairs={{0,4},{4,0},{8,12},{12,8},{16,20},{20,16},{24,28},{28,24},{1,5},{5... | collective-permute-start | bytes 1253384 | tf_op jit(solution)/shard_map/ppermute | solution.py:267
  34.5 3.4 %copy-done.2 = bf16[8,512,1024]{2,1,0:T(8,128)(2,1)S(1)} copy-done((bf16[8,512,1024]{2,1,0:T(8,128)(2,1)S(1)}, bf16[8,512,1024]{2,1,0:T(8,128)(2,1)}, u32[]{:S(2)}) %copy-start.2) | copy-done | bytes 8388632
  37.9 3.4 %copy-done.5 = bf16[8,512,1024]{2,1,0:T(8,128)(2,1)S(1)} copy-done((bf16[8,512,1024]{2,1,0:T(8,128)(2,1)S(1)}, bf16[8,512,1024]{2,1,0:T(8,128)(2,1)}, u32[]{:S(2)}) %copy-start.5) | copy-done | bytes 8388632
  41.3 2.0 %products.3 = (f32[48,2176]{1,0:T(8,128)S(1)}, f32[48,2048]{1,0:T(8,128)S(1)}) custom-call(s32[4]{0:T(128)S(1)} %pad_add_fusion.1.which_ref, bf16[96,512]{1,0:T(8,128)(2,1)S(1)} %get-tuple-element.15.both_ref, f32[48,128]{1,0:T(8,128)S(1)} %get-tuple-element.16.gram_ref, bf16[8,512,1024]{2,1,0:T(8,128)(2,1)S(1)} %copy-done.2, ...), custom_call_target="tpu_custom_call" | custom-call | flops 603979776 | bytes 786432 | tf_op jit(solution)/shard_map/products/pallas_call | solution.py:155
  45.1 4.1 %collective-permute-done.5 = f32[48,1024]{1,0:T(8,128)S(1)} collective-permute-done((f32[48,1024]{1,0:T(8,128)S(1)}, f32[48,1024]{1,0:T(8,128)S(1)}, u32[]{:S(2)}, u32[]{:S(2)}) %collective-permute-start.5) | collective-permute-done | bytes 196640 | tf_op jit(solution)/shard_map/ppermute | solution.py:267
  50.2 3.4 %collective-permute-start.6 = (f32[48,2176]{1,0:T(8,128)S(1)}, f32[48,2176]{1,0:T(8,128)S(1)}, u32[]{:S(2)}, u32[]{:S(2)}) collective-permute-start(f32[48,2176]{1,0:T(8,128)S(1)} %pad_maximum_fusion), channel_id=1, source_target_pairs={{0,16},{4,20},{8,24},{12,28},{16,0},{20,4},{24,8},{28,12},{1,17},{... | collective-permute-start | bytes 1253384 | tf_op jit(solution)/shard_map/ppermute | solution.py:267
  53.5 15.7 %collective-permute-done.6 = f32[48,2176]{1,0:T(8,128)S(1)} collective-permute-done((f32[48,2176]{1,0:T(8,128)S(1)}, f32[48,2176]{1,0:T(8,128)S(1)}, u32[]{:S(2)}, u32[]{:S(2)}) %collective-permute-start.6) | collective-permute-done | bytes 417824 | tf_op jit(solution)/shard_map/ppermute | solution.py:267
  69.4 1.5 %collective-permute-start.9 = (f32[48,1024]{1,0:T(8,128)S(1)}, f32[48,1024]{1,0:T(8,128)S(1)}, u32[]{:S(2)}, u32[]{:S(2)}) collective-permute-start(f32[48,1024]{1,0:T(8,128)S(1)} %get-tuple-element.23), channel_id=1, source_target_pairs={{0,4},{4,0},{8,12},{12,8},{16,20},{20,16},{24,28},{28,24},{1,5},{5... | collective-permute-start | bytes 589832 | tf_op jit(solution)/shard_map/ppermute | solution.py:267
  71.0 4.4 %collective-permute-done.7.refs_1_ = f32[48,1024]{1,0:T(8,128)S(1)} collective-permute-done((f32[48,1024]{1,0:T(8,128)S(1)}, f32[48,1024]{1,0:T(8,128)S(1)}, u32[]{:S(2)}, u32[]{:S(2)}) %collective-permute-start.7) | collective-permute-done | bytes 196640 | tf_op jit(solution)/shard_map/ppermute | solution.py:267
  75.4 1.5 %collective-permute-start.8 = (f32[48,2048]{1,0:T(8,128)S(1)}, f32[48,2048]{1,0:T(8,128)S(1)}, u32[]{:S(2)}, u32[]{:S(2)}) collective-permute-start(f32[48,2048]{1,0:T(8,128)S(1)} %pad_maximum_fusion.1), channel_id=1, source_target_pairs={{0,4},{4,0},{8,12},{12,8},{16,20},{20,16},{24,28},{28,24},{1,5},{5... | collective-permute-start | bytes 1179656 | tf_op jit(solution)/shard_map/ppermute | solution.py:267
  77.6 2.0 %inverse_factor.1.inverse_ref = f32[48,48]{1,0:T(8,128)S(1)} custom-call(f32[48,2176]{1,0:T(8,128)S(1)} %fusion.gram_ref.refs_0_), custom_call_target="tpu_custom_call" | custom-call | flops 20000000 | bytes 49152 | tf_op jit(solution)/shard_map/inverse_factor/pallas_call | solution.py:205
  79.6 2.6 %finish.2.refs_2_ = f32[48,8192]{1,0:T(8,128)} custom-call(s32[4]{0:T(128)S(1)} %pad_add_fusion.3.where_ref, f32[48,48]{1,0:T(8,128)S(1)} %inverse_factor.1.inverse_ref, f32[48,2176]{1,0:T(8,128)S(1)} %fusion.gram_ref.refs_0_, f32[48,1024]{1,0:T(8,128)S(1)} %collective-permute-done.7.refs_1_, f32[48,1024]{1,0:T(8,128)S(1)} %collective-permute-done.9.refs_2_), custom_call_target="tpu_custom_call" | custom-call | flops 56623104 | bytes 1572864 | tf_op jit(solution)/shard_map/finish/pallas_call | solution.py:245
  82.2 2.6 %collective-permute-done.8.refs_0_ = f32[48,2048]{1,0:T(8,128)S(1)} collective-permute-done((f32[48,2048]{1,0:T(8,128)S(1)}, f32[48,2048]{1,0:T(8,128)S(1)}, u32[]{:S(2)}, u32[]{:S(2)}) %collective-permute-start.8) | collective-permute-done | bytes 393248 | tf_op jit(solution)/shard_map/ppermute | solution.py:267
  84.8 1.2 %collective-permute-done.10.refs_1_ = f32[48,2048]{1,0:T(8,128)S(1)} collective-permute-done((f32[48,2048]{1,0:T(8,128)S(1)}, f32[48,2048]{1,0:T(8,128)S(1)}, u32[]{:S(2)}, u32[]{:S(2)}) %collective-permute-start.10) | collective-permute-done | bytes 393248 | tf_op jit(solution)/shard_map/ppermute | solution.py:267
  86.0 2.6 %finish.3 = f32[48,8192]{1,0:T(8,128)} custom-call(s32[4]{0:T(128)S(1)} %pad_add_fusion.where_ref, f32[48,48]{1,0:T(8,128)S(1)} %inverse_factor.1.inverse_ref, f32[48,2048]{1,0:T(8,128)S(1)} %collective-permute-done.8.refs_0_, f32[48,2048]{1,0:T(8,128)S(1)} %collective-permute-done.10.refs_1_, f32[48,8192]{1,0:T(8,128)} %finish.2.refs_2_), custom_call_target="tpu_custom_call", output_to_operand_aliasing={{}: (4, {})} | custom-call | flops 56623104 | bytes 1572864 | tf_op jit(solution)/shard_map/finish/pallas_call | solution.py:245
  (34 shorter events, 5.5 us)
Async XLA Ops:
  8.0 3.2 %copy-start = (bf16[8,512,1024]{2,1,0:T(8,128)(2,1)}, bf16[8,512,1024]{2,1,0:T(8,128)(2,1)S(1)}, u32[]{:S(2)}) copy-start(bf16[8,512,1024]{2,1,0:T(8,128)(2,1)S(1)} %get-tuple-element.17.head_ref) | copy-start | bytes 25165828
  11.2 3.2 %copy-start.3 = (bf16[8,512,1024]{2,1,0:T(8,128)(2,1)}, bf16[8,512,1024]{2,1,0:T(8,128)(2,1)S(1)}, u32[]{:S(2)}) copy-start(bf16[8,512,1024]{2,1,0:T(8,128)(2,1)S(1)} %get-tuple-element.18.rest_ref) | copy-start | bytes 25165828
  14.5 1.4 %collective-permute-start = (f32[48,512]{1,0:T(8,128)S(1)}, f32[48,512]{1,0:T(8,128)S(1)}, u32[]{:S(2)}, u32[]{:S(2)}) collective-permute-start(f32[48,512]{1,0:T(8,128)S(1)} %get-tuple-element.14), channel_id=1, source_target_pairs={{0,1},{1,0},{2,3},{3,2},{4,5},{5,4},{6,7},{7,6},{8,9},{9,8},{10,11... | collective-permute-start | bytes 294920 | tf_op jit(solution)/shard_map/ppermute | solution.py:267
  15.9 6.0 %collective-permute-start.1 = (f32[48,512]{1,0:T(8,128)S(1)}, f32[48,512]{1,0:T(8,128)S(1)}, u32[]{:S(2)}, u32[]{:S(2)}) collective-permute-start(f32[48,512]{1,0:T(8,128)S(1)} %add.75.first_ref), channel_id=1, source_target_pairs={{0,2},{1,3},{2,0},{3,1},{4,6},{5,7},{6,4},{7,5},{8,10},{9,11},{10,... | collective-permute-start | bytes 294920 | tf_op jit(solution)/shard_map/ppermute | solution.py:267
  22.4 3.4 %copy-start.1 = (bf16[8,512,1024]{2,1,0:T(8,128)(2,1)S(1)}, bf16[8,512,1024]{2,1,0:T(8,128)(2,1)}, u32[]{:S(2)}) copy-start(bf16[8,512,1024]{2,1,0:T(8,128)(2,1)} %copy-done) | copy-start | bytes 25165828
  25.7 3.4 %copy-start.4 = (bf16[8,512,1024]{2,1,0:T(8,128)(2,1)S(1)}, bf16[8,512,1024]{2,1,0:T(8,128)(2,1)}, u32[]{:S(2)}) copy-start(bf16[8,512,1024]{2,1,0:T(8,128)(2,1)} %copy-done.3) | copy-start | bytes 25165828
  31.1 12.2 %collective-permute-start.4 = (f32[48,2048]{1,0:T(8,128)S(1)}, f32[48,2048]{1,0:T(8,128)S(1)}, u32[]{:S(2)}, u32[]{:S(2)}) collective-permute-start(f32[48,2048]{1,0:T(8,128)S(1)} %get-tuple-element.22), channel_id=1, source_target_pairs={{0,8},{4,12},{8,0},{12,4},{16,24},{20,28},{24,16},{28,20},{1,9},{5... | collective-permute-start | bytes 1179656 | tf_op jit(solution)/shard_map/ppermute | solution.py:267
  33.0 11.1 %collective-permute-start.2 = (f32[48,2176]{1,0:T(8,128)S(1)}, f32[48,2176]{1,0:T(8,128)S(1)}, u32[]{:S(2)}, u32[]{:S(2)}) collective-permute-start(f32[48,2176]{1,0:T(8,128)S(1)} %get-tuple-element.19.refs_0_), channel_id=1, source_target_pairs={{0,4},{4,0},{8,12},{12,8},{16,20},{20,16},{24,28},{28,24},{1,5},{5... | collective-permute-start | bytes 1253384 | tf_op jit(solution)/shard_map/ppermute | solution.py:267
  34.5 3.4 %copy-start.2 = (bf16[8,512,1024]{2,1,0:T(8,128)(2,1)S(1)}, bf16[8,512,1024]{2,1,0:T(8,128)(2,1)}, u32[]{:S(2)}) copy-start(bf16[8,512,1024]{2,1,0:T(8,128)(2,1)} %copy-done) | copy-start | bytes 25165828
  37.9 3.4 %copy-start.5 = (bf16[8,512,1024]{2,1,0:T(8,128)(2,1)S(1)}, bf16[8,512,1024]{2,1,0:T(8,128)(2,1)}, u32[]{:S(2)}) copy-start(bf16[8,512,1024]{2,1,0:T(8,128)(2,1)} %copy-done.3) | copy-start | bytes 25165828
  43.4 5.7 %collective-permute-start.5 = (f32[48,1024]{1,0:T(8,128)S(1)}, f32[48,1024]{1,0:T(8,128)S(1)}, u32[]{:S(2)}, u32[]{:S(2)}) collective-permute-start(f32[48,1024]{1,0:T(8,128)S(1)} %slice.42), channel_id=1, source_target_pairs={{0,4},{4,0},{8,12},{12,8},{16,20},{20,16},{24,28},{28,24},{1,5},{5... | collective-permute-start | bytes 589832 | tf_op jit(solution)/shard_map/ppermute | solution.py:267
  44.1 6.0 %collective-permute-start.3 = (f32[48,1152]{1,0:T(8,128)S(1)}, f32[48,1152]{1,0:T(8,128)S(1)}, u32[]{:S(2)}, u32[]{:S(2)}) collective-permute-start(f32[48,1152]{1,0:T(8,128)S(1)} %slice.37), channel_id=1, source_target_pairs={{0,8},{4,12},{8,0},{12,4},{16,24},{20,28},{24,16},{28,20},{1,9},{5... | collective-permute-start | bytes 663560 | tf_op jit(solution)/shard_map/ppermute | solution.py:267
  50.2 19.1 %collective-permute-start.6 = (f32[48,2176]{1,0:T(8,128)S(1)}, f32[48,2176]{1,0:T(8,128)S(1)}, u32[]{:S(2)}, u32[]{:S(2)}) collective-permute-start(f32[48,2176]{1,0:T(8,128)S(1)} %pad_maximum_fusion), channel_id=1, source_target_pairs={{0,16},{4,20},{8,24},{12,28},{16,0},{20,4},{24,8},{28,12},{1,17},{... | collective-permute-start | bytes 1253384 | tf_op jit(solution)/shard_map/ppermute | solution.py:267
  69.4 6.0 %collective-permute-start.7 = (f32[48,1024]{1,0:T(8,128)S(1)}, f32[48,1024]{1,0:T(8,128)S(1)}, u32[]{:S(2)}, u32[]{:S(2)}) collective-permute-start(f32[48,1024]{1,0:T(8,128)S(1)} %get-tuple-element.24), channel_id=1, source_target_pairs={{0,8},{4,12},{8,0},{12,4},{16,24},{20,28},{24,16},{28,20},{1,9},{5... | collective-permute-start | bytes 589832 | tf_op jit(solution)/shard_map/ppermute | solution.py:267
  69.4 7.5 %collective-permute-start.9 = (f32[48,1024]{1,0:T(8,128)S(1)}, f32[48,1024]{1,0:T(8,128)S(1)}, u32[]{:S(2)}, u32[]{:S(2)}) collective-permute-start(f32[48,1024]{1,0:T(8,128)S(1)} %get-tuple-element.23), channel_id=1, source_target_pairs={{0,4},{4,0},{8,12},{12,8},{16,20},{20,16},{24,28},{28,24},{1,5},{5... | collective-permute-start | bytes 589832 | tf_op jit(solution)/shard_map/ppermute | solution.py:267
  75.4 9.3 %collective-permute-start.8 = (f32[48,2048]{1,0:T(8,128)S(1)}, f32[48,2048]{1,0:T(8,128)S(1)}, u32[]{:S(2)}, u32[]{:S(2)}) collective-permute-start(f32[48,2048]{1,0:T(8,128)S(1)} %pad_maximum_fusion.1), channel_id=1, source_target_pairs={{0,4},{4,0},{8,12},{12,8},{16,20},{20,16},{24,28},{28,24},{1,5},{5... | collective-permute-start | bytes 1179656 | tf_op jit(solution)/shard_map/ppermute | solution.py:267
  77.0 9.0 %collective-permute-start.10 = (f32[48,2048]{1,0:T(8,128)S(1)}, f32[48,2048]{1,0:T(8,128)S(1)}, u32[]{:S(2)}, u32[]{:S(2)}) collective-permute-start(f32[48,2048]{1,0:T(8,128)S(1)} %pad_maximum_fusion.2), channel_id=1, source_target_pairs={{0,8},{4,12},{8,0},{12,4},{16,24},{20,28},{24,16},{28,20},{1,9},{5... | collective-permute-start | bytes 1179656 | tf_op jit(solution)/shard_map/ppermute | solution.py:267

commit v5 on v4

--- a/solution.py
+++ b/solution.py
@@ -9,7 +9,7 @@
 
 F32 = jnp.float32
 BF16 = jnp.bfloat16
-VMEM_LIMIT = 30 * 1024 * 1024
+VMEM_LIMIT = 24 * 1024 * 1024
 LANES = 128
 CHUNKS = 1
 PANEL = 4
@@ -18,6 +18,7 @@
 ANYWHERE = pl.BlockSpec(memory_space=pl.ANY)
 WHOLE = pl.BlockSpec(memory_space=pltpu.VMEM)
 PARAMS = pltpu.CompilerParams(vmem_limit_bytes=VMEM_LIMIT)
+SMALL = pltpu.CompilerParams(vmem_limit_bytes=VMEM_LIMIT // 4)
 
 
 def split(x):
@@ -116,7 +117,7 @@
             jax.ShapeDtypeStruct((2 * rank, rows), BF16),
             jax.ShapeDtypeStruct((rank, LANES), F32),
         ],
-        compiler_params=PARAMS,
+        compiler_params=SMALL,
         cost_estimate=pl.CostEstimate(
             flops=rows * rank * rank * 18, bytes_accessed=24 * rank * rows, transcendentals=0
         ),
@@ -151,7 +152,6 @@
         if with_gram:
             grams.append((out, sub))
         widths.append(len(blocks) * sub + extra)
-    vmem = pltpu.MemorySpace.VMEM
     return pl.pallas_call(
         functools.partial(product_kernel, plan, grams),
         in_specs=[
@@ -172,8 +172,8 @@
         jnp.stack(which),
         both,
         gram,
-        pltpu.with_memory_space_constraint(head, vmem),
-        pltpu.with_memory_space_constraint(rest, vmem),
+        head,
+        rest,
         *after,
     )
 
@@ -208,7 +208,7 @@
         in_specs=[pl.BlockSpec((rank, LANES), lambda i: (0, start // LANES))],
         out_specs=pl.BlockSpec((rank, rank), lambda i: (0, 0)),
         out_shape=jax.ShapeDtypeStruct((rank, rank), F32),
-        compiler_params=PARAMS,
+        compiler_params=SMALL,
         cost_estimate=pl.CostEstimate(
             flops=20_000_000, bytes_accessed=8 * rank * LANES, transcendentals=rank
         ),
@@ -252,7 +252,7 @@
         ),
         out_shape=jax.ShapeDtypeStruct((rank, total), F32),
         input_output_aliases=aliases,
-        compiler_params=PARAMS,
+        compiler_params=SMALL,
         cost_estimate=pl.CostEstimate(
             flops=6 * rank * rank * width * count,
             bytes_accessed=8 * rank * width * count,

time: 88.9 us -> 88.9 us (level)
  no operation moved by 1% of the time
where the time goes in v5:
time: 88.9 us; the launch traced here: 88.6 us
  waiting for transfers between devices  33 us (37%)
  local copies, waits for them, and re-layouts  20 us (22%)
  Pallas kernels  19.7 us (22%)
  starting transfers between devices  15.2 us (17%)
    ppermute x11, waiting for transfers between devices, swap(): return lax.ppermute(value, axis, [(i, i ^ bit) for i in range(size)])  33 us
    unnamed x12, local copies, waits for them, and re-layouts  20 us
    ppermute x11, starting transfers between devices, swap(): return lax.ppermute(value, axis, [(i, i ^ bit) for i in range(size)])  15.2 us
    pallas_call x1, Pallas kernels, tall_partial(): pl.pallas_call(tall_kernel, in_specs=[pl.BlockSpec(memory_space=hbm)] * 2...  7.99 us
    pallas_call x2, Pallas kernels, finish(): pl.pallas_call(functools.partial(finish_kernel, [piece[1:] for piece in p...  5.21 us
    pallas_call x2, Pallas kernels, products(): pl.pallas_call(functools.partial(product_kernel, plan, grams), in_specs=[...  4.03 us
    pallas_call x1, Pallas kernels, inverse_factor(): pl.pallas_call(inverse_kernel, grid=(1,), in_specs=[pl.BlockSpec((rank, L...  2.01 us
  transfers between devices with their start and end apart: 11, of which 8 were waited for; matrix products, arithmetic and copies ran while one was open for 1% of the time, Pallas kernels for 7%

profile of v5, /device:TPU:0, one launch (start us, length us, event | category | flops | bytes accessed | tf_op | source)
XLA Modules:
  0.0 88.6 jit_solution(11787470997258162968)
XLA Ops:
  0.0 8.0 %tall_partial.1 = (f32[48,512]{1,0:T(8,128)S(1)}, bf16[8,512,1024]{2,1,0:T(8,128)(2,1)S(1)}, bf16[8,512,1024]{2,1,0:T(8,128)(2,1)S(1)}) custom-call(f32[512,8192]{1,0:T(8,128)} %x_hbm.1, f32[48,8192]{1,0:T(8,128)} %bitcast.9), custom_call_target="tpu_custom_call" | custom-call | flops 1207959552 | bytes 16777216 | tf_op jit(solution)/shard_map/tall_partial/pallas_call | solution.py:68
  8.0 3.2 %copy-done = bf16[8,512,1024]{2,1,0:T(8,128)(2,1)} copy-done((bf16[8,512,1024]{2,1,0:T(8,128)(2,1)}, bf16[8,512,1024]{2,1,0:T(8,128)(2,1)S(1)}, u32[]{:S(2)}) %copy-start) | copy-done | bytes 8388632
  11.3 3.2 %copy-done.3 = bf16[8,512,1024]{2,1,0:T(8,128)(2,1)} copy-done((bf16[8,512,1024]{2,1,0:T(8,128)(2,1)}, bf16[8,512,1024]{2,1,0:T(8,128)(2,1)S(1)}, u32[]{:S(2)}) %copy-start.3) | copy-done | bytes 8388632
  15.9 2.9 %collective-permute-start.1 = (f32[48,512]{1,0:T(8,128)S(1)}, f32[48,512]{1,0:T(8,128)S(1)}, u32[]{:S(2)}, u32[]{:S(2)}) collective-permute-start(f32[48,512]{1,0:T(8,128)S(1)} %add.75.first_ref), channel_id=1, source_target_pairs={{0,2},{1,3},{2,0},{3,1},{4,6},{5,7},{6,4},{7,5},{8,10},{9,11},{10,... | collective-permute-start | bytes 294920 | tf_op jit(solution)/shard_map/ppermute | solution.py:267
  18.9 3.0 %collective-permute-done.1.second_ref = f32[48,512]{1,0:T(8,128)S(1)} collective-permute-done((f32[48,512]{1,0:T(8,128)S(1)}, f32[48,512]{1,0:T(8,128)S(1)}, u32[]{:S(2)}, u32[]{:S(2)}) %collective-permute-start.1) | collective-permute-done | bytes 98336 | tf_op jit(solution)/shard_map/ppermute | solution.py:267
  22.4 3.4 %copy-done.1 = bf16[8,512,1024]{2,1,0:T(8,128)(2,1)S(1)} copy-done((bf16[8,512,1024]{2,1,0:T(8,128)(2,1)S(1)}, bf16[8,512,1024]{2,1,0:T(8,128)(2,1)}, u32[]{:S(2)}) %copy-start.1) | copy-done | bytes 8388632
  25.7 3.4 %copy-done.4 = bf16[8,512,1024]{2,1,0:T(8,128)(2,1)S(1)} copy-done((bf16[8,512,1024]{2,1,0:T(8,128)(2,1)S(1)}, bf16[8,512,1024]{2,1,0:T(8,128)(2,1)}, u32[]{:S(2)}) %copy-start.4) | copy-done | bytes 8388632
  29.1 2.0 %products.2 = (f32[48,2176]{1,0:T(8,128)S(1)}, f32[48,2048]{1,0:T(8,128)S(1)}) custom-call(s32[4]{0:T(128)S(1)} %pad_add_fusion.2.which_ref, bf16[96,512]{1,0:T(8,128)(2,1)S(1)} %get-tuple-element.15.both_ref, f32[48,128]{1,0:T(8,128)S(1)} %get-tuple-element.16.gram_ref, bf16[8,512,1024]{2,1,0:T(8,128)(2,1)S(1)} %copy-done.1, bf16[8,512,1024]{2,1,0:T(8,128)(2,1)S(1)} %copy-done.4), custom_call_target="tpu_custom_call" | custom-call | flops 603979776 | bytes 786432 | tf_op jit(solution)/shard_map/products/pallas_call | solution.py:155
  31.1 1.8 %collective-permute-start.4 = (f32[48,2048]{1,0:T(8,128)S(1)}, f32[48,2048]{1,0:T(8,128)S(1)}, u32[]{:S(2)}, u32[]{:S(2)}) collective-permute-start(f32[48,2048]{1,0:T(8,128)S(1)} %get-tuple-element.22), channel_id=1, source_target_pairs={{0,8},{4,12},{8,0},{12,4},{16,24},{20,28},{24,16},{28,20},{1,9},{5... | collective-permute-start | bytes 1179656 | tf_op jit(solution)/shard_map/ppermute | solution.py:267
  33.0 1.5 %collective-permute-start.2 = (f32[48,2176]{1,0:T(8,128)S(1)}, f32[48,2176]{1,0:T(8,128)S(1)}, u32[]{:S(2)}, u32[]{:S(2)}) collective-permute-start(f32[48,2176]{1,0:T(8,128)S(1)} %get-tuple-element.19.refs_0_), channel_id=1, source_target_pairs={{0,4},{4,0},{8,12},{12,8},{16,20},{20,16},{24,28},{28,24},{1,5},{5... | collective-permute-start | bytes 1253384 | tf_op jit(solution)/shard_map/ppermute | solution.py:267
  34.5 3.4 %copy-done.2 = bf16[8,512,1024]{2,1,0:T(8,128)(2,1)S(1)} copy-done((bf16[8,512,1024]{2,1,0:T(8,128)(2,1)S(1)}, bf16[8,512,1024]{2,1,0:T(8,128)(2,1)}, u32[]{:S(2)}) %copy-start.2) | copy-done | bytes 8388632
  37.9 3.4 %copy-done.5 = bf16[8,512,1024]{2,1,0:T(8,128)(2,1)S(1)} copy-done((bf16[8,512,1024]{2,1,0:T(8,128)(2,1)S(1)}, bf16[8,512,1024]{2,1,0:T(8,128)(2,1)}, u32[]{:S(2)}) %copy-start.5) | copy-done | bytes 8388632
  41.3 2.0 %products.3 = (f32[48,2176]{1,0:T(8,128)S(1)}, f32[48,2048]{1,0:T(8,128)S(1)}) custom-call(s32[4]{0:T(128)S(1)} %pad_add_fusion.1.which_ref, bf16[96,512]{1,0:T(8,128)(2,1)S(1)} %get-tuple-element.15.both_ref, f32[48,128]{1,0:T(8,128)S(1)} %get-tuple-element.16.gram_ref, bf16[8,512,1024]{2,1,0:T(8,128)(2,1)S(1)} %copy-done.2, ...), custom_call_target="tpu_custom_call" | custom-call | flops 603979776 | bytes 786432 | tf_op jit(solution)/shard_map/products/pallas_call | solution.py:155
  45.1 4.1 %collective-permute-done.5 = f32[48,1024]{1,0:T(8,128)S(1)} collective-permute-done((f32[48,1024]{1,0:T(8,128)S(1)}, f32[48,1024]{1,0:T(8,128)S(1)}, u32[]{:S(2)}, u32[]{:S(2)}) %collective-permute-start.5) | collective-permute-done | bytes 196640 | tf_op jit(solution)/shard_map/ppermute | solution.py:267
  50.2 3.4 %collective-permute-start.6 = (f32[48,2176]{1,0:T(8,128)S(1)}, f32[48,2176]{1,0:T(8,128)S(1)}, u32[]{:S(2)}, u32[]{:S(2)}) collective-permute-start(f32[48,2176]{1,0:T(8,128)S(1)} %pad_maximum_fusion), channel_id=1, source_target_pairs={{0,16},{4,20},{8,24},{12,28},{16,0},{20,4},{24,8},{28,12},{1,17},{... | collective-permute-start | bytes 1253384 | tf_op jit(solution)/shard_map/ppermute | solution.py:267
  53.5 15.7 %collective-permute-done.6 = f32[48,2176]{1,0:T(8,128)S(1)} collective-permute-done((f32[48,2176]{1,0:T(8,128)S(1)}, f32[48,2176]{1,0:T(8,128)S(1)}, u32[]{:S(2)}, u32[]{:S(2)}) %collective-permute-start.6) | collective-permute-done | bytes 417824 | tf_op jit(solution)/shard_map/ppermute | solution.py:267
  69.4 1.5 %collective-permute-start.9 = (f32[48,1024]{1,0:T(8,128)S(1)}, f32[48,1024]{1,0:T(8,128)S(1)}, u32[]{:S(2)}, u32[]{:S(2)}) collective-permute-start(f32[48,1024]{1,0:T(8,128)S(1)} %get-tuple-element.23), channel_id=1, source_target_pairs={{0,4},{4,0},{8,12},{12,8},{16,20},{20,16},{24,28},{28,24},{1,5},{5... | collective-permute-start | bytes 589832 | tf_op jit(solution)/shard_map/ppermute | solution.py:267
  71.0 4.4 %collective-permute-done.7.refs_1_ = f32[48,1024]{1,0:T(8,128)S(1)} collective-permute-done((f32[48,1024]{1,0:T(8,128)S(1)}, f32[48,1024]{1,0:T(8,128)S(1)}, u32[]{:S(2)}, u32[]{:S(2)}) %collective-permute-start.7) | collective-permute-done | bytes 196640 | tf_op jit(solution)/shard_map/ppermute | solution.py:267
  75.4 1.5 %collective-permute-start.8 = (f32[48,2048]{1,0:T(8,128)S(1)}, f32[48,2048]{1,0:T(8,128)S(1)}, u32[]{:S(2)}, u32[]{:S(2)}) collective-permute-start(f32[48,2048]{1,0:T(8,128)S(1)} %pad_maximum_fusion.1), channel_id=1, source_target_pairs={{0,4},{4,0},{8,12},{12,8},{16,20},{20,16},{24,28},{28,24},{1,5},{5... | collective-permute-start | bytes 1179656 | tf_op jit(solution)/shard_map/ppermute | solution.py:267
  77.6 2.0 %inverse_factor.1.inverse_ref = f32[48,48]{1,0:T(8,128)S(1)} custom-call(f32[48,2176]{1,0:T(8,128)S(1)} %fusion.gram_ref.refs_0_), custom_call_target="tpu_custom_call" | custom-call | flops 20000000 | bytes 49152 | tf_op jit(solution)/shard_map/inverse_factor/pallas_call | solution.py:205
  79.6 2.6 %finish.2.refs_2_ = f32[48,8192]{1,0:T(8,128)} custom-call(s32[4]{0:T(128)S(1)} %pad_add_fusion.3.where_ref, f32[48,48]{1,0:T(8,128)S(1)} %inverse_factor.1.inverse_ref, f32[48,2176]{1,0:T(8,128)S(1)} %fusion.gram_ref.refs_0_, f32[48,1024]{1,0:T(8,128)S(1)} %collective-permute-done.7.refs_1_, f32[48,1024]{1,0:T(8,128)S(1)} %collective-permute-done.9.refs_2_), custom_call_target="tpu_custom_call" | custom-call | flops 56623104 | bytes 1572864 | tf_op jit(solution)/shard_map/finish/pallas_call | solution.py:245
  82.2 2.6 %collective-permute-done.8.refs_0_ = f32[48,2048]{1,0:T(8,128)S(1)} collective-permute-done((f32[48,2048]{1,0:T(8,128)S(1)}, f32[48,2048]{1,0:T(8,128)S(1)}, u32[]{:S(2)}, u32[]{:S(2)}) %collective-permute-start.8) | collective-permute-done | bytes 393248 | tf_op jit(solution)/shard_map/ppermute | solution.py:267
  84.8 1.2 %collective-permute-done.10.refs_1_ = f32[48,2048]{1,0:T(8,128)S(1)} collective-permute-done((f32[48,2048]{1,0:T(8,128)S(1)}, f32[48,2048]{1,0:T(8,128)S(1)}, u32[]{:S(2)}, u32[]{:S(2)}) %collective-permute-start.10) | collective-permute-done | bytes 393248 | tf_op jit(solution)/shard_map/ppermute | solution.py:267
  86.0 2.6 %finish.3 = f32[48,8192]{1,0:T(8,128)} custom-call(s32[4]{0:T(128)S(1)} %pad_add_fusion.where_ref, f32[48,48]{1,0:T(8,128)S(1)} %inverse_factor.1.inverse_ref, f32[48,2048]{1,0:T(8,128)S(1)} %collective-permute-done.8.refs_0_, f32[48,2048]{1,0:T(8,128)S(1)} %collective-permute-done.10.refs_1_, f32[48,8192]{1,0:T(8,128)} %finish.2.refs_2_), custom_call_target="tpu_custom_call", output_to_operand_aliasing={{}: (4, {})} | custom-call | flops 56623104 | bytes 1572864 | tf_op jit(solution)/shard_map/finish/pallas_call | solution.py:245
  (34 shorter events, 5.5 us)
Async XLA Ops:
  8.0 3.2 %copy-start = (bf16[8,512,1024]{2,1,0:T(8,128)(2,1)}, bf16[8,512,1024]{2,1,0:T(8,128)(2,1)S(1)}, u32[]{:S(2)}) copy-start(bf16[8,512,1024]{2,1,0:T(8,128)(2,1)S(1)} %get-tuple-element.17.head_ref) | copy-start | bytes 25165828
  11.2 3.2 %copy-start.3 = (bf16[8,512,1024]{2,1,0:T(8,128)(2,1)}, bf16[8,512,1024]{2,1,0:T(8,128)(2,1)S(1)}, u32[]{:S(2)}) copy-start(bf16[8,512,1024]{2,1,0:T(8,128)(2,1)S(1)} %get-tuple-element.18.rest_ref) | copy-start | bytes 25165828
  14.5 1.4 %collective-permute-start = (f32[48,512]{1,0:T(8,128)S(1)}, f32[48,512]{1,0:T(8,128)S(1)}, u32[]{:S(2)}, u32[]{:S(2)}) collective-permute-start(f32[48,512]{1,0:T(8,128)S(1)} %get-tuple-element.14), channel_id=1, source_target_pairs={{0,1},{1,0},{2,3},{3,2},{4,5},{5,4},{6,7},{7,6},{8,9},{9,8},{10,11... | collective-permute-start | bytes 294920 | tf_op jit(solution)/shard_map/ppermute | solution.py:267
  15.9 6.0 %collective-permute-start.1 = (f32[48,512]{1,0:T(8,128)S(1)}, f32[48,512]{1,0:T(8,128)S(1)}, u32[]{:S(2)}, u32[]{:S(2)}) collective-permute-start(f32[48,512]{1,0:T(8,128)S(1)} %add.75.first_ref), channel_id=1, source_target_pairs={{0,2},{1,3},{2,0},{3,1},{4,6},{5,7},{6,4},{7,5},{8,10},{9,11},{10,... | collective-permute-start | bytes 294920 | tf_op jit(solution)/shard_map/ppermute | solution.py:267
  22.4 3.4 %copy-start.1 = (bf16[8,512,1024]{2,1,0:T(8,128)(2,1)S(1)}, bf16[8,512,1024]{2,1,0:T(8,128)(2,1)}, u32[]{:S(2)}) copy-start(bf16[8,512,1024]{2,1,0:T(8,128)(2,1)} %copy-done) | copy-start | bytes 25165828
  25.7 3.4 %copy-start.4 = (bf16[8,512,1024]{2,1,0:T(8,128)(2,1)S(1)}, bf16[8,512,1024]{2,1,0:T(8,128)(2,1)}, u32[]{:S(2)}) copy-start(bf16[8,512,1024]{2,1,0:T(8,128)(2,1)} %copy-done.3) | copy-start | bytes 25165828
  31.1 12.2 %collective-permute-start.4 = (f32[48,2048]{1,0:T(8,128)S(1)}, f32[48,2048]{1,0:T(8,128)S(1)}, u32[]{:S(2)}, u32[]{:S(2)}) collective-permute-start(f32[48,2048]{1,0:T(8,128)S(1)} %get-tuple-element.22), channel_id=1, source_target_pairs={{0,8},{4,12},{8,0},{12,4},{16,24},{20,28},{24,16},{28,20},{1,9},{5... | collective-permute-start | bytes 1179656 | tf_op jit(solution)/shard_map/ppermute | solution.py:267
  33.0 11.1 %collective-permute-start.2 = (f32[48,2176]{1,0:T(8,128)S(1)}, f32[48,2176]{1,0:T(8,128)S(1)}, u32[]{:S(2)}, u32[]{:S(2)}) collective-permute-start(f32[48,2176]{1,0:T(8,128)S(1)} %get-tuple-element.19.refs_0_), channel_id=1, source_target_pairs={{0,4},{4,0},{8,12},{12,8},{16,20},{20,16},{24,28},{28,24},{1,5},{5... | collective-permute-start | bytes 1253384 | tf_op jit(solution)/shard_map/ppermute | solution.py:267
  34.5 3.4 %copy-start.2 = (bf16[8,512,1024]{2,1,0:T(8,128)(2,1)S(1)}, bf16[8,512,1024]{2,1,0:T(8,128)(2,1)}, u32[]{:S(2)}) copy-start(bf16[8,512,1024]{2,1,0:T(8,128)(2,1)} %copy-done) | copy-start | bytes 25165828
  37.9 3.4 %copy-start.5 = (bf16[8,512,1024]{2,1,0:T(8,128)(2,1)S(1)}, bf16[8,512,1024]{2,1,0:T(8,128)(2,1)}, u32[]{:S(2)}) copy-start(bf16[8,512,1024]{2,1,0:T(8,128)(2,1)} %copy-done.3) | copy-start | bytes 25165828
  43.4 5.7 %collective-permute-start.5 = (f32[48,1024]{1,0:T(8,128)S(1)}, f32[48,1024]{1,0:T(8,128)S(1)}, u32[]{:S(2)}, u32[]{:S(2)}) collective-permute-start(f32[48,1024]{1,0:T(8,128)S(1)} %slice.42), channel_id=1, source_target_pairs={{0,4},{4,0},{8,12},{12,8},{16,20},{20,16},{24,28},{28,24},{1,5},{5... | collective-permute-start | bytes 589832 | tf_op jit(solution)/shard_map/ppermute | solution.py:267
  44.1 6.0 %collective-permute-start.3 = (f32[48,1152]{1,0:T(8,128)S(1)}, f32[48,1152]{1,0:T(8,128)S(1)}, u32[]{:S(2)}, u32[]{:S(2)}) collective-permute-start(f32[48,1152]{1,0:T(8,128)S(1)} %slice.37), channel_id=1, source_target_pairs={{0,8},{4,12},{8,0},{12,4},{16,24},{20,28},{24,16},{28,20},{1,9},{5... | collective-permute-start | bytes 663560 | tf_op jit(solution)/shard_map/ppermute | solution.py:267
  50.2 19.1 %collective-permute-start.6 = (f32[48,2176]{1,0:T(8,128)S(1)}, f32[48,2176]{1,0:T(8,128)S(1)}, u32[]{:S(2)}, u32[]{:S(2)}) collective-permute-start(f32[48,2176]{1,0:T(8,128)S(1)} %pad_maximum_fusion), channel_id=1, source_target_pairs={{0,16},{4,20},{8,24},{12,28},{16,0},{20,4},{24,8},{28,12},{1,17},{... | collective-permute-start | bytes 1253384 | tf_op jit(solution)/shard_map/ppermute | solution.py:267
  69.4 6.0 %collective-permute-start.7 = (f32[48,1024]{1,0:T(8,128)S(1)}, f32[48,1024]{1,0:T(8,128)S(1)}, u32[]{:S(2)}, u32[]{:S(2)}) collective-permute-start(f32[48,1024]{1,0:T(8,128)S(1)} %get-tuple-element.24), channel_id=1, source_target_pairs={{0,8},{4,12},{8,0},{12,4},{16,24},{20,28},{24,16},{28,20},{1,9},{5... | collective-permute-start | bytes 589832 | tf_op jit(solution)/shard_map/ppermute | solution.py:267
  69.4 7.5 %collective-permute-start.9 = (f32[48,1024]{1,0:T(8,128)S(1)}, f32[48,1024]{1,0:T(8,128)S(1)}, u32[]{:S(2)}, u32[]{:S(2)}) collective-permute-start(f32[48,1024]{1,0:T(8,128)S(1)} %get-tuple-element.23), channel_id=1, source_target_pairs={{0,4},{4,0},{8,12},{12,8},{16,20},{20,16},{24,28},{28,24},{1,5},{5... | collective-permute-start | bytes 589832 | tf_op jit(solution)/shard_map/ppermute | solution.py:267
  75.4 9.3 %collective-permute-start.8 = (f32[48,2048]{1,0:T(8,128)S(1)}, f32[48,2048]{1,0:T(8,128)S(1)}, u32[]{:S(2)}, u32[]{:S(2)}) collective-permute-start(f32[48,2048]{1,0:T(8,128)S(1)} %pad_maximum_fusion.1), channel_id=1, source_target_pairs={{0,4},{4,0},{8,12},{12,8},{16,20},{20,16},{24,28},{28,24},{1,5},{5... | collective-permute-start | bytes 1179656 | tf_op jit(solution)/shard_map/ppermute | solution.py:267
  77.0 9.0 %collective-permute-start.10 = (f32[48,2048]{1,0:T(8,128)S(1)}, f32[48,2048]{1,0:T(8,128)S(1)}, u32[]{:S(2)}, u32[]{:S(2)}) collective-permute-start(f32[48,2048]{1,0:T(8,128)S(1)} %pad_maximum_fusion.2), channel_id=1, source_target_pairs={{0,8},{4,12},{8,0},{12,4},{16,24},{20,28},{24,16},{28,20},{1,9},{5... | collective-permute-start | bytes 1179656 | tf_op jit(solution)/shard_map/ppermute | solution.py:267

commit v6 on v4

v6 whole, which is shorter than its diff:
```python
import functools

import jax
import jax.numpy as jnp
from jax import lax
from jax.experimental import pallas as pl
from jax.experimental.pallas import tpu as pltpu
from jax.sharding import PartitionSpec as P

F32 = jnp.float32
BF16 = jnp.bfloat16
VMEM_LIMIT = 40 * 1024 * 1024
LANES = 128
CHUNKS = 1
AHEAD = 6
UNIT = 512
PANEL = 4
LAST = (((1,), (1,)), ((), ()))
PLAIN = (((1,), (0,)), ((), ()))
ANYWHERE = pl.BlockSpec(memory_space=pl.ANY)
HBM = pl.BlockSpec(memory_space=pltpu.MemorySpace.HBM)
WHOLE = pl.BlockSpec(memory_space=pltpu.VMEM)
TABLE = pl.BlockSpec(memory_space=pltpu.SMEM)
PARAMS = pltpu.CompilerParams(vmem_limit_bytes=VMEM_LIMIT)


def split(x):
    head = x.astype(BF16)
    return head, (x - head.astype(F32)).astype(BF16)


def dot(a, b, dims):
    return lax.dot_general(a, b, dims, preferred_element_type=F32)


def in_hbm(x):
    return pltpu.with_memory_space_constraint(x, pltpu.MemorySpace.HBM)


def stream(copies, use):
    for copy in copies[:AHEAD]:
        copy.start()
    for k, copy in enumerate(copies):
        copy.wait()
        if k + AHEAD < len(copies):
            copies[k + AHEAD].start()
        use(k)


def tall_kernel(x_hbm, s_hbm, out_ref, x_buf, s_buf, x_sems, s_sem):
    blocks, _, unit = x_buf.shape
    rank = s_hbm.shape[0]
    copies = [
        pltpu.make_async_copy(x_hbm.at[:, pl.ds(k * unit, unit)], x_buf.at[k], x_sems.at[k])
        for k in range(blocks)
    ]
    sketch = pltpu.make_async_copy(s_hbm, s_buf, s_sem)
    sketch.start()

    def use(k):
        if k == 0:
            sketch.wait()
        s_head, s_rest = split(s_buf[:, k * unit : (k + 1) * unit])
        s_both = jnp.concatenate([s_head, s_rest], axis=0)
        x_head, x_rest = split(x_buf[k])
        both = dot(s_both, x_head, LAST)
        part = both[:rank] + (both[rank:] + dot(s_head, x_rest, LAST))
        if k == 0:
            out_ref[...] = part
        else:
            out_ref[...] += part

    stream(copies, use)


def tall_partial(probes, sketch_t):
    rows, cols = probes.shape
    rank = sketch_t.shape[0]
    unit = min(UNIT, cols)
    blocks = cols // unit
    return pl.pallas_call(
        tall_kernel,
        in_specs=[HBM, HBM],
        out_specs=WHOLE,
        out_shape=jax.ShapeDtypeStruct((rank, rows), F32),
        scratch_shapes=[
            pltpu.VMEM((blocks, rows, unit), F32),
            pltpu.VMEM((rank, cols), F32),
            pltpu.SemaphoreType.DMA((blocks,)),
            pltpu.SemaphoreType.DMA,
        ],
        compiler_params=PARAMS,
        cost_estimate=pl.CostEstimate(
            flops=6 * rows * cols * rank, bytes_accessed=4 * rows * cols, transcendentals=0
        ),
        name="tall_partial",
    )(in_hbm(probes), in_hbm(sketch_t))


def multiply_blocks(both_ref, which_ref, x_hbm, x_buf, sems, plan, outs):
    rank = outs[0].shape[0]
    unit = x_buf.shape[2]
    copies = [
        pltpu.make_async_copy(
            x_hbm.at[:, pl.ds(pl.multiple_of(which_ref[k] * unit, unit), unit)],
            x_buf.at[k],
            sems.at[k],
        )
        for k in range(len(plan))
    ]

    def use(k):
        both = both_ref[...]
        x_head, x_rest = split(x_buf[k])
        first = dot(both, x_head, PLAIN)
        second = dot(both[:rank], x_rest, PLAIN)
        out, offset = plan[k]
        outs[out][:, offset : offset + unit] = first[:rank] + (first[rank:] + second)

    return copies, use


def first_kernel(plan, grams, which_ref, one_ref, two_ref, x_hbm, both_ref, gram_ref, *refs):
    outs, (x_buf, sems) = refs[:-2], refs[-2:]
    copies, use = multiply_blocks(both_ref, which_ref, x_hbm, x_buf, sems, plan, outs)

    def use_first(k):
        if k == 0:
            tall = one_ref[...] + two_ref[...]
            head, rest = split(tall)
            both_ref[...] = jnp.concatenate([head, rest], axis=0)
        use(k)

    stream(copies, use_first)
    tall = one_ref[...] + two_ref[...]
    r = tall.shape[0]
    head, rest = split(tall)
    tail = (tall - head.astype(F32) - rest.astype(F32)).astype(BF16)
    three = jnp.concatenate([head, rest, tail], axis=0)
    g = dot(three, three, LAST)
    cross = g[:r, r : 2 * r] + g[r : 2 * r, :r]
    small = g[:r, 2 * r :] + g[2 * r :, :r] + g[r : 2 * r, r : 2 * r]
    gram = g[:r, :r] + (cross + small)
    gram_ref[...] = jnp.concatenate([gram, jnp.zeros((r, LANES - r), F32)], axis=1)
    for out, offset in grams:
        outs[out][:, offset : offset + LANES] = gram_ref[...]


def rest_kernel(plan, grams, which_ref, both_ref, gram_ref, x_hbm, after_ref, *refs):
    outs, (x_buf, sems) = refs[:-2], refs[-2:]
    copies, use = multiply_blocks(both_ref, which_ref, x_hbm, x_buf, sems, plan, outs)
    stream(copies, use)
    for out, offset in grams:
        outs[out][:, offset : offset + LANES] = gram_ref[...]


def layout(outputs, sub):
    unit = min(UNIT, sub)
    plan, grams, widths, which = [], [], [], []
    for out, (blocks, with_gram) in enumerate(outputs):
        extra = LANES if with_gram else 0
        for j, block in enumerate(blocks):
            for part in range(sub // unit):
                plan.append((out, j * sub + part * unit + (extra if j else 0)))
                which.append(block * (sub // unit) + part)
        if with_gram:
            grams.append((out, sub))
        widths.append(len(blocks) * sub + extra)
    return unit, plan, grams, widths, jnp.stack(which)


def products(kernel, inputs, in_specs, made, probes, outputs, sub, name):
    rows = probes.shape[0]
    rank = inputs[1].shape[0]
    unit, plan, grams, widths, which = layout(outputs, sub)
    shapes = [*made, *[jax.ShapeDtypeStruct((rank, width), F32) for width in widths]]
    return pl.pallas_call(
        functools.partial(kernel, plan, grams),
        in_specs=[TABLE, *in_specs],
        out_specs=[WHOLE] * len(shapes),
        out_shape=shapes,
        scratch_shapes=[
            pltpu.VMEM((len(plan), rows, unit), F32),
            pltpu.SemaphoreType.DMA((len(plan),)),
        ],
        compiler_params=PARAMS,
        cost_estimate=pl.CostEstimate(
            flops=6 * rows * rank * unit * len(plan),
            bytes_accessed=4 * rows * unit * len(plan),
            transcendentals=0,
        ),
        name=name,
    )(which, *inputs)


def first_products(one, two, probes, outputs, sub):
    rank, rows = one.shape
    made = [
        jax.ShapeDtypeStruct((2 * rank, rows), BF16),
        jax.ShapeDtypeStruct((rank, LANES), F32),
    ]
    both, gram, *outs = products(
        first_kernel,
        [one, two, in_hbm(probes)],
        [WHOLE, WHOLE, HBM],
        made,
        probes,
        outputs,
        sub,
        "first_products",
    )
    return both, gram, outs


def rest_products(both, gram, probes, outputs, sub, after):
    return products(
        rest_kernel,
        [both, gram, in_hbm(probes), after],
        [WHOLE, WHOLE, HBM, ANYWHERE],
        [],
        probes,
        outputs,
        sub,
        "rest_products",
    )


def inverse_kernel(gram_ref, out_ref):
    rank = out_ref.shape[0]
    rows = lax.broadcasted_iota(jnp.int32, (rank, LANES), 0)
    cols = lax.broadcasted_iota(jnp.int32, (rank, LANES), 1)
    work = jnp.where(cols < rank, gram_ref[...], (cols == rows + rank).astype(F32))
    scale = jnp.ones((rank, LANES), F32)
    for start in range(0, rank, PANEL):
        panel = [
            jnp.broadcast_to(work[:, k : k + 1], (rank, LANES))
            for k in range(start, start + PANEL)
        ]
        for j in range(PANEL):
            k = start + j
            over = 1.0 / panel[j][k : k + 1, :]
            scale = jnp.where(rows == k, over, scale)
            factor = jnp.where(rows > k, panel[j] * over, 0.0)
            work = work - factor * work[k : k + 1, :]
            for later in range(j + 1, PANEL):
                panel[later] = panel[later] - factor * panel[later][k : k + 1, :]
    out_ref[...] = (work * jnp.sqrt(scale))[:, rank : 2 * rank]


def inverse_factor(chunk, start):
    rank = chunk.shape[0]
    return pl.pallas_call(
        inverse_kernel,
        grid=(1,),
        in_specs=[pl.BlockSpec((rank, LANES), lambda i: (0, start // LANES))],
        out_specs=pl.BlockSpec((rank, rank), lambda i: (0, 0)),
        out_shape=jax.ShapeDtypeStruct((rank, rank), F32),
        compiler_params=PARAMS,
        cost_estimate=pl.CostEstimate(
            flops=20_000_000, bytes_accessed=8 * rank * LANES, transcendentals=rank
        ),
        name="inverse_factor",
    )(chunk)


def finish_kernel(plan, where_ref, inverse_ref, *refs):
    out_hbm, buf, sems = refs[-3:]
    _, rank, width = buf.shape
    head, rest = split(inverse_ref[...])
    both = jnp.concatenate([head, rest], axis=0)
    copies = []
    for k, (source, offset) in enumerate(plan):
        p_head, p_rest = split(refs[source][:, offset : offset + width])
        first = dot(both, p_head, PLAIN)
        buf[k] = first[:rank] + (first[rank:] + dot(head, p_rest, PLAIN))
        where = pl.ds(pl.multiple_of(where_ref[k] * width, width), width)
        copies.append(pltpu.make_async_copy(buf.at[k], out_hbm.at[:, where], sems.at[k]))
        copies[k].start()
    for copy in copies:
        copy.wait()


def finish(inverse, sources, pieces, width, total, before=None):
    rank = inverse.shape[0]
    count = len(pieces)
    in_specs = [TABLE, WHOLE, *[WHOLE] * len(sources)]
    args = [jnp.stack([piece[0] for piece in pieces]), inverse, *sources]
    aliases = {}
    if before is not None:
        in_specs.append(HBM)
        args.append(before)
        aliases = {len(args) - 1: 0}
    return pl.pallas_call(
        functools.partial(finish_kernel, [piece[1:] for piece in pieces]),
        in_specs=in_specs,
        out_specs=HBM,
        out_shape=jax.ShapeDtypeStruct((rank, total), F32),
        scratch_shapes=[
            pltpu.VMEM((count, rank, width), F32),
            pltpu.SemaphoreType.DMA((count,)),
        ],
        input_output_aliases=aliases,
        compiler_params=PARAMS,
        cost_estimate=pl.CostEstimate(
            flops=6 * rank * rank * width * count,
            bytes_accessed=8 * rank * width * count,
            transcendentals=0,
        ),
        name="finish",
    )(*args)


def body(n_pos, n_pix, probes, sketch):
    def swap(value, axis, size, bit):
        return lax.ppermute(value, axis, [(i, i ^ bit) for i in range(size)])

    def over(value, bit):
        return swap(value, "pos", n_pos, bit)

    me = lax.axis_index("pos").astype(jnp.int32)
    near, far = me & 1, (me >> 1) & 1
    cols = probes.shape[1]
    width = cols // (8 * CHUNKS)

    tall = tall_partial(probes, sketch.T)
    bit = 1
    while 2 * bit < n_pix:
        tall = tall + swap(tall, "pix", n_pix, bit)
        bit *= 2
    other = swap(tall, "pix", n_pix, bit)

    def block_a(c, p, q):
        return 8 * c + 2 * (near ^ p) + (far ^ q)

    def block_b(c, p, q):
        return 8 * c + 4 + 2 * (far ^ p) + (near ^ q)

    def outputs(c, p):
        return [
            ([block_a(c, p, 1), block_a(c, p, 0)], c == 0),
            ([block_b(c, p, 1), block_b(c, p, 0)], False),
        ]

    both, gram, first = first_products(tall, other, probes, outputs(0, 1), width)
    plan = [(c, p) for c in range(CHUNKS) for p in (1, 0) if (c, p) != (0, 1)]
    rest = rest_products(
        both, gram, probes, [out for c, p in plan for out in outputs(c, p)], width, first[0]
    )
    made = {(0, 1): first}
    made.update({key: rest[2 * k : 2 * k + 2] for k, key in enumerate(plan)})

    inverse, out = None, None
    for c in range(CHUNKS):
        g = LANES if c == 0 else 0
        away_a, away_b = made[c, 1]
        own_a, own_b = made[c, 0]
        sum_a = own_a + over(away_a, 1)
        sum_b = own_b + over(away_b, 2)
        got_a = over(sum_a[:, : width + g], 2)
        got_b = over(sum_b[:, :width], 1)
        whole = jnp.concatenate(
            [
                sum_a[:, width + g :] + got_a[:, :width],
                sum_a[:, width : width + g] + got_a[:, width:],
                sum_b[:, width:] + got_b,
            ],
            axis=1,
        )
        bit = 4
        while bit < n_pos:
            whole = whole + over(whole, bit)
            bit *= 2
        if c == 0:
            inverse = inverse_factor(whole, width)
        mine_a, mine_b = whole[:, :width], whole[:, width + g :]
        next_a = over(mine_a, 2)
        next_b = over(mine_b, 1)
        last_a = over(jnp.concatenate([mine_a, next_a], axis=1), 1)
        last_b = over(jnp.concatenate([mine_b, next_b], axis=1), 2)
        out = finish(
            inverse,
            [whole, next_a, next_b],
            [
                (block_a(c, 0, 0), 0, 0),
                (block_b(c, 0, 0), 0, width + g),
                (block_a(c, 0, 1), 1, 0),
                (block_b(c, 0, 1), 2, 0),
            ],
            width,
            cols,
            out,
        )
        out = finish(
            inverse,
            [last_a, last_b],
            [
                (block_a(c, 1, 0), 0, 0),
                (block_a(c, 1, 1), 0, width),
                (block_b(c, 1, 0), 1, 0),
                (block_b(c, 1, 1), 1, width),
            ],
            width,
            cols,
            out,
        )
    return out


def solution(mesh):
    in_specs = (P("pos", "pix"), P("pix", None))
    out_specs = P(None, "pix")
    run = functools.partial(body, mesh.shape["pos"], mesh.shape["pix"])
    return jax.shard_map(run, mesh=mesh, in_specs=in_specs, out_specs=out_specs, check_vma=False)
```

time: 88.9 us -> 77.3 us (0.87)
  local copies, waits for them, and re-layouts: 20 us -> 0.23 us
  Pallas kernels: 19.7 us -> 23.5 us
  waiting for transfers between devices: 33 us -> 36.1 us
  starting transfers between devices: 15.2 us -> 16.8 us
    unnamed x12 -> x0, local copies, waits for them, and re-layouts: 20 us -> none
    pallas_call x4 -> x3, Pallas kernels: 12.4 us -> 18.1 us  [the longest x2 9.44 us: products(): pl.pallas_call(functools.partial(kernel, plan, grams), in_specs=[TABLE, *...]
    ppermute x11, waiting for transfers between devices: 33 us -> 36.1 us  [swap(): return lax.ppermute(value, axis, [(i, i ^ bit) for i in range(size)])]
    pallas_call x2, Pallas kernels: 5.22 us -> 3.42 us  [finish(): pl.pallas_call(functools.partial(finish_kernel, [piece[1:] for piece in p...]
    ppermute x11, starting transfers between devices: 15.2 us -> 16.8 us  [swap(): return lax.ppermute(value, axis, [(i, i ^ bit) for i in range(size)])]
  transfers between devices with their start and end apart: 11 -> 11, of which waited for: 8 -> 11; matrix products, arithmetic and copies ran while one was open for 1% -> 1% of each run, Pallas kernels for 7% -> 11%
where the time goes in v6:
time: 77.3 us; the launch traced here: 77.2 us
  waiting for transfers between devices  36.1 us (47%)
  Pallas kernels  23.5 us (30%)
  starting transfers between devices  16.8 us (22%)
    ppermute x11, waiting for transfers between devices, swap(): return lax.ppermute(value, axis, [(i, i ^ bit) for i in range(size)])  36.1 us
    ppermute x11, starting transfers between devices, swap(): return lax.ppermute(value, axis, [(i, i ^ bit) for i in range(size)])  16.8 us
    pallas_call x2, Pallas kernels, products(): pl.pallas_call(functools.partial(kernel, plan, grams), in_specs=[TABLE, *...  9.44 us
    pallas_call x1, Pallas kernels, tall_partial(): pl.pallas_call(tall_kernel, in_specs=[HBM, HBM], out_specs=WHOLE, out_sha...  8.61 us
    pallas_call x2, Pallas kernels, finish(): pl.pallas_call(functools.partial(finish_kernel, [piece[1:] for piece in p...  3.42 us
    pallas_call x1, Pallas kernels, inverse_factor(): pl.pallas_call(inverse_kernel, grid=(1,), in_specs=[pl.BlockSpec((rank, L...  2.01 us
  transfers between devices with their start and end apart: 11, of which 11 were waited for; matrix products, arithmetic and copies ran while one was open for 1% of the time, Pallas kernels for 11%

profile of v6, /device:TPU:0, one launch (start us, length us, event | category | flops | bytes accessed | tf_op | source)
XLA Modules:
  0.0 77.2 jit_solution(17066383939765198659)
XLA Ops:
  0.0 8.6 %tall_partial.1 = f32[48,512]{1,0:T(8,128)S(1)} custom-call(f32[512,8192]{1,0:T(8,128)} %x_hbm.5, f32[48,8192]{1,0:T(8,128)} %bitcast.25), custom_call_target="tpu_custom_call" | custom-call | flops 1207959552 | bytes 16777216 | tf_op jit(solution)/shard_map/tall_partial/pallas_call | solution.py:81
  9.1 0.9 %collective-permute-done = f32[48,512]{1,0:T(8,128)S(1)} collective-permute-done((f32[48,512]{1,0:T(8,128)S(1)}, f32[48,512]{1,0:T(8,128)S(1)}, u32[]{:S(2)}, u32[]{:S(2)}) %collective-permute-start) | collective-permute-done | bytes 98336 | tf_op jit(solution)/shard_map/ppermute | solution.py:315
  10.1 2.9 %collective-permute-start.1 = (f32[48,512]{1,0:T(8,128)S(1)}, f32[48,512]{1,0:T(8,128)S(1)}, u32[]{:S(2)}, u32[]{:S(2)}) collective-permute-start(f32[48,512]{1,0:T(8,128)S(1)} %add.107.one_ref), channel_id=1, source_target_pairs={{0,2},{1,3},{2,0},{3,1},{4,6},{5,7},{6,4},{7,5},{8,10},{9,11},{10,... | collective-permute-start | bytes 294920 | tf_op jit(solution)/shard_map/ppermute | solution.py:315
  13.1 3.0 %collective-permute-done.1.two_ref = f32[48,512]{1,0:T(8,128)S(1)} collective-permute-done((f32[48,512]{1,0:T(8,128)S(1)}, f32[48,512]{1,0:T(8,128)S(1)}, u32[]{:S(2)}, u32[]{:S(2)}) %collective-permute-start.1) | collective-permute-done | bytes 98336 | tf_op jit(solution)/shard_map/ppermute | solution.py:315
  16.2 4.9 %first_products.1 = (bf16[96,512]{1,0:T(8,128)(2,1)S(1)}, f32[48,128]{1,0:T(8,128)S(1)}, f32[48,2176]{1,0:T(8,128)S(1)}, f32[48,2048]{1,0:T(8,128)S(1)}) custom-call(s32[8]{0:T(128)S(1)} %stack.106.which_ref, f32[48,512]{1,0:T(8,128)S(1)} %add.107.one_ref, f32[48,512]{1,0:T(8,128)S(1)} %collective-permute-done.1.two_ref, f32[512,8192]{1,0:T(8,128)} %x_hbm.5), custom_call_target="tpu_custom_call" | custom-call | flops 603979776 | bytes 8388608 | tf_op jit(solution)/shard_map/first_products/pallas_call | solution.py:177
  21.0 1.9 %collective-permute-start.4 = (f32[48,2048]{1,0:T(8,128)S(1)}, f32[48,2048]{1,0:T(8,128)S(1)}, u32[]{:S(2)}, u32[]{:S(2)}) collective-permute-start(f32[48,2048]{1,0:T(8,128)S(1)} %get-tuple-element.16), channel_id=1, source_target_pairs={{0,8},{4,12},{8,0},{12,4},{16,24},{20,28},{24,16},{28,20},{1,9},{5... | collective-permute-start | bytes 1179656 | tf_op jit(solution)/shard_map/ppermute | solution.py:315
  22.9 1.5 %collective-permute-start.2 = (f32[48,2176]{1,0:T(8,128)S(1)}, f32[48,2176]{1,0:T(8,128)S(1)}, u32[]{:S(2)}, u32[]{:S(2)}) collective-permute-start(f32[48,2176]{1,0:T(8,128)S(1)} %get-tuple-element.13.after_ref), channel_id=1, source_target_pairs={{0,4},{4,0},{8,12},{12,8},{16,20},{20,16},{24,28},{28,24},{1,5},{5... | collective-permute-start | bytes 1253384 | tf_op jit(solution)/shard_map/ppermute | solution.py:315
  24.5 4.6 %rest_products.1 = (f32[48,2176]{1,0:T(8,128)S(1)}, f32[48,2048]{1,0:T(8,128)S(1)}) custom-call(s32[8]{0:T(128)S(1)} %stack.97.which_ref, bf16[96,512]{1,0:T(8,128)(2,1)S(1)} %get-tuple-element.11.both_ref, f32[48,128]{1,0:T(8,128)S(1)} %get-tuple-element.12.gram_ref, f32[512,8192]{1,0:T(8,128)} %x_hbm.5, f32[48,2176]{1,0:T(8,128)S(1)} %get-tuple-element.13.after_ref), custom_call_target="tpu_custom_call" | custom-call | flops 603979776 | bytes 8388608 | tf_op jit(solution)/shard_map/rest_products/pallas_call | solution.py:177
  29.1 2.7 %collective-permute-done.4 = f32[48,2048]{1,0:T(8,128)S(1)} collective-permute-done((f32[48,2048]{1,0:T(8,128)S(1)}, f32[48,2048]{1,0:T(8,128)S(1)}, u32[]{:S(2)}, u32[]{:S(2)}) %collective-permute-start.4) | collective-permute-done | bytes 393248 | tf_op jit(solution)/shard_map/ppermute | solution.py:315
  31.9 1.4 %collective-permute-start.5 = (f32[48,1024]{1,0:T(8,128)S(1)}, f32[48,1024]{1,0:T(8,128)S(1)}, u32[]{:S(2)}, u32[]{:S(2)}) collective-permute-start(f32[48,1024]{1,0:T(8,128)S(1)} %slice.42), channel_id=1, source_target_pairs={{0,4},{4,0},{8,12},{12,8},{16,20},{20,16},{24,28},{28,24},{1,5},{5... | collective-permute-start | bytes 589832 | tf_op jit(solution)/shard_map/ppermute | solution.py:315
  33.7 1.3 %collective-permute-start.3 = (f32[48,1152]{1,0:T(8,128)S(1)}, f32[48,1152]{1,0:T(8,128)S(1)}, u32[]{:S(2)}, u32[]{:S(2)}) collective-permute-start(f32[48,1152]{1,0:T(8,128)S(1)} %slice.37), channel_id=1, source_target_pairs={{0,8},{4,12},{8,0},{12,4},{16,24},{20,28},{24,16},{28,20},{1,9},{5... | collective-permute-start | bytes 663560 | tf_op jit(solution)/shard_map/ppermute | solution.py:315
  35.0 2.7 %collective-permute-done.5 = f32[48,1024]{1,0:T(8,128)S(1)} collective-permute-done((f32[48,1024]{1,0:T(8,128)S(1)}, f32[48,1024]{1,0:T(8,128)S(1)}, u32[]{:S(2)}, u32[]{:S(2)}) %collective-permute-start.5) | collective-permute-done | bytes 196640 | tf_op jit(solution)/shard_map/ppermute | solution.py:315
  37.7 2.0 %collective-permute-done.3 = f32[48,1152]{1,0:T(8,128)S(1)} collective-permute-done((f32[48,1152]{1,0:T(8,128)S(1)}, f32[48,1152]{1,0:T(8,128)S(1)}, u32[]{:S(2)}, u32[]{:S(2)}) %collective-permute-start.3) | collective-permute-done | bytes 221216 | tf_op jit(solution)/shard_map/ppermute | solution.py:315
  39.8 3.9 %collective-permute-start.6 = (f32[48,2176]{1,0:T(8,128)S(1)}, f32[48,2176]{1,0:T(8,128)S(1)}, u32[]{:S(2)}, u32[]{:S(2)}) collective-permute-start(f32[48,2176]{1,0:T(8,128)S(1)} %pad_maximum_fusion), channel_id=1, source_target_pairs={{0,16},{4,20},{8,24},{12,28},{16,0},{20,4},{24,8},{28,12},{1,17},{... | collective-permute-start | bytes 1253384 | tf_op jit(solution)/shard_map/ppermute | solution.py:315
  43.7 14.6 %collective-permute-done.6 = f32[48,2176]{1,0:T(8,128)S(1)} collective-permute-done((f32[48,2176]{1,0:T(8,128)S(1)}, f32[48,2176]{1,0:T(8,128)S(1)}, u32[]{:S(2)}, u32[]{:S(2)}) %collective-permute-start.6) | collective-permute-done | bytes 417824 | tf_op jit(solution)/shard_map/ppermute | solution.py:315
  58.5 0.7 collective-permute-start.7
  59.1 0.9 %collective-permute-start.9 = (f32[48,1024]{1,0:T(8,128)S(1)}, f32[48,1024]{1,0:T(8,128)S(1)}, u32[]{:S(2)}, u32[]{:S(2)}) collective-permute-start(f32[48,1024]{1,0:T(8,128)S(1)} %get-tuple-element.17), channel_id=1, source_target_pairs={{0,4},{4,0},{8,12},{12,8},{16,20},{20,16},{24,28},{28,24},{1,5},{5... | collective-permute-start | bytes 589832 | tf_op jit(solution)/shard_map/ppermute | solution.py:315
  60.0 4.2 %collective-permute-done.7.refs_1_ = f32[48,1024]{1,0:T(8,128)S(1)} collective-permute-done((f32[48,1024]{1,0:T(8,128)S(1)}, f32[48,1024]{1,0:T(8,128)S(1)}, u32[]{:S(2)}, u32[]{:S(2)}) %collective-permute-start.7) | collective-permute-done | bytes 196640 | tf_op jit(solution)/shard_map/ppermute | solution.py:315
  64.2 1.5 %collective-permute-start.8 = (f32[48,2048]{1,0:T(8,128)S(1)}, f32[48,2048]{1,0:T(8,128)S(1)}, u32[]{:S(2)}, u32[]{:S(2)}) collective-permute-start(f32[48,2048]{1,0:T(8,128)S(1)} %pad_maximum_fusion.1), channel_id=1, source_target_pairs={{0,4},{4,0},{8,12},{12,8},{16,20},{20,16},{24,28},{28,24},{1,5},{5... | collective-permute-start | bytes 1179656 | tf_op jit(solution)/shard_map/ppermute | solution.py:315
  66.5 2.0 %inverse_factor.1.inverse_ref = f32[48,48]{1,0:T(8,128)S(1)} custom-call(f32[48,2176]{1,0:T(8,128)S(1)} %fusion.gram_ref.refs_0_), custom_call_target="tpu_custom_call" | custom-call | flops 20000000 | bytes 49152 | tf_op jit(solution)/shard_map/inverse_factor/pallas_call | solution.py:252
  68.5 1.7 %finish.2.refs_2_ = f32[48,8192]{1,0:T(8,128)} custom-call(s32[4]{0:T(128)S(1)} %pad_add_fusion.1.where_ref, f32[48,48]{1,0:T(8,128)S(1)} %inverse_factor.1.inverse_ref, f32[48,2176]{1,0:T(8,128)S(1)} %fusion.gram_ref.refs_0_, f32[48,1024]{1,0:T(8,128)S(1)} %collective-permute-done.7.refs_1_, f32[48,1024]{1,0:T(8,128)S(1)} %collective-permute-done.9.refs_2_), custom_call_target="tpu_custom_call" | custom-call | flops 56623104 | bytes 1572864 | tf_op jit(solution)/shard_map/finish/pallas_call | solution.py:293
  70.2 3.8 %collective-permute-done.8.refs_0_ = f32[48,2048]{1,0:T(8,128)S(1)} collective-permute-done((f32[48,2048]{1,0:T(8,128)S(1)}, f32[48,2048]{1,0:T(8,128)S(1)}, u32[]{:S(2)}, u32[]{:S(2)}) %collective-permute-start.8) | collective-permute-done | bytes 393248 | tf_op jit(solution)/shard_map/ppermute | solution.py:315
  74.0 1.5 %collective-permute-done.10.refs_1_ = f32[48,2048]{1,0:T(8,128)S(1)} collective-permute-done((f32[48,2048]{1,0:T(8,128)S(1)}, f32[48,2048]{1,0:T(8,128)S(1)}, u32[]{:S(2)}, u32[]{:S(2)}) %collective-permute-start.10) | collective-permute-done | bytes 393248 | tf_op jit(solution)/shard_map/ppermute | solution.py:315
  75.5 1.7 %finish.3 = f32[48,8192]{1,0:T(8,128)} custom-call(s32[4]{0:T(128)S(1)} %pad_add_fusion.where_ref, f32[48,48]{1,0:T(8,128)S(1)} %inverse_factor.1.inverse_ref, f32[48,2048]{1,0:T(8,128)S(1)} %collective-permute-done.8.refs_0_, f32[48,2048]{1,0:T(8,128)S(1)} %collective-permute-done.10.refs_1_, f32[48,8192]{1,0:T(8,128)} %finish.2.refs_2_), custom_call_target="tpu_custom_call", output_to_operand_aliasing={{}: (4, {})} | custom-call | flops 56623104 | bytes 1572864 | tf_op jit(solution)/shard_map/finish/pallas_call | solution.py:293
  (21 shorter events, 2.2 us)
Async XLA Ops:
  8.6 1.5 %collective-permute-start = (f32[48,512]{1,0:T(8,128)S(1)}, f32[48,512]{1,0:T(8,128)S(1)}, u32[]{:S(2)}, u32[]{:S(2)}) collective-permute-start(f32[48,512]{1,0:T(8,128)S(1)} %tall_partial.1), channel_id=1, source_target_pairs={{0,1},{1,0},{2,3},{3,2},{4,5},{5,4},{6,7},{7,6},{8,9},{9,8},{10,11... | collective-permute-start | bytes 294920 | tf_op jit(solution)/shard_map/ppermute | solution.py:315
  10.1 6.1 %collective-permute-start.1 = (f32[48,512]{1,0:T(8,128)S(1)}, f32[48,512]{1,0:T(8,128)S(1)}, u32[]{:S(2)}, u32[]{:S(2)}) collective-permute-start(f32[48,512]{1,0:T(8,128)S(1)} %add.107.one_ref), channel_id=1, source_target_pairs={{0,2},{1,3},{2,0},{3,1},{4,6},{5,7},{6,4},{7,5},{8,10},{9,11},{10,... | collective-permute-start | bytes 294920 | tf_op jit(solution)/shard_map/ppermute | solution.py:315
  21.0 10.7 %collective-permute-start.4 = (f32[48,2048]{1,0:T(8,128)S(1)}, f32[48,2048]{1,0:T(8,128)S(1)}, u32[]{:S(2)}, u32[]{:S(2)}) collective-permute-start(f32[48,2048]{1,0:T(8,128)S(1)} %get-tuple-element.16), channel_id=1, source_target_pairs={{0,8},{4,12},{8,0},{12,4},{16,24},{20,28},{24,16},{28,20},{1,9},{5... | collective-permute-start | bytes 1179656 | tf_op jit(solution)/shard_map/ppermute | solution.py:315
  22.9 10.7 %collective-permute-start.2 = (f32[48,2176]{1,0:T(8,128)S(1)}, f32[48,2176]{1,0:T(8,128)S(1)}, u32[]{:S(2)}, u32[]{:S(2)}) collective-permute-start(f32[48,2176]{1,0:T(8,128)S(1)} %get-tuple-element.13.after_ref), channel_id=1, source_target_pairs={{0,4},{4,0},{8,12},{12,8},{16,20},{20,16},{24,28},{28,24},{1,5},{5... | collective-permute-start | bytes 1253384 | tf_op jit(solution)/shard_map/ppermute | solution.py:315
  31.9 5.8 %collective-permute-start.5 = (f32[48,1024]{1,0:T(8,128)S(1)}, f32[48,1024]{1,0:T(8,128)S(1)}, u32[]{:S(2)}, u32[]{:S(2)}) collective-permute-start(f32[48,1024]{1,0:T(8,128)S(1)} %slice.42), channel_id=1, source_target_pairs={{0,4},{4,0},{8,12},{12,8},{16,20},{20,16},{24,28},{28,24},{1,5},{5... | collective-permute-start | bytes 589832 | tf_op jit(solution)/shard_map/ppermute | solution.py:315
  33.7 6.0 %collective-permute-start.3 = (f32[48,1152]{1,0:T(8,128)S(1)}, f32[48,1152]{1,0:T(8,128)S(1)}, u32[]{:S(2)}, u32[]{:S(2)}) collective-permute-start(f32[48,1152]{1,0:T(8,128)S(1)} %slice.37), channel_id=1, source_target_pairs={{0,8},{4,12},{8,0},{12,4},{16,24},{20,28},{24,16},{28,20},{1,9},{5... | collective-permute-start | bytes 663560 | tf_op jit(solution)/shard_map/ppermute | solution.py:315
  39.8 18.6 %collective-permute-start.6 = (f32[48,2176]{1,0:T(8,128)S(1)}, f32[48,2176]{1,0:T(8,128)S(1)}, u32[]{:S(2)}, u32[]{:S(2)}) collective-permute-start(f32[48,2176]{1,0:T(8,128)S(1)} %pad_maximum_fusion), channel_id=1, source_target_pairs={{0,16},{4,20},{8,24},{12,28},{16,0},{20,4},{24,8},{28,12},{1,17},{... | collective-permute-start | bytes 1253384 | tf_op jit(solution)/shard_map/ppermute | solution.py:315
  58.5 5.7 %collective-permute-start.7 = (f32[48,1024]{1,0:T(8,128)S(1)}, f32[48,1024]{1,0:T(8,128)S(1)}, u32[]{:S(2)}, u32[]{:S(2)}) collective-permute-start(f32[48,1024]{1,0:T(8,128)S(1)} %get-tuple-element.18), channel_id=1, source_target_pairs={{0,8},{4,12},{8,0},{12,4},{16,24},{20,28},{24,16},{28,20},{1,9},{5... | collective-permute-start | bytes 589832 | tf_op jit(solution)/shard_map/ppermute | solution.py:315
  59.1 6.8 %collective-permute-start.9 = (f32[48,1024]{1,0:T(8,128)S(1)}, f32[48,1024]{1,0:T(8,128)S(1)}, u32[]{:S(2)}, u32[]{:S(2)}) collective-permute-start(f32[48,1024]{1,0:T(8,128)S(1)} %get-tuple-element.17), channel_id=1, source_target_pairs={{0,4},{4,0},{8,12},{12,8},{16,20},{20,16},{24,28},{28,24},{1,5},{5... | collective-permute-start | bytes 589832 | tf_op jit(solution)/shard_map/ppermute | solution.py:315
  64.2 9.8 %collective-permute-start.8 = (f32[48,2048]{1,0:T(8,128)S(1)}, f32[48,2048]{1,0:T(8,128)S(1)}, u32[]{:S(2)}, u32[]{:S(2)}) collective-permute-start(f32[48,2048]{1,0:T(8,128)S(1)} %pad_maximum_fusion.1), channel_id=1, source_target_pairs={{0,4},{4,0},{8,12},{12,8},{16,20},{20,16},{24,28},{28,24},{1,5},{5... | collective-permute-start | bytes 1179656 | tf_op jit(solution)/shard_map/ppermute | solution.py:315
  66.0 9.5 %collective-permute-start.10 = (f32[48,2048]{1,0:T(8,128)S(1)}, f32[48,2048]{1,0:T(8,128)S(1)}, u32[]{:S(2)}, u32[]{:S(2)}) collective-permute-start(f32[48,2048]{1,0:T(8,128)S(1)} %pad_maximum_fusion.2), channel_id=1, source_target_pairs={{0,8},{4,12},{8,0},{12,4},{16,24},{20,28},{24,16},{28,20},{1,9},{5... | collective-permute-start | bytes 1179656 | tf_op jit(solution)/shard_map/ppermute | solution.py:315

commit v7 on v6

--- a/solution.py
+++ b/solution.py
@@ -11,7 +11,7 @@
 BF16 = jnp.bfloat16
 VMEM_LIMIT = 40 * 1024 * 1024
 LANES = 128
-CHUNKS = 1
+CHUNKS = 2
 AHEAD = 6
 UNIT = 512
 PANEL = 4
@@ -341,23 +341,26 @@
             ([block_b(c, p, 1), block_b(c, p, 0)], False),
         ]
 
-    both, gram, first = first_products(tall, other, probes, outputs(0, 1), width)
-    plan = [(c, p) for c in range(CHUNKS) for p in (1, 0) if (c, p) != (0, 1)]
-    rest = rest_products(
-        both, gram, probes, [out for c, p in plan for out in outputs(c, p)], width, first[0]
-    )
-    made = {(0, 1): first}
-    made.update({key: rest[2 * k : 2 * k + 2] for k, key in enumerate(plan)})
-
-    inverse, out = None, None
+    both, gram, away = first_products(tall, other, probes, outputs(0, 1), width)
+
+    inverse, out, after = None, None, away[0]
     for c in range(CHUNKS):
         g = LANES if c == 0 else 0
-        away_a, away_b = made[c, 1]
-        own_a, own_b = made[c, 0]
-        sum_a = own_a + over(away_a, 1)
+        last = c == CHUNKS - 1
+        made = rest_products(
+            both, gram, probes, outputs(c, 0) + ([] if last else outputs(c + 1, 1)), width, after
+        )
+        away_a, away_b = away
+        (own_a, own_b), away = made[:2], made[2:]
+        got_a = over(away_a, 1)
+        sum_a = own_a + got_a
         sum_b = own_b + over(away_b, 2)
-        got_a = over(sum_a[:, : width + g], 2)
-        got_b = over(sum_b[:, :width], 1)
+        after = got_a
+        send_a, send_b = sum_a[:, : width + g], sum_b[:, :width]
+        if c > 0:
+            send_a, send_b, whole = lax.optimization_barrier((send_a, send_b, whole))
+        got_a = over(send_a, 2)
+        got_b = over(send_b, 1)
         whole = jnp.concatenate(
             [
                 sum_a[:, width + g :] + got_a[:, :width],
@@ -366,43 +369,39 @@
             ],
             axis=1,
         )
+        total = whole
         bit = 4
         while bit < n_pos:
-            whole = whole + over(whole, bit)
+            total = total + over(total, bit)
             bit *= 2
         if c == 0:
-            inverse = inverse_factor(whole, width)
-        mine_a, mine_b = whole[:, :width], whole[:, width + g :]
+            inverse = inverse_factor(total, width)
+        mine_a, mine_b = total[:, :width], total[:, width + g :]
+        if c > 0:
+            mine_a, mine_b, inverse = lax.optimization_barrier((mine_a, mine_b, inverse))
         next_a = over(mine_a, 2)
         next_b = over(mine_b, 1)
         last_a = over(jnp.concatenate([mine_a, next_a], axis=1), 1)
         last_b = over(jnp.concatenate([mine_b, next_b], axis=1), 2)
-        out = finish(
-            inverse,
-            [whole, next_a, next_b],
-            [
-                (block_a(c, 0, 0), 0, 0),
-                (block_b(c, 0, 0), 0, width + g),
-                (block_a(c, 0, 1), 1, 0),
-                (block_b(c, 0, 1), 2, 0),
-            ],
-            width,
-            cols,
-            out,
-        )
-        out = finish(
-            inverse,
-            [last_a, last_b],
-            [
-                (block_a(c, 1, 0), 0, 0),
-                (block_a(c, 1, 1), 0, width),
-                (block_b(c, 1, 0), 1, 0),
-                (block_b(c, 1, 1), 1, width),
-            ],
-            width,
-            cols,
-            out,
-        )
+        sources = [total, next_a, next_b]
+        pieces = [
+            (block_a(c, 0, 0), 0, 0),
+            (block_b(c, 0, 0), 0, width + g),
+            (block_a(c, 0, 1), 1, 0),
+            (block_b(c, 0, 1), 2, 0),
+        ]
+        if last:
+            out = finish(inverse, sources, pieces, width, cols, out)
+            sources, pieces = [], []
+        k = len(sources)
+        sources += [last_a, last_b]
+        pieces += [
+            (block_a(c, 1, 0), k, 0),
+            (block_a(c, 1, 1), k, width),
+            (block_b(c, 1, 0), k + 1, 0),
+            (block_b(c, 1, 1), k + 1, width),
+        ]
+        out = finish(inverse, sources, pieces, width, cols, out)
     return out
 
 

time: 77.3 us -> 72.6 us (0.939)
  waiting for transfers between devices: 36.1 us -> 21 us
  starting transfers between devices: 16.8 us -> 24 us
  Pallas kernels: 23.5 us -> 26.3 us
    ppermute x11 -> x20, waiting for transfers between devices: 36.1 us -> 21 us  [swap(): return lax.ppermute(value, axis, [(i, i ^ bit) for i in range(size)])]
    ppermute x11 -> x20, starting transfers between devices: 16.8 us -> 24 us  [swap(): return lax.ppermute(value, axis, [(i, i ^ bit) for i in range(size)])]
    pallas_call x2 -> x3, Pallas kernels: 9.44 us -> 11 us  [products(): pl.pallas_call(functools.partial(kernel, plan, grams), in_specs=[TABLE, *...]
    pallas_call x2 -> x3, Pallas kernels: 3.42 us -> 4.72 us  [finish(): pl.pallas_call(functools.partial(finish_kernel, [piece[1:] for piece in p...]
  transfers between devices with their start and end apart: 11 -> 20, of which waited for: 11 -> 10; matrix products, arithmetic and copies ran while one was open for 1% -> 1% of each run, Pallas kernels for 11% -> 18%
where the time goes in v7:
time: 72.6 us; the launch traced here: 72.5 us
  Pallas kernels  26.3 us (36%)
  starting transfers between devices  24 us (33%)
  waiting for transfers between devices  21 us (29%)
    ppermute x20, starting transfers between devices, swap(): return lax.ppermute(value, axis, [(i, i ^ bit) for i in range(size)])  24 us
    ppermute x20, waiting for transfers between devices, swap(): return lax.ppermute(value, axis, [(i, i ^ bit) for i in range(size)])  21 us
    pallas_call x3, Pallas kernels, products(): pl.pallas_call(functools.partial(kernel, plan, grams), in_specs=[TABLE, *...  11 us
    pallas_call x1, Pallas kernels, tall_partial(): pl.pallas_call(tall_kernel, in_specs=[HBM, HBM], out_specs=WHOLE, out_sha...  8.61 us
    pallas_call x3, Pallas kernels, finish(): pl.pallas_call(functools.partial(finish_kernel, [piece[1:] for piece in p...  4.72 us
    pallas_call x1, Pallas kernels, inverse_factor(): pl.pallas_call(inverse_kernel, grid=(1,), in_specs=[pl.BlockSpec((rank, L...  2.01 us
  transfers between devices with their start and end apart: 20, of which 10 were waited for; matrix products, arithmetic and copies ran while one was open for 1% of the time, Pallas kernels for 18%

profile of v7, /device:TPU:0, one launch (start us, length us, event | category | flops | bytes accessed | tf_op | source)
XLA Modules:
  0.0 72.5 jit_solution(2805576268377439769)
XLA Ops:
  0.0 8.6 %tall_partial.1 = f32[48,512]{1,0:T(8,128)S(1)} custom-call(f32[512,8192]{1,0:T(8,128)} %x_hbm.7, f32[48,8192]{1,0:T(8,128)} %bitcast.17), custom_call_target="tpu_custom_call" | custom-call | flops 1207959552 | bytes 16777216 | tf_op jit(solution)/shard_map/tall_partial/pallas_call | solution.py:81
  9.1 0.9 %collective-permute-done = f32[48,512]{1,0:T(8,128)S(1)} collective-permute-done((f32[48,512]{1,0:T(8,128)S(1)}, f32[48,512]{1,0:T(8,128)S(1)}, u32[]{:S(2)}, u32[]{:S(2)}) %collective-permute-start) | collective-permute-done | bytes 98336 | tf_op jit(solution)/shard_map/ppermute | solution.py:315
  10.1 2.9 %collective-permute-start.1 = (f32[48,512]{1,0:T(8,128)S(1)}, f32[48,512]{1,0:T(8,128)S(1)}, u32[]{:S(2)}, u32[]{:S(2)}) collective-permute-start(f32[48,512]{1,0:T(8,128)S(1)} %add.153.one_ref), channel_id=1, source_target_pairs={{0,2},{1,3},{2,0},{3,1},{4,6},{5,7},{6,4},{7,5},{8,10},{9,11},{10,... | collective-permute-start | bytes 294920 | tf_op jit(solution)/shard_map/ppermute | solution.py:315
  13.1 3.0 %collective-permute-done.1.two_ref = f32[48,512]{1,0:T(8,128)S(1)} collective-permute-done((f32[48,512]{1,0:T(8,128)S(1)}, f32[48,512]{1,0:T(8,128)S(1)}, u32[]{:S(2)}, u32[]{:S(2)}) %collective-permute-start.1) | collective-permute-done | bytes 98336 | tf_op jit(solution)/shard_map/ppermute | solution.py:315
  16.2 3.4 %first_products.1 = (bf16[96,512]{1,0:T(8,128)(2,1)S(1)}, f32[48,128]{1,0:T(8,128)S(1)}, f32[48,1152]{1,0:T(8,128)S(1)}, f32[48,1024]{1,0:T(8,128)S(1)}) custom-call(s32[4]{0:T(128)S(1)} %pad_add_fusion.2.which_ref, f32[48,512]{1,0:T(8,128)S(1)} %add.153.one_ref, f32[48,512]{1,0:T(8,128)S(1)} %collective-permute-done.1.two_ref, f32[512,8192]{1,0:T(8,128)} %x_hbm.7), custom_call_target="tpu_custom_call" | custom-call | flops 301989888 | bytes 4194304 | tf_op jit(solution)/shard_map/first_products/pallas_call | solution.py:177
  19.5 1.9 %collective-permute-start.6 = (f32[48,1024]{1,0:T(8,128)S(1)}, f32[48,1024]{1,0:T(8,128)S(1)}, u32[]{:S(2)}, u32[]{:S(2)}) collective-permute-start(f32[48,1024]{1,0:T(8,128)S(1)} %get-tuple-element.29), channel_id=1, source_target_pairs={{0,8},{4,12},{8,0},{12,4},{16,24},{20,28},{24,16},{28,20},{1,9},{5... | collective-permute-start | bytes 589832 | tf_op jit(solution)/shard_map/ppermute | solution.py:315
  21.5 1.5 %collective-permute-start.2 = (f32[48,1152]{1,0:T(8,128)S(1)}, f32[48,1152]{1,0:T(8,128)S(1)}, u32[]{:S(2)}, u32[]{:S(2)}) collective-permute-start(f32[48,1152]{1,0:T(8,128)S(1)} %get-tuple-element.22.after_ref), channel_id=1, source_target_pairs={{0,4},{4,0},{8,12},{12,8},{16,20},{20,16},{24,28},{28,24},{1,5},{5... | collective-permute-start | bytes 663560 | tf_op jit(solution)/shard_map/ppermute | solution.py:315
  23.0 4.6 %rest_products.3 = (f32[48,1152]{1,0:T(8,128)S(1)}, f32[48,1024]{1,0:T(8,128)S(1)}, f32[48,1024]{1,0:T(8,128)S(1)}, f32[48,1024]{1,0:T(8,128)S(1)}) custom-call(s32[8]{0:T(128)S(1)} %stack.101.which_ref, bf16[96,512]{1,0:T(8,128)(2,1)S(1)} %get-tuple-element.20.both_ref, f32[48,128]{1,0:T(8,128)S(1)} %get-tuple-element.21.gram_ref, f32[512,8192]{1,0:T(8,128)} %x_hbm.7, ...), custom_call_target="tpu_custom_call" | custom-call | flops 603979776 | bytes 8388608 | tf_op jit(solution)/shard_map/rest_products/pallas_call | solution.py:177
  28.4 1.8 %collective-permute-start.7 = (f32[48,512]{1,0:T(8,128)S(1)}, f32[48,512]{1,0:T(8,128)S(1)}, u32[]{:S(2)}, u32[]{:S(2)}) collective-permute-start(f32[48,512]{1,0:T(8,128)S(1)} %slice.69), channel_id=1, source_target_pairs={{0,4},{4,0},{8,12},{12,8},{16,20},{20,16},{24,28},{28,24},{1,5},{5... | collective-permute-start | bytes 294920 | tf_op jit(solution)/shard_map/ppermute | solution.py:315
  30.3 1.6 %collective-permute-start.5 = (f32[48,640]{1,0:T(8,128)S(1)}, f32[48,640]{1,0:T(8,128)S(1)}, u32[]{:S(2)}, u32[]{:S(2)}) collective-permute-start(f32[48,640]{1,0:T(8,128)S(1)} %slice.64), channel_id=1, source_target_pairs={{0,8},{4,12},{8,0},{12,4},{16,24},{20,28},{24,16},{28,20},{1,9},{5... | collective-permute-start | bytes 368648 | tf_op jit(solution)/shard_map/ppermute | solution.py:315
  32.0 3.1 %rest_products.2 = (f32[48,1024]{1,0:T(8,128)S(1)}, f32[48,1024]{1,0:T(8,128)S(1)}) custom-call(s32[4]{0:T(128)S(1)} %pad_add_fusion.1.which_ref, bf16[96,512]{1,0:T(8,128)(2,1)S(1)} %get-tuple-element.20.both_ref, f32[48,128]{1,0:T(8,128)S(1)} %get-tuple-element.21.gram_ref, f32[512,8192]{1,0:T(8,128)} %x_hbm.7, f32[48,1152]{1,0:T(8,128)S(1)} %collective-permute-done.2.after_ref), custom_call_target="tpu_custom_call" | custom-call | flops 301989888 | bytes 4194304 | tf_op jit(solution)/shard_map/rest_products/pallas_call | solution.py:177
  35.9 1.3 %collective-permute-start.8 = (f32[48,512]{1,0:T(8,128)S(1)}, f32[48,512]{1,0:T(8,128)S(1)}, u32[]{:S(2)}, u32[]{:S(2)}) collective-permute-start(f32[48,512]{1,0:T(8,128)S(1)} %slice.61), channel_id=1, source_target_pairs={{0,8},{4,12},{8,0},{12,4},{16,24},{20,28},{24,16},{28,20},{1,9},{5... | collective-permute-start | bytes 294920 | tf_op jit(solution)/shard_map/ppermute | solution.py:315
  37.3 2.6 %collective-permute-start.11 = (f32[48,1152]{1,0:T(8,128)S(1)}, f32[48,1152]{1,0:T(8,128)S(1)}, u32[]{:S(2)}, u32[]{:S(2)}) collective-permute-start(f32[48,1152]{1,0:T(8,128)S(1)} %pad_maximum_fusion), channel_id=1, source_target_pairs={{0,16},{4,20},{8,24},{12,28},{16,0},{20,4},{24,8},{28,12},{1,17},{... | collective-permute-start | bytes 663560 | tf_op jit(solution)/shard_map/ppermute | solution.py:315
  40.7 3.8 %collective-permute-done.9 = f32[48,512]{1,0:T(8,128)S(1)} collective-permute-done((f32[48,512]{1,0:T(8,128)S(1)}, f32[48,512]{1,0:T(8,128)S(1)}, u32[]{:S(2)}, u32[]{:S(2)}) %collective-permute-start.9) | collective-permute-done | bytes 98336 | tf_op jit(solution)/shard_map/ppermute | solution.py:315
  44.9 8.5 %collective-permute-done.11 = f32[48,1152]{1,0:T(8,128)S(1)} collective-permute-done((f32[48,1152]{1,0:T(8,128)S(1)}, f32[48,1152]{1,0:T(8,128)S(1)}, u32[]{:S(2)}, u32[]{:S(2)}) %collective-permute-start.11) | collective-permute-done | bytes 221216 | tf_op jit(solution)/shard_map/ppermute | solution.py:315
  54.7 2.0 %inverse_factor.1.inverse_ref = f32[48,48]{1,0:T(8,128)S(1)} custom-call(f32[48,1152]{1,0:T(8,128)S(1)} %fusion.1.gram_ref.refs_0_), custom_call_target="tpu_custom_call" | custom-call | flops 20000000 | bytes 49152 | tf_op jit(solution)/shard_map/inverse_factor/pallas_call | solution.py:252
  56.8 1.4 %collective-permute-start.12 = (f32[48,512]{1,0:T(8,128)S(1)}, f32[48,512]{1,0:T(8,128)S(1)}, u32[]{:S(2)}, u32[]{:S(2)}) collective-permute-start(f32[48,512]{1,0:T(8,128)S(1)} %get-tuple-element.33), channel_id=1, source_target_pairs={{0,8},{4,12},{8,0},{12,4},{16,24},{20,28},{24,16},{28,20},{1,9},{5... | collective-permute-start | bytes 294920 | tf_op jit(solution)/shard_map/ppermute | solution.py:315
  58.2 1.6 %collective-permute-start.14 = (f32[48,512]{1,0:T(8,128)S(1)}, f32[48,512]{1,0:T(8,128)S(1)}, u32[]{:S(2)}, u32[]{:S(2)}) collective-permute-start(f32[48,512]{1,0:T(8,128)S(1)} %get-tuple-element.34), channel_id=1, source_target_pairs={{0,4},{4,0},{8,12},{12,8},{16,20},{20,16},{24,28},{28,24},{1,5},{5... | collective-permute-start | bytes 294920 | tf_op jit(solution)/shard_map/ppermute | solution.py:315
  61.3 2.2 %collective-permute-done.14.refs_2_ = f32[48,512]{1,0:T(8,128)S(1)} collective-permute-done((f32[48,512]{1,0:T(8,128)S(1)}, f32[48,512]{1,0:T(8,128)S(1)}, u32[]{:S(2)}, u32[]{:S(2)}) %collective-permute-start.14) | collective-permute-done | bytes 98336 | tf_op jit(solution)/shard_map/ppermute | solution.py:315
  63.6 1.1 %collective-permute-start.15 = (f32[48,1024]{1,0:T(8,128)S(1)}, f32[48,1024]{1,0:T(8,128)S(1)}, u32[]{:S(2)}, u32[]{:S(2)}) collective-permute-start(f32[48,1024]{1,0:T(8,128)S(1)} %pad_maximum_fusion.3), channel_id=1, source_target_pairs={{0,8},{4,12},{8,0},{12,4},{16,24},{20,28},{24,16},{28,20},{1,9},{5... | collective-permute-start | bytes 589832 | tf_op jit(solution)/shard_map/ppermute | solution.py:315
  64.7 1.3 %collective-permute-start.13 = (f32[48,1024]{1,0:T(8,128)S(1)}, f32[48,1024]{1,0:T(8,128)S(1)}, u32[]{:S(2)}, u32[]{:S(2)}) collective-permute-start(f32[48,1024]{1,0:T(8,128)S(1)} %pad_maximum_fusion.2), channel_id=1, source_target_pairs={{0,4},{4,0},{8,12},{12,8},{16,20},{20,16},{24,28},{28,24},{1,5},{5... | collective-permute-start | bytes 589832 | tf_op jit(solution)/shard_map/ppermute | solution.py:315
  67.7 1.7 %finish.3.refs_3_ = f32[48,8192]{1,0:T(8,128)} custom-call(s32[8]{0:T(128)S(1)} %stack.103.where_ref, f32[48,48]{1,0:T(8,128)S(1)} %inverse_factor.1.inverse_ref, f32[48,1152]{1,0:T(8,128)S(1)} %fusion.1.gram_ref.refs_0_, f32[48,512]{1,0:T(8,128)S(1)} %collective-permute-done.16.refs_1_, f32[48,512]{1,0:T(8,128)S(1)} %collective-permute-done.17.refs_2_, ...), custom_call_target="tpu_custom_call" | custom-call | flops 56623104 | bytes 1572864 | tf_op jit(solution)/shard_map/finish/pallas_call | solution.py:293
  69.4 1.5 %finish.4.refs_2_ = f32[48,8192]{1,0:T(8,128)} custom-call(s32[4]{0:T(128)S(1)} %pad_add_fusion.3.where_ref, f32[48,48]{1,0:T(8,128)S(1)} %inverse_factor.1.inverse_ref, f32[48,1024]{1,0:T(8,128)S(1)} %fusion.refs_0_, f32[48,512]{1,0:T(8,128)S(1)} %collective-permute-done.12.refs_1_, ...), custom_call_target="tpu_custom_call", output_to_operand_aliasing={{}: (5, {})} | custom-call | flops 28311552 | bytes 786432 | tf_op jit(solution)/shard_map/finish/pallas_call | solution.py:293
  71.0 1.5 %finish.5 = f32[48,8192]{1,0:T(8,128)} custom-call(s32[4]{0:T(128)S(1)} %pad_add_fusion.where_ref, f32[48,48]{1,0:T(8,128)S(1)} %inverse_factor.1.inverse_ref, f32[48,1024]{1,0:T(8,128)S(1)} %collective-permute-done.13.refs_0_, f32[48,1024]{1,0:T(8,128)S(1)} %collective-permute-done.15.refs_1_, f32[48,8192]{1,0:T(8,128)} %finish.4.refs_2_), custom_call_target="tpu_custom_call", output_to_operand_aliasing={{}: (4, {})} | custom-call | flops 28311552 | bytes 786432 | tf_op jit(solution)/shard_map/finish/pallas_call | solution.py:293
  (54 shorter events, 8.4 us)
Async XLA Ops:
  8.6 1.5 %collective-permute-start = (f32[48,512]{1,0:T(8,128)S(1)}, f32[48,512]{1,0:T(8,128)S(1)}, u32[]{:S(2)}, u32[]{:S(2)}) collective-permute-start(f32[48,512]{1,0:T(8,128)S(1)} %tall_partial.1), channel_id=1, source_target_pairs={{0,1},{1,0},{2,3},{3,2},{4,5},{5,4},{6,7},{7,6},{8,9},{9,8},{10,11... | collective-permute-start | bytes 294920 | tf_op jit(solution)/shard_map/ppermute | solution.py:315
  10.1 6.1 %collective-permute-start.1 = (f32[48,512]{1,0:T(8,128)S(1)}, f32[48,512]{1,0:T(8,128)S(1)}, u32[]{:S(2)}, u32[]{:S(2)}) collective-permute-start(f32[48,512]{1,0:T(8,128)S(1)} %add.153.one_ref), channel_id=1, source_target_pairs={{0,2},{1,3},{2,0},{3,1},{4,6},{5,7},{6,4},{7,5},{8,10},{9,11},{10,... | collective-permute-start | bytes 294920 | tf_op jit(solution)/shard_map/ppermute | solution.py:315
  19.5 8.9 %collective-permute-start.6 = (f32[48,1024]{1,0:T(8,128)S(1)}, f32[48,1024]{1,0:T(8,128)S(1)}, u32[]{:S(2)}, u32[]{:S(2)}) collective-permute-start(f32[48,1024]{1,0:T(8,128)S(1)} %get-tuple-element.29), channel_id=1, source_target_pairs={{0,8},{4,12},{8,0},{12,4},{16,24},{20,28},{24,16},{28,20},{1,9},{5... | collective-permute-start | bytes 589832 | tf_op jit(solution)/shard_map/ppermute | solution.py:315
  21.5 8.8 %collective-permute-start.2 = (f32[48,1152]{1,0:T(8,128)S(1)}, f32[48,1152]{1,0:T(8,128)S(1)}, u32[]{:S(2)}, u32[]{:S(2)}) collective-permute-start(f32[48,1152]{1,0:T(8,128)S(1)} %get-tuple-element.22.after_ref), channel_id=1, source_target_pairs={{0,4},{4,0},{8,12},{12,8},{16,20},{20,16},{24,28},{28,24},{1,5},{5... | collective-permute-start | bytes 663560 | tf_op jit(solution)/shard_map/ppermute | solution.py:315
  27.5 7.5 %collective-permute-start.4 = (f32[48,1024]{1,0:T(8,128)S(1)}, f32[48,1024]{1,0:T(8,128)S(1)}, u32[]{:S(2)}, u32[]{:S(2)}) collective-permute-start(f32[48,1024]{1,0:T(8,128)S(1)} %get-tuple-element.26), channel_id=1, source_target_pairs={{0,8},{4,12},{8,0},{12,4},{16,24},{20,28},{24,16},{28,20},{1,9},{5... | collective-permute-start | bytes 589832 | tf_op jit(solution)/shard_map/ppermute | solution.py:315
  28.1 7.0 %collective-permute-start.3 = (f32[48,1024]{1,0:T(8,128)S(1)}, f32[48,1024]{1,0:T(8,128)S(1)}, u32[]{:S(2)}, u32[]{:S(2)}) collective-permute-start(f32[48,1024]{1,0:T(8,128)S(1)} %get-tuple-element.24), channel_id=1, source_target_pairs={{0,4},{4,0},{8,12},{12,8},{16,20},{20,16},{24,28},{28,24},{1,5},{5... | collective-permute-start | bytes 589832 | tf_op jit(solution)/shard_map/ppermute | solution.py:315
  28.4 7.0 %collective-permute-start.7 = (f32[48,512]{1,0:T(8,128)S(1)}, f32[48,512]{1,0:T(8,128)S(1)}, u32[]{:S(2)}, u32[]{:S(2)}) collective-permute-start(f32[48,512]{1,0:T(8,128)S(1)} %slice.69), channel_id=1, source_target_pairs={{0,4},{4,0},{8,12},{12,8},{16,20},{20,16},{24,28},{28,24},{1,5},{5... | collective-permute-start | bytes 294920 | tf_op jit(solution)/shard_map/ppermute | solution.py:315
  30.3 5.5 %collective-permute-start.5 = (f32[48,640]{1,0:T(8,128)S(1)}, f32[48,640]{1,0:T(8,128)S(1)}, u32[]{:S(2)}, u32[]{:S(2)}) collective-permute-start(f32[48,640]{1,0:T(8,128)S(1)} %slice.64), channel_id=1, source_target_pairs={{0,8},{4,12},{8,0},{12,4},{16,24},{20,28},{24,16},{28,20},{1,9},{5... | collective-permute-start | bytes 368648 | tf_op jit(solution)/shard_map/ppermute | solution.py:315
  35.9 4.8 %collective-permute-start.8 = (f32[48,512]{1,0:T(8,128)S(1)}, f32[48,512]{1,0:T(8,128)S(1)}, u32[]{:S(2)}, u32[]{:S(2)}) collective-permute-start(f32[48,512]{1,0:T(8,128)S(1)} %slice.61), channel_id=1, source_target_pairs={{0,8},{4,12},{8,0},{12,4},{16,24},{20,28},{24,16},{28,20},{1,9},{5... | collective-permute-start | bytes 294920 | tf_op jit(solution)/shard_map/ppermute | solution.py:315
  37.3 16.2 %collective-permute-start.11 = (f32[48,1152]{1,0:T(8,128)S(1)}, f32[48,1152]{1,0:T(8,128)S(1)}, u32[]{:S(2)}, u32[]{:S(2)}) collective-permute-start(f32[48,1152]{1,0:T(8,128)S(1)} %pad_maximum_fusion), channel_id=1, source_target_pairs={{0,16},{4,20},{8,24},{12,28},{16,0},{20,4},{24,8},{28,12},{1,17},{... | collective-permute-start | bytes 663560 | tf_op jit(solution)/shard_map/ppermute | solution.py:315
  39.9 4.6 %collective-permute-start.9 = (f32[48,512]{1,0:T(8,128)S(1)}, f32[48,512]{1,0:T(8,128)S(1)}, u32[]{:S(2)}, u32[]{:S(2)}) collective-permute-start(f32[48,512]{1,0:T(8,128)S(1)} %slice.62), channel_id=1, source_target_pairs={{0,4},{4,0},{8,12},{12,8},{16,20},{20,16},{24,28},{28,24},{1,5},{5... | collective-permute-start | bytes 294920 | tf_op jit(solution)/shard_map/ppermute | solution.py:315
  44.5 12.2 %collective-permute-start.10 = (f32[48,1024]{1,0:T(8,128)S(1)}, f32[48,1024]{1,0:T(8,128)S(1)}, u32[]{:S(2)}, u32[]{:S(2)}) collective-permute-start(f32[48,1024]{1,0:T(8,128)S(1)} %pad_maximum_fusion.1), channel_id=1, source_target_pairs={{0,16},{4,20},{8,24},{12,28},{16,0},{20,4},{24,8},{28,12},{1,17},{... | collective-permute-start | bytes 589832 | tf_op jit(solution)/shard_map/ppermute | solution.py:315
  53.5 6.3 %collective-permute-start.17 = (f32[48,512]{1,0:T(8,128)S(1)}, f32[48,512]{1,0:T(8,128)S(1)}, u32[]{:S(2)}, u32[]{:S(2)}) collective-permute-start(f32[48,512]{1,0:T(8,128)S(1)} %get-tuple-element.35), channel_id=1, source_target_pairs={{0,4},{4,0},{8,12},{12,8},{16,20},{20,16},{24,28},{28,24},{1,5},{5... | collective-permute-start | bytes 294920 | tf_op jit(solution)/shard_map/ppermute | solution.py:315
  54.0 6.4 %collective-permute-start.16 = (f32[48,512]{1,0:T(8,128)S(1)}, f32[48,512]{1,0:T(8,128)S(1)}, u32[]{:S(2)}, u32[]{:S(2)}) collective-permute-start(f32[48,512]{1,0:T(8,128)S(1)} %get-tuple-element.36), channel_id=1, source_target_pairs={{0,8},{4,12},{8,0},{12,4},{16,24},{20,28},{24,16},{28,20},{1,9},{5... | collective-permute-start | bytes 294920 | tf_op jit(solution)/shard_map/ppermute | solution.py:315
  56.8 7.9 %collective-permute-start.12 = (f32[48,512]{1,0:T(8,128)S(1)}, f32[48,512]{1,0:T(8,128)S(1)}, u32[]{:S(2)}, u32[]{:S(2)}) collective-permute-start(f32[48,512]{1,0:T(8,128)S(1)} %get-tuple-element.33), channel_id=1, source_target_pairs={{0,8},{4,12},{8,0},{12,4},{16,24},{20,28},{24,16},{28,20},{1,9},{5... | collective-permute-start | bytes 294920 | tf_op jit(solution)/shard_map/ppermute | solution.py:315
  58.2 5.4 %collective-permute-start.14 = (f32[48,512]{1,0:T(8,128)S(1)}, f32[48,512]{1,0:T(8,128)S(1)}, u32[]{:S(2)}, u32[]{:S(2)}) collective-permute-start(f32[48,512]{1,0:T(8,128)S(1)} %get-tuple-element.34), channel_id=1, source_target_pairs={{0,4},{4,0},{8,12},{12,8},{16,20},{20,16},{24,28},{28,24},{1,5},{5... | collective-permute-start | bytes 294920 | tf_op jit(solution)/shard_map/ppermute | solution.py:315
  59.8 7.3 %collective-permute-start.19 = (f32[48,1024]{1,0:T(8,128)S(1)}, f32[48,1024]{1,0:T(8,128)S(1)}, u32[]{:S(2)}, u32[]{:S(2)}) collective-permute-start(f32[48,1024]{1,0:T(8,128)S(1)} %pad_maximum_fusion.5), channel_id=1, source_target_pairs={{0,8},{4,12},{8,0},{12,4},{16,24},{20,28},{24,16},{28,20},{1,9},{5... | collective-permute-start | bytes 589832 | tf_op jit(solution)/shard_map/ppermute | solution.py:315
  60.5 7.2 %collective-permute-start.18 = (f32[48,1024]{1,0:T(8,128)S(1)}, f32[48,1024]{1,0:T(8,128)S(1)}, u32[]{:S(2)}, u32[]{:S(2)}) collective-permute-start(f32[48,1024]{1,0:T(8,128)S(1)} %pad_maximum_fusion.4), channel_id=1, source_target_pairs={{0,4},{4,0},{8,12},{12,8},{16,20},{20,16},{24,28},{28,24},{1,5},{5... | collective-permute-start | bytes 589832 | tf_op jit(solution)/shard_map/ppermute | solution.py:315
  63.6 7.4 %collective-permute-start.15 = (f32[48,1024]{1,0:T(8,128)S(1)}, f32[48,1024]{1,0:T(8,128)S(1)}, u32[]{:S(2)}, u32[]{:S(2)}) collective-permute-start(f32[48,1024]{1,0:T(8,128)S(1)} %pad_maximum_fusion.3), channel_id=1, source_target_pairs={{0,8},{4,12},{8,0},{12,4},{16,24},{20,28},{24,16},{28,20},{1,9},{5... | collective-permute-start | bytes 589832 | tf_op jit(solution)/shard_map/ppermute | solution.py:315
  64.7 6.2 %collective-permute-start.13 = (f32[48,1024]{1,0:T(8,128)S(1)}, f32[48,1024]{1,0:T(8,128)S(1)}, u32[]{:S(2)}, u32[]{:S(2)}) collective-permute-start(f32[48,1024]{1,0:T(8,128)S(1)} %pad_maximum_fusion.2), channel_id=1, source_target_pairs={{0,4},{4,0},{8,12},{12,8},{16,20},{20,16},{24,28},{28,24},{1,5},{5... | collective-permute-start | bytes 589832 | tf_op jit(solution)/shard_map/ppermute | solution.py:315

commit v8 on v6

--- a/solution.py
+++ b/solution.py
@@ -11,8 +11,8 @@
 BF16 = jnp.bfloat16
 VMEM_LIMIT = 40 * 1024 * 1024
 LANES = 128
-CHUNKS = 1
-AHEAD = 6
+CHUNKS = 2
+AHEAD = 8
 UNIT = 512
 PANEL = 4
 LAST = (((1,), (1,)), ((), ()))
@@ -76,7 +76,7 @@
 def tall_partial(probes, sketch_t):
     rows, cols = probes.shape
     rank = sketch_t.shape[0]
-    unit = min(UNIT, cols)
+    unit = min(2 * UNIT, cols)
     blocks = cols // unit
     return pl.pallas_call(
         tall_kernel,
@@ -341,63 +341,69 @@
             ([block_b(c, p, 1), block_b(c, p, 0)], False),
         ]
 
-    both, gram, first = first_products(tall, other, probes, outputs(0, 1), width)
-    plan = [(c, p) for c in range(CHUNKS) for p in (1, 0) if (c, p) != (0, 1)]
-    rest = rest_products(
-        both, gram, probes, [out for c, p in plan for out in outputs(c, p)], width, first[0]
-    )
-    made = {(0, 1): first}
-    made.update({key: rest[2 * k : 2 * k + 2] for k, key in enumerate(plan)})
-
-    inverse, out = None, None
+    both, gram, away = first_products(tall, other, probes, outputs(0, 1), width)
+
+    def after(value, *others):
+        return lax.optimization_barrier((value, *others))[0]
+
+    whole, total = [], []
+    ready = away[0]
     for c in range(CHUNKS):
         g = LANES if c == 0 else 0
-        away_a, away_b = made[c, 1]
-        own_a, own_b = made[c, 0]
-        sum_a = own_a + over(away_a, 1)
+        more = outputs(c + 1, 1) if c + 1 < CHUNKS else []
+        made = rest_products(both, gram, probes, outputs(c, 0) + more, width, ready)
+        away_a, away_b = away
+        (own_a, own_b), away = made[:2], made[2:]
+        if c > 0:
+            away_a, away_b = after(away_a, whole[-1]), after(away_b, whole[-1])
+        ready = over(away_a, 1)
+        sum_a = own_a + ready
         sum_b = own_b + over(away_b, 2)
         got_a = over(sum_a[:, : width + g], 2)
         got_b = over(sum_b[:, :width], 1)
-        whole = jnp.concatenate(
-            [
-                sum_a[:, width + g :] + got_a[:, :width],
-                sum_a[:, width : width + g] + got_a[:, width:],
-                sum_b[:, width:] + got_b,
-            ],
-            axis=1,
+        whole.append(
+            jnp.concatenate(
+                [
+                    sum_a[:, width + g :] + got_a[:, :width],
+                    sum_a[:, width : width + g] + got_a[:, width:],
+                    sum_b[:, width:] + got_b,
+                ],
+                axis=1,
+            )
         )
+        added = whole[-1]
         bit = 4
         while bit < n_pos:
-            whole = whole + over(whole, bit)
+            added = added + over(added, bit)
             bit *= 2
-        if c == 0:
-            inverse = inverse_factor(whole, width)
-        mine_a, mine_b = whole[:, :width], whole[:, width + g :]
+        total.append(added)
+
+    out, inverse, done = None, None, ()
+    for c in range(CHUNKS):
+        g = LANES if c == 0 else 0
+        mine_a, mine_b = total[c][:, :width], total[c][:, width + g :]
+        wait = whole[c + 1 : c + 2] + ([] if c == 0 else [inverse, *done])
+        if wait:
+            mine_a, mine_b = after(mine_a, *wait), after(mine_b, *wait)
         next_a = over(mine_a, 2)
         next_b = over(mine_b, 1)
+        done = (next_a, next_b)
+        if c == 0:
+            inverse = inverse_factor(after(total[0], *done), width)
         last_a = over(jnp.concatenate([mine_a, next_a], axis=1), 1)
         last_b = over(jnp.concatenate([mine_b, next_b], axis=1), 2)
         out = finish(
             inverse,
-            [whole, next_a, next_b],
+            [total[c], next_a, next_b, last_a, last_b],
             [
                 (block_a(c, 0, 0), 0, 0),
                 (block_b(c, 0, 0), 0, width + g),
                 (block_a(c, 0, 1), 1, 0),
                 (block_b(c, 0, 1), 2, 0),
-            ],
-            width,
-            cols,
-            out,
-        )
-        out = finish(
-            inverse,
-            [last_a, last_b],
-            [
-                (block_a(c, 1, 0), 0, 0),
-                (block_a(c, 1, 1), 0, width),
-                (block_b(c, 1, 0), 1, 0),
-                (block_b(c, 1, 1), 1, width),
+                (block_a(c, 1, 0), 3, 0),
+                (block_a(c, 1, 1), 3, width),
+                (block_b(c, 1, 0), 4, 0),
+                (block_b(c, 1, 1), 4, width),
             ],
             width,
             cols,

time: 77.3 us -> 80 us (1.035)
  waiting for transfers between devices: 36.1 us -> 28.3 us
  starting transfers between devices: 16.8 us -> 23.3 us
  Pallas kernels: 23.5 us -> 27.3 us
    ppermute x11 -> x20, waiting for transfers between devices: 36.1 us -> 28.3 us  [swap(): return lax.ppermute(value, axis, [(i, i ^ bit) for i in range(size)])]
    ppermute x11 -> x20, starting transfers between devices: 16.8 us -> 23.3 us  [swap(): return lax.ppermute(value, axis, [(i, i ^ bit) for i in range(size)])]
    pallas_call x1, Pallas kernels: 8.61 us -> 11.1 us  [tall_partial(): pl.pallas_call(tall_kernel, in_specs=[HBM, HBM], out_specs=WHOLE, out_sha...]
    pallas_call x2 -> x3, Pallas kernels: 9.44 us -> 10.8 us  [products(): pl.pallas_call(functools.partial(kernel, plan, grams), in_specs=[TABLE, *...]
  transfers between devices with their start and end apart: 11 -> 20, of which waited for: 11 -> 13; matrix products, arithmetic and copies ran while one was open for 1% -> 1% of each run, Pallas kernels for 11% -> 14%
where the time goes in v8:
time: 80 us; the launch traced here: 79.9 us
  waiting for transfers between devices  28.3 us (35%)
  Pallas kernels  27.3 us (34%)
  starting transfers between devices  23.3 us (29%)
    ppermute x20, waiting for transfers between devices, swap(): return lax.ppermute(value, axis, [(i, i ^ bit) for i in range(size)])  28.3 us
    ppermute x20, starting transfers between devices, swap(): return lax.ppermute(value, axis, [(i, i ^ bit) for i in range(size)])  23.3 us
    pallas_call x1, Pallas kernels, tall_partial(): pl.pallas_call(tall_kernel, in_specs=[HBM, HBM], out_specs=WHOLE, out_sha...  11.1 us
    pallas_call x3, Pallas kernels, products(): pl.pallas_call(functools.partial(kernel, plan, grams), in_specs=[TABLE, *...  10.8 us
    pallas_call x2, Pallas kernels, finish(): pl.pallas_call(functools.partial(finish_kernel, [piece[1:] for piece in p...  3.39 us
    pallas_call x1, Pallas kernels, inverse_factor(): pl.pallas_call(inverse_kernel, grid=(1,), in_specs=[pl.BlockSpec((rank, L...  2.01 us
  transfers between devices with their start and end apart: 20, of which 13 were waited for; matrix products, arithmetic and copies ran while one was open for 1% of the time, Pallas kernels for 14%

profile of v8, /device:TPU:0, one launch (start us, length us, event | category | flops | bytes accessed | tf_op | source)
XLA Modules:
  0.0 79.9 jit_solution(9915834272354389808)
XLA Ops:
  0.0 11.1 %tall_partial.1 = f32[48,512]{1,0:T(8,128)S(1)} custom-call(f32[512,8192]{1,0:T(8,128)} %x_hbm.7, f32[48,8192]{1,0:T(8,128)} %bitcast.17), custom_call_target="tpu_custom_call" | custom-call | flops 1207959552 | bytes 16777216 | tf_op jit(solution)/shard_map/tall_partial/pallas_call | solution.py:81
  12.6 2.9 %collective-permute-start.1 = (f32[48,512]{1,0:T(8,128)S(1)}, f32[48,512]{1,0:T(8,128)S(1)}, u32[]{:S(2)}, u32[]{:S(2)}) collective-permute-start(f32[48,512]{1,0:T(8,128)S(1)} %add.158.one_ref), channel_id=1, source_target_pairs={{0,2},{1,3},{2,0},{3,1},{4,6},{5,7},{6,4},{7,5},{8,10},{9,11},{10,... | collective-permute-start | bytes 294920 | tf_op jit(solution)/shard_map/ppermute | solution.py:315
  15.6 3.0 %collective-permute-done.1.two_ref = f32[48,512]{1,0:T(8,128)S(1)} collective-permute-done((f32[48,512]{1,0:T(8,128)S(1)}, f32[48,512]{1,0:T(8,128)S(1)}, u32[]{:S(2)}, u32[]{:S(2)}) %collective-permute-start.1) | collective-permute-done | bytes 98336 | tf_op jit(solution)/shard_map/ppermute | solution.py:315
  18.6 3.4 %first_products.1 = (bf16[96,512]{1,0:T(8,128)(2,1)S(1)}, f32[48,128]{1,0:T(8,128)S(1)}, f32[48,1152]{1,0:T(8,128)S(1)}, f32[48,1024]{1,0:T(8,128)S(1)}) custom-call(s32[4]{0:T(128)S(1)} %pad_add_fusion.which_ref, f32[48,512]{1,0:T(8,128)S(1)} %add.158.one_ref, f32[48,512]{1,0:T(8,128)S(1)} %collective-permute-done.1.two_ref, f32[512,8192]{1,0:T(8,128)} %x_hbm.7), custom_call_target="tpu_custom_call" | custom-call | flops 301989888 | bytes 4194304 | tf_op jit(solution)/shard_map/first_products/pallas_call | solution.py:177
  22.0 1.9 %collective-permute-start.4 = (f32[48,1024]{1,0:T(8,128)S(1)}, f32[48,1024]{1,0:T(8,128)S(1)}, u32[]{:S(2)}, u32[]{:S(2)}) collective-permute-start(f32[48,1024]{1,0:T(8,128)S(1)} %get-tuple-element.27), channel_id=1, source_target_pairs={{0,8},{4,12},{8,0},{12,4},{16,24},{20,28},{24,16},{28,20},{1,9},{5... | collective-permute-start | bytes 589832 | tf_op jit(solution)/shard_map/ppermute | solution.py:315
  23.9 1.5 %collective-permute-start.2 = (f32[48,1152]{1,0:T(8,128)S(1)}, f32[48,1152]{1,0:T(8,128)S(1)}, u32[]{:S(2)}, u32[]{:S(2)}) collective-permute-start(f32[48,1152]{1,0:T(8,128)S(1)} %get-tuple-element.24.after_ref), channel_id=1, source_target_pairs={{0,4},{4,0},{8,12},{12,8},{16,20},{20,16},{24,28},{28,24},{1,5},{5... | collective-permute-start | bytes 663560 | tf_op jit(solution)/shard_map/ppermute | solution.py:315
  25.4 4.4 %rest_products.2 = (f32[48,1152]{1,0:T(8,128)S(1)}, f32[48,1024]{1,0:T(8,128)S(1)}, f32[48,1024]{1,0:T(8,128)S(1)}, f32[48,1024]{1,0:T(8,128)S(1)}) custom-call(s32[8]{0:T(128)S(1)} %stack.92.which_ref, bf16[96,512]{1,0:T(8,128)(2,1)S(1)} %get-tuple-element.22.both_ref, f32[48,128]{1,0:T(8,128)S(1)} %get-tuple-element.23.gram_ref, f32[512,8192]{1,0:T(8,128)} %x_hbm.7, ...), custom_call_target="tpu_custom_call" | custom-call | flops 603979776 | bytes 8388608 | tf_op jit(solution)/shard_map/rest_products/pallas_call | solution.py:177
  31.7 2.8 %collective-permute-done.5 = f32[48,512]{1,0:T(8,128)S(1)} collective-permute-done((f32[48,512]{1,0:T(8,128)S(1)}, f32[48,512]{1,0:T(8,128)S(1)}, u32[]{:S(2)}, u32[]{:S(2)}) %collective-permute-start.5) | collective-permute-done | bytes 98336 | tf_op jit(solution)/shard_map/ppermute | solution.py:315
  35.5 3.6 %collective-permute-start.6 = (f32[48,1152]{1,0:T(8,128)S(1)}, f32[48,1152]{1,0:T(8,128)S(1)}, u32[]{:S(2)}, u32[]{:S(2)}) collective-permute-start(f32[48,1152]{1,0:T(8,128)S(1)} %pad_maximum_fusion), channel_id=1, source_target_pairs={{0,16},{4,20},{8,24},{12,28},{16,0},{20,4},{24,8},{28,12},{1,17},{... | collective-permute-start | bytes 663560 | tf_op jit(solution)/shard_map/ppermute | solution.py:315
  39.5 1.3 %collective-permute-start.7 = (f32[48,1024]{1,0:T(8,128)S(1)}, f32[48,1024]{1,0:T(8,128)S(1)}, u32[]{:S(2)}, u32[]{:S(2)}) collective-permute-start(f32[48,1024]{1,0:T(8,128)S(1)} %get-tuple-element.30), channel_id=1, source_target_pairs={{0,4},{4,0},{8,12},{12,8},{16,20},{20,16},{24,28},{28,24},{1,5},{5... | collective-permute-start | bytes 589832 | tf_op jit(solution)/shard_map/ppermute | solution.py:315
  40.9 3.1 %rest_products.3 = (f32[48,1024]{1,0:T(8,128)S(1)}, f32[48,1024]{1,0:T(8,128)S(1)}) custom-call(s32[4]{0:T(128)S(1)} %pad_add_fusion.1.which_ref, bf16[96,512]{1,0:T(8,128)(2,1)S(1)} %get-tuple-element.22.both_ref, f32[48,128]{1,0:T(8,128)S(1)} %get-tuple-element.23.gram_ref, f32[512,8192]{1,0:T(8,128)} %x_hbm.7, f32[48,1152]{1,0:T(8,128)S(1)} %collective-permute-done.2.after_ref), custom_call_target="tpu_custom_call" | custom-call | flops 301989888 | bytes 4194304 | tf_op jit(solution)/shard_map/rest_products/pallas_call | solution.py:177
  44.0 3.2 %collective-permute-done.9 = f32[48,1024]{1,0:T(8,128)S(1)} collective-permute-done((f32[48,1024]{1,0:T(8,128)S(1)}, f32[48,1024]{1,0:T(8,128)S(1)}, u32[]{:S(2)}, u32[]{:S(2)}) %collective-permute-start.9) | collective-permute-done | bytes 196640 | tf_op jit(solution)/shard_map/ppermute | solution.py:315
  47.3 2.6 %collective-permute-start.10 = (f32[48,512]{1,0:T(8,128)S(1)}, f32[48,512]{1,0:T(8,128)S(1)}, u32[]{:S(2)}, u32[]{:S(2)}) collective-permute-start(f32[48,512]{1,0:T(8,128)S(1)} %slice.71), channel_id=1, source_target_pairs={{0,4},{4,0},{8,12},{12,8},{16,20},{20,16},{24,28},{28,24},{1,5},{5... | collective-permute-start | bytes 294920 | tf_op jit(solution)/shard_map/ppermute | solution.py:315
  50.3 2.6 %collective-permute-done.10 = f32[48,512]{1,0:T(8,128)S(1)} collective-permute-done((f32[48,512]{1,0:T(8,128)S(1)}, f32[48,512]{1,0:T(8,128)S(1)}, u32[]{:S(2)}, u32[]{:S(2)}) %collective-permute-start.10) | collective-permute-done | bytes 98336 | tf_op jit(solution)/shard_map/ppermute | solution.py:315
  52.9 2.7 %collective-permute-done.8 = f32[48,512]{1,0:T(8,128)S(1)} collective-permute-done((f32[48,512]{1,0:T(8,128)S(1)}, f32[48,512]{1,0:T(8,128)S(1)}, u32[]{:S(2)}, u32[]{:S(2)}) %collective-permute-start.8) | collective-permute-done | bytes 98336 | tf_op jit(solution)/shard_map/ppermute | solution.py:315
  56.0 4.3 %collective-permute-done.11.refs_1_ = f32[48,512]{1,0:T(8,128)S(1)} collective-permute-done((f32[48,512]{1,0:T(8,128)S(1)}, f32[48,512]{1,0:T(8,128)S(1)}, u32[]{:S(2)}, u32[]{:S(2)}) %collective-permute-start.11) | collective-permute-done | bytes 98336 | tf_op jit(solution)/shard_map/ppermute | solution.py:315
  61.3 2.2 %collective-permute-start.19 = (f32[48,1024]{1,0:T(8,128)S(1)}, f32[48,1024]{1,0:T(8,128)S(1)}, u32[]{:S(2)}, u32[]{:S(2)}) collective-permute-start(f32[48,1024]{1,0:T(8,128)S(1)} %pad_maximum_fusion.5), channel_id=1, source_target_pairs={{0,8},{4,12},{8,0},{12,4},{16,24},{20,28},{24,16},{28,20},{1,9},{5... | collective-permute-start | bytes 589832 | tf_op jit(solution)/shard_map/ppermute | solution.py:315
  63.5 2.0 %inverse_factor.1.inverse_ref = f32[48,48]{1,0:T(8,128)S(1)} custom-call(f32[48,1152]{1,0:T(8,128)S(1)} %fusion.1.gram_ref.refs_0_), custom_call_target="tpu_custom_call" | custom-call | flops 20000000 | bytes 49152 | tf_op jit(solution)/shard_map/inverse_factor/pallas_call | solution.py:252
  65.6 1.3 %collective-permute-start.15 = (f32[48,512]{1,0:T(8,128)S(1)}, f32[48,512]{1,0:T(8,128)S(1)}, u32[]{:S(2)}, u32[]{:S(2)}) collective-permute-start(f32[48,512]{1,0:T(8,128)S(1)} %get-tuple-element.38), channel_id=1, source_target_pairs={{0,4},{4,0},{8,12},{12,8},{16,20},{20,16},{24,28},{28,24},{1,5},{5... | collective-permute-start | bytes 294920 | tf_op jit(solution)/shard_map/ppermute | solution.py:315
  68.0 2.3 %collective-permute-done.15.refs_2_ = f32[48,512]{1,0:T(8,128)S(1)} collective-permute-done((f32[48,512]{1,0:T(8,128)S(1)}, f32[48,512]{1,0:T(8,128)S(1)}, u32[]{:S(2)}, u32[]{:S(2)}) %collective-permute-start.15) | collective-permute-done | bytes 98336 | tf_op jit(solution)/shard_map/ppermute | solution.py:315
  70.5 1.9 %collective-permute-done.14.refs_1_ = f32[48,512]{1,0:T(8,128)S(1)} collective-permute-done((f32[48,512]{1,0:T(8,128)S(1)}, f32[48,512]{1,0:T(8,128)S(1)}, u32[]{:S(2)}, u32[]{:S(2)}) %collective-permute-start.14) | collective-permute-done | bytes 98336 | tf_op jit(solution)/shard_map/ppermute | solution.py:315
  73.9 1.7 %finish.2.refs_5_ = f32[48,8192]{1,0:T(8,128)} custom-call(s32[8]{0:T(128)S(1)} %stack.99.where_ref, f32[48,48]{1,0:T(8,128)S(1)} %inverse_factor.1.inverse_ref, f32[48,1152]{1,0:T(8,128)S(1)} %fusion.1.gram_ref.refs_0_, f32[48,512]{1,0:T(8,128)S(1)} %collective-permute-done.11.refs_1_, f32[48,512]{1,0:T(8,128)S(1)} %collective-permute-done.12.refs_2_, ...), custom_call_target="tpu_custom_call" | custom-call | flops 56623104 | bytes 1572864 | tf_op jit(solution)/shard_map/finish/pallas_call | solution.py:293
  76.1 2.1 %collective-permute-done.16.refs_3_ = f32[48,1024]{1,0:T(8,128)S(1)} collective-permute-done((f32[48,1024]{1,0:T(8,128)S(1)}, f32[48,1024]{1,0:T(8,128)S(1)}, u32[]{:S(2)}, u32[]{:S(2)}) %collective-permute-start.16) | collective-permute-done | bytes 196640 | tf_op jit(solution)/shard_map/ppermute | solution.py:315
  78.2 1.7 %finish.3 = f32[48,8192]{1,0:T(8,128)} custom-call(s32[8]{0:T(128)S(1)} %stack.87.where_ref, f32[48,48]{1,0:T(8,128)S(1)} %inverse_factor.1.inverse_ref, f32[48,1024]{1,0:T(8,128)S(1)} %fusion.refs_0_, f32[48,512]{1,0:T(8,128)S(1)} %collective-permute-done.14.refs_1_, f32[48,512]{1,0:T(8,128)S(1)} %collective-permute-done.15.refs_2_, ...), custom_call_target="tpu_custom_call", output_to_operand_aliasing={{}: (7, {})} | custom-call | flops 56623104 | bytes 1572864 | tf_op jit(solution)/shard_map/finish/pallas_call | solution.py:293
  (52 shorter events, 10.1 us)
Async XLA Ops:
  11.1 1.5 %collective-permute-start = (f32[48,512]{1,0:T(8,128)S(1)}, f32[48,512]{1,0:T(8,128)S(1)}, u32[]{:S(2)}, u32[]{:S(2)}) collective-permute-start(f32[48,512]{1,0:T(8,128)S(1)} %tall_partial.1), channel_id=1, source_target_pairs={{0,1},{1,0},{2,3},{3,2},{4,5},{5,4},{6,7},{7,6},{8,9},{9,8},{10,11... | collective-permute-start | bytes 294920 | tf_op jit(solution)/shard_map/ppermute | solution.py:315
  12.6 6.0 %collective-permute-start.1 = (f32[48,512]{1,0:T(8,128)S(1)}, f32[48,512]{1,0:T(8,128)S(1)}, u32[]{:S(2)}, u32[]{:S(2)}) collective-permute-start(f32[48,512]{1,0:T(8,128)S(1)} %add.158.one_ref), channel_id=1, source_target_pairs={{0,2},{1,3},{2,0},{3,1},{4,6},{5,7},{6,4},{7,5},{8,10},{9,11},{10,... | collective-permute-start | bytes 294920 | tf_op jit(solution)/shard_map/ppermute | solution.py:315
  22.0 7.8 %collective-permute-start.4 = (f32[48,1024]{1,0:T(8,128)S(1)}, f32[48,1024]{1,0:T(8,128)S(1)}, u32[]{:S(2)}, u32[]{:S(2)}) collective-permute-start(f32[48,1024]{1,0:T(8,128)S(1)} %get-tuple-element.27), channel_id=1, source_target_pairs={{0,8},{4,12},{8,0},{12,4},{16,24},{20,28},{24,16},{28,20},{1,9},{5... | collective-permute-start | bytes 589832 | tf_op jit(solution)/shard_map/ppermute | solution.py:315
  23.9 6.6 %collective-permute-start.2 = (f32[48,1152]{1,0:T(8,128)S(1)}, f32[48,1152]{1,0:T(8,128)S(1)}, u32[]{:S(2)}, u32[]{:S(2)}) collective-permute-start(f32[48,1152]{1,0:T(8,128)S(1)} %get-tuple-element.24.after_ref), channel_id=1, source_target_pairs={{0,4},{4,0},{8,12},{12,8},{16,20},{20,16},{24,28},{28,24},{1,5},{5... | collective-permute-start | bytes 663560 | tf_op jit(solution)/shard_map/ppermute | solution.py:315
  29.9 4.7 %collective-permute-start.5 = (f32[48,512]{1,0:T(8,128)S(1)}, f32[48,512]{1,0:T(8,128)S(1)}, u32[]{:S(2)}, u32[]{:S(2)}) collective-permute-start(f32[48,512]{1,0:T(8,128)S(1)} %slice.66), channel_id=1, source_target_pairs={{0,4},{4,0},{8,12},{12,8},{16,20},{20,16},{24,28},{28,24},{1,5},{5... | collective-permute-start | bytes 294920 | tf_op jit(solution)/shard_map/ppermute | solution.py:315
  30.5 4.9 %collective-permute-start.3 = (f32[48,640]{1,0:T(8,128)S(1)}, f32[48,640]{1,0:T(8,128)S(1)}, u32[]{:S(2)}, u32[]{:S(2)}) collective-permute-start(f32[48,640]{1,0:T(8,128)S(1)} %slice.61), channel_id=1, source_target_pairs={{0,8},{4,12},{8,0},{12,4},{16,24},{20,28},{24,16},{28,20},{1,9},{5... | collective-permute-start | bytes 368648 | tf_op jit(solution)/shard_map/ppermute | solution.py:315
  35.5 14.7 %collective-permute-start.6 = (f32[48,1152]{1,0:T(8,128)S(1)}, f32[48,1152]{1,0:T(8,128)S(1)}, u32[]{:S(2)}, u32[]{:S(2)}) collective-permute-start(f32[48,1152]{1,0:T(8,128)S(1)} %pad_maximum_fusion), channel_id=1, source_target_pairs={{0,16},{4,20},{8,24},{12,28},{16,0},{20,4},{24,8},{28,12},{1,17},{... | collective-permute-start | bytes 663560 | tf_op jit(solution)/shard_map/ppermute | solution.py:315
  39.2 8.1 %collective-permute-start.9 = (f32[48,1024]{1,0:T(8,128)S(1)}, f32[48,1024]{1,0:T(8,128)S(1)}, u32[]{:S(2)}, u32[]{:S(2)}) collective-permute-start(f32[48,1024]{1,0:T(8,128)S(1)} %get-tuple-element.33), channel_id=1, source_target_pairs={{0,8},{4,12},{8,0},{12,4},{16,24},{20,28},{24,16},{28,20},{1,9},{5... | collective-permute-start | bytes 589832 | tf_op jit(solution)/shard_map/ppermute | solution.py:315
  39.5 10.3 %collective-permute-start.7 = (f32[48,1024]{1,0:T(8,128)S(1)}, f32[48,1024]{1,0:T(8,128)S(1)}, u32[]{:S(2)}, u32[]{:S(2)}) collective-permute-start(f32[48,1024]{1,0:T(8,128)S(1)} %get-tuple-element.30), channel_id=1, source_target_pairs={{0,4},{4,0},{8,12},{12,8},{16,20},{20,16},{24,28},{28,24},{1,5},{5... | collective-permute-start | bytes 589832 | tf_op jit(solution)/shard_map/ppermute | solution.py:315
  47.3 5.6 %collective-permute-start.10 = (f32[48,512]{1,0:T(8,128)S(1)}, f32[48,512]{1,0:T(8,128)S(1)}, u32[]{:S(2)}, u32[]{:S(2)}) collective-permute-start(f32[48,512]{1,0:T(8,128)S(1)} %slice.71), channel_id=1, source_target_pairs={{0,4},{4,0},{8,12},{12,8},{16,20},{20,16},{24,28},{28,24},{1,5},{5... | collective-permute-start | bytes 294920 | tf_op jit(solution)/shard_map/ppermute | solution.py:315
  49.9 5.7 %collective-permute-start.8 = (f32[48,512]{1,0:T(8,128)S(1)}, f32[48,512]{1,0:T(8,128)S(1)}, u32[]{:S(2)}, u32[]{:S(2)}) collective-permute-start(f32[48,512]{1,0:T(8,128)S(1)} %slice.69), channel_id=1, source_target_pairs={{0,8},{4,12},{8,0},{12,4},{16,24},{20,28},{24,16},{28,20},{1,9},{5... | collective-permute-start | bytes 294920 | tf_op jit(solution)/shard_map/ppermute | solution.py:315
  55.6 4.7 %collective-permute-start.11 = (f32[48,512]{1,0:T(8,128)S(1)}, f32[48,512]{1,0:T(8,128)S(1)}, u32[]{:S(2)}, u32[]{:S(2)}) collective-permute-start(f32[48,512]{1,0:T(8,128)S(1)} %get-tuple-element.34), channel_id=1, source_target_pairs={{0,8},{4,12},{8,0},{12,4},{16,24},{20,28},{24,16},{28,20},{1,9},{5... | collective-permute-start | bytes 294920 | tf_op jit(solution)/shard_map/ppermute | solution.py:315
  56.0 5.3 %collective-permute-start.12 = (f32[48,512]{1,0:T(8,128)S(1)}, f32[48,512]{1,0:T(8,128)S(1)}, u32[]{:S(2)}, u32[]{:S(2)}) collective-permute-start(f32[48,512]{1,0:T(8,128)S(1)} %get-tuple-element.35), channel_id=1, source_target_pairs={{0,4},{4,0},{8,12},{12,8},{16,20},{20,16},{24,28},{28,24},{1,5},{5... | collective-permute-start | bytes 294920 | tf_op jit(solution)/shard_map/ppermute | solution.py:315
  56.0 9.6 %collective-permute-start.13 = (f32[48,1024]{1,0:T(8,128)S(1)}, f32[48,1024]{1,0:T(8,128)S(1)}, u32[]{:S(2)}, u32[]{:S(2)}) collective-permute-start(f32[48,1024]{1,0:T(8,128)S(1)} %pad_maximum_fusion.1), channel_id=1, source_target_pairs={{0,16},{4,20},{8,24},{12,28},{16,0},{20,4},{24,8},{28,12},{1,17},{... | collective-permute-start | bytes 589832 | tf_op jit(solution)/shard_map/ppermute | solution.py:315
  61.3 12.5 %collective-permute-start.19 = (f32[48,1024]{1,0:T(8,128)S(1)}, f32[48,1024]{1,0:T(8,128)S(1)}, u32[]{:S(2)}, u32[]{:S(2)}) collective-permute-start(f32[48,1024]{1,0:T(8,128)S(1)} %pad_maximum_fusion.5), channel_id=1, source_target_pairs={{0,8},{4,12},{8,0},{12,4},{16,24},{20,28},{24,16},{28,20},{1,9},{5... | collective-permute-start | bytes 589832 | tf_op jit(solution)/shard_map/ppermute | solution.py:315
  65.6 4.7 %collective-permute-start.15 = (f32[48,512]{1,0:T(8,128)S(1)}, f32[48,512]{1,0:T(8,128)S(1)}, u32[]{:S(2)}, u32[]{:S(2)}) collective-permute-start(f32[48,512]{1,0:T(8,128)S(1)} %get-tuple-element.38), channel_id=1, source_target_pairs={{0,4},{4,0},{8,12},{12,8},{16,20},{20,16},{24,28},{28,24},{1,5},{5... | collective-permute-start | bytes 294920 | tf_op jit(solution)/shard_map/ppermute | solution.py:315
  66.9 7.0 %collective-permute-start.18 = (f32[48,1024]{1,0:T(8,128)S(1)}, f32[48,1024]{1,0:T(8,128)S(1)}, u32[]{:S(2)}, u32[]{:S(2)}) collective-permute-start(f32[48,1024]{1,0:T(8,128)S(1)} %pad_maximum_fusion.4), channel_id=1, source_target_pairs={{0,4},{4,0},{8,12},{12,8},{16,20},{20,16},{24,28},{28,24},{1,5},{5... | collective-permute-start | bytes 589832 | tf_op jit(solution)/shard_map/ppermute | solution.py:315
  67.8 4.6 %collective-permute-start.14 = (f32[48,512]{1,0:T(8,128)S(1)}, f32[48,512]{1,0:T(8,128)S(1)}, u32[]{:S(2)}, u32[]{:S(2)}) collective-permute-start(f32[48,512]{1,0:T(8,128)S(1)} %get-tuple-element.37), channel_id=1, source_target_pairs={{0,8},{4,12},{8,0},{12,4},{16,24},{20,28},{24,16},{28,20},{1,9},{5... | collective-permute-start | bytes 294920 | tf_op jit(solution)/shard_map/ppermute | solution.py:315
  70.3 5.7 %collective-permute-start.17 = (f32[48,1024]{1,0:T(8,128)S(1)}, f32[48,1024]{1,0:T(8,128)S(1)}, u32[]{:S(2)}, u32[]{:S(2)}) collective-permute-start(f32[48,1024]{1,0:T(8,128)S(1)} %pad_maximum_fusion.3), channel_id=1, source_target_pairs={{0,8},{4,12},{8,0},{12,4},{16,24},{20,28},{24,16},{28,20},{1,9},{5... | collective-permute-start | bytes 589832 | tf_op jit(solution)/shard_map/ppermute | solution.py:315
  72.4 5.7 %collective-permute-start.16 = (f32[48,1024]{1,0:T(8,128)S(1)}, f32[48,1024]{1,0:T(8,128)S(1)}, u32[]{:S(2)}, u32[]{:S(2)}) collective-permute-start(f32[48,1024]{1,0:T(8,128)S(1)} %pad_maximum_fusion.2), channel_id=1, source_target_pairs={{0,4},{4,0},{8,12},{12,8},{16,20},{20,16},{24,28},{28,24},{1,5},{5... | collective-permute-start | bytes 589832 | tf_op jit(solution)/shard_map/ppermute | solution.py:315

commit v9 on v8

--- a/solution.py
+++ b/solution.py
@@ -14,6 +14,7 @@
 CHUNKS = 2
 AHEAD = 8
 UNIT = 512
+TILE = 256
 PANEL = 4
 LAST = (((1,), (1,)), ((), ()))
 PLAIN = (((1,), (0,)), ((), ()))
@@ -31,6 +32,11 @@
 
 def dot(a, b, dims):
     return lax.dot_general(a, b, dims, preferred_element_type=F32)
+
+
+def tiles(size):
+    step = min(TILE, size)
+    return [slice(start, start + step) for start in range(0, size, step)]
 
 
 def in_hbm(x):
@@ -62,13 +68,17 @@
             sketch.wait()
         s_head, s_rest = split(s_buf[:, k * unit : (k + 1) * unit])
         s_both = jnp.concatenate([s_head, s_rest], axis=0)
-        x_head, x_rest = split(x_buf[k])
-        both = dot(s_both, x_head, LAST)
-        part = both[:rank] + (both[rank:] + dot(s_head, x_rest, LAST))
-        if k == 0:
-            out_ref[...] = part
-        else:
-            out_ref[...] += part
+        for rows in tiles(x_buf.shape[1]):
+            total = None
+            for cols in tiles(unit):
+                x_head, x_rest = split(x_buf[k, rows, cols])
+                both = dot(s_both[:, cols], x_head, LAST)
+                part = both[:rank] + (both[rank:] + dot(s_head[:, cols], x_rest, LAST))
+                total = part if total is None else total + part
+            if k == 0:
+                out_ref[:, rows] = total
+            else:
+                out_ref[:, rows] += total
 
     stream(copies, use)
 
@@ -76,7 +86,7 @@
 def tall_partial(probes, sketch_t):
     rows, cols = probes.shape
     rank = sketch_t.shape[0]
-    unit = min(2 * UNIT, cols)
+    unit = min(UNIT, cols)
     blocks = cols // unit
     return pl.pallas_call(
         tall_kernel,
@@ -110,12 +120,15 @@
     ]
 
     def use(k):
-        both = both_ref[...]
-        x_head, x_rest = split(x_buf[k])
-        first = dot(both, x_head, PLAIN)
-        second = dot(both[:rank], x_rest, PLAIN)
         out, offset = plan[k]
-        outs[out][:, offset : offset + unit] = first[:rank] + (first[rank:] + second)
+        for cols in tiles(unit):
+            total = None
+            for rows in tiles(x_buf.shape[1]):
+                x_head, x_rest = split(x_buf[k, rows, cols])
+                both = dot(both_ref[:, rows], x_head, PLAIN)
+                part = both[:rank] + (both[rank:] + dot(both_ref[:rank, rows], x_rest, PLAIN))
+                total = part if total is None else total + part
+            outs[out][:, offset + cols.start : offset + cols.stop] = total
 
     return copies, use
 
@@ -378,18 +391,17 @@
             bit *= 2
         total.append(added)
 
-    out, inverse, done = None, None, ()
+    out, inverse = None, None
     for c in range(CHUNKS):
         g = LANES if c == 0 else 0
         mine_a, mine_b = total[c][:, :width], total[c][:, width + g :]
-        wait = whole[c + 1 : c + 2] + ([] if c == 0 else [inverse, *done])
+        wait = whole[c + 1 : c + 2] + ([] if c == 0 else [inverse, last_a, last_b])
         if wait:
             mine_a, mine_b = after(mine_a, *wait), after(mine_b, *wait)
         next_a = over(mine_a, 2)
         next_b = over(mine_b, 1)
-        done = (next_a, next_b)
         if c == 0:
-            inverse = inverse_factor(after(total[0], *done), width)
+            inverse = inverse_factor(after(total[0], next_a, next_b), width)
         last_a = over(jnp.concatenate([mine_a, next_a], axis=1), 1)
         last_b = over(jnp.concatenate([mine_b, next_b], axis=1), 2)
         out = finish(

time: 80 us -> 80.6 us (level)
  waiting for transfers between devices: 28.3 us -> 30.8 us
  Pallas kernels: 27.3 us -> 25.6 us
    ppermute x20, waiting for transfers between devices: 28.3 us -> 30.8 us  [swap(): return lax.ppermute(value, axis, [(i, i ^ bit) for i in range(size)])]
    pallas_call x1, Pallas kernels: 11.1 us -> 9.47 us  [tall_partial(): pl.pallas_call(tall_kernel, in_specs=[HBM, HBM], out_specs=WHOLE, out_sha...]
where the time goes in v9:
time: 80.6 us; the launch traced here: 80.5 us
  waiting for transfers between devices  30.8 us (38%)
  Pallas kernels  25.6 us (32%)
  starting transfers between devices  23.1 us (29%)
    ppermute x20, waiting for transfers between devices, swap(): return lax.ppermute(value, axis, [(i, i ^ bit) for i in range(size)])  30.8 us
    ppermute x20, starting transfers between devices, swap(): return lax.ppermute(value, axis, [(i, i ^ bit) for i in range(size)])  23.1 us
    pallas_call x3, Pallas kernels, products(): pl.pallas_call(functools.partial(kernel, plan, grams), in_specs=[TABLE, *...  10.7 us
    pallas_call x1, Pallas kernels, tall_partial(): pl.pallas_call(tall_kernel, in_specs=[HBM, HBM], out_specs=WHOLE, out_sha...  9.47 us
    pallas_call x2, Pallas kernels, finish(): pl.pallas_call(functools.partial(finish_kernel, [piece[1:] for piece in p...  3.41 us
    pallas_call x1, Pallas kernels, inverse_factor(): pl.pallas_call(inverse_kernel, grid=(1,), in_specs=[pl.BlockSpec((rank, L...  2.01 us
  transfers between devices with their start and end apart: 20, of which 13 were waited for; matrix products, arithmetic and copies ran while one was open for 1% of the time, Pallas kernels for 14%

profile of v9, /device:TPU:0, one launch (start us, length us, event | category | flops | bytes accessed | tf_op | source)
XLA Modules:
  0.0 80.5 jit_solution(14877433217618403109)
XLA Ops:
  0.0 9.5 %tall_partial.1 = f32[48,512]{1,0:T(8,128)S(1)} custom-call(f32[512,8192]{1,0:T(8,128)} %x_hbm.7, f32[48,8192]{1,0:T(8,128)} %bitcast.17), custom_call_target="tpu_custom_call" | custom-call | flops 1207959552 | bytes 16777216 | tf_op jit(solution)/shard_map/tall_partial/pallas_call | solution.py:91
  11.0 2.9 %collective-permute-start.1 = (f32[48,512]{1,0:T(8,128)S(1)}, f32[48,512]{1,0:T(8,128)S(1)}, u32[]{:S(2)}, u32[]{:S(2)}) collective-permute-start(f32[48,512]{1,0:T(8,128)S(1)} %add.158.one_ref), channel_id=1, source_target_pairs={{0,2},{1,3},{2,0},{3,1},{4,6},{5,7},{6,4},{7,5},{8,10},{9,11},{10,... | collective-permute-start | bytes 294920 | tf_op jit(solution)/shard_map/ppermute | solution.py:328
  14.0 3.0 %collective-permute-done.1.two_ref = f32[48,512]{1,0:T(8,128)S(1)} collective-permute-done((f32[48,512]{1,0:T(8,128)S(1)}, f32[48,512]{1,0:T(8,128)S(1)}, u32[]{:S(2)}, u32[]{:S(2)}) %collective-permute-start.1) | collective-permute-done | bytes 98336 | tf_op jit(solution)/shard_map/ppermute | solution.py:328
  17.0 3.3 %first_products.1 = (bf16[96,512]{1,0:T(8,128)(2,1)S(1)}, f32[48,128]{1,0:T(8,128)S(1)}, f32[48,1152]{1,0:T(8,128)S(1)}, f32[48,1024]{1,0:T(8,128)S(1)}) custom-call(s32[4]{0:T(128)S(1)} %pad_add_fusion.which_ref, f32[48,512]{1,0:T(8,128)S(1)} %add.158.one_ref, f32[48,512]{1,0:T(8,128)S(1)} %collective-permute-done.1.two_ref, f32[512,8192]{1,0:T(8,128)} %x_hbm.7), custom_call_target="tpu_custom_call" | custom-call | flops 301989888 | bytes 4194304 | tf_op jit(solution)/shard_map/first_products/pallas_call | solution.py:190
  20.4 1.9 %collective-permute-start.4 = (f32[48,1024]{1,0:T(8,128)S(1)}, f32[48,1024]{1,0:T(8,128)S(1)}, u32[]{:S(2)}, u32[]{:S(2)}) collective-permute-start(f32[48,1024]{1,0:T(8,128)S(1)} %get-tuple-element.27), channel_id=1, source_target_pairs={{0,8},{4,12},{8,0},{12,4},{16,24},{20,28},{24,16},{28,20},{1,9},{5... | collective-permute-start | bytes 589832 | tf_op jit(solution)/shard_map/ppermute | solution.py:328
  23.8 4.3 %rest_products.2 = (f32[48,1152]{1,0:T(8,128)S(1)}, f32[48,1024]{1,0:T(8,128)S(1)}, f32[48,1024]{1,0:T(8,128)S(1)}, f32[48,1024]{1,0:T(8,128)S(1)}) custom-call(s32[8]{0:T(128)S(1)} %stack.92.which_ref, bf16[96,512]{1,0:T(8,128)(2,1)S(1)} %get-tuple-element.22.both_ref, f32[48,128]{1,0:T(8,128)S(1)} %get-tuple-element.23.gram_ref, f32[512,8192]{1,0:T(8,128)} %x_hbm.7, ...), custom_call_target="tpu_custom_call" | custom-call | flops 603979776 | bytes 8388608 | tf_op jit(solution)/shard_map/rest_products/pallas_call | solution.py:190
  30.1 2.8 %collective-permute-done.5 = f32[48,512]{1,0:T(8,128)S(1)} collective-permute-done((f32[48,512]{1,0:T(8,128)S(1)}, f32[48,512]{1,0:T(8,128)S(1)}, u32[]{:S(2)}, u32[]{:S(2)}) %collective-permute-start.5) | collective-permute-done | bytes 98336 | tf_op jit(solution)/shard_map/ppermute | solution.py:328
  33.8 3.6 %collective-permute-start.6 = (f32[48,1152]{1,0:T(8,128)S(1)}, f32[48,1152]{1,0:T(8,128)S(1)}, u32[]{:S(2)}, u32[]{:S(2)}) collective-permute-start(f32[48,1152]{1,0:T(8,128)S(1)} %pad_maximum_fusion), channel_id=1, source_target_pairs={{0,16},{4,20},{8,24},{12,28},{16,0},{20,4},{24,8},{28,12},{1,17},{... | collective-permute-start | bytes 663560 | tf_op jit(solution)/shard_map/ppermute | solution.py:328
  39.3 3.1 %rest_products.3 = (f32[48,1024]{1,0:T(8,128)S(1)}, f32[48,1024]{1,0:T(8,128)S(1)}) custom-call(s32[4]{0:T(128)S(1)} %pad_add_fusion.1.which_ref, bf16[96,512]{1,0:T(8,128)(2,1)S(1)} %get-tuple-element.22.both_ref, f32[48,128]{1,0:T(8,128)S(1)} %get-tuple-element.23.gram_ref, f32[512,8192]{1,0:T(8,128)} %x_hbm.7, f32[48,1152]{1,0:T(8,128)S(1)} %collective-permute-done.2.after_ref), custom_call_target="tpu_custom_call" | custom-call | flops 301989888 | bytes 4194304 | tf_op jit(solution)/shard_map/rest_products/pallas_call | solution.py:190
  42.3 3.2 %collective-permute-done.9 = f32[48,1024]{1,0:T(8,128)S(1)} collective-permute-done((f32[48,1024]{1,0:T(8,128)S(1)}, f32[48,1024]{1,0:T(8,128)S(1)}, u32[]{:S(2)}, u32[]{:S(2)}) %collective-permute-start.9) | collective-permute-done | bytes 196640 | tf_op jit(solution)/shard_map/ppermute | solution.py:328
  45.5 2.7 %collective-permute-start.10 = (f32[48,512]{1,0:T(8,128)S(1)}, f32[48,512]{1,0:T(8,128)S(1)}, u32[]{:S(2)}, u32[]{:S(2)}) collective-permute-start(f32[48,512]{1,0:T(8,128)S(1)} %slice.71), channel_id=1, source_target_pairs={{0,4},{4,0},{8,12},{12,8},{16,20},{20,16},{24,28},{28,24},{1,5},{5... | collective-permute-start | bytes 294920 | tf_op jit(solution)/shard_map/ppermute | solution.py:328
  48.6 2.7 %collective-permute-done.10 = f32[48,512]{1,0:T(8,128)S(1)} collective-permute-done((f32[48,512]{1,0:T(8,128)S(1)}, f32[48,512]{1,0:T(8,128)S(1)}, u32[]{:S(2)}, u32[]{:S(2)}) %collective-permute-start.10) | collective-permute-done | bytes 98336 | tf_op jit(solution)/shard_map/ppermute | solution.py:328
  51.3 2.6 %collective-permute-done.8 = f32[48,512]{1,0:T(8,128)S(1)} collective-permute-done((f32[48,512]{1,0:T(8,128)S(1)}, f32[48,512]{1,0:T(8,128)S(1)}, u32[]{:S(2)}, u32[]{:S(2)}) %collective-permute-start.8) | collective-permute-done | bytes 98336 | tf_op jit(solution)/shard_map/ppermute | solution.py:328
  54.3 4.3 %collective-permute-done.11.refs_1_ = f32[48,512]{1,0:T(8,128)S(1)} collective-permute-done((f32[48,512]{1,0:T(8,128)S(1)}, f32[48,512]{1,0:T(8,128)S(1)}, u32[]{:S(2)}, u32[]{:S(2)}) %collective-permute-start.11) | collective-permute-done | bytes 98336 | tf_op jit(solution)/shard_map/ppermute | solution.py:328
  59.0 1.8 %collective-permute-start.15 = (f32[48,1024]{1,0:T(8,128)S(1)}, f32[48,1024]{1,0:T(8,128)S(1)}, u32[]{:S(2)}, u32[]{:S(2)}) collective-permute-start(f32[48,1024]{1,0:T(8,128)S(1)} %pad_maximum_fusion.3), channel_id=1, source_target_pairs={{0,8},{4,12},{8,0},{12,4},{16,24},{20,28},{24,16},{28,20},{1,9},{5... | collective-permute-start | bytes 589832 | tf_op jit(solution)/shard_map/ppermute | solution.py:328
  60.9 2.0 %inverse_factor.1.inverse_ref = f32[48,48]{1,0:T(8,128)S(1)} custom-call(f32[48,1152]{1,0:T(8,128)S(1)} %fusion.1.gram_ref.refs_0_), custom_call_target="tpu_custom_call" | custom-call | flops 20000000 | bytes 49152 | tf_op jit(solution)/shard_map/inverse_factor/pallas_call | solution.py:265
  63.0 3.5 %collective-permute-done.15.refs_4_ = f32[48,1024]{1,0:T(8,128)S(1)} collective-permute-done((f32[48,1024]{1,0:T(8,128)S(1)}, f32[48,1024]{1,0:T(8,128)S(1)}, u32[]{:S(2)}, u32[]{:S(2)}) %collective-permute-start.15) | collective-permute-done | bytes 196640 | tf_op jit(solution)/shard_map/ppermute | solution.py:328
  66.6 1.7 %collective-permute-start.16 = (f32[48,512]{1,0:T(8,128)S(1)}, f32[48,512]{1,0:T(8,128)S(1)}, u32[]{:S(2)}, u32[]{:S(2)}) collective-permute-start(f32[48,512]{1,0:T(8,128)S(1)} %get-tuple-element.37), channel_id=1, source_target_pairs={{0,8},{4,12},{8,0},{12,4},{16,24},{20,28},{24,16},{28,20},{1,9},{5... | collective-permute-start | bytes 294920 | tf_op jit(solution)/shard_map/ppermute | solution.py:328
  68.3 2.8 %collective-permute-done.17.refs_2_ = f32[48,512]{1,0:T(8,128)S(1)} collective-permute-done((f32[48,512]{1,0:T(8,128)S(1)}, f32[48,512]{1,0:T(8,128)S(1)}, u32[]{:S(2)}, u32[]{:S(2)}) %collective-permute-start.17) | collective-permute-done | bytes 98336 | tf_op jit(solution)/shard_map/ppermute | solution.py:328
  71.2 1.8 %collective-permute-start.19 = (f32[48,1024]{1,0:T(8,128)S(1)}, f32[48,1024]{1,0:T(8,128)S(1)}, u32[]{:S(2)}, u32[]{:S(2)}) collective-permute-start(f32[48,1024]{1,0:T(8,128)S(1)} %pad_maximum_fusion.5), channel_id=1, source_target_pairs={{0,8},{4,12},{8,0},{12,4},{16,24},{20,28},{24,16},{28,20},{1,9},{5... | collective-permute-start | bytes 589832 | tf_op jit(solution)/shard_map/ppermute | solution.py:328
  73.4 1.7 %finish.2.refs_5_ = f32[48,8192]{1,0:T(8,128)} custom-call(s32[8]{0:T(128)S(1)} %stack.99.where_ref, f32[48,48]{1,0:T(8,128)S(1)} %inverse_factor.1.inverse_ref, f32[48,1152]{1,0:T(8,128)S(1)} %fusion.1.gram_ref.refs_0_, f32[48,512]{1,0:T(8,128)S(1)} %collective-permute-done.11.refs_1_, f32[48,512]{1,0:T(8,128)S(1)} %collective-permute-done.12.refs_2_, ...), custom_call_target="tpu_custom_call" | custom-call | flops 56623104 | bytes 1572864 | tf_op jit(solution)/shard_map/finish/pallas_call | solution.py:306
  75.2 1.8 %collective-permute-done.19.refs_4_ = f32[48,1024]{1,0:T(8,128)S(1)} collective-permute-done((f32[48,1024]{1,0:T(8,128)S(1)}, f32[48,1024]{1,0:T(8,128)S(1)}, u32[]{:S(2)}, u32[]{:S(2)}) %collective-permute-start.19) | collective-permute-done | bytes 196640 | tf_op jit(solution)/shard_map/ppermute | solution.py:328
  76.9 1.9 %collective-permute-done.18.refs_3_ = f32[48,1024]{1,0:T(8,128)S(1)} collective-permute-done((f32[48,1024]{1,0:T(8,128)S(1)}, f32[48,1024]{1,0:T(8,128)S(1)}, u32[]{:S(2)}, u32[]{:S(2)}) %collective-permute-start.18) | collective-permute-done | bytes 196640 | tf_op jit(solution)/shard_map/ppermute | solution.py:328
  78.8 1.7 %finish.3 = f32[48,8192]{1,0:T(8,128)} custom-call(s32[8]{0:T(128)S(1)} %stack.87.where_ref, f32[48,48]{1,0:T(8,128)S(1)} %inverse_factor.1.inverse_ref, f32[48,1024]{1,0:T(8,128)S(1)} %fusion.refs_0_, f32[48,512]{1,0:T(8,128)S(1)} %collective-permute-done.16.refs_1_, f32[48,512]{1,0:T(8,128)S(1)} %collective-permute-done.17.refs_2_, ...), custom_call_target="tpu_custom_call", output_to_operand_aliasing={{}: (7, {})} | custom-call | flops 56623104 | bytes 1572864 | tf_op jit(solution)/shard_map/finish/pallas_call | solution.py:306
  (52 shorter events, 9.7 us)
Async XLA Ops:
  9.5 1.5 %collective-permute-start = (f32[48,512]{1,0:T(8,128)S(1)}, f32[48,512]{1,0:T(8,128)S(1)}, u32[]{:S(2)}, u32[]{:S(2)}) collective-permute-start(f32[48,512]{1,0:T(8,128)S(1)} %tall_partial.1), channel_id=1, source_target_pairs={{0,1},{1,0},{2,3},{3,2},{4,5},{5,4},{6,7},{7,6},{8,9},{9,8},{10,11... | collective-permute-start | bytes 294920 | tf_op jit(solution)/shard_map/ppermute | solution.py:328
  11.0 6.1 %collective-permute-start.1 = (f32[48,512]{1,0:T(8,128)S(1)}, f32[48,512]{1,0:T(8,128)S(1)}, u32[]{:S(2)}, u32[]{:S(2)}) collective-permute-start(f32[48,512]{1,0:T(8,128)S(1)} %add.158.one_ref), channel_id=1, source_target_pairs={{0,2},{1,3},{2,0},{3,1},{4,6},{5,7},{6,4},{7,5},{8,10},{9,11},{10,... | collective-permute-start | bytes 294920 | tf_op jit(solution)/shard_map/ppermute | solution.py:328
  20.4 7.8 %collective-permute-start.4 = (f32[48,1024]{1,0:T(8,128)S(1)}, f32[48,1024]{1,0:T(8,128)S(1)}, u32[]{:S(2)}, u32[]{:S(2)}) collective-permute-start(f32[48,1024]{1,0:T(8,128)S(1)} %get-tuple-element.27), channel_id=1, source_target_pairs={{0,8},{4,12},{8,0},{12,4},{16,24},{20,28},{24,16},{28,20},{1,9},{5... | collective-permute-start | bytes 589832 | tf_op jit(solution)/shard_map/ppermute | solution.py:328
  22.2 6.6 %collective-permute-start.2 = (f32[48,1152]{1,0:T(8,128)S(1)}, f32[48,1152]{1,0:T(8,128)S(1)}, u32[]{:S(2)}, u32[]{:S(2)}) collective-permute-start(f32[48,1152]{1,0:T(8,128)S(1)} %get-tuple-element.24.after_ref), channel_id=1, source_target_pairs={{0,4},{4,0},{8,12},{12,8},{16,20},{20,16},{24,28},{28,24},{1,5},{5... | collective-permute-start | bytes 663560 | tf_op jit(solution)/shard_map/ppermute | solution.py:328
  28.2 4.7 %collective-permute-start.5 = (f32[48,512]{1,0:T(8,128)S(1)}, f32[48,512]{1,0:T(8,128)S(1)}, u32[]{:S(2)}, u32[]{:S(2)}) collective-permute-start(f32[48,512]{1,0:T(8,128)S(1)} %slice.66), channel_id=1, source_target_pairs={{0,4},{4,0},{8,12},{12,8},{16,20},{20,16},{24,28},{28,24},{1,5},{5... | collective-permute-start | bytes 294920 | tf_op jit(solution)/shard_map/ppermute | solution.py:328
  28.9 4.9 %collective-permute-start.3 = (f32[48,640]{1,0:T(8,128)S(1)}, f32[48,640]{1,0:T(8,128)S(1)}, u32[]{:S(2)}, u32[]{:S(2)}) collective-permute-start(f32[48,640]{1,0:T(8,128)S(1)} %slice.61), channel_id=1, source_target_pairs={{0,8},{4,12},{8,0},{12,4},{16,24},{20,28},{24,16},{28,20},{1,9},{5... | collective-permute-start | bytes 368648 | tf_op jit(solution)/shard_map/ppermute | solution.py:328
  33.8 14.7 %collective-permute-start.6 = (f32[48,1152]{1,0:T(8,128)S(1)}, f32[48,1152]{1,0:T(8,128)S(1)}, u32[]{:S(2)}, u32[]{:S(2)}) collective-permute-start(f32[48,1152]{1,0:T(8,128)S(1)} %pad_maximum_fusion), channel_id=1, source_target_pairs={{0,16},{4,20},{8,24},{12,28},{16,0},{20,4},{24,8},{28,12},{1,17},{... | collective-permute-start | bytes 663560 | tf_op jit(solution)/shard_map/ppermute | solution.py:328
  37.4 8.1 %collective-permute-start.9 = (f32[48,1024]{1,0:T(8,128)S(1)}, f32[48,1024]{1,0:T(8,128)S(1)}, u32[]{:S(2)}, u32[]{:S(2)}) collective-permute-start(f32[48,1024]{1,0:T(8,128)S(1)} %get-tuple-element.33), channel_id=1, source_target_pairs={{0,8},{4,12},{8,0},{12,4},{16,24},{20,28},{24,16},{28,20},{1,9},{5... | collective-permute-start | bytes 589832 | tf_op jit(solution)/shard_map/ppermute | solution.py:328
  37.9 10.3 %collective-permute-start.7 = (f32[48,1024]{1,0:T(8,128)S(1)}, f32[48,1024]{1,0:T(8,128)S(1)}, u32[]{:S(2)}, u32[]{:S(2)}) collective-permute-start(f32[48,1024]{1,0:T(8,128)S(1)} %get-tuple-element.30), channel_id=1, source_target_pairs={{0,4},{4,0},{8,12},{12,8},{16,20},{20,16},{24,28},{28,24},{1,5},{5... | collective-permute-start | bytes 589832 | tf_op jit(solution)/shard_map/ppermute | solution.py:328
  45.5 5.7 %collective-permute-start.10 = (f32[48,512]{1,0:T(8,128)S(1)}, f32[48,512]{1,0:T(8,128)S(1)}, u32[]{:S(2)}, u32[]{:S(2)}) collective-permute-start(f32[48,512]{1,0:T(8,128)S(1)} %slice.71), channel_id=1, source_target_pairs={{0,4},{4,0},{8,12},{12,8},{16,20},{20,16},{24,28},{28,24},{1,5},{5... | collective-permute-start | bytes 294920 | tf_op jit(solution)/shard_map/ppermute | solution.py:328
  48.2 5.7 %collective-permute-start.8 = (f32[48,512]{1,0:T(8,128)S(1)}, f32[48,512]{1,0:T(8,128)S(1)}, u32[]{:S(2)}, u32[]{:S(2)}) collective-permute-start(f32[48,512]{1,0:T(8,128)S(1)} %slice.69), channel_id=1, source_target_pairs={{0,8},{4,12},{8,0},{12,4},{16,24},{20,28},{24,16},{28,20},{1,9},{5... | collective-permute-start | bytes 294920 | tf_op jit(solution)/shard_map/ppermute | solution.py:328
  54.0 4.7 %collective-permute-start.11 = (f32[48,512]{1,0:T(8,128)S(1)}, f32[48,512]{1,0:T(8,128)S(1)}, u32[]{:S(2)}, u32[]{:S(2)}) collective-permute-start(f32[48,512]{1,0:T(8,128)S(1)} %get-tuple-element.34), channel_id=1, source_target_pairs={{0,8},{4,12},{8,0},{12,4},{16,24},{20,28},{24,16},{28,20},{1,9},{5... | collective-permute-start | bytes 294920 | tf_op jit(solution)/shard_map/ppermute | solution.py:328
  54.3 4.6 %collective-permute-start.12 = (f32[48,512]{1,0:T(8,128)S(1)}, f32[48,512]{1,0:T(8,128)S(1)}, u32[]{:S(2)}, u32[]{:S(2)}) collective-permute-start(f32[48,512]{1,0:T(8,128)S(1)} %get-tuple-element.35), channel_id=1, source_target_pairs={{0,4},{4,0},{8,12},{12,8},{16,20},{20,16},{24,28},{28,24},{1,5},{5... | collective-permute-start | bytes 294920 | tf_op jit(solution)/shard_map/ppermute | solution.py:328
  54.3 8.6 %collective-permute-start.13 = (f32[48,1024]{1,0:T(8,128)S(1)}, f32[48,1024]{1,0:T(8,128)S(1)}, u32[]{:S(2)}, u32[]{:S(2)}) collective-permute-start(f32[48,1024]{1,0:T(8,128)S(1)} %pad_maximum_fusion.1), channel_id=1, source_target_pairs={{0,16},{4,20},{8,24},{12,28},{16,0},{20,4},{24,8},{28,12},{1,17},{... | collective-permute-start | bytes 589832 | tf_op jit(solution)/shard_map/ppermute | solution.py:328
  59.0 7.6 %collective-permute-start.15 = (f32[48,1024]{1,0:T(8,128)S(1)}, f32[48,1024]{1,0:T(8,128)S(1)}, u32[]{:S(2)}, u32[]{:S(2)}) collective-permute-start(f32[48,1024]{1,0:T(8,128)S(1)} %pad_maximum_fusion.3), channel_id=1, source_target_pairs={{0,8},{4,12},{8,0},{12,4},{16,24},{20,28},{24,16},{28,20},{1,9},{5... | collective-permute-start | bytes 589832 | tf_op jit(solution)/shard_map/ppermute | solution.py:328
  60.8 5.8 %collective-permute-start.14 = (f32[48,1024]{1,0:T(8,128)S(1)}, f32[48,1024]{1,0:T(8,128)S(1)}, u32[]{:S(2)}, u32[]{:S(2)}) collective-permute-start(f32[48,1024]{1,0:T(8,128)S(1)} %pad_maximum_fusion.2), channel_id=1, source_target_pairs={{0,4},{4,0},{8,12},{12,8},{16,20},{20,16},{24,28},{28,24},{1,5},{5... | collective-permute-start | bytes 589832 | tf_op jit(solution)/shard_map/ppermute | solution.py:328
  66.5 4.6 %collective-permute-start.17 = (f32[48,512]{1,0:T(8,128)S(1)}, f32[48,512]{1,0:T(8,128)S(1)}, u32[]{:S(2)}, u32[]{:S(2)}) collective-permute-start(f32[48,512]{1,0:T(8,128)S(1)} %get-tuple-element.38), channel_id=1, source_target_pairs={{0,4},{4,0},{8,12},{12,8},{16,20},{20,16},{24,28},{28,24},{1,5},{5... | collective-permute-start | bytes 294920 | tf_op jit(solution)/shard_map/ppermute | solution.py:328
  66.6 6.4 %collective-permute-start.16 = (f32[48,512]{1,0:T(8,128)S(1)}, f32[48,512]{1,0:T(8,128)S(1)}, u32[]{:S(2)}, u32[]{:S(2)}) collective-permute-start(f32[48,512]{1,0:T(8,128)S(1)} %get-tuple-element.37), channel_id=1, source_target_pairs={{0,8},{4,12},{8,0},{12,4},{16,24},{20,28},{24,16},{28,20},{1,9},{5... | collective-permute-start | bytes 294920 | tf_op jit(solution)/shard_map/ppermute | solution.py:328
  71.2 5.7 %collective-permute-start.19 = (f32[48,1024]{1,0:T(8,128)S(1)}, f32[48,1024]{1,0:T(8,128)S(1)}, u32[]{:S(2)}, u32[]{:S(2)}) collective-permute-start(f32[48,1024]{1,0:T(8,128)S(1)} %pad_maximum_fusion.5), channel_id=1, source_target_pairs={{0,8},{4,12},{8,0},{12,4},{16,24},{20,28},{24,16},{28,20},{1,9},{5... | collective-permute-start | bytes 589832 | tf_op jit(solution)/shard_map/ppermute | solution.py:328
  73.0 5.7 %collective-permute-start.18 = (f32[48,1024]{1,0:T(8,128)S(1)}, f32[48,1024]{1,0:T(8,128)S(1)}, u32[]{:S(2)}, u32[]{:S(2)}) collective-permute-start(f32[48,1024]{1,0:T(8,128)S(1)} %pad_maximum_fusion.4), channel_id=1, source_target_pairs={{0,4},{4,0},{8,12},{12,8},{16,20},{20,16},{24,28},{28,24},{1,5},{5... | collective-permute-start | bytes 589832 | tf_op jit(solution)/shard_map/ppermute | solution.py:328

commit v10 on v9

--- a/solution.py
+++ b/solution.py
@@ -11,7 +11,7 @@
 BF16 = jnp.bfloat16
 VMEM_LIMIT = 40 * 1024 * 1024
 LANES = 128
-CHUNKS = 2
+CHUNKS = 1
 AHEAD = 8
 UNIT = 512
 TILE = 256
@@ -53,7 +53,7 @@
         use(k)
 
 
-def tall_kernel(x_hbm, s_hbm, out_ref, x_buf, s_buf, x_sems, s_sem):
+def tall_kernel(x_hbm, s_hbm, out_ref, x_buf, s_buf, acc_ref, x_sems, s_sem):
     blocks, _, unit = x_buf.shape
     rank = s_hbm.shape[0]
     copies = [
@@ -66,21 +66,17 @@
     def use(k):
         if k == 0:
             sketch.wait()
-        s_head, s_rest = split(s_buf[:, k * unit : (k + 1) * unit])
-        s_both = jnp.concatenate([s_head, s_rest], axis=0)
-        for rows in tiles(x_buf.shape[1]):
-            total = None
-            for cols in tiles(unit):
-                x_head, x_rest = split(x_buf[k, rows, cols])
-                both = dot(s_both[:, cols], x_head, LAST)
-                part = both[:rank] + (both[rank:] + dot(s_head[:, cols], x_rest, LAST))
-                total = part if total is None else total + part
-            if k == 0:
-                out_ref[:, rows] = total
-            else:
-                out_ref[:, rows] += total
+        s_both = jnp.concatenate(split(s_buf[:, k * unit : (k + 1) * unit]), axis=0)
+        x_head, x_rest = split(x_buf[k])
+        part = dot(x_head, s_both, LAST) + dot(x_rest, s_both, LAST)
+        if k == 0:
+            acc_ref[...] = part
+        else:
+            acc_ref[...] += part
 
     stream(copies, use)
+    acc = acc_ref[...].T
+    out_ref[...] = acc[:rank] + acc[rank:]
 
 
 def tall_partial(probes, sketch_t):
@@ -96,12 +92,13 @@
         scratch_shapes=[
             pltpu.VMEM((blocks, rows, unit), F32),
             pltpu.VMEM((rank, cols), F32),
+            pltpu.VMEM((rows, 2 * rank), F32),
             pltpu.SemaphoreType.DMA((blocks,)),
             pltpu.SemaphoreType.DMA,
         ],
         compiler_params=PARAMS,
         cost_estimate=pl.CostEstimate(
-            flops=6 * rows * cols * rank, bytes_accessed=4 * rows * cols, transcendentals=0
+            flops=8 * rows * cols * rank, bytes_accessed=4 * rows * cols, transcendentals=0
         ),
         name="tall_partial",
     )(in_hbm(probes), in_hbm(sketch_t))
@@ -133,9 +130,9 @@
     return copies, use
 
 
-def first_kernel(plan, grams, which_ref, one_ref, two_ref, x_hbm, both_ref, gram_ref, *refs):
+def first_kernel(plan, early, grams, table, one_ref, two_ref, x_hbm, both_ref, gram_ref, *refs):
     outs, (x_buf, sems) = refs[:-2], refs[-2:]
-    copies, use = multiply_blocks(both_ref, which_ref, x_hbm, x_buf, sems, plan, outs)
+    copies, use = multiply_blocks(both_ref, table, x_hbm, x_buf, sems, plan, outs)
 
     def use_first(k):
         if k == 0:
@@ -144,7 +141,12 @@
             both_ref[...] = jnp.concatenate([head, rest], axis=0)
         use(k)
 
-    stream(copies, use_first)
+    stream(copies[:early], use_first)
+
+    @pl.when(table[len(plan)] == 1)
+    def _():
+        stream(copies[early:], lambda k: use(early + k))
+
     tall = one_ref[...] + two_ref[...]
     r = tall.shape[0]
     head, rest = split(tall)
@@ -159,12 +161,20 @@
         outs[out][:, offset : offset + LANES] = gram_ref[...]
 
 
-def rest_kernel(plan, grams, which_ref, both_ref, gram_ref, x_hbm, after_ref, *refs):
-    outs, (x_buf, sems) = refs[:-2], refs[-2:]
-    copies, use = multiply_blocks(both_ref, which_ref, x_hbm, x_buf, sems, plan, outs)
-    stream(copies, use)
-    for out, offset in grams:
-        outs[out][:, offset : offset + LANES] = gram_ref[...]
+def rest_kernel(plan, grams, table, both_ref, gram_ref, x_hbm, *refs):
+    outs, (x_buf, sems) = refs[-4:-2], refs[-2:]
+    copies, use = multiply_blocks(both_ref, table, x_hbm, x_buf, sems, plan, outs)
+
+    @pl.when(table[len(plan)] == 0)
+    def _():
+        stream(copies, use)
+        for out, offset in grams:
+            outs[out][:, offset : offset + LANES] = gram_ref[...]
+
+    @pl.when(table[len(plan)] == 1)
+    def _():
+        for out_ref, made_ref in zip(outs, refs[:2]):
+            out_ref[...] = made_ref[...]
 
 
 def layout(outputs, sub):
@@ -179,63 +189,62 @@
         if with_gram:
             grams.append((out, sub))
         widths.append(len(blocks) * sub + extra)
-    return unit, plan, grams, widths, jnp.stack(which)
-
-
-def products(kernel, inputs, in_specs, made, probes, outputs, sub, name):
-    rows = probes.shape[0]
-    rank = inputs[1].shape[0]
-    unit, plan, grams, widths, which = layout(outputs, sub)
-    shapes = [*made, *[jax.ShapeDtypeStruct((rank, width), F32) for width in widths]]
+    return unit, plan, grams, widths, which
+
+
+def product_call(kernel, inputs, in_specs, shapes, rows, unit, count, name):
     return pl.pallas_call(
-        functools.partial(kernel, plan, grams),
+        kernel,
         in_specs=[TABLE, *in_specs],
         out_specs=[WHOLE] * len(shapes),
         out_shape=shapes,
         scratch_shapes=[
-            pltpu.VMEM((len(plan), rows, unit), F32),
-            pltpu.SemaphoreType.DMA((len(plan),)),
+            pltpu.VMEM((count, rows, unit), F32),
+            pltpu.SemaphoreType.DMA((count,)),
         ],
         compiler_params=PARAMS,
         cost_estimate=pl.CostEstimate(
-            flops=6 * rows * rank * unit * len(plan),
-            bytes_accessed=4 * rows * unit * len(plan),
+            flops=6 * rows * shapes[-1].shape[0] * unit * count,
+            bytes_accessed=4 * rows * unit * count,
             transcendentals=0,
         ),
         name=name,
-    )(which, *inputs)
-
-
-def first_products(one, two, probes, outputs, sub):
+    )(*inputs)
+
+
+def products(one, two, probes, away, own, sub, late):
     rank, rows = one.shape
+    unit, plan, grams, widths, which = layout(away + own, sub)
+    early = len(layout(away, sub)[1])
+    chunks = [jax.ShapeDtypeStruct((rank, width), F32) for width in widths]
     made = [
         jax.ShapeDtypeStruct((2 * rank, rows), BF16),
         jax.ShapeDtypeStruct((rank, LANES), F32),
     ]
-    both, gram, *outs = products(
-        first_kernel,
-        [one, two, in_hbm(probes)],
+    x = in_hbm(probes)
+    both, gram, *outs = product_call(
+        functools.partial(first_kernel, plan, early, grams),
+        [jnp.stack([*which, late]), one, two, x],
         [WHOLE, WHOLE, HBM],
-        made,
-        probes,
-        outputs,
-        sub,
+        made + chunks,
+        rows,
+        unit,
+        len(plan),
         "first_products",
     )
-    return both, gram, outs
-
-
-def rest_products(both, gram, probes, outputs, sub, after):
-    return products(
-        rest_kernel,
-        [both, gram, in_hbm(probes), after],
-        [WHOLE, WHOLE, HBM, ANYWHERE],
-        [],
-        probes,
-        outputs,
-        sub,
+    away_outs, own_outs = outs[: len(away)], outs[len(away) :]
+    unit, plan, grams, widths, which = layout(own, sub)
+    own_outs = product_call(
+        functools.partial(rest_kernel, plan, grams),
+        [jnp.stack([*which, late]), both, gram, x, *own_outs],
+        [WHOLE, WHOLE, HBM, WHOLE, WHOLE],
+        chunks[len(away) :],
+        rows,
+        unit,
+        len(plan),
         "rest_products",
     )
+    return away_outs, own_outs
 
 
 def inverse_kernel(gram_ref, out_ref):
@@ -354,74 +363,60 @@
             ([block_b(c, p, 1), block_b(c, p, 0)], False),
         ]
 
-    both, gram, away = first_products(tall, other, probes, outputs(0, 1), width)
-
-    def after(value, *others):
-        return lax.optimization_barrier((value, *others))[0]
-
-    whole, total = [], []
-    ready = away[0]
-    for c in range(CHUNKS):
-        g = LANES if c == 0 else 0
-        more = outputs(c + 1, 1) if c + 1 < CHUNKS else []
-        made = rest_products(both, gram, probes, outputs(c, 0) + more, width, ready)
-        away_a, away_b = away
-        (own_a, own_b), away = made[:2], made[2:]
-        if c > 0:
-            away_a, away_b = after(away_a, whole[-1]), after(away_b, whole[-1])
-        ready = over(away_a, 1)
-        sum_a = own_a + ready
-        sum_b = own_b + over(away_b, 2)
-        got_a = over(sum_a[:, : width + g], 2)
-        got_b = over(sum_b[:, :width], 1)
-        whole.append(
-            jnp.concatenate(
-                [
-                    sum_a[:, width + g :] + got_a[:, :width],
-                    sum_a[:, width : width + g] + got_a[:, width:],
-                    sum_b[:, width:] + got_b,
-                ],
-                axis=1,
-            )
-        )
-        added = whole[-1]
-        bit = 4
-        while bit < n_pos:
-            added = added + over(added, bit)
-            bit *= 2
-        total.append(added)
-
-    out, inverse = None, None
-    for c in range(CHUNKS):
-        g = LANES if c == 0 else 0
-        mine_a, mine_b = total[c][:, :width], total[c][:, width + g :]
-        wait = whole[c + 1 : c + 2] + ([] if c == 0 else [inverse, last_a, last_b])
-        if wait:
-            mine_a, mine_b = after(mine_a, *wait), after(mine_b, *wait)
-        next_a = over(mine_a, 2)
-        next_b = over(mine_b, 1)
-        if c == 0:
-            inverse = inverse_factor(after(total[0], next_a, next_b), width)
-        last_a = over(jnp.concatenate([mine_a, next_a], axis=1), 1)
-        last_b = over(jnp.concatenate([mine_b, next_b], axis=1), 2)
-        out = finish(
-            inverse,
-            [total[c], next_a, next_b, last_a, last_b],
-            [
-                (block_a(c, 0, 0), 0, 0),
-                (block_b(c, 0, 0), 0, width + g),
-                (block_a(c, 0, 1), 1, 0),
-                (block_b(c, 0, 1), 2, 0),
-                (block_a(c, 1, 0), 3, 0),
-                (block_a(c, 1, 1), 3, width),
-                (block_b(c, 1, 0), 4, 0),
-                (block_b(c, 1, 1), 4, width),
-            ],
-            width,
-            cols,
-            out,
-        )
-    return out
+    late = 1 - (lax.axis_index("pix").astype(jnp.int32) & 1)
+    (away_a, away_b), (own_a, own_b) = products(
+        tall, other, probes, outputs(0, 1), outputs(0, 0), width, late
+    )
+
+    g = LANES
+    sum_a = own_a + over(away_a, 1)
+    sum_b = own_b + over(away_b, 2)
+    got_a = over(sum_a[:, : width + g], 2)
+    got_b = over(sum_b[:, :width], 1)
+    total = jnp.concatenate(
+        [
+            sum_a[:, width + g :] + got_a[:, :width],
+            sum_a[:, width : width + g] + got_a[:, width:],
+            sum_b[:, width:] + got_b,
+        ],
+        axis=1,
+    )
+    bit = 4
+    while bit < n_pos:
+        total = total + over(total, bit)
+        bit *= 2
+    inverse = inverse_factor(total, width)
+
+    mine_a, mine_b = total[:, :width], total[:, width + g :]
+    next_a = over(mine_a, 2)
+    next_b = over(mine_b, 1)
+    last_a = over(jnp.concatenate([mine_a, next_a], axis=1), 1)
+    last_b = over(jnp.concatenate([mine_b, next_b], axis=1), 2)
+    out = finish(
+        inverse,
+        [total, next_a, next_b],
+        [
+            (block_a(0, 0, 0), 0, 0),
+            (block_b(0, 0, 0), 0, width + g),
+            (block_a(0, 0, 1), 1, 0),
+            (block_b(0, 0, 1), 2, 0),
+        ],
+        width,
+        cols,
+    )
+    return finish(
+        inverse,
+        [last_a, last_b],
+        [
+            (block_a(0, 1, 0), 0, 0),
+            (block_a(0, 1, 1), 0, width),
+            (block_b(0, 1, 0), 1, 0),
+            (block_b(0, 1, 1), 1, width),
+        ],
+        width,
+        cols,
+        out,
+    )
 
 
 def solution(mesh):

time: 80.6 us -> 78.5 us (0.974)
  starting transfers between devices: 23.1 us -> 18.2 us
  waiting for transfers between devices: 30.8 us -> 33.2 us
    ppermute x20 -> x11, starting transfers between devices: 23.1 us -> 18.2 us  [swap(): return lax.ppermute(value, axis, [(i, i ^ bit) for i in range(size)])]
    ppermute x20 -> x11, waiting for transfers between devices: 30.8 us -> 33.2 us  [swap(): return lax.ppermute(value, axis, [(i, i ^ bit) for i in range(size)])]
    pallas_call x1, Pallas kernels: 9.47 us -> 11.4 us  [tall_partial(): pl.pallas_call(tall_kernel, in_specs=[HBM, HBM], out_specs=WHOLE, out_sha...]
    pallas_call x3 -> x2, Pallas kernels: 10.7 us -> 9.23 us  [product_call(): pl.pallas_call(kernel, in_specs=[TABLE, *in_specs], out_specs=[WHOLE] * l...]
  transfers between devices with their start and end apart: 20 -> 11, of which waited for: 13 -> 10; matrix products, arithmetic and copies ran while one was open for 1% -> 1% of each run, Pallas kernels for 14% -> 6%
where the time goes in v10:
time: 78.5 us; the launch traced here: 78.3 us
  waiting for transfers between devices  33.2 us (42%)
  Pallas kernels  26.1 us (33%)
  starting transfers between devices  18.2 us (23%)
    ppermute x11, waiting for transfers between devices, swap(): return lax.ppermute(value, axis, [(i, i ^ bit) for i in range(size)])  33.2 us
    ppermute x11, starting transfers between devices, swap(): return lax.ppermute(value, axis, [(i, i ^ bit) for i in range(size)])  18.2 us
    pallas_call x1, Pallas kernels, tall_partial(): pl.pallas_call(tall_kernel, in_specs=[HBM, HBM], out_specs=WHOLE, out_sha...  11.4 us
    pallas_call x2, Pallas kernels, product_call(): pl.pallas_call(kernel, in_specs=[TABLE, *in_specs], out_specs=[WHOLE] * l...  9.23 us
    pallas_call x2, Pallas kernels, finish(): pl.pallas_call(functools.partial(finish_kernel, [piece[1:] for piece in p...  3.42 us
    pallas_call x1, Pallas kernels, inverse_factor(): pl.pallas_call(inverse_kernel, grid=(1,), in_specs=[pl.BlockSpec((rank, L...  2.01 us
  transfers between devices with their start and end apart: 11, of which 10 were waited for; matrix products, arithmetic and copies ran while one was open for 1% of the time, Pallas kernels for 6%

profile of v10, /device:TPU:0, one launch (start us, length us, event | category | flops | bytes accessed | tf_op | source)
XLA Modules:
  0.0 78.3 jit_solution(3802571714291979418)
XLA Ops:
  0.0 11.4 %tall_partial.1 = f32[48,512]{1,0:T(8,128)S(1)} custom-call(f32[512,8192]{1,0:T(8,128)} %x_hbm.5, f32[48,8192]{1,0:T(8,128)} %bitcast.26), custom_call_target="tpu_custom_call" | custom-call | flops 1610612736 | bytes 16777216 | tf_op jit(solution)/shard_map/tall_partial/pallas_call | solution.py:87
  12.0 0.9 %collective-permute-done = f32[48,512]{1,0:T(8,128)S(1)} collective-permute-done((f32[48,512]{1,0:T(8,128)S(1)}, f32[48,512]{1,0:T(8,128)S(1)}, u32[]{:S(2)}, u32[]{:S(2)}) %collective-permute-start) | collective-permute-done | bytes 98336 | tf_op jit(solution)/shard_map/ppermute | solution.py:337
  12.9 2.9 %collective-permute-start.1 = (f32[48,512]{1,0:T(8,128)S(1)}, f32[48,512]{1,0:T(8,128)S(1)}, u32[]{:S(2)}, u32[]{:S(2)}) collective-permute-start(f32[48,512]{1,0:T(8,128)S(1)} %add.111.one_ref), channel_id=1, source_target_pairs={{0,2},{1,3},{2,0},{3,1},{4,6},{5,7},{6,4},{7,5},{8,10},{9,11},{10,... | collective-permute-start | bytes 294920 | tf_op jit(solution)/shard_map/ppermute | solution.py:337
  16.0 3.0 %collective-permute-done.1.two_ref = f32[48,512]{1,0:T(8,128)S(1)} collective-permute-done((f32[48,512]{1,0:T(8,128)S(1)}, f32[48,512]{1,0:T(8,128)S(1)}, u32[]{:S(2)}, u32[]{:S(2)}) %collective-permute-start.1) | collective-permute-done | bytes 98336 | tf_op jit(solution)/shard_map/ppermute | solution.py:337
  19.0 8.5 %first_products.1 = (bf16[96,512]{1,0:T(8,128)(2,1)S(1)}, f32[48,128]{1,0:T(8,128)S(1)}, f32[48,2176]{1,0:T(8,128)S(1)}, f32[48,2048]{1,0:T(8,128)S(1)}, f32[48,2176]{1,0:T(8,128)S(1)}, /*index=5*/f32[48,2048]{1,0:T(8,128)S(1)}) custom-call(s32[17]{0:T(128)S(1)} %stack.119.table, f32[48,512]{1,0:T(8,128)S(1)} %add.111.one_ref, ...), custom_call_target="tpu_custom_call" | custom-call | flops 1207959552 | bytes 16777216 | tf_op jit(solution)/shard_map/first_products/pallas_call | solution.py:196
  27.5 1.9 %collective-permute-start.4 = (f32[48,2048]{1,0:T(8,128)S(1)}, f32[48,2048]{1,0:T(8,128)S(1)}, u32[]{:S(2)}, u32[]{:S(2)}) collective-permute-start(f32[48,2048]{1,0:T(8,128)S(1)} %get-tuple-element.20), channel_id=1, source_target_pairs={{0,8},{4,12},{8,0},{12,4},{16,24},{20,28},{24,16},{28,20},{1,9},{5... | collective-permute-start | bytes 1179656 | tf_op jit(solution)/shard_map/ppermute | solution.py:337
  29.4 1.5 %collective-permute-start.2 = (f32[48,2176]{1,0:T(8,128)S(1)}, f32[48,2176]{1,0:T(8,128)S(1)}, u32[]{:S(2)}, u32[]{:S(2)}) collective-permute-start(f32[48,2176]{1,0:T(8,128)S(1)} %get-tuple-element.18), channel_id=1, source_target_pairs={{0,4},{4,0},{8,12},{12,8},{16,20},{20,16},{24,28},{28,24},{1,5},{5... | collective-permute-start | bytes 1253384 | tf_op jit(solution)/shard_map/ppermute | solution.py:337
  31.7 4.4 %collective-permute-done.4 = f32[48,2048]{1,0:T(8,128)S(1)} collective-permute-done((f32[48,2048]{1,0:T(8,128)S(1)}, f32[48,2048]{1,0:T(8,128)S(1)}, u32[]{:S(2)}, u32[]{:S(2)}) %collective-permute-start.4) | collective-permute-done | bytes 393248 | tf_op jit(solution)/shard_map/ppermute | solution.py:337
  36.2 2.4 %collective-permute-start.5 = (f32[48,1024]{1,0:T(8,128)S(1)}, f32[48,1024]{1,0:T(8,128)S(1)}, u32[]{:S(2)}, u32[]{:S(2)}) collective-permute-start(f32[48,1024]{1,0:T(8,128)S(1)} %slice.42), channel_id=1, source_target_pairs={{0,4},{4,0},{8,12},{12,8},{16,20},{20,16},{24,28},{28,24},{1,5},{5... | collective-permute-start | bytes 589832 | tf_op jit(solution)/shard_map/ppermute | solution.py:337
  38.5 1.0 %collective-permute-done.2 = f32[48,2176]{1,0:T(8,128)S(1)} collective-permute-done((f32[48,2176]{1,0:T(8,128)S(1)}, f32[48,2176]{1,0:T(8,128)S(1)}, u32[]{:S(2)}, u32[]{:S(2)}) %collective-permute-start.2) | collective-permute-done | bytes 417824 | tf_op jit(solution)/shard_map/ppermute | solution.py:337
  39.6 1.5 %collective-permute-start.3 = (f32[48,1152]{1,0:T(8,128)S(1)}, f32[48,1152]{1,0:T(8,128)S(1)}, u32[]{:S(2)}, u32[]{:S(2)}) collective-permute-start(f32[48,1152]{1,0:T(8,128)S(1)} %slice.37), channel_id=1, source_target_pairs={{0,8},{4,12},{8,0},{12,4},{16,24},{20,28},{24,16},{28,20},{1,9},{5... | collective-permute-start | bytes 663560 | tf_op jit(solution)/shard_map/ppermute | solution.py:337
  41.1 1.0 %collective-permute-done.5 = f32[48,1024]{1,0:T(8,128)S(1)} collective-permute-done((f32[48,1024]{1,0:T(8,128)S(1)}, f32[48,1024]{1,0:T(8,128)S(1)}, u32[]{:S(2)}, u32[]{:S(2)}) %collective-permute-start.5) | collective-permute-done | bytes 196640 | tf_op jit(solution)/shard_map/ppermute | solution.py:337
  42.2 4.8 %collective-permute-done.3 = f32[48,1152]{1,0:T(8,128)S(1)} collective-permute-done((f32[48,1152]{1,0:T(8,128)S(1)}, f32[48,1152]{1,0:T(8,128)S(1)}, u32[]{:S(2)}, u32[]{:S(2)}) %collective-permute-start.3) | collective-permute-done | bytes 221216 | tf_op jit(solution)/shard_map/ppermute | solution.py:337
  47.1 3.3 %collective-permute-start.6 = (f32[48,2176]{1,0:T(8,128)S(1)}, f32[48,2176]{1,0:T(8,128)S(1)}, u32[]{:S(2)}, u32[]{:S(2)}) collective-permute-start(f32[48,2176]{1,0:T(8,128)S(1)} %pad_maximum_fusion), channel_id=1, source_target_pairs={{0,16},{4,20},{8,24},{12,28},{16,0},{20,4},{24,8},{28,12},{1,17},{... | collective-permute-start | bytes 1253384 | tf_op jit(solution)/shard_map/ppermute | solution.py:337
  50.3 10.5 %collective-permute-done.6 = f32[48,2176]{1,0:T(8,128)S(1)} collective-permute-done((f32[48,2176]{1,0:T(8,128)S(1)}, f32[48,2176]{1,0:T(8,128)S(1)}, u32[]{:S(2)}, u32[]{:S(2)}) %collective-permute-start.6) | collective-permute-done | bytes 417824 | tf_op jit(solution)/shard_map/ppermute | solution.py:337
  60.9 1.1 %collective-permute-start.7 = (f32[48,1024]{1,0:T(8,128)S(1)}, f32[48,1024]{1,0:T(8,128)S(1)}, u32[]{:S(2)}, u32[]{:S(2)}) collective-permute-start(f32[48,1024]{1,0:T(8,128)S(1)} %get-tuple-element.22), channel_id=1, source_target_pairs={{0,8},{4,12},{8,0},{12,4},{16,24},{20,28},{24,16},{28,20},{1,9},{5... | collective-permute-start | bytes 589832 | tf_op jit(solution)/shard_map/ppermute | solution.py:337
  62.8 4.4 %collective-permute-done.7.refs_1_ = f32[48,1024]{1,0:T(8,128)S(1)} collective-permute-done((f32[48,1024]{1,0:T(8,128)S(1)}, f32[48,1024]{1,0:T(8,128)S(1)}, u32[]{:S(2)}, u32[]{:S(2)}) %collective-permute-start.7) | collective-permute-done | bytes 196640 | tf_op jit(solution)/shard_map/ppermute | solution.py:337
  67.2 1.6 %collective-permute-start.8 = (f32[48,2048]{1,0:T(8,128)S(1)}, f32[48,2048]{1,0:T(8,128)S(1)}, u32[]{:S(2)}, u32[]{:S(2)}) collective-permute-start(f32[48,2048]{1,0:T(8,128)S(1)} %pad_maximum_fusion.1), channel_id=1, source_target_pairs={{0,4},{4,0},{8,12},{12,8},{16,20},{20,16},{24,28},{28,24},{1,5},{5... | collective-permute-start | bytes 1179656 | tf_op jit(solution)/shard_map/ppermute | solution.py:337
  68.8 0.8 %collective-permute-start.10 = (f32[48,2048]{1,0:T(8,128)S(1)}, f32[48,2048]{1,0:T(8,128)S(1)}, u32[]{:S(2)}, u32[]{:S(2)}) collective-permute-start(f32[48,2048]{1,0:T(8,128)S(1)} %pad_maximum_fusion.2), channel_id=1, source_target_pairs={{0,8},{4,12},{8,0},{12,4},{16,24},{20,28},{24,16},{28,20},{1,9},{5... | collective-permute-start | bytes 1179656 | tf_op jit(solution)/shard_map/ppermute | solution.py:337
  69.8 2.0 %inverse_factor.1.inverse_ref = f32[48,48]{1,0:T(8,128)S(1)} custom-call(f32[48,2176]{1,0:T(8,128)S(1)} %fusion.gram_ref.refs_0_), custom_call_target="tpu_custom_call" | custom-call | flops 20000000 | bytes 49152 | tf_op jit(solution)/shard_map/inverse_factor/pallas_call | solution.py:274
  71.8 1.7 %finish.2.refs_2_ = f32[48,8192]{1,0:T(8,128)} custom-call(s32[4]{0:T(128)S(1)} %pad_add_fusion.1.where_ref, f32[48,48]{1,0:T(8,128)S(1)} %inverse_factor.1.inverse_ref, f32[48,2176]{1,0:T(8,128)S(1)} %fusion.gram_ref.refs_0_, f32[48,1024]{1,0:T(8,128)S(1)} %collective-permute-done.7.refs_1_, f32[48,1024]{1,0:T(8,128)S(1)} %collective-permute-done.9.refs_2_), custom_call_target="tpu_custom_call" | custom-call | flops 56623104 | bytes 1572864 | tf_op jit(solution)/shard_map/finish/pallas_call | solution.py:315
  73.5 1.5 %collective-permute-done.8.refs_0_ = f32[48,2048]{1,0:T(8,128)S(1)} collective-permute-done((f32[48,2048]{1,0:T(8,128)S(1)}, f32[48,2048]{1,0:T(8,128)S(1)}, u32[]{:S(2)}, u32[]{:S(2)}) %collective-permute-start.8) | collective-permute-done | bytes 393248 | tf_op jit(solution)/shard_map/ppermute | solution.py:337
  75.0 1.6 %collective-permute-done.10.refs_1_ = f32[48,2048]{1,0:T(8,128)S(1)} collective-permute-done((f32[48,2048]{1,0:T(8,128)S(1)}, f32[48,2048]{1,0:T(8,128)S(1)}, u32[]{:S(2)}, u32[]{:S(2)}) %collective-permute-start.10) | collective-permute-done | bytes 393248 | tf_op jit(solution)/shard_map/ppermute | solution.py:337
  76.6 1.7 %finish.3 = f32[48,8192]{1,0:T(8,128)} custom-call(s32[4]{0:T(128)S(1)} %pad_add_fusion.where_ref, f32[48,48]{1,0:T(8,128)S(1)} %inverse_factor.1.inverse_ref, f32[48,2048]{1,0:T(8,128)S(1)} %collective-permute-done.8.refs_0_, f32[48,2048]{1,0:T(8,128)S(1)} %collective-permute-done.10.refs_1_, f32[48,8192]{1,0:T(8,128)} %finish.2.refs_2_), custom_call_target="tpu_custom_call", output_to_operand_aliasing={{}: (4, {})} | custom-call | flops 56623104 | bytes 1572864 | tf_op jit(solution)/shard_map/finish/pallas_call | solution.py:315
  (21 shorter events, 2.7 us)
Async XLA Ops:
  11.5 1.5 %collective-permute-start = (f32[48,512]{1,0:T(8,128)S(1)}, f32[48,512]{1,0:T(8,128)S(1)}, u32[]{:S(2)}, u32[]{:S(2)}) collective-permute-start(f32[48,512]{1,0:T(8,128)S(1)} %tall_partial.1), channel_id=1, source_target_pairs={{0,1},{1,0},{2,3},{3,2},{4,5},{5,4},{6,7},{7,6},{8,9},{9,8},{10,11... | collective-permute-start | bytes 294920 | tf_op jit(solution)/shard_map/ppermute | solution.py:337
  12.9 6.1 %collective-permute-start.1 = (f32[48,512]{1,0:T(8,128)S(1)}, f32[48,512]{1,0:T(8,128)S(1)}, u32[]{:S(2)}, u32[]{:S(2)}) collective-permute-start(f32[48,512]{1,0:T(8,128)S(1)} %add.111.one_ref), channel_id=1, source_target_pairs={{0,2},{1,3},{2,0},{3,1},{4,6},{5,7},{6,4},{7,5},{8,10},{9,11},{10,... | collective-permute-start | bytes 294920 | tf_op jit(solution)/shard_map/ppermute | solution.py:337
  27.5 8.5 %collective-permute-start.4 = (f32[48,2048]{1,0:T(8,128)S(1)}, f32[48,2048]{1,0:T(8,128)S(1)}, u32[]{:S(2)}, u32[]{:S(2)}) collective-permute-start(f32[48,2048]{1,0:T(8,128)S(1)} %get-tuple-element.20), channel_id=1, source_target_pairs={{0,8},{4,12},{8,0},{12,4},{16,24},{20,28},{24,16},{28,20},{1,9},{5... | collective-permute-start | bytes 1179656 | tf_op jit(solution)/shard_map/ppermute | solution.py:337
  29.4 10.1 %collective-permute-start.2 = (f32[48,2176]{1,0:T(8,128)S(1)}, f32[48,2176]{1,0:T(8,128)S(1)}, u32[]{:S(2)}, u32[]{:S(2)}) collective-permute-start(f32[48,2176]{1,0:T(8,128)S(1)} %get-tuple-element.18), channel_id=1, source_target_pairs={{0,4},{4,0},{8,12},{12,8},{16,20},{20,16},{24,28},{28,24},{1,5},{5... | collective-permute-start | bytes 1253384 | tf_op jit(solution)/shard_map/ppermute | solution.py:337
  36.2 6.0 %collective-permute-start.5 = (f32[48,1024]{1,0:T(8,128)S(1)}, f32[48,1024]{1,0:T(8,128)S(1)}, u32[]{:S(2)}, u32[]{:S(2)}) collective-permute-start(f32[48,1024]{1,0:T(8,128)S(1)} %slice.42), channel_id=1, source_target_pairs={{0,4},{4,0},{8,12},{12,8},{16,20},{20,16},{24,28},{28,24},{1,5},{5... | collective-permute-start | bytes 589832 | tf_op jit(solution)/shard_map/ppermute | solution.py:337
  39.6 7.4 %collective-permute-start.3 = (f32[48,1152]{1,0:T(8,128)S(1)}, f32[48,1152]{1,0:T(8,128)S(1)}, u32[]{:S(2)}, u32[]{:S(2)}) collective-permute-start(f32[48,1152]{1,0:T(8,128)S(1)} %slice.37), channel_id=1, source_target_pairs={{0,8},{4,12},{8,0},{12,4},{16,24},{20,28},{24,16},{28,20},{1,9},{5... | collective-permute-start | bytes 663560 | tf_op jit(solution)/shard_map/ppermute | solution.py:337
  47.1 13.7 %collective-permute-start.6 = (f32[48,2176]{1,0:T(8,128)S(1)}, f32[48,2176]{1,0:T(8,128)S(1)}, u32[]{:S(2)}, u32[]{:S(2)}) collective-permute-start(f32[48,2176]{1,0:T(8,128)S(1)} %pad_maximum_fusion), channel_id=1, source_target_pairs={{0,16},{4,20},{8,24},{12,28},{16,0},{20,4},{24,8},{28,12},{1,17},{... | collective-permute-start | bytes 1253384 | tf_op jit(solution)/shard_map/ppermute | solution.py:337
  60.9 6.2 %collective-permute-start.7 = (f32[48,1024]{1,0:T(8,128)S(1)}, f32[48,1024]{1,0:T(8,128)S(1)}, u32[]{:S(2)}, u32[]{:S(2)}) collective-permute-start(f32[48,1024]{1,0:T(8,128)S(1)} %get-tuple-element.22), channel_id=1, source_target_pairs={{0,8},{4,12},{8,0},{12,4},{16,24},{20,28},{24,16},{28,20},{1,9},{5... | collective-permute-start | bytes 589832 | tf_op jit(solution)/shard_map/ppermute | solution.py:337
  62.0 6.7 %collective-permute-start.9 = (f32[48,1024]{1,0:T(8,128)S(1)}, f32[48,1024]{1,0:T(8,128)S(1)}, u32[]{:S(2)}, u32[]{:S(2)}) collective-permute-start(f32[48,1024]{1,0:T(8,128)S(1)} %get-tuple-element.21), channel_id=1, source_target_pairs={{0,4},{4,0},{8,12},{12,8},{16,20},{20,16},{24,28},{28,24},{1,5},{5... | collective-permute-start | bytes 589832 | tf_op jit(solution)/shard_map/ppermute | solution.py:337
  67.2 7.8 %collective-permute-start.8 = (f32[48,2048]{1,0:T(8,128)S(1)}, f32[48,2048]{1,0:T(8,128)S(1)}, u32[]{:S(2)}, u32[]{:S(2)}) collective-permute-start(f32[48,2048]{1,0:T(8,128)S(1)} %pad_maximum_fusion.1), channel_id=1, source_target_pairs={{0,4},{4,0},{8,12},{12,8},{16,20},{20,16},{24,28},{28,24},{1,5},{5... | collective-permute-start | bytes 1179656 | tf_op jit(solution)/shard_map/ppermute | solution.py:337
  68.8 7.8 %collective-permute-start.10 = (f32[48,2048]{1,0:T(8,128)S(1)}, f32[48,2048]{1,0:T(8,128)S(1)}, u32[]{:S(2)}, u32[]{:S(2)}) collective-permute-start(f32[48,2048]{1,0:T(8,128)S(1)} %pad_maximum_fusion.2), channel_id=1, source_target_pairs={{0,8},{4,12},{8,0},{12,4},{16,24},{20,28},{24,16},{28,20},{1,9},{5... | collective-permute-start | bytes 1179656 | tf_op jit(solution)/shard_map/ppermute | solution.py:337

commit v11 on v9

--- a/solution.py
+++ b/solution.py
@@ -53,7 +53,7 @@
         use(k)
 
 
-def tall_kernel(x_hbm, s_hbm, out_ref, x_buf, s_buf, x_sems, s_sem):
+def tall_kernel(x_hbm, s_hbm, out_ref, x_buf, s_buf, head_buf, rest_buf, x_sems, s_sem):
     blocks, _, unit = x_buf.shape
     rank = s_hbm.shape[0]
     copies = [
@@ -68,17 +68,13 @@
             sketch.wait()
         s_head, s_rest = split(s_buf[:, k * unit : (k + 1) * unit])
         s_both = jnp.concatenate([s_head, s_rest], axis=0)
-        for rows in tiles(x_buf.shape[1]):
-            total = None
-            for cols in tiles(unit):
-                x_head, x_rest = split(x_buf[k, rows, cols])
-                both = dot(s_both[:, cols], x_head, LAST)
-                part = both[:rank] + (both[rank:] + dot(s_head[:, cols], x_rest, LAST))
-                total = part if total is None else total + part
-            if k == 0:
-                out_ref[:, rows] = total
-            else:
-                out_ref[:, rows] += total
+        head_buf[k % 2], rest_buf[k % 2] = split(x_buf[k])
+        both = dot(s_both, head_buf[k % 2], LAST)
+        part = both[:rank] + (both[rank:] + dot(s_head, rest_buf[k % 2], LAST))
+        if k == 0:
+            out_ref[...] = part
+        else:
+            out_ref[...] += part
 
     stream(copies, use)
 
@@ -96,6 +92,8 @@
         scratch_shapes=[
             pltpu.VMEM((blocks, rows, unit), F32),
             pltpu.VMEM((rank, cols), F32),
+            pltpu.VMEM((2, rows, unit), BF16),
+            pltpu.VMEM((2, rows, unit), BF16),
             pltpu.SemaphoreType.DMA((blocks,)),
             pltpu.SemaphoreType.DMA,
         ],
@@ -327,13 +325,22 @@
     def swap(value, axis, size, bit):
         return lax.ppermute(value, axis, [(i, i ^ bit) for i in range(size)])
 
-    def over(value, bit):
-        return swap(value, "pos", n_pos, bit)
+    def over(value, turn):
+        pairs = [
+            (i * n_pix + j, (i ^ (1 << ((turn + j + 1) % 2))) * n_pix + j)
+            for i in range(n_pos)
+            for j in range(n_pix)
+        ]
+        return lax.ppermute(value, ("pos", "pix"), pairs)
+
+    def after(value, *others):
+        return lax.optimization_barrier((value, *others))[0]
 
     me = lax.axis_index("pos").astype(jnp.int32)
-    near, far = me & 1, (me >> 1) & 1
+    odd = lax.axis_index("pix").astype(jnp.int32) & 1
+    first_bit, second_bit = (me >> (1 - odd)) & 1, (me >> odd) & 1
     cols = probes.shape[1]
-    width = cols // (8 * CHUNKS)
+    width = cols // (4 * CHUNKS)
 
     tall = tall_partial(probes, sketch.T)
     bit = 1
@@ -342,86 +349,54 @@
         bit *= 2
     other = swap(tall, "pix", n_pix, bit)
 
-    def block_a(c, p, q):
-        return 8 * c + 2 * (near ^ p) + (far ^ q)
-
-    def block_b(c, p, q):
-        return 8 * c + 4 + 2 * (far ^ p) + (near ^ q)
+    def block(c, p, q):
+        return 4 * c + 2 * (first_bit ^ p) + (second_bit ^ q)
 
     def outputs(c, p):
-        return [
-            ([block_a(c, p, 1), block_a(c, p, 0)], c == 0),
-            ([block_b(c, p, 1), block_b(c, p, 0)], False),
-        ]
+        return [([block(c, p, 1), block(c, p, 0)], c == 0)]
 
     both, gram, away = first_products(tall, other, probes, outputs(0, 1), width)
 
-    def after(value, *others):
-        return lax.optimization_barrier((value, *others))[0]
-
-    whole, total = [], []
-    ready = away[0]
+    ready, total = away[0], []
     for c in range(CHUNKS):
         g = LANES if c == 0 else 0
         more = outputs(c + 1, 1) if c + 1 < CHUNKS else []
-        made = rest_products(both, gram, probes, outputs(c, 0) + more, width, ready)
-        away_a, away_b = away
-        (own_a, own_b), away = made[:2], made[2:]
-        if c > 0:
-            away_a, away_b = after(away_a, whole[-1]), after(away_b, whole[-1])
-        ready = over(away_a, 1)
-        sum_a = own_a + ready
-        sum_b = own_b + over(away_b, 2)
-        got_a = over(sum_a[:, : width + g], 2)
-        got_b = over(sum_b[:, :width], 1)
-        whole.append(
-            jnp.concatenate(
-                [
-                    sum_a[:, width + g :] + got_a[:, :width],
-                    sum_a[:, width : width + g] + got_a[:, width:],
-                    sum_b[:, width:] + got_b,
-                ],
-                axis=1,
-            )
-        )
-        added = whole[-1]
+        own, *made = rest_products(both, gram, probes, outputs(c, 0) + more, width, ready)
+        ready = over(away[0], 0)
+        away = made
+        part = own + ready
+        if away:
+            away[0] = after(away[0], part)
+        got = over(part[:, : width + g], 1)
+        whole = part[:, width + g :] + got[:, :width]
+        if g:
+            whole = jnp.concatenate([whole, part[:, width : width + g] + got[:, width:]], axis=1)
         bit = 4
         while bit < n_pos:
-            added = added + over(added, bit)
+            whole = whole + swap(whole, "pos", n_pos, bit)
             bit *= 2
-        total.append(added)
-
-    out, inverse = None, None
+        total.append(whole)
+
+    inverse, sources, pieces = None, [], []
     for c in range(CHUNKS):
-        g = LANES if c == 0 else 0
-        mine_a, mine_b = total[c][:, :width], total[c][:, width + g :]
-        wait = whole[c + 1 : c + 2] + ([] if c == 0 else [inverse, last_a, last_b])
-        if wait:
-            mine_a, mine_b = after(mine_a, *wait), after(mine_b, *wait)
-        next_a = over(mine_a, 2)
-        next_b = over(mine_b, 1)
-        if c == 0:
-            inverse = inverse_factor(after(total[0], next_a, next_b), width)
-        last_a = over(jnp.concatenate([mine_a, next_a], axis=1), 1)
-        last_b = over(jnp.concatenate([mine_b, next_b], axis=1), 2)
-        out = finish(
-            inverse,
-            [total[c], next_a, next_b, last_a, last_b],
-            [
-                (block_a(c, 0, 0), 0, 0),
-                (block_b(c, 0, 0), 0, width + g),
-                (block_a(c, 0, 1), 1, 0),
-                (block_b(c, 0, 1), 2, 0),
-                (block_a(c, 1, 0), 3, 0),
-                (block_a(c, 1, 1), 3, width),
-                (block_b(c, 1, 0), 4, 0),
-                (block_b(c, 1, 1), 4, width),
-            ],
-            width,
-            cols,
-            out,
-        )
-    return out
+        mine = total[c][:, :width]
+        if inverse is not None:
+            mine = after(mine, inverse, far)
+        near = over(mine, 1)
+        if inverse is None:
+            inverse = inverse_factor(after(total[0], near), width)
+        far = over(jnp.concatenate([mine, near], axis=1), 0)
+        k = len(sources)
+        sources += [mine, near, far]
+        pieces += [
+            (block(c, 0, 0), k, 0),
+            (block(c, 0, 1), k + 1, 0),
+            (block(c, 1, 0), k + 2, 0),
+            (block(c, 1, 1), k + 2, width),
+        ]
+    out = finish(inverse, sources[:-1], pieces[:-2], width, cols)
+    pieces = [(where, 0, start) for where, _, start in pieces[-2:]]
+    return finish(inverse, sources[-1:], pieces, width, cols, out)
 
 
 def solution(mesh):

time: 80.6 us -> 84 us (1.042)
  waiting for transfers between devices: 30.8 us -> 42.5 us
  starting transfers between devices: 23.1 us -> 15.1 us
    ppermute x0 -> x8, waiting for transfers between devices: none -> 25.1 us  [over(): return lax.ppermute(value, ('pos', 'pix'), pairs)]
    ppermute x20 -> x4, starting transfers between devices: 23.1 us -> 6.41 us  [swap(): return lax.ppermute(value, axis, [(i, i ^ bit) for i in range(size)])]
    ppermute x20 -> x4, waiting for transfers between devices: 30.8 us -> 17.4 us  [swap(): return lax.ppermute(value, axis, [(i, i ^ bit) for i in range(size)])]
    ppermute x0 -> x8, starting transfers between devices: none -> 8.7 us  [over(): return lax.ppermute(value, ('pos', 'pix'), pairs)]
  transfers between devices with their start and end apart: 20 -> 12, of which waited for: 13 -> 10; matrix products, arithmetic and copies ran while one was open for 1% -> 1% of each run, Pallas kernels for 14% -> 13%
where the time goes in v11:
time: 84 us; the launch traced here: 83.9 us
  waiting for transfers between devices  42.5 us (51%)
  Pallas kernels  25.4 us (30%)
  starting transfers between devices  15.1 us (18%)
    ppermute x8, waiting for transfers between devices, over(): return lax.ppermute(value, ('pos', 'pix'), pairs)  25.1 us
    ppermute x4, waiting for transfers between devices, swap(): return lax.ppermute(value, axis, [(i, i ^ bit) for i in range(size)])  17.4 us
    pallas_call x3, Pallas kernels, products(): pl.pallas_call(functools.partial(kernel, plan, grams), in_specs=[TABLE, *...  10.7 us
    pallas_call x1, Pallas kernels, tall_partial(): pl.pallas_call(tall_kernel, in_specs=[HBM, HBM], out_specs=WHOLE, out_sha...  9.22 us
    ppermute x8, starting transfers between devices, over(): return lax.ppermute(value, ('pos', 'pix'), pairs)  8.7 us
    ppermute x4, starting transfers between devices, swap(): return lax.ppermute(value, axis, [(i, i ^ bit) for i in range(size)])  6.41 us
    pallas_call x2, Pallas kernels, finish(): pl.pallas_call(functools.partial(finish_kernel, [piece[1:] for piece in p...  3.41 us
    pallas_call x1, Pallas kernels, inverse_factor(): pl.pallas_call(inverse_kernel, grid=(1,), in_specs=[pl.BlockSpec((rank, L...  2.01 us
  transfers between devices with their start and end apart: 12, of which 10 were waited for; matrix products, arithmetic and copies ran while one was open for 1% of the time, Pallas kernels for 13%

profile of v11, /device:TPU:0, one launch (start us, length us, event | category | flops | bytes accessed | tf_op | source)
XLA Modules:
  0.0 83.9 jit_solution(12559723759263596379)
XLA Ops:
  0.0 9.2 %tall_partial.1 = f32[48,512]{1,0:T(8,128)S(1)} custom-call(f32[512,8192]{1,0:T(8,128)} %x_hbm.7, f32[48,8192]{1,0:T(8,128)} %bitcast.25), custom_call_target="tpu_custom_call" | custom-call | flops 1207959552 | bytes 16777216 | tf_op jit(solution)/shard_map/tall_partial/pallas_call | solution.py:87
  9.7 0.9 %collective-permute-done = f32[48,512]{1,0:T(8,128)S(1)} collective-permute-done((f32[48,512]{1,0:T(8,128)S(1)}, f32[48,512]{1,0:T(8,128)S(1)}, u32[]{:S(2)}, u32[]{:S(2)}) %collective-permute-start) | collective-permute-done | bytes 98336 | tf_op jit(solution)/shard_map/ppermute | solution.py:326
  10.7 2.9 %collective-permute-start.1 = (f32[48,512]{1,0:T(8,128)S(1)}, f32[48,512]{1,0:T(8,128)S(1)}, u32[]{:S(2)}, u32[]{:S(2)}) collective-permute-start(f32[48,512]{1,0:T(8,128)S(1)} %add.105.one_ref), channel_id=1, source_target_pairs={{0,2},{1,3},{2,0},{3,1},{4,6},{5,7},{6,4},{7,5},{8,10},{9,11},{10,... | collective-permute-start | bytes 294920 | tf_op jit(solution)/shard_map/ppermute | solution.py:326
  13.7 3.0 %collective-permute-done.1.two_ref = f32[48,512]{1,0:T(8,128)S(1)} collective-permute-done((f32[48,512]{1,0:T(8,128)S(1)}, f32[48,512]{1,0:T(8,128)S(1)}, u32[]{:S(2)}, u32[]{:S(2)}) %collective-permute-start.1) | collective-permute-done | bytes 98336 | tf_op jit(solution)/shard_map/ppermute | solution.py:326
  16.8 3.3 %first_products.1 = (bf16[96,512]{1,0:T(8,128)(2,1)S(1)}, f32[48,128]{1,0:T(8,128)S(1)}, f32[48,2176]{1,0:T(8,128)S(1)}) custom-call(s32[4]{0:T(128)S(1)} %pad_add_fusion.1.which_ref, f32[48,512]{1,0:T(8,128)S(1)} %add.105.one_ref, f32[48,512]{1,0:T(8,128)S(1)} %collective-permute-done.1.two_ref, f32[512,8192]{1,0:T(8,128)} %x_hbm.7), custom_call_target="tpu_custom_call" | custom-call | flops 301989888 | bytes 4194304 | tf_op jit(solution)/shard_map/first_products/pallas_call | solution.py:188
  20.1 1.9 %collective-permute-start.2 = (f32[48,2176]{1,0:T(8,128)S(1)}, f32[48,2176]{1,0:T(8,128)S(1)}, u32[]{:S(2)}, u32[]{:S(2)}) collective-permute-start(f32[48,2176]{1,0:T(8,128)S(1)} %get-tuple-element.15.after_ref), channel_id=1, source_target_pairs={{0,8},{1,5},{2,10},{3,7},{4,12},{5,1},{6,14},{7,3},{8,0},{9,13},{1... | collective-permute-start | bytes 1253384 | tf_op jit(solution)/shard_map/ppermute | solution.py:334
  22.1 4.3 %rest_products.2 = (f32[48,2176]{1,0:T(8,128)S(1)}, f32[48,2048]{1,0:T(8,128)S(1)}) custom-call(s32[8]{0:T(128)S(1)} %stack.98.which_ref, bf16[96,512]{1,0:T(8,128)(2,1)S(1)} %get-tuple-element.13.both_ref, f32[48,128]{1,0:T(8,128)S(1)} %get-tuple-element.14.gram_ref, f32[512,8192]{1,0:T(8,128)} %x_hbm.7, f32[48,2176]{1,0:T(8,128)S(1)} %get-tuple-element.15.after_ref), custom_call_target="tpu_custom_call" | custom-call | flops 603979776 | bytes 8388608 | tf_op jit(solution)/shard_map/rest_products/pallas_call | solution.py:188
  26.4 1.8 %collective-permute-done.2.after_ref = f32[48,2176]{1,0:T(8,128)S(1)} collective-permute-done((f32[48,2176]{1,0:T(8,128)S(1)}, f32[48,2176]{1,0:T(8,128)S(1)}, u32[]{:S(2)}, u32[]{:S(2)}) %collective-permute-start.2) | collective-permute-done | bytes 417824 | tf_op jit(solution)/shard_map/ppermute | solution.py:334
  28.3 1.8 %collective-permute-start.3 = (f32[48,1152]{1,0:T(8,128)S(1)}, f32[48,1152]{1,0:T(8,128)S(1)}, u32[]{:S(2)}, u32[]{:S(2)}) collective-permute-start(f32[48,1152]{1,0:T(8,128)S(1)} %slice.33), channel_id=1, source_target_pairs={{0,4},{1,9},{2,6},{3,11},{4,0},{5,13},{6,2},{7,15},{8,12},{9,1},{1... | collective-permute-start | bytes 663560 | tf_op jit(solution)/shard_map/ppermute | solution.py:334
  30.1 4.2 %collective-permute-done.3 = f32[48,1152]{1,0:T(8,128)S(1)} collective-permute-done((f32[48,1152]{1,0:T(8,128)S(1)}, f32[48,1152]{1,0:T(8,128)S(1)}, u32[]{:S(2)}, u32[]{:S(2)}) %collective-permute-start.3) | collective-permute-done | bytes 221216 | tf_op jit(solution)/shard_map/ppermute | solution.py:334
  34.4 2.9 %collective-permute-start.4 = (f32[48,1152]{1,0:T(8,128)S(1)}, f32[48,1152]{1,0:T(8,128)S(1)}, u32[]{:S(2)}, u32[]{:S(2)}) collective-permute-start(f32[48,1152]{1,0:T(8,128)S(1)} %pad_maximum_fusion.2), channel_id=1, source_target_pairs={{0,16},{4,20},{8,24},{12,28},{16,0},{20,4},{24,8},{28,12},{1,17},{... | collective-permute-start | bytes 663560 | tf_op jit(solution)/shard_map/ppermute | solution.py:326
  37.2 1.6 %collective-permute-start.6 = (f32[48,2048]{1,0:T(8,128)S(1)}, f32[48,2048]{1,0:T(8,128)S(1)}, u32[]{:S(2)}, u32[]{:S(2)}) collective-permute-start(f32[48,2048]{1,0:T(8,128)S(1)} %get-tuple-element.19), channel_id=1, source_target_pairs={{0,8},{1,5},{2,10},{3,7},{4,12},{5,1},{6,14},{7,3},{8,0},{9,13},{1... | collective-permute-start | bytes 1179656 | tf_op jit(solution)/shard_map/ppermute | solution.py:334
  38.8 6.6 %collective-permute-done.4 = f32[48,1152]{1,0:T(8,128)S(1)} collective-permute-done((f32[48,1152]{1,0:T(8,128)S(1)}, f32[48,1152]{1,0:T(8,128)S(1)}, u32[]{:S(2)}, u32[]{:S(2)}) %collective-permute-start.4) | collective-permute-done | bytes 221216 | tf_op jit(solution)/shard_map/ppermute | solution.py:326
  45.5 1.2 %collective-permute-start.5 = (f32[48,1024]{1,0:T(8,128)S(1)}, f32[48,1024]{1,0:T(8,128)S(1)}, u32[]{:S(2)}, u32[]{:S(2)}) collective-permute-start(f32[48,1024]{1,0:T(8,128)S(1)} %slice.37.refs_0_), channel_id=1, source_target_pairs={{0,4},{1,9},{2,6},{3,11},{4,0},{5,13},{6,2},{7,15},{8,12},{9,1},{1... | collective-permute-start | bytes 589832 | tf_op jit(solution)/shard_map/ppermute | solution.py:334
  46.7 3.1 %rest_products.3 = f32[48,2048]{1,0:T(8,128)S(1)} custom-call(s32[4]{0:T(128)S(1)} %pad_add_fusion.2.which_ref, bf16[96,512]{1,0:T(8,128)(2,1)S(1)} %get-tuple-element.13.both_ref, f32[48,128]{1,0:T(8,128)S(1)} %get-tuple-element.14.gram_ref, f32[512,8192]{1,0:T(8,128)} %x_hbm.7, f32[48,2176]{1,0:T(8,128)S(1)} %collective-permute-done.2.after_ref), custom_call_target="tpu_custom_call" | custom-call | flops 301989888 | bytes 4194304 | tf_op jit(solution)/shard_map/rest_products/pallas_call | solution.py:188
  49.9 1.0 %collective-permute-start.7 = (f32[48,1024]{1,0:T(8,128)S(1)}, f32[48,1024]{1,0:T(8,128)S(1)}, u32[]{:S(2)}, u32[]{:S(2)}) collective-permute-start(f32[48,1024]{1,0:T(8,128)S(1)} %slice.39), channel_id=1, source_target_pairs={{0,4},{1,9},{2,6},{3,11},{4,0},{5,13},{6,2},{7,15},{8,12},{9,1},{1... | collective-permute-start | bytes 589832 | tf_op jit(solution)/shard_map/ppermute | solution.py:334
  51.5 6.2 %collective-permute-done.7 = f32[48,1024]{1,0:T(8,128)S(1)} collective-permute-done((f32[48,1024]{1,0:T(8,128)S(1)}, f32[48,1024]{1,0:T(8,128)S(1)}, u32[]{:S(2)}, u32[]{:S(2)}) %collective-permute-start.7) | collective-permute-done | bytes 196640 | tf_op jit(solution)/shard_map/ppermute | solution.py:334
  57.8 2.0 %inverse_factor.1.inverse_ref = f32[48,48]{1,0:T(8,128)S(1)} custom-call(f32[48,1152]{1,0:T(8,128)S(1)} %fusion.gram_ref), custom_call_target="tpu_custom_call" | custom-call | flops 20000000 | bytes 49152 | tf_op jit(solution)/shard_map/inverse_factor/pallas_call | solution.py:263
  59.8 6.8 %collective-permute-done.8 = f32[48,1024]{1,0:T(8,128)S(1)} collective-permute-done((f32[48,1024]{1,0:T(8,128)S(1)}, f32[48,1024]{1,0:T(8,128)S(1)}, u32[]{:S(2)}, u32[]{:S(2)}) %collective-permute-start.8) | collective-permute-done | bytes 196640 | tf_op jit(solution)/shard_map/ppermute | solution.py:326
  66.6 1.0 %collective-permute-start.10 = (f32[48,1024]{1,0:T(8,128)S(1)}, f32[48,1024]{1,0:T(8,128)S(1)}, u32[]{:S(2)}, u32[]{:S(2)}) collective-permute-start(f32[48,1024]{1,0:T(8,128)S(1)} %add.117.refs_3_), channel_id=1, source_target_pairs={{0,4},{1,9},{2,6},{3,11},{4,0},{5,13},{6,2},{7,15},{8,12},{9,1},{1... | collective-permute-start | bytes 589832 | tf_op jit(solution)/shard_map/ppermute | solution.py:334
  67.6 6.9 %collective-permute-done.10.refs_4_ = f32[48,1024]{1,0:T(8,128)S(1)} collective-permute-done((f32[48,1024]{1,0:T(8,128)S(1)}, f32[48,1024]{1,0:T(8,128)S(1)}, u32[]{:S(2)}, u32[]{:S(2)}) %collective-permute-start.10) | collective-permute-done | bytes 196640 | tf_op jit(solution)/shard_map/ppermute | solution.py:334
  74.7 1.9 %finish.2.refs_1_ = f32[48,8192]{1,0:T(8,128)} custom-call(s32[6]{0:T(128)S(1)} %stack.115.where_ref, f32[48,48]{1,0:T(8,128)S(1)} %inverse_factor.1.inverse_ref, f32[48,1024]{1,0:T(8,128)S(1)} %slice.37.refs_0_, f32[48,1024]{1,0:T(8,128)S(1)} %collective-permute-done.5.refs_1_, f32[48,2048]{1,0:T(8,128)S(1)} %collective-permute-done.9.refs_2_, ...), custom_call_target="tpu_custom_call" | custom-call | flops 84934656 | bytes 2359296 | tf_op jit(solution)/shard_map/finish/pallas_call | solution.py:304
  76.6 5.7 %collective-permute-done.11.refs_0_ = f32[48,2048]{1,0:T(8,128)S(1)} collective-permute-done((f32[48,2048]{1,0:T(8,128)S(1)}, f32[48,2048]{1,0:T(8,128)S(1)}, u32[]{:S(2)}, u32[]{:S(2)}) %collective-permute-start.11) | collective-permute-done | bytes 393248 | tf_op jit(solution)/shard_map/ppermute | solution.py:334
  82.3 1.5 %finish.3 = f32[48,8192]{1,0:T(8,128)} custom-call(s32[2]{0:T(128)S(1)} %pad_add_fusion.where_ref, f32[48,48]{1,0:T(8,128)S(1)} %inverse_factor.1.inverse_ref, f32[48,2048]{1,0:T(8,128)S(1)} %collective-permute-done.11.refs_0_, f32[48,8192]{1,0:T(8,128)} %finish.2.refs_1_), custom_call_target="tpu_custom_call", output_to_operand_aliasing={{}: (3, {})} | custom-call | flops 28311552 | bytes 786432 | tf_op jit(solution)/shard_map/finish/pallas_call | solution.py:304
  (26 shorter events, 2.0 us)
Async XLA Ops:
  9.2 1.5 %collective-permute-start = (f32[48,512]{1,0:T(8,128)S(1)}, f32[48,512]{1,0:T(8,128)S(1)}, u32[]{:S(2)}, u32[]{:S(2)}) collective-permute-start(f32[48,512]{1,0:T(8,128)S(1)} %tall_partial.1), channel_id=1, source_target_pairs={{0,1},{1,0},{2,3},{3,2},{4,5},{5,4},{6,7},{7,6},{8,9},{9,8},{10,11... | collective-permute-start | bytes 294920 | tf_op jit(solution)/shard_map/ppermute | solution.py:326
  10.7 6.1 %collective-permute-start.1 = (f32[48,512]{1,0:T(8,128)S(1)}, f32[48,512]{1,0:T(8,128)S(1)}, u32[]{:S(2)}, u32[]{:S(2)}) collective-permute-start(f32[48,512]{1,0:T(8,128)S(1)} %add.105.one_ref), channel_id=1, source_target_pairs={{0,2},{1,3},{2,0},{3,1},{4,6},{5,7},{6,4},{7,5},{8,10},{9,11},{10,... | collective-permute-start | bytes 294920 | tf_op jit(solution)/shard_map/ppermute | solution.py:326
  20.1 8.1 %collective-permute-start.2 = (f32[48,2176]{1,0:T(8,128)S(1)}, f32[48,2176]{1,0:T(8,128)S(1)}, u32[]{:S(2)}, u32[]{:S(2)}) collective-permute-start(f32[48,2176]{1,0:T(8,128)S(1)} %get-tuple-element.15.after_ref), channel_id=1, source_target_pairs={{0,8},{1,5},{2,10},{3,7},{4,12},{5,1},{6,14},{7,3},{8,0},{9,13},{1... | collective-permute-start | bytes 1253384 | tf_op jit(solution)/shard_map/ppermute | solution.py:334
  28.3 6.0 %collective-permute-start.3 = (f32[48,1152]{1,0:T(8,128)S(1)}, f32[48,1152]{1,0:T(8,128)S(1)}, u32[]{:S(2)}, u32[]{:S(2)}) collective-permute-start(f32[48,1152]{1,0:T(8,128)S(1)} %slice.33), channel_id=1, source_target_pairs={{0,4},{1,9},{2,6},{3,11},{4,0},{5,13},{6,2},{7,15},{8,12},{9,1},{1... | collective-permute-start | bytes 663560 | tf_op jit(solution)/shard_map/ppermute | solution.py:334
  34.4 11.1 %collective-permute-start.4 = (f32[48,1152]{1,0:T(8,128)S(1)}, f32[48,1152]{1,0:T(8,128)S(1)}, u32[]{:S(2)}, u32[]{:S(2)}) collective-permute-start(f32[48,1152]{1,0:T(8,128)S(1)} %pad_maximum_fusion.2), channel_id=1, source_target_pairs={{0,16},{4,20},{8,24},{12,28},{16,0},{20,4},{24,8},{28,12},{1,17},{... | collective-permute-start | bytes 663560 | tf_op jit(solution)/shard_map/ppermute | solution.py:326
  37.2 12.6 %collective-permute-start.6 = (f32[48,2048]{1,0:T(8,128)S(1)}, f32[48,2048]{1,0:T(8,128)S(1)}, u32[]{:S(2)}, u32[]{:S(2)}) collective-permute-start(f32[48,2048]{1,0:T(8,128)S(1)} %get-tuple-element.19), channel_id=1, source_target_pairs={{0,8},{1,5},{2,10},{3,7},{4,12},{5,1},{6,14},{7,3},{8,0},{9,13},{1... | collective-permute-start | bytes 1179656 | tf_op jit(solution)/shard_map/ppermute | solution.py:334
  45.5 5.7 %collective-permute-start.5 = (f32[48,1024]{1,0:T(8,128)S(1)}, f32[48,1024]{1,0:T(8,128)S(1)}, u32[]{:S(2)}, u32[]{:S(2)}) collective-permute-start(f32[48,1024]{1,0:T(8,128)S(1)} %slice.37.refs_0_), channel_id=1, source_target_pairs={{0,4},{1,9},{2,6},{3,11},{4,0},{5,13},{6,2},{7,15},{8,12},{9,1},{1... | collective-permute-start | bytes 589832 | tf_op jit(solution)/shard_map/ppermute | solution.py:334
  49.9 7.8 %collective-permute-start.7 = (f32[48,1024]{1,0:T(8,128)S(1)}, f32[48,1024]{1,0:T(8,128)S(1)}, u32[]{:S(2)}, u32[]{:S(2)}) collective-permute-start(f32[48,1024]{1,0:T(8,128)S(1)} %slice.39), channel_id=1, source_target_pairs={{0,4},{1,9},{2,6},{3,11},{4,0},{5,13},{6,2},{7,15},{8,12},{9,1},{1... | collective-permute-start | bytes 589832 | tf_op jit(solution)/shard_map/ppermute | solution.py:334
  51.3 15.4 %collective-permute-start.9 = (f32[48,2048]{1,0:T(8,128)S(1)}, f32[48,2048]{1,0:T(8,128)S(1)}, u32[]{:S(2)}, u32[]{:S(2)}) collective-permute-start(f32[48,2048]{1,0:T(8,128)S(1)} %pad_maximum_fusion), channel_id=1, source_target_pairs={{0,8},{1,5},{2,10},{3,7},{4,12},{5,1},{6,14},{7,3},{8,0},{9,13},{1... | collective-permute-start | bytes 1179656 | tf_op jit(solution)/shard_map/ppermute | solution.py:334
  57.7 8.8 %collective-permute-start.8 = (f32[48,1024]{1,0:T(8,128)S(1)}, f32[48,1024]{1,0:T(8,128)S(1)}, u32[]{:S(2)}, u32[]{:S(2)}) collective-permute-start(f32[48,1024]{1,0:T(8,128)S(1)} %slice_add_fusion), channel_id=1, source_target_pairs={{0,16},{4,20},{8,24},{12,28},{16,0},{20,4},{24,8},{28,12},{1,17},{... | collective-permute-start | bytes 589832 | tf_op jit(solution)/shard_map/ppermute | solution.py:326
  66.6 7.8 %collective-permute-start.10 = (f32[48,1024]{1,0:T(8,128)S(1)}, f32[48,1024]{1,0:T(8,128)S(1)}, u32[]{:S(2)}, u32[]{:S(2)}) collective-permute-start(f32[48,1024]{1,0:T(8,128)S(1)} %add.117.refs_3_), channel_id=1, source_target_pairs={{0,4},{1,9},{2,6},{3,11},{4,0},{5,13},{6,2},{7,15},{8,12},{9,1},{1... | collective-permute-start | bytes 589832 | tf_op jit(solution)/shard_map/ppermute | solution.py:334
  74.5 7.8 %collective-permute-start.11 = (f32[48,2048]{1,0:T(8,128)S(1)}, f32[48,2048]{1,0:T(8,128)S(1)}, u32[]{:S(2)}, u32[]{:S(2)}) collective-permute-start(f32[48,2048]{1,0:T(8,128)S(1)} %pad_maximum_fusion.1), channel_id=1, source_target_pairs={{0,8},{1,5},{2,10},{3,7},{4,12},{5,1},{6,14},{7,3},{8,0},{9,13},{1... | collective-permute-start | bytes 1179656 | tf_op jit(solution)/shard_map/ppermute | solution.py:334

commit v12 on v7

--- a/solution.py
+++ b/solution.py
@@ -12,8 +12,9 @@
 VMEM_LIMIT = 40 * 1024 * 1024
 LANES = 128
 CHUNKS = 2
-AHEAD = 6
+AHEAD = 8
 UNIT = 512
+TILE = 256
 PANEL = 4
 LAST = (((1,), (1,)), ((), ()))
 PLAIN = (((1,), (0,)), ((), ()))
@@ -33,6 +34,11 @@
     return lax.dot_general(a, b, dims, preferred_element_type=F32)
 
 
+def tiles(size):
+    step = min(TILE, size)
+    return [slice(start, start + step) for start in range(0, size, step)]
+
+
 def in_hbm(x):
     return pltpu.with_memory_space_constraint(x, pltpu.MemorySpace.HBM)
 
@@ -47,22 +53,28 @@
         use(k)
 
 
-def tall_kernel(x_hbm, s_hbm, out_ref, x_buf, s_buf, x_sems, s_sem):
+def tall_kernel(x_hbm, s_hbm, out_ref, x_buf, s_buf, head_buf, rest_buf, x_sems, s_sems):
     blocks, _, unit = x_buf.shape
     rank = s_hbm.shape[0]
-    copies = [
-        pltpu.make_async_copy(x_hbm.at[:, pl.ds(k * unit, unit)], x_buf.at[k], x_sems.at[k])
-        for k in range(blocks)
-    ]
-    sketch = pltpu.make_async_copy(s_hbm, s_buf, s_sem)
-    sketch.start()
-
-    def use(k):
-        if k == 0:
-            sketch.wait()
-        s_head, s_rest = split(s_buf[:, k * unit : (k + 1) * unit])
+
+    def copies(k):
+        where = pl.ds(k * unit, unit)
+        return (
+            pltpu.make_async_copy(s_hbm.at[:, where], s_buf.at[k], s_sems.at[k]),
+            pltpu.make_async_copy(x_hbm.at[:, where], x_buf.at[k], x_sems.at[k]),
+        )
+
+    for k in range(blocks):
+        for copy in copies(k):
+            copy.start()
+    for k in range(blocks):
+        for copy in copies(k):
+            copy.wait()
+        s_head, s_rest = split(s_buf[k])
         s_both = jnp.concatenate([s_head, s_rest], axis=0)
         x_head, x_rest = split(x_buf[k])
+        head_buf[k] = x_head
+        rest_buf[k] = x_rest
         both = dot(s_both, x_head, LAST)
         part = both[:rank] + (both[rank:] + dot(s_head, x_rest, LAST))
         if k == 0:
@@ -70,13 +82,11 @@
         else:
             out_ref[...] += part
 
-    stream(copies, use)
-
 
 def tall_partial(probes, sketch_t):
     rows, cols = probes.shape
     rank = sketch_t.shape[0]
-    unit = min(UNIT, cols)
+    unit = min(2 * UNIT, cols)
     blocks = cols // unit
     return pl.pallas_call(
         tall_kernel,
@@ -85,9 +95,11 @@
         out_shape=jax.ShapeDtypeStruct((rank, rows), F32),
         scratch_shapes=[
             pltpu.VMEM((blocks, rows, unit), F32),
-            pltpu.VMEM((rank, cols), F32),
+            pltpu.VMEM((blocks, rank, unit), F32),
+            pltpu.VMEM((blocks, rows, unit), BF16),
+            pltpu.VMEM((blocks, rows, unit), BF16),
             pltpu.SemaphoreType.DMA((blocks,)),
-            pltpu.SemaphoreType.DMA,
+            pltpu.SemaphoreType.DMA((blocks,)),
         ],
         compiler_params=PARAMS,
         cost_estimate=pl.CostEstimate(
@@ -110,12 +122,15 @@
     ]
 
     def use(k):
-        both = both_ref[...]
-        x_head, x_rest = split(x_buf[k])
-        first = dot(both, x_head, PLAIN)
-        second = dot(both[:rank], x_rest, PLAIN)
         out, offset = plan[k]
-        outs[out][:, offset : offset + unit] = first[:rank] + (first[rank:] + second)
+        for cols in tiles(unit):
+            total = None
+            for rows in tiles(x_buf.shape[1]):
+                x_head, x_rest = split(x_buf[k, rows, cols])
+                both = dot(both_ref[:, rows], x_head, PLAIN)
+                part = both[:rank] + (both[rank:] + dot(both_ref[:rank, rows], x_rest, PLAIN))
+                total = part if total is None else total + part
+            outs[out][:, offset + cols.start : offset + cols.stop] = total
 
     return copies, use
 
@@ -343,7 +358,8 @@
 
     both, gram, away = first_products(tall, other, probes, outputs(0, 1), width)
 
-    inverse, out, after = None, None, away[0]
+    inverse, after = None, away[0]
+    sources, pieces = [], []
     for c in range(CHUNKS):
         g = LANES if c == 0 else 0
         last = c == CHUNKS - 1
@@ -352,10 +368,11 @@
         )
         away_a, away_b = away
         (own_a, own_b), away = made[:2], made[2:]
+        if c > 0:
+            away_a, away_b, sum_a, sum_b = lax.optimization_barrier((away_a, away_b, sum_a, sum_b))
         got_a = over(away_a, 1)
         sum_a = own_a + got_a
         sum_b = own_b + over(away_b, 2)
-        after = got_a
         send_a, send_b = sum_a[:, : width + g], sum_b[:, :width]
         if c > 0:
             send_a, send_b, whole = lax.optimization_barrier((send_a, send_b, whole))
@@ -369,7 +386,7 @@
             ],
             axis=1,
         )
-        total = whole
+        after = total = whole
         bit = 4
         while bit < n_pos:
             total = total + over(total, bit)
@@ -383,26 +400,21 @@
         next_b = over(mine_b, 1)
         last_a = over(jnp.concatenate([mine_a, next_a], axis=1), 1)
         last_b = over(jnp.concatenate([mine_b, next_b], axis=1), 2)
-        sources = [total, next_a, next_b]
-        pieces = [
-            (block_a(c, 0, 0), 0, 0),
-            (block_b(c, 0, 0), 0, width + g),
-            (block_a(c, 0, 1), 1, 0),
-            (block_b(c, 0, 1), 2, 0),
+        k = len(sources)
+        sources += [total, next_a, next_b, last_a, last_b]
+        pieces += [
+            (block_a(c, 0, 0), k, 0),
+            (block_b(c, 0, 0), k, width + g),
+            (block_a(c, 0, 1), k + 1, 0),
+            (block_b(c, 0, 1), k + 2, 0),
+            (block_a(c, 1, 0), k + 3, 0),
+            (block_a(c, 1, 1), k + 3, width),
+            (block_b(c, 1, 0), k + 4, 0),
+            (block_b(c, 1, 1), k + 4, width),
         ]
-        if last:
-            out = finish(inverse, sources, pieces, width, cols, out)
-            sources, pieces = [], []
-        k = len(sources)
-        sources += [last_a, last_b]
-        pieces += [
-            (block_a(c, 1, 0), k, 0),
-            (block_a(c, 1, 1), k, width),
-            (block_b(c, 1, 0), k + 1, 0),
-            (block_b(c, 1, 1), k + 1, width),
-        ]
-        out = finish(inverse, sources, pieces, width, cols, out)
-    return out
+    out = finish(inverse, sources[:-2], pieces[:-4], width, cols)
+    pieces = [(where, source - k - 3, start) for where, source, start in pieces[-4:]]
+    return finish(inverse, sources[-2:], pieces, width, cols, out)
 
 
 def solution(mesh):

time: 72.6 us -> 75.8 us (1.044)
  waiting for transfers between devices: 21 us -> 26.4 us
  Pallas kernels: 26.3 us -> 23.4 us
  starting transfers between devices: 24 us -> 24.9 us
    ppermute x20, waiting for transfers between devices: 21 us -> 26.4 us  [swap(): return lax.ppermute(value, axis, [(i, i ^ bit) for i in range(size)])]
    pallas_call x1, Pallas kernels: 8.61 us -> 7.27 us  [tall_partial(): pl.pallas_call(tall_kernel, in_specs=[HBM, HBM], out_specs=WHOLE, out_sha...]
    pallas_call x3 -> x2, Pallas kernels: 4.72 us -> 3.39 us  [finish(): pl.pallas_call(functools.partial(finish_kernel, [piece[1:] for piece in p...]
    ppermute x20, starting transfers between devices: 24 us -> 24.9 us  [swap(): return lax.ppermute(value, axis, [(i, i ^ bit) for i in range(size)])]
  transfers between devices with their start and end apart: 20 -> 20, of which waited for: 10 -> 10; matrix products, arithmetic and copies ran while one was open for 1% -> 1% of each run, Pallas kernels for 18% -> 15%
where the time goes in v12:
time: 75.8 us; the launch traced here: 75.7 us
  waiting for transfers between devices  26.4 us (35%)
  starting transfers between devices  24.9 us (33%)
  Pallas kernels  23.4 us (31%)
    ppermute x20, waiting for transfers between devices, swap(): return lax.ppermute(value, axis, [(i, i ^ bit) for i in range(size)])  26.4 us
    ppermute x20, starting transfers between devices, swap(): return lax.ppermute(value, axis, [(i, i ^ bit) for i in range(size)])  24.9 us
    pallas_call x3, Pallas kernels, products(): pl.pallas_call(functools.partial(kernel, plan, grams), in_specs=[TABLE, *...  10.7 us
    pallas_call x1, Pallas kernels, tall_partial(): pl.pallas_call(tall_kernel, in_specs=[HBM, HBM], out_specs=WHOLE, out_sha...  7.27 us
    pallas_call x2, Pallas kernels, finish(): pl.pallas_call(functools.partial(finish_kernel, [piece[1:] for piece in p...  3.39 us
    pallas_call x1, Pallas kernels, inverse_factor(): pl.pallas_call(inverse_kernel, grid=(1,), in_specs=[pl.BlockSpec((rank, L...  2.01 us
  transfers between devices with their start and end apart: 20, of which 10 were waited for; matrix products, arithmetic and copies ran while one was open for 1% of the time, Pallas kernels for 15%

profile of v12, /device:TPU:0, one launch (start us, length us, event | category | flops | bytes accessed | tf_op | source)
XLA Modules:
  0.0 75.7 jit_solution(13307890554909813178)
XLA Ops:
  0.0 7.3 %tall_partial.1 = f32[48,512]{1,0:T(8,128)S(1)} custom-call(f32[512,8192]{1,0:T(8,128)} %x_hbm.7, f32[48,8192]{1,0:T(8,128)} %bitcast.17), custom_call_target="tpu_custom_call" | custom-call | flops 1207959552 | bytes 16777216 | tf_op jit(solution)/shard_map/tall_partial/pallas_call | solution.py:91
  8.8 2.9 %collective-permute-start.1 = (f32[48,512]{1,0:T(8,128)S(1)}, f32[48,512]{1,0:T(8,128)S(1)}, u32[]{:S(2)}, u32[]{:S(2)}) collective-permute-start(f32[48,512]{1,0:T(8,128)S(1)} %add.153.one_ref), channel_id=1, source_target_pairs={{0,2},{1,3},{2,0},{3,1},{4,6},{5,7},{6,4},{7,5},{8,10},{9,11},{10,... | collective-permute-start | bytes 294920 | tf_op jit(solution)/shard_map/ppermute | solution.py:330
  11.8 3.0 %collective-permute-done.1.two_ref = f32[48,512]{1,0:T(8,128)S(1)} collective-permute-done((f32[48,512]{1,0:T(8,128)S(1)}, f32[48,512]{1,0:T(8,128)S(1)}, u32[]{:S(2)}, u32[]{:S(2)}) %collective-permute-start.1) | collective-permute-done | bytes 98336 | tf_op jit(solution)/shard_map/ppermute | solution.py:330
  14.8 3.3 %first_products.1 = (bf16[96,512]{1,0:T(8,128)(2,1)S(1)}, f32[48,128]{1,0:T(8,128)S(1)}, f32[48,1152]{1,0:T(8,128)S(1)}, f32[48,1024]{1,0:T(8,128)S(1)}) custom-call(s32[4]{0:T(128)S(1)} %pad_add_fusion.2.which_ref, f32[48,512]{1,0:T(8,128)S(1)} %add.153.one_ref, f32[48,512]{1,0:T(8,128)S(1)} %collective-permute-done.1.two_ref, f32[512,8192]{1,0:T(8,128)} %x_hbm.7), custom_call_target="tpu_custom_call" | custom-call | flops 301989888 | bytes 4194304 | tf_op jit(solution)/shard_map/first_products/pallas_call | solution.py:192
  18.2 1.9 %collective-permute-start.4 = (f32[48,1024]{1,0:T(8,128)S(1)}, f32[48,1024]{1,0:T(8,128)S(1)}, u32[]{:S(2)}, u32[]{:S(2)}) collective-permute-start(f32[48,1024]{1,0:T(8,128)S(1)} %get-tuple-element.27), channel_id=1, source_target_pairs={{0,8},{4,12},{8,0},{12,4},{16,24},{20,28},{24,16},{28,20},{1,9},{5... | collective-permute-start | bytes 589832 | tf_op jit(solution)/shard_map/ppermute | solution.py:330
  20.0 1.5 %collective-permute-start.2 = (f32[48,1152]{1,0:T(8,128)S(1)}, f32[48,1152]{1,0:T(8,128)S(1)}, u32[]{:S(2)}, u32[]{:S(2)}) collective-permute-start(f32[48,1152]{1,0:T(8,128)S(1)} %get-tuple-element.24.after_ref), channel_id=1, source_target_pairs={{0,4},{4,0},{8,12},{12,8},{16,20},{20,16},{24,28},{28,24},{1,5},{5... | collective-permute-start | bytes 663560 | tf_op jit(solution)/shard_map/ppermute | solution.py:330
  21.6 4.3 %rest_products.2 = (f32[48,1152]{1,0:T(8,128)S(1)}, f32[48,1024]{1,0:T(8,128)S(1)}, f32[48,1024]{1,0:T(8,128)S(1)}, f32[48,1024]{1,0:T(8,128)S(1)}) custom-call(s32[8]{0:T(128)S(1)} %stack.98.which_ref, bf16[96,512]{1,0:T(8,128)(2,1)S(1)} %get-tuple-element.22.both_ref, f32[48,128]{1,0:T(8,128)S(1)} %get-tuple-element.23.gram_ref, f32[512,8192]{1,0:T(8,128)} %x_hbm.7, ...), custom_call_target="tpu_custom_call" | custom-call | flops 603979776 | bytes 8388608 | tf_op jit(solution)/shard_map/rest_products/pallas_call | solution.py:192
  26.7 1.2 %collective-permute-start.3 = (f32[48,640]{1,0:T(8,128)S(1)}, f32[48,640]{1,0:T(8,128)S(1)}, u32[]{:S(2)}, u32[]{:S(2)}) collective-permute-start(f32[48,640]{1,0:T(8,128)S(1)} %slice.61), channel_id=1, source_target_pairs={{0,8},{4,12},{8,0},{12,4},{16,24},{20,28},{24,16},{28,20},{1,9},{5... | collective-permute-start | bytes 368648 | tf_op jit(solution)/shard_map/ppermute | solution.py:330
  28.8 1.6 %collective-permute-start.7 = (f32[48,1024]{1,0:T(8,128)S(1)}, f32[48,1024]{1,0:T(8,128)S(1)}, u32[]{:S(2)}, u32[]{:S(2)}) collective-permute-start(f32[48,1024]{1,0:T(8,128)S(1)} %get-tuple-element.33), channel_id=1, source_target_pairs={{0,8},{4,12},{8,0},{12,4},{16,24},{20,28},{24,16},{28,20},{1,9},{5... | collective-permute-start | bytes 589832 | tf_op jit(solution)/shard_map/ppermute | solution.py:330
  30.3 1.3 %collective-permute-done.5 = f32[48,512]{1,0:T(8,128)S(1)} collective-permute-done((f32[48,512]{1,0:T(8,128)S(1)}, f32[48,512]{1,0:T(8,128)S(1)}, u32[]{:S(2)}, u32[]{:S(2)}) %collective-permute-start.5) | collective-permute-done | bytes 98336 | tf_op jit(solution)/shard_map/ppermute | solution.py:330
  32.7 3.1 %rest_products.3 = (f32[48,1024]{1,0:T(8,128)S(1)}, f32[48,1024]{1,0:T(8,128)S(1)}) custom-call(s32[4]{0:T(128)S(1)} %pad_add_fusion.1.which_ref, bf16[96,512]{1,0:T(8,128)(2,1)S(1)} %get-tuple-element.22.both_ref, f32[48,128]{1,0:T(8,128)S(1)} %get-tuple-element.23.gram_ref, f32[512,8192]{1,0:T(8,128)} %x_hbm.7, f32[48,1152]{1,0:T(8,128)S(1)} %pad_maximum_fusion.after_ref), custom_call_target="tpu_custom_call" | custom-call | flops 301989888 | bytes 4194304 | tf_op jit(solution)/shard_map/rest_products/pallas_call | solution.py:192
  35.9 1.5 %collective-permute-start.8 = (f32[48,512]{1,0:T(8,128)S(1)}, f32[48,512]{1,0:T(8,128)S(1)}, u32[]{:S(2)}, u32[]{:S(2)}) collective-permute-start(f32[48,512]{1,0:T(8,128)S(1)} %slice.68), channel_id=1, source_target_pairs={{0,8},{4,12},{8,0},{12,4},{16,24},{20,28},{24,16},{28,20},{1,9},{5... | collective-permute-start | bytes 294920 | tf_op jit(solution)/shard_map/ppermute | solution.py:330
  37.4 2.6 %collective-permute-start.11 = (f32[48,1152]{1,0:T(8,128)S(1)}, f32[48,1152]{1,0:T(8,128)S(1)}, u32[]{:S(2)}, u32[]{:S(2)}) collective-permute-start(f32[48,1152]{1,0:T(8,128)S(1)} %pad_maximum_fusion.after_ref), channel_id=1, source_target_pairs={{0,16},{4,20},{8,24},{12,28},{16,0},{20,4},{24,8},{28,12},{1,17},{... | collective-permute-start | bytes 663560 | tf_op jit(solution)/shard_map/ppermute | solution.py:330
  40.7 3.9 %collective-permute-done.9 = f32[48,512]{1,0:T(8,128)S(1)} collective-permute-done((f32[48,512]{1,0:T(8,128)S(1)}, f32[48,512]{1,0:T(8,128)S(1)}, u32[]{:S(2)}, u32[]{:S(2)}) %collective-permute-start.9) | collective-permute-done | bytes 98336 | tf_op jit(solution)/shard_map/ppermute | solution.py:330
  44.6 2.8 %collective-permute-done.11 = f32[48,1152]{1,0:T(8,128)S(1)} collective-permute-done((f32[48,1152]{1,0:T(8,128)S(1)}, f32[48,1152]{1,0:T(8,128)S(1)}, u32[]{:S(2)}, u32[]{:S(2)}) %collective-permute-start.11) | collective-permute-done | bytes 221216 | tf_op jit(solution)/shard_map/ppermute | solution.py:330
  47.6 3.1 %collective-permute-start.10 = (f32[48,1024]{1,0:T(8,128)S(1)}, f32[48,1024]{1,0:T(8,128)S(1)}, u32[]{:S(2)}, u32[]{:S(2)}) collective-permute-start(f32[48,1024]{1,0:T(8,128)S(1)} %pad_maximum_fusion.1), channel_id=1, source_target_pairs={{0,16},{4,20},{8,24},{12,28},{16,0},{20,4},{24,8},{28,12},{1,17},{... | collective-permute-start | bytes 589832 | tf_op jit(solution)/shard_map/ppermute | solution.py:330
  51.7 2.0 %inverse_factor.1.inverse_ref = f32[48,48]{1,0:T(8,128)S(1)} custom-call(f32[48,1152]{1,0:T(8,128)S(1)} %fusion.1.gram_ref.refs_0_), custom_call_target="tpu_custom_call" | custom-call | flops 20000000 | bytes 49152 | tf_op jit(solution)/shard_map/inverse_factor/pallas_call | solution.py:267
  54.8 3.2 %collective-permute-done.10 = f32[48,1024]{1,0:T(8,128)S(1)} collective-permute-done((f32[48,1024]{1,0:T(8,128)S(1)}, f32[48,1024]{1,0:T(8,128)S(1)}, u32[]{:S(2)}, u32[]{:S(2)}) %collective-permute-start.10) | collective-permute-done | bytes 196640 | tf_op jit(solution)/shard_map/ppermute | solution.py:330
  58.7 2.0 %collective-permute-start.12 = (f32[48,512]{1,0:T(8,128)S(1)}, f32[48,512]{1,0:T(8,128)S(1)}, u32[]{:S(2)}, u32[]{:S(2)}) collective-permute-start(f32[48,512]{1,0:T(8,128)S(1)} %get-tuple-element.37), channel_id=1, source_target_pairs={{0,8},{4,12},{8,0},{12,4},{16,24},{20,28},{24,16},{28,20},{1,9},{5... | collective-permute-start | bytes 294920 | tf_op jit(solution)/shard_map/ppermute | solution.py:330
  60.7 2.1 %collective-permute-done.14.refs_7_ = f32[48,512]{1,0:T(8,128)S(1)} collective-permute-done((f32[48,512]{1,0:T(8,128)S(1)}, f32[48,512]{1,0:T(8,128)S(1)}, u32[]{:S(2)}, u32[]{:S(2)}) %collective-permute-start.14) | collective-permute-done | bytes 98336 | tf_op jit(solution)/shard_map/ppermute | solution.py:330
  62.9 5.6 %collective-permute-done.12.refs_6_ = f32[48,512]{1,0:T(8,128)S(1)} collective-permute-done((f32[48,512]{1,0:T(8,128)S(1)}, f32[48,512]{1,0:T(8,128)S(1)}, u32[]{:S(2)}, u32[]{:S(2)}) %collective-permute-start.12) | collective-permute-done | bytes 98336 | tf_op jit(solution)/shard_map/ppermute | solution.py:330
  69.8 1.9 %finish.2.refs_2_ = f32[48,8192]{1,0:T(8,128)} custom-call(s32[12]{0:T(128)S(1)} %stack.99.where_ref, f32[48,48]{1,0:T(8,128)S(1)} %inverse_factor.1.inverse_ref, f32[48,1152]{1,0:T(8,128)S(1)} %fusion.1.gram_ref.refs_0_, f32[48,512]{1,0:T(8,128)S(1)} %collective-permute-done.16.refs_1_, f32[48,512]{1,0:T(8,128)S(1)} %collective-permute-done.17.refs_2_, ...), custom_call_target="tpu_custom_call" | custom-call | flops 84934656 | bytes 2359296 | tf_op jit(solution)/shard_map/finish/pallas_call | solution.py:308
  71.7 2.5 %collective-permute-done.13.refs_0_ = f32[48,1024]{1,0:T(8,128)S(1)} collective-permute-done((f32[48,1024]{1,0:T(8,128)S(1)}, f32[48,1024]{1,0:T(8,128)S(1)}, u32[]{:S(2)}, u32[]{:S(2)}) %collective-permute-start.13) | collective-permute-done | bytes 196640 | tf_op jit(solution)/shard_map/ppermute | solution.py:330
  74.2 1.5 %finish.3 = f32[48,8192]{1,0:T(8,128)} custom-call(s32[4]{0:T(128)S(1)} %pad_add_fusion.where_ref, f32[48,48]{1,0:T(8,128)S(1)} %inverse_factor.1.inverse_ref, f32[48,1024]{1,0:T(8,128)S(1)} %collective-permute-done.13.refs_0_, f32[48,1024]{1,0:T(8,128)S(1)} %collective-permute-done.15.refs_1_, f32[48,8192]{1,0:T(8,128)} %finish.2.refs_2_), custom_call_target="tpu_custom_call", output_to_operand_aliasing={{}: (4, {})} | custom-call | flops 28311552 | bytes 786432 | tf_op jit(solution)/shard_map/finish/pallas_call | solution.py:308
  (52 shorter events, 9.4 us)
Async XLA Ops:
  7.3 1.5 %collective-permute-start = (f32[48,512]{1,0:T(8,128)S(1)}, f32[48,512]{1,0:T(8,128)S(1)}, u32[]{:S(2)}, u32[]{:S(2)}) collective-permute-start(f32[48,512]{1,0:T(8,128)S(1)} %tall_partial.1), channel_id=1, source_target_pairs={{0,1},{1,0},{2,3},{3,2},{4,5},{5,4},{6,7},{7,6},{8,9},{9,8},{10,11... | collective-permute-start | bytes 294920 | tf_op jit(solution)/shard_map/ppermute | solution.py:330
  8.8 6.0 %collective-permute-start.1 = (f32[48,512]{1,0:T(8,128)S(1)}, f32[48,512]{1,0:T(8,128)S(1)}, u32[]{:S(2)}, u32[]{:S(2)}) collective-permute-start(f32[48,512]{1,0:T(8,128)S(1)} %add.153.one_ref), channel_id=1, source_target_pairs={{0,2},{1,3},{2,0},{3,1},{4,6},{5,7},{6,4},{7,5},{8,10},{9,11},{10,... | collective-permute-start | bytes 294920 | tf_op jit(solution)/shard_map/ppermute | solution.py:330
  18.2 7.8 %collective-permute-start.4 = (f32[48,1024]{1,0:T(8,128)S(1)}, f32[48,1024]{1,0:T(8,128)S(1)}, u32[]{:S(2)}, u32[]{:S(2)}) collective-permute-start(f32[48,1024]{1,0:T(8,128)S(1)} %get-tuple-element.27), channel_id=1, source_target_pairs={{0,8},{4,12},{8,0},{12,4},{16,24},{20,28},{24,16},{28,20},{1,9},{5... | collective-permute-start | bytes 589832 | tf_op jit(solution)/shard_map/ppermute | solution.py:330
  20.0 6.7 %collective-permute-start.2 = (f32[48,1152]{1,0:T(8,128)S(1)}, f32[48,1152]{1,0:T(8,128)S(1)}, u32[]{:S(2)}, u32[]{:S(2)}) collective-permute-start(f32[48,1152]{1,0:T(8,128)S(1)} %get-tuple-element.24.after_ref), channel_id=1, source_target_pairs={{0,4},{4,0},{8,12},{12,8},{16,20},{20,16},{24,28},{28,24},{1,5},{5... | collective-permute-start | bytes 663560 | tf_op jit(solution)/shard_map/ppermute | solution.py:330
  26.0 5.6 %collective-permute-start.5 = (f32[48,512]{1,0:T(8,128)S(1)}, f32[48,512]{1,0:T(8,128)S(1)}, u32[]{:S(2)}, u32[]{:S(2)}) collective-permute-start(f32[48,512]{1,0:T(8,128)S(1)} %slice.66), channel_id=1, source_target_pairs={{0,4},{4,0},{8,12},{12,8},{16,20},{20,16},{24,28},{28,24},{1,5},{5... | collective-permute-start | bytes 294920 | tf_op jit(solution)/shard_map/ppermute | solution.py:330
  26.7 6.0 %collective-permute-start.3 = (f32[48,640]{1,0:T(8,128)S(1)}, f32[48,640]{1,0:T(8,128)S(1)}, u32[]{:S(2)}, u32[]{:S(2)}) collective-permute-start(f32[48,640]{1,0:T(8,128)S(1)} %slice.61), channel_id=1, source_target_pairs={{0,8},{4,12},{8,0},{12,4},{16,24},{20,28},{24,16},{28,20},{1,9},{5... | collective-permute-start | bytes 368648 | tf_op jit(solution)/shard_map/ppermute | solution.py:330
  28.0 7.9 %collective-permute-start.6 = (f32[48,1024]{1,0:T(8,128)S(1)}, f32[48,1024]{1,0:T(8,128)S(1)}, u32[]{:S(2)}, u32[]{:S(2)}) collective-permute-start(f32[48,1024]{1,0:T(8,128)S(1)} %get-tuple-element.31), channel_id=1, source_target_pairs={{0,4},{4,0},{8,12},{12,8},{16,20},{20,16},{24,28},{28,24},{1,5},{5... | collective-permute-start | bytes 589832 | tf_op jit(solution)/shard_map/ppermute | solution.py:330
  28.8 7.1 %collective-permute-start.7 = (f32[48,1024]{1,0:T(8,128)S(1)}, f32[48,1024]{1,0:T(8,128)S(1)}, u32[]{:S(2)}, u32[]{:S(2)}) collective-permute-start(f32[48,1024]{1,0:T(8,128)S(1)} %get-tuple-element.33), channel_id=1, source_target_pairs={{0,8},{4,12},{8,0},{12,4},{16,24},{20,28},{24,16},{28,20},{1,9},{5... | collective-permute-start | bytes 589832 | tf_op jit(solution)/shard_map/ppermute | solution.py:330
  35.9 4.8 %collective-permute-start.8 = (f32[48,512]{1,0:T(8,128)S(1)}, f32[48,512]{1,0:T(8,128)S(1)}, u32[]{:S(2)}, u32[]{:S(2)}) collective-permute-start(f32[48,512]{1,0:T(8,128)S(1)} %slice.68), channel_id=1, source_target_pairs={{0,8},{4,12},{8,0},{12,4},{16,24},{20,28},{24,16},{28,20},{1,9},{5... | collective-permute-start | bytes 294920 | tf_op jit(solution)/shard_map/ppermute | solution.py:330
  37.4 10.0 %collective-permute-start.11 = (f32[48,1152]{1,0:T(8,128)S(1)}, f32[48,1152]{1,0:T(8,128)S(1)}, u32[]{:S(2)}, u32[]{:S(2)}) collective-permute-start(f32[48,1152]{1,0:T(8,128)S(1)} %pad_maximum_fusion.after_ref), channel_id=1, source_target_pairs={{0,16},{4,20},{8,24},{12,28},{16,0},{20,4},{24,8},{28,12},{1,17},{... | collective-permute-start | bytes 663560 | tf_op jit(solution)/shard_map/ppermute | solution.py:330
  40.0 4.6 %collective-permute-start.9 = (f32[48,512]{1,0:T(8,128)S(1)}, f32[48,512]{1,0:T(8,128)S(1)}, u32[]{:S(2)}, u32[]{:S(2)}) collective-permute-start(f32[48,512]{1,0:T(8,128)S(1)} %slice.69), channel_id=1, source_target_pairs={{0,4},{4,0},{8,12},{12,8},{16,20},{20,16},{24,28},{28,24},{1,5},{5... | collective-permute-start | bytes 294920 | tf_op jit(solution)/shard_map/ppermute | solution.py:330
  47.5 6.2 %collective-permute-start.16 = (f32[48,512]{1,0:T(8,128)S(1)}, f32[48,512]{1,0:T(8,128)S(1)}, u32[]{:S(2)}, u32[]{:S(2)}) collective-permute-start(f32[48,512]{1,0:T(8,128)S(1)} %get-tuple-element.40), channel_id=1, source_target_pairs={{0,8},{4,12},{8,0},{12,4},{16,24},{20,28},{24,16},{28,20},{1,9},{5... | collective-permute-start | bytes 294920 | tf_op jit(solution)/shard_map/ppermute | solution.py:330
  47.6 10.5 %collective-permute-start.10 = (f32[48,1024]{1,0:T(8,128)S(1)}, f32[48,1024]{1,0:T(8,128)S(1)}, u32[]{:S(2)}, u32[]{:S(2)}) collective-permute-start(f32[48,1024]{1,0:T(8,128)S(1)} %pad_maximum_fusion.1), channel_id=1, source_target_pairs={{0,16},{4,20},{8,24},{12,28},{16,0},{20,4},{24,8},{28,12},{1,17},{... | collective-permute-start | bytes 589832 | tf_op jit(solution)/shard_map/ppermute | solution.py:330
  50.7 7.9 %collective-permute-start.17 = (f32[48,512]{1,0:T(8,128)S(1)}, f32[48,512]{1,0:T(8,128)S(1)}, u32[]{:S(2)}, u32[]{:S(2)}) collective-permute-start(f32[48,512]{1,0:T(8,128)S(1)} %get-tuple-element.39), channel_id=1, source_target_pairs={{0,4},{4,0},{8,12},{12,8},{16,20},{20,16},{24,28},{28,24},{1,5},{5... | collective-permute-start | bytes 294920 | tf_op jit(solution)/shard_map/ppermute | solution.py:330
  53.7 16.1 %collective-permute-start.18 = (f32[48,1024]{1,0:T(8,128)S(1)}, f32[48,1024]{1,0:T(8,128)S(1)}, u32[]{:S(2)}, u32[]{:S(2)}) collective-permute-start(f32[48,1024]{1,0:T(8,128)S(1)} %pad_maximum_fusion.4), channel_id=1, source_target_pairs={{0,4},{4,0},{8,12},{12,8},{16,20},{20,16},{24,28},{28,24},{1,5},{5... | collective-permute-start | bytes 589832 | tf_op jit(solution)/shard_map/ppermute | solution.py:330
  58.1 4.7 %collective-permute-start.14 = (f32[48,512]{1,0:T(8,128)S(1)}, f32[48,512]{1,0:T(8,128)S(1)}, u32[]{:S(2)}, u32[]{:S(2)}) collective-permute-start(f32[48,512]{1,0:T(8,128)S(1)} %get-tuple-element.38), channel_id=1, source_target_pairs={{0,4},{4,0},{8,12},{12,8},{16,20},{20,16},{24,28},{28,24},{1,5},{5... | collective-permute-start | bytes 294920 | tf_op jit(solution)/shard_map/ppermute | solution.py:330
  58.6 11.2 %collective-permute-start.19 = (f32[48,1024]{1,0:T(8,128)S(1)}, f32[48,1024]{1,0:T(8,128)S(1)}, u32[]{:S(2)}, u32[]{:S(2)}) collective-permute-start(f32[48,1024]{1,0:T(8,128)S(1)} %pad_maximum_fusion.5), channel_id=1, source_target_pairs={{0,8},{4,12},{8,0},{12,4},{16,24},{20,28},{24,16},{28,20},{1,9},{5... | collective-permute-start | bytes 589832 | tf_op jit(solution)/shard_map/ppermute | solution.py:330
  58.7 9.7 %collective-permute-start.12 = (f32[48,512]{1,0:T(8,128)S(1)}, f32[48,512]{1,0:T(8,128)S(1)}, u32[]{:S(2)}, u32[]{:S(2)}) collective-permute-start(f32[48,512]{1,0:T(8,128)S(1)} %get-tuple-element.37), channel_id=1, source_target_pairs={{0,8},{4,12},{8,0},{12,4},{16,24},{20,28},{24,16},{28,20},{1,9},{5... | collective-permute-start | bytes 294920 | tf_op jit(solution)/shard_map/ppermute | solution.py:330
  62.8 8.9 %collective-permute-start.15 = (f32[48,1024]{1,0:T(8,128)S(1)}, f32[48,1024]{1,0:T(8,128)S(1)}, u32[]{:S(2)}, u32[]{:S(2)}) collective-permute-start(f32[48,1024]{1,0:T(8,128)S(1)} %pad_maximum_fusion.3), channel_id=1, source_target_pairs={{0,8},{4,12},{8,0},{12,4},{16,24},{20,28},{24,16},{28,20},{1,9},{5... | collective-permute-start | bytes 589832 | tf_op jit(solution)/shard_map/ppermute | solution.py:330
  68.5 5.7 %collective-permute-start.13 = (f32[48,1024]{1,0:T(8,128)S(1)}, f32[48,1024]{1,0:T(8,128)S(1)}, u32[]{:S(2)}, u32[]{:S(2)}) collective-permute-start(f32[48,1024]{1,0:T(8,128)S(1)} %pad_maximum_fusion.2), channel_id=1, source_target_pairs={{0,4},{4,0},{8,12},{12,8},{16,20},{20,16},{24,28},{28,24},{1,5},{5... | collective-permute-start | bytes 589832 | tf_op jit(solution)/shard_map/ppermute | solution.py:330

commit v13 on v12

--- a/solution.py
+++ b/solution.py
@@ -135,19 +135,18 @@
     return copies, use
 
 
-def first_kernel(plan, grams, which_ref, one_ref, two_ref, x_hbm, both_ref, gram_ref, *refs):
+def first_kernel(plan, grams, which_ref, tall_ref, x_hbm, both_ref, gram_ref, *refs):
     outs, (x_buf, sems) = refs[:-2], refs[-2:]
     copies, use = multiply_blocks(both_ref, which_ref, x_hbm, x_buf, sems, plan, outs)
 
     def use_first(k):
         if k == 0:
-            tall = one_ref[...] + two_ref[...]
-            head, rest = split(tall)
+            head, rest = split(tall_ref[...])
             both_ref[...] = jnp.concatenate([head, rest], axis=0)
         use(k)
 
     stream(copies, use_first)
-    tall = one_ref[...] + two_ref[...]
+    tall = tall_ref[...]
     r = tall.shape[0]
     head, rest = split(tall)
     tail = (tall - head.astype(F32) - rest.astype(F32)).astype(BF16)
@@ -186,7 +185,7 @@
 
 def products(kernel, inputs, in_specs, made, probes, outputs, sub, name):
     rows = probes.shape[0]
-    rank = inputs[1].shape[0]
+    rank = made[1].shape[0] if made else inputs[1].shape[0]
     unit, plan, grams, widths, which = layout(outputs, sub)
     shapes = [*made, *[jax.ShapeDtypeStruct((rank, width), F32) for width in widths]]
     return pl.pallas_call(
@@ -208,16 +207,16 @@
     )(which, *inputs)
 
 
-def first_products(one, two, probes, outputs, sub):
-    rank, rows = one.shape
+def first_products(tall, probes, outputs, sub):
+    rank, rows = tall.shape
     made = [
         jax.ShapeDtypeStruct((2 * rank, rows), BF16),
         jax.ShapeDtypeStruct((rank, LANES), F32),
     ]
     both, gram, *outs = products(
         first_kernel,
-        [one, two, in_hbm(probes)],
-        [WHOLE, WHOLE, HBM],
+        [tall, in_hbm(probes)],
+        [WHOLE, HBM],
         made,
         probes,
         outputs,
@@ -338,11 +337,14 @@
     width = cols // (8 * CHUNKS)
 
     tall = tall_partial(probes, sketch.T)
-    bit = 1
-    while 2 * bit < n_pix:
-        tall = tall + swap(tall, "pix", n_pix, bit)
-        bit *= 2
-    other = swap(tall, "pix", n_pix, bit)
+    if n_pix == 4:
+        even = (lax.axis_index("pix") & 1) == 0
+        tall = tall + lax.ppermute(tall, "pix", [(1, 0), (3, 2)])
+        tall = tall + lax.ppermute(tall, "pix", [(0, 2), (2, 0)])
+        handed = lax.ppermute(tall, "pix", [(0, 1), (2, 3)])
+        tall = jnp.where(even, tall, handed)
+    else:
+        tall = lax.psum(tall, "pix")
 
     def block_a(c, p, q):
         return 8 * c + 2 * (near ^ p) + (far ^ q)
@@ -356,7 +358,7 @@
             ([block_b(c, p, 1), block_b(c, p, 0)], False),
         ]
 
-    both, gram, away = first_products(tall, other, probes, outputs(0, 1), width)
+    both, gram, away = first_products(tall, probes, outputs(0, 1), width)
 
     inverse, after = None, away[0]
     sources, pieces = [], []
@@ -368,11 +370,10 @@
         )
         away_a, away_b = away
         (own_a, own_b), away = made[:2], made[2:]
-        if c > 0:
-            away_a, away_b, sum_a, sum_b = lax.optimization_barrier((away_a, away_b, sum_a, sum_b))
         got_a = over(away_a, 1)
         sum_a = own_a + got_a
         sum_b = own_b + over(away_b, 2)
+        after = got_a
         send_a, send_b = sum_a[:, : width + g], sum_b[:, :width]
         if c > 0:
             send_a, send_b, whole = lax.optimization_barrier((send_a, send_b, whole))
@@ -386,7 +387,7 @@
             ],
             axis=1,
         )
-        after = total = whole
+        total = whole
         bit = 4
         while bit < n_pos:
             total = total + over(total, bit)

time: 75.8 us -> 77.9 us (1.028)
  starting transfers between devices: 24.9 us -> 27.2 us
    ppermute x0 -> x3, starting transfers between devices: none -> 7.46 us  [the longest x1 4.88 us: body(): tall = tall + lax.ppermute(tall, 'pix', [(0, 2), (2, 0)])]
    ppermute x20 -> x18, waiting for transfers between devices: 26.4 us -> 20.7 us  [swap(): return lax.ppermute(value, axis, [(i, i ^ bit) for i in range(size)])]
    ppermute x0 -> x3, waiting for transfers between devices: none -> 5.3 us  [the longest x1 2.56 us: body(): tall = tall + lax.ppermute(tall, 'pix', [(0, 2), (2, 0)])]
    ppermute x20 -> x18, starting transfers between devices: 24.9 us -> 19.7 us  [swap(): return lax.ppermute(value, axis, [(i, i ^ bit) for i in range(size)])]
  transfers between devices with their start and end apart: 20 -> 21, of which waited for: 10 -> 15; matrix products, arithmetic and copies ran while one was open for 1% -> 1% of each run, Pallas kernels for 15% -> 15%
where the time goes in v13:
time: 77.9 us; the launch traced here: 77.7 us
  starting transfers between devices  27.2 us (35%)
  waiting for transfers between devices  26 us (33%)
  Pallas kernels  23.4 us (30%)
    ppermute x18, waiting for transfers between devices, swap(): return lax.ppermute(value, axis, [(i, i ^ bit) for i in range(size)])  20.7 us
    ppermute x18, starting transfers between devices, swap(): return lax.ppermute(value, axis, [(i, i ^ bit) for i in range(size)])  19.7 us
    pallas_call x3, Pallas kernels, products(): pl.pallas_call(functools.partial(kernel, plan, grams), in_specs=[TABLE, *...  10.7 us
    pallas_call x1, Pallas kernels, tall_partial(): pl.pallas_call(tall_kernel, in_specs=[HBM, HBM], out_specs=WHOLE, out_sha...  7.27 us
    ppermute x1, starting transfers between devices, body(): tall = tall + lax.ppermute(tall, 'pix', [(0, 2), (2, 0)])  4.88 us
    pallas_call x2, Pallas kernels, finish(): pl.pallas_call(functools.partial(finish_kernel, [piece[1:] for piece in p...  3.4 us
    ppermute x1, waiting for transfers between devices, body(): tall = tall + lax.ppermute(tall, 'pix', [(0, 2), (2, 0)])  2.56 us
    pallas_call x1, Pallas kernels, inverse_factor(): pl.pallas_call(inverse_kernel, grid=(1,), in_specs=[pl.BlockSpec((rank, L...  2.01 us
  transfers between devices with their start and end apart: 21, of which 15 were waited for; matrix products, arithmetic and copies ran while one was open for 1% of the time, Pallas kernels for 15%

profile of v13, /device:TPU:0, one launch (start us, length us, event | category | flops | bytes accessed | tf_op | source)
XLA Modules:
  0.0 77.7 jit_solution(8488083625806465457)
XLA Ops:
  0.0 7.3 %tall_partial.1 = f32[48,512]{1,0:T(8,128)S(1)} custom-call(f32[512,8192]{1,0:T(8,128)} %x_hbm.7, f32[48,8192]{1,0:T(8,128)} %bitcast.17), custom_call_target="tpu_custom_call" | custom-call | flops 1207959552 | bytes 16777216 | tf_op jit(solution)/shard_map/tall_partial/pallas_call | solution.py:91
  7.3 1.3 %collective-permute-start = (f32[48,512]{1,0:T(8,128)S(1)}, f32[48,512]{1,0:T(8,128)S(1)}, u32[]{:S(2)}, u32[]{:S(2)}) collective-permute-start(f32[48,512]{1,0:T(8,128)S(1)} %tall_partial.1), channel_id=1, source_target_pairs={{1,0},{3,2},{5,4},{7,6},{9,8},{11,10},{13,12},{15,14},{17,16},{19,... | collective-permute-start | bytes 294920 | tf_op jit(solution)/shard_map/ppermute | solution.py:342
  8.6 1.9 %collective-permute-done = f32[48,512]{1,0:T(8,128)S(1)} collective-permute-done((f32[48,512]{1,0:T(8,128)S(1)}, f32[48,512]{1,0:T(8,128)S(1)}, u32[]{:S(2)}, u32[]{:S(2)}) %collective-permute-start) | collective-permute-done | bytes 98336 | tf_op jit(solution)/shard_map/ppermute | solution.py:342
  10.5 4.9 %collective-permute-start.1 = (f32[48,512]{1,0:T(8,128)S(1)}, f32[48,512]{1,0:T(8,128)S(1)}, u32[]{:S(2)}, u32[]{:S(2)}) collective-permute-start(f32[48,512]{1,0:T(8,128)S(1)} %add.156), channel_id=1, source_target_pairs={{0,2},{2,0},{4,6},{6,4},{8,10},{10,8},{12,14},{14,12},{16,18},{18,... | collective-permute-start | bytes 294920 | tf_op jit(solution)/shard_map/ppermute | solution.py:343
  15.4 2.6 %collective-permute-done.1 = f32[48,512]{1,0:T(8,128)S(1)} collective-permute-done((f32[48,512]{1,0:T(8,128)S(1)}, f32[48,512]{1,0:T(8,128)S(1)}, u32[]{:S(2)}, u32[]{:S(2)}) %collective-permute-start.1) | collective-permute-done | bytes 98336 | tf_op jit(solution)/shard_map/ppermute | solution.py:343
  18.0 1.3 %collective-permute-start.2 = (f32[48,512]{1,0:T(8,128)S(1)}, f32[48,512]{1,0:T(8,128)S(1)}, u32[]{:S(2)}, u32[]{:S(2)}) collective-permute-start(f32[48,512]{1,0:T(8,128)S(1)} %add.157), channel_id=1, source_target_pairs={{0,1},{2,3},{4,5},{6,7},{8,9},{10,11},{12,13},{14,15},{16,17},{18,... | collective-permute-start | bytes 294920 | tf_op jit(solution)/shard_map/ppermute | solution.py:344
  20.2 3.3 %first_products.1 = (bf16[96,512]{1,0:T(8,128)(2,1)S(1)}, f32[48,128]{1,0:T(8,128)S(1)}, f32[48,1152]{1,0:T(8,128)S(1)}, f32[48,1024]{1,0:T(8,128)S(1)}) custom-call(s32[4]{0:T(128)S(1)} %pad_add_fusion.2.which_ref, f32[48,512]{1,0:T(8,128)S(1)} %broadcast_select_fusion.tall_ref, f32[512,8192]{1,0:T(8,128)} %x_hbm.7), custom_call_target="tpu_custom_call" | custom-call | flops 301989888 | bytes 4194304 | tf_op jit(solution)/shard_map/first_products/pallas_call | solution.py:191
  23.6 2.2 %collective-permute-start.7 = (f32[48,1024]{1,0:T(8,128)S(1)}, f32[48,1024]{1,0:T(8,128)S(1)}, u32[]{:S(2)}, u32[]{:S(2)}) collective-permute-start(f32[48,1024]{1,0:T(8,128)S(1)} %get-tuple-element.29), channel_id=1, source_target_pairs={{0,8},{4,12},{8,0},{12,4},{16,24},{20,28},{24,16},{28,20},{1,9},{5... | collective-permute-start | bytes 589832 | tf_op jit(solution)/shard_map/ppermute | solution.py:329
  25.8 1.5 %collective-permute-start.3 = (f32[48,1152]{1,0:T(8,128)S(1)}, f32[48,1152]{1,0:T(8,128)S(1)}, u32[]{:S(2)}, u32[]{:S(2)}) collective-permute-start(f32[48,1152]{1,0:T(8,128)S(1)} %get-tuple-element.22.after_ref), channel_id=1, source_target_pairs={{0,4},{4,0},{8,12},{12,8},{16,20},{20,16},{24,28},{28,24},{1,5},{5... | collective-permute-start | bytes 663560 | tf_op jit(solution)/shard_map/ppermute | solution.py:329
  27.3 4.3 %rest_products.3 = (f32[48,1152]{1,0:T(8,128)S(1)}, f32[48,1024]{1,0:T(8,128)S(1)}, f32[48,1024]{1,0:T(8,128)S(1)}, f32[48,1024]{1,0:T(8,128)S(1)}) custom-call(s32[8]{0:T(128)S(1)} %stack.98.which_ref, bf16[96,512]{1,0:T(8,128)(2,1)S(1)} %get-tuple-element.20.both_ref, f32[48,128]{1,0:T(8,128)S(1)} %get-tuple-element.21.gram_ref, f32[512,8192]{1,0:T(8,128)} %x_hbm.7, ...), custom_call_target="tpu_custom_call" | custom-call | flops 603979776 | bytes 8388608 | tf_op jit(solution)/shard_map/rest_products/pallas_call | solution.py:191
  32.4 1.9 %collective-permute-start.8 = (f32[48,512]{1,0:T(8,128)S(1)}, f32[48,512]{1,0:T(8,128)S(1)}, u32[]{:S(2)}, u32[]{:S(2)}) collective-permute-start(f32[48,512]{1,0:T(8,128)S(1)} %slice.69), channel_id=1, source_target_pairs={{0,4},{4,0},{8,12},{12,8},{16,20},{20,16},{24,28},{28,24},{1,5},{5... | collective-permute-start | bytes 294920 | tf_op jit(solution)/shard_map/ppermute | solution.py:329
  34.4 1.6 %collective-permute-start.6 = (f32[48,640]{1,0:T(8,128)S(1)}, f32[48,640]{1,0:T(8,128)S(1)}, u32[]{:S(2)}, u32[]{:S(2)}) collective-permute-start(f32[48,640]{1,0:T(8,128)S(1)} %slice.64), channel_id=1, source_target_pairs={{0,8},{4,12},{8,0},{12,4},{16,24},{20,28},{24,16},{28,20},{1,9},{5... | collective-permute-start | bytes 368648 | tf_op jit(solution)/shard_map/ppermute | solution.py:329
  36.1 3.1 %rest_products.2 = (f32[48,1024]{1,0:T(8,128)S(1)}, f32[48,1024]{1,0:T(8,128)S(1)}) custom-call(s32[4]{0:T(128)S(1)} %pad_add_fusion.1.which_ref, bf16[96,512]{1,0:T(8,128)(2,1)S(1)} %get-tuple-element.20.both_ref, f32[48,128]{1,0:T(8,128)S(1)} %get-tuple-element.21.gram_ref, f32[512,8192]{1,0:T(8,128)} %x_hbm.7, f32[48,1152]{1,0:T(8,128)S(1)} %collective-permute-done.3.after_ref), custom_call_target="tpu_custom_call" | custom-call | flops 301989888 | bytes 4194304 | tf_op jit(solution)/shard_map/rest_products/pallas_call | solution.py:191
  41.6 2.7 %collective-permute-start.12 = (f32[48,1152]{1,0:T(8,128)S(1)}, f32[48,1152]{1,0:T(8,128)S(1)}, u32[]{:S(2)}, u32[]{:S(2)}) collective-permute-start(f32[48,1152]{1,0:T(8,128)S(1)} %pad_maximum_fusion), channel_id=1, source_target_pairs={{0,16},{4,20},{8,24},{12,28},{16,0},{20,4},{24,8},{28,12},{1,17},{... | collective-permute-start | bytes 663560 | tf_op jit(solution)/shard_map/ppermute | solution.py:329
  44.4 1.5 %collective-permute-start.10 = (f32[48,512]{1,0:T(8,128)S(1)}, f32[48,512]{1,0:T(8,128)S(1)}, u32[]{:S(2)}, u32[]{:S(2)}) collective-permute-start(f32[48,512]{1,0:T(8,128)S(1)} %slice.62), channel_id=1, source_target_pairs={{0,4},{4,0},{8,12},{12,8},{16,20},{20,16},{24,28},{28,24},{1,5},{5... | collective-permute-start | bytes 294920 | tf_op jit(solution)/shard_map/ppermute | solution.py:329
  46.7 2.2 %collective-permute-done.10 = f32[48,512]{1,0:T(8,128)S(1)} collective-permute-done((f32[48,512]{1,0:T(8,128)S(1)}, f32[48,512]{1,0:T(8,128)S(1)}, u32[]{:S(2)}, u32[]{:S(2)}) %collective-permute-start.10) | collective-permute-done | bytes 98336 | tf_op jit(solution)/shard_map/ppermute | solution.py:329
  49.7 9.5 %collective-permute-done.12 = f32[48,1152]{1,0:T(8,128)S(1)} collective-permute-done((f32[48,1152]{1,0:T(8,128)S(1)}, f32[48,1152]{1,0:T(8,128)S(1)}, u32[]{:S(2)}, u32[]{:S(2)}) %collective-permute-start.12) | collective-permute-done | bytes 221216 | tf_op jit(solution)/shard_map/ppermute | solution.py:329
  59.3 1.2 %collective-permute-start.18 = (f32[48,512]{1,0:T(8,128)S(1)}, f32[48,512]{1,0:T(8,128)S(1)}, u32[]{:S(2)}, u32[]{:S(2)}) collective-permute-start(f32[48,512]{1,0:T(8,128)S(1)} %get-tuple-element.35), channel_id=1, source_target_pairs={{0,4},{4,0},{8,12},{12,8},{16,20},{20,16},{24,28},{28,24},{1,5},{5... | collective-permute-start | bytes 294920 | tf_op jit(solution)/shard_map/ppermute | solution.py:329
  60.8 2.0 %inverse_factor.1.inverse_ref = f32[48,48]{1,0:T(8,128)S(1)} custom-call(f32[48,1152]{1,0:T(8,128)S(1)} %fusion.1.gram_ref.refs_0_), custom_call_target="tpu_custom_call" | custom-call | flops 20000000 | bytes 49152 | tf_op jit(solution)/shard_map/inverse_factor/pallas_call | solution.py:266
  62.8 1.8 %collective-permute-start.13 = (f32[48,512]{1,0:T(8,128)S(1)}, f32[48,512]{1,0:T(8,128)S(1)}, u32[]{:S(2)}, u32[]{:S(2)}) collective-permute-start(f32[48,512]{1,0:T(8,128)S(1)} %get-tuple-element.33), channel_id=1, source_target_pairs={{0,8},{4,12},{8,0},{12,4},{16,24},{20,28},{24,16},{28,20},{1,9},{5... | collective-permute-start | bytes 294920 | tf_op jit(solution)/shard_map/ppermute | solution.py:329
  67.1 3.2 %collective-permute-done.15.refs_7_ = f32[48,512]{1,0:T(8,128)S(1)} collective-permute-done((f32[48,512]{1,0:T(8,128)S(1)}, f32[48,512]{1,0:T(8,128)S(1)}, u32[]{:S(2)}, u32[]{:S(2)}) %collective-permute-start.15) | collective-permute-done | bytes 98336 | tf_op jit(solution)/shard_map/ppermute | solution.py:329
  71.4 2.0 %collective-permute-done.19.refs_3_ = f32[48,1024]{1,0:T(8,128)S(1)} collective-permute-done((f32[48,1024]{1,0:T(8,128)S(1)}, f32[48,1024]{1,0:T(8,128)S(1)}, u32[]{:S(2)}, u32[]{:S(2)}) %collective-permute-start.19) | collective-permute-done | bytes 196640 | tf_op jit(solution)/shard_map/ppermute | solution.py:329
  73.7 1.9 %finish.2.refs_2_ = f32[48,8192]{1,0:T(8,128)} custom-call(s32[12]{0:T(128)S(1)} %stack.99.where_ref, f32[48,48]{1,0:T(8,128)S(1)} %inverse_factor.1.inverse_ref, f32[48,1152]{1,0:T(8,128)S(1)} %fusion.1.gram_ref.refs_0_, f32[48,512]{1,0:T(8,128)S(1)} %collective-permute-done.17.refs_1_, f32[48,512]{1,0:T(8,128)S(1)} %collective-permute-done.18.refs_2_, ...), custom_call_target="tpu_custom_call" | custom-call | flops 84934656 | bytes 2359296 | tf_op jit(solution)/shard_map/finish/pallas_call | solution.py:307
  76.2 1.5 %finish.3 = f32[48,8192]{1,0:T(8,128)} custom-call(s32[4]{0:T(128)S(1)} %pad_add_fusion.where_ref, f32[48,48]{1,0:T(8,128)S(1)} %inverse_factor.1.inverse_ref, f32[48,1024]{1,0:T(8,128)S(1)} %collective-permute-done.14.refs_0_, f32[48,1024]{1,0:T(8,128)S(1)} %collective-permute-done.16.refs_1_, f32[48,8192]{1,0:T(8,128)} %finish.2.refs_2_), custom_call_target="tpu_custom_call", output_to_operand_aliasing={{}: (4, {})} | custom-call | flops 28311552 | bytes 786432 | tf_op jit(solution)/shard_map/finish/pallas_call | solution.py:307
  (56 shorter events, 10.7 us)
Async XLA Ops:
  7.3 3.2 %collective-permute-start = (f32[48,512]{1,0:T(8,128)S(1)}, f32[48,512]{1,0:T(8,128)S(1)}, u32[]{:S(2)}, u32[]{:S(2)}) collective-permute-start(f32[48,512]{1,0:T(8,128)S(1)} %tall_partial.1), channel_id=1, source_target_pairs={{1,0},{3,2},{5,4},{7,6},{9,8},{11,10},{13,12},{15,14},{17,16},{19,... | collective-permute-start | bytes 294920 | tf_op jit(solution)/shard_map/ppermute | solution.py:342
  10.5 7.5 %collective-permute-start.1 = (f32[48,512]{1,0:T(8,128)S(1)}, f32[48,512]{1,0:T(8,128)S(1)}, u32[]{:S(2)}, u32[]{:S(2)}) collective-permute-start(f32[48,512]{1,0:T(8,128)S(1)} %add.156), channel_id=1, source_target_pairs={{0,2},{2,0},{4,6},{6,4},{8,10},{10,8},{12,14},{14,12},{16,18},{18,... | collective-permute-start | bytes 294920 | tf_op jit(solution)/shard_map/ppermute | solution.py:343
  18.0 2.2 %collective-permute-start.2 = (f32[48,512]{1,0:T(8,128)S(1)}, f32[48,512]{1,0:T(8,128)S(1)}, u32[]{:S(2)}, u32[]{:S(2)}) collective-permute-start(f32[48,512]{1,0:T(8,128)S(1)} %add.157), channel_id=1, source_target_pairs={{0,1},{2,3},{4,5},{6,7},{8,9},{10,11},{12,13},{14,15},{16,17},{18,... | collective-permute-start | bytes 294920 | tf_op jit(solution)/shard_map/ppermute | solution.py:344
  23.6 8.7 %collective-permute-start.7 = (f32[48,1024]{1,0:T(8,128)S(1)}, f32[48,1024]{1,0:T(8,128)S(1)}, u32[]{:S(2)}, u32[]{:S(2)}) collective-permute-start(f32[48,1024]{1,0:T(8,128)S(1)} %get-tuple-element.29), channel_id=1, source_target_pairs={{0,8},{4,12},{8,0},{12,4},{16,24},{20,28},{24,16},{28,20},{1,9},{5... | collective-permute-start | bytes 589832 | tf_op jit(solution)/shard_map/ppermute | solution.py:329
  25.8 8.6 %collective-permute-start.3 = (f32[48,1152]{1,0:T(8,128)S(1)}, f32[48,1152]{1,0:T(8,128)S(1)}, u32[]{:S(2)}, u32[]{:S(2)}) collective-permute-start(f32[48,1152]{1,0:T(8,128)S(1)} %get-tuple-element.22.after_ref), channel_id=1, source_target_pairs={{0,4},{4,0},{8,12},{12,8},{16,20},{20,16},{24,28},{28,24},{1,5},{5... | collective-permute-start | bytes 663560 | tf_op jit(solution)/shard_map/ppermute | solution.py:329
  31.7 7.7 %collective-permute-start.4 = (f32[48,1024]{1,0:T(8,128)S(1)}, f32[48,1024]{1,0:T(8,128)S(1)}, u32[]{:S(2)}, u32[]{:S(2)}) collective-permute-start(f32[48,1024]{1,0:T(8,128)S(1)} %get-tuple-element.24), channel_id=1, source_target_pairs={{0,4},{4,0},{8,12},{12,8},{16,20},{20,16},{24,28},{28,24},{1,5},{5... | collective-permute-start | bytes 589832 | tf_op jit(solution)/shard_map/ppermute | solution.py:329
  32.3 7.6 %collective-permute-start.5 = (f32[48,1024]{1,0:T(8,128)S(1)}, f32[48,1024]{1,0:T(8,128)S(1)}, u32[]{:S(2)}, u32[]{:S(2)}) collective-permute-start(f32[48,1024]{1,0:T(8,128)S(1)} %get-tuple-element.26), channel_id=1, source_target_pairs={{0,8},{4,12},{8,0},{12,4},{16,24},{20,28},{24,16},{28,20},{1,9},{5... | collective-permute-start | bytes 589832 | tf_op jit(solution)/shard_map/ppermute | solution.py:329
  32.4 8.1 %collective-permute-start.8 = (f32[48,512]{1,0:T(8,128)S(1)}, f32[48,512]{1,0:T(8,128)S(1)}, u32[]{:S(2)}, u32[]{:S(2)}) collective-permute-start(f32[48,512]{1,0:T(8,128)S(1)} %slice.69), channel_id=1, source_target_pairs={{0,4},{4,0},{8,12},{12,8},{16,20},{20,16},{24,28},{28,24},{1,5},{5... | collective-permute-start | bytes 294920 | tf_op jit(solution)/shard_map/ppermute | solution.py:329
  34.4 6.8 %collective-permute-start.6 = (f32[48,640]{1,0:T(8,128)S(1)}, f32[48,640]{1,0:T(8,128)S(1)}, u32[]{:S(2)}, u32[]{:S(2)}) collective-permute-start(f32[48,640]{1,0:T(8,128)S(1)} %slice.64), channel_id=1, source_target_pairs={{0,8},{4,12},{8,0},{12,4},{16,24},{20,28},{24,16},{28,20},{1,9},{5... | collective-permute-start | bytes 368648 | tf_op jit(solution)/shard_map/ppermute | solution.py:329
  41.2 5.5 %collective-permute-start.9 = (f32[48,512]{1,0:T(8,128)S(1)}, f32[48,512]{1,0:T(8,128)S(1)}, u32[]{:S(2)}, u32[]{:S(2)}) collective-permute-start(f32[48,512]{1,0:T(8,128)S(1)} %slice.61), channel_id=1, source_target_pairs={{0,8},{4,12},{8,0},{12,4},{16,24},{20,28},{24,16},{28,20},{1,9},{5... | collective-permute-start | bytes 294920 | tf_op jit(solution)/shard_map/ppermute | solution.py:329
  41.6 17.6 %collective-permute-start.12 = (f32[48,1152]{1,0:T(8,128)S(1)}, f32[48,1152]{1,0:T(8,128)S(1)}, u32[]{:S(2)}, u32[]{:S(2)}) collective-permute-start(f32[48,1152]{1,0:T(8,128)S(1)} %pad_maximum_fusion), channel_id=1, source_target_pairs={{0,16},{4,20},{8,24},{12,28},{16,0},{20,4},{24,8},{28,12},{1,17},{... | collective-permute-start | bytes 663560 | tf_op jit(solution)/shard_map/ppermute | solution.py:329
  44.4 4.6 %collective-permute-start.10 = (f32[48,512]{1,0:T(8,128)S(1)}, f32[48,512]{1,0:T(8,128)S(1)}, u32[]{:S(2)}, u32[]{:S(2)}) collective-permute-start(f32[48,512]{1,0:T(8,128)S(1)} %slice.62), channel_id=1, source_target_pairs={{0,4},{4,0},{8,12},{12,8},{16,20},{20,16},{24,28},{28,24},{1,5},{5... | collective-permute-start | bytes 294920 | tf_op jit(solution)/shard_map/ppermute | solution.py:329
  49.0 13.8 %collective-permute-start.11 = (f32[48,1024]{1,0:T(8,128)S(1)}, f32[48,1024]{1,0:T(8,128)S(1)}, u32[]{:S(2)}, u32[]{:S(2)}) collective-permute-start(f32[48,1024]{1,0:T(8,128)S(1)} %pad_maximum_fusion.1), channel_id=1, source_target_pairs={{0,16},{4,20},{8,24},{12,28},{16,0},{20,4},{24,8},{28,12},{1,17},{... | collective-permute-start | bytes 589832 | tf_op jit(solution)/shard_map/ppermute | solution.py:329
  59.3 7.5 %collective-permute-start.18 = (f32[48,512]{1,0:T(8,128)S(1)}, f32[48,512]{1,0:T(8,128)S(1)}, u32[]{:S(2)}, u32[]{:S(2)}) collective-permute-start(f32[48,512]{1,0:T(8,128)S(1)} %get-tuple-element.35), channel_id=1, source_target_pairs={{0,4},{4,0},{8,12},{12,8},{16,20},{20,16},{24,28},{28,24},{1,5},{5... | collective-permute-start | bytes 294920 | tf_op jit(solution)/shard_map/ppermute | solution.py:329
  60.5 5.1 %collective-permute-start.17 = (f32[48,512]{1,0:T(8,128)S(1)}, f32[48,512]{1,0:T(8,128)S(1)}, u32[]{:S(2)}, u32[]{:S(2)}) collective-permute-start(f32[48,512]{1,0:T(8,128)S(1)} %get-tuple-element.36), channel_id=1, source_target_pairs={{0,8},{4,12},{8,0},{12,4},{16,24},{20,28},{24,16},{28,20},{1,9},{5... | collective-permute-start | bytes 294920 | tf_op jit(solution)/shard_map/ppermute | solution.py:329
  62.8 7.6 %collective-permute-start.13 = (f32[48,512]{1,0:T(8,128)S(1)}, f32[48,512]{1,0:T(8,128)S(1)}, u32[]{:S(2)}, u32[]{:S(2)}) collective-permute-start(f32[48,512]{1,0:T(8,128)S(1)} %get-tuple-element.33), channel_id=1, source_target_pairs={{0,8},{4,12},{8,0},{12,4},{16,24},{20,28},{24,16},{28,20},{1,9},{5... | collective-permute-start | bytes 294920 | tf_op jit(solution)/shard_map/ppermute | solution.py:329
  64.6 5.7 %collective-permute-start.15 = (f32[48,512]{1,0:T(8,128)S(1)}, f32[48,512]{1,0:T(8,128)S(1)}, u32[]{:S(2)}, u32[]{:S(2)}) collective-permute-start(f32[48,512]{1,0:T(8,128)S(1)} %get-tuple-element.34), channel_id=1, source_target_pairs={{0,4},{4,0},{8,12},{12,8},{16,20},{20,16},{24,28},{28,24},{1,5},{5... | collective-permute-start | bytes 294920 | tf_op jit(solution)/shard_map/ppermute | solution.py:329
  65.6 7.8 %collective-permute-start.19 = (f32[48,1024]{1,0:T(8,128)S(1)}, f32[48,1024]{1,0:T(8,128)S(1)}, u32[]{:S(2)}, u32[]{:S(2)}) collective-permute-start(f32[48,1024]{1,0:T(8,128)S(1)} %pad_maximum_fusion.4), channel_id=1, source_target_pairs={{0,4},{4,0},{8,12},{12,8},{16,20},{20,16},{24,28},{28,24},{1,5},{5... | collective-permute-start | bytes 589832 | tf_op jit(solution)/shard_map/ppermute | solution.py:329
  66.8 6.9 %collective-permute-start.20 = (f32[48,1024]{1,0:T(8,128)S(1)}, f32[48,1024]{1,0:T(8,128)S(1)}, u32[]{:S(2)}, u32[]{:S(2)}) collective-permute-start(f32[48,1024]{1,0:T(8,128)S(1)} %pad_maximum_fusion.5), channel_id=1, source_target_pairs={{0,8},{4,12},{8,0},{12,4},{16,24},{20,28},{24,16},{28,20},{1,9},{5... | collective-permute-start | bytes 589832 | tf_op jit(solution)/shard_map/ppermute | solution.py:329
  70.3 5.7 %collective-permute-start.16 = (f32[48,1024]{1,0:T(8,128)S(1)}, f32[48,1024]{1,0:T(8,128)S(1)}, u32[]{:S(2)}, u32[]{:S(2)}) collective-permute-start(f32[48,1024]{1,0:T(8,128)S(1)} %pad_maximum_fusion.3), channel_id=1, source_target_pairs={{0,8},{4,12},{8,0},{12,4},{16,24},{20,28},{24,16},{28,20},{1,9},{5... | collective-permute-start | bytes 589832 | tf_op jit(solution)/shard_map/ppermute | solution.py:329
  70.4 5.7 %collective-permute-start.14 = (f32[48,1024]{1,0:T(8,128)S(1)}, f32[48,1024]{1,0:T(8,128)S(1)}, u32[]{:S(2)}, u32[]{:S(2)}) collective-permute-start(f32[48,1024]{1,0:T(8,128)S(1)} %pad_maximum_fusion.2), channel_id=1, source_target_pairs={{0,4},{4,0},{8,12},{12,8},{16,20},{20,16},{24,28},{28,24},{1,5},{5... | collective-permute-start | bytes 589832 | tf_op jit(solution)/shard_map/ppermute | solution.py:329

commit v14 on v12

--- a/solution.py
+++ b/solution.py
@@ -139,15 +139,18 @@
     outs, (x_buf, sems) = refs[:-2], refs[-2:]
     copies, use = multiply_blocks(both_ref, which_ref, x_hbm, x_buf, sems, plan, outs)
 
+    def whole_tall():
+        odd = which_ref[len(plan)] == 1
+        one, two = one_ref[...], two_ref[...]
+        return jnp.concatenate([jnp.where(odd, two, one), jnp.where(odd, one, two)], axis=1)
+
     def use_first(k):
         if k == 0:
-            tall = one_ref[...] + two_ref[...]
-            head, rest = split(tall)
-            both_ref[...] = jnp.concatenate([head, rest], axis=0)
+            both_ref[...] = jnp.concatenate(split(whole_tall()), axis=0)
         use(k)
 
     stream(copies, use_first)
-    tall = one_ref[...] + two_ref[...]
+    tall = whole_tall()
     r = tall.shape[0]
     head, rest = split(tall)
     tail = (tall - head.astype(F32) - rest.astype(F32)).astype(BF16)
@@ -181,10 +184,10 @@
         if with_gram:
             grams.append((out, sub))
         widths.append(len(blocks) * sub + extra)
-    return unit, plan, grams, widths, jnp.stack(which)
-
-
-def products(kernel, inputs, in_specs, made, probes, outputs, sub, name):
+    return unit, plan, grams, widths, which
+
+
+def products(kernel, inputs, in_specs, made, probes, outputs, sub, name, table=()):
     rows = probes.shape[0]
     rank = inputs[1].shape[0]
     unit, plan, grams, widths, which = layout(outputs, sub)
@@ -205,11 +208,11 @@
             transcendentals=0,
         ),
         name=name,
-    )(which, *inputs)
-
-
-def first_products(one, two, probes, outputs, sub):
-    rank, rows = one.shape
+    )(jnp.stack([*which, *table]), *inputs)
+
+
+def first_products(one, two, odd, probes, outputs, sub):
+    rank, rows = one.shape[0], 2 * one.shape[1]
     made = [
         jax.ShapeDtypeStruct((2 * rank, rows), BF16),
         jax.ShapeDtypeStruct((rank, LANES), F32),
@@ -223,6 +226,7 @@
         outputs,
         sub,
         "first_products",
+        (odd,),
     )
     return both, gram, outs
 
@@ -338,11 +342,18 @@
     width = cols // (8 * CHUNKS)
 
     tall = tall_partial(probes, sketch.T)
-    bit = 1
-    while 2 * bit < n_pix:
-        tall = tall + swap(tall, "pix", n_pix, bit)
-        bit *= 2
-    other = swap(tall, "pix", n_pix, bit)
+    odd = lax.axis_index("pix").astype(jnp.int32) & 1
+    if n_pix == 4:
+        tall = tall + swap(tall, "pix", n_pix, 1)
+        middle = tall.shape[1] // 2
+        half = jnp.where(odd == 1, tall[:, middle:], tall[:, :middle])
+        half = half + swap(half, "pix", n_pix, 2)
+        rest = swap(half, "pix", n_pix, 1)
+    else:
+        tall = lax.psum(tall, "pix")
+        middle = tall.shape[1] // 2
+        half = jnp.where(odd == 1, tall[:, middle:], tall[:, :middle])
+        rest = jnp.where(odd == 1, tall[:, :middle], tall[:, middle:])
 
     def block_a(c, p, q):
         return 8 * c + 2 * (near ^ p) + (far ^ q)
@@ -356,20 +367,21 @@
             ([block_b(c, p, 1), block_b(c, p, 0)], False),
         ]
 
-    both, gram, away = first_products(tall, other, probes, outputs(0, 1), width)
-
-    inverse, after = None, away[0]
+    both, gram, away = first_products(half, rest, odd, probes, outputs(0, 1), width)
+
+    plan = [(c, p) for c in range(CHUNKS) for p in (1, 0) if (c, p) != (0, 1)]
+    rest = rest_products(
+        both, gram, probes, [out for c, p in plan for out in outputs(c, p)], width, away[0]
+    )
+    made = {(0, 1): away}
+    made.update({key: rest[2 * k : 2 * k + 2] for k, key in enumerate(plan)})
+
+    inverse = None
     sources, pieces = [], []
     for c in range(CHUNKS):
         g = LANES if c == 0 else 0
-        last = c == CHUNKS - 1
-        made = rest_products(
-            both, gram, probes, outputs(c, 0) + ([] if last else outputs(c + 1, 1)), width, after
-        )
-        away_a, away_b = away
-        (own_a, own_b), away = made[:2], made[2:]
-        if c > 0:
-            away_a, away_b, sum_a, sum_b = lax.optimization_barrier((away_a, away_b, sum_a, sum_b))
+        away_a, away_b = made[c, 1]
+        own_a, own_b = made[c, 0]
         got_a = over(away_a, 1)
         sum_a = own_a + got_a
         sum_b = own_b + over(away_b, 2)
@@ -386,7 +398,7 @@
             ],
             axis=1,
         )
-        after = total = whole
+        total = whole
         bit = 4
         while bit < n_pos:
             total = total + over(total, bit)

time: 75.8 us -> 76.3 us (level)
  waiting for transfers between devices: 26.4 us -> 32.9 us
  starting transfers between devices: 24.9 us -> 20.4 us
  Pallas kernels: 23.4 us -> 21.8 us
    ppermute x20 -> x21, waiting for transfers between devices: 26.4 us -> 32.9 us  [swap(): return lax.ppermute(value, axis, [(i, i ^ bit) for i in range(size)])]
    ppermute x20 -> x21, starting transfers between devices: 24.9 us -> 20.4 us  [swap(): return lax.ppermute(value, axis, [(i, i ^ bit) for i in range(size)])]
    pallas_call x3 -> x2, Pallas kernels: 10.7 us -> 9.14 us  [products(): pl.pallas_call(functools.partial(kernel, plan, grams), in_specs=[TABLE, *...]
  transfers between devices with their start and end apart: 20 -> 21, of which waited for: 10 -> 14; matrix products, arithmetic and copies ran while one was open for 1% -> 1% of each run, Pallas kernels for 15% -> 13%
where the time goes in v14:
time: 76.3 us; the launch traced here: 76.1 us
  waiting for transfers between devices  32.9 us (43%)
  Pallas kernels  21.8 us (29%)
  starting transfers between devices  20.4 us (27%)
    ppermute x21, waiting for transfers between devices, swap(): return lax.ppermute(value, axis, [(i, i ^ bit) for i in range(size)])  32.9 us
    ppermute x21, starting transfers between devices, swap(): return lax.ppermute(value, axis, [(i, i ^ bit) for i in range(size)])  20.4 us
    pallas_call x2, Pallas kernels, products(): pl.pallas_call(functools.partial(kernel, plan, grams), in_specs=[TABLE, *...  9.14 us
    pallas_call x1, Pallas kernels, tall_partial(): pl.pallas_call(tall_kernel, in_specs=[HBM, HBM], out_specs=WHOLE, out_sha...  7.27 us
    pallas_call x2, Pallas kernels, finish(): pl.pallas_call(functools.partial(finish_kernel, [piece[1:] for piece in p...  3.39 us
    pallas_call x1, Pallas kernels, inverse_factor(): pl.pallas_call(inverse_kernel, grid=(1,), in_specs=[pl.BlockSpec((rank, L...  2.01 us
  transfers between devices with their start and end apart: 21, of which 14 were waited for; matrix products, arithmetic and copies ran while one was open for 1% of the time, Pallas kernels for 13%

profile of v14, /device:TPU:0, one launch (start us, length us, event | category | flops | bytes accessed | tf_op | source)
XLA Modules:
  0.0 76.1 jit_solution(10028205554917221326)
XLA Ops:
  0.0 7.3 %tall_partial.1 = f32[48,512]{1,0:T(8,128)S(1)} custom-call(f32[512,8192]{1,0:T(8,128)} %x_hbm.5, f32[48,8192]{1,0:T(8,128)} %bitcast.18), custom_call_target="tpu_custom_call" | custom-call | flops 1207959552 | bytes 16777216 | tf_op jit(solution)/shard_map/tall_partial/pallas_call | solution.py:91
  7.8 0.9 %collective-permute-done = f32[48,512]{1,0:T(8,128)S(1)} collective-permute-done((f32[48,512]{1,0:T(8,128)S(1)}, f32[48,512]{1,0:T(8,128)S(1)}, u32[]{:S(2)}, u32[]{:S(2)}) %collective-permute-start) | collective-permute-done | bytes 98336 | tf_op jit(solution)/shard_map/ppermute | solution.py:334
  8.8 2.9 %collective-permute-start.1 = (f32[48,256]{1,0:T(8,128)S(1)}, f32[48,256]{1,0:T(8,128)S(1)}, u32[]{:S(2)}, u32[]{:S(2)}) collective-permute-start(f32[48,256]{1,0:T(8,128)S(1)} %slice_select_fusion), channel_id=1, source_target_pairs={{0,2},{1,3},{2,0},{3,1},{4,6},{5,7},{6,4},{7,5},{8,10},{9,11},{10,... | collective-permute-start | bytes 147464 | tf_op jit(solution)/shard_map/ppermute | solution.py:334
  11.7 2.1 %collective-permute-done.1 = f32[48,256]{1,0:T(8,128)S(1)} collective-permute-done((f32[48,256]{1,0:T(8,128)S(1)}, f32[48,256]{1,0:T(8,128)S(1)}, u32[]{:S(2)}, u32[]{:S(2)}) %collective-permute-start.1) | collective-permute-done | bytes 49184 | tf_op jit(solution)/shard_map/ppermute | solution.py:334
  14.0 1.1 %collective-permute-done.2.two_ref = f32[48,256]{1,0:T(8,128)S(1)} collective-permute-done((f32[48,256]{1,0:T(8,128)S(1)}, f32[48,256]{1,0:T(8,128)S(1)}, u32[]{:S(2)}, u32[]{:S(2)}) %collective-permute-start.2) | collective-permute-done | bytes 49184 | tf_op jit(solution)/shard_map/ppermute | solution.py:334
  15.1 3.3 %first_products.1 = (bf16[96,512]{1,0:T(8,128)(2,1)S(1)}, f32[48,128]{1,0:T(8,128)S(1)}, f32[48,1152]{1,0:T(8,128)S(1)}, f32[48,1024]{1,0:T(8,128)S(1)}) custom-call(s32[5]{0:T(128)S(1)} %stack.98.which_ref, f32[48,256]{1,0:T(8,128)S(1)} %fusion.4.one_ref, f32[48,256]{1,0:T(8,128)S(1)} %collective-permute-done.2.two_ref, f32[512,8192]{1,0:T(8,128)} %x_hbm.5), custom_call_target="tpu_custom_call" | custom-call | flops 301989888 | bytes 4194304 | tf_op jit(solution)/shard_map/first_products/pallas_call | solution.py:195
  18.5 2.1 %collective-permute-start.7 = (f32[48,1024]{1,0:T(8,128)S(1)}, f32[48,1024]{1,0:T(8,128)S(1)}, u32[]{:S(2)}, u32[]{:S(2)}) collective-permute-start(f32[48,1024]{1,0:T(8,128)S(1)} %get-tuple-element.29), channel_id=1, source_target_pairs={{0,8},{4,12},{8,0},{12,4},{16,24},{20,28},{24,16},{28,20},{1,9},{5... | collective-permute-start | bytes 589832 | tf_op jit(solution)/shard_map/ppermute | solution.py:334
  20.7 1.6 %collective-permute-start.5 = (f32[48,1152]{1,0:T(8,128)S(1)}, f32[48,1152]{1,0:T(8,128)S(1)}, u32[]{:S(2)}, u32[]{:S(2)}) collective-permute-start(f32[48,1152]{1,0:T(8,128)S(1)} %get-tuple-element.22.after_ref), channel_id=1, source_target_pairs={{0,4},{4,0},{8,12},{12,8},{16,20},{20,16},{24,28},{28,24},{1,5},{5... | collective-permute-start | bytes 663560 | tf_op jit(solution)/shard_map/ppermute | solution.py:334
  22.2 5.8 %rest_products.1 = (f32[48,1152]{1,0:T(8,128)S(1)}, f32[48,1024]{1,0:T(8,128)S(1)}, f32[48,1024]{1,0:T(8,128)S(1)}, f32[48,1024]{1,0:T(8,128)S(1)}, f32[48,1024]{1,0:T(8,128)S(1)}, /*index=5*/f32[48,1024]{1,0:T(8,128)S(1)}) custom-call(s32[12]{0:T(128)S(1)} %stack.92.which_ref, bf16[96,512]{1,0:T(8,128)(2,1)S(1)} %get-tuple-element.20.both_ref, ...), custom_call_target="tpu_custom_call" | custom-call | flops 905969664 | bytes 12582912 | tf_op jit(solution)/shard_map/rest_products/pallas_call | solution.py:195
  28.7 2.0 %collective-permute-start.8 = (f32[48,512]{1,0:T(8,128)S(1)}, f32[48,512]{1,0:T(8,128)S(1)}, u32[]{:S(2)}, u32[]{:S(2)}) collective-permute-start(f32[48,512]{1,0:T(8,128)S(1)} %slice.79), channel_id=1, source_target_pairs={{0,4},{4,0},{8,12},{12,8},{16,20},{20,16},{24,28},{28,24},{1,5},{5... | collective-permute-start | bytes 294920 | tf_op jit(solution)/shard_map/ppermute | solution.py:334
  30.7 4.9 %collective-permute-done.3 = f32[48,1024]{1,0:T(8,128)S(1)} collective-permute-done((f32[48,1024]{1,0:T(8,128)S(1)}, f32[48,1024]{1,0:T(8,128)S(1)}, u32[]{:S(2)}, u32[]{:S(2)}) %collective-permute-start.3) | collective-permute-done | bytes 196640 | tf_op jit(solution)/shard_map/ppermute | solution.py:334
  36.6 7.3 %collective-permute-done.6 = f32[48,640]{1,0:T(8,128)S(1)} collective-permute-done((f32[48,640]{1,0:T(8,128)S(1)}, f32[48,640]{1,0:T(8,128)S(1)}, u32[]{:S(2)}, u32[]{:S(2)}) %collective-permute-start.6) | collective-permute-done | bytes 122912 | tf_op jit(solution)/shard_map/ppermute | solution.py:334
  44.7 4.6 %collective-permute-done.9 = f32[48,512]{1,0:T(8,128)S(1)} collective-permute-done((f32[48,512]{1,0:T(8,128)S(1)}, f32[48,512]{1,0:T(8,128)S(1)}, u32[]{:S(2)}, u32[]{:S(2)}) %collective-permute-start.9) | collective-permute-done | bytes 98336 | tf_op jit(solution)/shard_map/ppermute | solution.py:334
  49.3 1.0 %collective-permute-done.10 = f32[48,512]{1,0:T(8,128)S(1)} collective-permute-done((f32[48,512]{1,0:T(8,128)S(1)}, f32[48,512]{1,0:T(8,128)S(1)}, u32[]{:S(2)}, u32[]{:S(2)}) %collective-permute-start.10) | collective-permute-done | bytes 98336 | tf_op jit(solution)/shard_map/ppermute | solution.py:334
  50.4 1.4 %collective-permute-start.11 = (f32[48,1024]{1,0:T(8,128)S(1)}, f32[48,1024]{1,0:T(8,128)S(1)}, u32[]{:S(2)}, u32[]{:S(2)}) collective-permute-start(f32[48,1024]{1,0:T(8,128)S(1)} %pad_maximum_fusion.1), channel_id=1, source_target_pairs={{0,16},{4,20},{8,24},{12,28},{16,0},{20,4},{24,8},{28,12},{1,17},{... | collective-permute-start | bytes 589832 | tf_op jit(solution)/shard_map/ppermute | solution.py:334
  51.8 7.0 %collective-permute-done.12 = f32[48,1152]{1,0:T(8,128)S(1)} collective-permute-done((f32[48,1152]{1,0:T(8,128)S(1)}, f32[48,1152]{1,0:T(8,128)S(1)}, u32[]{:S(2)}, u32[]{:S(2)}) %collective-permute-start.12) | collective-permute-done | bytes 221216 | tf_op jit(solution)/shard_map/ppermute | solution.py:334
  59.0 2.0 %inverse_factor.1.inverse_ref = f32[48,48]{1,0:T(8,128)S(1)} custom-call(f32[48,1152]{1,0:T(8,128)S(1)} %fusion.1.gram_ref.refs_0_), custom_call_target="tpu_custom_call" | custom-call | flops 20000000 | bytes 49152 | tf_op jit(solution)/shard_map/inverse_factor/pallas_call | solution.py:271
  61.0 2.1 %collective-permute-start.13 = (f32[48,512]{1,0:T(8,128)S(1)}, f32[48,512]{1,0:T(8,128)S(1)}, u32[]{:S(2)}, u32[]{:S(2)}) collective-permute-start(f32[48,512]{1,0:T(8,128)S(1)} %get-tuple-element.33), channel_id=1, source_target_pairs={{0,8},{4,12},{8,0},{12,4},{16,24},{20,28},{24,16},{28,20},{1,9},{5... | collective-permute-start | bytes 294920 | tf_op jit(solution)/shard_map/ppermute | solution.py:334
  63.1 1.9 %collective-permute-start.15 = (f32[48,512]{1,0:T(8,128)S(1)}, f32[48,512]{1,0:T(8,128)S(1)}, u32[]{:S(2)}, u32[]{:S(2)}) collective-permute-start(f32[48,512]{1,0:T(8,128)S(1)} %get-tuple-element.34), channel_id=1, source_target_pairs={{0,4},{4,0},{8,12},{12,8},{16,20},{20,16},{24,28},{28,24},{1,5},{5... | collective-permute-start | bytes 294920 | tf_op jit(solution)/shard_map/ppermute | solution.py:334
  65.1 1.5 %collective-permute-start.19 = (f32[48,1024]{1,0:T(8,128)S(1)}, f32[48,1024]{1,0:T(8,128)S(1)}, u32[]{:S(2)}, u32[]{:S(2)}) collective-permute-start(f32[48,1024]{1,0:T(8,128)S(1)} %pad_maximum_fusion.4), channel_id=1, source_target_pairs={{0,4},{4,0},{8,12},{12,8},{16,20},{20,16},{24,28},{28,24},{1,5},{5... | collective-permute-start | bytes 589832 | tf_op jit(solution)/shard_map/ppermute | solution.py:334
  66.7 2.0 %collective-permute-done.15.refs_7_ = f32[48,512]{1,0:T(8,128)S(1)} collective-permute-done((f32[48,512]{1,0:T(8,128)S(1)}, f32[48,512]{1,0:T(8,128)S(1)}, u32[]{:S(2)}, u32[]{:S(2)}) %collective-permute-start.15) | collective-permute-done | bytes 98336 | tf_op jit(solution)/shard_map/ppermute | solution.py:334
  68.9 2.1 %collective-permute-start.14 = (f32[48,1024]{1,0:T(8,128)S(1)}, f32[48,1024]{1,0:T(8,128)S(1)}, u32[]{:S(2)}, u32[]{:S(2)}) collective-permute-start(f32[48,1024]{1,0:T(8,128)S(1)} %pad_maximum_fusion.2), channel_id=1, source_target_pairs={{0,4},{4,0},{8,12},{12,8},{16,20},{20,16},{24,28},{28,24},{1,5},{5... | collective-permute-start | bytes 589832 | tf_op jit(solution)/shard_map/ppermute | solution.py:334
  72.3 1.9 %finish.2.refs_2_ = f32[48,8192]{1,0:T(8,128)} custom-call(s32[12]{0:T(128)S(1)} %stack.99.where_ref, f32[48,48]{1,0:T(8,128)S(1)} %inverse_factor.1.inverse_ref, f32[48,1152]{1,0:T(8,128)S(1)} %fusion.1.gram_ref.refs_0_, f32[48,512]{1,0:T(8,128)S(1)} %collective-permute-done.17.refs_1_, f32[48,512]{1,0:T(8,128)S(1)} %collective-permute-done.18.refs_2_, ...), custom_call_target="tpu_custom_call" | custom-call | flops 84934656 | bytes 2359296 | tf_op jit(solution)/shard_map/finish/pallas_call | solution.py:312
  74.6 1.5 %finish.3 = f32[48,8192]{1,0:T(8,128)} custom-call(s32[4]{0:T(128)S(1)} %pad_add_fusion.where_ref, f32[48,48]{1,0:T(8,128)S(1)} %inverse_factor.1.inverse_ref, f32[48,1024]{1,0:T(8,128)S(1)} %collective-permute-done.14.refs_0_, f32[48,1024]{1,0:T(8,128)S(1)} %collective-permute-done.16.refs_1_, f32[48,8192]{1,0:T(8,128)} %finish.2.refs_2_), custom_call_target="tpu_custom_call", output_to_operand_aliasing={{}: (4, {})} | custom-call | flops 28311552 | bytes 786432 | tf_op jit(solution)/shard_map/finish/pallas_call | solution.py:312
  (54 shorter events, 5.6 us)
Async XLA Ops:
  7.3 1.5 %collective-permute-start = (f32[48,512]{1,0:T(8,128)S(1)}, f32[48,512]{1,0:T(8,128)S(1)}, u32[]{:S(2)}, u32[]{:S(2)}) collective-permute-start(f32[48,512]{1,0:T(8,128)S(1)} %tall_partial.1), channel_id=1, source_target_pairs={{0,1},{1,0},{2,3},{3,2},{4,5},{5,4},{6,7},{7,6},{8,9},{9,8},{10,11... | collective-permute-start | bytes 294920 | tf_op jit(solution)/shard_map/ppermute | solution.py:334
  8.8 5.0 %collective-permute-start.1 = (f32[48,256]{1,0:T(8,128)S(1)}, f32[48,256]{1,0:T(8,128)S(1)}, u32[]{:S(2)}, u32[]{:S(2)}) collective-permute-start(f32[48,256]{1,0:T(8,128)S(1)} %slice_select_fusion), channel_id=1, source_target_pairs={{0,2},{1,3},{2,0},{3,1},{4,6},{5,7},{6,4},{7,5},{8,10},{9,11},{10,... | collective-permute-start | bytes 147464 | tf_op jit(solution)/shard_map/ppermute | solution.py:334
  13.8 1.3 %collective-permute-start.2 = (f32[48,256]{1,0:T(8,128)S(1)}, f32[48,256]{1,0:T(8,128)S(1)}, u32[]{:S(2)}, u32[]{:S(2)}) collective-permute-start(f32[48,256]{1,0:T(8,128)S(1)} %fusion.4.one_ref), channel_id=1, source_target_pairs={{0,1},{1,0},{2,3},{3,2},{4,5},{5,4},{6,7},{7,6},{8,9},{9,8},{10,11... | collective-permute-start | bytes 147464 | tf_op jit(solution)/shard_map/ppermute | solution.py:334
  18.5 10.2 %collective-permute-start.7 = (f32[48,1024]{1,0:T(8,128)S(1)}, f32[48,1024]{1,0:T(8,128)S(1)}, u32[]{:S(2)}, u32[]{:S(2)}) collective-permute-start(f32[48,1024]{1,0:T(8,128)S(1)} %get-tuple-element.29), channel_id=1, source_target_pairs={{0,8},{4,12},{8,0},{12,4},{16,24},{20,28},{24,16},{28,20},{1,9},{5... | collective-permute-start | bytes 589832 | tf_op jit(solution)/shard_map/ppermute | solution.py:334
  20.7 15.0 %collective-permute-start.5 = (f32[48,1152]{1,0:T(8,128)S(1)}, f32[48,1152]{1,0:T(8,128)S(1)}, u32[]{:S(2)}, u32[]{:S(2)}) collective-permute-start(f32[48,1152]{1,0:T(8,128)S(1)} %get-tuple-element.22.after_ref), channel_id=1, source_target_pairs={{0,4},{4,0},{8,12},{12,8},{16,20},{20,16},{24,28},{28,24},{1,5},{5... | collective-permute-start | bytes 663560 | tf_op jit(solution)/shard_map/ppermute | solution.py:334
  28.0 7.5 %collective-permute-start.3 = (f32[48,1024]{1,0:T(8,128)S(1)}, f32[48,1024]{1,0:T(8,128)S(1)}, u32[]{:S(2)}, u32[]{:S(2)}) collective-permute-start(f32[48,1024]{1,0:T(8,128)S(1)} %get-tuple-element.24), channel_id=1, source_target_pairs={{0,4},{4,0},{8,12},{12,8},{16,20},{20,16},{24,28},{28,24},{1,5},{5... | collective-permute-start | bytes 589832 | tf_op jit(solution)/shard_map/ppermute | solution.py:334
  28.6 7.0 %collective-permute-start.4 = (f32[48,1024]{1,0:T(8,128)S(1)}, f32[48,1024]{1,0:T(8,128)S(1)}, u32[]{:S(2)}, u32[]{:S(2)}) collective-permute-start(f32[48,1024]{1,0:T(8,128)S(1)} %get-tuple-element.26), channel_id=1, source_target_pairs={{0,8},{4,12},{8,0},{12,4},{16,24},{20,28},{24,16},{28,20},{1,9},{5... | collective-permute-start | bytes 589832 | tf_op jit(solution)/shard_map/ppermute | solution.py:334
  28.7 7.9 %collective-permute-start.8 = (f32[48,512]{1,0:T(8,128)S(1)}, f32[48,512]{1,0:T(8,128)S(1)}, u32[]{:S(2)}, u32[]{:S(2)}) collective-permute-start(f32[48,512]{1,0:T(8,128)S(1)} %slice.79), channel_id=1, source_target_pairs={{0,4},{4,0},{8,12},{12,8},{16,20},{20,16},{24,28},{28,24},{1,5},{5... | collective-permute-start | bytes 294920 | tf_op jit(solution)/shard_map/ppermute | solution.py:334
  35.7 8.2 %collective-permute-start.6 = (f32[48,640]{1,0:T(8,128)S(1)}, f32[48,640]{1,0:T(8,128)S(1)}, u32[]{:S(2)}, u32[]{:S(2)}) collective-permute-start(f32[48,640]{1,0:T(8,128)S(1)} %slice.74), channel_id=1, source_target_pairs={{0,8},{4,12},{8,0},{12,4},{16,24},{20,28},{24,16},{28,20},{1,9},{5... | collective-permute-start | bytes 368648 | tf_op jit(solution)/shard_map/ppermute | solution.py:334
  44.0 5.3 %collective-permute-start.9 = (f32[48,512]{1,0:T(8,128)S(1)}, f32[48,512]{1,0:T(8,128)S(1)}, u32[]{:S(2)}, u32[]{:S(2)}) collective-permute-start(f32[48,512]{1,0:T(8,128)S(1)} %slice.71), channel_id=1, source_target_pairs={{0,8},{4,12},{8,0},{12,4},{16,24},{20,28},{24,16},{28,20},{1,9},{5... | collective-permute-start | bytes 294920 | tf_op jit(solution)/shard_map/ppermute | solution.py:334
  44.1 14.7 %collective-permute-start.12 = (f32[48,1152]{1,0:T(8,128)S(1)}, f32[48,1152]{1,0:T(8,128)S(1)}, u32[]{:S(2)}, u32[]{:S(2)}) collective-permute-start(f32[48,1152]{1,0:T(8,128)S(1)} %pad_maximum_fusion), channel_id=1, source_target_pairs={{0,16},{4,20},{8,24},{12,28},{16,0},{20,4},{24,8},{28,12},{1,17},{... | collective-permute-start | bytes 663560 | tf_op jit(solution)/shard_map/ppermute | solution.py:334
  44.7 5.6 %collective-permute-start.10 = (f32[48,512]{1,0:T(8,128)S(1)}, f32[48,512]{1,0:T(8,128)S(1)}, u32[]{:S(2)}, u32[]{:S(2)}) collective-permute-start(f32[48,512]{1,0:T(8,128)S(1)} %slice.72), channel_id=1, source_target_pairs={{0,4},{4,0},{8,12},{12,8},{16,20},{20,16},{24,28},{28,24},{1,5},{5... | collective-permute-start | bytes 294920 | tf_op jit(solution)/shard_map/ppermute | solution.py:334
  50.4 10.6 %collective-permute-start.11 = (f32[48,1024]{1,0:T(8,128)S(1)}, f32[48,1024]{1,0:T(8,128)S(1)}, u32[]{:S(2)}, u32[]{:S(2)}) collective-permute-start(f32[48,1024]{1,0:T(8,128)S(1)} %pad_maximum_fusion.1), channel_id=1, source_target_pairs={{0,16},{4,20},{8,24},{12,28},{16,0},{20,4},{24,8},{28,12},{1,17},{... | collective-permute-start | bytes 589832 | tf_op jit(solution)/shard_map/ppermute | solution.py:334
  58.8 7.8 %collective-permute-start.18 = (f32[48,512]{1,0:T(8,128)S(1)}, f32[48,512]{1,0:T(8,128)S(1)}, u32[]{:S(2)}, u32[]{:S(2)}) collective-permute-start(f32[48,512]{1,0:T(8,128)S(1)} %get-tuple-element.35), channel_id=1, source_target_pairs={{0,4},{4,0},{8,12},{12,8},{16,20},{20,16},{24,28},{28,24},{1,5},{5... | collective-permute-start | bytes 294920 | tf_op jit(solution)/shard_map/ppermute | solution.py:334
  58.9 6.2 %collective-permute-start.17 = (f32[48,512]{1,0:T(8,128)S(1)}, f32[48,512]{1,0:T(8,128)S(1)}, u32[]{:S(2)}, u32[]{:S(2)}) collective-permute-start(f32[48,512]{1,0:T(8,128)S(1)} %get-tuple-element.36), channel_id=1, source_target_pairs={{0,8},{4,12},{8,0},{12,4},{16,24},{20,28},{24,16},{28,20},{1,9},{5... | collective-permute-start | bytes 294920 | tf_op jit(solution)/shard_map/ppermute | solution.py:334
  61.0 7.8 %collective-permute-start.13 = (f32[48,512]{1,0:T(8,128)S(1)}, f32[48,512]{1,0:T(8,128)S(1)}, u32[]{:S(2)}, u32[]{:S(2)}) collective-permute-start(f32[48,512]{1,0:T(8,128)S(1)} %get-tuple-element.33), channel_id=1, source_target_pairs={{0,8},{4,12},{8,0},{12,4},{16,24},{20,28},{24,16},{28,20},{1,9},{5... | collective-permute-start | bytes 294920 | tf_op jit(solution)/shard_map/ppermute | solution.py:334
  63.1 5.6 %collective-permute-start.15 = (f32[48,512]{1,0:T(8,128)S(1)}, f32[48,512]{1,0:T(8,128)S(1)}, u32[]{:S(2)}, u32[]{:S(2)}) collective-permute-start(f32[48,512]{1,0:T(8,128)S(1)} %get-tuple-element.34), channel_id=1, source_target_pairs={{0,4},{4,0},{8,12},{12,8},{16,20},{20,16},{24,28},{28,24},{1,5},{5... | collective-permute-start | bytes 294920 | tf_op jit(solution)/shard_map/ppermute | solution.py:334
  65.1 6.4 %collective-permute-start.19 = (f32[48,1024]{1,0:T(8,128)S(1)}, f32[48,1024]{1,0:T(8,128)S(1)}, u32[]{:S(2)}, u32[]{:S(2)}) collective-permute-start(f32[48,1024]{1,0:T(8,128)S(1)} %pad_maximum_fusion.4), channel_id=1, source_target_pairs={{0,4},{4,0},{8,12},{12,8},{16,20},{20,16},{24,28},{28,24},{1,5},{5... | collective-permute-start | bytes 589832 | tf_op jit(solution)/shard_map/ppermute | solution.py:334
  66.6 5.7 %collective-permute-start.20 = (f32[48,1024]{1,0:T(8,128)S(1)}, f32[48,1024]{1,0:T(8,128)S(1)}, u32[]{:S(2)}, u32[]{:S(2)}) collective-permute-start(f32[48,1024]{1,0:T(8,128)S(1)} %pad_maximum_fusion.5), channel_id=1, source_target_pairs={{0,8},{4,12},{8,0},{12,4},{16,24},{20,28},{24,16},{28,20},{1,9},{5... | collective-permute-start | bytes 589832 | tf_op jit(solution)/shard_map/ppermute | solution.py:334
  68.7 5.7 %collective-permute-start.16 = (f32[48,1024]{1,0:T(8,128)S(1)}, f32[48,1024]{1,0:T(8,128)S(1)}, u32[]{:S(2)}, u32[]{:S(2)}) collective-permute-start(f32[48,1024]{1,0:T(8,128)S(1)} %pad_maximum_fusion.3), channel_id=1, source_target_pairs={{0,8},{4,12},{8,0},{12,4},{16,24},{20,28},{24,16},{28,20},{1,9},{5... | collective-permute-start | bytes 589832 | tf_op jit(solution)/shard_map/ppermute | solution.py:334
  68.9 5.7 %collective-permute-start.14 = (f32[48,1024]{1,0:T(8,128)S(1)}, f32[48,1024]{1,0:T(8,128)S(1)}, u32[]{:S(2)}, u32[]{:S(2)}) collective-permute-start(f32[48,1024]{1,0:T(8,128)S(1)} %pad_maximum_fusion.2), channel_id=1, source_target_pairs={{0,4},{4,0},{8,12},{12,8},{16,20},{20,16},{24,28},{28,24},{1,5},{5... | collective-permute-start | bytes 589832 | tf_op jit(solution)/shard_map/ppermute | solution.py:334

commit v15 on v14

--- a/solution.py
+++ b/solution.py
@@ -135,22 +135,24 @@
     return copies, use
 
 
-def first_kernel(plan, grams, which_ref, one_ref, two_ref, x_hbm, both_ref, gram_ref, *refs):
+def first_kernel(plan, early, grams, table, one_ref, two_ref, x_hbm, both_ref, gram_ref, *refs):
     outs, (x_buf, sems) = refs[:-2], refs[-2:]
-    copies, use = multiply_blocks(both_ref, which_ref, x_hbm, x_buf, sems, plan, outs)
-
-    def whole_tall():
-        odd = which_ref[len(plan)] == 1
-        one, two = one_ref[...], two_ref[...]
-        return jnp.concatenate([jnp.where(odd, two, one), jnp.where(odd, one, two)], axis=1)
+    copies, use = multiply_blocks(both_ref, table, x_hbm, x_buf, sems, plan, outs)
 
     def use_first(k):
         if k == 0:
-            both_ref[...] = jnp.concatenate(split(whole_tall()), axis=0)
+            tall = one_ref[...] + two_ref[...]
+            head, rest = split(tall)
+            both_ref[...] = jnp.concatenate([head, rest], axis=0)
         use(k)
 
-    stream(copies, use_first)
-    tall = whole_tall()
+    stream(copies[:early], use_first)
+
+    @pl.when(table[len(plan)] == 1)
+    def _():
+        stream(copies[early:], lambda k: use(early + k))
+
+    tall = one_ref[...] + two_ref[...]
     r = tall.shape[0]
     head, rest = split(tall)
     tail = (tall - head.astype(F32) - rest.astype(F32)).astype(BF16)
@@ -164,12 +166,21 @@
         outs[out][:, offset : offset + LANES] = gram_ref[...]
 
 
-def rest_kernel(plan, grams, which_ref, both_ref, gram_ref, x_hbm, after_ref, *refs):
-    outs, (x_buf, sems) = refs[:-2], refs[-2:]
-    copies, use = multiply_blocks(both_ref, which_ref, x_hbm, x_buf, sems, plan, outs)
-    stream(copies, use)
-    for out, offset in grams:
-        outs[out][:, offset : offset + LANES] = gram_ref[...]
+def rest_kernel(plan, grams, table, both_ref, gram_ref, x_hbm, *refs):
+    count = len(refs) // 2 - 1
+    outs, (x_buf, sems) = refs[count:-2], refs[-2:]
+    copies, use = multiply_blocks(both_ref, table, x_hbm, x_buf, sems, plan, outs)
+
+    @pl.when(table[len(plan)] == 0)
+    def _():
+        stream(copies, use)
+        for out, offset in grams:
+            outs[out][:, offset : offset + LANES] = gram_ref[...]
+
+    @pl.when(table[len(plan)] == 1)
+    def _():
+        for out_ref, made_ref in zip(outs, refs[:count]):
+            out_ref[...] = made_ref[...]
 
 
 def layout(outputs, sub):
@@ -187,61 +198,59 @@
     return unit, plan, grams, widths, which
 
 
-def products(kernel, inputs, in_specs, made, probes, outputs, sub, name, table=()):
-    rows = probes.shape[0]
-    rank = inputs[1].shape[0]
-    unit, plan, grams, widths, which = layout(outputs, sub)
-    shapes = [*made, *[jax.ShapeDtypeStruct((rank, width), F32) for width in widths]]
+def product_call(kernel, inputs, in_specs, shapes, rows, unit, count, name):
     return pl.pallas_call(
-        functools.partial(kernel, plan, grams),
+        kernel,
         in_specs=[TABLE, *in_specs],
         out_specs=[WHOLE] * len(shapes),
         out_shape=shapes,
         scratch_shapes=[
-            pltpu.VMEM((len(plan), rows, unit), F32),
-            pltpu.SemaphoreType.DMA((len(plan),)),
+            pltpu.VMEM((count, rows, unit), F32),
+            pltpu.SemaphoreType.DMA((count,)),
         ],
         compiler_params=PARAMS,
         cost_estimate=pl.CostEstimate(
-            flops=6 * rows * rank * unit * len(plan),
-            bytes_accessed=4 * rows * unit * len(plan),
+            flops=6 * rows * shapes[-1].shape[0] * unit * count,
+            bytes_accessed=4 * rows * unit * count,
             transcendentals=0,
         ),
         name=name,
-    )(jnp.stack([*which, *table]), *inputs)
-
-
-def first_products(one, two, odd, probes, outputs, sub):
-    rank, rows = one.shape[0], 2 * one.shape[1]
+    )(*inputs)
+
+
+def products(one, two, probes, away, own, sub, late):
+    rank, rows = one.shape
+    unit, plan, grams, widths, which = layout(away + own, sub)
+    early = len(layout(away, sub)[1])
+    chunks = [jax.ShapeDtypeStruct((rank, width), F32) for width in widths]
     made = [
         jax.ShapeDtypeStruct((2 * rank, rows), BF16),
         jax.ShapeDtypeStruct((rank, LANES), F32),
     ]
-    both, gram, *outs = products(
-        first_kernel,
-        [one, two, in_hbm(probes)],
+    x = in_hbm(probes)
+    both, gram, *outs = product_call(
+        functools.partial(first_kernel, plan, early, grams),
+        [jnp.stack([*which, late]), one, two, x],
         [WHOLE, WHOLE, HBM],
-        made,
-        probes,
-        outputs,
-        sub,
+        made + chunks,
+        rows,
+        unit,
+        len(plan),
         "first_products",
-        (odd,),
     )
-    return both, gram, outs
-
-
-def rest_products(both, gram, probes, outputs, sub, after):
-    return products(
-        rest_kernel,
-        [both, gram, in_hbm(probes), after],
-        [WHOLE, WHOLE, HBM, ANYWHERE],
-        [],
-        probes,
-        outputs,
-        sub,
+    away_outs, own_outs = outs[: len(away)], outs[len(away) :]
+    unit, plan, grams, widths, which = layout(own, sub)
+    own_outs = product_call(
+        functools.partial(rest_kernel, plan, grams),
+        [jnp.stack([*which, late]), both, gram, x, *own_outs],
+        [WHOLE, WHOLE, HBM, *[WHOLE] * len(own_outs)],
+        chunks[len(away) :],
+        rows,
+        unit,
+        len(plan),
         "rest_products",
     )
+    return away_outs, own_outs
 
 
 def inverse_kernel(gram_ref, out_ref):
@@ -342,18 +351,11 @@
     width = cols // (8 * CHUNKS)
 
     tall = tall_partial(probes, sketch.T)
-    odd = lax.axis_index("pix").astype(jnp.int32) & 1
-    if n_pix == 4:
-        tall = tall + swap(tall, "pix", n_pix, 1)
-        middle = tall.shape[1] // 2
-        half = jnp.where(odd == 1, tall[:, middle:], tall[:, :middle])
-        half = half + swap(half, "pix", n_pix, 2)
-        rest = swap(half, "pix", n_pix, 1)
-    else:
-        tall = lax.psum(tall, "pix")
-        middle = tall.shape[1] // 2
-        half = jnp.where(odd == 1, tall[:, middle:], tall[:, :middle])
-        rest = jnp.where(odd == 1, tall[:, :middle], tall[:, middle:])
+    bit = 1
+    while 2 * bit < n_pix:
+        tall = tall + swap(tall, "pix", n_pix, bit)
+        bit *= 2
+    other = swap(tall, "pix", n_pix, bit)
 
     def block_a(c, p, q):
         return 8 * c + 2 * (near ^ p) + (far ^ q)
@@ -367,53 +369,65 @@
             ([block_b(c, p, 1), block_b(c, p, 0)], False),
         ]
 
-    both, gram, away = first_products(half, rest, odd, probes, outputs(0, 1), width)
-
+    late = lax.axis_index("pix").astype(jnp.int32) & 1
     plan = [(c, p) for c in range(CHUNKS) for p in (1, 0) if (c, p) != (0, 1)]
-    rest = rest_products(
-        both, gram, probes, [out for c, p in plan for out in outputs(c, p)], width, away[0]
+    away, rest = products(
+        tall, other, probes, outputs(0, 1), [o for c, p in plan for o in outputs(c, p)], width, late
     )
     made = {(0, 1): away}
     made.update({key: rest[2 * k : 2 * k + 2] for k, key in enumerate(plan)})
 
-    inverse = None
-    sources, pieces = [], []
+    def after(value, *others):
+        return lax.optimization_barrier((value, *others))[0]
+
+    whole, total = [], []
     for c in range(CHUNKS):
         g = LANES if c == 0 else 0
         away_a, away_b = made[c, 1]
         own_a, own_b = made[c, 0]
-        got_a = over(away_a, 1)
-        sum_a = own_a + got_a
+        if c > 0:
+            away_a, away_b = after(away_a, sum_a, sum_b), after(away_b, sum_a, sum_b)
+        sum_a = own_a + over(away_a, 1)
         sum_b = own_b + over(away_b, 2)
         send_a, send_b = sum_a[:, : width + g], sum_b[:, :width]
         if c > 0:
-            send_a, send_b, whole = lax.optimization_barrier((send_a, send_b, whole))
+            send_a, send_b = after(send_a, whole[-1]), after(send_b, whole[-1])
         got_a = over(send_a, 2)
         got_b = over(send_b, 1)
-        whole = jnp.concatenate(
-            [
-                sum_a[:, width + g :] + got_a[:, :width],
-                sum_a[:, width : width + g] + got_a[:, width:],
-                sum_b[:, width:] + got_b,
-            ],
-            axis=1,
+        whole.append(
+            jnp.concatenate(
+                [
+                    sum_a[:, width + g :] + got_a[:, :width],
+                    sum_a[:, width : width + g] + got_a[:, width:],
+                    sum_b[:, width:] + got_b,
+                ],
+                axis=1,
+            )
         )
-        total = whole
+        added = whole[-1]
         bit = 4
         while bit < n_pos:
-            total = total + over(total, bit)
+            added = added + over(added, bit)
             bit *= 2
-        if c == 0:
-            inverse = inverse_factor(total, width)
-        mine_a, mine_b = total[:, :width], total[:, width + g :]
+        total.append(added)
+
+    inverse = inverse_factor(total[0], width)
+    sources, pieces = [], []
+    for c in range(CHUNKS):
+        g = LANES if c == 0 else 0
+        mine_a, mine_b = total[c][:, :width], total[c][:, width + g :]
         if c > 0:
-            mine_a, mine_b, inverse = lax.optimization_barrier((mine_a, mine_b, inverse))
+            mine_a, mine_b = after(mine_a, inverse), after(mine_b, inverse)
         next_a = over(mine_a, 2)
         next_b = over(mine_b, 1)
-        last_a = over(jnp.concatenate([mine_a, next_a], axis=1), 1)
-        last_b = over(jnp.concatenate([mine_b, next_b], axis=1), 2)
+        both_a = jnp.concatenate([mine_a, next_a], axis=1)
+        both_b = jnp.concatenate([mine_b, next_b], axis=1)
+        if c + 1 < CHUNKS:
+            both_a, both_b = after(both_a, total[c + 1]), after(both_b, total[c + 1])
+        last_a = over(both_a, 1)
+        last_b = over(both_b, 2)
         k = len(sources)
-        sources += [total, next_a, next_b, last_a, last_b]
+        sources += [total[c], next_a, next_b, last_a, last_b]
         pieces += [
             (block_a(c, 0, 0), k, 0),
             (block_b(c, 0, 0), k, width + g),

time: 76.3 us -> 80.7 us (1.058)
  starting transfers between devices: 20.4 us -> 23.7 us
    ppermute x21 -> x20, starting transfers between devices: 20.4 us -> 23.7 us  [swap(): return lax.ppermute(value, axis, [(i, i ^ bit) for i in range(size)])]
    ppermute x21 -> x20, waiting for transfers between devices: 32.9 us -> 33.5 us  [swap(): return lax.ppermute(value, axis, [(i, i ^ bit) for i in range(size)])]
  transfers between devices with their start and end apart: 21 -> 20, of which waited for: 14 -> 13; matrix products, arithmetic and copies ran while one was open for 1% -> 1% of each run, Pallas kernels for 13% -> 12%
where the time goes in v15:
time: 80.7 us; the launch traced here: 80.5 us
  waiting for transfers between devices  33.5 us (42%)
  starting transfers between devices  23.7 us (29%)
  Pallas kernels  22.2 us (28%)
    ppermute x20, waiting for transfers between devices, swap(): return lax.ppermute(value, axis, [(i, i ^ bit) for i in range(size)])  33.5 us
    ppermute x20, starting transfers between devices, swap(): return lax.ppermute(value, axis, [(i, i ^ bit) for i in range(size)])  23.7 us
    pallas_call x2, Pallas kernels, product_call(): pl.pallas_call(kernel, in_specs=[TABLE, *in_specs], out_specs=[WHOLE] * l...  9.52 us
    pallas_call x1, Pallas kernels, tall_partial(): pl.pallas_call(tall_kernel, in_specs=[HBM, HBM], out_specs=WHOLE, out_sha...  7.28 us
    pallas_call x2, Pallas kernels, finish(): pl.pallas_call(functools.partial(finish_kernel, [piece[1:] for piece in p...  3.4 us
    pallas_call x1, Pallas kernels, inverse_factor(): pl.pallas_call(inverse_kernel, grid=(1,), in_specs=[pl.BlockSpec((rank, L...  2.01 us
  transfers between devices with their start and end apart: 20, of which 13 were waited for; matrix products, arithmetic and copies ran while one was open for 1% of the time, Pallas kernels for 12%

profile of v15, /device:TPU:0, one launch (start us, length us, event | category | flops | bytes accessed | tf_op | source)
XLA Modules:
  0.0 80.5 jit_solution(16114981925484321746)
XLA Ops:
  0.0 7.3 %tall_partial.1 = f32[48,512]{1,0:T(8,128)S(1)} custom-call(f32[512,8192]{1,0:T(8,128)} %x_hbm.5, f32[48,8192]{1,0:T(8,128)} %bitcast.18), custom_call_target="tpu_custom_call" | custom-call | flops 1207959552 | bytes 16777216 | tf_op jit(solution)/shard_map/tall_partial/pallas_call | solution.py:91
  8.8 2.9 %collective-permute-start.1 = (f32[48,512]{1,0:T(8,128)S(1)}, f32[48,512]{1,0:T(8,128)S(1)}, u32[]{:S(2)}, u32[]{:S(2)}) collective-permute-start(f32[48,512]{1,0:T(8,128)S(1)} %add.158.one_ref), channel_id=1, source_target_pairs={{0,2},{1,3},{2,0},{3,1},{4,6},{5,7},{6,4},{7,5},{8,10},{9,11},{10,... | collective-permute-start | bytes 294920 | tf_op jit(solution)/shard_map/ppermute | solution.py:343
  11.8 3.0 %collective-permute-done.1.two_ref = f32[48,512]{1,0:T(8,128)S(1)} collective-permute-done((f32[48,512]{1,0:T(8,128)S(1)}, f32[48,512]{1,0:T(8,128)S(1)}, u32[]{:S(2)}, u32[]{:S(2)}) %collective-permute-start.1) | collective-permute-done | bytes 98336 | tf_op jit(solution)/shard_map/ppermute | solution.py:343
  14.8 3.6 %first_products.1 = (bf16[96,512]{1,0:T(8,128)(2,1)S(1)}, f32[48,128]{1,0:T(8,128)S(1)}, f32[48,1152]{1,0:T(8,128)S(1)}, f32[48,1024]{1,0:T(8,128)S(1)}, f32[48,...) custom-call(s32[17]{0:T(128)S(1)} %stack.111.table, ...), custom_call_target="tpu_custom_call" | custom-call | flops 1207959552 | bytes 16777216 | tf_op jit(solution)/shard_map/first_products/pallas_call | solution.py:202
  18.4 1.9 %collective-permute-start.4 = (f32[48,1024]{1,0:T(8,128)S(1)}, f32[48,1024]{1,0:T(8,128)S(1)}, u32[]{:S(2)}, u32[]{:S(2)}) collective-permute-start(f32[48,1024]{1,0:T(8,128)S(1)} %get-tuple-element.40), channel_id=1, source_target_pairs={{0,8},{4,12},{8,0},{12,4},{16,24},{20,28},{24,16},{28,20},{1,9},{5... | collective-permute-start | bytes 589832 | tf_op jit(solution)/shard_map/ppermute | solution.py:343
  21.8 5.9 %rest_products.1 = (f32[48,1152]{1,0:T(8,128)S(1)}, f32[48,1024]{1,0:T(8,128)S(1)}, f32[48,1024]{1,0:T(8,128)S(1)}, f32[48,1024]{1,0:T(8,128)S(1)}, f32[48,1024]{1,0:T(8,128)S(1)}, /*index=5*/f32[48,1024]{1,0:T(8,128)S(1)}) custom-call(s32[13]{0:T(128)S(1)} %stack.106.table, bf16[96,512]{1,0:T(8,128)(2,1)S(1)} %get-tuple-element.29.both_ref, ...), custom_call_target="tpu_custom_call" | custom-call | flops 905969664 | bytes 12582912 | tf_op jit(solution)/shard_map/rest_products/pallas_call | solution.py:202
  28.8 1.7 %collective-permute-start.7 = (f32[48,1024]{1,0:T(8,128)S(1)}, f32[48,1024]{1,0:T(8,128)S(1)}, u32[]{:S(2)}, u32[]{:S(2)}) collective-permute-start(f32[48,1024]{1,0:T(8,128)S(1)} %get-tuple-element.43), channel_id=1, source_target_pairs={{0,4},{4,0},{8,12},{12,8},{16,20},{20,16},{24,28},{28,24},{1,5},{5... | collective-permute-start | bytes 589832 | tf_op jit(solution)/shard_map/ppermute | solution.py:343
  30.5 1.6 %collective-permute-start.9 = (f32[48,1024]{1,0:T(8,128)S(1)}, f32[48,1024]{1,0:T(8,128)S(1)}, u32[]{:S(2)}, u32[]{:S(2)}) collective-permute-start(f32[48,1024]{1,0:T(8,128)S(1)} %get-tuple-element.47), channel_id=1, source_target_pairs={{0,8},{4,12},{8,0},{12,4},{16,24},{20,28},{24,16},{28,20},{1,9},{5... | collective-permute-start | bytes 589832 | tf_op jit(solution)/shard_map/ppermute | solution.py:343
  32.6 2.2 %collective-permute-done.3 = f32[48,640]{1,0:T(8,128)S(1)} collective-permute-done((f32[48,640]{1,0:T(8,128)S(1)}, f32[48,640]{1,0:T(8,128)S(1)}, u32[]{:S(2)}, u32[]{:S(2)}) %collective-permute-start.3) | collective-permute-done | bytes 122912 | tf_op jit(solution)/shard_map/ppermute | solution.py:343
  34.8 4.0 %collective-permute-done.9 = f32[48,1024]{1,0:T(8,128)S(1)} collective-permute-done((f32[48,1024]{1,0:T(8,128)S(1)}, f32[48,1024]{1,0:T(8,128)S(1)}, u32[]{:S(2)}, u32[]{:S(2)}) %collective-permute-start.9) | collective-permute-done | bytes 196640 | tf_op jit(solution)/shard_map/ppermute | solution.py:343
  38.8 1.6 %collective-permute-start.10 = (f32[48,512]{1,0:T(8,128)S(1)}, f32[48,512]{1,0:T(8,128)S(1)}, u32[]{:S(2)}, u32[]{:S(2)}) collective-permute-start(f32[48,512]{1,0:T(8,128)S(1)} %slice.70), channel_id=1, source_target_pairs={{0,4},{4,0},{8,12},{12,8},{16,20},{20,16},{24,28},{28,24},{1,5},{5... | collective-permute-start | bytes 294920 | tf_op jit(solution)/shard_map/ppermute | solution.py:343
  40.4 2.6 %collective-permute-start.6 = (f32[48,1152]{1,0:T(8,128)S(1)}, f32[48,1152]{1,0:T(8,128)S(1)}, u32[]{:S(2)}, u32[]{:S(2)}) collective-permute-start(f32[48,1152]{1,0:T(8,128)S(1)} %pad_maximum_fusion), channel_id=1, source_target_pairs={{0,16},{4,20},{8,24},{12,28},{16,0},{20,4},{24,8},{28,12},{1,17},{... | collective-permute-start | bytes 663560 | tf_op jit(solution)/shard_map/ppermute | solution.py:343
  43.6 6.1 %collective-permute-done.8 = f32[48,512]{1,0:T(8,128)S(1)} collective-permute-done((f32[48,512]{1,0:T(8,128)S(1)}, f32[48,512]{1,0:T(8,128)S(1)}, u32[]{:S(2)}, u32[]{:S(2)}) %collective-permute-start.8) | collective-permute-done | bytes 98336 | tf_op jit(solution)/shard_map/ppermute | solution.py:343
  49.7 3.2 %collective-permute-done.6 = f32[48,1152]{1,0:T(8,128)S(1)} collective-permute-done((f32[48,1152]{1,0:T(8,128)S(1)}, f32[48,1152]{1,0:T(8,128)S(1)}, u32[]{:S(2)}, u32[]{:S(2)}) %collective-permute-start.6) | collective-permute-done | bytes 221216 | tf_op jit(solution)/shard_map/ppermute | solution.py:343
  53.5 3.2 %collective-permute-start.16 = (f32[48,512]{1,0:T(8,128)S(1)}, f32[48,512]{1,0:T(8,128)S(1)}, u32[]{:S(2)}, u32[]{:S(2)}) collective-permute-start(f32[48,512]{1,0:T(8,128)S(1)} %get-tuple-element.54), channel_id=1, source_target_pairs={{0,8},{4,12},{8,0},{12,4},{16,24},{20,28},{24,16},{28,20},{1,9},{5... | collective-permute-start | bytes 294920 | tf_op jit(solution)/shard_map/ppermute | solution.py:343
  56.7 2.0 %inverse_factor.1.inverse_ref = f32[48,48]{1,0:T(8,128)S(1)} custom-call(f32[48,1152]{1,0:T(8,128)S(1)} %fusion.1.gram_ref.refs_0_), custom_call_target="tpu_custom_call" | custom-call | flops 20000000 | bytes 49152 | tf_op jit(solution)/shard_map/inverse_factor/pallas_call | solution.py:280
  58.7 5.3 %collective-permute-done.11 = f32[48,1024]{1,0:T(8,128)S(1)} collective-permute-done((f32[48,1024]{1,0:T(8,128)S(1)}, f32[48,1024]{1,0:T(8,128)S(1)}, u32[]{:S(2)}, u32[]{:S(2)}) %collective-permute-start.11) | collective-permute-done | bytes 196640 | tf_op jit(solution)/shard_map/ppermute | solution.py:343
  64.1 1.8 %collective-permute-start.14 = (f32[48,512]{1,0:T(8,128)S(1)}, f32[48,512]{1,0:T(8,128)S(1)}, u32[]{:S(2)}, u32[]{:S(2)}) collective-permute-start(f32[48,512]{1,0:T(8,128)S(1)} %get-tuple-element.50), channel_id=1, source_target_pairs={{0,4},{4,0},{8,12},{12,8},{16,20},{20,16},{24,28},{28,24},{1,5},{5... | collective-permute-start | bytes 294920 | tf_op jit(solution)/shard_map/ppermute | solution.py:343
  66.4 1.9 %collective-permute-start.19 = (f32[48,1024]{1,0:T(8,128)S(1)}, f32[48,1024]{1,0:T(8,128)S(1)}, u32[]{:S(2)}, u32[]{:S(2)}) collective-permute-start(f32[48,1024]{1,0:T(8,128)S(1)} %pad_maximum_fusion.5), channel_id=1, source_target_pairs={{0,8},{4,12},{8,0},{12,4},{16,24},{20,28},{24,16},{28,20},{1,9},{5... | collective-permute-start | bytes 589832 | tf_op jit(solution)/shard_map/ppermute | solution.py:343
  69.5 2.2 %collective-permute-done.12.refs_6_ = f32[48,512]{1,0:T(8,128)S(1)} collective-permute-done((f32[48,512]{1,0:T(8,128)S(1)}, f32[48,512]{1,0:T(8,128)S(1)}, u32[]{:S(2)}, u32[]{:S(2)}) %collective-permute-start.12) | collective-permute-done | bytes 98336 | tf_op jit(solution)/shard_map/ppermute | solution.py:343
  71.9 1.9 %collective-permute-done.18.refs_3_ = f32[48,1024]{1,0:T(8,128)S(1)} collective-permute-done((f32[48,1024]{1,0:T(8,128)S(1)}, f32[48,1024]{1,0:T(8,128)S(1)}, u32[]{:S(2)}, u32[]{:S(2)}) %collective-permute-start.18) | collective-permute-done | bytes 196640 | tf_op jit(solution)/shard_map/ppermute | solution.py:343
  73.9 2.0 %collective-permute-done.19.refs_4_ = f32[48,1024]{1,0:T(8,128)S(1)} collective-permute-done((f32[48,1024]{1,0:T(8,128)S(1)}, f32[48,1024]{1,0:T(8,128)S(1)}, u32[]{:S(2)}, u32[]{:S(2)}) %collective-permute-start.19) | collective-permute-done | bytes 196640 | tf_op jit(solution)/shard_map/ppermute | solution.py:343
  75.9 1.9 %finish.2.refs_2_ = f32[48,8192]{1,0:T(8,128)} custom-call(s32[12]{0:T(128)S(1)} %stack.112.where_ref, f32[48,48]{1,0:T(8,128)S(1)} %inverse_factor.1.inverse_ref, f32[48,1152]{1,0:T(8,128)S(1)} %fusion.1.gram_ref.refs_0_, f32[48,512]{1,0:T(8,128)S(1)} %collective-permute-done.16.refs_1_, f32[48,512]{1,0:T(8,128)S(1)} %collective-permute-done.17.refs_2_, ...), custom_call_target="tpu_custom_call" | custom-call | flops 84934656 | bytes 2359296 | tf_op jit(solution)/shard_map/finish/pallas_call | solution.py:321
  78.8 1.5 %finish.3 = f32[48,8192]{1,0:T(8,128)} custom-call(s32[4]{0:T(128)S(1)} %pad_add_fusion.where_ref, f32[48,48]{1,0:T(8,128)S(1)} %inverse_factor.1.inverse_ref, f32[48,1024]{1,0:T(8,128)S(1)} %collective-permute-done.13.refs_0_, f32[48,1024]{1,0:T(8,128)S(1)} %collective-permute-done.15.refs_1_, f32[48,8192]{1,0:T(8,128)} %finish.2.refs_2_), custom_call_target="tpu_custom_call", output_to_operand_aliasing={{}: (4, {})} | custom-call | flops 28311552 | bytes 786432 | tf_op jit(solution)/shard_map/finish/pallas_call | solution.py:321
  (50 shorter events, 8.9 us)
Async XLA Ops:
  7.3 1.5 %collective-permute-start = (f32[48,512]{1,0:T(8,128)S(1)}, f32[48,512]{1,0:T(8,128)S(1)}, u32[]{:S(2)}, u32[]{:S(2)}) collective-permute-start(f32[48,512]{1,0:T(8,128)S(1)} %tall_partial.1), channel_id=1, source_target_pairs={{0,1},{1,0},{2,3},{3,2},{4,5},{5,4},{6,7},{7,6},{8,9},{9,8},{10,11... | collective-permute-start | bytes 294920 | tf_op jit(solution)/shard_map/ppermute | solution.py:343
  8.8 6.1 %collective-permute-start.1 = (f32[48,512]{1,0:T(8,128)S(1)}, f32[48,512]{1,0:T(8,128)S(1)}, u32[]{:S(2)}, u32[]{:S(2)}) collective-permute-start(f32[48,512]{1,0:T(8,128)S(1)} %add.158.one_ref), channel_id=1, source_target_pairs={{0,2},{1,3},{2,0},{3,1},{4,6},{5,7},{6,4},{7,5},{8,10},{9,11},{10,... | collective-permute-start | bytes 294920 | tf_op jit(solution)/shard_map/ppermute | solution.py:343
  18.4 9.4 %collective-permute-start.4 = (f32[48,1024]{1,0:T(8,128)S(1)}, f32[48,1024]{1,0:T(8,128)S(1)}, u32[]{:S(2)}, u32[]{:S(2)}) collective-permute-start(f32[48,1024]{1,0:T(8,128)S(1)} %get-tuple-element.40), channel_id=1, source_target_pairs={{0,8},{4,12},{8,0},{12,4},{16,24},{20,28},{24,16},{28,20},{1,9},{5... | collective-permute-start | bytes 589832 | tf_op jit(solution)/shard_map/ppermute | solution.py:343
  20.3 8.2 %collective-permute-start.2 = (f32[48,1152]{1,0:T(8,128)S(1)}, f32[48,1152]{1,0:T(8,128)S(1)}, u32[]{:S(2)}, u32[]{:S(2)}) collective-permute-start(f32[48,1152]{1,0:T(8,128)S(1)} %get-tuple-element.38), channel_id=1, source_target_pairs={{0,4},{4,0},{8,12},{12,8},{16,20},{20,16},{24,28},{28,24},{1,5},{5... | collective-permute-start | bytes 663560 | tf_op jit(solution)/shard_map/ppermute | solution.py:343
  27.9 4.7 %collective-permute-start.5 = (f32[48,512]{1,0:T(8,128)S(1)}, f32[48,512]{1,0:T(8,128)S(1)}, u32[]{:S(2)}, u32[]{:S(2)}) collective-permute-start(f32[48,512]{1,0:T(8,128)S(1)} %slice.66), channel_id=1, source_target_pairs={{0,4},{4,0},{8,12},{12,8},{16,20},{20,16},{24,28},{28,24},{1,5},{5... | collective-permute-start | bytes 294920 | tf_op jit(solution)/shard_map/ppermute | solution.py:343
  28.5 6.3 %collective-permute-start.3 = (f32[48,640]{1,0:T(8,128)S(1)}, f32[48,640]{1,0:T(8,128)S(1)}, u32[]{:S(2)}, u32[]{:S(2)}) collective-permute-start(f32[48,640]{1,0:T(8,128)S(1)} %slice.61), channel_id=1, source_target_pairs={{0,8},{4,12},{8,0},{12,4},{16,24},{20,28},{24,16},{28,20},{1,9},{5... | collective-permute-start | bytes 368648 | tf_op jit(solution)/shard_map/ppermute | solution.py:343
  28.8 14.2 %collective-permute-start.7 = (f32[48,1024]{1,0:T(8,128)S(1)}, f32[48,1024]{1,0:T(8,128)S(1)}, u32[]{:S(2)}, u32[]{:S(2)}) collective-permute-start(f32[48,1024]{1,0:T(8,128)S(1)} %get-tuple-element.43), channel_id=1, source_target_pairs={{0,4},{4,0},{8,12},{12,8},{16,20},{20,16},{24,28},{28,24},{1,5},{5... | collective-permute-start | bytes 589832 | tf_op jit(solution)/shard_map/ppermute | solution.py:343
  30.5 8.3 %collective-permute-start.9 = (f32[48,1024]{1,0:T(8,128)S(1)}, f32[48,1024]{1,0:T(8,128)S(1)}, u32[]{:S(2)}, u32[]{:S(2)}) collective-permute-start(f32[48,1024]{1,0:T(8,128)S(1)} %get-tuple-element.47), channel_id=1, source_target_pairs={{0,8},{4,12},{8,0},{12,4},{16,24},{20,28},{24,16},{28,20},{1,9},{5... | collective-permute-start | bytes 589832 | tf_op jit(solution)/shard_map/ppermute | solution.py:343
  38.8 4.7 %collective-permute-start.10 = (f32[48,512]{1,0:T(8,128)S(1)}, f32[48,512]{1,0:T(8,128)S(1)}, u32[]{:S(2)}, u32[]{:S(2)}) collective-permute-start(f32[48,512]{1,0:T(8,128)S(1)} %slice.70), channel_id=1, source_target_pairs={{0,4},{4,0},{8,12},{12,8},{16,20},{20,16},{24,28},{28,24},{1,5},{5... | collective-permute-start | bytes 294920 | tf_op jit(solution)/shard_map/ppermute | solution.py:343
  40.4 12.5 %collective-permute-start.6 = (f32[48,1152]{1,0:T(8,128)S(1)}, f32[48,1152]{1,0:T(8,128)S(1)}, u32[]{:S(2)}, u32[]{:S(2)}) collective-permute-start(f32[48,1152]{1,0:T(8,128)S(1)} %pad_maximum_fusion), channel_id=1, source_target_pairs={{0,16},{4,20},{8,24},{12,28},{16,0},{20,4},{24,8},{28,12},{1,17},{... | collective-permute-start | bytes 663560 | tf_op jit(solution)/shard_map/ppermute | solution.py:343
  43.0 6.6 %collective-permute-start.8 = (f32[48,512]{1,0:T(8,128)S(1)}, f32[48,512]{1,0:T(8,128)S(1)}, u32[]{:S(2)}, u32[]{:S(2)}) collective-permute-start(f32[48,512]{1,0:T(8,128)S(1)} %slice.68), channel_id=1, source_target_pairs={{0,8},{4,12},{8,0},{12,4},{16,24},{20,28},{24,16},{28,20},{1,9},{5... | collective-permute-start | bytes 294920 | tf_op jit(solution)/shard_map/ppermute | solution.py:343
  53.0 5.8 %collective-permute-start.17 = (f32[48,512]{1,0:T(8,128)S(1)}, f32[48,512]{1,0:T(8,128)S(1)}, u32[]{:S(2)}, u32[]{:S(2)}) collective-permute-start(f32[48,512]{1,0:T(8,128)S(1)} %get-tuple-element.53), channel_id=1, source_target_pairs={{0,4},{4,0},{8,12},{12,8},{16,20},{20,16},{24,28},{28,24},{1,5},{5... | collective-permute-start | bytes 294920 | tf_op jit(solution)/shard_map/ppermute | solution.py:343
  53.4 10.6 %collective-permute-start.11 = (f32[48,1024]{1,0:T(8,128)S(1)}, f32[48,1024]{1,0:T(8,128)S(1)}, u32[]{:S(2)}, u32[]{:S(2)}) collective-permute-start(f32[48,1024]{1,0:T(8,128)S(1)} %pad_maximum_fusion.1), channel_id=1, source_target_pairs={{0,16},{4,20},{8,24},{12,28},{16,0},{20,4},{24,8},{28,12},{1,17},{... | collective-permute-start | bytes 589832 | tf_op jit(solution)/shard_map/ppermute | solution.py:343
  53.5 12.4 %collective-permute-start.16 = (f32[48,512]{1,0:T(8,128)S(1)}, f32[48,512]{1,0:T(8,128)S(1)}, u32[]{:S(2)}, u32[]{:S(2)}) collective-permute-start(f32[48,512]{1,0:T(8,128)S(1)} %get-tuple-element.54), channel_id=1, source_target_pairs={{0,8},{4,12},{8,0},{12,4},{16,24},{20,28},{24,16},{28,20},{1,9},{5... | collective-permute-start | bytes 294920 | tf_op jit(solution)/shard_map/ppermute | solution.py:343
  64.1 5.3 %collective-permute-start.14 = (f32[48,512]{1,0:T(8,128)S(1)}, f32[48,512]{1,0:T(8,128)S(1)}, u32[]{:S(2)}, u32[]{:S(2)}) collective-permute-start(f32[48,512]{1,0:T(8,128)S(1)} %get-tuple-element.50), channel_id=1, source_target_pairs={{0,4},{4,0},{8,12},{12,8},{16,20},{20,16},{24,28},{28,24},{1,5},{5... | collective-permute-start | bytes 294920 | tf_op jit(solution)/shard_map/ppermute | solution.py:343
  65.9 5.8 %collective-permute-start.12 = (f32[48,512]{1,0:T(8,128)S(1)}, f32[48,512]{1,0:T(8,128)S(1)}, u32[]{:S(2)}, u32[]{:S(2)}) collective-permute-start(f32[48,512]{1,0:T(8,128)S(1)} %get-tuple-element.49), channel_id=1, source_target_pairs={{0,8},{4,12},{8,0},{12,4},{16,24},{20,28},{24,16},{28,20},{1,9},{5... | collective-permute-start | bytes 294920 | tf_op jit(solution)/shard_map/ppermute | solution.py:343
  66.0 7.9 %collective-permute-start.18 = (f32[48,1024]{1,0:T(8,128)S(1)}, f32[48,1024]{1,0:T(8,128)S(1)}, u32[]{:S(2)}, u32[]{:S(2)}) collective-permute-start(f32[48,1024]{1,0:T(8,128)S(1)} %pad_maximum_fusion.4), channel_id=1, source_target_pairs={{0,4},{4,0},{8,12},{12,8},{16,20},{20,16},{24,28},{28,24},{1,5},{5... | collective-permute-start | bytes 589832 | tf_op jit(solution)/shard_map/ppermute | solution.py:343
  66.4 9.5 %collective-permute-start.19 = (f32[48,1024]{1,0:T(8,128)S(1)}, f32[48,1024]{1,0:T(8,128)S(1)}, u32[]{:S(2)}, u32[]{:S(2)}) collective-permute-start(f32[48,1024]{1,0:T(8,128)S(1)} %pad_maximum_fusion.5), channel_id=1, source_target_pairs={{0,8},{4,12},{8,0},{12,4},{16,24},{20,28},{24,16},{28,20},{1,9},{5... | collective-permute-start | bytes 589832 | tf_op jit(solution)/shard_map/ppermute | solution.py:343
  69.4 9.4 %collective-permute-start.15 = (f32[48,1024]{1,0:T(8,128)S(1)}, f32[48,1024]{1,0:T(8,128)S(1)}, u32[]{:S(2)}, u32[]{:S(2)}) collective-permute-start(f32[48,1024]{1,0:T(8,128)S(1)} %pad_maximum_fusion.3), channel_id=1, source_target_pairs={{0,8},{4,12},{8,0},{12,4},{16,24},{20,28},{24,16},{28,20},{1,9},{5... | collective-permute-start | bytes 589832 | tf_op jit(solution)/shard_map/ppermute | solution.py:343
  71.7 7.2 %collective-permute-start.13 = (f32[48,1024]{1,0:T(8,128)S(1)}, f32[48,1024]{1,0:T(8,128)S(1)}, u32[]{:S(2)}, u32[]{:S(2)}) collective-permute-start(f32[48,1024]{1,0:T(8,128)S(1)} %pad_maximum_fusion.2), channel_id=1, source_target_pairs={{0,4},{4,0},{8,12},{12,8},{16,20},{20,16},{24,28},{28,24},{1,5},{5... | collective-permute-start | bytes 589832 | tf_op jit(solution)/shard_map/ppermute | solution.py:343

commit v16 on v7

--- a/solution.py
+++ b/solution.py
@@ -47,22 +47,28 @@
         use(k)
 
 
-def tall_kernel(x_hbm, s_hbm, out_ref, x_buf, s_buf, x_sems, s_sem):
+def tall_kernel(x_hbm, s_hbm, out_ref, x_buf, s_buf, head_buf, rest_buf, x_sems, s_sems):
     blocks, _, unit = x_buf.shape
     rank = s_hbm.shape[0]
-    copies = [
-        pltpu.make_async_copy(x_hbm.at[:, pl.ds(k * unit, unit)], x_buf.at[k], x_sems.at[k])
-        for k in range(blocks)
-    ]
-    sketch = pltpu.make_async_copy(s_hbm, s_buf, s_sem)
-    sketch.start()
-
-    def use(k):
-        if k == 0:
-            sketch.wait()
-        s_head, s_rest = split(s_buf[:, k * unit : (k + 1) * unit])
+
+    def copies(k):
+        where = pl.ds(k * unit, unit)
+        return (
+            pltpu.make_async_copy(s_hbm.at[:, where], s_buf.at[k], s_sems.at[k]),
+            pltpu.make_async_copy(x_hbm.at[:, where], x_buf.at[k], x_sems.at[k]),
+        )
+
+    for k in range(blocks):
+        for copy in copies(k):
+            copy.start()
+    for k in range(blocks):
+        for copy in copies(k):
+            copy.wait()
+        s_head, s_rest = split(s_buf[k])
         s_both = jnp.concatenate([s_head, s_rest], axis=0)
         x_head, x_rest = split(x_buf[k])
+        head_buf[k] = x_head
+        rest_buf[k] = x_rest
         both = dot(s_both, x_head, LAST)
         part = both[:rank] + (both[rank:] + dot(s_head, x_rest, LAST))
         if k == 0:
@@ -70,13 +76,11 @@
         else:
             out_ref[...] += part
 
-    stream(copies, use)
-
 
 def tall_partial(probes, sketch_t):
     rows, cols = probes.shape
     rank = sketch_t.shape[0]
-    unit = min(UNIT, cols)
+    unit = min(2 * UNIT, cols)
     blocks = cols // unit
     return pl.pallas_call(
         tall_kernel,
@@ -85,9 +89,11 @@
         out_shape=jax.ShapeDtypeStruct((rank, rows), F32),
         scratch_shapes=[
             pltpu.VMEM((blocks, rows, unit), F32),
-            pltpu.VMEM((rank, cols), F32),
+            pltpu.VMEM((blocks, rank, unit), F32),
+            pltpu.VMEM((blocks, rows, unit), BF16),
+            pltpu.VMEM((blocks, rows, unit), BF16),
             pltpu.SemaphoreType.DMA((blocks,)),
-            pltpu.SemaphoreType.DMA,
+            pltpu.SemaphoreType.DMA((blocks,)),
         ],
         compiler_params=PARAMS,
         cost_estimate=pl.CostEstimate(

time: 72.6 us -> 71.3 us (0.982)
  Pallas kernels: 26.3 us -> 25 us
    pallas_call x1, Pallas kernels: 8.61 us -> 7.27 us  [tall_partial(): pl.pallas_call(tall_kernel, in_specs=[HBM, HBM], out_specs=WHOLE, out_sha...]
where the time goes in v16:
time: 71.3 us; the launch traced here: 71.1 us
  Pallas kernels  25 us (35%)
  starting transfers between devices  24.1 us (34%)
  waiting for transfers between devices  20.9 us (29%)
    ppermute x20, starting transfers between devices, swap(): return lax.ppermute(value, axis, [(i, i ^ bit) for i in range(size)])  24.1 us
    ppermute x20, waiting for transfers between devices, swap(): return lax.ppermute(value, axis, [(i, i ^ bit) for i in range(size)])  20.9 us
    pallas_call x3, Pallas kernels, products(): pl.pallas_call(functools.partial(kernel, plan, grams), in_specs=[TABLE, *...  11 us
    pallas_call x1, Pallas kernels, tall_partial(): pl.pallas_call(tall_kernel, in_specs=[HBM, HBM], out_specs=WHOLE, out_sha...  7.27 us
    pallas_call x3, Pallas kernels, finish(): pl.pallas_call(functools.partial(finish_kernel, [piece[1:] for piece in p...  4.72 us
    pallas_call x1, Pallas kernels, inverse_factor(): pl.pallas_call(inverse_kernel, grid=(1,), in_specs=[pl.BlockSpec((rank, L...  2.01 us
  transfers between devices with their start and end apart: 20, of which 10 were waited for; matrix products, arithmetic and copies ran while one was open for 1% of the time, Pallas kernels for 18%

profile of v16, /device:TPU:0, one launch (start us, length us, event | category | flops | bytes accessed | tf_op | source)
XLA Modules:
  0.0 71.1 jit_solution(10597608025428114490)
XLA Ops:
  0.0 7.3 %tall_partial.1 = f32[48,512]{1,0:T(8,128)S(1)} custom-call(f32[512,8192]{1,0:T(8,128)} %x_hbm.7, f32[48,8192]{1,0:T(8,128)} %bitcast.17), custom_call_target="tpu_custom_call" | custom-call | flops 1207959552 | bytes 16777216 | tf_op jit(solution)/shard_map/tall_partial/pallas_call | solution.py:85
  7.8 0.9 %collective-permute-done = f32[48,512]{1,0:T(8,128)S(1)} collective-permute-done((f32[48,512]{1,0:T(8,128)S(1)}, f32[48,512]{1,0:T(8,128)S(1)}, u32[]{:S(2)}, u32[]{:S(2)}) %collective-permute-start) | collective-permute-done | bytes 98336 | tf_op jit(solution)/shard_map/ppermute | solution.py:321
  8.8 2.9 %collective-permute-start.1 = (f32[48,512]{1,0:T(8,128)S(1)}, f32[48,512]{1,0:T(8,128)S(1)}, u32[]{:S(2)}, u32[]{:S(2)}) collective-permute-start(f32[48,512]{1,0:T(8,128)S(1)} %add.153.one_ref), channel_id=1, source_target_pairs={{0,2},{1,3},{2,0},{3,1},{4,6},{5,7},{6,4},{7,5},{8,10},{9,11},{10,... | collective-permute-start | bytes 294920 | tf_op jit(solution)/shard_map/ppermute | solution.py:321
  11.8 3.0 %collective-permute-done.1.two_ref = f32[48,512]{1,0:T(8,128)S(1)} collective-permute-done((f32[48,512]{1,0:T(8,128)S(1)}, f32[48,512]{1,0:T(8,128)S(1)}, u32[]{:S(2)}, u32[]{:S(2)}) %collective-permute-start.1) | collective-permute-done | bytes 98336 | tf_op jit(solution)/shard_map/ppermute | solution.py:321
  14.8 3.4 %first_products.1 = (bf16[96,512]{1,0:T(8,128)(2,1)S(1)}, f32[48,128]{1,0:T(8,128)S(1)}, f32[48,1152]{1,0:T(8,128)S(1)}, f32[48,1024]{1,0:T(8,128)S(1)}) custom-call(s32[4]{0:T(128)S(1)} %pad_add_fusion.2.which_ref, f32[48,512]{1,0:T(8,128)S(1)} %add.153.one_ref, f32[48,512]{1,0:T(8,128)S(1)} %collective-permute-done.1.two_ref, f32[512,8192]{1,0:T(8,128)} %x_hbm.7), custom_call_target="tpu_custom_call" | custom-call | flops 301989888 | bytes 4194304 | tf_op jit(solution)/shard_map/first_products/pallas_call | solution.py:183
  18.2 1.9 %collective-permute-start.6 = (f32[48,1024]{1,0:T(8,128)S(1)}, f32[48,1024]{1,0:T(8,128)S(1)}, u32[]{:S(2)}, u32[]{:S(2)}) collective-permute-start(f32[48,1024]{1,0:T(8,128)S(1)} %get-tuple-element.29), channel_id=1, source_target_pairs={{0,8},{4,12},{8,0},{12,4},{16,24},{20,28},{24,16},{28,20},{1,9},{5... | collective-permute-start | bytes 589832 | tf_op jit(solution)/shard_map/ppermute | solution.py:321
  20.1 1.5 %collective-permute-start.2 = (f32[48,1152]{1,0:T(8,128)S(1)}, f32[48,1152]{1,0:T(8,128)S(1)}, u32[]{:S(2)}, u32[]{:S(2)}) collective-permute-start(f32[48,1152]{1,0:T(8,128)S(1)} %get-tuple-element.22.after_ref), channel_id=1, source_target_pairs={{0,4},{4,0},{8,12},{12,8},{16,20},{20,16},{24,28},{28,24},{1,5},{5... | collective-permute-start | bytes 663560 | tf_op jit(solution)/shard_map/ppermute | solution.py:321
  21.6 4.6 %rest_products.3 = (f32[48,1152]{1,0:T(8,128)S(1)}, f32[48,1024]{1,0:T(8,128)S(1)}, f32[48,1024]{1,0:T(8,128)S(1)}, f32[48,1024]{1,0:T(8,128)S(1)}) custom-call(s32[8]{0:T(128)S(1)} %stack.101.which_ref, bf16[96,512]{1,0:T(8,128)(2,1)S(1)} %get-tuple-element.20.both_ref, f32[48,128]{1,0:T(8,128)S(1)} %get-tuple-element.21.gram_ref, f32[512,8192]{1,0:T(8,128)} %x_hbm.7, ...), custom_call_target="tpu_custom_call" | custom-call | flops 603979776 | bytes 8388608 | tf_op jit(solution)/shard_map/rest_products/pallas_call | solution.py:183
  27.1 1.8 %collective-permute-start.7 = (f32[48,512]{1,0:T(8,128)S(1)}, f32[48,512]{1,0:T(8,128)S(1)}, u32[]{:S(2)}, u32[]{:S(2)}) collective-permute-start(f32[48,512]{1,0:T(8,128)S(1)} %slice.69), channel_id=1, source_target_pairs={{0,4},{4,0},{8,12},{12,8},{16,20},{20,16},{24,28},{28,24},{1,5},{5... | collective-permute-start | bytes 294920 | tf_op jit(solution)/shard_map/ppermute | solution.py:321
  29.0 1.6 %collective-permute-start.5 = (f32[48,640]{1,0:T(8,128)S(1)}, f32[48,640]{1,0:T(8,128)S(1)}, u32[]{:S(2)}, u32[]{:S(2)}) collective-permute-start(f32[48,640]{1,0:T(8,128)S(1)} %slice.64), channel_id=1, source_target_pairs={{0,8},{4,12},{8,0},{12,4},{16,24},{20,28},{24,16},{28,20},{1,9},{5... | collective-permute-start | bytes 368648 | tf_op jit(solution)/shard_map/ppermute | solution.py:321
  30.6 3.1 %rest_products.2 = (f32[48,1024]{1,0:T(8,128)S(1)}, f32[48,1024]{1,0:T(8,128)S(1)}) custom-call(s32[4]{0:T(128)S(1)} %pad_add_fusion.1.which_ref, bf16[96,512]{1,0:T(8,128)(2,1)S(1)} %get-tuple-element.20.both_ref, f32[48,128]{1,0:T(8,128)S(1)} %get-tuple-element.21.gram_ref, f32[512,8192]{1,0:T(8,128)} %x_hbm.7, f32[48,1152]{1,0:T(8,128)S(1)} %collective-permute-done.2.after_ref), custom_call_target="tpu_custom_call" | custom-call | flops 301989888 | bytes 4194304 | tf_op jit(solution)/shard_map/rest_products/pallas_call | solution.py:183
  34.5 1.3 %collective-permute-start.8 = (f32[48,512]{1,0:T(8,128)S(1)}, f32[48,512]{1,0:T(8,128)S(1)}, u32[]{:S(2)}, u32[]{:S(2)}) collective-permute-start(f32[48,512]{1,0:T(8,128)S(1)} %slice.61), channel_id=1, source_target_pairs={{0,8},{4,12},{8,0},{12,4},{16,24},{20,28},{24,16},{28,20},{1,9},{5... | collective-permute-start | bytes 294920 | tf_op jit(solution)/shard_map/ppermute | solution.py:321
  35.9 2.6 %collective-permute-start.11 = (f32[48,1152]{1,0:T(8,128)S(1)}, f32[48,1152]{1,0:T(8,128)S(1)}, u32[]{:S(2)}, u32[]{:S(2)}) collective-permute-start(f32[48,1152]{1,0:T(8,128)S(1)} %pad_maximum_fusion), channel_id=1, source_target_pairs={{0,16},{4,20},{8,24},{12,28},{16,0},{20,4},{24,8},{28,12},{1,17},{... | collective-permute-start | bytes 663560 | tf_op jit(solution)/shard_map/ppermute | solution.py:321
  39.3 3.8 %collective-permute-done.9 = f32[48,512]{1,0:T(8,128)S(1)} collective-permute-done((f32[48,512]{1,0:T(8,128)S(1)}, f32[48,512]{1,0:T(8,128)S(1)}, u32[]{:S(2)}, u32[]{:S(2)}) %collective-permute-start.9) | collective-permute-done | bytes 98336 | tf_op jit(solution)/shard_map/ppermute | solution.py:321
  43.6 8.5 %collective-permute-done.11 = f32[48,1152]{1,0:T(8,128)S(1)} collective-permute-done((f32[48,1152]{1,0:T(8,128)S(1)}, f32[48,1152]{1,0:T(8,128)S(1)}, u32[]{:S(2)}, u32[]{:S(2)}) %collective-permute-start.11) | collective-permute-done | bytes 221216 | tf_op jit(solution)/shard_map/ppermute | solution.py:321
  53.4 2.0 %inverse_factor.1.inverse_ref = f32[48,48]{1,0:T(8,128)S(1)} custom-call(f32[48,1152]{1,0:T(8,128)S(1)} %fusion.1.gram_ref.refs_0_), custom_call_target="tpu_custom_call" | custom-call | flops 20000000 | bytes 49152 | tf_op jit(solution)/shard_map/inverse_factor/pallas_call | solution.py:258
  55.4 1.4 %collective-permute-start.12 = (f32[48,512]{1,0:T(8,128)S(1)}, f32[48,512]{1,0:T(8,128)S(1)}, u32[]{:S(2)}, u32[]{:S(2)}) collective-permute-start(f32[48,512]{1,0:T(8,128)S(1)} %get-tuple-element.33), channel_id=1, source_target_pairs={{0,8},{4,12},{8,0},{12,4},{16,24},{20,28},{24,16},{28,20},{1,9},{5... | collective-permute-start | bytes 294920 | tf_op jit(solution)/shard_map/ppermute | solution.py:321
  56.8 1.6 %collective-permute-start.14 = (f32[48,512]{1,0:T(8,128)S(1)}, f32[48,512]{1,0:T(8,128)S(1)}, u32[]{:S(2)}, u32[]{:S(2)}) collective-permute-start(f32[48,512]{1,0:T(8,128)S(1)} %get-tuple-element.34), channel_id=1, source_target_pairs={{0,4},{4,0},{8,12},{12,8},{16,20},{20,16},{24,28},{28,24},{1,5},{5... | collective-permute-start | bytes 294920 | tf_op jit(solution)/shard_map/ppermute | solution.py:321
  60.0 2.2 %collective-permute-done.14.refs_2_ = f32[48,512]{1,0:T(8,128)S(1)} collective-permute-done((f32[48,512]{1,0:T(8,128)S(1)}, f32[48,512]{1,0:T(8,128)S(1)}, u32[]{:S(2)}, u32[]{:S(2)}) %collective-permute-start.14) | collective-permute-done | bytes 98336 | tf_op jit(solution)/shard_map/ppermute | solution.py:321
  62.2 1.1 %collective-permute-start.15 = (f32[48,1024]{1,0:T(8,128)S(1)}, f32[48,1024]{1,0:T(8,128)S(1)}, u32[]{:S(2)}, u32[]{:S(2)}) collective-permute-start(f32[48,1024]{1,0:T(8,128)S(1)} %pad_maximum_fusion.3), channel_id=1, source_target_pairs={{0,8},{4,12},{8,0},{12,4},{16,24},{20,28},{24,16},{28,20},{1,9},{5... | collective-permute-start | bytes 589832 | tf_op jit(solution)/shard_map/ppermute | solution.py:321
  63.4 1.3 %collective-permute-start.13 = (f32[48,1024]{1,0:T(8,128)S(1)}, f32[48,1024]{1,0:T(8,128)S(1)}, u32[]{:S(2)}, u32[]{:S(2)}) collective-permute-start(f32[48,1024]{1,0:T(8,128)S(1)} %pad_maximum_fusion.2), channel_id=1, source_target_pairs={{0,4},{4,0},{8,12},{12,8},{16,20},{20,16},{24,28},{28,24},{1,5},{5... | collective-permute-start | bytes 589832 | tf_op jit(solution)/shard_map/ppermute | solution.py:321
  66.4 1.7 %finish.3.refs_3_ = f32[48,8192]{1,0:T(8,128)} custom-call(s32[8]{0:T(128)S(1)} %stack.103.where_ref, f32[48,48]{1,0:T(8,128)S(1)} %inverse_factor.1.inverse_ref, f32[48,1152]{1,0:T(8,128)S(1)} %fusion.1.gram_ref.refs_0_, f32[48,512]{1,0:T(8,128)S(1)} %collective-permute-done.16.refs_1_, f32[48,512]{1,0:T(8,128)S(1)} %collective-permute-done.17.refs_2_, ...), custom_call_target="tpu_custom_call" | custom-call | flops 56623104 | bytes 1572864 | tf_op jit(solution)/shard_map/finish/pallas_call | solution.py:299
  68.1 1.5 %finish.4.refs_2_ = f32[48,8192]{1,0:T(8,128)} custom-call(s32[4]{0:T(128)S(1)} %pad_add_fusion.3.where_ref, f32[48,48]{1,0:T(8,128)S(1)} %inverse_factor.1.inverse_ref, f32[48,1024]{1,0:T(8,128)S(1)} %fusion.refs_0_, f32[48,512]{1,0:T(8,128)S(1)} %collective-permute-done.12.refs_1_, ...), custom_call_target="tpu_custom_call", output_to_operand_aliasing={{}: (5, {})} | custom-call | flops 28311552 | bytes 786432 | tf_op jit(solution)/shard_map/finish/pallas_call | solution.py:299
  69.6 1.5 %finish.5 = f32[48,8192]{1,0:T(8,128)} custom-call(s32[4]{0:T(128)S(1)} %pad_add_fusion.where_ref, f32[48,48]{1,0:T(8,128)S(1)} %inverse_factor.1.inverse_ref, f32[48,1024]{1,0:T(8,128)S(1)} %collective-permute-done.13.refs_0_, f32[48,1024]{1,0:T(8,128)S(1)} %collective-permute-done.15.refs_1_, f32[48,8192]{1,0:T(8,128)} %finish.4.refs_2_), custom_call_target="tpu_custom_call", output_to_operand_aliasing={{}: (4, {})} | custom-call | flops 28311552 | bytes 786432 | tf_op jit(solution)/shard_map/finish/pallas_call | solution.py:299
  (54 shorter events, 8.3 us)
Async XLA Ops:
  7.3 1.5 %collective-permute-start = (f32[48,512]{1,0:T(8,128)S(1)}, f32[48,512]{1,0:T(8,128)S(1)}, u32[]{:S(2)}, u32[]{:S(2)}) collective-permute-start(f32[48,512]{1,0:T(8,128)S(1)} %tall_partial.1), channel_id=1, source_target_pairs={{0,1},{1,0},{2,3},{3,2},{4,5},{5,4},{6,7},{7,6},{8,9},{9,8},{10,11... | collective-permute-start | bytes 294920 | tf_op jit(solution)/shard_map/ppermute | solution.py:321
  8.8 6.0 %collective-permute-start.1 = (f32[48,512]{1,0:T(8,128)S(1)}, f32[48,512]{1,0:T(8,128)S(1)}, u32[]{:S(2)}, u32[]{:S(2)}) collective-permute-start(f32[48,512]{1,0:T(8,128)S(1)} %add.153.one_ref), channel_id=1, source_target_pairs={{0,2},{1,3},{2,0},{3,1},{4,6},{5,7},{6,4},{7,5},{8,10},{9,11},{10,... | collective-permute-start | bytes 294920 | tf_op jit(solution)/shard_map/ppermute | solution.py:321
  18.2 8.9 %collective-permute-start.6 = (f32[48,1024]{1,0:T(8,128)S(1)}, f32[48,1024]{1,0:T(8,128)S(1)}, u32[]{:S(2)}, u32[]{:S(2)}) collective-permute-start(f32[48,1024]{1,0:T(8,128)S(1)} %get-tuple-element.29), channel_id=1, source_target_pairs={{0,8},{4,12},{8,0},{12,4},{16,24},{20,28},{24,16},{28,20},{1,9},{5... | collective-permute-start | bytes 589832 | tf_op jit(solution)/shard_map/ppermute | solution.py:321
  20.1 8.8 %collective-permute-start.2 = (f32[48,1152]{1,0:T(8,128)S(1)}, f32[48,1152]{1,0:T(8,128)S(1)}, u32[]{:S(2)}, u32[]{:S(2)}) collective-permute-start(f32[48,1152]{1,0:T(8,128)S(1)} %get-tuple-element.22.after_ref), channel_id=1, source_target_pairs={{0,4},{4,0},{8,12},{12,8},{16,20},{20,16},{24,28},{28,24},{1,5},{5... | collective-permute-start | bytes 663560 | tf_op jit(solution)/shard_map/ppermute | solution.py:321
  26.2 7.5 %collective-permute-start.4 = (f32[48,1024]{1,0:T(8,128)S(1)}, f32[48,1024]{1,0:T(8,128)S(1)}, u32[]{:S(2)}, u32[]{:S(2)}) collective-permute-start(f32[48,1024]{1,0:T(8,128)S(1)} %get-tuple-element.26), channel_id=1, source_target_pairs={{0,8},{4,12},{8,0},{12,4},{16,24},{20,28},{24,16},{28,20},{1,9},{5... | collective-permute-start | bytes 589832 | tf_op jit(solution)/shard_map/ppermute | solution.py:321
  26.7 7.0 %collective-permute-start.3 = (f32[48,1024]{1,0:T(8,128)S(1)}, f32[48,1024]{1,0:T(8,128)S(1)}, u32[]{:S(2)}, u32[]{:S(2)}) collective-permute-start(f32[48,1024]{1,0:T(8,128)S(1)} %get-tuple-element.24), channel_id=1, source_target_pairs={{0,4},{4,0},{8,12},{12,8},{16,20},{20,16},{24,28},{28,24},{1,5},{5... | collective-permute-start | bytes 589832 | tf_op jit(solution)/shard_map/ppermute | solution.py:321
  27.1 7.0 %collective-permute-start.7 = (f32[48,512]{1,0:T(8,128)S(1)}, f32[48,512]{1,0:T(8,128)S(1)}, u32[]{:S(2)}, u32[]{:S(2)}) collective-permute-start(f32[48,512]{1,0:T(8,128)S(1)} %slice.69), channel_id=1, source_target_pairs={{0,4},{4,0},{8,12},{12,8},{16,20},{20,16},{24,28},{28,24},{1,5},{5... | collective-permute-start | bytes 294920 | tf_op jit(solution)/shard_map/ppermute | solution.py:321
  29.0 5.5 %collective-permute-start.5 = (f32[48,640]{1,0:T(8,128)S(1)}, f32[48,640]{1,0:T(8,128)S(1)}, u32[]{:S(2)}, u32[]{:S(2)}) collective-permute-start(f32[48,640]{1,0:T(8,128)S(1)} %slice.64), channel_id=1, source_target_pairs={{0,8},{4,12},{8,0},{12,4},{16,24},{20,28},{24,16},{28,20},{1,9},{5... | collective-permute-start | bytes 368648 | tf_op jit(solution)/shard_map/ppermute | solution.py:321
  34.5 4.8 %collective-permute-start.8 = (f32[48,512]{1,0:T(8,128)S(1)}, f32[48,512]{1,0:T(8,128)S(1)}, u32[]{:S(2)}, u32[]{:S(2)}) collective-permute-start(f32[48,512]{1,0:T(8,128)S(1)} %slice.61), channel_id=1, source_target_pairs={{0,8},{4,12},{8,0},{12,4},{16,24},{20,28},{24,16},{28,20},{1,9},{5... | collective-permute-start | bytes 294920 | tf_op jit(solution)/shard_map/ppermute | solution.py:321
  35.9 16.2 %collective-permute-start.11 = (f32[48,1152]{1,0:T(8,128)S(1)}, f32[48,1152]{1,0:T(8,128)S(1)}, u32[]{:S(2)}, u32[]{:S(2)}) collective-permute-start(f32[48,1152]{1,0:T(8,128)S(1)} %pad_maximum_fusion), channel_id=1, source_target_pairs={{0,16},{4,20},{8,24},{12,28},{16,0},{20,4},{24,8},{28,12},{1,17},{... | collective-permute-start | bytes 663560 | tf_op jit(solution)/shard_map/ppermute | solution.py:321
  38.5 4.6 %collective-permute-start.9 = (f32[48,512]{1,0:T(8,128)S(1)}, f32[48,512]{1,0:T(8,128)S(1)}, u32[]{:S(2)}, u32[]{:S(2)}) collective-permute-start(f32[48,512]{1,0:T(8,128)S(1)} %slice.62), channel_id=1, source_target_pairs={{0,4},{4,0},{8,12},{12,8},{16,20},{20,16},{24,28},{28,24},{1,5},{5... | collective-permute-start | bytes 294920 | tf_op jit(solution)/shard_map/ppermute | solution.py:321
  43.2 12.2 %collective-permute-start.10 = (f32[48,1024]{1,0:T(8,128)S(1)}, f32[48,1024]{1,0:T(8,128)S(1)}, u32[]{:S(2)}, u32[]{:S(2)}) collective-permute-start(f32[48,1024]{1,0:T(8,128)S(1)} %pad_maximum_fusion.1), channel_id=1, source_target_pairs={{0,16},{4,20},{8,24},{12,28},{16,0},{20,4},{24,8},{28,12},{1,17},{... | collective-permute-start | bytes 589832 | tf_op jit(solution)/shard_map/ppermute | solution.py:321
  52.2 6.3 %collective-permute-start.17 = (f32[48,512]{1,0:T(8,128)S(1)}, f32[48,512]{1,0:T(8,128)S(1)}, u32[]{:S(2)}, u32[]{:S(2)}) collective-permute-start(f32[48,512]{1,0:T(8,128)S(1)} %get-tuple-element.35), channel_id=1, source_target_pairs={{0,4},{4,0},{8,12},{12,8},{16,20},{20,16},{24,28},{28,24},{1,5},{5... | collective-permute-start | bytes 294920 | tf_op jit(solution)/shard_map/ppermute | solution.py:321
  52.7 6.4 %collective-permute-start.16 = (f32[48,512]{1,0:T(8,128)S(1)}, f32[48,512]{1,0:T(8,128)S(1)}, u32[]{:S(2)}, u32[]{:S(2)}) collective-permute-start(f32[48,512]{1,0:T(8,128)S(1)} %get-tuple-element.36), channel_id=1, source_target_pairs={{0,8},{4,12},{8,0},{12,4},{16,24},{20,28},{24,16},{28,20},{1,9},{5... | collective-permute-start | bytes 294920 | tf_op jit(solution)/shard_map/ppermute | solution.py:321
  55.4 7.9 %collective-permute-start.12 = (f32[48,512]{1,0:T(8,128)S(1)}, f32[48,512]{1,0:T(8,128)S(1)}, u32[]{:S(2)}, u32[]{:S(2)}) collective-permute-start(f32[48,512]{1,0:T(8,128)S(1)} %get-tuple-element.33), channel_id=1, source_target_pairs={{0,8},{4,12},{8,0},{12,4},{16,24},{20,28},{24,16},{28,20},{1,9},{5... | collective-permute-start | bytes 294920 | tf_op jit(solution)/shard_map/ppermute | solution.py:321
  56.8 5.4 %collective-permute-start.14 = (f32[48,512]{1,0:T(8,128)S(1)}, f32[48,512]{1,0:T(8,128)S(1)}, u32[]{:S(2)}, u32[]{:S(2)}) collective-permute-start(f32[48,512]{1,0:T(8,128)S(1)} %get-tuple-element.34), channel_id=1, source_target_pairs={{0,4},{4,0},{8,12},{12,8},{16,20},{20,16},{24,28},{28,24},{1,5},{5... | collective-permute-start | bytes 294920 | tf_op jit(solution)/shard_map/ppermute | solution.py:321
  58.4 7.3 %collective-permute-start.19 = (f32[48,1024]{1,0:T(8,128)S(1)}, f32[48,1024]{1,0:T(8,128)S(1)}, u32[]{:S(2)}, u32[]{:S(2)}) collective-permute-start(f32[48,1024]{1,0:T(8,128)S(1)} %pad_maximum_fusion.5), channel_id=1, source_target_pairs={{0,8},{4,12},{8,0},{12,4},{16,24},{20,28},{24,16},{28,20},{1,9},{5... | collective-permute-start | bytes 589832 | tf_op jit(solution)/shard_map/ppermute | solution.py:321
  59.1 7.2 %collective-permute-start.18 = (f32[48,1024]{1,0:T(8,128)S(1)}, f32[48,1024]{1,0:T(8,128)S(1)}, u32[]{:S(2)}, u32[]{:S(2)}) collective-permute-start(f32[48,1024]{1,0:T(8,128)S(1)} %pad_maximum_fusion.4), channel_id=1, source_target_pairs={{0,4},{4,0},{8,12},{12,8},{16,20},{20,16},{24,28},{28,24},{1,5},{5... | collective-permute-start | bytes 589832 | tf_op jit(solution)/shard_map/ppermute | solution.py:321
  62.2 7.4 %collective-permute-start.15 = (f32[48,1024]{1,0:T(8,128)S(1)}, f32[48,1024]{1,0:T(8,128)S(1)}, u32[]{:S(2)}, u32[]{:S(2)}) collective-permute-start(f32[48,1024]{1,0:T(8,128)S(1)} %pad_maximum_fusion.3), channel_id=1, source_target_pairs={{0,8},{4,12},{8,0},{12,4},{16,24},{20,28},{24,16},{28,20},{1,9},{5... | collective-permute-start | bytes 589832 | tf_op jit(solution)/shard_map/ppermute | solution.py:321
  63.4 6.3 %collective-permute-start.13 = (f32[48,1024]{1,0:T(8,128)S(1)}, f32[48,1024]{1,0:T(8,128)S(1)}, u32[]{:S(2)}, u32[]{:S(2)}) collective-permute-start(f32[48,1024]{1,0:T(8,128)S(1)} %pad_maximum_fusion.2), channel_id=1, source_target_pairs={{0,4},{4,0},{8,12},{12,8},{16,20},{20,16},{24,28},{28,24},{1,5},{5... | collective-permute-start | bytes 589832 | tf_op jit(solution)/shard_map/ppermute | solution.py:321

commit v17 on v16

--- a/solution.py
+++ b/solution.py
@@ -12,8 +12,9 @@
 VMEM_LIMIT = 40 * 1024 * 1024
 LANES = 128
 CHUNKS = 2
-AHEAD = 6
-UNIT = 512
+AHEAD = 16
+UNIT = 256
+TILE = 256
 PANEL = 4
 LAST = (((1,), (1,)), ((), ()))
 PLAIN = (((1,), (0,)), ((), ()))
@@ -31,6 +32,11 @@
 
 def dot(a, b, dims):
     return lax.dot_general(a, b, dims, preferred_element_type=F32)
+
+
+def tiles(size):
+    step = min(TILE, size)
+    return [slice(start, start + step) for start in range(0, size, step)]
 
 
 def in_hbm(x):
@@ -80,7 +86,7 @@
 def tall_partial(probes, sketch_t):
     rows, cols = probes.shape
     rank = sketch_t.shape[0]
-    unit = min(2 * UNIT, cols)
+    unit = min(4 * UNIT, cols)
     blocks = cols // unit
     return pl.pallas_call(
         tall_kernel,
@@ -116,12 +122,15 @@
     ]
 
     def use(k):
-        both = both_ref[...]
-        x_head, x_rest = split(x_buf[k])
-        first = dot(both, x_head, PLAIN)
-        second = dot(both[:rank], x_rest, PLAIN)
         out, offset = plan[k]
-        outs[out][:, offset : offset + unit] = first[:rank] + (first[rank:] + second)
+        for cols in tiles(unit):
+            total = None
+            for rows in tiles(x_buf.shape[1]):
+                x_head, x_rest = split(x_buf[k, rows, cols])
+                both = dot(both_ref[:, rows], x_head, PLAIN)
+                part = both[:rank] + (both[rank:] + dot(both_ref[:rank, rows], x_rest, PLAIN))
+                total = part if total is None else total + part
+            outs[out][:, offset + cols.start : offset + cols.stop] = total
 
     return copies, use
 
@@ -321,10 +330,18 @@
         return lax.ppermute(value, axis, [(i, i ^ bit) for i in range(size)])
 
     def over(value, bit):
-        return swap(value, "pos", n_pos, bit)
+        if bit > 2:
+            return swap(value, "pos", n_pos, bit)
+        pairs = [
+            (i * n_pix + j, (i ^ (bit if j % 2 else 3 - bit)) * n_pix + j)
+            for i in range(n_pos)
+            for j in range(n_pix)
+        ]
+        return lax.ppermute(value, ("pos", "pix"), pairs)
 
     me = lax.axis_index("pos").astype(jnp.int32)
-    near, far = me & 1, (me >> 1) & 1
+    odd = lax.axis_index("pix").astype(jnp.int32) & 1
+    near, far = (me >> (1 - odd)) & 1, (me >> odd) & 1
     cols = probes.shape[1]
     width = cols // (8 * CHUNKS)
 

time: 71.3 us -> 73.8 us (1.035)
  Pallas kernels: 25 us -> 27.9 us
  waiting for transfers between devices: 20.9 us -> 19.7 us
  starting transfers between devices: 24.1 us -> 24.9 us
    ppermute x0 -> x16, starting transfers between devices: none -> 18.3 us  [over(): return lax.ppermute(value, ('pos', 'pix'), pairs)]
    ppermute x20 -> x4, starting transfers between devices: 24.1 us -> 6.61 us  [swap(): return lax.ppermute(value, axis, [(i, i ^ bit) for i in range(size)])]
    ppermute x20 -> x4, waiting for transfers between devices: 20.9 us -> 10 us  [swap(): return lax.ppermute(value, axis, [(i, i ^ bit) for i in range(size)])]
    ppermute x0 -> x16, waiting for transfers between devices: none -> 9.66 us  [over(): return lax.ppermute(value, ('pos', 'pix'), pairs)]
    pallas_call x3, Pallas kernels: 11 us -> 13.9 us  [products(): pl.pallas_call(functools.partial(kernel, plan, grams), in_specs=[TABLE, *...]
  transfers between devices with their start and end apart: 20 -> 20, of which waited for: 10 -> 10; matrix products, arithmetic and copies ran while one was open for 1% -> 1% of each run, Pallas kernels for 18% -> 20%
where the time goes in v17:
time: 73.8 us; the launch traced here: 73.7 us
  Pallas kernels  27.9 us (38%)
  starting transfers between devices  24.9 us (34%)
  waiting for transfers between devices  19.7 us (27%)
    ppermute x16, starting transfers between devices, over(): return lax.ppermute(value, ('pos', 'pix'), pairs)  18.3 us
    pallas_call x3, Pallas kernels, products(): pl.pallas_call(functools.partial(kernel, plan, grams), in_specs=[TABLE, *...  13.9 us
    ppermute x4, waiting for transfers between devices, swap(): return lax.ppermute(value, axis, [(i, i ^ bit) for i in range(size)])  10 us
    ppermute x16, waiting for transfers between devices, over(): return lax.ppermute(value, ('pos', 'pix'), pairs)  9.66 us
    pallas_call x1, Pallas kernels, tall_partial(): pl.pallas_call(tall_kernel, in_specs=[HBM, HBM], out_specs=WHOLE, out_sha...  7.27 us
    ppermute x4, starting transfers between devices, swap(): return lax.ppermute(value, axis, [(i, i ^ bit) for i in range(size)])  6.61 us
    pallas_call x3, Pallas kernels, finish(): pl.pallas_call(functools.partial(finish_kernel, [piece[1:] for piece in p...  4.72 us
    pallas_call x1, Pallas kernels, inverse_factor(): pl.pallas_call(inverse_kernel, grid=(1,), in_specs=[pl.BlockSpec((rank, L...  2.01 us
  transfers between devices with their start and end apart: 20, of which 10 were waited for; matrix products, arithmetic and copies ran while one was open for 1% of the time, Pallas kernels for 20%

profile of v17, /device:TPU:0, one launch (start us, length us, event | category | flops | bytes accessed | tf_op | source)
XLA Modules:
  0.0 73.7 jit_solution(5223175646767891654)
XLA Ops:
  0.0 7.3 %tall_partial.1 = f32[48,512]{1,0:T(8,128)S(1)} custom-call(f32[512,8192]{1,0:T(8,128)} %x_hbm.7, f32[48,8192]{1,0:T(8,128)} %bitcast.49), custom_call_target="tpu_custom_call" | custom-call | flops 1207959552 | bytes 16777216 | tf_op jit(solution)/shard_map/tall_partial/pallas_call | solution.py:91
  8.8 2.9 %collective-permute-start.1 = (f32[48,512]{1,0:T(8,128)S(1)}, f32[48,512]{1,0:T(8,128)S(1)}, u32[]{:S(2)}, u32[]{:S(2)}) collective-permute-start(f32[48,512]{1,0:T(8,128)S(1)} %add.209.one_ref), channel_id=1, source_target_pairs={{0,2},{1,3},{2,0},{3,1},{4,6},{5,7},{6,4},{7,5},{8,10},{9,11},{10,... | collective-permute-start | bytes 294920 | tf_op jit(solution)/shard_map/ppermute | solution.py:330
  11.8 3.0 %collective-permute-done.1.two_ref = f32[48,512]{1,0:T(8,128)S(1)} collective-permute-done((f32[48,512]{1,0:T(8,128)S(1)}, f32[48,512]{1,0:T(8,128)S(1)}, u32[]{:S(2)}, u32[]{:S(2)}) %collective-permute-start.1) | collective-permute-done | bytes 98336 | tf_op jit(solution)/shard_map/ppermute | solution.py:330
  14.8 4.1 %first_products.1 = (bf16[96,512]{1,0:T(8,128)(2,1)S(1)}, f32[48,128]{1,0:T(8,128)S(1)}, f32[48,1152]{1,0:T(8,128)S(1)}, f32[48,1024]{1,0:T(8,128)S(1)}) custom-call(s32[8]{0:T(128)S(1)} %stack.184.which_ref, f32[48,512]{1,0:T(8,128)S(1)} %add.209.one_ref, f32[48,512]{1,0:T(8,128)S(1)} %collective-permute-done.1.two_ref, f32[512,8192]{1,0:T(8,128)} %x_hbm.7), custom_call_target="tpu_custom_call" | custom-call | flops 301989888 | bytes 4194304 | tf_op jit(solution)/shard_map/first_products/pallas_call | solution.py:192
  18.9 1.8 %collective-permute-start.6 = (f32[48,1024]{1,0:T(8,128)S(1)}, f32[48,1024]{1,0:T(8,128)S(1)}, u32[]{:S(2)}, u32[]{:S(2)}) collective-permute-start(f32[48,1024]{1,0:T(8,128)S(1)} %get-tuple-element.29), channel_id=1, source_target_pairs={{0,4},{1,9},{2,6},{3,11},{4,0},{5,13},{6,2},{7,15},{8,12},{9,1},{1... | collective-permute-start | bytes 589832 | tf_op jit(solution)/shard_map/ppermute | solution.py:340
  20.8 1.6 %collective-permute-start.2 = (f32[48,1152]{1,0:T(8,128)S(1)}, f32[48,1152]{1,0:T(8,128)S(1)}, u32[]{:S(2)}, u32[]{:S(2)}) collective-permute-start(f32[48,1152]{1,0:T(8,128)S(1)} %get-tuple-element.22.after_ref), channel_id=1, source_target_pairs={{0,8},{1,5},{2,10},{3,7},{4,12},{5,1},{6,14},{7,3},{8,0},{9,13},{1... | collective-permute-start | bytes 663560 | tf_op jit(solution)/shard_map/ppermute | solution.py:340
  22.4 6.0 %rest_products.3 = (f32[48,1152]{1,0:T(8,128)S(1)}, f32[48,1024]{1,0:T(8,128)S(1)}, f32[48,1024]{1,0:T(8,128)S(1)}, f32[48,1024]{1,0:T(8,128)S(1)}) custom-call(s32[16]{0:T(128)S(1)} %stack.201.which_ref, bf16[96,512]{1,0:T(8,128)(2,1)S(1)} %get-tuple-element.20.both_ref, f32[48,128]{1,0:T(8,128)S(1)} %get-tuple-element.21.gram_ref, f32[512,8192]{1,0:T(8,128)} %x_hbm.7, ...), custom_call_target="tpu_custom_call" | custom-call | flops 603979776 | bytes 8388608 | tf_op jit(solution)/shard_map/rest_products/pallas_call | solution.py:192
  29.3 1.9 %collective-permute-start.7 = (f32[48,512]{1,0:T(8,128)S(1)}, f32[48,512]{1,0:T(8,128)S(1)}, u32[]{:S(2)}, u32[]{:S(2)}) collective-permute-start(f32[48,512]{1,0:T(8,128)S(1)} %slice.69), channel_id=1, source_target_pairs={{0,8},{1,5},{2,10},{3,7},{4,12},{5,1},{6,14},{7,3},{8,0},{9,13},{1... | collective-permute-start | bytes 294920 | tf_op jit(solution)/shard_map/ppermute | solution.py:340
  31.3 1.6 %collective-permute-start.5 = (f32[48,640]{1,0:T(8,128)S(1)}, f32[48,640]{1,0:T(8,128)S(1)}, u32[]{:S(2)}, u32[]{:S(2)}) collective-permute-start(f32[48,640]{1,0:T(8,128)S(1)} %slice.64), channel_id=1, source_target_pairs={{0,4},{1,9},{2,6},{3,11},{4,0},{5,13},{6,2},{7,15},{8,12},{9,1},{1... | collective-permute-start | bytes 368648 | tf_op jit(solution)/shard_map/ppermute | solution.py:340
  32.9 3.8 %rest_products.2 = (f32[48,1024]{1,0:T(8,128)S(1)}, f32[48,1024]{1,0:T(8,128)S(1)}) custom-call(s32[8]{0:T(128)S(1)} %stack.175.which_ref, bf16[96,512]{1,0:T(8,128)(2,1)S(1)} %get-tuple-element.20.both_ref, f32[48,128]{1,0:T(8,128)S(1)} %get-tuple-element.21.gram_ref, f32[512,8192]{1,0:T(8,128)} %x_hbm.7, f32[48,1152]{1,0:T(8,128)S(1)} %collective-permute-done.2.after_ref), custom_call_target="tpu_custom_call" | custom-call | flops 301989888 | bytes 4194304 | tf_op jit(solution)/shard_map/rest_products/pallas_call | solution.py:192
  38.0 2.6 %collective-permute-start.11 = (f32[48,1152]{1,0:T(8,128)S(1)}, f32[48,1152]{1,0:T(8,128)S(1)}, u32[]{:S(2)}, u32[]{:S(2)}) collective-permute-start(f32[48,1152]{1,0:T(8,128)S(1)} %pad_maximum_fusion), channel_id=1, source_target_pairs={{0,16},{4,20},{8,24},{12,28},{16,0},{20,4},{24,8},{28,12},{1,17},{... | collective-permute-start | bytes 663560 | tf_op jit(solution)/shard_map/ppermute | solution.py:330
  40.6 1.0 %collective-permute-start.9 = (f32[48,512]{1,0:T(8,128)S(1)}, f32[48,512]{1,0:T(8,128)S(1)}, u32[]{:S(2)}, u32[]{:S(2)}) collective-permute-start(f32[48,512]{1,0:T(8,128)S(1)} %slice.62), channel_id=1, source_target_pairs={{0,8},{1,5},{2,10},{3,7},{4,12},{5,1},{6,14},{7,3},{8,0},{9,13},{1... | collective-permute-start | bytes 294920 | tf_op jit(solution)/shard_map/ppermute | solution.py:340
  41.6 5.5 %collective-permute-done.9 = f32[48,512]{1,0:T(8,128)S(1)} collective-permute-done((f32[48,512]{1,0:T(8,128)S(1)}, f32[48,512]{1,0:T(8,128)S(1)}, u32[]{:S(2)}, u32[]{:S(2)}) %collective-permute-start.9) | collective-permute-done | bytes 98336 | tf_op jit(solution)/shard_map/ppermute | solution.py:340
  47.8 5.2 %collective-permute-done.11 = f32[48,1152]{1,0:T(8,128)S(1)} collective-permute-done((f32[48,1152]{1,0:T(8,128)S(1)}, f32[48,1152]{1,0:T(8,128)S(1)}, u32[]{:S(2)}, u32[]{:S(2)}) %collective-permute-start.11) | collective-permute-done | bytes 221216 | tf_op jit(solution)/shard_map/ppermute | solution.py:330
  53.1 2.2 %collective-permute-start.17 = (f32[48,512]{1,0:T(8,128)S(1)}, f32[48,512]{1,0:T(8,128)S(1)}, u32[]{:S(2)}, u32[]{:S(2)}) collective-permute-start(f32[48,512]{1,0:T(8,128)S(1)} %get-tuple-element.35), channel_id=1, source_target_pairs={{0,8},{1,5},{2,10},{3,7},{4,12},{5,1},{6,14},{7,3},{8,0},{9,13},{1... | collective-permute-start | bytes 294920 | tf_op jit(solution)/shard_map/ppermute | solution.py:340
  55.8 2.0 %inverse_factor.1.inverse_ref = f32[48,48]{1,0:T(8,128)S(1)} custom-call(f32[48,1152]{1,0:T(8,128)S(1)} %fusion.1.gram_ref.refs_0_), custom_call_target="tpu_custom_call" | custom-call | flops 20000000 | bytes 49152 | tf_op jit(solution)/shard_map/inverse_factor/pallas_call | solution.py:267
  59.7 1.5 %collective-permute-start.19 = (f32[48,1024]{1,0:T(8,128)S(1)}, f32[48,1024]{1,0:T(8,128)S(1)}, u32[]{:S(2)}, u32[]{:S(2)}) collective-permute-start(f32[48,1024]{1,0:T(8,128)S(1)} %pad_maximum_fusion.5), channel_id=1, source_target_pairs={{0,4},{1,9},{2,6},{3,11},{4,0},{5,13},{6,2},{7,15},{8,12},{9,1},{1... | collective-permute-start | bytes 589832 | tf_op jit(solution)/shard_map/ppermute | solution.py:340
  61.2 1.8 %collective-permute-start.18 = (f32[48,1024]{1,0:T(8,128)S(1)}, f32[48,1024]{1,0:T(8,128)S(1)}, u32[]{:S(2)}, u32[]{:S(2)}) collective-permute-start(f32[48,1024]{1,0:T(8,128)S(1)} %pad_maximum_fusion.4), channel_id=1, source_target_pairs={{0,8},{1,5},{2,10},{3,7},{4,12},{5,1},{6,14},{7,3},{8,0},{9,13},{1... | collective-permute-start | bytes 589832 | tf_op jit(solution)/shard_map/ppermute | solution.py:340
  63.0 1.8 %collective-permute-done.14.refs_2_ = f32[48,512]{1,0:T(8,128)S(1)} collective-permute-done((f32[48,512]{1,0:T(8,128)S(1)}, f32[48,512]{1,0:T(8,128)S(1)}, u32[]{:S(2)}, u32[]{:S(2)}) %collective-permute-start.14) | collective-permute-done | bytes 98336 | tf_op jit(solution)/shard_map/ppermute | solution.py:340
  64.8 1.1 %collective-permute-start.15 = (f32[48,1024]{1,0:T(8,128)S(1)}, f32[48,1024]{1,0:T(8,128)S(1)}, u32[]{:S(2)}, u32[]{:S(2)}) collective-permute-start(f32[48,1024]{1,0:T(8,128)S(1)} %pad_maximum_fusion.3), channel_id=1, source_target_pairs={{0,4},{1,9},{2,6},{3,11},{4,0},{5,13},{6,2},{7,15},{8,12},{9,1},{1... | collective-permute-start | bytes 589832 | tf_op jit(solution)/shard_map/ppermute | solution.py:340
  66.8 1.2 %collective-permute-done.19.refs_4_ = f32[48,1024]{1,0:T(8,128)S(1)} collective-permute-done((f32[48,1024]{1,0:T(8,128)S(1)}, f32[48,1024]{1,0:T(8,128)S(1)}, u32[]{:S(2)}, u32[]{:S(2)}) %collective-permute-start.19) | collective-permute-done | bytes 196640 | tf_op jit(solution)/shard_map/ppermute | solution.py:340
  68.9 1.7 %finish.3.refs_3_ = f32[48,8192]{1,0:T(8,128)} custom-call(s32[8]{0:T(128)S(1)} %stack.215.where_ref, f32[48,48]{1,0:T(8,128)S(1)} %inverse_factor.1.inverse_ref, f32[48,1152]{1,0:T(8,128)S(1)} %fusion.1.gram_ref.refs_0_, f32[48,512]{1,0:T(8,128)S(1)} %collective-permute-done.16.refs_1_, f32[48,512]{1,0:T(8,128)S(1)} %collective-permute-done.17.refs_2_, ...), custom_call_target="tpu_custom_call" | custom-call | flops 56623104 | bytes 1572864 | tf_op jit(solution)/shard_map/finish/pallas_call | solution.py:308
  70.6 1.5 %finish.4.refs_2_ = f32[48,8192]{1,0:T(8,128)} custom-call(s32[4]{0:T(128)S(1)} %pad_add_fusion.1.where_ref, f32[48,48]{1,0:T(8,128)S(1)} %inverse_factor.1.inverse_ref, f32[48,1024]{1,0:T(8,128)S(1)} %fusion.refs_0_, f32[48,512]{1,0:T(8,128)S(1)} %collective-permute-done.12.refs_1_, ...), custom_call_target="tpu_custom_call", output_to_operand_aliasing={{}: (5, {})} | custom-call | flops 28311552 | bytes 786432 | tf_op jit(solution)/shard_map/finish/pallas_call | solution.py:308
  72.2 1.5 %finish.5 = f32[48,8192]{1,0:T(8,128)} custom-call(s32[4]{0:T(128)S(1)} %pad_add_fusion.where_ref, f32[48,48]{1,0:T(8,128)S(1)} %inverse_factor.1.inverse_ref, f32[48,1024]{1,0:T(8,128)S(1)} %collective-permute-done.13.refs_0_, f32[48,1024]{1,0:T(8,128)S(1)} %collective-permute-done.15.refs_1_, f32[48,8192]{1,0:T(8,128)} %finish.4.refs_2_), custom_call_target="tpu_custom_call", output_to_operand_aliasing={{}: (4, {})} | custom-call | flops 28311552 | bytes 786432 | tf_op jit(solution)/shard_map/finish/pallas_call | solution.py:308
  (54 shorter events, 8.7 us)
Async XLA Ops:
  7.3 1.5 %collective-permute-start = (f32[48,512]{1,0:T(8,128)S(1)}, f32[48,512]{1,0:T(8,128)S(1)}, u32[]{:S(2)}, u32[]{:S(2)}) collective-permute-start(f32[48,512]{1,0:T(8,128)S(1)} %tall_partial.1), channel_id=1, source_target_pairs={{0,1},{1,0},{2,3},{3,2},{4,5},{5,4},{6,7},{7,6},{8,9},{9,8},{10,11... | collective-permute-start | bytes 294920 | tf_op jit(solution)/shard_map/ppermute | solution.py:330
  8.8 6.0 %collective-permute-start.1 = (f32[48,512]{1,0:T(8,128)S(1)}, f32[48,512]{1,0:T(8,128)S(1)}, u32[]{:S(2)}, u32[]{:S(2)}) collective-permute-start(f32[48,512]{1,0:T(8,128)S(1)} %add.209.one_ref), channel_id=1, source_target_pairs={{0,2},{1,3},{2,0},{3,1},{4,6},{5,7},{6,4},{7,5},{8,10},{9,11},{10,... | collective-permute-start | bytes 294920 | tf_op jit(solution)/shard_map/ppermute | solution.py:330
  18.9 10.4 %collective-permute-start.6 = (f32[48,1024]{1,0:T(8,128)S(1)}, f32[48,1024]{1,0:T(8,128)S(1)}, u32[]{:S(2)}, u32[]{:S(2)}) collective-permute-start(f32[48,1024]{1,0:T(8,128)S(1)} %get-tuple-element.29), channel_id=1, source_target_pairs={{0,4},{1,9},{2,6},{3,11},{4,0},{5,13},{6,2},{7,15},{8,12},{9,1},{1... | collective-permute-start | bytes 589832 | tf_op jit(solution)/shard_map/ppermute | solution.py:340
  20.8 10.5 %collective-permute-start.2 = (f32[48,1152]{1,0:T(8,128)S(1)}, f32[48,1152]{1,0:T(8,128)S(1)}, u32[]{:S(2)}, u32[]{:S(2)}) collective-permute-start(f32[48,1152]{1,0:T(8,128)S(1)} %get-tuple-element.22.after_ref), channel_id=1, source_target_pairs={{0,8},{1,5},{2,10},{3,7},{4,12},{5,1},{6,14},{7,3},{8,0},{9,13},{1... | collective-permute-start | bytes 663560 | tf_op jit(solution)/shard_map/ppermute | solution.py:340
  28.5 8.3 %collective-permute-start.4 = (f32[48,1024]{1,0:T(8,128)S(1)}, f32[48,1024]{1,0:T(8,128)S(1)}, u32[]{:S(2)}, u32[]{:S(2)}) collective-permute-start(f32[48,1024]{1,0:T(8,128)S(1)} %get-tuple-element.26), channel_id=1, source_target_pairs={{0,4},{1,9},{2,6},{3,11},{4,0},{5,13},{6,2},{7,15},{8,12},{9,1},{1... | collective-permute-start | bytes 589832 | tf_op jit(solution)/shard_map/ppermute | solution.py:340
  29.1 7.7 %collective-permute-start.3 = (f32[48,1024]{1,0:T(8,128)S(1)}, f32[48,1024]{1,0:T(8,128)S(1)}, u32[]{:S(2)}, u32[]{:S(2)}) collective-permute-start(f32[48,1024]{1,0:T(8,128)S(1)} %get-tuple-element.24), channel_id=1, source_target_pairs={{0,8},{1,5},{2,10},{3,7},{4,12},{5,1},{6,14},{7,3},{8,0},{9,13},{1... | collective-permute-start | bytes 589832 | tf_op jit(solution)/shard_map/ppermute | solution.py:340
  29.3 7.5 %collective-permute-start.7 = (f32[48,512]{1,0:T(8,128)S(1)}, f32[48,512]{1,0:T(8,128)S(1)}, u32[]{:S(2)}, u32[]{:S(2)}) collective-permute-start(f32[48,512]{1,0:T(8,128)S(1)} %slice.69), channel_id=1, source_target_pairs={{0,8},{1,5},{2,10},{3,7},{4,12},{5,1},{6,14},{7,3},{8,0},{9,13},{1... | collective-permute-start | bytes 294920 | tf_op jit(solution)/shard_map/ppermute | solution.py:340
  31.3 5.5 %collective-permute-start.5 = (f32[48,640]{1,0:T(8,128)S(1)}, f32[48,640]{1,0:T(8,128)S(1)}, u32[]{:S(2)}, u32[]{:S(2)}) collective-permute-start(f32[48,640]{1,0:T(8,128)S(1)} %slice.64), channel_id=1, source_target_pairs={{0,4},{1,9},{2,6},{3,11},{4,0},{5,13},{6,2},{7,15},{8,12},{9,1},{1... | collective-permute-start | bytes 368648 | tf_op jit(solution)/shard_map/ppermute | solution.py:340
  36.9 4.7 %collective-permute-start.8 = (f32[48,512]{1,0:T(8,128)S(1)}, f32[48,512]{1,0:T(8,128)S(1)}, u32[]{:S(2)}, u32[]{:S(2)}) collective-permute-start(f32[48,512]{1,0:T(8,128)S(1)} %slice.61), channel_id=1, source_target_pairs={{0,4},{1,9},{2,6},{3,11},{4,0},{5,13},{6,2},{7,15},{8,12},{9,1},{1... | collective-permute-start | bytes 294920 | tf_op jit(solution)/shard_map/ppermute | solution.py:340
  38.0 15.0 %collective-permute-start.11 = (f32[48,1152]{1,0:T(8,128)S(1)}, f32[48,1152]{1,0:T(8,128)S(1)}, u32[]{:S(2)}, u32[]{:S(2)}) collective-permute-start(f32[48,1152]{1,0:T(8,128)S(1)} %pad_maximum_fusion), channel_id=1, source_target_pairs={{0,16},{4,20},{8,24},{12,28},{16,0},{20,4},{24,8},{28,12},{1,17},{... | collective-permute-start | bytes 663560 | tf_op jit(solution)/shard_map/ppermute | solution.py:330
  40.6 6.6 %collective-permute-start.9 = (f32[48,512]{1,0:T(8,128)S(1)}, f32[48,512]{1,0:T(8,128)S(1)}, u32[]{:S(2)}, u32[]{:S(2)}) collective-permute-start(f32[48,512]{1,0:T(8,128)S(1)} %slice.62), channel_id=1, source_target_pairs={{0,8},{1,5},{2,10},{3,7},{4,12},{5,1},{6,14},{7,3},{8,0},{9,13},{1... | collective-permute-start | bytes 294920 | tf_op jit(solution)/shard_map/ppermute | solution.py:340
  47.2 11.4 %collective-permute-start.10 = (f32[48,1024]{1,0:T(8,128)S(1)}, f32[48,1024]{1,0:T(8,128)S(1)}, u32[]{:S(2)}, u32[]{:S(2)}) collective-permute-start(f32[48,1024]{1,0:T(8,128)S(1)} %pad_maximum_fusion.1), channel_id=1, source_target_pairs={{0,16},{4,20},{8,24},{12,28},{16,0},{20,4},{24,8},{28,12},{1,17},{... | collective-permute-start | bytes 589832 | tf_op jit(solution)/shard_map/ppermute | solution.py:330
  53.1 6.6 %collective-permute-start.17 = (f32[48,512]{1,0:T(8,128)S(1)}, f32[48,512]{1,0:T(8,128)S(1)}, u32[]{:S(2)}, u32[]{:S(2)}) collective-permute-start(f32[48,512]{1,0:T(8,128)S(1)} %get-tuple-element.35), channel_id=1, source_target_pairs={{0,8},{1,5},{2,10},{3,7},{4,12},{5,1},{6,14},{7,3},{8,0},{9,13},{1... | collective-permute-start | bytes 294920 | tf_op jit(solution)/shard_map/ppermute | solution.py:340
  55.3 5.9 %collective-permute-start.16 = (f32[48,512]{1,0:T(8,128)S(1)}, f32[48,512]{1,0:T(8,128)S(1)}, u32[]{:S(2)}, u32[]{:S(2)}) collective-permute-start(f32[48,512]{1,0:T(8,128)S(1)} %get-tuple-element.36), channel_id=1, source_target_pairs={{0,4},{1,9},{2,6},{3,11},{4,0},{5,13},{6,2},{7,15},{8,12},{9,1},{1... | collective-permute-start | bytes 294920 | tf_op jit(solution)/shard_map/ppermute | solution.py:340
  58.7 7.2 %collective-permute-start.12 = (f32[48,512]{1,0:T(8,128)S(1)}, f32[48,512]{1,0:T(8,128)S(1)}, u32[]{:S(2)}, u32[]{:S(2)}) collective-permute-start(f32[48,512]{1,0:T(8,128)S(1)} %get-tuple-element.33), channel_id=1, source_target_pairs={{0,4},{1,9},{2,6},{3,11},{4,0},{5,13},{6,2},{7,15},{8,12},{9,1},{1... | collective-permute-start | bytes 294920 | tf_op jit(solution)/shard_map/ppermute | solution.py:340
  59.5 5.2 %collective-permute-start.14 = (f32[48,512]{1,0:T(8,128)S(1)}, f32[48,512]{1,0:T(8,128)S(1)}, u32[]{:S(2)}, u32[]{:S(2)}) collective-permute-start(f32[48,512]{1,0:T(8,128)S(1)} %get-tuple-element.34), channel_id=1, source_target_pairs={{0,8},{1,5},{2,10},{3,7},{4,12},{5,1},{6,14},{7,3},{8,0},{9,13},{1... | collective-permute-start | bytes 294920 | tf_op jit(solution)/shard_map/ppermute | solution.py:340
  59.7 8.4 %collective-permute-start.19 = (f32[48,1024]{1,0:T(8,128)S(1)}, f32[48,1024]{1,0:T(8,128)S(1)}, u32[]{:S(2)}, u32[]{:S(2)}) collective-permute-start(f32[48,1024]{1,0:T(8,128)S(1)} %pad_maximum_fusion.5), channel_id=1, source_target_pairs={{0,4},{1,9},{2,6},{3,11},{4,0},{5,13},{6,2},{7,15},{8,12},{9,1},{1... | collective-permute-start | bytes 589832 | tf_op jit(solution)/shard_map/ppermute | solution.py:340
  61.2 7.7 %collective-permute-start.18 = (f32[48,1024]{1,0:T(8,128)S(1)}, f32[48,1024]{1,0:T(8,128)S(1)}, u32[]{:S(2)}, u32[]{:S(2)}) collective-permute-start(f32[48,1024]{1,0:T(8,128)S(1)} %pad_maximum_fusion.4), channel_id=1, source_target_pairs={{0,8},{1,5},{2,10},{3,7},{4,12},{5,1},{6,14},{7,3},{8,0},{9,13},{1... | collective-permute-start | bytes 589832 | tf_op jit(solution)/shard_map/ppermute | solution.py:340
  64.8 7.3 %collective-permute-start.15 = (f32[48,1024]{1,0:T(8,128)S(1)}, f32[48,1024]{1,0:T(8,128)S(1)}, u32[]{:S(2)}, u32[]{:S(2)}) collective-permute-start(f32[48,1024]{1,0:T(8,128)S(1)} %pad_maximum_fusion.3), channel_id=1, source_target_pairs={{0,4},{1,9},{2,6},{3,11},{4,0},{5,13},{6,2},{7,15},{8,12},{9,1},{1... | collective-permute-start | bytes 589832 | tf_op jit(solution)/shard_map/ppermute | solution.py:340
  66.0 6.2 %collective-permute-start.13 = (f32[48,1024]{1,0:T(8,128)S(1)}, f32[48,1024]{1,0:T(8,128)S(1)}, u32[]{:S(2)}, u32[]{:S(2)}) collective-permute-start(f32[48,1024]{1,0:T(8,128)S(1)} %pad_maximum_fusion.2), channel_id=1, source_target_pairs={{0,8},{1,5},{2,10},{3,7},{4,12},{5,1},{6,14},{7,3},{8,0},{9,13},{1... | collective-permute-start | bytes 589832 | tf_op jit(solution)/shard_map/ppermute | solution.py:340

commit v18 on v12

--- a/solution.py
+++ b/solution.py
@@ -181,7 +181,7 @@
         if with_gram:
             grams.append((out, sub))
         widths.append(len(blocks) * sub + extra)
-    return unit, plan, grams, widths, jnp.stack(which)
+    return unit, plan, grams, widths, which
 
 
 def products(kernel, inputs, in_specs, made, probes, outputs, sub, name):
@@ -205,7 +205,7 @@
             transcendentals=0,
         ),
         name=name,
-    )(which, *inputs)
+    )(jnp.stack(which), *inputs)
 
 
 def first_products(one, two, probes, outputs, sub):
@@ -330,10 +330,18 @@
         return lax.ppermute(value, axis, [(i, i ^ bit) for i in range(size)])
 
     def over(value, bit):
-        return swap(value, "pos", n_pos, bit)
+        if bit > 2:
+            return swap(value, "pos", n_pos, bit)
+        pairs = [
+            (i * n_pix + j, (i ^ (bit if j % 2 else 3 - bit)) * n_pix + j)
+            for i in range(n_pos)
+            for j in range(n_pix)
+        ]
+        return lax.ppermute(value, ("pos", "pix"), pairs)
 
     me = lax.axis_index("pos").astype(jnp.int32)
-    near, far = me & 1, (me >> 1) & 1
+    odd = lax.axis_index("pix").astype(jnp.int32) & 1
+    near, far = (me >> (1 - odd)) & 1, (me >> odd) & 1
     cols = probes.shape[1]
     width = cols // (8 * CHUNKS)
 
@@ -358,24 +366,25 @@
 
     both, gram, away = first_products(tall, other, probes, outputs(0, 1), width)
 
-    inverse, after = None, away[0]
+    plan = [(c, p) for c in range(CHUNKS) for p in (1, 0) if (c, p) != (0, 1)]
+    rest = rest_products(
+        both, gram, probes, [out for c, p in plan for out in outputs(c, p)], width, away[0]
+    )
+    made = {(0, 1): away}
+    made.update({key: rest[2 * k : 2 * k + 2] for k, key in enumerate(plan)})
+
+    inverse = None
     sources, pieces = [], []
     for c in range(CHUNKS):
         g = LANES if c == 0 else 0
-        last = c == CHUNKS - 1
-        made = rest_products(
-            both, gram, probes, outputs(c, 0) + ([] if last else outputs(c + 1, 1)), width, after
-        )
-        away_a, away_b = away
-        (own_a, own_b), away = made[:2], made[2:]
+        away_a, away_b = made[c, 1]
+        own_a, own_b = made[c, 0]
         if c > 0:
-            away_a, away_b, sum_a, sum_b = lax.optimization_barrier((away_a, away_b, sum_a, sum_b))
+            own_a, own_b, whole = lax.optimization_barrier((own_a, own_b, whole))
         got_a = over(away_a, 1)
         sum_a = own_a + got_a
         sum_b = own_b + over(away_b, 2)
         send_a, send_b = sum_a[:, : width + g], sum_b[:, :width]
-        if c > 0:
-            send_a, send_b, whole = lax.optimization_barrier((send_a, send_b, whole))
         got_a = over(send_a, 2)
         got_b = over(send_b, 1)
         whole = jnp.concatenate(
@@ -386,7 +395,7 @@
             ],
             axis=1,
         )
-        after = total = whole
+        total = whole
         bit = 4
         while bit < n_pos:
             total = total + over(total, bit)

time: 75.8 us -> 74.4 us (0.982)
  Pallas kernels: 23.4 us -> 21.8 us
  starting transfers between devices: 24.9 us -> 26.4 us
  waiting for transfers between devices: 26.4 us -> 25.1 us
    ppermute x0 -> x16, starting transfers between devices: none -> 18.1 us  [over(): return lax.ppermute(value, ('pos', 'pix'), pairs)]
    ppermute x20 -> x4, starting transfers between devices: 24.9 us -> 8.33 us  [swap(): return lax.ppermute(value, axis, [(i, i ^ bit) for i in range(size)])]
    ppermute x20 -> x4, waiting for transfers between devices: 26.4 us -> 10.4 us  [swap(): return lax.ppermute(value, axis, [(i, i ^ bit) for i in range(size)])]
    ppermute x0 -> x16, waiting for transfers between devices: none -> 14.7 us  [over(): return lax.ppermute(value, ('pos', 'pix'), pairs)]
    pallas_call x3 -> x2, Pallas kernels: 10.7 us -> 9.14 us  [products(): pl.pallas_call(functools.partial(kernel, plan, grams), in_specs=[TABLE, *...]
  transfers between devices with their start and end apart: 20 -> 20, of which waited for: 10 -> 13; matrix products, arithmetic and copies ran while one was open for 1% -> 1% of each run, Pallas kernels for 15% -> 13%
where the time goes in v18:
time: 74.4 us; the launch traced here: 74.3 us
  starting transfers between devices  26.4 us (35%)
  waiting for transfers between devices  25.1 us (34%)
  Pallas kernels  21.8 us (29%)
    ppermute x16, starting transfers between devices, over(): return lax.ppermute(value, ('pos', 'pix'), pairs)  18.1 us
    ppermute x16, waiting for transfers between devices, over(): return lax.ppermute(value, ('pos', 'pix'), pairs)  14.7 us
    ppermute x4, waiting for transfers between devices, swap(): return lax.ppermute(value, axis, [(i, i ^ bit) for i in range(size)])  10.4 us
    pallas_call x2, Pallas kernels, products(): pl.pallas_call(functools.partial(kernel, plan, grams), in_specs=[TABLE, *...  9.14 us
    ppermute x4, starting transfers between devices, swap(): return lax.ppermute(value, axis, [(i, i ^ bit) for i in range(size)])  8.33 us
    pallas_call x1, Pallas kernels, tall_partial(): pl.pallas_call(tall_kernel, in_specs=[HBM, HBM], out_specs=WHOLE, out_sha...  7.27 us
    pallas_call x2, Pallas kernels, finish(): pl.pallas_call(functools.partial(finish_kernel, [piece[1:] for piece in p...  3.4 us
    pallas_call x1, Pallas kernels, inverse_factor(): pl.pallas_call(inverse_kernel, grid=(1,), in_specs=[pl.BlockSpec((rank, L...  2.01 us
  transfers between devices with their start and end apart: 20, of which 13 were waited for; matrix products, arithmetic and copies ran while one was open for 1% of the time, Pallas kernels for 13%

profile of v18, /device:TPU:0, one launch (start us, length us, event | category | flops | bytes accessed | tf_op | source)
XLA Modules:
  0.0 74.3 jit_solution(8983343617494374029)
XLA Ops:
  0.0 7.3 %tall_partial.1 = f32[48,512]{1,0:T(8,128)S(1)} custom-call(f32[512,8192]{1,0:T(8,128)} %x_hbm.5, f32[48,8192]{1,0:T(8,128)} %bitcast.17), custom_call_target="tpu_custom_call" | custom-call | flops 1207959552 | bytes 16777216 | tf_op jit(solution)/shard_map/tall_partial/pallas_call | solution.py:91
  8.8 2.9 %collective-permute-start.1 = (f32[48,512]{1,0:T(8,128)S(1)}, f32[48,512]{1,0:T(8,128)S(1)}, u32[]{:S(2)}, u32[]{:S(2)}) collective-permute-start(f32[48,512]{1,0:T(8,128)S(1)} %add.158.one_ref), channel_id=1, source_target_pairs={{0,2},{1,3},{2,0},{3,1},{4,6},{5,7},{6,4},{7,5},{8,10},{9,11},{10,... | collective-permute-start | bytes 294920 | tf_op jit(solution)/shard_map/ppermute | solution.py:330
  11.8 3.0 %collective-permute-done.1.two_ref = f32[48,512]{1,0:T(8,128)S(1)} collective-permute-done((f32[48,512]{1,0:T(8,128)S(1)}, f32[48,512]{1,0:T(8,128)S(1)}, u32[]{:S(2)}, u32[]{:S(2)}) %collective-permute-start.1) | collective-permute-done | bytes 98336 | tf_op jit(solution)/shard_map/ppermute | solution.py:330
  14.8 3.3 %first_products.1 = (bf16[96,512]{1,0:T(8,128)(2,1)S(1)}, f32[48,128]{1,0:T(8,128)S(1)}, f32[48,1152]{1,0:T(8,128)S(1)}, f32[48,1024]{1,0:T(8,128)S(1)}) custom-call(s32[4]{0:T(128)S(1)} %pad_add_fusion.1.which_ref, f32[48,512]{1,0:T(8,128)S(1)} %add.158.one_ref, f32[48,512]{1,0:T(8,128)S(1)} %collective-permute-done.1.two_ref, f32[512,8192]{1,0:T(8,128)} %x_hbm.5), custom_call_target="tpu_custom_call" | custom-call | flops 301989888 | bytes 4194304 | tf_op jit(solution)/shard_map/first_products/pallas_call | solution.py:192
  18.2 1.8 %collective-permute-start.4 = (f32[48,1024]{1,0:T(8,128)S(1)}, f32[48,1024]{1,0:T(8,128)S(1)}, u32[]{:S(2)}, u32[]{:S(2)}) collective-permute-start(f32[48,1024]{1,0:T(8,128)S(1)} %get-tuple-element.27), channel_id=1, source_target_pairs={{0,4},{1,9},{2,6},{3,11},{4,0},{5,13},{6,2},{7,15},{8,12},{9,1},{1... | collective-permute-start | bytes 589832 | tf_op jit(solution)/shard_map/ppermute | solution.py:340
  19.9 1.6 %collective-permute-start.2 = (f32[48,1152]{1,0:T(8,128)S(1)}, f32[48,1152]{1,0:T(8,128)S(1)}, u32[]{:S(2)}, u32[]{:S(2)}) collective-permute-start(f32[48,1152]{1,0:T(8,128)S(1)} %get-tuple-element.22.after_ref), channel_id=1, source_target_pairs={{0,8},{1,5},{2,10},{3,7},{4,12},{5,1},{6,14},{7,3},{8,0},{9,13},{1... | collective-permute-start | bytes 663560 | tf_op jit(solution)/shard_map/ppermute | solution.py:340
  21.6 5.8 %rest_products.1 = (f32[48,1152]{1,0:T(8,128)S(1)}, f32[48,1024]{1,0:T(8,128)S(1)}, f32[48,1024]{1,0:T(8,128)S(1)}, f32[48,1024]{1,0:T(8,128)S(1)}, f32[48,1024]{1,0:T(8,128)S(1)}, /*index=5*/f32[48,1024]{1,0:T(8,128)S(1)}) custom-call(s32[12]{0:T(128)S(1)} %stack.89.which_ref, bf16[96,512]{1,0:T(8,128)(2,1)S(1)} %get-tuple-element.20.both_ref, ...), custom_call_target="tpu_custom_call" | custom-call | flops 905969664 | bytes 12582912 | tf_op jit(solution)/shard_map/rest_products/pallas_call | solution.py:192
  28.0 1.6 %collective-permute-start.6 = (f32[48,1024]{1,0:T(8,128)S(1)}, f32[48,1024]{1,0:T(8,128)S(1)}, u32[]{:S(2)}, u32[]{:S(2)}) collective-permute-start(f32[48,1024]{1,0:T(8,128)S(1)} %get-tuple-element.29), channel_id=1, source_target_pairs={{0,8},{1,5},{2,10},{3,7},{4,12},{5,1},{6,14},{7,3},{8,0},{9,13},{1... | collective-permute-start | bytes 589832 | tf_op jit(solution)/shard_map/ppermute | solution.py:340
  30.2 1.6 %collective-permute-start.3 = (f32[48,640]{1,0:T(8,128)S(1)}, f32[48,640]{1,0:T(8,128)S(1)}, u32[]{:S(2)}, u32[]{:S(2)}) collective-permute-start(f32[48,640]{1,0:T(8,128)S(1)} %slice.61), channel_id=1, source_target_pairs={{0,4},{1,9},{2,6},{3,11},{4,0},{5,13},{6,2},{7,15},{8,12},{9,1},{1... | collective-permute-start | bytes 368648 | tf_op jit(solution)/shard_map/ppermute | solution.py:340
  31.7 1.5 %collective-permute-done.5 = f32[48,512]{1,0:T(8,128)S(1)} collective-permute-done((f32[48,512]{1,0:T(8,128)S(1)}, f32[48,512]{1,0:T(8,128)S(1)}, u32[]{:S(2)}, u32[]{:S(2)}) %collective-permute-start.5) | collective-permute-done | bytes 98336 | tf_op jit(solution)/shard_map/ppermute | solution.py:340
  33.2 3.4 %collective-permute-done.3 = f32[48,640]{1,0:T(8,128)S(1)} collective-permute-done((f32[48,640]{1,0:T(8,128)S(1)}, f32[48,640]{1,0:T(8,128)S(1)}, u32[]{:S(2)}, u32[]{:S(2)}) %collective-permute-start.3) | collective-permute-done | bytes 122912 | tf_op jit(solution)/shard_map/ppermute | solution.py:340
  37.6 2.6 %collective-permute-start.11 = (f32[48,1152]{1,0:T(8,128)S(1)}, f32[48,1152]{1,0:T(8,128)S(1)}, u32[]{:S(2)}, u32[]{:S(2)}) collective-permute-start(f32[48,1152]{1,0:T(8,128)S(1)} %pad_maximum_fusion), channel_id=1, source_target_pairs={{0,16},{4,20},{8,24},{12,28},{16,0},{20,4},{24,8},{28,12},{1,17},{... | collective-permute-start | bytes 663560 | tf_op jit(solution)/shard_map/ppermute | solution.py:330
  41.7 5.4 %collective-permute-done.9 = f32[48,512]{1,0:T(8,128)S(1)} collective-permute-done((f32[48,512]{1,0:T(8,128)S(1)}, f32[48,512]{1,0:T(8,128)S(1)}, u32[]{:S(2)}, u32[]{:S(2)}) %collective-permute-start.9) | collective-permute-done | bytes 98336 | tf_op jit(solution)/shard_map/ppermute | solution.py:340
  47.1 2.3 %collective-permute-start.10 = (f32[48,1024]{1,0:T(8,128)S(1)}, f32[48,1024]{1,0:T(8,128)S(1)}, u32[]{:S(2)}, u32[]{:S(2)}) collective-permute-start(f32[48,1024]{1,0:T(8,128)S(1)} %pad_maximum_fusion.1), channel_id=1, source_target_pairs={{0,16},{4,20},{8,24},{12,28},{16,0},{20,4},{24,8},{28,12},{1,17},{... | collective-permute-start | bytes 589832 | tf_op jit(solution)/shard_map/ppermute | solution.py:330
  49.4 6.4 %collective-permute-done.11 = f32[48,1152]{1,0:T(8,128)S(1)} collective-permute-done((f32[48,1152]{1,0:T(8,128)S(1)}, f32[48,1152]{1,0:T(8,128)S(1)}, u32[]{:S(2)}, u32[]{:S(2)}) %collective-permute-start.11) | collective-permute-done | bytes 221216 | tf_op jit(solution)/shard_map/ppermute | solution.py:330
  57.1 2.0 %inverse_factor.1.inverse_ref = f32[48,48]{1,0:T(8,128)S(1)} custom-call(f32[48,1152]{1,0:T(8,128)S(1)} %fusion.1.gram_ref.refs_0_), custom_call_target="tpu_custom_call" | custom-call | flops 20000000 | bytes 49152 | tf_op jit(solution)/shard_map/inverse_factor/pallas_call | solution.py:267
  60.2 1.9 %collective-permute-start.14 = (f32[48,512]{1,0:T(8,128)S(1)}, f32[48,512]{1,0:T(8,128)S(1)}, u32[]{:S(2)}, u32[]{:S(2)}) collective-permute-start(f32[48,512]{1,0:T(8,128)S(1)} %get-tuple-element.34), channel_id=1, source_target_pairs={{0,8},{1,5},{2,10},{3,7},{4,12},{5,1},{6,14},{7,3},{8,0},{9,13},{1... | collective-permute-start | bytes 294920 | tf_op jit(solution)/shard_map/ppermute | solution.py:340
  62.1 1.3 %collective-permute-start.18 = (f32[48,1024]{1,0:T(8,128)S(1)}, f32[48,1024]{1,0:T(8,128)S(1)}, u32[]{:S(2)}, u32[]{:S(2)}) collective-permute-start(f32[48,1024]{1,0:T(8,128)S(1)} %pad_maximum_fusion.4), channel_id=1, source_target_pairs={{0,8},{1,5},{2,10},{3,7},{4,12},{5,1},{6,14},{7,3},{8,0},{9,13},{1... | collective-permute-start | bytes 589832 | tf_op jit(solution)/shard_map/ppermute | solution.py:340
  63.4 1.2 %collective-permute-start.19 = (f32[48,1024]{1,0:T(8,128)S(1)}, f32[48,1024]{1,0:T(8,128)S(1)}, u32[]{:S(2)}, u32[]{:S(2)}) collective-permute-start(f32[48,1024]{1,0:T(8,128)S(1)} %pad_maximum_fusion.5), channel_id=1, source_target_pairs={{0,4},{1,9},{2,6},{3,11},{4,0},{5,13},{6,2},{7,15},{8,12},{9,1},{1... | collective-permute-start | bytes 589832 | tf_op jit(solution)/shard_map/ppermute | solution.py:340
  65.8 1.2 %collective-permute-start.15 = (f32[48,1024]{1,0:T(8,128)S(1)}, f32[48,1024]{1,0:T(8,128)S(1)}, u32[]{:S(2)}, u32[]{:S(2)}) collective-permute-start(f32[48,1024]{1,0:T(8,128)S(1)} %pad_maximum_fusion.3), channel_id=1, source_target_pairs={{0,4},{1,9},{2,6},{3,11},{4,0},{5,13},{6,2},{7,15},{8,12},{9,1},{1... | collective-permute-start | bytes 589832 | tf_op jit(solution)/shard_map/ppermute | solution.py:340
  67.0 1.6 %collective-permute-start.13 = (f32[48,1024]{1,0:T(8,128)S(1)}, f32[48,1024]{1,0:T(8,128)S(1)}, u32[]{:S(2)}, u32[]{:S(2)}) collective-permute-start(f32[48,1024]{1,0:T(8,128)S(1)} %pad_maximum_fusion.2), channel_id=1, source_target_pairs={{0,8},{1,5},{2,10},{3,7},{4,12},{5,1},{6,14},{7,3},{8,0},{9,13},{1... | collective-permute-start | bytes 589832 | tf_op jit(solution)/shard_map/ppermute | solution.py:340
  68.8 1.2 %collective-permute-done.18.refs_3_ = f32[48,1024]{1,0:T(8,128)S(1)} collective-permute-done((f32[48,1024]{1,0:T(8,128)S(1)}, f32[48,1024]{1,0:T(8,128)S(1)}, u32[]{:S(2)}, u32[]{:S(2)}) %collective-permute-start.18) | collective-permute-done | bytes 196640 | tf_op jit(solution)/shard_map/ppermute | solution.py:340
  70.1 1.9 %finish.2.refs_2_ = f32[48,8192]{1,0:T(8,128)} custom-call(s32[12]{0:T(128)S(1)} %stack.95.where_ref, f32[48,48]{1,0:T(8,128)S(1)} %inverse_factor.1.inverse_ref, f32[48,1152]{1,0:T(8,128)S(1)} %fusion.1.gram_ref.refs_0_, f32[48,512]{1,0:T(8,128)S(1)} %collective-permute-done.16.refs_1_, f32[48,512]{1,0:T(8,128)S(1)} %collective-permute-done.17.refs_2_, ...), custom_call_target="tpu_custom_call" | custom-call | flops 84934656 | bytes 2359296 | tf_op jit(solution)/shard_map/finish/pallas_call | solution.py:308
  72.7 1.5 %finish.3 = f32[48,8192]{1,0:T(8,128)} custom-call(s32[4]{0:T(128)S(1)} %pad_add_fusion.where_ref, f32[48,48]{1,0:T(8,128)S(1)} %inverse_factor.1.inverse_ref, f32[48,1024]{1,0:T(8,128)S(1)} %collective-permute-done.13.refs_0_, f32[48,1024]{1,0:T(8,128)S(1)} %collective-permute-done.15.refs_1_, f32[48,8192]{1,0:T(8,128)} %finish.2.refs_2_), custom_call_target="tpu_custom_call", output_to_operand_aliasing={{}: (4, {})} | custom-call | flops 28311552 | bytes 786432 | tf_op jit(solution)/shard_map/finish/pallas_call | solution.py:308
  (50 shorter events, 9.9 us)
Async XLA Ops:
  7.3 1.5 %collective-permute-start = (f32[48,512]{1,0:T(8,128)S(1)}, f32[48,512]{1,0:T(8,128)S(1)}, u32[]{:S(2)}, u32[]{:S(2)}) collective-permute-start(f32[48,512]{1,0:T(8,128)S(1)} %tall_partial.1), channel_id=1, source_target_pairs={{0,1},{1,0},{2,3},{3,2},{4,5},{5,4},{6,7},{7,6},{8,9},{9,8},{10,11... | collective-permute-start | bytes 294920 | tf_op jit(solution)/shard_map/ppermute | solution.py:330
  8.8 6.0 %collective-permute-start.1 = (f32[48,512]{1,0:T(8,128)S(1)}, f32[48,512]{1,0:T(8,128)S(1)}, u32[]{:S(2)}, u32[]{:S(2)}) collective-permute-start(f32[48,512]{1,0:T(8,128)S(1)} %add.158.one_ref), channel_id=1, source_target_pairs={{0,2},{1,3},{2,0},{3,1},{4,6},{5,7},{6,4},{7,5},{8,10},{9,11},{10,... | collective-permute-start | bytes 294920 | tf_op jit(solution)/shard_map/ppermute | solution.py:330
  18.2 9.3 %collective-permute-start.4 = (f32[48,1024]{1,0:T(8,128)S(1)}, f32[48,1024]{1,0:T(8,128)S(1)}, u32[]{:S(2)}, u32[]{:S(2)}) collective-permute-start(f32[48,1024]{1,0:T(8,128)S(1)} %get-tuple-element.27), channel_id=1, source_target_pairs={{0,4},{1,9},{2,6},{3,11},{4,0},{5,13},{6,2},{7,15},{8,12},{9,1},{1... | collective-permute-start | bytes 589832 | tf_op jit(solution)/shard_map/ppermute | solution.py:340
  19.9 10.2 %collective-permute-start.2 = (f32[48,1152]{1,0:T(8,128)S(1)}, f32[48,1152]{1,0:T(8,128)S(1)}, u32[]{:S(2)}, u32[]{:S(2)}) collective-permute-start(f32[48,1152]{1,0:T(8,128)S(1)} %get-tuple-element.22.after_ref), channel_id=1, source_target_pairs={{0,8},{1,5},{2,10},{3,7},{4,12},{5,1},{6,14},{7,3},{8,0},{9,13},{1... | collective-permute-start | bytes 663560 | tf_op jit(solution)/shard_map/ppermute | solution.py:340
  27.5 5.7 %collective-permute-start.5 = (f32[48,512]{1,0:T(8,128)S(1)}, f32[48,512]{1,0:T(8,128)S(1)}, u32[]{:S(2)}, u32[]{:S(2)}) collective-permute-start(f32[48,512]{1,0:T(8,128)S(1)} %slice.66), channel_id=1, source_target_pairs={{0,8},{1,5},{2,10},{3,7},{4,12},{5,1},{6,14},{7,3},{8,0},{9,13},{1... | collective-permute-start | bytes 294920 | tf_op jit(solution)/shard_map/ppermute | solution.py:340
  28.0 9.0 %collective-permute-start.6 = (f32[48,1024]{1,0:T(8,128)S(1)}, f32[48,1024]{1,0:T(8,128)S(1)}, u32[]{:S(2)}, u32[]{:S(2)}) collective-permute-start(f32[48,1024]{1,0:T(8,128)S(1)} %get-tuple-element.29), channel_id=1, source_target_pairs={{0,8},{1,5},{2,10},{3,7},{4,12},{5,1},{6,14},{7,3},{8,0},{9,13},{1... | collective-permute-start | bytes 589832 | tf_op jit(solution)/shard_map/ppermute | solution.py:340
  29.6 10.6 %collective-permute-start.8 = (f32[48,1024]{1,0:T(8,128)S(1)}, f32[48,1024]{1,0:T(8,128)S(1)}, u32[]{:S(2)}, u32[]{:S(2)}) collective-permute-start(f32[48,1024]{1,0:T(8,128)S(1)} %get-tuple-element.31), channel_id=1, source_target_pairs={{0,4},{1,9},{2,6},{3,11},{4,0},{5,13},{6,2},{7,15},{8,12},{9,1},{1... | collective-permute-start | bytes 589832 | tf_op jit(solution)/shard_map/ppermute | solution.py:340
  30.2 6.4 %collective-permute-start.3 = (f32[48,640]{1,0:T(8,128)S(1)}, f32[48,640]{1,0:T(8,128)S(1)}, u32[]{:S(2)}, u32[]{:S(2)}) collective-permute-start(f32[48,640]{1,0:T(8,128)S(1)} %slice.61), channel_id=1, source_target_pairs={{0,4},{1,9},{2,6},{3,11},{4,0},{5,13},{6,2},{7,15},{8,12},{9,1},{1... | collective-permute-start | bytes 368648 | tf_op jit(solution)/shard_map/ppermute | solution.py:340
  37.0 4.7 %collective-permute-start.7 = (f32[48,512]{1,0:T(8,128)S(1)}, f32[48,512]{1,0:T(8,128)S(1)}, u32[]{:S(2)}, u32[]{:S(2)}) collective-permute-start(f32[48,512]{1,0:T(8,128)S(1)} %slice.68), channel_id=1, source_target_pairs={{0,4},{1,9},{2,6},{3,11},{4,0},{5,13},{6,2},{7,15},{8,12},{9,1},{1... | collective-permute-start | bytes 294920 | tf_op jit(solution)/shard_map/ppermute | solution.py:340
  37.6 18.2 %collective-permute-start.11 = (f32[48,1152]{1,0:T(8,128)S(1)}, f32[48,1152]{1,0:T(8,128)S(1)}, u32[]{:S(2)}, u32[]{:S(2)}) collective-permute-start(f32[48,1152]{1,0:T(8,128)S(1)} %pad_maximum_fusion), channel_id=1, source_target_pairs={{0,16},{4,20},{8,24},{12,28},{16,0},{20,4},{24,8},{28,12},{1,17},{... | collective-permute-start | bytes 663560 | tf_op jit(solution)/shard_map/ppermute | solution.py:330
  40.2 6.8 %collective-permute-start.9 = (f32[48,512]{1,0:T(8,128)S(1)}, f32[48,512]{1,0:T(8,128)S(1)}, u32[]{:S(2)}, u32[]{:S(2)}) collective-permute-start(f32[48,512]{1,0:T(8,128)S(1)} %slice.70), channel_id=1, source_target_pairs={{0,8},{1,5},{2,10},{3,7},{4,12},{5,1},{6,14},{7,3},{8,0},{9,13},{1... | collective-permute-start | bytes 294920 | tf_op jit(solution)/shard_map/ppermute | solution.py:340
  47.1 12.0 %collective-permute-start.10 = (f32[48,1024]{1,0:T(8,128)S(1)}, f32[48,1024]{1,0:T(8,128)S(1)}, u32[]{:S(2)}, u32[]{:S(2)}) collective-permute-start(f32[48,1024]{1,0:T(8,128)S(1)} %pad_maximum_fusion.1), channel_id=1, source_target_pairs={{0,16},{4,20},{8,24},{12,28},{16,0},{20,4},{24,8},{28,12},{1,17},{... | collective-permute-start | bytes 589832 | tf_op jit(solution)/shard_map/ppermute | solution.py:330
  55.9 7.5 %collective-permute-start.17 = (f32[48,512]{1,0:T(8,128)S(1)}, f32[48,512]{1,0:T(8,128)S(1)}, u32[]{:S(2)}, u32[]{:S(2)}) collective-permute-start(f32[48,512]{1,0:T(8,128)S(1)} %get-tuple-element.35), channel_id=1, source_target_pairs={{0,8},{1,5},{2,10},{3,7},{4,12},{5,1},{6,14},{7,3},{8,0},{9,13},{1... | collective-permute-start | bytes 294920 | tf_op jit(solution)/shard_map/ppermute | solution.py:340
  55.9 6.2 %collective-permute-start.16 = (f32[48,512]{1,0:T(8,128)S(1)}, f32[48,512]{1,0:T(8,128)S(1)}, u32[]{:S(2)}, u32[]{:S(2)}) collective-permute-start(f32[48,512]{1,0:T(8,128)S(1)} %get-tuple-element.36), channel_id=1, source_target_pairs={{0,4},{1,9},{2,6},{3,11},{4,0},{5,13},{6,2},{7,15},{8,12},{9,1},{1... | collective-permute-start | bytes 294920 | tf_op jit(solution)/shard_map/ppermute | solution.py:340
  59.1 7.8 %collective-permute-start.12 = (f32[48,512]{1,0:T(8,128)S(1)}, f32[48,512]{1,0:T(8,128)S(1)}, u32[]{:S(2)}, u32[]{:S(2)}) collective-permute-start(f32[48,512]{1,0:T(8,128)S(1)} %get-tuple-element.33), channel_id=1, source_target_pairs={{0,4},{1,9},{2,6},{3,11},{4,0},{5,13},{6,2},{7,15},{8,12},{9,1},{1... | collective-permute-start | bytes 294920 | tf_op jit(solution)/shard_map/ppermute | solution.py:340
  60.2 5.6 %collective-permute-start.14 = (f32[48,512]{1,0:T(8,128)S(1)}, f32[48,512]{1,0:T(8,128)S(1)}, u32[]{:S(2)}, u32[]{:S(2)}) collective-permute-start(f32[48,512]{1,0:T(8,128)S(1)} %get-tuple-element.34), channel_id=1, source_target_pairs={{0,8},{1,5},{2,10},{3,7},{4,12},{5,1},{6,14},{7,3},{8,0},{9,13},{1... | collective-permute-start | bytes 294920 | tf_op jit(solution)/shard_map/ppermute | solution.py:340
  62.1 7.8 %collective-permute-start.18 = (f32[48,1024]{1,0:T(8,128)S(1)}, f32[48,1024]{1,0:T(8,128)S(1)}, u32[]{:S(2)}, u32[]{:S(2)}) collective-permute-start(f32[48,1024]{1,0:T(8,128)S(1)} %pad_maximum_fusion.4), channel_id=1, source_target_pairs={{0,8},{1,5},{2,10},{3,7},{4,12},{5,1},{6,14},{7,3},{8,0},{9,13},{1... | collective-permute-start | bytes 589832 | tf_op jit(solution)/shard_map/ppermute | solution.py:340
  63.4 6.7 %collective-permute-start.19 = (f32[48,1024]{1,0:T(8,128)S(1)}, f32[48,1024]{1,0:T(8,128)S(1)}, u32[]{:S(2)}, u32[]{:S(2)}) collective-permute-start(f32[48,1024]{1,0:T(8,128)S(1)} %pad_maximum_fusion.5), channel_id=1, source_target_pairs={{0,4},{1,9},{2,6},{3,11},{4,0},{5,13},{6,2},{7,15},{8,12},{9,1},{1... | collective-permute-start | bytes 589832 | tf_op jit(solution)/shard_map/ppermute | solution.py:340
  65.8 6.5 %collective-permute-start.15 = (f32[48,1024]{1,0:T(8,128)S(1)}, f32[48,1024]{1,0:T(8,128)S(1)}, u32[]{:S(2)}, u32[]{:S(2)}) collective-permute-start(f32[48,1024]{1,0:T(8,128)S(1)} %pad_maximum_fusion.3), channel_id=1, source_target_pairs={{0,4},{1,9},{2,6},{3,11},{4,0},{5,13},{6,2},{7,15},{8,12},{9,1},{1... | collective-permute-start | bytes 589832 | tf_op jit(solution)/shard_map/ppermute | solution.py:340
  67.0 5.7 %collective-permute-start.13 = (f32[48,1024]{1,0:T(8,128)S(1)}, f32[48,1024]{1,0:T(8,128)S(1)}, u32[]{:S(2)}, u32[]{:S(2)}) collective-permute-start(f32[48,1024]{1,0:T(8,128)S(1)} %pad_maximum_fusion.2), channel_id=1, source_target_pairs={{0,8},{1,5},{2,10},{3,7},{4,12},{5,1},{6,14},{7,3},{8,0},{9,13},{1... | collective-permute-start | bytes 589832 | tf_op jit(solution)/shard_map/ppermute | solution.py:340

commit v19 on v11

--- a/solution.py
+++ b/solution.py
@@ -53,36 +53,40 @@
         use(k)
 
 
-def tall_kernel(x_hbm, s_hbm, out_ref, x_buf, s_buf, head_buf, rest_buf, x_sems, s_sem):
+def tall_kernel(x_hbm, s_hbm, out_ref, x_buf, s_buf, head_buf, rest_buf, x_sems, s_sems):
     blocks, _, unit = x_buf.shape
     rank = s_hbm.shape[0]
-    copies = [
-        pltpu.make_async_copy(x_hbm.at[:, pl.ds(k * unit, unit)], x_buf.at[k], x_sems.at[k])
-        for k in range(blocks)
-    ]
-    sketch = pltpu.make_async_copy(s_hbm, s_buf, s_sem)
-    sketch.start()
-
-    def use(k):
-        if k == 0:
-            sketch.wait()
-        s_head, s_rest = split(s_buf[:, k * unit : (k + 1) * unit])
+
+    def copies(k):
+        where = pl.ds(k * unit, unit)
+        return (
+            pltpu.make_async_copy(s_hbm.at[:, where], s_buf.at[k], s_sems.at[k]),
+            pltpu.make_async_copy(x_hbm.at[:, where], x_buf.at[k], x_sems.at[k]),
+        )
+
+    for k in range(blocks):
+        for copy in copies(k):
+            copy.start()
+    for k in range(blocks):
+        for copy in copies(k):
+            copy.wait()
+        s_head, s_rest = split(s_buf[k])
         s_both = jnp.concatenate([s_head, s_rest], axis=0)
-        head_buf[k % 2], rest_buf[k % 2] = split(x_buf[k])
-        both = dot(s_both, head_buf[k % 2], LAST)
-        part = both[:rank] + (both[rank:] + dot(s_head, rest_buf[k % 2], LAST))
+        x_head, x_rest = split(x_buf[k])
+        head_buf[k] = x_head
+        rest_buf[k] = x_rest
+        both = dot(s_both, x_head, LAST)
+        part = both[:rank] + (both[rank:] + dot(s_head, x_rest, LAST))
         if k == 0:
             out_ref[...] = part
         else:
             out_ref[...] += part
 
-    stream(copies, use)
-
 
 def tall_partial(probes, sketch_t):
     rows, cols = probes.shape
     rank = sketch_t.shape[0]
-    unit = min(UNIT, cols)
+    unit = min(2 * UNIT, cols)
     blocks = cols // unit
     return pl.pallas_call(
         tall_kernel,
@@ -91,11 +95,11 @@
         out_shape=jax.ShapeDtypeStruct((rank, rows), F32),
         scratch_shapes=[
             pltpu.VMEM((blocks, rows, unit), F32),
-            pltpu.VMEM((rank, cols), F32),
-            pltpu.VMEM((2, rows, unit), BF16),
-            pltpu.VMEM((2, rows, unit), BF16),
+            pltpu.VMEM((blocks, rank, unit), F32),
+            pltpu.VMEM((blocks, rows, unit), BF16),
+            pltpu.VMEM((blocks, rows, unit), BF16),
             pltpu.SemaphoreType.DMA((blocks,)),
-            pltpu.SemaphoreType.DMA,
+            pltpu.SemaphoreType.DMA((blocks,)),
         ],
         compiler_params=PARAMS,
         cost_estimate=pl.CostEstimate(
@@ -357,34 +361,31 @@
 
     both, gram, away = first_products(tall, other, probes, outputs(0, 1), width)
 
-    ready, total = away[0], []
+    whole, total, send = [], [], None
     for c in range(CHUNKS):
         g = LANES if c == 0 else 0
         more = outputs(c + 1, 1) if c + 1 < CHUNKS else []
+        ready = away[0] if c == 0 else whole[-1]
         own, *made = rest_products(both, gram, probes, outputs(c, 0) + more, width, ready)
-        ready = over(away[0], 0)
-        away = made
-        part = own + ready
-        if away:
-            away[0] = after(away[0], part)
-        got = over(part[:, : width + g], 1)
-        whole = part[:, width + g :] + got[:, :width]
+        sent = away[0] if c == 0 else after(away[0], send)
+        part, away = own + over(sent, 0), made
+        send = part[:, : width + g]
+        got = over(send, 1)
+        added = part[:, width + g :] + got[:, :width]
         if g:
-            whole = jnp.concatenate([whole, part[:, width : width + g] + got[:, width:]], axis=1)
+            added = jnp.concatenate([added, part[:, width : width + g] + got[:, width:]], axis=1)
+        whole.append(added)
         bit = 4
         while bit < n_pos:
-            whole = whole + swap(whole, "pos", n_pos, bit)
+            added = added + swap(added, "pos", n_pos, bit)
             bit *= 2
-        total.append(whole)
-
-    inverse, sources, pieces = None, [], []
+        total.append(added)
+
+    inverse = inverse_factor(total[0], width)
+    sources, pieces = [], []
     for c in range(CHUNKS):
         mine = total[c][:, :width]
-        if inverse is not None:
-            mine = after(mine, inverse, far)
         near = over(mine, 1)
-        if inverse is None:
-            inverse = inverse_factor(after(total[0], near), width)
         far = over(jnp.concatenate([mine, near], axis=1), 0)
         k = len(sources)
         sources += [mine, near, far]

time: 84 us -> 75.6 us (0.90)
  waiting for transfers between devices: 42.5 us -> 32 us
  starting transfers between devices: 15.1 us -> 19.1 us
  Pallas kernels: 25.4 us -> 23.4 us
    ppermute x8, waiting for transfers between devices: 25.1 us -> 17.9 us  [over(): return lax.ppermute(value, ('pos', 'pix'), pairs)]
    ppermute x4, waiting for transfers between devices: 17.4 us -> 14.2 us  [swap(): return lax.ppermute(value, axis, [(i, i ^ bit) for i in range(size)])]
    ppermute x4, starting transfers between devices: 6.41 us -> 8.95 us  [swap(): return lax.ppermute(value, axis, [(i, i ^ bit) for i in range(size)])]
    pallas_call x1, Pallas kernels: 9.22 us -> 7.27 us  [tall_partial(): pl.pallas_call(tall_kernel, in_specs=[HBM, HBM], out_specs=WHOLE, out_sha...]
    ppermute x8, starting transfers between devices: 8.7 us -> 10.2 us  [over(): return lax.ppermute(value, ('pos', 'pix'), pairs)]
  transfers between devices with their start and end apart: 12 -> 12, of which waited for: 10 -> 11; matrix products, arithmetic and copies ran while one was open for 1% -> 1% of each run, Pallas kernels for 13% -> 15%
where the time goes in v19:
time: 75.6 us; the launch traced here: 75.5 us
  waiting for transfers between devices  32 us (42%)
  Pallas kernels  23.4 us (31%)
  starting transfers between devices  19.1 us (25%)
    ppermute x8, waiting for transfers between devices, over(): return lax.ppermute(value, ('pos', 'pix'), pairs)  17.9 us
    ppermute x4, waiting for transfers between devices, swap(): return lax.ppermute(value, axis, [(i, i ^ bit) for i in range(size)])  14.2 us
    pallas_call x3, Pallas kernels, products(): pl.pallas_call(functools.partial(kernel, plan, grams), in_specs=[TABLE, *...  10.7 us
    ppermute x8, starting transfers between devices, over(): return lax.ppermute(value, ('pos', 'pix'), pairs)  10.2 us
    ppermute x4, starting transfers between devices, swap(): return lax.ppermute(value, axis, [(i, i ^ bit) for i in range(size)])  8.95 us
    pallas_call x1, Pallas kernels, tall_partial(): pl.pallas_call(tall_kernel, in_specs=[HBM, HBM], out_specs=WHOLE, out_sha...  7.27 us
    pallas_call x2, Pallas kernels, finish(): pl.pallas_call(functools.partial(finish_kernel, [piece[1:] for piece in p...  3.41 us
    pallas_call x1, Pallas kernels, inverse_factor(): pl.pallas_call(inverse_kernel, grid=(1,), in_specs=[pl.BlockSpec((rank, L...  2.01 us
  transfers between devices with their start and end apart: 12, of which 11 were waited for; matrix products, arithmetic and copies ran while one was open for 1% of the time, Pallas kernels for 15%

profile of v19, /device:TPU:0, one launch (start us, length us, event | category | flops | bytes accessed | tf_op | source)
XLA Modules:
  0.0 75.5 jit_solution(6659306852526229112)
XLA Ops:
  0.0 7.3 %tall_partial.1 = f32[48,512]{1,0:T(8,128)S(1)} custom-call(f32[512,8192]{1,0:T(8,128)} %x_hbm.7, f32[48,8192]{1,0:T(8,128)} %bitcast.25), custom_call_target="tpu_custom_call" | custom-call | flops 1207959552 | bytes 16777216 | tf_op jit(solution)/shard_map/tall_partial/pallas_call | solution.py:91
  8.8 2.9 %collective-permute-start.1 = (f32[48,512]{1,0:T(8,128)S(1)}, f32[48,512]{1,0:T(8,128)S(1)}, u32[]{:S(2)}, u32[]{:S(2)}) collective-permute-start(f32[48,512]{1,0:T(8,128)S(1)} %add.105.one_ref), channel_id=1, source_target_pairs={{0,2},{1,3},{2,0},{3,1},{4,6},{5,7},{6,4},{7,5},{8,10},{9,11},{10,... | collective-permute-start | bytes 294920 | tf_op jit(solution)/shard_map/ppermute | solution.py:330
  11.8 3.0 %collective-permute-done.1.two_ref = f32[48,512]{1,0:T(8,128)S(1)} collective-permute-done((f32[48,512]{1,0:T(8,128)S(1)}, f32[48,512]{1,0:T(8,128)S(1)}, u32[]{:S(2)}, u32[]{:S(2)}) %collective-permute-start.1) | collective-permute-done | bytes 98336 | tf_op jit(solution)/shard_map/ppermute | solution.py:330
  14.8 3.3 %first_products.1 = (bf16[96,512]{1,0:T(8,128)(2,1)S(1)}, f32[48,128]{1,0:T(8,128)S(1)}, f32[48,2176]{1,0:T(8,128)S(1)}) custom-call(s32[4]{0:T(128)S(1)} %pad_add_fusion.1.which_ref, f32[48,512]{1,0:T(8,128)S(1)} %add.105.one_ref, f32[48,512]{1,0:T(8,128)S(1)} %collective-permute-done.1.two_ref, f32[512,8192]{1,0:T(8,128)} %x_hbm.7), custom_call_target="tpu_custom_call" | custom-call | flops 301989888 | bytes 4194304 | tf_op jit(solution)/shard_map/first_products/pallas_call | solution.py:192
  18.2 1.9 %collective-permute-start.2 = (f32[48,2176]{1,0:T(8,128)S(1)}, f32[48,2176]{1,0:T(8,128)S(1)}, u32[]{:S(2)}, u32[]{:S(2)}) collective-permute-start(f32[48,2176]{1,0:T(8,128)S(1)} %get-tuple-element.13.after_ref), channel_id=1, source_target_pairs={{0,8},{1,5},{2,10},{3,7},{4,12},{5,1},{6,14},{7,3},{8,0},{9,13},{1... | collective-permute-start | bytes 1253384 | tf_op jit(solution)/shard_map/ppermute | solution.py:338
  20.1 4.3 %rest_products.2 = (f32[48,2176]{1,0:T(8,128)S(1)}, f32[48,2048]{1,0:T(8,128)S(1)}) custom-call(s32[8]{0:T(128)S(1)} %stack.98.which_ref, bf16[96,512]{1,0:T(8,128)(2,1)S(1)} %get-tuple-element.11.both_ref, f32[48,128]{1,0:T(8,128)S(1)} %get-tuple-element.12.gram_ref, f32[512,8192]{1,0:T(8,128)} %x_hbm.7, f32[48,2176]{1,0:T(8,128)S(1)} %get-tuple-element.13.after_ref), custom_call_target="tpu_custom_call" | custom-call | flops 603979776 | bytes 8388608 | tf_op jit(solution)/shard_map/rest_products/pallas_call | solution.py:192
  24.5 1.8 %collective-permute-done.2 = f32[48,2176]{1,0:T(8,128)S(1)} collective-permute-done((f32[48,2176]{1,0:T(8,128)S(1)}, f32[48,2176]{1,0:T(8,128)S(1)}, u32[]{:S(2)}, u32[]{:S(2)}) %collective-permute-start.2) | collective-permute-done | bytes 417824 | tf_op jit(solution)/shard_map/ppermute | solution.py:338
  26.3 1.8 %collective-permute-start.3 = (f32[48,1152]{1,0:T(8,128)S(1)}, f32[48,1152]{1,0:T(8,128)S(1)}, u32[]{:S(2)}, u32[]{:S(2)}) collective-permute-start(f32[48,1152]{1,0:T(8,128)S(1)} %slice.33), channel_id=1, source_target_pairs={{0,4},{1,9},{2,6},{3,11},{4,0},{5,13},{6,2},{7,15},{8,12},{9,1},{1... | collective-permute-start | bytes 663560 | tf_op jit(solution)/shard_map/ppermute | solution.py:338
  28.2 1.6 %collective-permute-start.5 = (f32[48,2048]{1,0:T(8,128)S(1)}, f32[48,2048]{1,0:T(8,128)S(1)}, u32[]{:S(2)}, u32[]{:S(2)}) collective-permute-start(f32[48,2048]{1,0:T(8,128)S(1)} %get-tuple-element.16), channel_id=1, source_target_pairs={{0,8},{1,5},{2,10},{3,7},{4,12},{5,1},{6,14},{7,3},{8,0},{9,13},{1... | collective-permute-start | bytes 1179656 | tf_op jit(solution)/shard_map/ppermute | solution.py:338
  29.8 4.9 %collective-permute-done.3 = f32[48,1152]{1,0:T(8,128)S(1)} collective-permute-done((f32[48,1152]{1,0:T(8,128)S(1)}, f32[48,1152]{1,0:T(8,128)S(1)}, u32[]{:S(2)}, u32[]{:S(2)}) %collective-permute-start.3) | collective-permute-done | bytes 221216 | tf_op jit(solution)/shard_map/ppermute | solution.py:338
  34.8 3.1 %rest_products.3 = f32[48,2048]{1,0:T(8,128)S(1)} custom-call(s32[4]{0:T(128)S(1)} %pad_add_fusion.2.which_ref, bf16[96,512]{1,0:T(8,128)(2,1)S(1)} %get-tuple-element.11.both_ref, f32[48,128]{1,0:T(8,128)S(1)} %get-tuple-element.12.gram_ref, f32[512,8192]{1,0:T(8,128)} %x_hbm.7, f32[48,1152]{1,0:T(8,128)S(1)} %pad_maximum_fusion.2.after_ref), custom_call_target="tpu_custom_call" | custom-call | flops 301989888 | bytes 4194304 | tf_op jit(solution)/shard_map/rest_products/pallas_call | solution.py:192
  37.9 1.8 %collective-permute-start.6 = (f32[48,1024]{1,0:T(8,128)S(1)}, f32[48,1024]{1,0:T(8,128)S(1)}, u32[]{:S(2)}, u32[]{:S(2)}) collective-permute-start(f32[48,1024]{1,0:T(8,128)S(1)} %slice.38), channel_id=1, source_target_pairs={{0,4},{1,9},{2,6},{3,11},{4,0},{5,13},{6,2},{7,15},{8,12},{9,1},{1... | collective-permute-start | bytes 589832 | tf_op jit(solution)/shard_map/ppermute | solution.py:338
  39.7 2.6 %collective-permute-start.4 = (f32[48,1152]{1,0:T(8,128)S(1)}, f32[48,1152]{1,0:T(8,128)S(1)}, u32[]{:S(2)}, u32[]{:S(2)}) collective-permute-start(f32[48,1152]{1,0:T(8,128)S(1)} %pad_maximum_fusion.2.after_ref), channel_id=1, source_target_pairs={{0,16},{4,20},{8,24},{12,28},{16,0},{20,4},{24,8},{28,12},{1,17},{... | collective-permute-start | bytes 663560 | tf_op jit(solution)/shard_map/ppermute | solution.py:330
  43.7 2.9 %collective-permute-start.7 = (f32[48,1024]{1,0:T(8,128)S(1)}, f32[48,1024]{1,0:T(8,128)S(1)}, u32[]{:S(2)}, u32[]{:S(2)}) collective-permute-start(f32[48,1024]{1,0:T(8,128)S(1)} %slice_add_fusion), channel_id=1, source_target_pairs={{0,16},{4,20},{8,24},{12,28},{16,0},{20,4},{24,8},{28,12},{1,17},{... | collective-permute-start | bytes 589832 | tf_op jit(solution)/shard_map/ppermute | solution.py:330
  46.6 9.5 %collective-permute-done.4 = f32[48,1152]{1,0:T(8,128)S(1)} collective-permute-done((f32[48,1152]{1,0:T(8,128)S(1)}, f32[48,1152]{1,0:T(8,128)S(1)}, u32[]{:S(2)}, u32[]{:S(2)}) %collective-permute-start.4) | collective-permute-done | bytes 221216 | tf_op jit(solution)/shard_map/ppermute | solution.py:330
  56.1 1.4 %collective-permute-start.10 = (f32[48,1024]{1,0:T(8,128)S(1)}, f32[48,1024]{1,0:T(8,128)S(1)}, u32[]{:S(2)}, u32[]{:S(2)}) collective-permute-start(f32[48,1024]{1,0:T(8,128)S(1)} %slice.39.refs_0_), channel_id=1, source_target_pairs={{0,4},{1,9},{2,6},{3,11},{4,0},{5,13},{6,2},{7,15},{8,12},{9,1},{1... | collective-permute-start | bytes 589832 | tf_op jit(solution)/shard_map/ppermute | solution.py:338
  58.2 1.4 %collective-permute-start.8 = (f32[48,1024]{1,0:T(8,128)S(1)}, f32[48,1024]{1,0:T(8,128)S(1)}, u32[]{:S(2)}, u32[]{:S(2)}) collective-permute-start(f32[48,1024]{1,0:T(8,128)S(1)} %add.117.refs_3_), channel_id=1, source_target_pairs={{0,4},{1,9},{2,6},{3,11},{4,0},{5,13},{6,2},{7,15},{8,12},{9,1},{1... | collective-permute-start | bytes 589832 | tf_op jit(solution)/shard_map/ppermute | solution.py:338
  59.6 2.3 %collective-permute-done.10.refs_1_ = f32[48,1024]{1,0:T(8,128)S(1)} collective-permute-done((f32[48,1024]{1,0:T(8,128)S(1)}, f32[48,1024]{1,0:T(8,128)S(1)}, u32[]{:S(2)}, u32[]{:S(2)}) %collective-permute-start.10) | collective-permute-done | bytes 196640 | tf_op jit(solution)/shard_map/ppermute | solution.py:338
  62.0 3.4 %collective-permute-done.8.refs_4_ = f32[48,1024]{1,0:T(8,128)S(1)} collective-permute-done((f32[48,1024]{1,0:T(8,128)S(1)}, f32[48,1024]{1,0:T(8,128)S(1)}, u32[]{:S(2)}, u32[]{:S(2)}) %collective-permute-start.8) | collective-permute-done | bytes 196640 | tf_op jit(solution)/shard_map/ppermute | solution.py:338
  65.9 2.0 %inverse_factor.1.inverse_ref = f32[48,48]{1,0:T(8,128)S(1)} custom-call(f32[48,1152]{1,0:T(8,128)S(1)} %fusion.gram_ref), custom_call_target="tpu_custom_call" | custom-call | flops 20000000 | bytes 49152 | tf_op jit(solution)/shard_map/inverse_factor/pallas_call | solution.py:267
  67.9 1.9 %collective-permute-done.11.refs_2_ = f32[48,2048]{1,0:T(8,128)S(1)} collective-permute-done((f32[48,2048]{1,0:T(8,128)S(1)}, f32[48,2048]{1,0:T(8,128)S(1)}, u32[]{:S(2)}, u32[]{:S(2)}) %collective-permute-start.11) | collective-permute-done | bytes 393248 | tf_op jit(solution)/shard_map/ppermute | solution.py:338
  69.7 1.9 %finish.2.refs_1_ = f32[48,8192]{1,0:T(8,128)} custom-call(s32[6]{0:T(128)S(1)} %stack.115.where_ref, f32[48,48]{1,0:T(8,128)S(1)} %inverse_factor.1.inverse_ref, f32[48,1024]{1,0:T(8,128)S(1)} %slice.39.refs_0_, f32[48,1024]{1,0:T(8,128)S(1)} %collective-permute-done.10.refs_1_, f32[48,2048]{1,0:T(8,128)S(1)} %collective-permute-done.11.refs_2_, ...), custom_call_target="tpu_custom_call" | custom-call | flops 84934656 | bytes 2359296 | tf_op jit(solution)/shard_map/finish/pallas_call | solution.py:308
  71.6 2.3 %collective-permute-done.9.refs_0_ = f32[48,2048]{1,0:T(8,128)S(1)} collective-permute-done((f32[48,2048]{1,0:T(8,128)S(1)}, f32[48,2048]{1,0:T(8,128)S(1)}, u32[]{:S(2)}, u32[]{:S(2)}) %collective-permute-start.9) | collective-permute-done | bytes 393248 | tf_op jit(solution)/shard_map/ppermute | solution.py:338
  73.9 1.5 %finish.3 = f32[48,8192]{1,0:T(8,128)} custom-call(s32[2]{0:T(128)S(1)} %pad_add_fusion.where_ref, f32[48,48]{1,0:T(8,128)S(1)} %inverse_factor.1.inverse_ref, f32[48,2048]{1,0:T(8,128)S(1)} %collective-permute-done.9.refs_0_, f32[48,8192]{1,0:T(8,128)} %finish.2.refs_1_), custom_call_target="tpu_custom_call", output_to_operand_aliasing={{}: (3, {})} | custom-call | flops 28311552 | bytes 786432 | tf_op jit(solution)/shard_map/finish/pallas_call | solution.py:308
  (26 shorter events, 4.6 us)
Async XLA Ops:
  7.3 1.5 %collective-permute-start = (f32[48,512]{1,0:T(8,128)S(1)}, f32[48,512]{1,0:T(8,128)S(1)}, u32[]{:S(2)}, u32[]{:S(2)}) collective-permute-start(f32[48,512]{1,0:T(8,128)S(1)} %tall_partial.1), channel_id=1, source_target_pairs={{0,1},{1,0},{2,3},{3,2},{4,5},{5,4},{6,7},{7,6},{8,9},{9,8},{10,11... | collective-permute-start | bytes 294920 | tf_op jit(solution)/shard_map/ppermute | solution.py:330
  8.8 6.0 %collective-permute-start.1 = (f32[48,512]{1,0:T(8,128)S(1)}, f32[48,512]{1,0:T(8,128)S(1)}, u32[]{:S(2)}, u32[]{:S(2)}) collective-permute-start(f32[48,512]{1,0:T(8,128)S(1)} %add.105.one_ref), channel_id=1, source_target_pairs={{0,2},{1,3},{2,0},{3,1},{4,6},{5,7},{6,4},{7,5},{8,10},{9,11},{10,... | collective-permute-start | bytes 294920 | tf_op jit(solution)/shard_map/ppermute | solution.py:330
  18.2 8.1 %collective-permute-start.2 = (f32[48,2176]{1,0:T(8,128)S(1)}, f32[48,2176]{1,0:T(8,128)S(1)}, u32[]{:S(2)}, u32[]{:S(2)}) collective-permute-start(f32[48,2176]{1,0:T(8,128)S(1)} %get-tuple-element.13.after_ref), channel_id=1, source_target_pairs={{0,8},{1,5},{2,10},{3,7},{4,12},{5,1},{6,14},{7,3},{8,0},{9,13},{1... | collective-permute-start | bytes 1253384 | tf_op jit(solution)/shard_map/ppermute | solution.py:338
  26.3 8.4 %collective-permute-start.3 = (f32[48,1152]{1,0:T(8,128)S(1)}, f32[48,1152]{1,0:T(8,128)S(1)}, u32[]{:S(2)}, u32[]{:S(2)}) collective-permute-start(f32[48,1152]{1,0:T(8,128)S(1)} %slice.33), channel_id=1, source_target_pairs={{0,4},{1,9},{2,6},{3,11},{4,0},{5,13},{6,2},{7,15},{8,12},{9,1},{1... | collective-permute-start | bytes 663560 | tf_op jit(solution)/shard_map/ppermute | solution.py:338
  28.2 9.6 %collective-permute-start.5 = (f32[48,2048]{1,0:T(8,128)S(1)}, f32[48,2048]{1,0:T(8,128)S(1)}, u32[]{:S(2)}, u32[]{:S(2)}) collective-permute-start(f32[48,2048]{1,0:T(8,128)S(1)} %get-tuple-element.16), channel_id=1, source_target_pairs={{0,8},{1,5},{2,10},{3,7},{4,12},{5,1},{6,14},{7,3},{8,0},{9,13},{1... | collective-permute-start | bytes 1179656 | tf_op jit(solution)/shard_map/ppermute | solution.py:338
  37.9 5.7 %collective-permute-start.6 = (f32[48,1024]{1,0:T(8,128)S(1)}, f32[48,1024]{1,0:T(8,128)S(1)}, u32[]{:S(2)}, u32[]{:S(2)}) collective-permute-start(f32[48,1024]{1,0:T(8,128)S(1)} %slice.38), channel_id=1, source_target_pairs={{0,4},{1,9},{2,6},{3,11},{4,0},{5,13},{6,2},{7,15},{8,12},{9,1},{1... | collective-permute-start | bytes 589832 | tf_op jit(solution)/shard_map/ppermute | solution.py:338
  39.7 16.3 %collective-permute-start.4 = (f32[48,1152]{1,0:T(8,128)S(1)}, f32[48,1152]{1,0:T(8,128)S(1)}, u32[]{:S(2)}, u32[]{:S(2)}) collective-permute-start(f32[48,1152]{1,0:T(8,128)S(1)} %pad_maximum_fusion.2.after_ref), channel_id=1, source_target_pairs={{0,16},{4,20},{8,24},{12,28},{16,0},{20,4},{24,8},{28,12},{1,17},{... | collective-permute-start | bytes 663560 | tf_op jit(solution)/shard_map/ppermute | solution.py:330
  43.7 14.5 %collective-permute-start.7 = (f32[48,1024]{1,0:T(8,128)S(1)}, f32[48,1024]{1,0:T(8,128)S(1)}, u32[]{:S(2)}, u32[]{:S(2)}) collective-permute-start(f32[48,1024]{1,0:T(8,128)S(1)} %slice_add_fusion), channel_id=1, source_target_pairs={{0,16},{4,20},{8,24},{12,28},{16,0},{20,4},{24,8},{28,12},{1,17},{... | collective-permute-start | bytes 589832 | tf_op jit(solution)/shard_map/ppermute | solution.py:330
  56.1 5.7 %collective-permute-start.10 = (f32[48,1024]{1,0:T(8,128)S(1)}, f32[48,1024]{1,0:T(8,128)S(1)}, u32[]{:S(2)}, u32[]{:S(2)}) collective-permute-start(f32[48,1024]{1,0:T(8,128)S(1)} %slice.39.refs_0_), channel_id=1, source_target_pairs={{0,4},{1,9},{2,6},{3,11},{4,0},{5,13},{6,2},{7,15},{8,12},{9,1},{1... | collective-permute-start | bytes 589832 | tf_op jit(solution)/shard_map/ppermute | solution.py:338
  58.2 7.1 %collective-permute-start.8 = (f32[48,1024]{1,0:T(8,128)S(1)}, f32[48,1024]{1,0:T(8,128)S(1)}, u32[]{:S(2)}, u32[]{:S(2)}) collective-permute-start(f32[48,1024]{1,0:T(8,128)S(1)} %add.117.refs_3_), channel_id=1, source_target_pairs={{0,4},{1,9},{2,6},{3,11},{4,0},{5,13},{6,2},{7,15},{8,12},{9,1},{1... | collective-permute-start | bytes 589832 | tf_op jit(solution)/shard_map/ppermute | solution.py:338
  61.9 7.8 %collective-permute-start.11 = (f32[48,2048]{1,0:T(8,128)S(1)}, f32[48,2048]{1,0:T(8,128)S(1)}, u32[]{:S(2)}, u32[]{:S(2)}) collective-permute-start(f32[48,2048]{1,0:T(8,128)S(1)} %pad_maximum_fusion.1), channel_id=1, source_target_pairs={{0,8},{1,5},{2,10},{3,7},{4,12},{5,1},{6,14},{7,3},{8,0},{9,13},{1... | collective-permute-start | bytes 1179656 | tf_op jit(solution)/shard_map/ppermute | solution.py:338
  65.3 8.6 %collective-permute-start.9 = (f32[48,2048]{1,0:T(8,128)S(1)}, f32[48,2048]{1,0:T(8,128)S(1)}, u32[]{:S(2)}, u32[]{:S(2)}) collective-permute-start(f32[48,2048]{1,0:T(8,128)S(1)} %pad_maximum_fusion), channel_id=1, source_target_pairs={{0,8},{1,5},{2,10},{3,7},{4,12},{5,1},{6,14},{7,3},{8,0},{9,13},{1... | collective-permute-start | bytes 1179656 | tf_op jit(solution)/shard_map/ppermute | solution.py:338

commit v20 on v16

--- a/solution.py
+++ b/solution.py
@@ -47,7 +47,7 @@
         use(k)
 
 
-def tall_kernel(x_hbm, s_hbm, out_ref, x_buf, s_buf, head_buf, rest_buf, x_sems, s_sems):
+def tall_kernel(x_hbm, s_hbm, out_ref, x_buf, s_buf, head_buf, rest_buf, acc, x_sems, s_sems):
     blocks, _, unit = x_buf.shape
     rank = s_hbm.shape[0]
 
@@ -64,17 +64,17 @@
     for k in range(blocks):
         for copy in copies(k):
             copy.wait()
-        s_head, s_rest = split(s_buf[k])
-        s_both = jnp.concatenate([s_head, s_rest], axis=0)
+        s_both = jnp.concatenate(split(s_buf[k]), axis=0)
         x_head, x_rest = split(x_buf[k])
         head_buf[k] = x_head
         rest_buf[k] = x_rest
-        both = dot(s_both, x_head, LAST)
-        part = both[:rank] + (both[rank:] + dot(s_head, x_rest, LAST))
+        part = dot(x_head, s_both, LAST) + dot(x_rest, s_both, LAST)
         if k == 0:
-            out_ref[...] = part
+            acc[...] = part
         else:
-            out_ref[...] += part
+            acc[...] += part
+    both = acc[...].T
+    out_ref[...] = both[:rank] + both[rank:]
 
 
 def tall_partial(probes, sketch_t):
@@ -92,6 +92,7 @@
             pltpu.VMEM((blocks, rank, unit), F32),
             pltpu.VMEM((blocks, rows, unit), BF16),
             pltpu.VMEM((blocks, rows, unit), BF16),
+            pltpu.VMEM((rows, 2 * rank), F32),
             pltpu.SemaphoreType.DMA((blocks,)),
             pltpu.SemaphoreType.DMA((blocks,)),
         ],
@@ -321,10 +322,18 @@
         return lax.ppermute(value, axis, [(i, i ^ bit) for i in range(size)])
 
     def over(value, bit):
-        return swap(value, "pos", n_pos, bit)
+        if bit > 2:
+            return swap(value, "pos", n_pos, bit)
+        pairs = [
+            (i * n_pix + j, (i ^ (bit if j % 2 else 3 - bit)) * n_pix + j)
+            for i in range(n_pos)
+            for j in range(n_pix)
+        ]
+        return lax.ppermute(value, ("pos", "pix"), pairs)
 
     me = lax.axis_index("pos").astype(jnp.int32)
-    near, far = me & 1, (me >> 1) & 1
+    odd = lax.axis_index("pix").astype(jnp.int32) & 1
+    near, far = (me >> (1 - odd)) & 1, (me >> odd) & 1
     cols = probes.shape[1]
     width = cols // (8 * CHUNKS)
 

time: 71.3 us -> 73.1 us (1.025)
  Pallas kernels: 25 us -> 26.5 us
  starting transfers between devices: 24.1 us -> 25 us
    ppermute x0 -> x16, starting transfers between devices: none -> 18.2 us  [over(): return lax.ppermute(value, ('pos', 'pix'), pairs)]
    ppermute x20 -> x4, starting transfers between devices: 24.1 us -> 6.86 us  [swap(): return lax.ppermute(value, axis, [(i, i ^ bit) for i in range(size)])]
    ppermute x20 -> x4, waiting for transfers between devices: 20.9 us -> 10 us  [swap(): return lax.ppermute(value, axis, [(i, i ^ bit) for i in range(size)])]
    ppermute x0 -> x16, waiting for transfers between devices: none -> 10.4 us  [over(): return lax.ppermute(value, ('pos', 'pix'), pairs)]
    pallas_call x1, Pallas kernels: 7.27 us -> 8.72 us  [tall_partial(): pl.pallas_call(tall_kernel, in_specs=[HBM, HBM], out_specs=WHOLE, out_sha...]
  transfers between devices with their start and end apart: 20 -> 20, of which waited for: 10 -> 11; matrix products, arithmetic and copies ran while one was open for 1% -> 1% of each run, Pallas kernels for 18% -> 18%
where the time goes in v20:
time: 73.1 us; the launch traced here: 73 us
  Pallas kernels  26.5 us (36%)
  starting transfers between devices  25 us (34%)
  waiting for transfers between devices  20.4 us (28%)
    ppermute x16, starting transfers between devices, over(): return lax.ppermute(value, ('pos', 'pix'), pairs)  18.2 us
    pallas_call x3, Pallas kernels, products(): pl.pallas_call(functools.partial(kernel, plan, grams), in_specs=[TABLE, *...  11 us
    ppermute x16, waiting for transfers between devices, over(): return lax.ppermute(value, ('pos', 'pix'), pairs)  10.4 us
    ppermute x4, waiting for transfers between devices, swap(): return lax.ppermute(value, axis, [(i, i ^ bit) for i in range(size)])  10 us
    pallas_call x1, Pallas kernels, tall_partial(): pl.pallas_call(tall_kernel, in_specs=[HBM, HBM], out_specs=WHOLE, out_sha...  8.72 us
    ppermute x4, starting transfers between devices, swap(): return lax.ppermute(value, axis, [(i, i ^ bit) for i in range(size)])  6.86 us
    pallas_call x3, Pallas kernels, finish(): pl.pallas_call(functools.partial(finish_kernel, [piece[1:] for piece in p...  4.72 us
    pallas_call x1, Pallas kernels, inverse_factor(): pl.pallas_call(inverse_kernel, grid=(1,), in_specs=[pl.BlockSpec((rank, L...  2.01 us
  transfers between devices with their start and end apart: 20, of which 11 were waited for; matrix products, arithmetic and copies ran while one was open for 1% of the time, Pallas kernels for 18%

profile of v20, /device:TPU:0, one launch (start us, length us, event | category | flops | bytes accessed | tf_op | source)
XLA Modules:
  0.0 73.0 jit_solution(16253538069641570086)
XLA Ops:
  0.0 8.7 %tall_partial.1 = f32[48,512]{1,0:T(8,128)S(1)} custom-call(f32[512,8192]{1,0:T(8,128)} %x_hbm.7, f32[48,8192]{1,0:T(8,128)} %bitcast.17), custom_call_target="tpu_custom_call" | custom-call | flops 1207959552 | bytes 16777216 | tf_op jit(solution)/shard_map/tall_partial/pallas_call | solution.py:85
  10.2 2.9 %collective-permute-start.1 = (f32[48,512]{1,0:T(8,128)S(1)}, f32[48,512]{1,0:T(8,128)S(1)}, u32[]{:S(2)}, u32[]{:S(2)}) collective-permute-start(f32[48,512]{1,0:T(8,128)S(1)} %add.153.one_ref), channel_id=1, source_target_pairs={{0,2},{1,3},{2,0},{3,1},{4,6},{5,7},{6,4},{7,5},{8,10},{9,11},{10,... | collective-permute-start | bytes 294920 | tf_op jit(solution)/shard_map/ppermute | solution.py:322
  13.2 3.0 %collective-permute-done.1.two_ref = f32[48,512]{1,0:T(8,128)S(1)} collective-permute-done((f32[48,512]{1,0:T(8,128)S(1)}, f32[48,512]{1,0:T(8,128)S(1)}, u32[]{:S(2)}, u32[]{:S(2)}) %collective-permute-start.1) | collective-permute-done | bytes 98336 | tf_op jit(solution)/shard_map/ppermute | solution.py:322
  16.3 3.4 %first_products.1 = (bf16[96,512]{1,0:T(8,128)(2,1)S(1)}, f32[48,128]{1,0:T(8,128)S(1)}, f32[48,1152]{1,0:T(8,128)S(1)}, f32[48,1024]{1,0:T(8,128)S(1)}) custom-call(s32[4]{0:T(128)S(1)} %pad_add_fusion.2.which_ref, f32[48,512]{1,0:T(8,128)S(1)} %add.153.one_ref, f32[48,512]{1,0:T(8,128)S(1)} %collective-permute-done.1.two_ref, f32[512,8192]{1,0:T(8,128)} %x_hbm.7), custom_call_target="tpu_custom_call" | custom-call | flops 301989888 | bytes 4194304 | tf_op jit(solution)/shard_map/first_products/pallas_call | solution.py:184
  19.6 1.8 %collective-permute-start.6 = (f32[48,1024]{1,0:T(8,128)S(1)}, f32[48,1024]{1,0:T(8,128)S(1)}, u32[]{:S(2)}, u32[]{:S(2)}) collective-permute-start(f32[48,1024]{1,0:T(8,128)S(1)} %get-tuple-element.29), channel_id=1, source_target_pairs={{0,4},{1,9},{2,6},{3,11},{4,0},{5,13},{6,2},{7,15},{8,12},{9,1},{1... | collective-permute-start | bytes 589832 | tf_op jit(solution)/shard_map/ppermute | solution.py:332
  21.5 1.6 %collective-permute-start.2 = (f32[48,1152]{1,0:T(8,128)S(1)}, f32[48,1152]{1,0:T(8,128)S(1)}, u32[]{:S(2)}, u32[]{:S(2)}) collective-permute-start(f32[48,1152]{1,0:T(8,128)S(1)} %get-tuple-element.22.after_ref), channel_id=1, source_target_pairs={{0,8},{1,5},{2,10},{3,7},{4,12},{5,1},{6,14},{7,3},{8,0},{9,13},{1... | collective-permute-start | bytes 663560 | tf_op jit(solution)/shard_map/ppermute | solution.py:332
  23.1 4.6 %rest_products.3 = (f32[48,1152]{1,0:T(8,128)S(1)}, f32[48,1024]{1,0:T(8,128)S(1)}, f32[48,1024]{1,0:T(8,128)S(1)}, f32[48,1024]{1,0:T(8,128)S(1)}) custom-call(s32[8]{0:T(128)S(1)} %stack.101.which_ref, bf16[96,512]{1,0:T(8,128)(2,1)S(1)} %get-tuple-element.20.both_ref, f32[48,128]{1,0:T(8,128)S(1)} %get-tuple-element.21.gram_ref, f32[512,8192]{1,0:T(8,128)} %x_hbm.7, ...), custom_call_target="tpu_custom_call" | custom-call | flops 603979776 | bytes 8388608 | tf_op jit(solution)/shard_map/rest_products/pallas_call | solution.py:184
  28.5 1.9 %collective-permute-start.7 = (f32[48,512]{1,0:T(8,128)S(1)}, f32[48,512]{1,0:T(8,128)S(1)}, u32[]{:S(2)}, u32[]{:S(2)}) collective-permute-start(f32[48,512]{1,0:T(8,128)S(1)} %slice.69), channel_id=1, source_target_pairs={{0,8},{1,5},{2,10},{3,7},{4,12},{5,1},{6,14},{7,3},{8,0},{9,13},{1... | collective-permute-start | bytes 294920 | tf_op jit(solution)/shard_map/ppermute | solution.py:332
  30.5 1.6 %collective-permute-start.5 = (f32[48,640]{1,0:T(8,128)S(1)}, f32[48,640]{1,0:T(8,128)S(1)}, u32[]{:S(2)}, u32[]{:S(2)}) collective-permute-start(f32[48,640]{1,0:T(8,128)S(1)} %slice.64), channel_id=1, source_target_pairs={{0,4},{1,9},{2,6},{3,11},{4,0},{5,13},{6,2},{7,15},{8,12},{9,1},{1... | collective-permute-start | bytes 368648 | tf_op jit(solution)/shard_map/ppermute | solution.py:332
  32.1 3.1 %rest_products.2 = (f32[48,1024]{1,0:T(8,128)S(1)}, f32[48,1024]{1,0:T(8,128)S(1)}) custom-call(s32[4]{0:T(128)S(1)} %pad_add_fusion.1.which_ref, bf16[96,512]{1,0:T(8,128)(2,1)S(1)} %get-tuple-element.20.both_ref, f32[48,128]{1,0:T(8,128)S(1)} %get-tuple-element.21.gram_ref, f32[512,8192]{1,0:T(8,128)} %x_hbm.7, f32[48,1152]{1,0:T(8,128)S(1)} %collective-permute-done.2.after_ref), custom_call_target="tpu_custom_call" | custom-call | flops 301989888 | bytes 4194304 | tf_op jit(solution)/shard_map/rest_products/pallas_call | solution.py:184
  35.9 1.2 %collective-permute-start.8 = (f32[48,512]{1,0:T(8,128)S(1)}, f32[48,512]{1,0:T(8,128)S(1)}, u32[]{:S(2)}, u32[]{:S(2)}) collective-permute-start(f32[48,512]{1,0:T(8,128)S(1)} %slice.61), channel_id=1, source_target_pairs={{0,4},{1,9},{2,6},{3,11},{4,0},{5,13},{6,2},{7,15},{8,12},{9,1},{1... | collective-permute-start | bytes 294920 | tf_op jit(solution)/shard_map/ppermute | solution.py:332
  37.2 2.6 %collective-permute-start.11 = (f32[48,1152]{1,0:T(8,128)S(1)}, f32[48,1152]{1,0:T(8,128)S(1)}, u32[]{:S(2)}, u32[]{:S(2)}) collective-permute-start(f32[48,1152]{1,0:T(8,128)S(1)} %pad_maximum_fusion), channel_id=1, source_target_pairs={{0,16},{4,20},{8,24},{12,28},{16,0},{20,4},{24,8},{28,12},{1,17},{... | collective-permute-start | bytes 663560 | tf_op jit(solution)/shard_map/ppermute | solution.py:322
  40.8 5.3 %collective-permute-done.9 = f32[48,512]{1,0:T(8,128)S(1)} collective-permute-done((f32[48,512]{1,0:T(8,128)S(1)}, f32[48,512]{1,0:T(8,128)S(1)}, u32[]{:S(2)}, u32[]{:S(2)}) %collective-permute-start.9) | collective-permute-done | bytes 98336 | tf_op jit(solution)/shard_map/ppermute | solution.py:332
  47.0 5.2 %collective-permute-done.11 = f32[48,1152]{1,0:T(8,128)S(1)} collective-permute-done((f32[48,1152]{1,0:T(8,128)S(1)}, f32[48,1152]{1,0:T(8,128)S(1)}, u32[]{:S(2)}, u32[]{:S(2)}) %collective-permute-start.11) | collective-permute-done | bytes 221216 | tf_op jit(solution)/shard_map/ppermute | solution.py:322
  52.3 2.2 %collective-permute-start.17 = (f32[48,512]{1,0:T(8,128)S(1)}, f32[48,512]{1,0:T(8,128)S(1)}, u32[]{:S(2)}, u32[]{:S(2)}) collective-permute-start(f32[48,512]{1,0:T(8,128)S(1)} %get-tuple-element.35), channel_id=1, source_target_pairs={{0,8},{1,5},{2,10},{3,7},{4,12},{5,1},{6,14},{7,3},{8,0},{9,13},{1... | collective-permute-start | bytes 294920 | tf_op jit(solution)/shard_map/ppermute | solution.py:332
  55.0 2.0 %inverse_factor.1.inverse_ref = f32[48,48]{1,0:T(8,128)S(1)} custom-call(f32[48,1152]{1,0:T(8,128)S(1)} %fusion.1.gram_ref.refs_0_), custom_call_target="tpu_custom_call" | custom-call | flops 20000000 | bytes 49152 | tf_op jit(solution)/shard_map/inverse_factor/pallas_call | solution.py:259
  59.1 1.3 %collective-permute-start.19 = (f32[48,1024]{1,0:T(8,128)S(1)}, f32[48,1024]{1,0:T(8,128)S(1)}, u32[]{:S(2)}, u32[]{:S(2)}) collective-permute-start(f32[48,1024]{1,0:T(8,128)S(1)} %pad_maximum_fusion.5), channel_id=1, source_target_pairs={{0,4},{1,9},{2,6},{3,11},{4,0},{5,13},{6,2},{7,15},{8,12},{9,1},{1... | collective-permute-start | bytes 589832 | tf_op jit(solution)/shard_map/ppermute | solution.py:332
  60.4 1.8 %collective-permute-start.18 = (f32[48,1024]{1,0:T(8,128)S(1)}, f32[48,1024]{1,0:T(8,128)S(1)}, u32[]{:S(2)}, u32[]{:S(2)}) collective-permute-start(f32[48,1024]{1,0:T(8,128)S(1)} %pad_maximum_fusion.4), channel_id=1, source_target_pairs={{0,8},{1,5},{2,10},{3,7},{4,12},{5,1},{6,14},{7,3},{8,0},{9,13},{1... | collective-permute-start | bytes 589832 | tf_op jit(solution)/shard_map/ppermute | solution.py:332
  62.2 1.9 %collective-permute-done.14.refs_2_ = f32[48,512]{1,0:T(8,128)S(1)} collective-permute-done((f32[48,512]{1,0:T(8,128)S(1)}, f32[48,512]{1,0:T(8,128)S(1)}, u32[]{:S(2)}, u32[]{:S(2)}) %collective-permute-start.14) | collective-permute-done | bytes 98336 | tf_op jit(solution)/shard_map/ppermute | solution.py:332
  64.1 1.0 %collective-permute-start.15 = (f32[48,1024]{1,0:T(8,128)S(1)}, f32[48,1024]{1,0:T(8,128)S(1)}, u32[]{:S(2)}, u32[]{:S(2)}) collective-permute-start(f32[48,1024]{1,0:T(8,128)S(1)} %pad_maximum_fusion.3), channel_id=1, source_target_pairs={{0,4},{1,9},{2,6},{3,11},{4,0},{5,13},{6,2},{7,15},{8,12},{9,1},{1... | collective-permute-start | bytes 589832 | tf_op jit(solution)/shard_map/ppermute | solution.py:332
  66.0 1.2 %collective-permute-done.19.refs_4_ = f32[48,1024]{1,0:T(8,128)S(1)} collective-permute-done((f32[48,1024]{1,0:T(8,128)S(1)}, f32[48,1024]{1,0:T(8,128)S(1)}, u32[]{:S(2)}, u32[]{:S(2)}) %collective-permute-start.19) | collective-permute-done | bytes 196640 | tf_op jit(solution)/shard_map/ppermute | solution.py:332
  68.2 1.7 %finish.3.refs_3_ = f32[48,8192]{1,0:T(8,128)} custom-call(s32[8]{0:T(128)S(1)} %stack.103.where_ref, f32[48,48]{1,0:T(8,128)S(1)} %inverse_factor.1.inverse_ref, f32[48,1152]{1,0:T(8,128)S(1)} %fusion.1.gram_ref.refs_0_, f32[48,512]{1,0:T(8,128)S(1)} %collective-permute-done.16.refs_1_, f32[48,512]{1,0:T(8,128)S(1)} %collective-permute-done.17.refs_2_, ...), custom_call_target="tpu_custom_call" | custom-call | flops 56623104 | bytes 1572864 | tf_op jit(solution)/shard_map/finish/pallas_call | solution.py:300
  69.9 1.5 %finish.4.refs_2_ = f32[48,8192]{1,0:T(8,128)} custom-call(s32[4]{0:T(128)S(1)} %pad_add_fusion.3.where_ref, f32[48,48]{1,0:T(8,128)S(1)} %inverse_factor.1.inverse_ref, f32[48,1024]{1,0:T(8,128)S(1)} %fusion.refs_0_, f32[48,512]{1,0:T(8,128)S(1)} %collective-permute-done.12.refs_1_, ...), custom_call_target="tpu_custom_call", output_to_operand_aliasing={{}: (5, {})} | custom-call | flops 28311552 | bytes 786432 | tf_op jit(solution)/shard_map/finish/pallas_call | solution.py:300
  71.5 1.5 %finish.5 = f32[48,8192]{1,0:T(8,128)} custom-call(s32[4]{0:T(128)S(1)} %pad_add_fusion.where_ref, f32[48,48]{1,0:T(8,128)S(1)} %inverse_factor.1.inverse_ref, f32[48,1024]{1,0:T(8,128)S(1)} %collective-permute-done.13.refs_0_, f32[48,1024]{1,0:T(8,128)S(1)} %collective-permute-done.15.refs_1_, f32[48,8192]{1,0:T(8,128)} %finish.4.refs_2_), custom_call_target="tpu_custom_call", output_to_operand_aliasing={{}: (4, {})} | custom-call | flops 28311552 | bytes 786432 | tf_op jit(solution)/shard_map/finish/pallas_call | solution.py:300
  (54 shorter events, 9.8 us)
Async XLA Ops:
  8.7 1.5 %collective-permute-start = (f32[48,512]{1,0:T(8,128)S(1)}, f32[48,512]{1,0:T(8,128)S(1)}, u32[]{:S(2)}, u32[]{:S(2)}) collective-permute-start(f32[48,512]{1,0:T(8,128)S(1)} %tall_partial.1), channel_id=1, source_target_pairs={{0,1},{1,0},{2,3},{3,2},{4,5},{5,4},{6,7},{7,6},{8,9},{9,8},{10,11... | collective-permute-start | bytes 294920 | tf_op jit(solution)/shard_map/ppermute | solution.py:322
  10.2 6.1 %collective-permute-start.1 = (f32[48,512]{1,0:T(8,128)S(1)}, f32[48,512]{1,0:T(8,128)S(1)}, u32[]{:S(2)}, u32[]{:S(2)}) collective-permute-start(f32[48,512]{1,0:T(8,128)S(1)} %add.153.one_ref), channel_id=1, source_target_pairs={{0,2},{1,3},{2,0},{3,1},{4,6},{5,7},{6,4},{7,5},{8,10},{9,11},{10,... | collective-permute-start | bytes 294920 | tf_op jit(solution)/shard_map/ppermute | solution.py:322
  19.6 8.9 %collective-permute-start.6 = (f32[48,1024]{1,0:T(8,128)S(1)}, f32[48,1024]{1,0:T(8,128)S(1)}, u32[]{:S(2)}, u32[]{:S(2)}) collective-permute-start(f32[48,1024]{1,0:T(8,128)S(1)} %get-tuple-element.29), channel_id=1, source_target_pairs={{0,4},{1,9},{2,6},{3,11},{4,0},{5,13},{6,2},{7,15},{8,12},{9,1},{1... | collective-permute-start | bytes 589832 | tf_op jit(solution)/shard_map/ppermute | solution.py:332
  21.5 9.0 %collective-permute-start.2 = (f32[48,1152]{1,0:T(8,128)S(1)}, f32[48,1152]{1,0:T(8,128)S(1)}, u32[]{:S(2)}, u32[]{:S(2)}) collective-permute-start(f32[48,1152]{1,0:T(8,128)S(1)} %get-tuple-element.22.after_ref), channel_id=1, source_target_pairs={{0,8},{1,5},{2,10},{3,7},{4,12},{5,1},{6,14},{7,3},{8,0},{9,13},{1... | collective-permute-start | bytes 663560 | tf_op jit(solution)/shard_map/ppermute | solution.py:332
  27.7 7.5 %collective-permute-start.4 = (f32[48,1024]{1,0:T(8,128)S(1)}, f32[48,1024]{1,0:T(8,128)S(1)}, u32[]{:S(2)}, u32[]{:S(2)}) collective-permute-start(f32[48,1024]{1,0:T(8,128)S(1)} %get-tuple-element.26), channel_id=1, source_target_pairs={{0,4},{1,9},{2,6},{3,11},{4,0},{5,13},{6,2},{7,15},{8,12},{9,1},{1... | collective-permute-start | bytes 589832 | tf_op jit(solution)/shard_map/ppermute | solution.py:332
  28.2 7.0 %collective-permute-start.3 = (f32[48,1024]{1,0:T(8,128)S(1)}, f32[48,1024]{1,0:T(8,128)S(1)}, u32[]{:S(2)}, u32[]{:S(2)}) collective-permute-start(f32[48,1024]{1,0:T(8,128)S(1)} %get-tuple-element.24), channel_id=1, source_target_pairs={{0,8},{1,5},{2,10},{3,7},{4,12},{5,1},{6,14},{7,3},{8,0},{9,13},{1... | collective-permute-start | bytes 589832 | tf_op jit(solution)/shard_map/ppermute | solution.py:332
  28.5 7.1 %collective-permute-start.7 = (f32[48,512]{1,0:T(8,128)S(1)}, f32[48,512]{1,0:T(8,128)S(1)}, u32[]{:S(2)}, u32[]{:S(2)}) collective-permute-start(f32[48,512]{1,0:T(8,128)S(1)} %slice.69), channel_id=1, source_target_pairs={{0,8},{1,5},{2,10},{3,7},{4,12},{5,1},{6,14},{7,3},{8,0},{9,13},{1... | collective-permute-start | bytes 294920 | tf_op jit(solution)/shard_map/ppermute | solution.py:332
  30.5 5.3 %collective-permute-start.5 = (f32[48,640]{1,0:T(8,128)S(1)}, f32[48,640]{1,0:T(8,128)S(1)}, u32[]{:S(2)}, u32[]{:S(2)}) collective-permute-start(f32[48,640]{1,0:T(8,128)S(1)} %slice.64), channel_id=1, source_target_pairs={{0,4},{1,9},{2,6},{3,11},{4,0},{5,13},{6,2},{7,15},{8,12},{9,1},{1... | collective-permute-start | bytes 368648 | tf_op jit(solution)/shard_map/ppermute | solution.py:332
  35.9 4.9 %collective-permute-start.8 = (f32[48,512]{1,0:T(8,128)S(1)}, f32[48,512]{1,0:T(8,128)S(1)}, u32[]{:S(2)}, u32[]{:S(2)}) collective-permute-start(f32[48,512]{1,0:T(8,128)S(1)} %slice.61), channel_id=1, source_target_pairs={{0,4},{1,9},{2,6},{3,11},{4,0},{5,13},{6,2},{7,15},{8,12},{9,1},{1... | collective-permute-start | bytes 294920 | tf_op jit(solution)/shard_map/ppermute | solution.py:332
  37.2 15.0 %collective-permute-start.11 = (f32[48,1152]{1,0:T(8,128)S(1)}, f32[48,1152]{1,0:T(8,128)S(1)}, u32[]{:S(2)}, u32[]{:S(2)}) collective-permute-start(f32[48,1152]{1,0:T(8,128)S(1)} %pad_maximum_fusion), channel_id=1, source_target_pairs={{0,16},{4,20},{8,24},{12,28},{16,0},{20,4},{24,8},{28,12},{1,17},{... | collective-permute-start | bytes 663560 | tf_op jit(solution)/shard_map/ppermute | solution.py:322
  39.7 6.4 %collective-permute-start.9 = (f32[48,512]{1,0:T(8,128)S(1)}, f32[48,512]{1,0:T(8,128)S(1)}, u32[]{:S(2)}, u32[]{:S(2)}) collective-permute-start(f32[48,512]{1,0:T(8,128)S(1)} %slice.62), channel_id=1, source_target_pairs={{0,8},{1,5},{2,10},{3,7},{4,12},{5,1},{6,14},{7,3},{8,0},{9,13},{1... | collective-permute-start | bytes 294920 | tf_op jit(solution)/shard_map/ppermute | solution.py:332
  46.1 11.7 %collective-permute-start.10 = (f32[48,1024]{1,0:T(8,128)S(1)}, f32[48,1024]{1,0:T(8,128)S(1)}, u32[]{:S(2)}, u32[]{:S(2)}) collective-permute-start(f32[48,1024]{1,0:T(8,128)S(1)} %pad_maximum_fusion.1), channel_id=1, source_target_pairs={{0,16},{4,20},{8,24},{12,28},{16,0},{20,4},{24,8},{28,12},{1,17},{... | collective-permute-start | bytes 589832 | tf_op jit(solution)/shard_map/ppermute | solution.py:322
  52.3 6.8 %collective-permute-start.17 = (f32[48,512]{1,0:T(8,128)S(1)}, f32[48,512]{1,0:T(8,128)S(1)}, u32[]{:S(2)}, u32[]{:S(2)}) collective-permute-start(f32[48,512]{1,0:T(8,128)S(1)} %get-tuple-element.35), channel_id=1, source_target_pairs={{0,8},{1,5},{2,10},{3,7},{4,12},{5,1},{6,14},{7,3},{8,0},{9,13},{1... | collective-permute-start | bytes 294920 | tf_op jit(solution)/shard_map/ppermute | solution.py:332
  54.5 5.9 %collective-permute-start.16 = (f32[48,512]{1,0:T(8,128)S(1)}, f32[48,512]{1,0:T(8,128)S(1)}, u32[]{:S(2)}, u32[]{:S(2)}) collective-permute-start(f32[48,512]{1,0:T(8,128)S(1)} %get-tuple-element.36), channel_id=1, source_target_pairs={{0,4},{1,9},{2,6},{3,11},{4,0},{5,13},{6,2},{7,15},{8,12},{9,1},{1... | collective-permute-start | bytes 294920 | tf_op jit(solution)/shard_map/ppermute | solution.py:332
  57.9 7.2 %collective-permute-start.12 = (f32[48,512]{1,0:T(8,128)S(1)}, f32[48,512]{1,0:T(8,128)S(1)}, u32[]{:S(2)}, u32[]{:S(2)}) collective-permute-start(f32[48,512]{1,0:T(8,128)S(1)} %get-tuple-element.33), channel_id=1, source_target_pairs={{0,4},{1,9},{2,6},{3,11},{4,0},{5,13},{6,2},{7,15},{8,12},{9,1},{1... | collective-permute-start | bytes 294920 | tf_op jit(solution)/shard_map/ppermute | solution.py:332
  58.7 5.3 %collective-permute-start.14 = (f32[48,512]{1,0:T(8,128)S(1)}, f32[48,512]{1,0:T(8,128)S(1)}, u32[]{:S(2)}, u32[]{:S(2)}) collective-permute-start(f32[48,512]{1,0:T(8,128)S(1)} %get-tuple-element.34), channel_id=1, source_target_pairs={{0,8},{1,5},{2,10},{3,7},{4,12},{5,1},{6,14},{7,3},{8,0},{9,13},{1... | collective-permute-start | bytes 294920 | tf_op jit(solution)/shard_map/ppermute | solution.py:332
  59.1 8.1 %collective-permute-start.19 = (f32[48,1024]{1,0:T(8,128)S(1)}, f32[48,1024]{1,0:T(8,128)S(1)}, u32[]{:S(2)}, u32[]{:S(2)}) collective-permute-start(f32[48,1024]{1,0:T(8,128)S(1)} %pad_maximum_fusion.5), channel_id=1, source_target_pairs={{0,4},{1,9},{2,6},{3,11},{4,0},{5,13},{6,2},{7,15},{8,12},{9,1},{1... | collective-permute-start | bytes 589832 | tf_op jit(solution)/shard_map/ppermute | solution.py:332
  60.4 7.8 %collective-permute-start.18 = (f32[48,1024]{1,0:T(8,128)S(1)}, f32[48,1024]{1,0:T(8,128)S(1)}, u32[]{:S(2)}, u32[]{:S(2)}) collective-permute-start(f32[48,1024]{1,0:T(8,128)S(1)} %pad_maximum_fusion.4), channel_id=1, source_target_pairs={{0,8},{1,5},{2,10},{3,7},{4,12},{5,1},{6,14},{7,3},{8,0},{9,13},{1... | collective-permute-start | bytes 589832 | tf_op jit(solution)/shard_map/ppermute | solution.py:332
  64.1 7.4 %collective-permute-start.15 = (f32[48,1024]{1,0:T(8,128)S(1)}, f32[48,1024]{1,0:T(8,128)S(1)}, u32[]{:S(2)}, u32[]{:S(2)}) collective-permute-start(f32[48,1024]{1,0:T(8,128)S(1)} %pad_maximum_fusion.3), channel_id=1, source_target_pairs={{0,4},{1,9},{2,6},{3,11},{4,0},{5,13},{6,2},{7,15},{8,12},{9,1},{1... | collective-permute-start | bytes 589832 | tf_op jit(solution)/shard_map/ppermute | solution.py:332
  65.1 6.3 %collective-permute-start.13 = (f32[48,1024]{1,0:T(8,128)S(1)}, f32[48,1024]{1,0:T(8,128)S(1)}, u32[]{:S(2)}, u32[]{:S(2)}) collective-permute-start(f32[48,1024]{1,0:T(8,128)S(1)} %pad_maximum_fusion.2), channel_id=1, source_target_pairs={{0,8},{1,5},{2,10},{3,7},{4,12},{5,1},{6,14},{7,3},{8,0},{9,13},{1... | collective-permute-start | bytes 589832 | tf_op jit(solution)/shard_map/ppermute | solution.py:332

commit v21 on v16

--- a/solution.py
+++ b/solution.py
@@ -11,7 +11,7 @@
 BF16 = jnp.bfloat16
 VMEM_LIMIT = 40 * 1024 * 1024
 LANES = 128
-CHUNKS = 2
+SHARES = (3, 5)
 AHEAD = 6
 UNIT = 512
 PANEL = 4
@@ -103,24 +103,23 @@
     )(in_hbm(probes), in_hbm(sketch_t))
 
 
-def multiply_blocks(both_ref, which_ref, x_hbm, x_buf, sems, plan, outs):
+def multiply_blocks(both_ref, start_ref, x_hbm, x_buf, sems, plan, outs):
     rank = outs[0].shape[0]
-    unit = x_buf.shape[2]
     copies = [
         pltpu.make_async_copy(
-            x_hbm.at[:, pl.ds(pl.multiple_of(which_ref[k] * unit, unit), unit)],
-            x_buf.at[k],
+            x_hbm.at[:, pl.ds(pl.multiple_of(start_ref[k] * LANES, LANES), unit)],
+            x_buf.at[k, :, pl.ds(0, unit)],
             sems.at[k],
         )
-        for k in range(len(plan))
+        for k, (_, _, unit) in enumerate(plan)
     ]
 
     def use(k):
         both = both_ref[...]
-        x_head, x_rest = split(x_buf[k])
+        out, offset, unit = plan[k]
+        x_head, x_rest = split(x_buf[k, :, :unit])
         first = dot(both, x_head, PLAIN)
         second = dot(both[:rank], x_rest, PLAIN)
-        out, offset = plan[k]
         outs[out][:, offset : offset + unit] = first[:rank] + (first[rank:] + second)
 
     return copies, use
@@ -160,25 +159,24 @@
         outs[out][:, offset : offset + LANES] = gram_ref[...]
 
 
-def layout(outputs, sub):
-    unit = min(UNIT, sub)
-    plan, grams, widths, which = [], [], [], []
-    for out, (blocks, with_gram) in enumerate(outputs):
+def layout(outputs):
+    plan, grams, widths, starts = [], [], [], []
+    for out, (blocks, sub, with_gram) in enumerate(outputs):
         extra = LANES if with_gram else 0
         for j, block in enumerate(blocks):
-            for part in range(sub // unit):
-                plan.append((out, j * sub + part * unit + (extra if j else 0)))
-                which.append(block * (sub // unit) + part)
+            plan.append((out, j * sub + (extra if j else 0), sub))
+            starts.append(block)
         if with_gram:
             grams.append((out, sub))
         widths.append(len(blocks) * sub + extra)
-    return unit, plan, grams, widths, jnp.stack(which)
-
-
-def products(kernel, inputs, in_specs, made, probes, outputs, sub, name):
+    return plan, grams, widths, jnp.stack(starts)
+
+
+def products(kernel, inputs, in_specs, made, probes, outputs, name):
     rows = probes.shape[0]
     rank = inputs[1].shape[0]
-    unit, plan, grams, widths, which = layout(outputs, sub)
+    plan, grams, widths, starts = layout(outputs)
+    unit = max(entry[2] for entry in plan)
     shapes = [*made, *[jax.ShapeDtypeStruct((rank, width), F32) for width in widths]]
     return pl.pallas_call(
         functools.partial(kernel, plan, grams),
@@ -196,10 +194,10 @@
             transcendentals=0,
         ),
         name=name,
-    )(which, *inputs)
-
-
-def first_products(one, two, probes, outputs, sub):
+    )(starts, *inputs)
+
+
+def first_products(one, two, probes, outputs):
     rank, rows = one.shape
     made = [
         jax.ShapeDtypeStruct((2 * rank, rows), BF16),
@@ -212,13 +210,12 @@
         made,
         probes,
         outputs,
-        sub,
         "first_products",
     )
     return both, gram, outs
 
 
-def rest_products(both, gram, probes, outputs, sub, after):
+def rest_products(both, gram, probes, outputs, after):
     return products(
         rest_kernel,
         [both, gram, in_hbm(probes), after],
@@ -226,7 +223,6 @@
         [],
         probes,
         outputs,
-        sub,
         "rest_products",
     )
 
@@ -271,16 +267,17 @@
 
 def finish_kernel(plan, where_ref, inverse_ref, *refs):
     out_hbm, buf, sems = refs[-3:]
-    _, rank, width = buf.shape
+    rank = buf.shape[1]
     head, rest = split(inverse_ref[...])
     both = jnp.concatenate([head, rest], axis=0)
     copies = []
-    for k, (source, offset) in enumerate(plan):
+    for k, (source, offset, width) in enumerate(plan):
         p_head, p_rest = split(refs[source][:, offset : offset + width])
         first = dot(both, p_head, PLAIN)
-        buf[k] = first[:rank] + (first[rank:] + dot(head, p_rest, PLAIN))
-        where = pl.ds(pl.multiple_of(where_ref[k] * width, width), width)
-        copies.append(pltpu.make_async_copy(buf.at[k], out_hbm.at[:, where], sems.at[k]))
+        buf[k, :, :width] = first[:rank] + (first[rank:] + dot(head, p_rest, PLAIN))
+        where = pl.ds(pl.multiple_of(where_ref[k] * LANES, LANES), width)
+        part = buf.at[k, :, pl.ds(0, width)]
+        copies.append(pltpu.make_async_copy(part, out_hbm.at[:, where], sems.at[k]))
         copies[k].start()
     for copy in copies:
         copy.wait()
@@ -297,7 +294,7 @@
         args.append(before)
         aliases = {len(args) - 1: 0}
     return pl.pallas_call(
-        functools.partial(finish_kernel, [piece[1:] for piece in pieces]),
+        functools.partial(finish_kernel, [(*piece[1:], width) for piece in pieces]),
         in_specs=in_specs,
         out_specs=HBM,
         out_shape=jax.ShapeDtypeStruct((rank, total), F32),
@@ -326,7 +323,8 @@
     me = lax.axis_index("pos").astype(jnp.int32)
     near, far = me & 1, (me >> 1) & 1
     cols = probes.shape[1]
-    width = cols // (8 * CHUNKS)
+    widths = [cols // 8 * share // sum(SHARES) for share in SHARES]
+    firsts = [8 * sum(widths[:c]) // LANES for c in range(len(widths))]
 
     tall = tall_partial(probes, sketch.T)
     bit = 1
@@ -336,25 +334,25 @@
     other = swap(tall, "pix", n_pix, bit)
 
     def block_a(c, p, q):
-        return 8 * c + 2 * (near ^ p) + (far ^ q)
+        return firsts[c] + (2 * (near ^ p) + (far ^ q)) * (widths[c] // LANES)
 
     def block_b(c, p, q):
-        return 8 * c + 4 + 2 * (far ^ p) + (near ^ q)
+        return firsts[c] + (4 + 2 * (far ^ p) + (near ^ q)) * (widths[c] // LANES)
 
     def outputs(c, p):
         return [
-            ([block_a(c, p, 1), block_a(c, p, 0)], c == 0),
-            ([block_b(c, p, 1), block_b(c, p, 0)], False),
+            ([block_a(c, p, 1), block_a(c, p, 0)], widths[c], c == 0),
+            ([block_b(c, p, 1), block_b(c, p, 0)], widths[c], False),
         ]
 
-    both, gram, away = first_products(tall, other, probes, outputs(0, 1), width)
+    both, gram, away = first_products(tall, other, probes, outputs(0, 1))
 
     inverse, out, after = None, None, away[0]
-    for c in range(CHUNKS):
+    for c, width in enumerate(widths):
         g = LANES if c == 0 else 0
-        last = c == CHUNKS - 1
+        last = c == len(widths) - 1
         made = rest_products(
-            both, gram, probes, outputs(c, 0) + ([] if last else outputs(c + 1, 1)), width, after
+            both, gram, probes, outputs(c, 0) + ([] if last else outputs(c + 1, 1)), after
         )
         away_a, away_b = away
         (own_a, own_b), away = made[:2], made[2:]
@@ -380,13 +378,14 @@
         while bit < n_pos:
             total = total + over(total, bit)
             bit *= 2
-        if c == 0:
-            inverse = inverse_factor(total, width)
         mine_a, mine_b = total[:, :width], total[:, width + g :]
         if c > 0:
-            mine_a, mine_b, inverse = lax.optimization_barrier((mine_a, mine_b, inverse))
+            mine_a, mine_b, *_ = lax.optimization_barrier((mine_a, mine_b, inverse, last_a, last_b))
         next_a = over(mine_a, 2)
         next_b = over(mine_b, 1)
+        if c == 0:
+            held = lax.optimization_barrier((total, next_a, next_b))[0]
+            inverse = inverse_factor(held, width)
         last_a = over(jnp.concatenate([mine_a, next_a], axis=1), 1)
         last_b = over(jnp.concatenate([mine_b, next_b], axis=1), 2)
         sources = [total, next_a, next_b]

time: 71.3 us -> 74.6 us (1.046)
  starting transfers between devices: 24.1 us -> 30.9 us
  waiting for transfers between devices: 20.9 us -> 17.1 us
    ppermute x20, starting transfers between devices: 24.1 us -> 30.9 us  [swap(): return lax.ppermute(value, axis, [(i, i ^ bit) for i in range(size)])]
    ppermute x20, waiting for transfers between devices: 20.9 us -> 17.1 us  [swap(): return lax.ppermute(value, axis, [(i, i ^ bit) for i in range(size)])]
  transfers between devices with their start and end apart: 20 -> 20, of which waited for: 10 -> 13; matrix products, arithmetic and copies ran while one was open for 1% -> 1% of each run, Pallas kernels for 18% -> 18%
where the time goes in v21:
time: 74.6 us; the launch traced here: 74.4 us
  starting transfers between devices  30.9 us (41%)
  Pallas kernels  25.3 us (34%)
  waiting for transfers between devices  17.1 us (23%)
    ppermute x20, starting transfers between devices, swap(): return lax.ppermute(value, axis, [(i, i ^ bit) for i in range(size)])  30.9 us
    ppermute x20, waiting for transfers between devices, swap(): return lax.ppermute(value, axis, [(i, i ^ bit) for i in range(size)])  17.1 us
    pallas_call x3, Pallas kernels, products(): pl.pallas_call(functools.partial(kernel, plan, grams), in_specs=[TABLE, *...  11.2 us
    pallas_call x1, Pallas kernels, tall_partial(): pl.pallas_call(tall_kernel, in_specs=[HBM, HBM], out_specs=WHOLE, out_sha...  7.27 us
    pallas_call x3, Pallas kernels, finish(): pl.pallas_call(functools.partial(finish_kernel, [(*piece[1:], width) for...  4.78 us
    pallas_call x1, Pallas kernels, inverse_factor(): pl.pallas_call(inverse_kernel, grid=(1,), in_specs=[pl.BlockSpec((rank, L...  2.01 us
  transfers between devices with their start and end apart: 20, of which 13 were waited for; matrix products, arithmetic and copies ran while one was open for 1% of the time, Pallas kernels for 18%

profile of v21, /device:TPU:0, one launch (start us, length us, event | category | flops | bytes accessed | tf_op | source)
XLA Modules:
  0.0 74.4 jit_solution(5493289570212244206)
XLA Ops:
  0.0 7.3 %tall_partial.1 = f32[48,512]{1,0:T(8,128)S(1)} custom-call(f32[512,8192]{1,0:T(8,128)} %x_hbm.7, f32[48,8192]{1,0:T(8,128)} %bitcast.17), custom_call_target="tpu_custom_call" | custom-call | flops 1207959552 | bytes 16777216 | tf_op jit(solution)/shard_map/tall_partial/pallas_call | solution.py:85
  8.8 2.9 %collective-permute-start.1 = (f32[48,512]{1,0:T(8,128)S(1)}, f32[48,512]{1,0:T(8,128)S(1)}, u32[]{:S(2)}, u32[]{:S(2)}) collective-permute-start(f32[48,512]{1,0:T(8,128)S(1)} %add.74.one_ref), channel_id=1, source_target_pairs={{0,2},{1,3},{2,0},{3,1},{4,6},{5,7},{6,4},{7,5},{8,10},{9,11},{10,... | collective-permute-start | bytes 294920 | tf_op jit(solution)/shard_map/ppermute | solution.py:318
  11.8 3.0 %collective-permute-done.1.two_ref = f32[48,512]{1,0:T(8,128)S(1)} collective-permute-done((f32[48,512]{1,0:T(8,128)S(1)}, f32[48,512]{1,0:T(8,128)S(1)}, u32[]{:S(2)}, u32[]{:S(2)}) %collective-permute-start.1) | collective-permute-done | bytes 98336 | tf_op jit(solution)/shard_map/ppermute | solution.py:318
  14.8 3.1 %first_products.1 = (bf16[96,512]{1,0:T(8,128)(2,1)S(1)}, f32[48,128]{1,0:T(8,128)S(1)}, f32[48,896]{1,0:T(8,128)S(1)}, f32[48,768]{1,0:T(8,128)S(1)}) custom-call(s32[4]{0:T(128)S(1)} %pad_add_fusion.1.which_ref, f32[48,512]{1,0:T(8,128)S(1)} %add.74.one_ref, f32[48,512]{1,0:T(8,128)S(1)} %collective-permute-done.1.two_ref, f32[512,8192]{1,0:T(8,128)} %x_hbm.7), custom_call_target="tpu_custom_call" | custom-call | flops 226492416 | bytes 3145728 | tf_op jit(solution)/shard_map/first_products/pallas_call | solution.py:181
  18.0 1.9 %collective-permute-start.4 = (f32[48,768]{1,0:T(8,128)S(1)}, f32[48,768]{1,0:T(8,128)S(1)}, u32[]{:S(2)}, u32[]{:S(2)}) collective-permute-start(f32[48,768]{1,0:T(8,128)S(1)} %get-tuple-element.25), channel_id=1, source_target_pairs={{0,8},{4,12},{8,0},{12,4},{16,24},{20,28},{24,16},{28,20},{1,9},{5... | collective-permute-start | bytes 442376 | tf_op jit(solution)/shard_map/ppermute | solution.py:318
  19.9 1.5 %collective-permute-start.2 = (f32[48,896]{1,0:T(8,128)S(1)}, f32[48,896]{1,0:T(8,128)S(1)}, u32[]{:S(2)}, u32[]{:S(2)}) collective-permute-start(f32[48,896]{1,0:T(8,128)S(1)} %get-tuple-element.22.after_ref), channel_id=1, source_target_pairs={{0,4},{4,0},{8,12},{12,8},{16,20},{20,16},{24,28},{28,24},{1,5},{5... | collective-permute-start | bytes 516104 | tf_op jit(solution)/shard_map/ppermute | solution.py:318
  21.4 4.6 %rest_products.2 = (f32[48,896]{1,0:T(8,128)S(1)}, f32[48,768]{1,0:T(8,128)S(1)}, f32[48,1280]{1,0:T(8,128)S(1)}, f32[48,1280]{1,0:T(8,128)S(1)}) custom-call(s32[8]{0:T(128)S(1)} %stack.91.which_ref, bf16[96,512]{1,0:T(8,128)(2,1)S(1)} %get-tuple-element.20.both_ref, f32[48,128]{1,0:T(8,128)S(1)} %get-tuple-element.21.gram_ref, f32[512,8192]{1,0:T(8,128)} %x_hbm.7, ...), custom_call_target="tpu_custom_call" | custom-call | flops 754974720 | bytes 10485760 | tf_op jit(solution)/shard_map/rest_products/pallas_call | solution.py:181
  27.0 1.7 %collective-permute-start.9 = (f32[48,1280]{1,0:T(8,128)S(1)}, f32[48,1280]{1,0:T(8,128)S(1)}, u32[]{:S(2)}, u32[]{:S(2)}) collective-permute-start(f32[48,1280]{1,0:T(8,128)S(1)} %get-tuple-element.28), channel_id=1, source_target_pairs={{0,4},{4,0},{8,12},{12,8},{16,20},{20,16},{24,28},{28,24},{1,5},{5... | collective-permute-start | bytes 737288 | tf_op jit(solution)/shard_map/ppermute | solution.py:318
  28.8 1.6 %collective-permute-start.3 = (f32[48,512]{1,0:T(8,128)S(1)}, f32[48,512]{1,0:T(8,128)S(1)}, u32[]{:S(2)}, u32[]{:S(2)}) collective-permute-start(f32[48,512]{1,0:T(8,128)S(1)} %slice.61), channel_id=1, source_target_pairs={{0,8},{4,12},{8,0},{12,4},{16,24},{20,28},{24,16},{28,20},{1,9},{5... | collective-permute-start | bytes 294920 | tf_op jit(solution)/shard_map/ppermute | solution.py:318
  30.4 3.5 %rest_products.3 = (f32[48,1280]{1,0:T(8,128)S(1)}, f32[48,1280]{1,0:T(8,128)S(1)}) custom-call(s32[4]{0:T(128)S(1)} %pad_add_fusion.2.which_ref, bf16[96,512]{1,0:T(8,128)(2,1)S(1)} %get-tuple-element.20.both_ref, f32[48,128]{1,0:T(8,128)S(1)} %get-tuple-element.21.gram_ref, f32[512,8192]{1,0:T(8,128)} %x_hbm.7, f32[48,896]{1,0:T(8,128)S(1)} %collective-permute-done.2.after_ref), custom_call_target="tpu_custom_call" | custom-call | flops 377487360 | bytes 5242880 | tf_op jit(solution)/shard_map/rest_products/pallas_call | solution.py:181
  35.9 2.5 %collective-permute-start.6 = (f32[48,896]{1,0:T(8,128)S(1)}, f32[48,896]{1,0:T(8,128)S(1)}, u32[]{:S(2)}, u32[]{:S(2)}) collective-permute-start(f32[48,896]{1,0:T(8,128)S(1)} %pad_maximum_fusion.3), channel_id=1, source_target_pairs={{0,16},{4,20},{8,24},{12,28},{16,0},{20,4},{24,8},{28,12},{1,17},{... | collective-permute-start | bytes 516104 | tf_op jit(solution)/shard_map/ppermute | solution.py:318
  40.3 3.0 %collective-permute-done.12 = f32[48,640]{1,0:T(8,128)S(1)} collective-permute-done((f32[48,640]{1,0:T(8,128)S(1)}, f32[48,640]{1,0:T(8,128)S(1)}, u32[]{:S(2)}, u32[]{:S(2)}) %collective-permute-start.12) | collective-permute-done | bytes 122912 | tf_op jit(solution)/shard_map/ppermute | solution.py:318
  46.5 4.6 %collective-permute-start.7 = (f32[48,384]{1,0:T(8,128)S(1)}, f32[48,384]{1,0:T(8,128)S(1)}, u32[]{:S(2)}, u32[]{:S(2)}) collective-permute-start(f32[48,384]{1,0:T(8,128)S(1)} %get-tuple-element.38), channel_id=1, source_target_pairs={{0,8},{4,12},{8,0},{12,4},{16,24},{20,28},{24,16},{28,20},{1,9},{5... | collective-permute-start | bytes 221192 | tf_op jit(solution)/shard_map/ppermute | solution.py:318
  51.2 2.2 %collective-permute-done.7.refs_1_ = f32[48,384]{1,0:T(8,128)S(1)} collective-permute-done((f32[48,384]{1,0:T(8,128)S(1)}, f32[48,384]{1,0:T(8,128)S(1)}, u32[]{:S(2)}, u32[]{:S(2)}) %collective-permute-start.7) | collective-permute-done | bytes 73760 | tf_op jit(solution)/shard_map/ppermute | solution.py:318
  53.4 2.2 %collective-permute-start.14 = (f32[48,768]{1,0:T(8,128)S(1)}, f32[48,768]{1,0:T(8,128)S(1)}, u32[]{:S(2)}, u32[]{:S(2)}) collective-permute-start(f32[48,768]{1,0:T(8,128)S(1)} %pad_maximum_fusion.4), channel_id=1, source_target_pairs={{0,4},{4,0},{8,12},{12,8},{16,20},{20,16},{24,28},{28,24},{1,5},{5... | collective-permute-start | bytes 442376 | tf_op jit(solution)/shard_map/ppermute | solution.py:318
  55.7 2.0 %inverse_factor.1.inverse_ref = f32[48,48]{1,0:T(8,128)S(1)} custom-call(f32[48,896]{1,0:T(8,128)S(1)} %fusion.1.gram_ref.refs_0_), custom_call_target="tpu_custom_call" | custom-call | flops 20000000 | bytes 49152 | tf_op jit(solution)/shard_map/inverse_factor/pallas_call | solution.py:254
  58.8 2.0 %collective-permute-start.18 = (f32[48,640]{1,0:T(8,128)S(1)}, f32[48,640]{1,0:T(8,128)S(1)}, u32[]{:S(2)}, u32[]{:S(2)}) collective-permute-start(f32[48,640]{1,0:T(8,128)S(1)} %get-tuple-element.34), channel_id=1, source_target_pairs={{0,4},{4,0},{8,12},{12,8},{16,20},{20,16},{24,28},{28,24},{1,5},{5... | collective-permute-start | bytes 368648 | tf_op jit(solution)/shard_map/ppermute | solution.py:318
  60.8 1.9 %collective-permute-start.16 = (f32[48,640]{1,0:T(8,128)S(1)}, f32[48,640]{1,0:T(8,128)S(1)}, u32[]{:S(2)}, u32[]{:S(2)}) collective-permute-start(f32[48,640]{1,0:T(8,128)S(1)} %get-tuple-element.33), channel_id=1, source_target_pairs={{0,8},{4,12},{8,0},{12,4},{16,24},{20,28},{24,16},{28,20},{1,9},{5... | collective-permute-start | bytes 368648 | tf_op jit(solution)/shard_map/ppermute | solution.py:318
  62.7 2.3 %collective-permute-done.18.refs_2_ = f32[48,640]{1,0:T(8,128)S(1)} collective-permute-done((f32[48,640]{1,0:T(8,128)S(1)}, f32[48,640]{1,0:T(8,128)S(1)}, u32[]{:S(2)}, u32[]{:S(2)}) %collective-permute-start.18) | collective-permute-done | bytes 122912 | tf_op jit(solution)/shard_map/ppermute | solution.py:318
  65.0 1.6 %collective-permute-start.19 = (f32[48,1280]{1,0:T(8,128)S(1)}, f32[48,1280]{1,0:T(8,128)S(1)}, u32[]{:S(2)}, u32[]{:S(2)}) collective-permute-start(f32[48,1280]{1,0:T(8,128)S(1)} %pad_maximum_fusion.2), channel_id=1, source_target_pairs={{0,8},{4,12},{8,0},{12,4},{16,24},{20,28},{24,16},{28,20},{1,9},{5... | collective-permute-start | bytes 737288 | tf_op jit(solution)/shard_map/ppermute | solution.py:318
  68.0 1.6 %finish.3.refs_3_ = f32[48,8192]{1,0:T(8,128)} custom-call(s32[8]{0:T(128)S(1)} %stack.103.where_ref, f32[48,48]{1,0:T(8,128)S(1)} %inverse_factor.1.inverse_ref, f32[48,896]{1,0:T(8,128)S(1)} %fusion.1.gram_ref.refs_0_, f32[48,384]{1,0:T(8,128)S(1)} %collective-permute-done.7.refs_1_, f32[48,384]{1,0:T(8,128)S(1)} %collective-permute-done.8.refs_2_, ...), custom_call_target="tpu_custom_call" | custom-call | flops 42467328 | bytes 1179648 | tf_op jit(solution)/shard_map/finish/pallas_call | solution.py:296
  69.6 1.6 %finish.4.refs_2_ = f32[48,8192]{1,0:T(8,128)} custom-call(s32[4]{0:T(128)S(1)} %pad_add_fusion.3.where_ref, f32[48,48]{1,0:T(8,128)S(1)} %inverse_factor.1.inverse_ref, f32[48,1280]{1,0:T(8,128)S(1)} %fusion.refs_0_, f32[48,640]{1,0:T(8,128)S(1)} %collective-permute-done.16.refs_1_, ...), custom_call_target="tpu_custom_call", output_to_operand_aliasing={{}: (5, {})} | custom-call | flops 35389440 | bytes 983040 | tf_op jit(solution)/shard_map/finish/pallas_call | solution.py:296
  71.3 1.6 %collective-permute-done.17.refs_0_ = f32[48,1280]{1,0:T(8,128)S(1)} collective-permute-done((f32[48,1280]{1,0:T(8,128)S(1)}, f32[48,1280]{1,0:T(8,128)S(1)}, u32[]{:S(2)}, u32[]{:S(2)}) %collective-permute-start.17) | collective-permute-done | bytes 245792 | tf_op jit(solution)/shard_map/ppermute | solution.py:318
  72.9 1.6 %finish.5 = f32[48,8192]{1,0:T(8,128)} custom-call(s32[4]{0:T(128)S(1)} %pad_add_fusion.where_ref, f32[48,48]{1,0:T(8,128)S(1)} %inverse_factor.1.inverse_ref, f32[48,1280]{1,0:T(8,128)S(1)} %collective-permute-done.17.refs_0_, f32[48,1280]{1,0:T(8,128)S(1)} %collective-permute-done.19.refs_1_, f32[48,8192]{1,0:T(8,128)} %finish.4.refs_2_), custom_call_target="tpu_custom_call", output_to_operand_aliasing={{}: (4, {})} | custom-call | flops 35389440 | bytes 983040 | tf_op jit(solution)/shard_map/finish/pallas_call | solution.py:296
  (54 shorter events, 12.2 us)
Async XLA Ops:
  7.3 1.5 %collective-permute-start = (f32[48,512]{1,0:T(8,128)S(1)}, f32[48,512]{1,0:T(8,128)S(1)}, u32[]{:S(2)}, u32[]{:S(2)}) collective-permute-start(f32[48,512]{1,0:T(8,128)S(1)} %tall_partial.1), channel_id=1, source_target_pairs={{0,1},{1,0},{2,3},{3,2},{4,5},{5,4},{6,7},{7,6},{8,9},{9,8},{10,11... | collective-permute-start | bytes 294920 | tf_op jit(solution)/shard_map/ppermute | solution.py:318
  8.8 6.0 %collective-permute-start.1 = (f32[48,512]{1,0:T(8,128)S(1)}, f32[48,512]{1,0:T(8,128)S(1)}, u32[]{:S(2)}, u32[]{:S(2)}) collective-permute-start(f32[48,512]{1,0:T(8,128)S(1)} %add.74.one_ref), channel_id=1, source_target_pairs={{0,2},{1,3},{2,0},{3,1},{4,6},{5,7},{6,4},{7,5},{8,10},{9,11},{10,... | collective-permute-start | bytes 294920 | tf_op jit(solution)/shard_map/ppermute | solution.py:318
  18.0 8.1 %collective-permute-start.4 = (f32[48,768]{1,0:T(8,128)S(1)}, f32[48,768]{1,0:T(8,128)S(1)}, u32[]{:S(2)}, u32[]{:S(2)}) collective-permute-start(f32[48,768]{1,0:T(8,128)S(1)} %get-tuple-element.25), channel_id=1, source_target_pairs={{0,8},{4,12},{8,0},{12,4},{16,24},{20,28},{24,16},{28,20},{1,9},{5... | collective-permute-start | bytes 442376 | tf_op jit(solution)/shard_map/ppermute | solution.py:318
  19.9 8.8 %collective-permute-start.2 = (f32[48,896]{1,0:T(8,128)S(1)}, f32[48,896]{1,0:T(8,128)S(1)}, u32[]{:S(2)}, u32[]{:S(2)}) collective-permute-start(f32[48,896]{1,0:T(8,128)S(1)} %get-tuple-element.22.after_ref), channel_id=1, source_target_pairs={{0,4},{4,0},{8,12},{12,8},{16,20},{20,16},{24,28},{28,24},{1,5},{5... | collective-permute-start | bytes 516104 | tf_op jit(solution)/shard_map/ppermute | solution.py:318
  26.1 7.8 %collective-permute-start.5 = (f32[48,384]{1,0:T(8,128)S(1)}, f32[48,384]{1,0:T(8,128)S(1)}, u32[]{:S(2)}, u32[]{:S(2)}) collective-permute-start(f32[48,384]{1,0:T(8,128)S(1)} %slice.66), channel_id=1, source_target_pairs={{0,4},{4,0},{8,12},{12,8},{16,20},{20,16},{24,28},{28,24},{1,5},{5... | collective-permute-start | bytes 221192 | tf_op jit(solution)/shard_map/ppermute | solution.py:318
  26.8 7.4 %collective-permute-start.10 = (f32[48,1280]{1,0:T(8,128)S(1)}, f32[48,1280]{1,0:T(8,128)S(1)}, u32[]{:S(2)}, u32[]{:S(2)}) collective-permute-start(f32[48,1280]{1,0:T(8,128)S(1)} %get-tuple-element.30), channel_id=1, source_target_pairs={{0,8},{4,12},{8,0},{12,4},{16,24},{20,28},{24,16},{28,20},{1,9},{5... | collective-permute-start | bytes 737288 | tf_op jit(solution)/shard_map/ppermute | solution.py:318
  27.0 7.4 %collective-permute-start.9 = (f32[48,1280]{1,0:T(8,128)S(1)}, f32[48,1280]{1,0:T(8,128)S(1)}, u32[]{:S(2)}, u32[]{:S(2)}) collective-permute-start(f32[48,1280]{1,0:T(8,128)S(1)} %get-tuple-element.28), channel_id=1, source_target_pairs={{0,4},{4,0},{8,12},{12,8},{16,20},{20,16},{24,28},{28,24},{1,5},{5... | collective-permute-start | bytes 737288 | tf_op jit(solution)/shard_map/ppermute | solution.py:318
  28.8 6.5 %collective-permute-start.3 = (f32[48,512]{1,0:T(8,128)S(1)}, f32[48,512]{1,0:T(8,128)S(1)}, u32[]{:S(2)}, u32[]{:S(2)}) collective-permute-start(f32[48,512]{1,0:T(8,128)S(1)} %slice.61), channel_id=1, source_target_pairs={{0,8},{4,12},{8,0},{12,4},{16,24},{20,28},{24,16},{28,20},{1,9},{5... | collective-permute-start | bytes 294920 | tf_op jit(solution)/shard_map/ppermute | solution.py:318
  35.3 5.0 %collective-permute-start.11 = (f32[48,640]{1,0:T(8,128)S(1)}, f32[48,640]{1,0:T(8,128)S(1)}, u32[]{:S(2)}, u32[]{:S(2)}) collective-permute-start(f32[48,640]{1,0:T(8,128)S(1)} %slice.70), channel_id=1, source_target_pairs={{0,8},{4,12},{8,0},{12,4},{16,24},{20,28},{24,16},{28,20},{1,9},{5... | collective-permute-start | bytes 368648 | tf_op jit(solution)/shard_map/ppermute | solution.py:318
  35.9 8.7 %collective-permute-start.6 = (f32[48,896]{1,0:T(8,128)S(1)}, f32[48,896]{1,0:T(8,128)S(1)}, u32[]{:S(2)}, u32[]{:S(2)}) collective-permute-start(f32[48,896]{1,0:T(8,128)S(1)} %pad_maximum_fusion.3), channel_id=1, source_target_pairs={{0,16},{4,20},{8,24},{12,28},{16,0},{20,4},{24,8},{28,12},{1,17},{... | collective-permute-start | bytes 516104 | tf_op jit(solution)/shard_map/ppermute | solution.py:318
  38.4 4.9 %collective-permute-start.12 = (f32[48,640]{1,0:T(8,128)S(1)}, f32[48,640]{1,0:T(8,128)S(1)}, u32[]{:S(2)}, u32[]{:S(2)}) collective-permute-start(f32[48,640]{1,0:T(8,128)S(1)} %slice.71), channel_id=1, source_target_pairs={{0,4},{4,0},{8,12},{12,8},{16,20},{20,16},{24,28},{28,24},{1,5},{5... | collective-permute-start | bytes 368648 | tf_op jit(solution)/shard_map/ppermute | solution.py:318
  44.6 6.5 %collective-permute-start.8 = (f32[48,384]{1,0:T(8,128)S(1)}, f32[48,384]{1,0:T(8,128)S(1)}, u32[]{:S(2)}, u32[]{:S(2)}) collective-permute-start(f32[48,384]{1,0:T(8,128)S(1)} %get-tuple-element.37), channel_id=1, source_target_pairs={{0,4},{4,0},{8,12},{12,8},{16,20},{20,16},{24,28},{28,24},{1,5},{5... | collective-permute-start | bytes 221192 | tf_op jit(solution)/shard_map/ppermute | solution.py:318
  46.0 11.7 %collective-permute-start.13 = (f32[48,1280]{1,0:T(8,128)S(1)}, f32[48,1280]{1,0:T(8,128)S(1)}, u32[]{:S(2)}, u32[]{:S(2)}) collective-permute-start(f32[48,1280]{1,0:T(8,128)S(1)} %pad_maximum_fusion), channel_id=1, source_target_pairs={{0,16},{4,20},{8,24},{12,28},{16,0},{20,4},{24,8},{28,12},{1,17},{... | collective-permute-start | bytes 737288 | tf_op jit(solution)/shard_map/ppermute | solution.py:318
  46.5 6.9 %collective-permute-start.7 = (f32[48,384]{1,0:T(8,128)S(1)}, f32[48,384]{1,0:T(8,128)S(1)}, u32[]{:S(2)}, u32[]{:S(2)}) collective-permute-start(f32[48,384]{1,0:T(8,128)S(1)} %get-tuple-element.38), channel_id=1, source_target_pairs={{0,8},{4,12},{8,0},{12,4},{16,24},{20,28},{24,16},{28,20},{1,9},{5... | collective-permute-start | bytes 221192 | tf_op jit(solution)/shard_map/ppermute | solution.py:318
  51.1 6.7 %collective-permute-start.15 = (f32[48,768]{1,0:T(8,128)S(1)}, f32[48,768]{1,0:T(8,128)S(1)}, u32[]{:S(2)}, u32[]{:S(2)}) collective-permute-start(f32[48,768]{1,0:T(8,128)S(1)} %pad_maximum_fusion.5), channel_id=1, source_target_pairs={{0,8},{4,12},{8,0},{12,4},{16,24},{20,28},{24,16},{28,20},{1,9},{5... | collective-permute-start | bytes 442376 | tf_op jit(solution)/shard_map/ppermute | solution.py:318
  53.4 5.4 %collective-permute-start.14 = (f32[48,768]{1,0:T(8,128)S(1)}, f32[48,768]{1,0:T(8,128)S(1)}, u32[]{:S(2)}, u32[]{:S(2)}) collective-permute-start(f32[48,768]{1,0:T(8,128)S(1)} %pad_maximum_fusion.4), channel_id=1, source_target_pairs={{0,4},{4,0},{8,12},{12,8},{16,20},{20,16},{24,28},{28,24},{1,5},{5... | collective-permute-start | bytes 442376 | tf_op jit(solution)/shard_map/ppermute | solution.py:318
  58.8 6.2 %collective-permute-start.18 = (f32[48,640]{1,0:T(8,128)S(1)}, f32[48,640]{1,0:T(8,128)S(1)}, u32[]{:S(2)}, u32[]{:S(2)}) collective-permute-start(f32[48,640]{1,0:T(8,128)S(1)} %get-tuple-element.34), channel_id=1, source_target_pairs={{0,4},{4,0},{8,12},{12,8},{16,20},{20,16},{24,28},{28,24},{1,5},{5... | collective-permute-start | bytes 368648 | tf_op jit(solution)/shard_map/ppermute | solution.py:318
  60.8 5.8 %collective-permute-start.16 = (f32[48,640]{1,0:T(8,128)S(1)}, f32[48,640]{1,0:T(8,128)S(1)}, u32[]{:S(2)}, u32[]{:S(2)}) collective-permute-start(f32[48,640]{1,0:T(8,128)S(1)} %get-tuple-element.33), channel_id=1, source_target_pairs={{0,8},{4,12},{8,0},{12,4},{16,24},{20,28},{24,16},{28,20},{1,9},{5... | collective-permute-start | bytes 368648 | tf_op jit(solution)/shard_map/ppermute | solution.py:318
  65.0 6.3 %collective-permute-start.19 = (f32[48,1280]{1,0:T(8,128)S(1)}, f32[48,1280]{1,0:T(8,128)S(1)}, u32[]{:S(2)}, u32[]{:S(2)}) collective-permute-start(f32[48,1280]{1,0:T(8,128)S(1)} %pad_maximum_fusion.2), channel_id=1, source_target_pairs={{0,8},{4,12},{8,0},{12,4},{16,24},{20,28},{24,16},{28,20},{1,9},{5... | collective-permute-start | bytes 737288 | tf_op jit(solution)/shard_map/ppermute | solution.py:318
  66.6 6.3 %collective-permute-start.17 = (f32[48,1280]{1,0:T(8,128)S(1)}, f32[48,1280]{1,0:T(8,128)S(1)}, u32[]{:S(2)}, u32[]{:S(2)}) collective-permute-start(f32[48,1280]{1,0:T(8,128)S(1)} %pad_maximum_fusion.1), channel_id=1, source_target_pairs={{0,4},{4,0},{8,12},{12,8},{16,20},{20,16},{24,28},{28,24},{1,5},{5... | collective-permute-start | bytes 737288 | tf_op jit(solution)/shard_map/ppermute | solution.py:318

commit v22 on v16

--- a/solution.py
+++ b/solution.py
@@ -229,6 +229,23 @@
         sub,
         "rest_products",
     )
+
+
+def hold_kernel(*refs):
+    pass
+
+
+def hold(arrays, after, flops):
+    count = len(arrays)
+    return pl.pallas_call(
+        hold_kernel,
+        in_specs=[ANYWHERE] * (count + 1),
+        out_specs=[ANYWHERE] * count,
+        out_shape=[jax.ShapeDtypeStruct(array.shape, array.dtype) for array in arrays],
+        input_output_aliases={k: k for k in range(count)},
+        cost_estimate=pl.CostEstimate(flops=flops, bytes_accessed=0, transcendentals=0),
+        name="hold",
+    )(*arrays, after)
 
 
 def inverse_kernel(gram_ref, out_ref):
@@ -349,15 +366,21 @@
 
     both, gram, away = first_products(tall, other, probes, outputs(0, 1), width)
 
-    inverse, out, after = None, None, away[0]
+    plan = [(c, p) for c in range(CHUNKS) for p in (1, 0) if (c, p) != (0, 1)]
+    rest = rest_products(
+        both, gram, probes, [out for c, p in plan for out in outputs(c, p)], width, away[0]
+    )
+    made = {(0, 1): away}
+    made.update({key: rest[2 * k : 2 * k + 2] for k, key in enumerate(plan)})
+
+    inverse, out, after = None, None, None
     for c in range(CHUNKS):
         g = LANES if c == 0 else 0
         last = c == CHUNKS - 1
-        made = rest_products(
-            both, gram, probes, outputs(c, 0) + ([] if last else outputs(c + 1, 1)), width, after
-        )
-        away_a, away_b = away
-        (own_a, own_b), away = made[:2], made[2:]
+        away_a, away_b = made[c, 1]
+        own_a, own_b = made[c, 0]
+        if c > 0:
+            own_a, own_b = hold([own_a, own_b], after, 6 * probes.shape[0] * width * 4 * own_a.shape[0])
         got_a = over(away_a, 1)
         sum_a = own_a + got_a
         sum_b = own_b + over(away_b, 2)

time: 71.3 us -> 72.6 us (1.018)
  waiting for transfers between devices: 20.9 us -> 22.9 us
  Pallas kernels: 25 us -> 23.2 us
  other arithmetic: 0.64 us -> 2.42 us
    ppermute x20, waiting for transfers between devices: 20.9 us -> 22.9 us  [swap(): return lax.ppermute(value, axis, [(i, i ^ bit) for i in range(size)])]
    pallas_call x3 -> x2, Pallas kernels: 11 us -> 9.2 us  [products(): pl.pallas_call(functools.partial(kernel, plan, grams), in_specs=[TABLE, *...]
    add x2, other arithmetic: 0.05 us -> 0.98 us  [body(): sum_a = own_a + got_a]
    add x2, other arithmetic: 0.06 us -> 0.98 us  [body(): sum_b = own_b + over(away_b, 2)]
  transfers between devices with their start and end apart: 20 -> 20, of which waited for: 10 -> 9; matrix products, arithmetic and copies ran while one was open for 1% -> 4% of each run, Pallas kernels for 18% -> 15%
where the time goes in v22:
time: 72.6 us; the launch traced here: 72.5 us
  starting transfers between devices  23.5 us (32%)
  Pallas kernels  23.2 us (32%)
  waiting for transfers between devices  22.9 us (32%)
  other arithmetic  2.42 us (3%)
    ppermute x20, starting transfers between devices, swap(): return lax.ppermute(value, axis, [(i, i ^ bit) for i in range(size)])  23.5 us
    ppermute x20, waiting for transfers between devices, swap(): return lax.ppermute(value, axis, [(i, i ^ bit) for i in range(size)])  22.9 us
    pallas_call x2, Pallas kernels, products(): pl.pallas_call(functools.partial(kernel, plan, grams), in_specs=[TABLE, *...  9.2 us
    pallas_call x1, Pallas kernels, tall_partial(): pl.pallas_call(tall_kernel, in_specs=[HBM, HBM], out_specs=WHOLE, out_sha...  7.27 us
    pallas_call x3, Pallas kernels, finish(): pl.pallas_call(functools.partial(finish_kernel, [piece[1:] for piece in p...  4.72 us
    pallas_call x1, Pallas kernels, inverse_factor(): pl.pallas_call(inverse_kernel, grid=(1,), in_specs=[pl.BlockSpec((rank, L...  2.01 us
  transfers between devices with their start and end apart: 20, of which 9 were waited for; matrix products, arithmetic and copies ran while one was open for 4% of the time, Pallas kernels for 15%

profile of v22, /device:TPU:0, one launch (start us, length us, event | category | flops | bytes accessed | tf_op | source)
XLA Modules:
  0.0 72.5 jit_solution(2813511862223084070)
XLA Ops:
  0.0 7.3 %tall_partial.1 = f32[48,512]{1,0:T(8,128)S(1)} custom-call(f32[512,8192]{1,0:T(8,128)} %x_hbm.5, f32[48,8192]{1,0:T(8,128)} %bitcast.17), custom_call_target="tpu_custom_call" | custom-call | flops 1207959552 | bytes 16777216 | tf_op jit(solution)/shard_map/tall_partial/pallas_call | solution.py:85
  8.8 2.9 %collective-permute-start.1 = (f32[48,512]{1,0:T(8,128)S(1)}, f32[48,512]{1,0:T(8,128)S(1)}, u32[]{:S(2)}, u32[]{:S(2)}) collective-permute-start(f32[48,512]{1,0:T(8,128)S(1)} %add.158.one_ref), channel_id=1, source_target_pairs={{0,2},{1,3},{2,0},{3,1},{4,6},{5,7},{6,4},{7,5},{8,10},{9,11},{10,... | collective-permute-start | bytes 294920 | tf_op jit(solution)/shard_map/ppermute | solution.py:338
  11.8 3.0 %collective-permute-done.1.two_ref = f32[48,512]{1,0:T(8,128)S(1)} collective-permute-done((f32[48,512]{1,0:T(8,128)S(1)}, f32[48,512]{1,0:T(8,128)S(1)}, u32[]{:S(2)}, u32[]{:S(2)}) %collective-permute-start.1) | collective-permute-done | bytes 98336 | tf_op jit(solution)/shard_map/ppermute | solution.py:338
  14.8 3.4 %first_products.1 = (bf16[96,512]{1,0:T(8,128)(2,1)S(1)}, f32[48,128]{1,0:T(8,128)S(1)}, f32[48,1152]{1,0:T(8,128)S(1)}, f32[48,1024]{1,0:T(8,128)S(1)}) custom-call(s32[4]{0:T(128)S(1)} %pad_add_fusion.1.which_ref, f32[48,512]{1,0:T(8,128)S(1)} %add.158.one_ref, f32[48,512]{1,0:T(8,128)S(1)} %collective-permute-done.1.two_ref, f32[512,8192]{1,0:T(8,128)} %x_hbm.5), custom_call_target="tpu_custom_call" | custom-call | flops 301989888 | bytes 4194304 | tf_op jit(solution)/shard_map/first_products/pallas_call | solution.py:183
  18.2 1.9 %collective-permute-start.6 = (f32[48,1024]{1,0:T(8,128)S(1)}, f32[48,1024]{1,0:T(8,128)S(1)}, u32[]{:S(2)}, u32[]{:S(2)}) collective-permute-start(f32[48,1024]{1,0:T(8,128)S(1)} %get-tuple-element.33), channel_id=1, source_target_pairs={{0,8},{4,12},{8,0},{12,4},{16,24},{20,28},{24,16},{28,20},{1,9},{5... | collective-permute-start | bytes 589832 | tf_op jit(solution)/shard_map/ppermute | solution.py:338
  20.1 1.6 %collective-permute-start.2 = (f32[48,1152]{1,0:T(8,128)S(1)}, f32[48,1152]{1,0:T(8,128)S(1)}, u32[]{:S(2)}, u32[]{:S(2)}) collective-permute-start(f32[48,1152]{1,0:T(8,128)S(1)} %get-tuple-element.24.after_ref), channel_id=1, source_target_pairs={{0,4},{4,0},{8,12},{12,8},{16,20},{20,16},{24,28},{28,24},{1,5},{5... | collective-permute-start | bytes 663560 | tf_op jit(solution)/shard_map/ppermute | solution.py:338
  21.7 5.8 %rest_products.1 = (f32[48,1152]{1,0:T(8,128)S(1)}, f32[48,1024]{1,0:T(8,128)S(1)}, f32[48,1024]{1,0:T(8,128)S(1)}, f32[48,1024]{1,0:T(8,128)S(1)}, f32[48,1024]{1,0:T(8,128)S(1)}, /*index=5*/f32[48,1024]{1,0:T(8,128)S(1)}) custom-call(s32[12]{0:T(128)S(1)} %stack.92.which_ref, bf16[96,512]{1,0:T(8,128)(2,1)S(1)} %get-tuple-element.22.both_ref, ...), custom_call_target="tpu_custom_call" | custom-call | flops 905969664 | bytes 12582912 | tf_op jit(solution)/shard_map/rest_products/pallas_call | solution.py:183
  28.4 1.8 %collective-permute-start.7 = (f32[48,512]{1,0:T(8,128)S(1)}, f32[48,512]{1,0:T(8,128)S(1)}, u32[]{:S(2)}, u32[]{:S(2)}) collective-permute-start(f32[48,512]{1,0:T(8,128)S(1)} %slice.69), channel_id=1, source_target_pairs={{0,4},{4,0},{8,12},{12,8},{16,20},{20,16},{24,28},{28,24},{1,5},{5... | collective-permute-start | bytes 294920 | tf_op jit(solution)/shard_map/ppermute | solution.py:338
  30.3 1.6 %collective-permute-start.5 = (f32[48,640]{1,0:T(8,128)S(1)}, f32[48,640]{1,0:T(8,128)S(1)}, u32[]{:S(2)}, u32[]{:S(2)}) collective-permute-start(f32[48,640]{1,0:T(8,128)S(1)} %slice.64), channel_id=1, source_target_pairs={{0,8},{4,12},{8,0},{12,4},{16,24},{20,28},{24,16},{28,20},{1,9},{5... | collective-permute-start | bytes 368648 | tf_op jit(solution)/shard_map/ppermute | solution.py:338
  31.9 2.6 %collective-permute-done.4 = f32[48,1024]{1,0:T(8,128)S(1)} collective-permute-done((f32[48,1024]{1,0:T(8,128)S(1)}, f32[48,1024]{1,0:T(8,128)S(1)}, u32[]{:S(2)}, u32[]{:S(2)}) %collective-permute-start.4) | collective-permute-done | bytes 196640 | tf_op jit(solution)/shard_map/ppermute | solution.py:338
  34.5 1.0 %add.160 = f32[48,1024]{1,0:T(8,128)S(1)} add(f32[48,1024]{1,0:T(8,128)} %get-tuple-element.29, f32[48,1024]{1,0:T(8,128)S(1)} %collective-permute-done.4) | non-fusion elementwise | flops 49152 | bytes 589824 | tf_op jit(solution)/shard_map/add | solution.py:386
  35.5 1.0 %add.159 = f32[48,1024]{1,0:T(8,128)S(1)} add(f32[48,1024]{1,0:T(8,128)} %get-tuple-element.27, f32[48,1024]{1,0:T(8,128)S(1)} %collective-permute-done.3) | non-fusion elementwise | flops 49152 | bytes 589824 | tf_op jit(solution)/shard_map/add | solution.py:385
  37.3 2.6 %collective-permute-start.11 = (f32[48,1152]{1,0:T(8,128)S(1)}, f32[48,1152]{1,0:T(8,128)S(1)}, u32[]{:S(2)}, u32[]{:S(2)}) collective-permute-start(f32[48,1152]{1,0:T(8,128)S(1)} %pad_maximum_fusion), channel_id=1, source_target_pairs={{0,16},{4,20},{8,24},{12,28},{16,0},{20,4},{24,8},{28,12},{1,17},{... | collective-permute-start | bytes 663560 | tf_op jit(solution)/shard_map/ppermute | solution.py:338
  41.3 3.2 %collective-permute-done.9 = f32[48,512]{1,0:T(8,128)S(1)} collective-permute-done((f32[48,512]{1,0:T(8,128)S(1)}, f32[48,512]{1,0:T(8,128)S(1)}, u32[]{:S(2)}, u32[]{:S(2)}) %collective-permute-start.9) | collective-permute-done | bytes 98336 | tf_op jit(solution)/shard_map/ppermute | solution.py:338
  44.9 8.5 %collective-permute-done.11 = f32[48,1152]{1,0:T(8,128)S(1)} collective-permute-done((f32[48,1152]{1,0:T(8,128)S(1)}, f32[48,1152]{1,0:T(8,128)S(1)}, u32[]{:S(2)}, u32[]{:S(2)}) %collective-permute-start.11) | collective-permute-done | bytes 221216 | tf_op jit(solution)/shard_map/ppermute | solution.py:338
  54.7 2.0 %inverse_factor.1.inverse_ref = f32[48,48]{1,0:T(8,128)S(1)} custom-call(f32[48,1152]{1,0:T(8,128)S(1)} %fusion.1.gram_ref.refs_0_), custom_call_target="tpu_custom_call" | custom-call | flops 20000000 | bytes 49152 | tf_op jit(solution)/shard_map/inverse_factor/pallas_call | solution.py:275
  56.8 1.4 %collective-permute-start.12 = (f32[48,512]{1,0:T(8,128)S(1)}, f32[48,512]{1,0:T(8,128)S(1)}, u32[]{:S(2)}, u32[]{:S(2)}) collective-permute-start(f32[48,512]{1,0:T(8,128)S(1)} %get-tuple-element.37), channel_id=1, source_target_pairs={{0,8},{4,12},{8,0},{12,4},{16,24},{20,28},{24,16},{28,20},{1,9},{5... | collective-permute-start | bytes 294920 | tf_op jit(solution)/shard_map/ppermute | solution.py:338
  58.2 1.6 %collective-permute-start.14 = (f32[48,512]{1,0:T(8,128)S(1)}, f32[48,512]{1,0:T(8,128)S(1)}, u32[]{:S(2)}, u32[]{:S(2)}) collective-permute-start(f32[48,512]{1,0:T(8,128)S(1)} %get-tuple-element.38), channel_id=1, source_target_pairs={{0,4},{4,0},{8,12},{12,8},{16,20},{20,16},{24,28},{28,24},{1,5},{5... | collective-permute-start | bytes 294920 | tf_op jit(solution)/shard_map/ppermute | solution.py:338
  61.3 2.2 %collective-permute-done.14.refs_2_ = f32[48,512]{1,0:T(8,128)S(1)} collective-permute-done((f32[48,512]{1,0:T(8,128)S(1)}, f32[48,512]{1,0:T(8,128)S(1)}, u32[]{:S(2)}, u32[]{:S(2)}) %collective-permute-start.14) | collective-permute-done | bytes 98336 | tf_op jit(solution)/shard_map/ppermute | solution.py:338
  63.5 1.2 %collective-permute-start.15 = (f32[48,1024]{1,0:T(8,128)S(1)}, f32[48,1024]{1,0:T(8,128)S(1)}, u32[]{:S(2)}, u32[]{:S(2)}) collective-permute-start(f32[48,1024]{1,0:T(8,128)S(1)} %pad_maximum_fusion.3), channel_id=1, source_target_pairs={{0,8},{4,12},{8,0},{12,4},{16,24},{20,28},{24,16},{28,20},{1,9},{5... | collective-permute-start | bytes 589832 | tf_op jit(solution)/shard_map/ppermute | solution.py:338
  64.7 1.3 %collective-permute-start.13 = (f32[48,1024]{1,0:T(8,128)S(1)}, f32[48,1024]{1,0:T(8,128)S(1)}, u32[]{:S(2)}, u32[]{:S(2)}) collective-permute-start(f32[48,1024]{1,0:T(8,128)S(1)} %pad_maximum_fusion.2), channel_id=1, source_target_pairs={{0,4},{4,0},{8,12},{12,8},{16,20},{20,16},{24,28},{28,24},{1,5},{5... | collective-permute-start | bytes 589832 | tf_op jit(solution)/shard_map/ppermute | solution.py:338
  67.7 1.7 %finish.3.refs_3_ = f32[48,8192]{1,0:T(8,128)} custom-call(s32[8]{0:T(128)S(1)} %stack.99.where_ref, f32[48,48]{1,0:T(8,128)S(1)} %inverse_factor.1.inverse_ref, f32[48,1152]{1,0:T(8,128)S(1)} %fusion.1.gram_ref.refs_0_, f32[48,512]{1,0:T(8,128)S(1)} %collective-permute-done.16.refs_1_, f32[48,512]{1,0:T(8,128)S(1)} %collective-permute-done.17.refs_2_, ...), custom_call_target="tpu_custom_call" | custom-call | flops 56623104 | bytes 1572864 | tf_op jit(solution)/shard_map/finish/pallas_call | solution.py:316
  69.4 1.5 %finish.4.refs_2_ = f32[48,8192]{1,0:T(8,128)} custom-call(s32[4]{0:T(128)S(1)} %pad_add_fusion.2.where_ref, f32[48,48]{1,0:T(8,128)S(1)} %inverse_factor.1.inverse_ref, f32[48,1024]{1,0:T(8,128)S(1)} %fusion.refs_0_, f32[48,512]{1,0:T(8,128)S(1)} %collective-permute-done.12.refs_1_, ...), custom_call_target="tpu_custom_call", output_to_operand_aliasing={{}: (5, {})} | custom-call | flops 28311552 | bytes 786432 | tf_op jit(solution)/shard_map/finish/pallas_call | solution.py:316
  71.0 1.5 %finish.5 = f32[48,8192]{1,0:T(8,128)} custom-call(s32[4]{0:T(128)S(1)} %pad_add_fusion.where_ref, f32[48,48]{1,0:T(8,128)S(1)} %inverse_factor.1.inverse_ref, f32[48,1024]{1,0:T(8,128)S(1)} %collective-permute-done.13.refs_0_, f32[48,1024]{1,0:T(8,128)S(1)} %collective-permute-done.15.refs_1_, f32[48,8192]{1,0:T(8,128)} %finish.4.refs_2_), custom_call_target="tpu_custom_call", output_to_operand_aliasing={{}: (4, {})} | custom-call | flops 28311552 | bytes 786432 | tf_op jit(solution)/shard_map/finish/pallas_call | solution.py:316
  (59 shorter events, 9.8 us)
Async XLA Ops:
  7.3 1.5 %collective-permute-start = (f32[48,512]{1,0:T(8,128)S(1)}, f32[48,512]{1,0:T(8,128)S(1)}, u32[]{:S(2)}, u32[]{:S(2)}) collective-permute-start(f32[48,512]{1,0:T(8,128)S(1)} %tall_partial.1), channel_id=1, source_target_pairs={{0,1},{1,0},{2,3},{3,2},{4,5},{5,4},{6,7},{7,6},{8,9},{9,8},{10,11... | collective-permute-start | bytes 294920 | tf_op jit(solution)/shard_map/ppermute | solution.py:338
  8.8 6.0 %collective-permute-start.1 = (f32[48,512]{1,0:T(8,128)S(1)}, f32[48,512]{1,0:T(8,128)S(1)}, u32[]{:S(2)}, u32[]{:S(2)}) collective-permute-start(f32[48,512]{1,0:T(8,128)S(1)} %add.158.one_ref), channel_id=1, source_target_pairs={{0,2},{1,3},{2,0},{3,1},{4,6},{5,7},{6,4},{7,5},{8,10},{9,11},{10,... | collective-permute-start | bytes 294920 | tf_op jit(solution)/shard_map/ppermute | solution.py:338
  18.2 10.2 %collective-permute-start.6 = (f32[48,1024]{1,0:T(8,128)S(1)}, f32[48,1024]{1,0:T(8,128)S(1)}, u32[]{:S(2)}, u32[]{:S(2)}) collective-permute-start(f32[48,1024]{1,0:T(8,128)S(1)} %get-tuple-element.33), channel_id=1, source_target_pairs={{0,8},{4,12},{8,0},{12,4},{16,24},{20,28},{24,16},{28,20},{1,9},{5... | collective-permute-start | bytes 589832 | tf_op jit(solution)/shard_map/ppermute | solution.py:338
  20.1 10.1 %collective-permute-start.2 = (f32[48,1152]{1,0:T(8,128)S(1)}, f32[48,1152]{1,0:T(8,128)S(1)}, u32[]{:S(2)}, u32[]{:S(2)}) collective-permute-start(f32[48,1152]{1,0:T(8,128)S(1)} %get-tuple-element.24.after_ref), channel_id=1, source_target_pairs={{0,4},{4,0},{8,12},{12,8},{16,20},{20,16},{24,28},{28,24},{1,5},{5... | collective-permute-start | bytes 663560 | tf_op jit(solution)/shard_map/ppermute | solution.py:338
  27.5 2.7 %copy-start = (f32[48,1024]{1,0:T(8,128)}, f32[48,1024]{1,0:T(8,128)S(1)}, u32[]{:S(2)}) copy-start(f32[48,1024]{1,0:T(8,128)S(1)} %get-tuple-element.25.refs_0_) | copy-start | bytes 589828
  27.6 2.7 %copy-start.1 = (f32[48,1024]{1,0:T(8,128)}, f32[48,1024]{1,0:T(8,128)S(1)}, u32[]{:S(2)}) copy-start(f32[48,1024]{1,0:T(8,128)S(1)} %get-tuple-element.26.refs_1_) | copy-start | bytes 589828
  27.6 6.9 %collective-permute-start.4 = (f32[48,1024]{1,0:T(8,128)S(1)}, f32[48,1024]{1,0:T(8,128)S(1)}, u32[]{:S(2)}, u32[]{:S(2)}) collective-permute-start(f32[48,1024]{1,0:T(8,128)S(1)} %get-tuple-element.30), channel_id=1, source_target_pairs={{0,8},{4,12},{8,0},{12,4},{16,24},{20,28},{24,16},{28,20},{1,9},{5... | collective-permute-start | bytes 589832 | tf_op jit(solution)/shard_map/ppermute | solution.py:338
  28.1 7.4 %collective-permute-start.3 = (f32[48,1024]{1,0:T(8,128)S(1)}, f32[48,1024]{1,0:T(8,128)S(1)}, u32[]{:S(2)}, u32[]{:S(2)}) collective-permute-start(f32[48,1024]{1,0:T(8,128)S(1)} %get-tuple-element.28), channel_id=1, source_target_pairs={{0,4},{4,0},{8,12},{12,8},{16,20},{20,16},{24,28},{28,24},{1,5},{5... | collective-permute-start | bytes 589832 | tf_op jit(solution)/shard_map/ppermute | solution.py:338
  28.4 8.0 %collective-permute-start.7 = (f32[48,512]{1,0:T(8,128)S(1)}, f32[48,512]{1,0:T(8,128)S(1)}, u32[]{:S(2)}, u32[]{:S(2)}) collective-permute-start(f32[48,512]{1,0:T(8,128)S(1)} %slice.69), channel_id=1, source_target_pairs={{0,4},{4,0},{8,12},{12,8},{16,20},{20,16},{24,28},{28,24},{1,5},{5... | collective-permute-start | bytes 294920 | tf_op jit(solution)/shard_map/ppermute | solution.py:338
  30.2 1.7 %copy-start.2 = (f32[48,1152]{1,0:T(8,128)}, f32[48,1152]{1,0:T(8,128)S(1)}, u32[]{:S(2)}) copy-start(f32[48,1152]{1,0:T(8,128)S(1)} %collective-permute-done.2.refs_2_) | copy-start | bytes 663556
  30.3 6.2 %collective-permute-start.5 = (f32[48,640]{1,0:T(8,128)S(1)}, f32[48,640]{1,0:T(8,128)S(1)}, u32[]{:S(2)}, u32[]{:S(2)}) collective-permute-start(f32[48,640]{1,0:T(8,128)S(1)} %slice.64), channel_id=1, source_target_pairs={{0,8},{4,12},{8,0},{12,4},{16,24},{20,28},{24,16},{28,20},{1,9},{5... | collective-permute-start | bytes 368648 | tf_op jit(solution)/shard_map/ppermute | solution.py:338
  36.6 4.7 %collective-permute-start.8 = (f32[48,512]{1,0:T(8,128)S(1)}, f32[48,512]{1,0:T(8,128)S(1)}, u32[]{:S(2)}, u32[]{:S(2)}) collective-permute-start(f32[48,512]{1,0:T(8,128)S(1)} %slice.61), channel_id=1, source_target_pairs={{0,8},{4,12},{8,0},{12,4},{16,24},{20,28},{24,16},{28,20},{1,9},{5... | collective-permute-start | bytes 294920 | tf_op jit(solution)/shard_map/ppermute | solution.py:338
  37.3 16.1 %collective-permute-start.11 = (f32[48,1152]{1,0:T(8,128)S(1)}, f32[48,1152]{1,0:T(8,128)S(1)}, u32[]{:S(2)}, u32[]{:S(2)}) collective-permute-start(f32[48,1152]{1,0:T(8,128)S(1)} %pad_maximum_fusion), channel_id=1, source_target_pairs={{0,16},{4,20},{8,24},{12,28},{16,0},{20,4},{24,8},{28,12},{1,17},{... | collective-permute-start | bytes 663560 | tf_op jit(solution)/shard_map/ppermute | solution.py:338
  39.9 4.6 %collective-permute-start.9 = (f32[48,512]{1,0:T(8,128)S(1)}, f32[48,512]{1,0:T(8,128)S(1)}, u32[]{:S(2)}, u32[]{:S(2)}) collective-permute-start(f32[48,512]{1,0:T(8,128)S(1)} %slice.62), channel_id=1, source_target_pairs={{0,4},{4,0},{8,12},{12,8},{16,20},{20,16},{24,28},{28,24},{1,5},{5... | collective-permute-start | bytes 294920 | tf_op jit(solution)/shard_map/ppermute | solution.py:338
  44.5 12.2 %collective-permute-start.10 = (f32[48,1024]{1,0:T(8,128)S(1)}, f32[48,1024]{1,0:T(8,128)S(1)}, u32[]{:S(2)}, u32[]{:S(2)}) collective-permute-start(f32[48,1024]{1,0:T(8,128)S(1)} %pad_maximum_fusion.1), channel_id=1, source_target_pairs={{0,16},{4,20},{8,24},{12,28},{16,0},{20,4},{24,8},{28,12},{1,17},{... | collective-permute-start | bytes 589832 | tf_op jit(solution)/shard_map/ppermute | solution.py:338
  53.5 6.3 %collective-permute-start.17 = (f32[48,512]{1,0:T(8,128)S(1)}, f32[48,512]{1,0:T(8,128)S(1)}, u32[]{:S(2)}, u32[]{:S(2)}) collective-permute-start(f32[48,512]{1,0:T(8,128)S(1)} %get-tuple-element.39), channel_id=1, source_target_pairs={{0,4},{4,0},{8,12},{12,8},{16,20},{20,16},{24,28},{28,24},{1,5},{5... | collective-permute-start | bytes 294920 | tf_op jit(solution)/shard_map/ppermute | solution.py:338
  54.0 6.5 %collective-permute-start.16 = (f32[48,512]{1,0:T(8,128)S(1)}, f32[48,512]{1,0:T(8,128)S(1)}, u32[]{:S(2)}, u32[]{:S(2)}) collective-permute-start(f32[48,512]{1,0:T(8,128)S(1)} %get-tuple-element.40), channel_id=1, source_target_pairs={{0,8},{4,12},{8,0},{12,4},{16,24},{20,28},{24,16},{28,20},{1,9},{5... | collective-permute-start | bytes 294920 | tf_op jit(solution)/shard_map/ppermute | solution.py:338
  56.8 7.9 %collective-permute-start.12 = (f32[48,512]{1,0:T(8,128)S(1)}, f32[48,512]{1,0:T(8,128)S(1)}, u32[]{:S(2)}, u32[]{:S(2)}) collective-permute-start(f32[48,512]{1,0:T(8,128)S(1)} %get-tuple-element.37), channel_id=1, source_target_pairs={{0,8},{4,12},{8,0},{12,4},{16,24},{20,28},{24,16},{28,20},{1,9},{5... | collective-permute-start | bytes 294920 | tf_op jit(solution)/shard_map/ppermute | solution.py:338
  58.2 5.4 %collective-permute-start.14 = (f32[48,512]{1,0:T(8,128)S(1)}, f32[48,512]{1,0:T(8,128)S(1)}, u32[]{:S(2)}, u32[]{:S(2)}) collective-permute-start(f32[48,512]{1,0:T(8,128)S(1)} %get-tuple-element.38), channel_id=1, source_target_pairs={{0,4},{4,0},{8,12},{12,8},{16,20},{20,16},{24,28},{28,24},{1,5},{5... | collective-permute-start | bytes 294920 | tf_op jit(solution)/shard_map/ppermute | solution.py:338
  59.8 7.3 %collective-permute-start.19 = (f32[48,1024]{1,0:T(8,128)S(1)}, f32[48,1024]{1,0:T(8,128)S(1)}, u32[]{:S(2)}, u32[]{:S(2)}) collective-permute-start(f32[48,1024]{1,0:T(8,128)S(1)} %pad_maximum_fusion.5), channel_id=1, source_target_pairs={{0,8},{4,12},{8,0},{12,4},{16,24},{20,28},{24,16},{28,20},{1,9},{5... | collective-permute-start | bytes 589832 | tf_op jit(solution)/shard_map/ppermute | solution.py:338
  60.5 7.2 %collective-permute-start.18 = (f32[48,1024]{1,0:T(8,128)S(1)}, f32[48,1024]{1,0:T(8,128)S(1)}, u32[]{:S(2)}, u32[]{:S(2)}) collective-permute-start(f32[48,1024]{1,0:T(8,128)S(1)} %pad_maximum_fusion.4), channel_id=1, source_target_pairs={{0,4},{4,0},{8,12},{12,8},{16,20},{20,16},{24,28},{28,24},{1,5},{5... | collective-permute-start | bytes 589832 | tf_op jit(solution)/shard_map/ppermute | solution.py:338
  63.5 7.4 %collective-permute-start.15 = (f32[48,1024]{1,0:T(8,128)S(1)}, f32[48,1024]{1,0:T(8,128)S(1)}, u32[]{:S(2)}, u32[]{:S(2)}) collective-permute-start(f32[48,1024]{1,0:T(8,128)S(1)} %pad_maximum_fusion.3), channel_id=1, source_target_pairs={{0,8},{4,12},{8,0},{12,4},{16,24},{20,28},{24,16},{28,20},{1,9},{5... | collective-permute-start | bytes 589832 | tf_op jit(solution)/shard_map/ppermute | solution.py:338
  64.7 6.2 %collective-permute-start.13 = (f32[48,1024]{1,0:T(8,128)S(1)}, f32[48,1024]{1,0:T(8,128)S(1)}, u32[]{:S(2)}, u32[]{:S(2)}) collective-permute-start(f32[48,1024]{1,0:T(8,128)S(1)} %pad_maximum_fusion.2), channel_id=1, source_target_pairs={{0,4},{4,0},{8,12},{12,8},{16,20},{20,16},{24,28},{28,24},{1,5},{5... | collective-permute-start | bytes 589832 | tf_op jit(solution)/shard_map/ppermute | solution.py:338

commit v23 on v22

--- a/solution.py
+++ b/solution.py
@@ -231,18 +231,19 @@
     )
 
 
-def hold_kernel(*refs):
-    pass
+def hold_kernel(count, *refs):
+    for k in range(count):
+        refs[count + 1 + k][...] = refs[k][...]
 
 
 def hold(arrays, after, flops):
     count = len(arrays)
     return pl.pallas_call(
-        hold_kernel,
-        in_specs=[ANYWHERE] * (count + 1),
-        out_specs=[ANYWHERE] * count,
+        functools.partial(hold_kernel, count),
+        in_specs=[WHOLE] * count + [ANYWHERE],
+        out_specs=[WHOLE] * count,
         out_shape=[jax.ShapeDtypeStruct(array.shape, array.dtype) for array in arrays],
-        input_output_aliases={k: k for k in range(count)},
+        compiler_params=PARAMS,
         cost_estimate=pl.CostEstimate(flops=flops, bytes_accessed=0, transcendentals=0),
         name="hold",
     )(*arrays, after)

time: 72.6 us -> 72.6 us (level)
  other arithmetic: 2.42 us -> 0.57 us
  waiting for transfers between devices: 22.9 us -> 24.2 us
    ppermute x20, waiting for transfers between devices: 22.9 us -> 24.2 us  [swap(): return lax.ppermute(value, axis, [(i, i ^ bit) for i in range(size)])]
    add x2, other arithmetic: 0.98 us -> 0.05 us  [body(): sum_b = own_b + over(away_b, 2)]
    add x2, other arithmetic: 0.98 us -> 0.06 us  [body(): sum_a = own_a + got_a]
  transfers between devices with their start and end apart: 20 -> 20, of which waited for: 9 -> 11; matrix products, arithmetic and copies ran while one was open for 4% -> 1% of each run, Pallas kernels for 15% -> 15%
where the time goes in v23:
time: 72.6 us; the launch traced here: 72.4 us
  waiting for transfers between devices  24.2 us (33%)
  starting transfers between devices  24 us (33%)
  Pallas kernels  23.2 us (32%)
    ppermute x20, waiting for transfers between devices, swap(): return lax.ppermute(value, axis, [(i, i ^ bit) for i in range(size)])  24.2 us
    ppermute x20, starting transfers between devices, swap(): return lax.ppermute(value, axis, [(i, i ^ bit) for i in range(size)])  24 us
    pallas_call x2, Pallas kernels, products(): pl.pallas_call(functools.partial(kernel, plan, grams), in_specs=[TABLE, *...  9.2 us
    pallas_call x1, Pallas kernels, tall_partial(): pl.pallas_call(tall_kernel, in_specs=[HBM, HBM], out_specs=WHOLE, out_sha...  7.27 us
    pallas_call x3, Pallas kernels, finish(): pl.pallas_call(functools.partial(finish_kernel, [piece[1:] for piece in p...  4.72 us
    pallas_call x1, Pallas kernels, inverse_factor(): pl.pallas_call(inverse_kernel, grid=(1,), in_specs=[pl.BlockSpec((rank, L...  2.01 us
  transfers between devices with their start and end apart: 20, of which 11 were waited for; matrix products, arithmetic and copies ran while one was open for 1% of the time, Pallas kernels for 15%

profile of v23, /device:TPU:0, one launch (start us, length us, event | category | flops | bytes accessed | tf_op | source)
XLA Modules:
  0.0 72.4 jit_solution(16612646883414158225)
XLA Ops:
  0.0 7.3 %tall_partial.1 = f32[48,512]{1,0:T(8,128)S(1)} custom-call(f32[512,8192]{1,0:T(8,128)} %x_hbm.5, f32[48,8192]{1,0:T(8,128)} %bitcast.17), custom_call_target="tpu_custom_call" | custom-call | flops 1207959552 | bytes 16777216 | tf_op jit(solution)/shard_map/tall_partial/pallas_call | solution.py:85
  8.8 2.9 %collective-permute-start.1 = (f32[48,512]{1,0:T(8,128)S(1)}, f32[48,512]{1,0:T(8,128)S(1)}, u32[]{:S(2)}, u32[]{:S(2)}) collective-permute-start(f32[48,512]{1,0:T(8,128)S(1)} %add.158.one_ref), channel_id=1, source_target_pairs={{0,2},{1,3},{2,0},{3,1},{4,6},{5,7},{6,4},{7,5},{8,10},{9,11},{10,... | collective-permute-start | bytes 294920 | tf_op jit(solution)/shard_map/ppermute | solution.py:339
  11.8 3.0 %collective-permute-done.1.two_ref = f32[48,512]{1,0:T(8,128)S(1)} collective-permute-done((f32[48,512]{1,0:T(8,128)S(1)}, f32[48,512]{1,0:T(8,128)S(1)}, u32[]{:S(2)}, u32[]{:S(2)}) %collective-permute-start.1) | collective-permute-done | bytes 98336 | tf_op jit(solution)/shard_map/ppermute | solution.py:339
  14.8 3.4 %first_products.1 = (bf16[96,512]{1,0:T(8,128)(2,1)S(1)}, f32[48,128]{1,0:T(8,128)S(1)}, f32[48,1152]{1,0:T(8,128)S(1)}, f32[48,1024]{1,0:T(8,128)S(1)}) custom-call(s32[4]{0:T(128)S(1)} %pad_add_fusion.1.which_ref, f32[48,512]{1,0:T(8,128)S(1)} %add.158.one_ref, f32[48,512]{1,0:T(8,128)S(1)} %collective-permute-done.1.two_ref, f32[512,8192]{1,0:T(8,128)} %x_hbm.5), custom_call_target="tpu_custom_call" | custom-call | flops 301989888 | bytes 4194304 | tf_op jit(solution)/shard_map/first_products/pallas_call | solution.py:183
  18.2 1.9 %collective-permute-start.6 = (f32[48,1024]{1,0:T(8,128)S(1)}, f32[48,1024]{1,0:T(8,128)S(1)}, u32[]{:S(2)}, u32[]{:S(2)}) collective-permute-start(f32[48,1024]{1,0:T(8,128)S(1)} %get-tuple-element.33), channel_id=1, source_target_pairs={{0,8},{4,12},{8,0},{12,4},{16,24},{20,28},{24,16},{28,20},{1,9},{5... | collective-permute-start | bytes 589832 | tf_op jit(solution)/shard_map/ppermute | solution.py:339
  20.1 1.6 %collective-permute-start.2 = (f32[48,1152]{1,0:T(8,128)S(1)}, f32[48,1152]{1,0:T(8,128)S(1)}, u32[]{:S(2)}, u32[]{:S(2)}) collective-permute-start(f32[48,1152]{1,0:T(8,128)S(1)} %get-tuple-element.24.after_ref), channel_id=1, source_target_pairs={{0,4},{4,0},{8,12},{12,8},{16,20},{20,16},{24,28},{28,24},{1,5},{5... | collective-permute-start | bytes 663560 | tf_op jit(solution)/shard_map/ppermute | solution.py:339
  21.7 5.8 %rest_products.1 = (f32[48,1152]{1,0:T(8,128)S(1)}, f32[48,1024]{1,0:T(8,128)S(1)}, f32[48,1024]{1,0:T(8,128)S(1)}, f32[48,1024]{1,0:T(8,128)S(1)}, f32[48,1024]{1,0:T(8,128)S(1)}, /*index=5*/f32[48,1024]{1,0:T(8,128)S(1)}) custom-call(s32[12]{0:T(128)S(1)} %stack.92.which_ref, bf16[96,512]{1,0:T(8,128)(2,1)S(1)} %get-tuple-element.22.both_ref, ...), custom_call_target="tpu_custom_call" | custom-call | flops 905969664 | bytes 12582912 | tf_op jit(solution)/shard_map/rest_products/pallas_call | solution.py:183
  28.4 1.8 %collective-permute-start.7 = (f32[48,512]{1,0:T(8,128)S(1)}, f32[48,512]{1,0:T(8,128)S(1)}, u32[]{:S(2)}, u32[]{:S(2)}) collective-permute-start(f32[48,512]{1,0:T(8,128)S(1)} %slice.69), channel_id=1, source_target_pairs={{0,4},{4,0},{8,12},{12,8},{16,20},{20,16},{24,28},{28,24},{1,5},{5... | collective-permute-start | bytes 294920 | tf_op jit(solution)/shard_map/ppermute | solution.py:339
  30.3 1.6 %collective-permute-start.5 = (f32[48,640]{1,0:T(8,128)S(1)}, f32[48,640]{1,0:T(8,128)S(1)}, u32[]{:S(2)}, u32[]{:S(2)}) collective-permute-start(f32[48,640]{1,0:T(8,128)S(1)} %slice.64), channel_id=1, source_target_pairs={{0,8},{4,12},{8,0},{12,4},{16,24},{20,28},{24,16},{28,20},{1,9},{5... | collective-permute-start | bytes 368648 | tf_op jit(solution)/shard_map/ppermute | solution.py:339
  31.9 2.6 %collective-permute-done.4 = f32[48,1024]{1,0:T(8,128)S(1)} collective-permute-done((f32[48,1024]{1,0:T(8,128)S(1)}, f32[48,1024]{1,0:T(8,128)S(1)}, u32[]{:S(2)}, u32[]{:S(2)}) %collective-permute-start.4) | collective-permute-done | bytes 196640 | tf_op jit(solution)/shard_map/ppermute | solution.py:339
  35.9 1.3 %collective-permute-start.8 = (f32[48,512]{1,0:T(8,128)S(1)}, f32[48,512]{1,0:T(8,128)S(1)}, u32[]{:S(2)}, u32[]{:S(2)}) collective-permute-start(f32[48,512]{1,0:T(8,128)S(1)} %slice.61), channel_id=1, source_target_pairs={{0,8},{4,12},{8,0},{12,4},{16,24},{20,28},{24,16},{28,20},{1,9},{5... | collective-permute-start | bytes 294920 | tf_op jit(solution)/shard_map/ppermute | solution.py:339
  37.3 2.6 %collective-permute-start.11 = (f32[48,1152]{1,0:T(8,128)S(1)}, f32[48,1152]{1,0:T(8,128)S(1)}, u32[]{:S(2)}, u32[]{:S(2)}) collective-permute-start(f32[48,1152]{1,0:T(8,128)S(1)} %pad_maximum_fusion), channel_id=1, source_target_pairs={{0,16},{4,20},{8,24},{12,28},{16,0},{20,4},{24,8},{28,12},{1,17},{... | collective-permute-start | bytes 663560 | tf_op jit(solution)/shard_map/ppermute | solution.py:339
  40.6 3.8 %collective-permute-done.9 = f32[48,512]{1,0:T(8,128)S(1)} collective-permute-done((f32[48,512]{1,0:T(8,128)S(1)}, f32[48,512]{1,0:T(8,128)S(1)}, u32[]{:S(2)}, u32[]{:S(2)}) %collective-permute-start.9) | collective-permute-done | bytes 98336 | tf_op jit(solution)/shard_map/ppermute | solution.py:339
  44.9 8.5 %collective-permute-done.11 = f32[48,1152]{1,0:T(8,128)S(1)} collective-permute-done((f32[48,1152]{1,0:T(8,128)S(1)}, f32[48,1152]{1,0:T(8,128)S(1)}, u32[]{:S(2)}, u32[]{:S(2)}) %collective-permute-start.11) | collective-permute-done | bytes 221216 | tf_op jit(solution)/shard_map/ppermute | solution.py:339
  54.7 2.0 %inverse_factor.1.inverse_ref = f32[48,48]{1,0:T(8,128)S(1)} custom-call(f32[48,1152]{1,0:T(8,128)S(1)} %fusion.1.gram_ref.refs_0_), custom_call_target="tpu_custom_call" | custom-call | flops 20000000 | bytes 49152 | tf_op jit(solution)/shard_map/inverse_factor/pallas_call | solution.py:276
  56.7 1.4 %collective-permute-start.12 = (f32[48,512]{1,0:T(8,128)S(1)}, f32[48,512]{1,0:T(8,128)S(1)}, u32[]{:S(2)}, u32[]{:S(2)}) collective-permute-start(f32[48,512]{1,0:T(8,128)S(1)} %get-tuple-element.37), channel_id=1, source_target_pairs={{0,8},{4,12},{8,0},{12,4},{16,24},{20,28},{24,16},{28,20},{1,9},{5... | collective-permute-start | bytes 294920 | tf_op jit(solution)/shard_map/ppermute | solution.py:339
  58.2 1.6 %collective-permute-start.14 = (f32[48,512]{1,0:T(8,128)S(1)}, f32[48,512]{1,0:T(8,128)S(1)}, u32[]{:S(2)}, u32[]{:S(2)}) collective-permute-start(f32[48,512]{1,0:T(8,128)S(1)} %get-tuple-element.38), channel_id=1, source_target_pairs={{0,4},{4,0},{8,12},{12,8},{16,20},{20,16},{24,28},{28,24},{1,5},{5... | collective-permute-start | bytes 294920 | tf_op jit(solution)/shard_map/ppermute | solution.py:339
  61.3 2.2 %collective-permute-done.14.refs_2_ = f32[48,512]{1,0:T(8,128)S(1)} collective-permute-done((f32[48,512]{1,0:T(8,128)S(1)}, f32[48,512]{1,0:T(8,128)S(1)}, u32[]{:S(2)}, u32[]{:S(2)}) %collective-permute-start.14) | collective-permute-done | bytes 98336 | tf_op jit(solution)/shard_map/ppermute | solution.py:339
  63.5 1.1 %collective-permute-start.15 = (f32[48,1024]{1,0:T(8,128)S(1)}, f32[48,1024]{1,0:T(8,128)S(1)}, u32[]{:S(2)}, u32[]{:S(2)}) collective-permute-start(f32[48,1024]{1,0:T(8,128)S(1)} %pad_maximum_fusion.3), channel_id=1, source_target_pairs={{0,8},{4,12},{8,0},{12,4},{16,24},{20,28},{24,16},{28,20},{1,9},{5... | collective-permute-start | bytes 589832 | tf_op jit(solution)/shard_map/ppermute | solution.py:339
  64.7 1.2 %collective-permute-start.13 = (f32[48,1024]{1,0:T(8,128)S(1)}, f32[48,1024]{1,0:T(8,128)S(1)}, u32[]{:S(2)}, u32[]{:S(2)}) collective-permute-start(f32[48,1024]{1,0:T(8,128)S(1)} %pad_maximum_fusion.2), channel_id=1, source_target_pairs={{0,4},{4,0},{8,12},{12,8},{16,20},{20,16},{24,28},{28,24},{1,5},{5... | collective-permute-start | bytes 589832 | tf_op jit(solution)/shard_map/ppermute | solution.py:339
  66.0 1.0 %collective-permute-done.19.refs_4_ = f32[48,1024]{1,0:T(8,128)S(1)} collective-permute-done((f32[48,1024]{1,0:T(8,128)S(1)}, f32[48,1024]{1,0:T(8,128)S(1)}, u32[]{:S(2)}, u32[]{:S(2)}) %collective-permute-start.19) | collective-permute-done | bytes 196640 | tf_op jit(solution)/shard_map/ppermute | solution.py:339
  67.7 1.7 %finish.3.refs_3_ = f32[48,8192]{1,0:T(8,128)} custom-call(s32[8]{0:T(128)S(1)} %stack.99.where_ref, f32[48,48]{1,0:T(8,128)S(1)} %inverse_factor.1.inverse_ref, f32[48,1152]{1,0:T(8,128)S(1)} %fusion.1.gram_ref.refs_0_, f32[48,512]{1,0:T(8,128)S(1)} %collective-permute-done.16.refs_1_, f32[48,512]{1,0:T(8,128)S(1)} %collective-permute-done.17.refs_2_, ...), custom_call_target="tpu_custom_call" | custom-call | flops 56623104 | bytes 1572864 | tf_op jit(solution)/shard_map/finish/pallas_call | solution.py:317
  69.4 1.5 %finish.4.refs_2_ = f32[48,8192]{1,0:T(8,128)} custom-call(s32[4]{0:T(128)S(1)} %pad_add_fusion.2.where_ref, f32[48,48]{1,0:T(8,128)S(1)} %inverse_factor.1.inverse_ref, f32[48,1024]{1,0:T(8,128)S(1)} %fusion.refs_0_, f32[48,512]{1,0:T(8,128)S(1)} %collective-permute-done.12.refs_1_, ...), custom_call_target="tpu_custom_call", output_to_operand_aliasing={{}: (5, {})} | custom-call | flops 28311552 | bytes 786432 | tf_op jit(solution)/shard_map/finish/pallas_call | solution.py:317
  70.9 1.5 %finish.5 = f32[48,8192]{1,0:T(8,128)} custom-call(s32[4]{0:T(128)S(1)} %pad_add_fusion.where_ref, f32[48,48]{1,0:T(8,128)S(1)} %inverse_factor.1.inverse_ref, f32[48,1024]{1,0:T(8,128)S(1)} %collective-permute-done.13.refs_0_, f32[48,1024]{1,0:T(8,128)S(1)} %collective-permute-done.15.refs_1_, f32[48,8192]{1,0:T(8,128)} %finish.4.refs_2_), custom_call_target="tpu_custom_call", output_to_operand_aliasing={{}: (4, {})} | custom-call | flops 28311552 | bytes 786432 | tf_op jit(solution)/shard_map/finish/pallas_call | solution.py:317
  (53 shorter events, 8.8 us)
Async XLA Ops:
  7.3 1.5 %collective-permute-start = (f32[48,512]{1,0:T(8,128)S(1)}, f32[48,512]{1,0:T(8,128)S(1)}, u32[]{:S(2)}, u32[]{:S(2)}) collective-permute-start(f32[48,512]{1,0:T(8,128)S(1)} %tall_partial.1), channel_id=1, source_target_pairs={{0,1},{1,0},{2,3},{3,2},{4,5},{5,4},{6,7},{7,6},{8,9},{9,8},{10,11... | collective-permute-start | bytes 294920 | tf_op jit(solution)/shard_map/ppermute | solution.py:339
  8.8 6.0 %collective-permute-start.1 = (f32[48,512]{1,0:T(8,128)S(1)}, f32[48,512]{1,0:T(8,128)S(1)}, u32[]{:S(2)}, u32[]{:S(2)}) collective-permute-start(f32[48,512]{1,0:T(8,128)S(1)} %add.158.one_ref), channel_id=1, source_target_pairs={{0,2},{1,3},{2,0},{3,1},{4,6},{5,7},{6,4},{7,5},{8,10},{9,11},{10,... | collective-permute-start | bytes 294920 | tf_op jit(solution)/shard_map/ppermute | solution.py:339
  18.2 10.2 %collective-permute-start.6 = (f32[48,1024]{1,0:T(8,128)S(1)}, f32[48,1024]{1,0:T(8,128)S(1)}, u32[]{:S(2)}, u32[]{:S(2)}) collective-permute-start(f32[48,1024]{1,0:T(8,128)S(1)} %get-tuple-element.33), channel_id=1, source_target_pairs={{0,8},{4,12},{8,0},{12,4},{16,24},{20,28},{24,16},{28,20},{1,9},{5... | collective-permute-start | bytes 589832 | tf_op jit(solution)/shard_map/ppermute | solution.py:339
  20.1 10.1 %collective-permute-start.2 = (f32[48,1152]{1,0:T(8,128)S(1)}, f32[48,1152]{1,0:T(8,128)S(1)}, u32[]{:S(2)}, u32[]{:S(2)}) collective-permute-start(f32[48,1152]{1,0:T(8,128)S(1)} %get-tuple-element.24.after_ref), channel_id=1, source_target_pairs={{0,4},{4,0},{8,12},{12,8},{16,20},{20,16},{24,28},{28,24},{1,5},{5... | collective-permute-start | bytes 663560 | tf_op jit(solution)/shard_map/ppermute | solution.py:339
  27.5 6.9 %collective-permute-start.4 = (f32[48,1024]{1,0:T(8,128)S(1)}, f32[48,1024]{1,0:T(8,128)S(1)}, u32[]{:S(2)}, u32[]{:S(2)}) collective-permute-start(f32[48,1024]{1,0:T(8,128)S(1)} %get-tuple-element.30), channel_id=1, source_target_pairs={{0,8},{4,12},{8,0},{12,4},{16,24},{20,28},{24,16},{28,20},{1,9},{5... | collective-permute-start | bytes 589832 | tf_op jit(solution)/shard_map/ppermute | solution.py:339
  28.1 6.5 %collective-permute-start.3 = (f32[48,1024]{1,0:T(8,128)S(1)}, f32[48,1024]{1,0:T(8,128)S(1)}, u32[]{:S(2)}, u32[]{:S(2)}) collective-permute-start(f32[48,1024]{1,0:T(8,128)S(1)} %get-tuple-element.28), channel_id=1, source_target_pairs={{0,4},{4,0},{8,12},{12,8},{16,20},{20,16},{24,28},{28,24},{1,5},{5... | collective-permute-start | bytes 589832 | tf_op jit(solution)/shard_map/ppermute | solution.py:339
  28.4 7.0 %collective-permute-start.7 = (f32[48,512]{1,0:T(8,128)S(1)}, f32[48,512]{1,0:T(8,128)S(1)}, u32[]{:S(2)}, u32[]{:S(2)}) collective-permute-start(f32[48,512]{1,0:T(8,128)S(1)} %slice.69), channel_id=1, source_target_pairs={{0,4},{4,0},{8,12},{12,8},{16,20},{20,16},{24,28},{28,24},{1,5},{5... | collective-permute-start | bytes 294920 | tf_op jit(solution)/shard_map/ppermute | solution.py:339
  30.3 5.6 %collective-permute-start.5 = (f32[48,640]{1,0:T(8,128)S(1)}, f32[48,640]{1,0:T(8,128)S(1)}, u32[]{:S(2)}, u32[]{:S(2)}) collective-permute-start(f32[48,640]{1,0:T(8,128)S(1)} %slice.64), channel_id=1, source_target_pairs={{0,8},{4,12},{8,0},{12,4},{16,24},{20,28},{24,16},{28,20},{1,9},{5... | collective-permute-start | bytes 368648 | tf_op jit(solution)/shard_map/ppermute | solution.py:339
  35.9 4.8 %collective-permute-start.8 = (f32[48,512]{1,0:T(8,128)S(1)}, f32[48,512]{1,0:T(8,128)S(1)}, u32[]{:S(2)}, u32[]{:S(2)}) collective-permute-start(f32[48,512]{1,0:T(8,128)S(1)} %slice.61), channel_id=1, source_target_pairs={{0,8},{4,12},{8,0},{12,4},{16,24},{20,28},{24,16},{28,20},{1,9},{5... | collective-permute-start | bytes 294920 | tf_op jit(solution)/shard_map/ppermute | solution.py:339
  37.3 16.2 %collective-permute-start.11 = (f32[48,1152]{1,0:T(8,128)S(1)}, f32[48,1152]{1,0:T(8,128)S(1)}, u32[]{:S(2)}, u32[]{:S(2)}) collective-permute-start(f32[48,1152]{1,0:T(8,128)S(1)} %pad_maximum_fusion), channel_id=1, source_target_pairs={{0,16},{4,20},{8,24},{12,28},{16,0},{20,4},{24,8},{28,12},{1,17},{... | collective-permute-start | bytes 663560 | tf_op jit(solution)/shard_map/ppermute | solution.py:339
  39.9 4.6 %collective-permute-start.9 = (f32[48,512]{1,0:T(8,128)S(1)}, f32[48,512]{1,0:T(8,128)S(1)}, u32[]{:S(2)}, u32[]{:S(2)}) collective-permute-start(f32[48,512]{1,0:T(8,128)S(1)} %slice.62), channel_id=1, source_target_pairs={{0,4},{4,0},{8,12},{12,8},{16,20},{20,16},{24,28},{28,24},{1,5},{5... | collective-permute-start | bytes 294920 | tf_op jit(solution)/shard_map/ppermute | solution.py:339
  44.5 12.1 %collective-permute-start.10 = (f32[48,1024]{1,0:T(8,128)S(1)}, f32[48,1024]{1,0:T(8,128)S(1)}, u32[]{:S(2)}, u32[]{:S(2)}) collective-permute-start(f32[48,1024]{1,0:T(8,128)S(1)} %pad_maximum_fusion.1), channel_id=1, source_target_pairs={{0,16},{4,20},{8,24},{12,28},{16,0},{20,4},{24,8},{28,12},{1,17},{... | collective-permute-start | bytes 589832 | tf_op jit(solution)/shard_map/ppermute | solution.py:339
  53.5 6.3 %collective-permute-start.17 = (f32[48,512]{1,0:T(8,128)S(1)}, f32[48,512]{1,0:T(8,128)S(1)}, u32[]{:S(2)}, u32[]{:S(2)}) collective-permute-start(f32[48,512]{1,0:T(8,128)S(1)} %get-tuple-element.39), channel_id=1, source_target_pairs={{0,4},{4,0},{8,12},{12,8},{16,20},{20,16},{24,28},{28,24},{1,5},{5... | collective-permute-start | bytes 294920 | tf_op jit(solution)/shard_map/ppermute | solution.py:339
  54.0 6.4 %collective-permute-start.16 = (f32[48,512]{1,0:T(8,128)S(1)}, f32[48,512]{1,0:T(8,128)S(1)}, u32[]{:S(2)}, u32[]{:S(2)}) collective-permute-start(f32[48,512]{1,0:T(8,128)S(1)} %get-tuple-element.40), channel_id=1, source_target_pairs={{0,8},{4,12},{8,0},{12,4},{16,24},{20,28},{24,16},{28,20},{1,9},{5... | collective-permute-start | bytes 294920 | tf_op jit(solution)/shard_map/ppermute | solution.py:339
  56.7 7.9 %collective-permute-start.12 = (f32[48,512]{1,0:T(8,128)S(1)}, f32[48,512]{1,0:T(8,128)S(1)}, u32[]{:S(2)}, u32[]{:S(2)}) collective-permute-start(f32[48,512]{1,0:T(8,128)S(1)} %get-tuple-element.37), channel_id=1, source_target_pairs={{0,8},{4,12},{8,0},{12,4},{16,24},{20,28},{24,16},{28,20},{1,9},{5... | collective-permute-start | bytes 294920 | tf_op jit(solution)/shard_map/ppermute | solution.py:339
  58.2 5.3 %collective-permute-start.14 = (f32[48,512]{1,0:T(8,128)S(1)}, f32[48,512]{1,0:T(8,128)S(1)}, u32[]{:S(2)}, u32[]{:S(2)}) collective-permute-start(f32[48,512]{1,0:T(8,128)S(1)} %get-tuple-element.38), channel_id=1, source_target_pairs={{0,4},{4,0},{8,12},{12,8},{16,20},{20,16},{24,28},{28,24},{1,5},{5... | collective-permute-start | bytes 294920 | tf_op jit(solution)/shard_map/ppermute | solution.py:339
  59.8 7.3 %collective-permute-start.19 = (f32[48,1024]{1,0:T(8,128)S(1)}, f32[48,1024]{1,0:T(8,128)S(1)}, u32[]{:S(2)}, u32[]{:S(2)}) collective-permute-start(f32[48,1024]{1,0:T(8,128)S(1)} %pad_maximum_fusion.5), channel_id=1, source_target_pairs={{0,8},{4,12},{8,0},{12,4},{16,24},{20,28},{24,16},{28,20},{1,9},{5... | collective-permute-start | bytes 589832 | tf_op jit(solution)/shard_map/ppermute | solution.py:339
  60.4 7.2 %collective-permute-start.18 = (f32[48,1024]{1,0:T(8,128)S(1)}, f32[48,1024]{1,0:T(8,128)S(1)}, u32[]{:S(2)}, u32[]{:S(2)}) collective-permute-start(f32[48,1024]{1,0:T(8,128)S(1)} %pad_maximum_fusion.4), channel_id=1, source_target_pairs={{0,4},{4,0},{8,12},{12,8},{16,20},{20,16},{24,28},{28,24},{1,5},{5... | collective-permute-start | bytes 589832 | tf_op jit(solution)/shard_map/ppermute | solution.py:339
  63.5 7.4 %collective-permute-start.15 = (f32[48,1024]{1,0:T(8,128)S(1)}, f32[48,1024]{1,0:T(8,128)S(1)}, u32[]{:S(2)}, u32[]{:S(2)}) collective-permute-start(f32[48,1024]{1,0:T(8,128)S(1)} %pad_maximum_fusion.3), channel_id=1, source_target_pairs={{0,8},{4,12},{8,0},{12,4},{16,24},{20,28},{24,16},{28,20},{1,9},{5... | collective-permute-start | bytes 589832 | tf_op jit(solution)/shard_map/ppermute | solution.py:339
  64.7 6.2 %collective-permute-start.13 = (f32[48,1024]{1,0:T(8,128)S(1)}, f32[48,1024]{1,0:T(8,128)S(1)}, u32[]{:S(2)}, u32[]{:S(2)}) collective-permute-start(f32[48,1024]{1,0:T(8,128)S(1)} %pad_maximum_fusion.2), channel_id=1, source_target_pairs={{0,4},{4,0},{8,12},{12,8},{16,20},{20,16},{24,28},{28,24},{1,5},{5... | collective-permute-start | bytes 589832 | tf_op jit(solution)/shard_map/ppermute | solution.py:339

commit v24 on v16

--- a/solution.py
+++ b/solution.py
@@ -349,19 +349,22 @@
 
     both, gram, away = first_products(tall, other, probes, outputs(0, 1), width)
 
-    inverse, out, after = None, None, away[0]
+    aways = [away] + [
+        rest_products(both, gram, probes, outputs(c, 1), width, away[0]) for c in range(1, CHUNKS)
+    ]
+    ready = over(away[0], 1)
+    owns = rest_products(
+        both, gram, probes, [o for c in range(CHUNKS) for o in outputs(c, 0)], width, ready
+    )
+
+    inverse, out = None, None
     for c in range(CHUNKS):
         g = LANES if c == 0 else 0
         last = c == CHUNKS - 1
-        made = rest_products(
-            both, gram, probes, outputs(c, 0) + ([] if last else outputs(c + 1, 1)), width, after
-        )
-        away_a, away_b = away
-        (own_a, own_b), away = made[:2], made[2:]
-        got_a = over(away_a, 1)
+        (away_a, away_b), (own_a, own_b) = aways[c], owns[2 * c : 2 * c + 2]
+        got_a = ready if c == 0 else over(away_a, 1)
         sum_a = own_a + got_a
         sum_b = own_b + over(away_b, 2)
-        after = got_a
         send_a, send_b = sum_a[:, : width + g], sum_b[:, :width]
         if c > 0:
             send_a, send_b, whole = lax.optimization_barrier((send_a, send_b, whole))

time: 71.3 us -> 73 us (1.024)
  waiting for transfers between devices: 20.9 us -> 22.9 us
    ppermute x20, waiting for transfers between devices: 20.9 us -> 22.9 us  [swap(): return lax.ppermute(value, axis, [(i, i ^ bit) for i in range(size)])]
  transfers between devices with their start and end apart: 20 -> 20, of which waited for: 10 -> 9; matrix products, arithmetic and copies ran while one was open for 1% -> 1% of each run, Pallas kernels for 18% -> 18%
where the time goes in v24:
time: 73 us; the launch traced here: 72.9 us
  Pallas kernels  25 us (34%)
  starting transfers between devices  23.9 us (33%)
  waiting for transfers between devices  22.9 us (31%)
    ppermute x20, starting transfers between devices, swap(): return lax.ppermute(value, axis, [(i, i ^ bit) for i in range(size)])  23.9 us
    ppermute x20, waiting for transfers between devices, swap(): return lax.ppermute(value, axis, [(i, i ^ bit) for i in range(size)])  22.9 us
    pallas_call x3, Pallas kernels, products(): pl.pallas_call(functools.partial(kernel, plan, grams), in_specs=[TABLE, *...  11 us
    pallas_call x1, Pallas kernels, tall_partial(): pl.pallas_call(tall_kernel, in_specs=[HBM, HBM], out_specs=WHOLE, out_sha...  7.27 us
    pallas_call x3, Pallas kernels, finish(): pl.pallas_call(functools.partial(finish_kernel, [piece[1:] for piece in p...  4.72 us
    pallas_call x1, Pallas kernels, inverse_factor(): pl.pallas_call(inverse_kernel, grid=(1,), in_specs=[pl.BlockSpec((rank, L...  2.01 us
  transfers between devices with their start and end apart: 20, of which 9 were waited for; matrix products, arithmetic and copies ran while one was open for 1% of the time, Pallas kernels for 18%

profile of v24, /device:TPU:0, one launch (start us, length us, event | category | flops | bytes accessed | tf_op | source)
XLA Modules:
  0.0 72.9 jit_solution(1939972520253334696)
XLA Ops:
  0.0 7.3 %tall_partial.1 = f32[48,512]{1,0:T(8,128)S(1)} custom-call(f32[512,8192]{1,0:T(8,128)} %x_hbm.7, f32[48,8192]{1,0:T(8,128)} %bitcast.17), custom_call_target="tpu_custom_call" | custom-call | flops 1207959552 | bytes 16777216 | tf_op jit(solution)/shard_map/tall_partial/pallas_call | solution.py:85
  8.8 2.9 %collective-permute-start.1 = (f32[48,512]{1,0:T(8,128)S(1)}, f32[48,512]{1,0:T(8,128)S(1)}, u32[]{:S(2)}, u32[]{:S(2)}) collective-permute-start(f32[48,512]{1,0:T(8,128)S(1)} %add.158.one_ref), channel_id=1, source_target_pairs={{0,2},{1,3},{2,0},{3,1},{4,6},{5,7},{6,4},{7,5},{8,10},{9,11},{10,... | collective-permute-start | bytes 294920 | tf_op jit(solution)/shard_map/ppermute | solution.py:321
  11.8 3.0 %collective-permute-done.1.two_ref = f32[48,512]{1,0:T(8,128)S(1)} collective-permute-done((f32[48,512]{1,0:T(8,128)S(1)}, f32[48,512]{1,0:T(8,128)S(1)}, u32[]{:S(2)}, u32[]{:S(2)}) %collective-permute-start.1) | collective-permute-done | bytes 98336 | tf_op jit(solution)/shard_map/ppermute | solution.py:321
  14.8 3.4 %first_products.1 = (bf16[96,512]{1,0:T(8,128)(2,1)S(1)}, f32[48,128]{1,0:T(8,128)S(1)}, f32[48,1152]{1,0:T(8,128)S(1)}, f32[48,1024]{1,0:T(8,128)S(1)}) custom-call(s32[4]{0:T(128)S(1)} %pad_add_fusion.1.which_ref, f32[48,512]{1,0:T(8,128)S(1)} %add.158.one_ref, f32[48,512]{1,0:T(8,128)S(1)} %collective-permute-done.1.two_ref, f32[512,8192]{1,0:T(8,128)} %x_hbm.7), custom_call_target="tpu_custom_call" | custom-call | flops 301989888 | bytes 4194304 | tf_op jit(solution)/shard_map/first_products/pallas_call | solution.py:183
  18.2 1.8 %collective-permute-start.2 = (f32[48,1152]{1,0:T(8,128)S(1)}, f32[48,1152]{1,0:T(8,128)S(1)}, u32[]{:S(2)}, u32[]{:S(2)}) collective-permute-start(f32[48,1152]{1,0:T(8,128)S(1)} %get-tuple-element.22.after_ref), channel_id=1, source_target_pairs={{0,4},{4,0},{8,12},{12,8},{16,20},{20,16},{24,28},{28,24},{1,5},{5... | collective-permute-start | bytes 663560 | tf_op jit(solution)/shard_map/ppermute | solution.py:321
  20.0 1.6 %collective-permute-start.6 = (f32[48,1024]{1,0:T(8,128)S(1)}, f32[48,1024]{1,0:T(8,128)S(1)}, u32[]{:S(2)}, u32[]{:S(2)}) collective-permute-start(f32[48,1024]{1,0:T(8,128)S(1)} %get-tuple-element.29), channel_id=1, source_target_pairs={{0,8},{4,12},{8,0},{12,4},{16,24},{20,28},{24,16},{28,20},{1,9},{5... | collective-permute-start | bytes 589832 | tf_op jit(solution)/shard_map/ppermute | solution.py:321
  21.6 3.1 %rest_products.3 = (f32[48,1024]{1,0:T(8,128)S(1)}, f32[48,1024]{1,0:T(8,128)S(1)}) custom-call(s32[4]{0:T(128)S(1)} %pad_add_fusion.2.which_ref, bf16[96,512]{1,0:T(8,128)(2,1)S(1)} %get-tuple-element.20.both_ref, f32[48,128]{1,0:T(8,128)S(1)} %get-tuple-element.21.gram_ref, f32[512,8192]{1,0:T(8,128)} %x_hbm.7, f32[48,1152]{1,0:T(8,128)S(1)} %get-tuple-element.22.after_ref), custom_call_target="tpu_custom_call" | custom-call | flops 301989888 | bytes 4194304 | tf_op jit(solution)/shard_map/rest_products/pallas_call | solution.py:183
  25.6 4.6 %rest_products.2 = (f32[48,1152]{1,0:T(8,128)S(1)}, f32[48,1024]{1,0:T(8,128)S(1)}, f32[48,1024]{1,0:T(8,128)S(1)}, f32[48,1024]{1,0:T(8,128)S(1)}) custom-call(s32[8]{0:T(128)S(1)} %stack.95.which_ref, bf16[96,512]{1,0:T(8,128)(2,1)S(1)} %get-tuple-element.20.both_ref, f32[48,128]{1,0:T(8,128)S(1)} %get-tuple-element.21.gram_ref, f32[512,8192]{1,0:T(8,128)} %x_hbm.7, ...), custom_call_target="tpu_custom_call" | custom-call | flops 603979776 | bytes 8388608 | tf_op jit(solution)/shard_map/rest_products/pallas_call | solution.py:183
  30.3 1.8 %collective-permute-start.7 = (f32[48,512]{1,0:T(8,128)S(1)}, f32[48,512]{1,0:T(8,128)S(1)}, u32[]{:S(2)}, u32[]{:S(2)}) collective-permute-start(f32[48,512]{1,0:T(8,128)S(1)} %slice.69), channel_id=1, source_target_pairs={{0,4},{4,0},{8,12},{12,8},{16,20},{20,16},{24,28},{28,24},{1,5},{5... | collective-permute-start | bytes 294920 | tf_op jit(solution)/shard_map/ppermute | solution.py:321
  32.1 1.6 %collective-permute-start.5 = (f32[48,640]{1,0:T(8,128)S(1)}, f32[48,640]{1,0:T(8,128)S(1)}, u32[]{:S(2)}, u32[]{:S(2)}) collective-permute-start(f32[48,640]{1,0:T(8,128)S(1)} %slice.64), channel_id=1, source_target_pairs={{0,8},{4,12},{8,0},{12,4},{16,24},{20,28},{24,16},{28,20},{1,9},{5... | collective-permute-start | bytes 368648 | tf_op jit(solution)/shard_map/ppermute | solution.py:321
  35.0 2.3 %collective-permute-done.5 = f32[48,640]{1,0:T(8,128)S(1)} collective-permute-done((f32[48,640]{1,0:T(8,128)S(1)}, f32[48,640]{1,0:T(8,128)S(1)}, u32[]{:S(2)}, u32[]{:S(2)}) %collective-permute-start.5) | collective-permute-done | bytes 122912 | tf_op jit(solution)/shard_map/ppermute | solution.py:321
  37.3 2.0 %collective-permute-start.8 = (f32[48,512]{1,0:T(8,128)S(1)}, f32[48,512]{1,0:T(8,128)S(1)}, u32[]{:S(2)}, u32[]{:S(2)}) collective-permute-start(f32[48,512]{1,0:T(8,128)S(1)} %slice.61), channel_id=1, source_target_pairs={{0,8},{4,12},{8,0},{12,4},{16,24},{20,28},{24,16},{28,20},{1,9},{5... | collective-permute-start | bytes 294920 | tf_op jit(solution)/shard_map/ppermute | solution.py:321
  39.4 2.6 %collective-permute-start.11 = (f32[48,1152]{1,0:T(8,128)S(1)}, f32[48,1152]{1,0:T(8,128)S(1)}, u32[]{:S(2)}, u32[]{:S(2)}) collective-permute-start(f32[48,1152]{1,0:T(8,128)S(1)} %pad_maximum_fusion), channel_id=1, source_target_pairs={{0,16},{4,20},{8,24},{12,28},{16,0},{20,4},{24,8},{28,12},{1,17},{... | collective-permute-start | bytes 663560 | tf_op jit(solution)/shard_map/ppermute | solution.py:321
  42.5 4.6 %collective-permute-done.9 = f32[48,512]{1,0:T(8,128)S(1)} collective-permute-done((f32[48,512]{1,0:T(8,128)S(1)}, f32[48,512]{1,0:T(8,128)S(1)}, u32[]{:S(2)}, u32[]{:S(2)}) %collective-permute-start.9) | collective-permute-done | bytes 98336 | tf_op jit(solution)/shard_map/ppermute | solution.py:321
  47.2 7.3 %collective-permute-done.11 = f32[48,1152]{1,0:T(8,128)S(1)} collective-permute-done((f32[48,1152]{1,0:T(8,128)S(1)}, f32[48,1152]{1,0:T(8,128)S(1)}, u32[]{:S(2)}, u32[]{:S(2)}) %collective-permute-start.11) | collective-permute-done | bytes 221216 | tf_op jit(solution)/shard_map/ppermute | solution.py:321
  55.1 2.0 %inverse_factor.1.inverse_ref = f32[48,48]{1,0:T(8,128)S(1)} custom-call(f32[48,1152]{1,0:T(8,128)S(1)} %fusion.1.gram_ref.refs_0_), custom_call_target="tpu_custom_call" | custom-call | flops 20000000 | bytes 49152 | tf_op jit(solution)/shard_map/inverse_factor/pallas_call | solution.py:258
  57.2 2.1 %collective-permute-start.12 = (f32[48,512]{1,0:T(8,128)S(1)}, f32[48,512]{1,0:T(8,128)S(1)}, u32[]{:S(2)}, u32[]{:S(2)}) collective-permute-start(f32[48,512]{1,0:T(8,128)S(1)} %get-tuple-element.33), channel_id=1, source_target_pairs={{0,8},{4,12},{8,0},{12,4},{16,24},{20,28},{24,16},{28,20},{1,9},{5... | collective-permute-start | bytes 294920 | tf_op jit(solution)/shard_map/ppermute | solution.py:321
  59.3 1.5 %collective-permute-start.14 = (f32[48,512]{1,0:T(8,128)S(1)}, f32[48,512]{1,0:T(8,128)S(1)}, u32[]{:S(2)}, u32[]{:S(2)}) collective-permute-start(f32[48,512]{1,0:T(8,128)S(1)} %get-tuple-element.34), channel_id=1, source_target_pairs={{0,4},{4,0},{8,12},{12,8},{16,20},{20,16},{24,28},{28,24},{1,5},{5... | collective-permute-start | bytes 294920 | tf_op jit(solution)/shard_map/ppermute | solution.py:321
  61.0 1.4 %collective-permute-start.18 = (f32[48,1024]{1,0:T(8,128)S(1)}, f32[48,1024]{1,0:T(8,128)S(1)}, u32[]{:S(2)}, u32[]{:S(2)}) collective-permute-start(f32[48,1024]{1,0:T(8,128)S(1)} %pad_maximum_fusion.4), channel_id=1, source_target_pairs={{0,4},{4,0},{8,12},{12,8},{16,20},{20,16},{24,28},{28,24},{1,5},{5... | collective-permute-start | bytes 589832 | tf_op jit(solution)/shard_map/ppermute | solution.py:321
  62.4 2.2 %collective-permute-done.14.refs_2_ = f32[48,512]{1,0:T(8,128)S(1)} collective-permute-done((f32[48,512]{1,0:T(8,128)S(1)}, f32[48,512]{1,0:T(8,128)S(1)}, u32[]{:S(2)}, u32[]{:S(2)}) %collective-permute-start.14) | collective-permute-done | bytes 98336 | tf_op jit(solution)/shard_map/ppermute | solution.py:321
  64.7 1.9 %collective-permute-start.13 = (f32[48,1024]{1,0:T(8,128)S(1)}, f32[48,1024]{1,0:T(8,128)S(1)}, u32[]{:S(2)}, u32[]{:S(2)}) collective-permute-start(f32[48,1024]{1,0:T(8,128)S(1)} %pad_maximum_fusion.2), channel_id=1, source_target_pairs={{0,4},{4,0},{8,12},{12,8},{16,20},{20,16},{24,28},{28,24},{1,5},{5... | collective-permute-start | bytes 589832 | tf_op jit(solution)/shard_map/ppermute | solution.py:321
  68.1 1.7 %finish.3.refs_3_ = f32[48,8192]{1,0:T(8,128)} custom-call(s32[8]{0:T(128)S(1)} %stack.103.where_ref, f32[48,48]{1,0:T(8,128)S(1)} %inverse_factor.1.inverse_ref, f32[48,1152]{1,0:T(8,128)S(1)} %fusion.1.gram_ref.refs_0_, f32[48,512]{1,0:T(8,128)S(1)} %collective-permute-done.16.refs_1_, f32[48,512]{1,0:T(8,128)S(1)} %collective-permute-done.17.refs_2_, ...), custom_call_target="tpu_custom_call" | custom-call | flops 56623104 | bytes 1572864 | tf_op jit(solution)/shard_map/finish/pallas_call | solution.py:299
  69.8 1.5 %finish.4.refs_2_ = f32[48,8192]{1,0:T(8,128)} custom-call(s32[4]{0:T(128)S(1)} %pad_add_fusion.3.where_ref, f32[48,48]{1,0:T(8,128)S(1)} %inverse_factor.1.inverse_ref, f32[48,1024]{1,0:T(8,128)S(1)} %fusion.refs_0_, f32[48,512]{1,0:T(8,128)S(1)} %collective-permute-done.12.refs_1_, ...), custom_call_target="tpu_custom_call", output_to_operand_aliasing={{}: (5, {})} | custom-call | flops 28311552 | bytes 786432 | tf_op jit(solution)/shard_map/finish/pallas_call | solution.py:299
  71.4 1.5 %finish.5 = f32[48,8192]{1,0:T(8,128)} custom-call(s32[4]{0:T(128)S(1)} %pad_add_fusion.where_ref, f32[48,48]{1,0:T(8,128)S(1)} %inverse_factor.1.inverse_ref, f32[48,1024]{1,0:T(8,128)S(1)} %collective-permute-done.13.refs_0_, f32[48,1024]{1,0:T(8,128)S(1)} %collective-permute-done.15.refs_1_, f32[48,8192]{1,0:T(8,128)} %finish.4.refs_2_), custom_call_target="tpu_custom_call", output_to_operand_aliasing={{}: (4, {})} | custom-call | flops 28311552 | bytes 786432 | tf_op jit(solution)/shard_map/finish/pallas_call | solution.py:299
  (54 shorter events, 7.1 us)
Async XLA Ops:
  7.3 1.5 %collective-permute-start = (f32[48,512]{1,0:T(8,128)S(1)}, f32[48,512]{1,0:T(8,128)S(1)}, u32[]{:S(2)}, u32[]{:S(2)}) collective-permute-start(f32[48,512]{1,0:T(8,128)S(1)} %tall_partial.1), channel_id=1, source_target_pairs={{0,1},{1,0},{2,3},{3,2},{4,5},{5,4},{6,7},{7,6},{8,9},{9,8},{10,11... | collective-permute-start | bytes 294920 | tf_op jit(solution)/shard_map/ppermute | solution.py:321
  8.8 6.0 %collective-permute-start.1 = (f32[48,512]{1,0:T(8,128)S(1)}, f32[48,512]{1,0:T(8,128)S(1)}, u32[]{:S(2)}, u32[]{:S(2)}) collective-permute-start(f32[48,512]{1,0:T(8,128)S(1)} %add.158.one_ref), channel_id=1, source_target_pairs={{0,2},{1,3},{2,0},{3,1},{4,6},{5,7},{6,4},{7,5},{8,10},{9,11},{10,... | collective-permute-start | bytes 294920 | tf_op jit(solution)/shard_map/ppermute | solution.py:321
  18.2 7.4 %collective-permute-start.2 = (f32[48,1152]{1,0:T(8,128)S(1)}, f32[48,1152]{1,0:T(8,128)S(1)}, u32[]{:S(2)}, u32[]{:S(2)}) collective-permute-start(f32[48,1152]{1,0:T(8,128)S(1)} %get-tuple-element.22.after_ref), channel_id=1, source_target_pairs={{0,4},{4,0},{8,12},{12,8},{16,20},{20,16},{24,28},{28,24},{1,5},{5... | collective-permute-start | bytes 663560 | tf_op jit(solution)/shard_map/ppermute | solution.py:321
  20.0 10.2 %collective-permute-start.6 = (f32[48,1024]{1,0:T(8,128)S(1)}, f32[48,1024]{1,0:T(8,128)S(1)}, u32[]{:S(2)}, u32[]{:S(2)}) collective-permute-start(f32[48,1024]{1,0:T(8,128)S(1)} %get-tuple-element.29), channel_id=1, source_target_pairs={{0,8},{4,12},{8,0},{12,4},{16,24},{20,28},{24,16},{28,20},{1,9},{5... | collective-permute-start | bytes 589832 | tf_op jit(solution)/shard_map/ppermute | solution.py:321
  24.7 9.0 %collective-permute-start.4 = (f32[48,1024]{1,0:T(8,128)S(1)}, f32[48,1024]{1,0:T(8,128)S(1)}, u32[]{:S(2)}, u32[]{:S(2)}) collective-permute-start(f32[48,1024]{1,0:T(8,128)S(1)} %get-tuple-element.26), channel_id=1, source_target_pairs={{0,8},{4,12},{8,0},{12,4},{16,24},{20,28},{24,16},{28,20},{1,9},{5... | collective-permute-start | bytes 589832 | tf_op jit(solution)/shard_map/ppermute | solution.py:321
  25.2 8.6 %collective-permute-start.3 = (f32[48,1024]{1,0:T(8,128)S(1)}, f32[48,1024]{1,0:T(8,128)S(1)}, u32[]{:S(2)}, u32[]{:S(2)}) collective-permute-start(f32[48,1024]{1,0:T(8,128)S(1)} %get-tuple-element.24), channel_id=1, source_target_pairs={{0,4},{4,0},{8,12},{12,8},{16,20},{20,16},{24,28},{28,24},{1,5},{5... | collective-permute-start | bytes 589832 | tf_op jit(solution)/shard_map/ppermute | solution.py:321
  30.3 4.7 %collective-permute-start.7 = (f32[48,512]{1,0:T(8,128)S(1)}, f32[48,512]{1,0:T(8,128)S(1)}, u32[]{:S(2)}, u32[]{:S(2)}) collective-permute-start(f32[48,512]{1,0:T(8,128)S(1)} %slice.69), channel_id=1, source_target_pairs={{0,4},{4,0},{8,12},{12,8},{16,20},{20,16},{24,28},{28,24},{1,5},{5... | collective-permute-start | bytes 294920 | tf_op jit(solution)/shard_map/ppermute | solution.py:321
  32.1 5.1 %collective-permute-start.5 = (f32[48,640]{1,0:T(8,128)S(1)}, f32[48,640]{1,0:T(8,128)S(1)}, u32[]{:S(2)}, u32[]{:S(2)}) collective-permute-start(f32[48,640]{1,0:T(8,128)S(1)} %slice.64), channel_id=1, source_target_pairs={{0,8},{4,12},{8,0},{12,4},{16,24},{20,28},{24,16},{28,20},{1,9},{5... | collective-permute-start | bytes 368648 | tf_op jit(solution)/shard_map/ppermute | solution.py:321
  37.3 5.2 %collective-permute-start.8 = (f32[48,512]{1,0:T(8,128)S(1)}, f32[48,512]{1,0:T(8,128)S(1)}, u32[]{:S(2)}, u32[]{:S(2)}) collective-permute-start(f32[48,512]{1,0:T(8,128)S(1)} %slice.61), channel_id=1, source_target_pairs={{0,8},{4,12},{8,0},{12,4},{16,24},{20,28},{24,16},{28,20},{1,9},{5... | collective-permute-start | bytes 294920 | tf_op jit(solution)/shard_map/ppermute | solution.py:321
  39.4 15.1 %collective-permute-start.11 = (f32[48,1152]{1,0:T(8,128)S(1)}, f32[48,1152]{1,0:T(8,128)S(1)}, u32[]{:S(2)}, u32[]{:S(2)}) collective-permute-start(f32[48,1152]{1,0:T(8,128)S(1)} %pad_maximum_fusion), channel_id=1, source_target_pairs={{0,16},{4,20},{8,24},{12,28},{16,0},{20,4},{24,8},{28,12},{1,17},{... | collective-permute-start | bytes 663560 | tf_op jit(solution)/shard_map/ppermute | solution.py:321
  41.9 5.1 %collective-permute-start.9 = (f32[48,512]{1,0:T(8,128)S(1)}, f32[48,512]{1,0:T(8,128)S(1)}, u32[]{:S(2)}, u32[]{:S(2)}) collective-permute-start(f32[48,512]{1,0:T(8,128)S(1)} %slice.62), channel_id=1, source_target_pairs={{0,4},{4,0},{8,12},{12,8},{16,20},{20,16},{24,28},{28,24},{1,5},{5... | collective-permute-start | bytes 294920 | tf_op jit(solution)/shard_map/ppermute | solution.py:321
  47.1 10.1 %collective-permute-start.10 = (f32[48,1024]{1,0:T(8,128)S(1)}, f32[48,1024]{1,0:T(8,128)S(1)}, u32[]{:S(2)}, u32[]{:S(2)}) collective-permute-start(f32[48,1024]{1,0:T(8,128)S(1)} %pad_maximum_fusion.1), channel_id=1, source_target_pairs={{0,16},{4,20},{8,24},{12,28},{16,0},{20,4},{24,8},{28,12},{1,17},{... | collective-permute-start | bytes 589832 | tf_op jit(solution)/shard_map/ppermute | solution.py:321
  54.6 6.3 %collective-permute-start.17 = (f32[48,512]{1,0:T(8,128)S(1)}, f32[48,512]{1,0:T(8,128)S(1)}, u32[]{:S(2)}, u32[]{:S(2)}) collective-permute-start(f32[48,512]{1,0:T(8,128)S(1)} %get-tuple-element.35), channel_id=1, source_target_pairs={{0,4},{4,0},{8,12},{12,8},{16,20},{20,16},{24,28},{28,24},{1,5},{5... | collective-permute-start | bytes 294920 | tf_op jit(solution)/shard_map/ppermute | solution.py:321
  55.1 5.8 %collective-permute-start.16 = (f32[48,512]{1,0:T(8,128)S(1)}, f32[48,512]{1,0:T(8,128)S(1)}, u32[]{:S(2)}, u32[]{:S(2)}) collective-permute-start(f32[48,512]{1,0:T(8,128)S(1)} %get-tuple-element.36), channel_id=1, source_target_pairs={{0,8},{4,12},{8,0},{12,4},{16,24},{20,28},{24,16},{28,20},{1,9},{5... | collective-permute-start | bytes 294920 | tf_op jit(solution)/shard_map/ppermute | solution.py:321
  57.2 7.5 %collective-permute-start.12 = (f32[48,512]{1,0:T(8,128)S(1)}, f32[48,512]{1,0:T(8,128)S(1)}, u32[]{:S(2)}, u32[]{:S(2)}) collective-permute-start(f32[48,512]{1,0:T(8,128)S(1)} %get-tuple-element.33), channel_id=1, source_target_pairs={{0,8},{4,12},{8,0},{12,4},{16,24},{20,28},{24,16},{28,20},{1,9},{5... | collective-permute-start | bytes 294920 | tf_op jit(solution)/shard_map/ppermute | solution.py:321
  59.3 5.3 %collective-permute-start.14 = (f32[48,512]{1,0:T(8,128)S(1)}, f32[48,512]{1,0:T(8,128)S(1)}, u32[]{:S(2)}, u32[]{:S(2)}) collective-permute-start(f32[48,512]{1,0:T(8,128)S(1)} %get-tuple-element.34), channel_id=1, source_target_pairs={{0,4},{4,0},{8,12},{12,8},{16,20},{20,16},{24,28},{28,24},{1,5},{5... | collective-permute-start | bytes 294920 | tf_op jit(solution)/shard_map/ppermute | solution.py:321
  60.8 6.7 %collective-permute-start.19 = (f32[48,1024]{1,0:T(8,128)S(1)}, f32[48,1024]{1,0:T(8,128)S(1)}, u32[]{:S(2)}, u32[]{:S(2)}) collective-permute-start(f32[48,1024]{1,0:T(8,128)S(1)} %pad_maximum_fusion.5), channel_id=1, source_target_pairs={{0,8},{4,12},{8,0},{12,4},{16,24},{20,28},{24,16},{28,20},{1,9},{5... | collective-permute-start | bytes 589832 | tf_op jit(solution)/shard_map/ppermute | solution.py:321
  61.0 7.1 %collective-permute-start.18 = (f32[48,1024]{1,0:T(8,128)S(1)}, f32[48,1024]{1,0:T(8,128)S(1)}, u32[]{:S(2)}, u32[]{:S(2)}) collective-permute-start(f32[48,1024]{1,0:T(8,128)S(1)} %pad_maximum_fusion.4), channel_id=1, source_target_pairs={{0,4},{4,0},{8,12},{12,8},{16,20},{20,16},{24,28},{28,24},{1,5},{5... | collective-permute-start | bytes 589832 | tf_op jit(solution)/shard_map/ppermute | solution.py:321
  64.6 6.8 %collective-permute-start.15 = (f32[48,1024]{1,0:T(8,128)S(1)}, f32[48,1024]{1,0:T(8,128)S(1)}, u32[]{:S(2)}, u32[]{:S(2)}) collective-permute-start(f32[48,1024]{1,0:T(8,128)S(1)} %pad_maximum_fusion.3), channel_id=1, source_target_pairs={{0,8},{4,12},{8,0},{12,4},{16,24},{20,28},{24,16},{28,20},{1,9},{5... | collective-permute-start | bytes 589832 | tf_op jit(solution)/shard_map/ppermute | solution.py:321
  64.7 6.6 %collective-permute-start.13 = (f32[48,1024]{1,0:T(8,128)S(1)}, f32[48,1024]{1,0:T(8,128)S(1)}, u32[]{:S(2)}, u32[]{:S(2)}) collective-permute-start(f32[48,1024]{1,0:T(8,128)S(1)} %pad_maximum_fusion.2), channel_id=1, source_target_pairs={{0,4},{4,0},{8,12},{12,8},{16,20},{20,16},{24,28},{28,24},{1,5},{5... | collective-permute-start | bytes 589832 | tf_op jit(solution)/shard_map/ppermute | solution.py:321

commit v25 on v12

--- a/solution.py
+++ b/solution.py
@@ -368,11 +368,10 @@
         )
         away_a, away_b = away
         (own_a, own_b), away = made[:2], made[2:]
-        if c > 0:
-            away_a, away_b, sum_a, sum_b = lax.optimization_barrier((away_a, away_b, sum_a, sum_b))
         got_a = over(away_a, 1)
         sum_a = own_a + got_a
         sum_b = own_b + over(away_b, 2)
+        after = got_a
         send_a, send_b = sum_a[:, : width + g], sum_b[:, :width]
         if c > 0:
             send_a, send_b, whole = lax.optimization_barrier((send_a, send_b, whole))
@@ -386,7 +385,7 @@
             ],
             axis=1,
         )
-        after = total = whole
+        total = whole
         bit = 4
         while bit < n_pos:
             total = total + over(total, bit)

time: 75.8 us -> 70.2 us (0.926)
  waiting for transfers between devices: 26.4 us -> 21.8 us
  starting transfers between devices: 24.9 us -> 23.8 us
    ppermute x20, waiting for transfers between devices: 26.4 us -> 21.8 us  [swap(): return lax.ppermute(value, axis, [(i, i ^ bit) for i in range(size)])]
    ppermute x20, starting transfers between devices: 24.9 us -> 23.8 us  [swap(): return lax.ppermute(value, axis, [(i, i ^ bit) for i in range(size)])]
  transfers between devices with their start and end apart: 20 -> 20, of which waited for: 10 -> 12; matrix products, arithmetic and copies ran while one was open for 1% -> 1% of each run, Pallas kernels for 15% -> 16%
where the time goes in v25:
time: 70.2 us; the launch traced here: 70 us
  starting transfers between devices  23.8 us (34%)
  Pallas kernels  23.4 us (33%)
  waiting for transfers between devices  21.8 us (31%)
    ppermute x20, starting transfers between devices, swap(): return lax.ppermute(value, axis, [(i, i ^ bit) for i in range(size)])  23.8 us
    ppermute x20, waiting for transfers between devices, swap(): return lax.ppermute(value, axis, [(i, i ^ bit) for i in range(size)])  21.8 us
    pallas_call x3, Pallas kernels, products(): pl.pallas_call(functools.partial(kernel, plan, grams), in_specs=[TABLE, *...  10.7 us
    pallas_call x1, Pallas kernels, tall_partial(): pl.pallas_call(tall_kernel, in_specs=[HBM, HBM], out_specs=WHOLE, out_sha...  7.27 us
    pallas_call x2, Pallas kernels, finish(): pl.pallas_call(functools.partial(finish_kernel, [piece[1:] for piece in p...  3.4 us
    pallas_call x1, Pallas kernels, inverse_factor(): pl.pallas_call(inverse_kernel, grid=(1,), in_specs=[pl.BlockSpec((rank, L...  2.01 us
  transfers between devices with their start and end apart: 20, of which 12 were waited for; matrix products, arithmetic and copies ran while one was open for 1% of the time, Pallas kernels for 16%

profile of v25, /device:TPU:0, one launch (start us, length us, event | category | flops | bytes accessed | tf_op | source)
XLA Modules:
  0.0 70.0 jit_solution(14343815819387740397)
XLA Ops:
  0.0 7.3 %tall_partial.1 = f32[48,512]{1,0:T(8,128)S(1)} custom-call(f32[512,8192]{1,0:T(8,128)} %x_hbm.7, f32[48,8192]{1,0:T(8,128)} %bitcast.17), custom_call_target="tpu_custom_call" | custom-call | flops 1207959552 | bytes 16777216 | tf_op jit(solution)/shard_map/tall_partial/pallas_call | solution.py:91
  7.8 0.9 %collective-permute-done = f32[48,512]{1,0:T(8,128)S(1)} collective-permute-done((f32[48,512]{1,0:T(8,128)S(1)}, f32[48,512]{1,0:T(8,128)S(1)}, u32[]{:S(2)}, u32[]{:S(2)}) %collective-permute-start) | collective-permute-done | bytes 98336 | tf_op jit(solution)/shard_map/ppermute | solution.py:330
  8.8 2.9 %collective-permute-start.1 = (f32[48,512]{1,0:T(8,128)S(1)}, f32[48,512]{1,0:T(8,128)S(1)}, u32[]{:S(2)}, u32[]{:S(2)}) collective-permute-start(f32[48,512]{1,0:T(8,128)S(1)} %add.153.one_ref), channel_id=1, source_target_pairs={{0,2},{1,3},{2,0},{3,1},{4,6},{5,7},{6,4},{7,5},{8,10},{9,11},{10,... | collective-permute-start | bytes 294920 | tf_op jit(solution)/shard_map/ppermute | solution.py:330
  11.8 3.0 %collective-permute-done.1.two_ref = f32[48,512]{1,0:T(8,128)S(1)} collective-permute-done((f32[48,512]{1,0:T(8,128)S(1)}, f32[48,512]{1,0:T(8,128)S(1)}, u32[]{:S(2)}, u32[]{:S(2)}) %collective-permute-start.1) | collective-permute-done | bytes 98336 | tf_op jit(solution)/shard_map/ppermute | solution.py:330
  14.8 3.3 %first_products.1 = (bf16[96,512]{1,0:T(8,128)(2,1)S(1)}, f32[48,128]{1,0:T(8,128)S(1)}, f32[48,1152]{1,0:T(8,128)S(1)}, f32[48,1024]{1,0:T(8,128)S(1)}) custom-call(s32[4]{0:T(128)S(1)} %pad_add_fusion.2.which_ref, f32[48,512]{1,0:T(8,128)S(1)} %add.153.one_ref, f32[48,512]{1,0:T(8,128)S(1)} %collective-permute-done.1.two_ref, f32[512,8192]{1,0:T(8,128)} %x_hbm.7), custom_call_target="tpu_custom_call" | custom-call | flops 301989888 | bytes 4194304 | tf_op jit(solution)/shard_map/first_products/pallas_call | solution.py:192
  18.2 1.9 %collective-permute-start.6 = (f32[48,1024]{1,0:T(8,128)S(1)}, f32[48,1024]{1,0:T(8,128)S(1)}, u32[]{:S(2)}, u32[]{:S(2)}) collective-permute-start(f32[48,1024]{1,0:T(8,128)S(1)} %get-tuple-element.29), channel_id=1, source_target_pairs={{0,8},{4,12},{8,0},{12,4},{16,24},{20,28},{24,16},{28,20},{1,9},{5... | collective-permute-start | bytes 589832 | tf_op jit(solution)/shard_map/ppermute | solution.py:330
  20.1 1.5 %collective-permute-start.2 = (f32[48,1152]{1,0:T(8,128)S(1)}, f32[48,1152]{1,0:T(8,128)S(1)}, u32[]{:S(2)}, u32[]{:S(2)}) collective-permute-start(f32[48,1152]{1,0:T(8,128)S(1)} %get-tuple-element.22.after_ref), channel_id=1, source_target_pairs={{0,4},{4,0},{8,12},{12,8},{16,20},{20,16},{24,28},{28,24},{1,5},{5... | collective-permute-start | bytes 663560 | tf_op jit(solution)/shard_map/ppermute | solution.py:330
  21.6 4.3 %rest_products.3 = (f32[48,1152]{1,0:T(8,128)S(1)}, f32[48,1024]{1,0:T(8,128)S(1)}, f32[48,1024]{1,0:T(8,128)S(1)}, f32[48,1024]{1,0:T(8,128)S(1)}) custom-call(s32[8]{0:T(128)S(1)} %stack.98.which_ref, bf16[96,512]{1,0:T(8,128)(2,1)S(1)} %get-tuple-element.20.both_ref, f32[48,128]{1,0:T(8,128)S(1)} %get-tuple-element.21.gram_ref, f32[512,8192]{1,0:T(8,128)} %x_hbm.7, ...), custom_call_target="tpu_custom_call" | custom-call | flops 603979776 | bytes 8388608 | tf_op jit(solution)/shard_map/rest_products/pallas_call | solution.py:192
  26.8 1.8 %collective-permute-start.7 = (f32[48,512]{1,0:T(8,128)S(1)}, f32[48,512]{1,0:T(8,128)S(1)}, u32[]{:S(2)}, u32[]{:S(2)}) collective-permute-start(f32[48,512]{1,0:T(8,128)S(1)} %slice.69), channel_id=1, source_target_pairs={{0,4},{4,0},{8,12},{12,8},{16,20},{20,16},{24,28},{28,24},{1,5},{5... | collective-permute-start | bytes 294920 | tf_op jit(solution)/shard_map/ppermute | solution.py:330
  28.8 1.6 %collective-permute-start.5 = (f32[48,640]{1,0:T(8,128)S(1)}, f32[48,640]{1,0:T(8,128)S(1)}, u32[]{:S(2)}, u32[]{:S(2)}) collective-permute-start(f32[48,640]{1,0:T(8,128)S(1)} %slice.64), channel_id=1, source_target_pairs={{0,8},{4,12},{8,0},{12,4},{16,24},{20,28},{24,16},{28,20},{1,9},{5... | collective-permute-start | bytes 368648 | tf_op jit(solution)/shard_map/ppermute | solution.py:330
  30.4 3.1 %rest_products.2 = (f32[48,1024]{1,0:T(8,128)S(1)}, f32[48,1024]{1,0:T(8,128)S(1)}) custom-call(s32[4]{0:T(128)S(1)} %pad_add_fusion.1.which_ref, bf16[96,512]{1,0:T(8,128)(2,1)S(1)} %get-tuple-element.20.both_ref, f32[48,128]{1,0:T(8,128)S(1)} %get-tuple-element.21.gram_ref, f32[512,8192]{1,0:T(8,128)} %x_hbm.7, f32[48,1152]{1,0:T(8,128)S(1)} %collective-permute-done.2.after_ref), custom_call_target="tpu_custom_call" | custom-call | flops 301989888 | bytes 4194304 | tf_op jit(solution)/shard_map/rest_products/pallas_call | solution.py:192
  35.4 2.6 %collective-permute-start.11 = (f32[48,1152]{1,0:T(8,128)S(1)}, f32[48,1152]{1,0:T(8,128)S(1)}, u32[]{:S(2)}, u32[]{:S(2)}) collective-permute-start(f32[48,1152]{1,0:T(8,128)S(1)} %pad_maximum_fusion), channel_id=1, source_target_pairs={{0,16},{4,20},{8,24},{12,28},{16,0},{20,4},{24,8},{28,12},{1,17},{... | collective-permute-start | bytes 663560 | tf_op jit(solution)/shard_map/ppermute | solution.py:330
  38.0 1.1 %collective-permute-start.9 = (f32[48,512]{1,0:T(8,128)S(1)}, f32[48,512]{1,0:T(8,128)S(1)}, u32[]{:S(2)}, u32[]{:S(2)}) collective-permute-start(f32[48,512]{1,0:T(8,128)S(1)} %slice.62), channel_id=1, source_target_pairs={{0,4},{4,0},{8,12},{12,8},{16,20},{20,16},{24,28},{28,24},{1,5},{5... | collective-permute-start | bytes 294920 | tf_op jit(solution)/shard_map/ppermute | solution.py:330
  39.2 3.4 %collective-permute-done.9 = f32[48,512]{1,0:T(8,128)S(1)} collective-permute-done((f32[48,512]{1,0:T(8,128)S(1)}, f32[48,512]{1,0:T(8,128)S(1)}, u32[]{:S(2)}, u32[]{:S(2)}) %collective-permute-start.9) | collective-permute-done | bytes 98336 | tf_op jit(solution)/shard_map/ppermute | solution.py:330
  43.0 8.7 %collective-permute-done.11 = f32[48,1152]{1,0:T(8,128)S(1)} collective-permute-done((f32[48,1152]{1,0:T(8,128)S(1)}, f32[48,1152]{1,0:T(8,128)S(1)}, u32[]{:S(2)}, u32[]{:S(2)}) %collective-permute-start.11) | collective-permute-done | bytes 221216 | tf_op jit(solution)/shard_map/ppermute | solution.py:330
  53.2 2.0 %inverse_factor.1.inverse_ref = f32[48,48]{1,0:T(8,128)S(1)} custom-call(f32[48,1152]{1,0:T(8,128)S(1)} %fusion.1.gram_ref.refs_0_), custom_call_target="tpu_custom_call" | custom-call | flops 20000000 | bytes 49152 | tf_op jit(solution)/shard_map/inverse_factor/pallas_call | solution.py:267
  55.2 1.5 %collective-permute-start.12 = (f32[48,512]{1,0:T(8,128)S(1)}, f32[48,512]{1,0:T(8,128)S(1)}, u32[]{:S(2)}, u32[]{:S(2)}) collective-permute-start(f32[48,512]{1,0:T(8,128)S(1)} %get-tuple-element.33), channel_id=1, source_target_pairs={{0,8},{4,12},{8,0},{12,4},{16,24},{20,28},{24,16},{28,20},{1,9},{5... | collective-permute-start | bytes 294920 | tf_op jit(solution)/shard_map/ppermute | solution.py:330
  56.8 1.3 %collective-permute-start.14 = (f32[48,512]{1,0:T(8,128)S(1)}, f32[48,512]{1,0:T(8,128)S(1)}, u32[]{:S(2)}, u32[]{:S(2)}) collective-permute-start(f32[48,512]{1,0:T(8,128)S(1)} %get-tuple-element.34), channel_id=1, source_target_pairs={{0,4},{4,0},{8,12},{12,8},{16,20},{20,16},{24,28},{28,24},{1,5},{5... | collective-permute-start | bytes 294920 | tf_op jit(solution)/shard_map/ppermute | solution.py:330
  59.6 2.3 %collective-permute-done.14.refs_7_ = f32[48,512]{1,0:T(8,128)S(1)} collective-permute-done((f32[48,512]{1,0:T(8,128)S(1)}, f32[48,512]{1,0:T(8,128)S(1)}, u32[]{:S(2)}, u32[]{:S(2)}) %collective-permute-start.14) | collective-permute-done | bytes 98336 | tf_op jit(solution)/shard_map/ppermute | solution.py:330
  61.9 0.9 %collective-permute-start.15 = (f32[48,1024]{1,0:T(8,128)S(1)}, f32[48,1024]{1,0:T(8,128)S(1)}, u32[]{:S(2)}, u32[]{:S(2)}) collective-permute-start(f32[48,1024]{1,0:T(8,128)S(1)} %pad_maximum_fusion.3), channel_id=1, source_target_pairs={{0,8},{4,12},{8,0},{12,4},{16,24},{20,28},{24,16},{28,20},{1,9},{5... | collective-permute-start | bytes 589832 | tf_op jit(solution)/shard_map/ppermute | solution.py:330
  62.8 1.3 %collective-permute-start.13 = (f32[48,1024]{1,0:T(8,128)S(1)}, f32[48,1024]{1,0:T(8,128)S(1)}, u32[]{:S(2)}, u32[]{:S(2)}) collective-permute-start(f32[48,1024]{1,0:T(8,128)S(1)} %pad_maximum_fusion.2), channel_id=1, source_target_pairs={{0,4},{4,0},{8,12},{12,8},{16,20},{20,16},{24,28},{28,24},{1,5},{5... | collective-permute-start | bytes 589832 | tf_op jit(solution)/shard_map/ppermute | solution.py:330
  64.2 1.8 %collective-permute-done.18.refs_3_ = f32[48,1024]{1,0:T(8,128)S(1)} collective-permute-done((f32[48,1024]{1,0:T(8,128)S(1)}, f32[48,1024]{1,0:T(8,128)S(1)}, u32[]{:S(2)}, u32[]{:S(2)}) %collective-permute-start.18) | collective-permute-done | bytes 196640 | tf_op jit(solution)/shard_map/ppermute | solution.py:330
  66.2 1.9 %finish.2.refs_2_ = f32[48,8192]{1,0:T(8,128)} custom-call(s32[12]{0:T(128)S(1)} %stack.99.where_ref, f32[48,48]{1,0:T(8,128)S(1)} %inverse_factor.1.inverse_ref, f32[48,1152]{1,0:T(8,128)S(1)} %fusion.1.gram_ref.refs_0_, f32[48,512]{1,0:T(8,128)S(1)} %collective-permute-done.16.refs_1_, f32[48,512]{1,0:T(8,128)S(1)} %collective-permute-done.17.refs_2_, ...), custom_call_target="tpu_custom_call" | custom-call | flops 84934656 | bytes 2359296 | tf_op jit(solution)/shard_map/finish/pallas_call | solution.py:308
  68.5 1.5 %finish.3 = f32[48,8192]{1,0:T(8,128)} custom-call(s32[4]{0:T(128)S(1)} %pad_add_fusion.where_ref, f32[48,48]{1,0:T(8,128)S(1)} %inverse_factor.1.inverse_ref, f32[48,1024]{1,0:T(8,128)S(1)} %collective-permute-done.13.refs_0_, f32[48,1024]{1,0:T(8,128)S(1)} %collective-permute-done.15.refs_1_, f32[48,8192]{1,0:T(8,128)} %finish.2.refs_2_), custom_call_target="tpu_custom_call", output_to_operand_aliasing={{}: (4, {})} | custom-call | flops 28311552 | bytes 786432 | tf_op jit(solution)/shard_map/finish/pallas_call | solution.py:308
  (52 shorter events, 7.8 us)
Async XLA Ops:
  7.3 1.5 %collective-permute-start = (f32[48,512]{1,0:T(8,128)S(1)}, f32[48,512]{1,0:T(8,128)S(1)}, u32[]{:S(2)}, u32[]{:S(2)}) collective-permute-start(f32[48,512]{1,0:T(8,128)S(1)} %tall_partial.1), channel_id=1, source_target_pairs={{0,1},{1,0},{2,3},{3,2},{4,5},{5,4},{6,7},{7,6},{8,9},{9,8},{10,11... | collective-permute-start | bytes 294920 | tf_op jit(solution)/shard_map/ppermute | solution.py:330
  8.8 6.0 %collective-permute-start.1 = (f32[48,512]{1,0:T(8,128)S(1)}, f32[48,512]{1,0:T(8,128)S(1)}, u32[]{:S(2)}, u32[]{:S(2)}) collective-permute-start(f32[48,512]{1,0:T(8,128)S(1)} %add.153.one_ref), channel_id=1, source_target_pairs={{0,2},{1,3},{2,0},{3,1},{4,6},{5,7},{6,4},{7,5},{8,10},{9,11},{10,... | collective-permute-start | bytes 294920 | tf_op jit(solution)/shard_map/ppermute | solution.py:330
  18.2 8.6 %collective-permute-start.6 = (f32[48,1024]{1,0:T(8,128)S(1)}, f32[48,1024]{1,0:T(8,128)S(1)}, u32[]{:S(2)}, u32[]{:S(2)}) collective-permute-start(f32[48,1024]{1,0:T(8,128)S(1)} %get-tuple-element.29), channel_id=1, source_target_pairs={{0,8},{4,12},{8,0},{12,4},{16,24},{20,28},{24,16},{28,20},{1,9},{5... | collective-permute-start | bytes 589832 | tf_op jit(solution)/shard_map/ppermute | solution.py:330
  20.1 8.6 %collective-permute-start.2 = (f32[48,1152]{1,0:T(8,128)S(1)}, f32[48,1152]{1,0:T(8,128)S(1)}, u32[]{:S(2)}, u32[]{:S(2)}) collective-permute-start(f32[48,1152]{1,0:T(8,128)S(1)} %get-tuple-element.22.after_ref), channel_id=1, source_target_pairs={{0,4},{4,0},{8,12},{12,8},{16,20},{20,16},{24,28},{28,24},{1,5},{5... | collective-permute-start | bytes 663560 | tf_op jit(solution)/shard_map/ppermute | solution.py:330
  25.9 7.5 %collective-permute-start.3 = (f32[48,1024]{1,0:T(8,128)S(1)}, f32[48,1024]{1,0:T(8,128)S(1)}, u32[]{:S(2)}, u32[]{:S(2)}) collective-permute-start(f32[48,1024]{1,0:T(8,128)S(1)} %get-tuple-element.24), channel_id=1, source_target_pairs={{0,4},{4,0},{8,12},{12,8},{16,20},{20,16},{24,28},{28,24},{1,5},{5... | collective-permute-start | bytes 589832 | tf_op jit(solution)/shard_map/ppermute | solution.py:330
  26.6 6.9 %collective-permute-start.4 = (f32[48,1024]{1,0:T(8,128)S(1)}, f32[48,1024]{1,0:T(8,128)S(1)}, u32[]{:S(2)}, u32[]{:S(2)}) collective-permute-start(f32[48,1024]{1,0:T(8,128)S(1)} %get-tuple-element.26), channel_id=1, source_target_pairs={{0,8},{4,12},{8,0},{12,4},{16,24},{20,28},{24,16},{28,20},{1,9},{5... | collective-permute-start | bytes 589832 | tf_op jit(solution)/shard_map/ppermute | solution.py:330
  26.8 6.9 %collective-permute-start.7 = (f32[48,512]{1,0:T(8,128)S(1)}, f32[48,512]{1,0:T(8,128)S(1)}, u32[]{:S(2)}, u32[]{:S(2)}) collective-permute-start(f32[48,512]{1,0:T(8,128)S(1)} %slice.69), channel_id=1, source_target_pairs={{0,4},{4,0},{8,12},{12,8},{16,20},{20,16},{24,28},{28,24},{1,5},{5... | collective-permute-start | bytes 294920 | tf_op jit(solution)/shard_map/ppermute | solution.py:330
  28.8 5.7 %collective-permute-start.5 = (f32[48,640]{1,0:T(8,128)S(1)}, f32[48,640]{1,0:T(8,128)S(1)}, u32[]{:S(2)}, u32[]{:S(2)}) collective-permute-start(f32[48,640]{1,0:T(8,128)S(1)} %slice.64), channel_id=1, source_target_pairs={{0,8},{4,12},{8,0},{12,4},{16,24},{20,28},{24,16},{28,20},{1,9},{5... | collective-permute-start | bytes 368648 | tf_op jit(solution)/shard_map/ppermute | solution.py:330
  34.5 4.7 %collective-permute-start.8 = (f32[48,512]{1,0:T(8,128)S(1)}, f32[48,512]{1,0:T(8,128)S(1)}, u32[]{:S(2)}, u32[]{:S(2)}) collective-permute-start(f32[48,512]{1,0:T(8,128)S(1)} %slice.61), channel_id=1, source_target_pairs={{0,8},{4,12},{8,0},{12,4},{16,24},{20,28},{24,16},{28,20},{1,9},{5... | collective-permute-start | bytes 294920 | tf_op jit(solution)/shard_map/ppermute | solution.py:330
  35.4 16.4 %collective-permute-start.11 = (f32[48,1152]{1,0:T(8,128)S(1)}, f32[48,1152]{1,0:T(8,128)S(1)}, u32[]{:S(2)}, u32[]{:S(2)}) collective-permute-start(f32[48,1152]{1,0:T(8,128)S(1)} %pad_maximum_fusion), channel_id=1, source_target_pairs={{0,16},{4,20},{8,24},{12,28},{16,0},{20,4},{24,8},{28,12},{1,17},{... | collective-permute-start | bytes 663560 | tf_op jit(solution)/shard_map/ppermute | solution.py:330
  38.0 4.6 %collective-permute-start.9 = (f32[48,512]{1,0:T(8,128)S(1)}, f32[48,512]{1,0:T(8,128)S(1)}, u32[]{:S(2)}, u32[]{:S(2)}) collective-permute-start(f32[48,512]{1,0:T(8,128)S(1)} %slice.62), channel_id=1, source_target_pairs={{0,4},{4,0},{8,12},{12,8},{16,20},{20,16},{24,28},{28,24},{1,5},{5... | collective-permute-start | bytes 294920 | tf_op jit(solution)/shard_map/ppermute | solution.py:330
  42.7 12.5 %collective-permute-start.10 = (f32[48,1024]{1,0:T(8,128)S(1)}, f32[48,1024]{1,0:T(8,128)S(1)}, u32[]{:S(2)}, u32[]{:S(2)}) collective-permute-start(f32[48,1024]{1,0:T(8,128)S(1)} %pad_maximum_fusion.1), channel_id=1, source_target_pairs={{0,16},{4,20},{8,24},{12,28},{16,0},{20,4},{24,8},{28,12},{1,17},{... | collective-permute-start | bytes 589832 | tf_op jit(solution)/shard_map/ppermute | solution.py:330
  51.8 7.1 %collective-permute-start.17 = (f32[48,512]{1,0:T(8,128)S(1)}, f32[48,512]{1,0:T(8,128)S(1)}, u32[]{:S(2)}, u32[]{:S(2)}) collective-permute-start(f32[48,512]{1,0:T(8,128)S(1)} %get-tuple-element.35), channel_id=1, source_target_pairs={{0,4},{4,0},{8,12},{12,8},{16,20},{20,16},{24,28},{28,24},{1,5},{5... | collective-permute-start | bytes 294920 | tf_op jit(solution)/shard_map/ppermute | solution.py:330
  52.6 5.5 %collective-permute-start.16 = (f32[48,512]{1,0:T(8,128)S(1)}, f32[48,512]{1,0:T(8,128)S(1)}, u32[]{:S(2)}, u32[]{:S(2)}) collective-permute-start(f32[48,512]{1,0:T(8,128)S(1)} %get-tuple-element.36), channel_id=1, source_target_pairs={{0,8},{4,12},{8,0},{12,4},{16,24},{20,28},{24,16},{28,20},{1,9},{5... | collective-permute-start | bytes 294920 | tf_op jit(solution)/shard_map/ppermute | solution.py:330
  55.2 7.5 %collective-permute-start.12 = (f32[48,512]{1,0:T(8,128)S(1)}, f32[48,512]{1,0:T(8,128)S(1)}, u32[]{:S(2)}, u32[]{:S(2)}) collective-permute-start(f32[48,512]{1,0:T(8,128)S(1)} %get-tuple-element.33), channel_id=1, source_target_pairs={{0,8},{4,12},{8,0},{12,4},{16,24},{20,28},{24,16},{28,20},{1,9},{5... | collective-permute-start | bytes 294920 | tf_op jit(solution)/shard_map/ppermute | solution.py:330
  56.8 5.1 %collective-permute-start.14 = (f32[48,512]{1,0:T(8,128)S(1)}, f32[48,512]{1,0:T(8,128)S(1)}, u32[]{:S(2)}, u32[]{:S(2)}) collective-permute-start(f32[48,512]{1,0:T(8,128)S(1)} %get-tuple-element.34), channel_id=1, source_target_pairs={{0,4},{4,0},{8,12},{12,8},{16,20},{20,16},{24,28},{28,24},{1,5},{5... | collective-permute-start | bytes 294920 | tf_op jit(solution)/shard_map/ppermute | solution.py:330
  58.1 8.0 %collective-permute-start.18 = (f32[48,1024]{1,0:T(8,128)S(1)}, f32[48,1024]{1,0:T(8,128)S(1)}, u32[]{:S(2)}, u32[]{:S(2)}) collective-permute-start(f32[48,1024]{1,0:T(8,128)S(1)} %pad_maximum_fusion.4), channel_id=1, source_target_pairs={{0,4},{4,0},{8,12},{12,8},{16,20},{20,16},{24,28},{28,24},{1,5},{5... | collective-permute-start | bytes 589832 | tf_op jit(solution)/shard_map/ppermute | solution.py:330
  58.9 7.3 %collective-permute-start.19 = (f32[48,1024]{1,0:T(8,128)S(1)}, f32[48,1024]{1,0:T(8,128)S(1)}, u32[]{:S(2)}, u32[]{:S(2)}) collective-permute-start(f32[48,1024]{1,0:T(8,128)S(1)} %pad_maximum_fusion.5), channel_id=1, source_target_pairs={{0,8},{4,12},{8,0},{12,4},{16,24},{20,28},{24,16},{28,20},{1,9},{5... | collective-permute-start | bytes 589832 | tf_op jit(solution)/shard_map/ppermute | solution.py:330
  61.9 6.4 %collective-permute-start.15 = (f32[48,1024]{1,0:T(8,128)S(1)}, f32[48,1024]{1,0:T(8,128)S(1)}, u32[]{:S(2)}, u32[]{:S(2)}) collective-permute-start(f32[48,1024]{1,0:T(8,128)S(1)} %pad_maximum_fusion.3), channel_id=1, source_target_pairs={{0,8},{4,12},{8,0},{12,4},{16,24},{20,28},{24,16},{28,20},{1,9},{5... | collective-permute-start | bytes 589832 | tf_op jit(solution)/shard_map/ppermute | solution.py:330
  62.8 5.7 %collective-permute-start.13 = (f32[48,1024]{1,0:T(8,128)S(1)}, f32[48,1024]{1,0:T(8,128)S(1)}, u32[]{:S(2)}, u32[]{:S(2)}) collective-permute-start(f32[48,1024]{1,0:T(8,128)S(1)} %pad_maximum_fusion.2), channel_id=1, source_target_pairs={{0,4},{4,0},{8,12},{12,8},{16,20},{20,16},{24,28},{28,24},{1,5},{5... | collective-permute-start | bytes 589832 | tf_op jit(solution)/shard_map/ppermute | solution.py:330

commit v26 on v25

--- a/solution.py
+++ b/solution.py
@@ -86,7 +86,7 @@
 def tall_partial(probes, sketch_t):
     rows, cols = probes.shape
     rank = sketch_t.shape[0]
-    unit = min(2 * UNIT, cols)
+    unit = min(UNIT, cols)
     blocks = cols // unit
     return pl.pallas_call(
         tall_kernel,

time: 70.2 us -> 70 us (level)
  no operation moved by 1% of the time
where the time goes in v26:
time: 70 us; the launch traced here: 69.9 us
  starting transfers between devices  23.7 us (34%)
  Pallas kernels  23.2 us (33%)
  waiting for transfers between devices  22 us (31%)
    ppermute x20, starting transfers between devices, swap(): return lax.ppermute(value, axis, [(i, i ^ bit) for i in range(size)])  23.7 us
    ppermute x20, waiting for transfers between devices, swap(): return lax.ppermute(value, axis, [(i, i ^ bit) for i in range(size)])  22 us
    pallas_call x3, Pallas kernels, products(): pl.pallas_call(functools.partial(kernel, plan, grams), in_specs=[TABLE, *...  10.7 us
    pallas_call x1, Pallas kernels, tall_partial(): pl.pallas_call(tall_kernel, in_specs=[HBM, HBM], out_specs=WHOLE, out_sha...  7.09 us
    pallas_call x2, Pallas kernels, finish(): pl.pallas_call(functools.partial(finish_kernel, [piece[1:] for piece in p...  3.39 us
    pallas_call x1, Pallas kernels, inverse_factor(): pl.pallas_call(inverse_kernel, grid=(1,), in_specs=[pl.BlockSpec((rank, L...  2.01 us
  transfers between devices with their start and end apart: 20, of which 12 were waited for; matrix products, arithmetic and copies ran while one was open for 1% of the time, Pallas kernels for 16%

profile of v26, /device:TPU:0, one launch (start us, length us, event | category | flops | bytes accessed | tf_op | source)
XLA Modules:
  0.0 69.9 jit_solution(14079014632580651528)
XLA Ops:
  0.0 7.1 %tall_partial.1 = f32[48,512]{1,0:T(8,128)S(1)} custom-call(f32[512,8192]{1,0:T(8,128)} %x_hbm.7, f32[48,8192]{1,0:T(8,128)} %bitcast.17), custom_call_target="tpu_custom_call" | custom-call | flops 1207959552 | bytes 16777216 | tf_op jit(solution)/shard_map/tall_partial/pallas_call | solution.py:91
  7.6 0.9 %collective-permute-done = f32[48,512]{1,0:T(8,128)S(1)} collective-permute-done((f32[48,512]{1,0:T(8,128)S(1)}, f32[48,512]{1,0:T(8,128)S(1)}, u32[]{:S(2)}, u32[]{:S(2)}) %collective-permute-start) | collective-permute-done | bytes 98336 | tf_op jit(solution)/shard_map/ppermute | solution.py:330
  8.6 2.9 %collective-permute-start.1 = (f32[48,512]{1,0:T(8,128)S(1)}, f32[48,512]{1,0:T(8,128)S(1)}, u32[]{:S(2)}, u32[]{:S(2)}) collective-permute-start(f32[48,512]{1,0:T(8,128)S(1)} %add.153.one_ref), channel_id=1, source_target_pairs={{0,2},{1,3},{2,0},{3,1},{4,6},{5,7},{6,4},{7,5},{8,10},{9,11},{10,... | collective-permute-start | bytes 294920 | tf_op jit(solution)/shard_map/ppermute | solution.py:330
  11.6 3.0 %collective-permute-done.1.two_ref = f32[48,512]{1,0:T(8,128)S(1)} collective-permute-done((f32[48,512]{1,0:T(8,128)S(1)}, f32[48,512]{1,0:T(8,128)S(1)}, u32[]{:S(2)}, u32[]{:S(2)}) %collective-permute-start.1) | collective-permute-done | bytes 98336 | tf_op jit(solution)/shard_map/ppermute | solution.py:330
  14.6 3.3 %first_products.1 = (bf16[96,512]{1,0:T(8,128)(2,1)S(1)}, f32[48,128]{1,0:T(8,128)S(1)}, f32[48,1152]{1,0:T(8,128)S(1)}, f32[48,1024]{1,0:T(8,128)S(1)}) custom-call(s32[4]{0:T(128)S(1)} %pad_add_fusion.2.which_ref, f32[48,512]{1,0:T(8,128)S(1)} %add.153.one_ref, f32[48,512]{1,0:T(8,128)S(1)} %collective-permute-done.1.two_ref, f32[512,8192]{1,0:T(8,128)} %x_hbm.7), custom_call_target="tpu_custom_call" | custom-call | flops 301989888 | bytes 4194304 | tf_op jit(solution)/shard_map/first_products/pallas_call | solution.py:192
  18.0 1.9 %collective-permute-start.6 = (f32[48,1024]{1,0:T(8,128)S(1)}, f32[48,1024]{1,0:T(8,128)S(1)}, u32[]{:S(2)}, u32[]{:S(2)}) collective-permute-start(f32[48,1024]{1,0:T(8,128)S(1)} %get-tuple-element.29), channel_id=1, source_target_pairs={{0,8},{4,12},{8,0},{12,4},{16,24},{20,28},{24,16},{28,20},{1,9},{5... | collective-permute-start | bytes 589832 | tf_op jit(solution)/shard_map/ppermute | solution.py:330
  19.9 1.5 %collective-permute-start.2 = (f32[48,1152]{1,0:T(8,128)S(1)}, f32[48,1152]{1,0:T(8,128)S(1)}, u32[]{:S(2)}, u32[]{:S(2)}) collective-permute-start(f32[48,1152]{1,0:T(8,128)S(1)} %get-tuple-element.22.after_ref), channel_id=1, source_target_pairs={{0,4},{4,0},{8,12},{12,8},{16,20},{20,16},{24,28},{28,24},{1,5},{5... | collective-permute-start | bytes 663560 | tf_op jit(solution)/shard_map/ppermute | solution.py:330
  21.4 4.3 %rest_products.3 = (f32[48,1152]{1,0:T(8,128)S(1)}, f32[48,1024]{1,0:T(8,128)S(1)}, f32[48,1024]{1,0:T(8,128)S(1)}, f32[48,1024]{1,0:T(8,128)S(1)}) custom-call(s32[8]{0:T(128)S(1)} %stack.98.which_ref, bf16[96,512]{1,0:T(8,128)(2,1)S(1)} %get-tuple-element.20.both_ref, f32[48,128]{1,0:T(8,128)S(1)} %get-tuple-element.21.gram_ref, f32[512,8192]{1,0:T(8,128)} %x_hbm.7, ...), custom_call_target="tpu_custom_call" | custom-call | flops 603979776 | bytes 8388608 | tf_op jit(solution)/shard_map/rest_products/pallas_call | solution.py:192
  26.7 1.8 %collective-permute-start.7 = (f32[48,512]{1,0:T(8,128)S(1)}, f32[48,512]{1,0:T(8,128)S(1)}, u32[]{:S(2)}, u32[]{:S(2)}) collective-permute-start(f32[48,512]{1,0:T(8,128)S(1)} %slice.69), channel_id=1, source_target_pairs={{0,4},{4,0},{8,12},{12,8},{16,20},{20,16},{24,28},{28,24},{1,5},{5... | collective-permute-start | bytes 294920 | tf_op jit(solution)/shard_map/ppermute | solution.py:330
  28.6 1.6 %collective-permute-start.5 = (f32[48,640]{1,0:T(8,128)S(1)}, f32[48,640]{1,0:T(8,128)S(1)}, u32[]{:S(2)}, u32[]{:S(2)}) collective-permute-start(f32[48,640]{1,0:T(8,128)S(1)} %slice.64), channel_id=1, source_target_pairs={{0,8},{4,12},{8,0},{12,4},{16,24},{20,28},{24,16},{28,20},{1,9},{5... | collective-permute-start | bytes 368648 | tf_op jit(solution)/shard_map/ppermute | solution.py:330
  30.2 3.1 %rest_products.2 = (f32[48,1024]{1,0:T(8,128)S(1)}, f32[48,1024]{1,0:T(8,128)S(1)}) custom-call(s32[4]{0:T(128)S(1)} %pad_add_fusion.1.which_ref, bf16[96,512]{1,0:T(8,128)(2,1)S(1)} %get-tuple-element.20.both_ref, f32[48,128]{1,0:T(8,128)S(1)} %get-tuple-element.21.gram_ref, f32[512,8192]{1,0:T(8,128)} %x_hbm.7, f32[48,1152]{1,0:T(8,128)S(1)} %collective-permute-done.2.after_ref), custom_call_target="tpu_custom_call" | custom-call | flops 301989888 | bytes 4194304 | tf_op jit(solution)/shard_map/rest_products/pallas_call | solution.py:192
  35.2 2.6 %collective-permute-start.11 = (f32[48,1152]{1,0:T(8,128)S(1)}, f32[48,1152]{1,0:T(8,128)S(1)}, u32[]{:S(2)}, u32[]{:S(2)}) collective-permute-start(f32[48,1152]{1,0:T(8,128)S(1)} %pad_maximum_fusion), channel_id=1, source_target_pairs={{0,16},{4,20},{8,24},{12,28},{16,0},{20,4},{24,8},{28,12},{1,17},{... | collective-permute-start | bytes 663560 | tf_op jit(solution)/shard_map/ppermute | solution.py:330
  37.8 1.1 %collective-permute-start.9 = (f32[48,512]{1,0:T(8,128)S(1)}, f32[48,512]{1,0:T(8,128)S(1)}, u32[]{:S(2)}, u32[]{:S(2)}) collective-permute-start(f32[48,512]{1,0:T(8,128)S(1)} %slice.62), channel_id=1, source_target_pairs={{0,4},{4,0},{8,12},{12,8},{16,20},{20,16},{24,28},{28,24},{1,5},{5... | collective-permute-start | bytes 294920 | tf_op jit(solution)/shard_map/ppermute | solution.py:330
  39.0 3.4 %collective-permute-done.9 = f32[48,512]{1,0:T(8,128)S(1)} collective-permute-done((f32[48,512]{1,0:T(8,128)S(1)}, f32[48,512]{1,0:T(8,128)S(1)}, u32[]{:S(2)}, u32[]{:S(2)}) %collective-permute-start.9) | collective-permute-done | bytes 98336 | tf_op jit(solution)/shard_map/ppermute | solution.py:330
  42.8 8.7 %collective-permute-done.11 = f32[48,1152]{1,0:T(8,128)S(1)} collective-permute-done((f32[48,1152]{1,0:T(8,128)S(1)}, f32[48,1152]{1,0:T(8,128)S(1)}, u32[]{:S(2)}, u32[]{:S(2)}) %collective-permute-start.11) | collective-permute-done | bytes 221216 | tf_op jit(solution)/shard_map/ppermute | solution.py:330
  53.0 2.0 %inverse_factor.1.inverse_ref = f32[48,48]{1,0:T(8,128)S(1)} custom-call(f32[48,1152]{1,0:T(8,128)S(1)} %fusion.1.gram_ref.refs_0_), custom_call_target="tpu_custom_call" | custom-call | flops 20000000 | bytes 49152 | tf_op jit(solution)/shard_map/inverse_factor/pallas_call | solution.py:267
  55.1 1.6 %collective-permute-start.12 = (f32[48,512]{1,0:T(8,128)S(1)}, f32[48,512]{1,0:T(8,128)S(1)}, u32[]{:S(2)}, u32[]{:S(2)}) collective-permute-start(f32[48,512]{1,0:T(8,128)S(1)} %get-tuple-element.33), channel_id=1, source_target_pairs={{0,8},{4,12},{8,0},{12,4},{16,24},{20,28},{24,16},{28,20},{1,9},{5... | collective-permute-start | bytes 294920 | tf_op jit(solution)/shard_map/ppermute | solution.py:330
  56.7 1.2 %collective-permute-start.14 = (f32[48,512]{1,0:T(8,128)S(1)}, f32[48,512]{1,0:T(8,128)S(1)}, u32[]{:S(2)}, u32[]{:S(2)}) collective-permute-start(f32[48,512]{1,0:T(8,128)S(1)} %get-tuple-element.34), channel_id=1, source_target_pairs={{0,4},{4,0},{8,12},{12,8},{16,20},{20,16},{24,28},{28,24},{1,5},{5... | collective-permute-start | bytes 294920 | tf_op jit(solution)/shard_map/ppermute | solution.py:330
  59.4 2.3 %collective-permute-done.14.refs_7_ = f32[48,512]{1,0:T(8,128)S(1)} collective-permute-done((f32[48,512]{1,0:T(8,128)S(1)}, f32[48,512]{1,0:T(8,128)S(1)}, u32[]{:S(2)}, u32[]{:S(2)}) %collective-permute-start.14) | collective-permute-done | bytes 98336 | tf_op jit(solution)/shard_map/ppermute | solution.py:330
  61.7 0.9 %collective-permute-start.15 = (f32[48,1024]{1,0:T(8,128)S(1)}, f32[48,1024]{1,0:T(8,128)S(1)}, u32[]{:S(2)}, u32[]{:S(2)}) collective-permute-start(f32[48,1024]{1,0:T(8,128)S(1)} %pad_maximum_fusion.3), channel_id=1, source_target_pairs={{0,8},{4,12},{8,0},{12,4},{16,24},{20,28},{24,16},{28,20},{1,9},{5... | collective-permute-start | bytes 589832 | tf_op jit(solution)/shard_map/ppermute | solution.py:330
  62.6 1.1 %collective-permute-start.13 = (f32[48,1024]{1,0:T(8,128)S(1)}, f32[48,1024]{1,0:T(8,128)S(1)}, u32[]{:S(2)}, u32[]{:S(2)}) collective-permute-start(f32[48,1024]{1,0:T(8,128)S(1)} %pad_maximum_fusion.2), channel_id=1, source_target_pairs={{0,4},{4,0},{8,12},{12,8},{16,20},{20,16},{24,28},{28,24},{1,5},{5... | collective-permute-start | bytes 589832 | tf_op jit(solution)/shard_map/ppermute | solution.py:330
  63.9 1.9 %collective-permute-done.18.refs_3_ = f32[48,1024]{1,0:T(8,128)S(1)} collective-permute-done((f32[48,1024]{1,0:T(8,128)S(1)}, f32[48,1024]{1,0:T(8,128)S(1)}, u32[]{:S(2)}, u32[]{:S(2)}) %collective-permute-start.18) | collective-permute-done | bytes 196640 | tf_op jit(solution)/shard_map/ppermute | solution.py:330
  66.1 1.9 %finish.2.refs_2_ = f32[48,8192]{1,0:T(8,128)} custom-call(s32[12]{0:T(128)S(1)} %stack.99.where_ref, f32[48,48]{1,0:T(8,128)S(1)} %inverse_factor.1.inverse_ref, f32[48,1152]{1,0:T(8,128)S(1)} %fusion.1.gram_ref.refs_0_, f32[48,512]{1,0:T(8,128)S(1)} %collective-permute-done.16.refs_1_, f32[48,512]{1,0:T(8,128)S(1)} %collective-permute-done.17.refs_2_, ...), custom_call_target="tpu_custom_call" | custom-call | flops 84934656 | bytes 2359296 | tf_op jit(solution)/shard_map/finish/pallas_call | solution.py:308
  68.4 1.5 %finish.3 = f32[48,8192]{1,0:T(8,128)} custom-call(s32[4]{0:T(128)S(1)} %pad_add_fusion.where_ref, f32[48,48]{1,0:T(8,128)S(1)} %inverse_factor.1.inverse_ref, f32[48,1024]{1,0:T(8,128)S(1)} %collective-permute-done.13.refs_0_, f32[48,1024]{1,0:T(8,128)S(1)} %collective-permute-done.15.refs_1_, f32[48,8192]{1,0:T(8,128)} %finish.2.refs_2_), custom_call_target="tpu_custom_call", output_to_operand_aliasing={{}: (4, {})} | custom-call | flops 28311552 | bytes 786432 | tf_op jit(solution)/shard_map/finish/pallas_call | solution.py:308
  (52 shorter events, 7.9 us)
Async XLA Ops:
  7.1 1.5 %collective-permute-start = (f32[48,512]{1,0:T(8,128)S(1)}, f32[48,512]{1,0:T(8,128)S(1)}, u32[]{:S(2)}, u32[]{:S(2)}) collective-permute-start(f32[48,512]{1,0:T(8,128)S(1)} %tall_partial.1), channel_id=1, source_target_pairs={{0,1},{1,0},{2,3},{3,2},{4,5},{5,4},{6,7},{7,6},{8,9},{9,8},{10,11... | collective-permute-start | bytes 294920 | tf_op jit(solution)/shard_map/ppermute | solution.py:330
  8.6 6.0 %collective-permute-start.1 = (f32[48,512]{1,0:T(8,128)S(1)}, f32[48,512]{1,0:T(8,128)S(1)}, u32[]{:S(2)}, u32[]{:S(2)}) collective-permute-start(f32[48,512]{1,0:T(8,128)S(1)} %add.153.one_ref), channel_id=1, source_target_pairs={{0,2},{1,3},{2,0},{3,1},{4,6},{5,7},{6,4},{7,5},{8,10},{9,11},{10,... | collective-permute-start | bytes 294920 | tf_op jit(solution)/shard_map/ppermute | solution.py:330
  18.0 8.6 %collective-permute-start.6 = (f32[48,1024]{1,0:T(8,128)S(1)}, f32[48,1024]{1,0:T(8,128)S(1)}, u32[]{:S(2)}, u32[]{:S(2)}) collective-permute-start(f32[48,1024]{1,0:T(8,128)S(1)} %get-tuple-element.29), channel_id=1, source_target_pairs={{0,8},{4,12},{8,0},{12,4},{16,24},{20,28},{24,16},{28,20},{1,9},{5... | collective-permute-start | bytes 589832 | tf_op jit(solution)/shard_map/ppermute | solution.py:330
  19.9 8.6 %collective-permute-start.2 = (f32[48,1152]{1,0:T(8,128)S(1)}, f32[48,1152]{1,0:T(8,128)S(1)}, u32[]{:S(2)}, u32[]{:S(2)}) collective-permute-start(f32[48,1152]{1,0:T(8,128)S(1)} %get-tuple-element.22.after_ref), channel_id=1, source_target_pairs={{0,4},{4,0},{8,12},{12,8},{16,20},{20,16},{24,28},{28,24},{1,5},{5... | collective-permute-start | bytes 663560 | tf_op jit(solution)/shard_map/ppermute | solution.py:330
  25.8 7.5 %collective-permute-start.3 = (f32[48,1024]{1,0:T(8,128)S(1)}, f32[48,1024]{1,0:T(8,128)S(1)}, u32[]{:S(2)}, u32[]{:S(2)}) collective-permute-start(f32[48,1024]{1,0:T(8,128)S(1)} %get-tuple-element.24), channel_id=1, source_target_pairs={{0,4},{4,0},{8,12},{12,8},{16,20},{20,16},{24,28},{28,24},{1,5},{5... | collective-permute-start | bytes 589832 | tf_op jit(solution)/shard_map/ppermute | solution.py:330
  26.4 6.9 %collective-permute-start.4 = (f32[48,1024]{1,0:T(8,128)S(1)}, f32[48,1024]{1,0:T(8,128)S(1)}, u32[]{:S(2)}, u32[]{:S(2)}) collective-permute-start(f32[48,1024]{1,0:T(8,128)S(1)} %get-tuple-element.26), channel_id=1, source_target_pairs={{0,8},{4,12},{8,0},{12,4},{16,24},{20,28},{24,16},{28,20},{1,9},{5... | collective-permute-start | bytes 589832 | tf_op jit(solution)/shard_map/ppermute | solution.py:330
  26.7 6.9 %collective-permute-start.7 = (f32[48,512]{1,0:T(8,128)S(1)}, f32[48,512]{1,0:T(8,128)S(1)}, u32[]{:S(2)}, u32[]{:S(2)}) collective-permute-start(f32[48,512]{1,0:T(8,128)S(1)} %slice.69), channel_id=1, source_target_pairs={{0,4},{4,0},{8,12},{12,8},{16,20},{20,16},{24,28},{28,24},{1,5},{5... | collective-permute-start | bytes 294920 | tf_op jit(solution)/shard_map/ppermute | solution.py:330
  28.6 5.7 %collective-permute-start.5 = (f32[48,640]{1,0:T(8,128)S(1)}, f32[48,640]{1,0:T(8,128)S(1)}, u32[]{:S(2)}, u32[]{:S(2)}) collective-permute-start(f32[48,640]{1,0:T(8,128)S(1)} %slice.64), channel_id=1, source_target_pairs={{0,8},{4,12},{8,0},{12,4},{16,24},{20,28},{24,16},{28,20},{1,9},{5... | collective-permute-start | bytes 368648 | tf_op jit(solution)/shard_map/ppermute | solution.py:330
  34.3 4.7 %collective-permute-start.8 = (f32[48,512]{1,0:T(8,128)S(1)}, f32[48,512]{1,0:T(8,128)S(1)}, u32[]{:S(2)}, u32[]{:S(2)}) collective-permute-start(f32[48,512]{1,0:T(8,128)S(1)} %slice.61), channel_id=1, source_target_pairs={{0,8},{4,12},{8,0},{12,4},{16,24},{20,28},{24,16},{28,20},{1,9},{5... | collective-permute-start | bytes 294920 | tf_op jit(solution)/shard_map/ppermute | solution.py:330
  35.2 16.4 %collective-permute-start.11 = (f32[48,1152]{1,0:T(8,128)S(1)}, f32[48,1152]{1,0:T(8,128)S(1)}, u32[]{:S(2)}, u32[]{:S(2)}) collective-permute-start(f32[48,1152]{1,0:T(8,128)S(1)} %pad_maximum_fusion), channel_id=1, source_target_pairs={{0,16},{4,20},{8,24},{12,28},{16,0},{20,4},{24,8},{28,12},{1,17},{... | collective-permute-start | bytes 663560 | tf_op jit(solution)/shard_map/ppermute | solution.py:330
  37.8 4.6 %collective-permute-start.9 = (f32[48,512]{1,0:T(8,128)S(1)}, f32[48,512]{1,0:T(8,128)S(1)}, u32[]{:S(2)}, u32[]{:S(2)}) collective-permute-start(f32[48,512]{1,0:T(8,128)S(1)} %slice.62), channel_id=1, source_target_pairs={{0,4},{4,0},{8,12},{12,8},{16,20},{20,16},{24,28},{28,24},{1,5},{5... | collective-permute-start | bytes 294920 | tf_op jit(solution)/shard_map/ppermute | solution.py:330
  42.5 12.5 %collective-permute-start.10 = (f32[48,1024]{1,0:T(8,128)S(1)}, f32[48,1024]{1,0:T(8,128)S(1)}, u32[]{:S(2)}, u32[]{:S(2)}) collective-permute-start(f32[48,1024]{1,0:T(8,128)S(1)} %pad_maximum_fusion.1), channel_id=1, source_target_pairs={{0,16},{4,20},{8,24},{12,28},{16,0},{20,4},{24,8},{28,12},{1,17},{... | collective-permute-start | bytes 589832 | tf_op jit(solution)/shard_map/ppermute | solution.py:330
  51.6 7.2 %collective-permute-start.17 = (f32[48,512]{1,0:T(8,128)S(1)}, f32[48,512]{1,0:T(8,128)S(1)}, u32[]{:S(2)}, u32[]{:S(2)}) collective-permute-start(f32[48,512]{1,0:T(8,128)S(1)} %get-tuple-element.35), channel_id=1, source_target_pairs={{0,4},{4,0},{8,12},{12,8},{16,20},{20,16},{24,28},{28,24},{1,5},{5... | collective-permute-start | bytes 294920 | tf_op jit(solution)/shard_map/ppermute | solution.py:330
  52.5 5.4 %collective-permute-start.16 = (f32[48,512]{1,0:T(8,128)S(1)}, f32[48,512]{1,0:T(8,128)S(1)}, u32[]{:S(2)}, u32[]{:S(2)}) collective-permute-start(f32[48,512]{1,0:T(8,128)S(1)} %get-tuple-element.36), channel_id=1, source_target_pairs={{0,8},{4,12},{8,0},{12,4},{16,24},{20,28},{24,16},{28,20},{1,9},{5... | collective-permute-start | bytes 294920 | tf_op jit(solution)/shard_map/ppermute | solution.py:330
  55.1 7.6 %collective-permute-start.12 = (f32[48,512]{1,0:T(8,128)S(1)}, f32[48,512]{1,0:T(8,128)S(1)}, u32[]{:S(2)}, u32[]{:S(2)}) collective-permute-start(f32[48,512]{1,0:T(8,128)S(1)} %get-tuple-element.33), channel_id=1, source_target_pairs={{0,8},{4,12},{8,0},{12,4},{16,24},{20,28},{24,16},{28,20},{1,9},{5... | collective-permute-start | bytes 294920 | tf_op jit(solution)/shard_map/ppermute | solution.py:330
  56.7 5.0 %collective-permute-start.14 = (f32[48,512]{1,0:T(8,128)S(1)}, f32[48,512]{1,0:T(8,128)S(1)}, u32[]{:S(2)}, u32[]{:S(2)}) collective-permute-start(f32[48,512]{1,0:T(8,128)S(1)} %get-tuple-element.34), channel_id=1, source_target_pairs={{0,4},{4,0},{8,12},{12,8},{16,20},{20,16},{24,28},{28,24},{1,5},{5... | collective-permute-start | bytes 294920 | tf_op jit(solution)/shard_map/ppermute | solution.py:330
  57.9 8.0 %collective-permute-start.18 = (f32[48,1024]{1,0:T(8,128)S(1)}, f32[48,1024]{1,0:T(8,128)S(1)}, u32[]{:S(2)}, u32[]{:S(2)}) collective-permute-start(f32[48,1024]{1,0:T(8,128)S(1)} %pad_maximum_fusion.4), channel_id=1, source_target_pairs={{0,4},{4,0},{8,12},{12,8},{16,20},{20,16},{24,28},{28,24},{1,5},{5... | collective-permute-start | bytes 589832 | tf_op jit(solution)/shard_map/ppermute | solution.py:330
  58.8 7.3 %collective-permute-start.19 = (f32[48,1024]{1,0:T(8,128)S(1)}, f32[48,1024]{1,0:T(8,128)S(1)}, u32[]{:S(2)}, u32[]{:S(2)}) collective-permute-start(f32[48,1024]{1,0:T(8,128)S(1)} %pad_maximum_fusion.5), channel_id=1, source_target_pairs={{0,8},{4,12},{8,0},{12,4},{16,24},{20,28},{24,16},{28,20},{1,9},{5... | collective-permute-start | bytes 589832 | tf_op jit(solution)/shard_map/ppermute | solution.py:330
  61.7 6.5 %collective-permute-start.15 = (f32[48,1024]{1,0:T(8,128)S(1)}, f32[48,1024]{1,0:T(8,128)S(1)}, u32[]{:S(2)}, u32[]{:S(2)}) collective-permute-start(f32[48,1024]{1,0:T(8,128)S(1)} %pad_maximum_fusion.3), channel_id=1, source_target_pairs={{0,8},{4,12},{8,0},{12,4},{16,24},{20,28},{24,16},{28,20},{1,9},{5... | collective-permute-start | bytes 589832 | tf_op jit(solution)/shard_map/ppermute | solution.py:330
  62.6 5.7 %collective-permute-start.13 = (f32[48,1024]{1,0:T(8,128)S(1)}, f32[48,1024]{1,0:T(8,128)S(1)}, u32[]{:S(2)}, u32[]{:S(2)}) collective-permute-start(f32[48,1024]{1,0:T(8,128)S(1)} %pad_maximum_fusion.2), channel_id=1, source_target_pairs={{0,4},{4,0},{8,12},{12,8},{16,20},{20,16},{24,28},{28,24},{1,5},{5... | collective-permute-start | bytes 589832 | tf_op jit(solution)/shard_map/ppermute | solution.py:330
